TPU v7x, 32 devices: a whole 2x2x4 slice. The times are simulated.
32 devices in a mesh: pipe: 2 (over core), tensor: 16 (over z, y, x).
Axes of the slice: x: 2, y: 2, z: 4, core: 2. Of those that a mesh axis runs over, the one named last changes fastest.
Arguments:
- output_gradient: bfloat16 [2, 16, 2, 256, 1024], P('pipe', 'tensor'), may hold values from -6 to 6
- forward_input: bfloat16 [2, 2, 512, 8192], P('pipe', None, None, 'tensor'), may hold values from -6 to 6
- saved_rank_outputs: bfloat16 [2, 2, 512, 64], P('pipe', None, 'tensor'), may hold values from -6 to 6
- projection_weight: bfloat16 [2, 16, 4096, 1024], P('pipe', 'tensor'), may hold values from -0.0625 to 0.0625
- adapter_down_maps: bfloat16 [2, 8, 64, 8192], P('pipe', None, None, 'tensor'), may hold values from -0.75 to 0.75
- adapter_up_maps: bfloat16 [2, 16, 8, 32, 1024], P('pipe', 'tensor'), may hold values from -0.0625 to 0.0625
- segment_adapter_class: int32 [2, 2, 4], P('pipe'), may hold values from 0 to 7
- live_segment_table: int32 [2, 2], P('pipe'), may hold values from 1 to 4, as said below
Outputs:
- grad_prev: bfloat16 [2, 2, 512, 8192], P('pipe', None, None, 'tensor')
- down_map_gradient: bfloat16 [2, 8, 64, 8192], P('pipe', None, None, 'tensor')
- up_map_gradient: bfloat16 [2, 16, 8, 32, 1024], P('pipe', 'tensor')
Inputs may be any that keep to these rules, and one draw needn't show every extreme that they name: The first live_segment_table segments of a microbatch are live; some microbatch has all 4 live.
All inputs are finite; a program needn't handle non-finite values.
Results may differ from a plain program's by a relative error of at most 0.0049.
Values may be sent and summed in bfloat16 or wider, within the bound.
No kernel may reach another device: no remote copies, remote signals or barrier semaphores. Data moves between devices by JAX's collectives and lax.ppermute only.
A program may use at most 128 MiB of HBM per device.

v0:
```python
import jax
import jax.numpy as jnp
from jax import lax
from jax.sharding import PartitionSpec as P

SEG = 128


def partner(value, axis, apart):
    mask = 2**apart
    pairs = [(source, source ^ mask) for source in range(lax.axis_size(axis))]
    return lax.ppermute(value, axis, pairs)


def shifted(block, axis, distance):
    devices = range(lax.axis_size(axis))
    route = [((i - distance) % len(devices), i) for i in devices]
    return lax.ppermute(block, axis, route)


def choose_segment_rows(class_indicator, segment_lookup):
    return jnp.einsum(
        "pzw,wlq->pzlq", class_indicator, segment_lookup, preferred_element_type=jnp.float32
    ).astype(jnp.bfloat16)


def shards(
    output_gradient,
    forward_input,
    saved_rank_outputs,
    projection_weight,
    adapter_down_maps,
    adapter_up_maps,
    segment_adapter_class,
    live_segment_table,
):
    grad_tile = output_gradient[0, 0]
    micro_count, tile_rows, tile_cols = grad_tile.shape
    weight = projection_weight[0, 0]
    up_matrix_tile = adapter_up_maps[0, 0]
    rank_part = up_matrix_tile.shape[1]
    rank_extent = adapter_down_maps.shape[2]
    local_portion = adapter_down_maps.shape[3]
    group_size = lax.axis_size("tensor")
    total_bits = group_size.bit_length() - 1
    low_size = min(group_size, 8)
    low_bits = low_size.bit_length() - 1
    high_size = group_size // low_size
    position = lax.axis_index("tensor")
    high_index = position // low_size
    batch_rows = tile_rows * high_size
    seg_count = batch_rows // SEG
    row_ids = high_index * tile_rows + jnp.arange(tile_rows, dtype=jnp.int32)
    live_count = live_segment_table[0]
    keep_rows = (row_ids // SEG)[None, :] < live_count[:, None]
    masked_tile = jnp.where(keep_rows[:, :, None], grad_tile, jnp.zeros_like(grad_tile))

    def project(rows_block):
        return jnp.einsum("mrd,id->mri", rows_block, weight, preferred_element_type=jnp.float32)

    def place(own_part, received, level):
        leading = position >> level & 1 == 0
        return jnp.where(
            leading,
            jnp.concatenate([own_part, received], 1),
            jnp.concatenate([received, own_part], 1),
        )

    gathered = masked_tile
    products = project(masked_tile)
    for level in range(low_bits, total_bits):
        received = partner(gathered, "tensor", level)
        products = place(products, project(received), level)
        gathered = place(gathered, received, level)
    reduced = products
    for level in reversed(range(low_bits)):
        half_cols = reduced.shape[2] // 2
        lower_half = reduced[:, :, :half_cols]
        upper_half = reduced[:, :, half_cols:]
        upper_side = position >> level & 1 == 1
        kept_half = jnp.where(upper_side, upper_half, lower_half)
        sent_half = jnp.where(upper_side, lower_half, upper_half)
        reduced = kept_half + partner(sent_half, "tensor", level)
    classes = segment_adapter_class[0]
    class_indicator = (
        classes[:, :, None] == jnp.arange(up_matrix_tile.shape[0], dtype=jnp.int32)[None, None, :]
    ).astype(jnp.bfloat16)
    selected_up_matrix = choose_segment_rows(class_indicator, up_matrix_tile)
    grad_segs = gathered.reshape(micro_count, seg_count, SEG, tile_cols)
    partial_rank = jnp.einsum(
        "mskd,msrd->mskr", grad_segs, selected_up_matrix, preferred_element_type=jnp.float32
    )
    padded_rank = jnp.zeros((micro_count, seg_count, SEG, rank_extent), jnp.float32)
    padded_rank = lax.dynamic_update_slice_in_dim(
        padded_rank, partial_rank, high_index * rank_part, 3
    )
    lowrank = lax.psum(padded_rank, "tensor").astype(jnp.bfloat16)
    selected_down_matrix = choose_segment_rows(class_indicator, adapter_down_maps[0])
    adapter = jnp.einsum(
        "mskr,msrd->mskd", lowrank, selected_down_matrix, preferred_element_type=jnp.float32
    )
    input_gradient = (reduced + adapter.reshape(micro_count, batch_rows, local_portion)).astype(
        jnp.bfloat16
    )
    grad_prev = shifted(input_gradient, "pipe", -1)
    inputs_seg = forward_input[0].reshape(micro_count, seg_count, SEG, local_portion)
    segment_down_matrix = jnp.einsum(
        "mskr,mskd->msrd", lowrank, inputs_seg, preferred_element_type=jnp.float32
    )
    hidden = lax.all_gather(saved_rank_outputs[0], "tensor", axis=1, tiled=True)
    hidden_part = lax.dynamic_slice_in_dim(hidden, high_index * rank_part, rank_part, 2)
    hidden_seg = hidden_part.reshape(micro_count, seg_count, SEG, rank_part)
    segment_up_matrix = jnp.einsum(
        "mskr,mskd->msrd", hidden_seg, grad_segs, preferred_element_type=jnp.float32
    )
    wide_class_indicator = class_indicator.astype(jnp.float32)
    down_map_gradient = jnp.einsum(
        "exk,exlq->klq", wide_class_indicator, segment_down_matrix, precision=lax.Precision.HIGHEST
    ).astype(jnp.bfloat16)
    up_map_gradient = jnp.einsum(
        "exk,exlq->klq", wide_class_indicator, segment_up_matrix, precision=lax.Precision.HIGHEST
    ).astype(jnp.bfloat16)
    return (grad_prev[None], down_map_gradient[None], up_map_gradient[None, None])


def solution(mesh):
    in_specs = (
        P("pipe", "tensor", None, None, None),
        P("pipe", None, None, "tensor"),
        P("pipe", None, "tensor", None),
        P("pipe", "tensor", None, None),
        P("pipe", None, None, "tensor"),
        P("pipe", "tensor", None, None, None),
        P("pipe", None, None),
        P("pipe", None),
    )
    out_specs = (
        P("pipe", None, None, "tensor"),
        P("pipe", None, None, "tensor"),
        P("pipe", "tensor", None, None, None),
    )
    return jax.shard_map(shards, mesh=mesh, in_specs=in_specs, out_specs=out_specs, check_vma=False)
```

profile of v0, /device:TPU:0, one launch (start us, length us, event | category | flops | bytes accessed | tf_op | source)
XLA Modules:
  0.0 544.3 jit_solution(13468567775985908077)
XLA Ops:
  0.6 0.0 copy-start
  0.7 0.8 broadcast_compare_fusion
  1.5 1.4 bitcast_select_fusion
  2.9 0.0 copy-start.3
  2.9 4.1 collective-permute-start
  7.0 7.3 %fusion.2 = f32[2,256,4096]{2,1,0:T(8,128)S(1)} fusion(bf16[1,1,4096,1024]{3,2,1,0:T(8,128)(2,1)} %param.11, bf16[1,1,2,256,1024]{4,3,2,1,0:T(8,128)(2,1)} %param.8, pred[2,256]{1,0:T(4,128)(4,1)S(1)} %broadcast_compare_fusion), kind=kOutput, calls=%fused_computation.3 | convolution fusion | flops 4295491584 | bytes 17826304 | tf_op jit(solution)/shard_map/mrd,id->mri/dot_general | solution.py:59
  14.3 0.0 copy-done.3
  14.3 38.3 %collective-permute-done = bf16[2,256,1024]{2,1,0:T(8,128)(2,1)S(1)} collective-permute-done((bf16[2,256,1024]{2,1,0:T(8,128)(2,1)S(1)}, bf16[2,256,1024]{2,1,0:T(8,128)(2,1)S(1)}, u32[]{:S(2)}, u32[]{:S(2)}) %collective-permute-start) | collective-permute-done | bytes 1048608 | tf_op jit(solution)/shard_map/ppermute | solution.py:12
  52.6 0.0 copy-start.4
  52.6 7.3 %fusion = f32[2,256,4096]{2,1,0:T(8,128)S(1)} fusion(bf16[2,256,1024]{2,1,0:T(8,128)(2,1)S(1)} %collective-permute-done, bf16[1,1,4096,1024]{3,2,1,0:T(8,128)(2,1)} %param.11), kind=kOutput, calls=%fused_computation.1 | convolution fusion | flops 4294967296 | bytes 17825792 | tf_op jit(solution)/shard_map/mrd,id->mri/dot_general | solution.py:59
  60.0 0.0 copy-done.4
  60.0 6.8 %maximum_select_fusion = f32[2,512,4096]{2,1,0:T(8,128)} fusion(f32[2,256,4096]{2,1,0:T(8,128)S(1)} %fusion, f32[2,256,4096]{2,1,0:T(8,128)S(1)} %fusion.2, pred[]{:T(512)S(6)} %eq.31), kind=kLoop, calls=%fused_computation | loop fusion | flops 12582912 | bytes 33554432 | tf_op jit(solution)/shard_map/jit(_where)/select_n | solution.py:63
  66.8 11.7 %slice_select_fusion = f32[2,512,2048]{2,1,0:T(8,128)} fusion(f32[2,512,4096]{2,1,0:T(8,128)} %maximum_select_fusion, pred[]{:T(512)S(6)} %eq.30), kind=kLoop, calls=%fused_computation.6 | loop fusion | flops 2097152 | bytes 25165824 | tf_op jit(solution)/shard_map/jit(_where)/select_n | solution.py:82
  78.5 0.7 collective-permute-start.1
  79.2 181.2 %collective-permute-done.1 = f32[2,512,2048]{2,1,0:T(8,128)} collective-permute-done((f32[2,512,2048]{2,1,0:T(8,128)}, f32[2,512,2048]{2,1,0:T(8,128)}, u32[]{:S(2)}, u32[]{:S(2)}) %collective-permute-start.1) | collective-permute-done | bytes 8388640 | tf_op jit(solution)/shard_map/ppermute | solution.py:12
  260.4 9.8 %select_add_fusion = f32[2,512,2048]{2,1,0:T(8,128)S(1)} fusion(f32[2,512,2048]{2,1,0:T(8,128)} %collective-permute-done.1, f32[2,512,4096]{2,1,0:T(8,128)} %maximum_select_fusion, pred[]{:T(512)S(6)} %eq.30), kind=kLoop, calls=%fused_computation.5 | loop fusion | flops 4194304 | bytes 33554432 | tf_op jit(solution)/shard_map/add | solution.py:83
  270.2 0.0 copy-start.1
  270.2 3.3 slice_select_fusion.1
  273.5 1.1 copy-done.1
  274.7 1.3 collective-permute-start.2
  276.0 89.9 %collective-permute-done.2 = f32[2,512,1024]{2,1,0:T(8,128)} collective-permute-done((f32[2,512,1024]{2,1,0:T(8,128)}, f32[2,512,1024]{2,1,0:T(8,128)}, u32[]{:S(2)}, u32[]{:S(2)}) %collective-permute-start.2) | collective-permute-done | bytes 4194336 | tf_op jit(solution)/shard_map/ppermute | solution.py:12
  365.8 6.1 %select_add_fusion.1 = f32[2,512,1024]{2,1,0:T(8,128)S(1)} fusion(f32[2,512,1024]{2,1,0:T(8,128)} %collective-permute-done.2, f32[2,512,2048]{2,1,0:T(8,128)} %copy-done.1, pred[]{:T(512)S(6)} %eq.29), kind=kLoop, calls=%fused_computation.7 | loop fusion | flops 2097152 | bytes 16777216 | tf_op jit(solution)/shard_map/add | solution.py:83
  372.0 0.0 copy-start.2
  372.0 1.9 copy-done.2
  373.9 0.0 copy-start.5
  373.9 0.0 copy-start.8
  373.9 0.0 copy-start.6
  374.0 1.8 slice_select_fusion.2
  375.8 1.3 collective-permute-start.3
  377.0 0.0 copy-done.5
  377.1 0.0 copy-done.8
  377.1 0.5 fusion.17
  377.5 0.0 copy-done.6
  377.5 1.3 fusion.15
  378.8 3.4 maximum_select_fusion.1
  382.2 0.8 convolution_dynamic-update-slice_fusion
  383.0 111.8 %all-reduce.1 = bf16[2,4,128,64]{2,3,1,0:T(8,128)(2,1)S(1)} all-reduce(f32[2,4,128,64]{2,3,1,0:T(8,128)S(1)} %convolution_dynamic-update-slice_fusion), channel_id=1, replica_groups=mesh['pipe'=2,'tensor'=16] {'tensor'}, use_global_device_ids=true, to_apply=%region_0.1 | all-reduce | flops 65536 | bytes 393216 | tf_op jit(solution)/shard_map/psum | solution.py:97
  494.8 1.5 fusion.14
  496.4 0.0 copy-start.7
  496.4 0.0 collective-permute-done.3
  496.4 3.7 fusion.4
  500.1 0.1 collective-permute-start.4
  500.2 0.0 copy-done.7
  500.2 36.9 %all-gather = bf16[1,2,512,64]{3,2,1,0:T(8,128)(2,1)S(1)} all-gather(bf16[1,2,32,64]{3,2,1,0:T(8,128)(2,1)S(1)} %copy-done.7), channel_id=2, replica_groups=mesh['pipe'=2,'tensor'=16] {'tensor'}, dimensions={2}, use_global_device_ids=true | all-gather | bytes 139264 | tf_op jit(solution)/shard_map/all_gather | solution.py:110
  537.1 0.1 constant_dynamic-slice_fusion
  537.2 0.0 copy-done
  537.2 0.3 fusion.35
  537.5 1.7 fusion.8
  539.2 0.9 copy.11
  540.1 0.4 fusion.34
  540.6 1.7 fusion.7
  542.3 1.1 copy.12
  543.4 0.0 collective-permute-done.4
  543.4 1.0 copy.38
  (2 shorter events, 0.0 us)
Async XLA Ops:
  0.6 536.6 %copy-start = (bf16[1,2,512,512]{3,2,1,0:T(8,128)(2,1)S(1)}, bf16[1,2,512,512]{3,2,1,0:T(8,128)(2,1)}, u32[]{:S(2)}) copy-start(bf16[1,2,512,512]{3,2,1,0:T(8,128)(2,1)} %param.9) | copy-start | bytes 3145732
  2.9 11.4 %copy-start.3 = (bf16[2,256,1024]{2,1,0:T(8,128)(2,1)}, bf16[2,256,1024]{2,1,0:T(8,128)(2,1)S(1)}, u32[]{:S(2)}) copy-start(bf16[2,256,1024]{2,1,0:T(8,128)(2,1)S(1)} %bitcast_select_fusion) | copy-start | bytes 3145732
  2.9 49.7 %collective-permute-start = (bf16[2,256,1024]{2,1,0:T(8,128)(2,1)S(1)}, bf16[2,256,1024]{2,1,0:T(8,128)(2,1)S(1)}, u32[]{:S(2)}, u32[]{:S(2)}) collective-permute-start(bf16[2,256,1024]{2,1,0:T(8,128)(2,1)S(1)} %bitcast_select_fusion), channel_id=1, source_target_pairs={{0,8},{1,9},{2,10},{3,11},{4,12},{5,13},{6,14},{7,15},{8,0},{9,1},... | collective-permute-start | bytes 3145736 | tf_op jit(solution)/shard_map/ppermute | solution.py:12
  52.6 7.4 %copy-start.4 = (bf16[2,256,1024]{2,1,0:T(8,128)(2,1)}, bf16[2,256,1024]{2,1,0:T(8,128)(2,1)S(1)}, u32[]{:S(2)}) copy-start(bf16[2,256,1024]{2,1,0:T(8,128)(2,1)S(1)} %collective-permute-done) | copy-start | bytes 3145732
  78.5 182.0 %collective-permute-start.1 = (f32[2,512,2048]{2,1,0:T(8,128)}, f32[2,512,2048]{2,1,0:T(8,128)}, u32[]{:S(2)}, u32[]{:S(2)}) collective-permute-start(f32[2,512,2048]{2,1,0:T(8,128)} %slice_select_fusion), channel_id=1, source_target_pairs={{0,4},{1,5},{2,6},{3,7},{4,0},{5,1},{6,2},{7,3},{8,12},{9,13},{10,... | collective-permute-start | bytes 25165832 | tf_op jit(solution)/shard_map/ppermute | solution.py:12
  270.2 4.5 copy-start.1
  274.7 91.2 %collective-permute-start.2 = (f32[2,512,1024]{2,1,0:T(8,128)}, f32[2,512,1024]{2,1,0:T(8,128)}, u32[]{:S(2)}, u32[]{:S(2)}) collective-permute-start(f32[2,512,1024]{2,1,0:T(8,128)} %slice_select_fusion.1), channel_id=1, source_target_pairs={{0,2},{1,3},{2,0},{3,1},{4,6},{5,7},{6,4},{7,5},{8,10},{9,11},{10,... | collective-permute-start | bytes 12582920 | tf_op jit(solution)/shard_map/ppermute | solution.py:12
  372.0 2.0 copy-start.2
  373.9 3.1 copy-start.5
  373.9 3.1 copy-start.8
  373.9 3.6 copy-start.6
  375.8 120.6 %collective-permute-start.3 = (f32[2,512,512]{2,1,0:T(8,128)}, f32[2,512,512]{2,1,0:T(8,128)}, u32[]{:S(2)}, u32[]{:S(2)}) collective-permute-start(f32[2,512,512]{2,1,0:T(8,128)} %slice_select_fusion.2), channel_id=1, source_target_pairs={{0,1},{1,0},{2,3},{3,2},{4,5},{5,4},{6,7},{7,6},{8,9},{9,8},{10,11... | collective-permute-start | bytes 6291464 | tf_op jit(solution)/shard_map/ppermute | solution.py:12
  496.4 3.9 copy-start.7
  500.1 43.2 %collective-permute-start.4 = (bf16[2,512,512]{2,1,0:T(8,128)(2,1)S(1)}, bf16[2,512,512]{2,1,0:T(8,128)(2,1)S(1)}, u32[]{:S(2)}, u32[]{:S(2)}) collective-permute-start(bf16[2,512,512]{2,1,0:T(8,128)(2,1)S(1)} %fusion.4), channel_id=1, source_target_pairs={{16,0},{0,16},{17,1},{1,17},{18,2},{2,18},{19,3},{3,19},{20,4},{4,... | collective-permute-start | bytes 3145736 | tf_op jit(solution)/shard_map/ppermute | solution.py:18
where the time goes:
time: 545 us; the launch traced here: 544 us
  waiting for transfers between devices  309 us (57%)
  blocking collectives  149 us (27%)
  other arithmetic  48.9 us (9%)
  matrix products  22.8 us (4%)
  starting transfers between devices  7.44 us (1%)
  local copies, waits for them, and re-layouts  6.29 us (1%)
    ppermute x4, waiting for transfers between devices, partner(): return lax.ppermute(value, axis, pairs)  309 us
    psum x1, blocking collectives, shards(): lowrank = lax.psum(padded_rank, 'tensor').astype(jnp.bfloat16)  112 us
    all_gather x1, blocking collectives, shards(): hidden = lax.all_gather(saved_rank_outputs[0], 'tensor', axis=1, tiled=True)  36.9 us
    select_n x3, other arithmetic, shards(): sent_half = jnp.where(upper_side, lower_half, upper_half)  16.8 us
    add x2, other arithmetic, shards(): reduced = kept_half + partner(sent_half, 'tensor', level)  15.9 us
    dot_general x2, matrix products, project(): jnp.einsum('mrd,id->mri', rows_block, weight, preferred_element_type=jnp....  14.6 us
  transfers between devices with their start and end apart: 5, of which 3 were waited for; matrix products, arithmetic and copies ran while one was open for 4% of the time, Pallas kernels for 0%

commit v1 on v0

v1 whole, which is shorter than its diff:
```python
import jax
import jax.numpy as jnp
from jax import lax
from jax.experimental import pallas as pl
from jax.experimental.pallas import tpu as pltpu
from jax.sharding import PartitionSpec as P

SEG = 128
BF16 = jnp.bfloat16
F32 = jnp.float32


def partner(value, mask):
    pairs = [(source, source ^ mask) for source in range(lax.axis_size("tensor"))]
    return lax.ppermute(value, "tensor", pairs)


def relay(value, mask):
    sections, tiles = lax.axis_size("pipe"), lax.axis_size("tensor")
    pairs = [
        (p * tiles + t, (p - 1) % sections * tiles + (t ^ mask))
        for p in range(sections)
        for t in range(tiles)
    ]
    return lax.ppermute(value, ("pipe", "tensor"), pairs)


def product_body(table_ref, limit_ref, rows_ref, weight_ref, out_ref):
    value = lax.dot_general(
        rows_ref[...], weight_ref[0], (((1,), (1,)), ((), ())), preferred_element_type=F32
    )
    row = lax.broadcasted_iota(jnp.int32, value.shape, 0)
    out_ref[0] = jnp.where(row < limit_ref[0], value, 0.0).astype(out_ref.dtype)


def product(rows, weight_blocks, table, limit, dtype):
    count, depth = rows.shape
    _, width, _ = weight_blocks.shape
    blocks = table.shape[0]
    return pl.pallas_call(
        product_body,
        grid_spec=pltpu.PrefetchScalarGridSpec(
            num_scalar_prefetch=2,
            grid=(blocks,),
            in_specs=[
                pl.BlockSpec((count, depth), lambda k, table, limit: (0, 0)),
                pl.BlockSpec((1, width, depth), lambda k, table, limit: (table[k], 0, 0)),
            ],
            out_specs=pl.BlockSpec((1, count, width), lambda k, table, limit: (k, 0, 0)),
        ),
        out_shape=jax.ShapeDtypeStruct((blocks, count, width), dtype),
        compiler_params=pltpu.CompilerParams(vmem_limit_bytes=24 * 2**20),
        cost_estimate=pl.CostEstimate(
            flops=2 * blocks * count * width * depth,
            bytes_accessed=2 * (blocks * width * depth + count * depth + blocks * count * width),
            transcendentals=0,
        ),
    )(table, limit, rows, weight_blocks)


def unrelate(parts, own):
    bits = len(parts).bit_length() - 1
    for bit in range(bits):
        swap = (own >> bit) & 1 == 1
        parts = [jnp.where(swap, parts[k ^ (1 << bit)], parts[k]) for k in range(len(parts))]
    return parts


def shards(
    output_gradient,
    forward_input,
    saved_rank_outputs,
    projection_weight,
    adapter_down_maps,
    adapter_up_maps,
    segment_adapter_class,
    live_segment_table,
):
    grad_tile = output_gradient[0, 0]
    micro_count, tile_rows, tile_cols = grad_tile.shape
    up_tile = adapter_up_maps[0, 0]
    class_count, rank_part, _ = up_tile.shape
    down = adapter_down_maps[0]
    rank = down.shape[1]
    portion = down.shape[2]
    tiles = lax.axis_size("tensor")
    low_size = min(tiles, 8)
    low_bits = low_size.bit_length() - 1
    high_size = tiles // low_size
    position = lax.axis_index("tensor")
    low = position % low_size
    high = position // low_size
    batch_rows = tile_rows * high_size
    weight_blocks = projection_weight[0, 0].reshape(low_size, portion, tile_cols)
    classes = segment_adapter_class[0]
    live_count = live_segment_table[0]

    grads = [[grad_tile[m] for m in range(micro_count)]]
    for k in range(1, high_size):
        grads.append([partner(grad_tile[m], k * low_size) for m in range(micro_count)])

    def row_classes(block):
        segs = (block * tile_rows + jnp.arange(tile_rows, dtype=jnp.int32)) // SEG
        chosen = jnp.zeros((micro_count, tile_rows), jnp.int32)
        for s in range(classes.shape[1]):
            chosen = jnp.where(segs[None, :] == s, classes[:, s : s + 1], chosen)
        alive = segs[None, :] < live_count[:, None]
        chosen = jnp.where(alive, chosen, -1).reshape(1, micro_count * tile_rows)
        return chosen == jnp.arange(class_count, dtype=jnp.int32)[:, None]

    indicator = [row_classes(high ^ k) for k in range(high_size)]

    def order_of(m):
        bits = list(range(low_bits))
        if m % 2 == 1 and low_bits > 1:
            bits[0], bits[1] = bits[1], bits[0]
        return bits

    def relative_blocks(bits, first):
        blocks = [first]
        for bit in reversed(bits):
            blocks = blocks + [b | 1 << bit for b in blocks]
        return jnp.array(blocks, jnp.int32) ^ low

    def base_sum(k, m):
        bits = order_of(m)
        limit = jnp.clip(live_count[m] * SEG - (high ^ k) * tile_rows, 0, tile_rows)[None]
        rows = grads[k][m]
        sent = product(rows, weight_blocks, relative_blocks(bits[1:], 1 << bits[0]), limit, BF16)
        got = partner(sent, 1 << bits[0])
        total = product(rows, weight_blocks, relative_blocks(bits[1:], 0), limit, F32)
        for bit in bits[1:]:
            total = total + got
            half = total.shape[0] // 2
            got = total[half:].astype(BF16)
            total = total[:half]
            if bit == bits[-1]:
                return total[0], relay(got[0], 1 << bit)
            got = partner(got, 1 << bit)

    up_flat = up_tile.reshape(class_count * rank_part, tile_cols)
    own_rank = []
    for k in range(high_size):
        rows = jnp.concatenate(grads[k], 0)
        every = lax.dot_general(
            up_flat, rows, (((1,), (1,)), ((), ())), preferred_element_type=F32
        ).reshape(class_count, rank_part, micro_count * tile_rows)
        part = jnp.sum(jnp.where(indicator[k][:, None, :], every, 0.0), 0)
        for bit in range(low_bits):
            part = part + partner(part, 1 << bit)
        own_rank.append(part.astype(BF16))

    sums = [[base_sum(k, m) for m in range(micro_count)] for k in range(high_size)]

    ranks = [own_rank]
    for j in range(1, high_size):
        got = partner(jnp.stack(own_rank), j * low_size)
        ranks.append([got[k ^ j] for k in range(high_size)])
    by_rank = [
        jnp.concatenate(unrelate([ranks[j][k] for j in range(high_size)], high), 0)
        for k in range(high_size)
    ]
    spread = [
        jnp.where(indicator[k][:, None, :], by_rank[k][None], jnp.zeros((), BF16)).reshape(
            class_count * rank, micro_count * tile_rows
        )
        for k in range(high_size)
    ]

    down_flat = down.reshape(class_count * rank, portion)
    finished = []
    for k in range(high_size):
        adapter = lax.dot_general(
            spread[k], down_flat, (((0,), (0,)), ((), ())), preferred_element_type=F32
        ).reshape(micro_count, tile_rows, portion)
        done = []
        for m in range(micro_count):
            own_sum, got = sums[k][m]
            kept = relay((own_sum + adapter[m]).astype(BF16), 0)
            done.append((kept.astype(F32) + got.astype(F32)).astype(BF16))
        finished.append(jnp.stack(done))
    grad_prev = jnp.concatenate(unrelate(finished, high), 1)

    inputs = forward_input[0].reshape(micro_count, high_size, tile_rows, portion)
    spread_rows = jnp.stack(
        unrelate(
            [s.reshape(class_count * rank, micro_count, tile_rows) for s in spread], high
        ),
        2,
    )
    down_map_gradient = lax.dot_general(
        spread_rows.reshape(class_count * rank, -1),
        inputs.reshape(-1, portion),
        (((1,), (0,)), ((), ())),
        preferred_element_type=F32,
    ).astype(BF16)

    hidden = saved_rank_outputs[0]
    for bit in range(low_bits):
        got = partner(hidden, 1 << bit)
        upper = (position >> bit) & 1 == 1
        hidden = jnp.where(
            upper, jnp.concatenate([got, hidden], 1), jnp.concatenate([hidden, got], 1)
        )
    up_total = 0.0
    for k in range(high_size):
        rank_start = (high ^ k) * rank_part
        wanted = lax.dynamic_slice_in_dim(hidden, rank_start, rank_part, 2)
        if k > 0:
            wanted = partner(wanted, k * low_size)
        wanted = wanted.reshape(micro_count * tile_rows, rank_part).T
        wide = jnp.where(indicator[k][:, None, :], wanted[None], jnp.zeros((), BF16))
        up_total = up_total + lax.dot_general(
            wide.reshape(class_count * rank_part, -1),
            jnp.concatenate(grads[k], 0),
            (((1,), (0,)), ((), ())),
            preferred_element_type=F32,
        )
    up_map_gradient = up_total.astype(BF16)
    return (
        grad_prev[None],
        down_map_gradient.reshape(1, class_count, rank, portion),
        up_map_gradient.reshape(1, 1, class_count, rank_part, tile_cols),
    )


def solution(mesh):
    in_specs = (
        P("pipe", "tensor", None, None, None),
        P("pipe", None, None, "tensor"),
        P("pipe", None, "tensor", None),
        P("pipe", "tensor", None, None),
        P("pipe", None, None, "tensor"),
        P("pipe", "tensor", None, None, None),
        P("pipe", None, None),
        P("pipe", None),
    )
    out_specs = (
        P("pipe", None, None, "tensor"),
        P("pipe", None, None, "tensor"),
        P("pipe", "tensor", None, None, None),
    )
    return jax.shard_map(shards, mesh=mesh, in_specs=in_specs, out_specs=out_specs, check_vma=False)
```

time: 545 us -> 192 us (0.35)
  waiting for transfers between devices: 309 us -> 64.9 us
  blocking collectives: 149 us -> 0 us
  other arithmetic: 48.9 us -> 14.3 us
  Pallas kernels: 0 us -> 32.1 us
  starting transfers between devices: 7.44 us -> 33.2 us
  local copies, waits for them, and re-layouts: 6.29 us -> 31.9 us
  matrix products: 22.8 us -> 11.9 us
    ppermute x5 -> x29, waiting for transfers between devices: 309 us -> 64.9 us  [the longest x21 57.1 us: partner(): return lax.ppermute(value, 'tensor', pairs)]
    psum x1 -> x0, blocking collectives: 112 us -> none  [shards(): lowrank = lax.psum(padded_rank, 'tensor').astype(jnp.bfloat16)]
    all_gather x1 -> x0, blocking collectives: 36.9 us -> none  [shards(): hidden = lax.all_gather(saved_rank_outputs[0], 'tensor', axis=1, tiled=True)]
    pallas_call x0 -> x8, Pallas kernels: none -> 32.1 us  [product(): pl.pallas_call(product_body, grid_spec=pltpu.PrefetchScalarGridSpec(num_s...]
    select_n x7 -> x10, other arithmetic: 28.4 us -> 1.67 us  [the longest x3 1.52 us: unrelate(): jnp.where(swap, parts[k ^ 1 << bit], parts[k])]
    ppermute x5 -> x29, starting transfers between devices: 7.44 us -> 33.2 us  [the longest x21 28.8 us: partner(): return lax.ppermute(value, 'tensor', pairs)]
    unnamed x21 -> x59, local copies, waits for them, and re-layouts: 6.14 us -> 18.7 us
    dot_general x10 -> x7, matrix products: 22.8 us -> 11.9 us  [the longest x2 3.85 us: shards(): lax.dot_general(wide.reshape(class_count * rank_part, -1), jnp.concatenat...]
  transfers between devices with their start and end apart: 5 -> 29, of which waited for: 3 -> 9; matrix products, arithmetic and copies ran while one was open for 4% -> 21% of each run, Pallas kernels for 0% -> 17%
where the time goes in v1:
time: 192 us; the launch traced here: 191 us
  waiting for transfers between devices  64.9 us (34%)
  starting transfers between devices  33.2 us (17%)
  Pallas kernels  32.1 us (17%)
  local copies, waits for them, and re-layouts  31.9 us (17%)
  other arithmetic  14.3 us (7%)
  matrix products  11.9 us (6%)
  between operations  2.68 us (1%)
    ppermute x21, waiting for transfers between devices, partner(): return lax.ppermute(value, 'tensor', pairs)  57.1 us
    pallas_call x8, Pallas kernels, product(): pl.pallas_call(product_body, grid_spec=pltpu.PrefetchScalarGridSpec(num_s...  32.1 us
    ppermute x21, starting transfers between devices, partner(): return lax.ppermute(value, 'tensor', pairs)  28.8 us
    unnamed x59, local copies, waits for them, and re-layouts  18.7 us
    ppermute x8, waiting for transfers between devices, relay(): return lax.ppermute(value, ('pipe', 'tensor'), pairs)  7.87 us
    add x8, other arithmetic, base_sum(): total = total + got  7.06 us
    ppermute x8, starting transfers between devices, relay(): return lax.ppermute(value, ('pipe', 'tensor'), pairs)  4.37 us
    select_n x2, local copies, waits for them, and re-layouts, unrelate(): jnp.where(swap, parts[k ^ 1 << bit], parts[k])  3.92 us
  transfers between devices with their start and end apart: 29, of which 9 were waited for; matrix products, arithmetic and copies ran while one was open for 21% of the time, Pallas kernels for 17%

profile of v1, /device:TPU:0, one launch (start us, length us, event | category | flops | bytes accessed | tf_op | source)
XLA Modules:
  0.0 191.0 jit_solution(2718134600234237293)
XLA Ops:
  0.7 3.0 %collective-permute-start.25 = (bf16[2,32,64]{2,1,0:T(8,128)(2,1)}, bf16[2,32,64]{2,1,0:T(8,128)(2,1)S(1)}, u32[]{:S(2)}, u32[]{:S(2)}) collective-permute-start(bf16[2,32,64]{2,1,0:T(8,128)(2,1)} %bitcast.130), channel_id=1, source_target_pairs={{0,1},{1,0},{2,3},{3,2},{4,5},{5,4},{6,7},{7,6},{8,9},{9,8},{10,11... | collective-permute-start | bytes 24584 | tf_op jit(solution)/shard_map/ppermute | solution.py:15
  3.7 2.2 %slice_bitcast_fusion.5 = (bf16[256,1024]{1,0:T(8,128)(2,1)}, bf16[256,1024]{1,0:T(8,128)(2,1)}) fusion(bf16[1,1,2,256,1024]{4,3,2,1,0:T(8,128)(2,1)} %param.16), kind=kLoop, calls=%fused_computation.45 | loop fusion | bytes 2097152 | tf_op jit(solution)/shard_map/squeeze | solution.py:100
  5.9 2.6 %collective-permute-start = (bf16[256,1024]{1,0:T(8,128)(2,1)}, bf16[256,1024]{1,0:T(8,128)(2,1)}, u32[]{:S(2)}, u32[]{:S(2)}) collective-permute-start(bf16[256,1024]{1,0:T(8,128)(2,1)} %get-tuple-element.13.rows_ref), channel_id=1, source_target_pairs={{0,8},{1,9},{2,10},{3,11},{4,12},{5,13},{6,14},{7,15},{8,0},{9,1},... | collective-permute-start | bytes 1572872 | tf_op jit(solution)/shard_map/ppermute | solution.py:15
  9.3 1.7 fusion.2
  11.3 0.7 fusion.19
  12.7 3.4 %copy-done.1 = bf16[1,1,4096,1024]{3,2,1,0:T(8,128)(2,1)S(1)} copy-done((bf16[1,1,4096,1024]{3,2,1,0:T(8,128)(2,1)S(1)}, bf16[1,1,4096,1024]{3,2,1,0:T(8,128)(2,1)}, u32[]{:S(2)}) %copy-start.1) | copy-done | bytes 8388632
  16.1 4.4 %shard_map.180 = bf16[4,256,512]{2,1,0:T(8,128)(2,1)} custom-call(s32[4]{0:T(128)S(1)} %broadcast_xor_fusion.2.table_ref, s32[1]{0:T(128)} %bitcast.25.limit_ref, bf16[256,1024]{1,0:T(8,128)(2,1)} %get-tuple-element.13.rows_ref, bf16[8,512,1024]{2,1,0:T(8,128)(2,1)S(1)} %bitcast.102), custom_call_target="tpu_custom_call" | custom-call | flops 1073741824 | bytes 5767168 | tf_op jit(solution)/shard_map/pallas_call | solution.py:40
  20.5 1.8 collective-permute-start.17
  22.4 3.5 %shard_map.179 = f32[4,256,512]{2,1,0:T(8,128)S(1)} custom-call(s32[4]{0:T(128)S(1)} %broadcast_xor_fusion.3.table_ref, s32[1]{0:T(128)} %bitcast.25.limit_ref, bf16[256,1024]{1,0:T(8,128)(2,1)} %get-tuple-element.13.rows_ref, bf16[8,512,1024]{2,1,0:T(8,128)(2,1)S(1)} %bitcast.103), custom_call_target="tpu_custom_call" | custom-call | flops 1073741824 | bytes 5767168 | tf_op jit(solution)/shard_map/pallas_call | solution.py:40
  26.6 1.6 collective-permute-start.26
  28.2 3.4 %copy-done.2 = bf16[1,1,4096,1024]{3,2,1,0:T(8,128)(2,1)S(1)} copy-done((bf16[1,1,4096,1024]{3,2,1,0:T(8,128)(2,1)S(1)}, bf16[1,1,4096,1024]{3,2,1,0:T(8,128)(2,1)}, u32[]{:S(2)}) %copy-start.2) | copy-done | bytes 8388632
  31.6 4.4 %shard_map.182 = bf16[4,256,512]{2,1,0:T(8,128)(2,1)} custom-call(s32[4]{0:T(128)S(1)} %broadcast_xor_fusion.table_ref, s32[1]{0:T(128)} %bitcast.31.limit_ref, bf16[256,1024]{1,0:T(8,128)(2,1)} %get-tuple-element.14.rows_ref, bf16[8,512,1024]{2,1,0:T(8,128)(2,1)S(1)} %bitcast.104), custom_call_target="tpu_custom_call" | custom-call | flops 1073741824 | bytes 5767168 | tf_op jit(solution)/shard_map/pallas_call | solution.py:40
  36.1 1.6 collective-permute-start.27
  37.7 3.4 %copy-done.3 = bf16[1,1,4096,1024]{3,2,1,0:T(8,128)(2,1)S(1)} copy-done((bf16[1,1,4096,1024]{3,2,1,0:T(8,128)(2,1)S(1)}, bf16[1,1,4096,1024]{3,2,1,0:T(8,128)(2,1)}, u32[]{:S(2)}) %copy-start.3) | copy-done | bytes 8388632
  41.1 3.5 %shard_map.181 = f32[4,256,512]{2,1,0:T(8,128)S(1)} custom-call(s32[4]{0:T(128)S(1)} %broadcast_xor_fusion.1.table_ref, s32[1]{0:T(128)} %bitcast.31.limit_ref, bf16[256,1024]{1,0:T(8,128)(2,1)} %get-tuple-element.14.rows_ref, bf16[8,512,1024]{2,1,0:T(8,128)(2,1)S(1)} %bitcast.105), custom_call_target="tpu_custom_call" | custom-call | flops 1073741824 | bytes 5767168 | tf_op jit(solution)/shard_map/pallas_call | solution.py:40
  44.7 1.3 copy-done.5
  46.0 9.5 %collective-permute-done.27 = bf16[2,128,64]{2,1,0:T(8,128)(2,1)S(1)} collective-permute-done((bf16[2,128,64]{2,1,0:T(8,128)(2,1)S(1)}, bf16[2,128,64]{2,1,0:T(8,128)(2,1)S(1)}, u32[]{:S(2)}, u32[]{:S(2)}) %collective-permute-start.27) | collective-permute-done | bytes 32800 | tf_op jit(solution)/shard_map/ppermute | solution.py:15
  55.6 0.8 constant_dynamic-slice_fusion
  56.4 1.6 collective-permute-start.28
  58.1 0.9 add.165
  59.0 1.6 collective-permute-start.4
  60.6 2.6 %fusion.1 = f32[256,1024]{1,0:T(8,128)} fusion(bf16[256,512]{1,0:T(8,128)(2,1)S(1)} %bitcast.126, bf16[256,1024]{1,0:T(8,128)(2,1)} %get-tuple-element.14.rows_ref, bf16[256,1024]{1,0:T(8,128)(2,1)} %get-tuple-element.13.rows_ref), kind=kOutput, calls=%fused_computation.18 | convolution fusion | flops 270532608 | bytes 2359296 | tf_op jit(solution)/shard_map/dot_general | solution.py:213
  63.2 2.7 %collective-permute-done.28 = bf16[2,256,32]{2,1,0:T(8,128)(2,1)S(1)} collective-permute-done((bf16[2,256,32]{2,1,0:T(8,128)(2,1)}, bf16[2,256,32]{2,1,0:T(8,128)(2,1)S(1)}, u32[]{:S(2)}, u32[]{:S(2)}) %collective-permute-start.28) | collective-permute-done | bytes 32800 | tf_op jit(solution)/shard_map/ppermute | solution.py:15
  65.8 1.5 collective-permute-start.21
  67.6 4.2 %collective-permute-done.5 = f32[32,512]{1,0:T(8,128)S(1)} collective-permute-done((f32[32,512]{1,0:T(8,128)S(1)}, f32[32,512]{1,0:T(8,128)S(1)}, u32[]{:S(2)}, u32[]{:S(2)}) %collective-permute-start.5) | collective-permute-done | bytes 65568 | tf_op jit(solution)/shard_map/ppermute | solution.py:15
  71.8 1.1 constant_dynamic-update-slice_fusion.1
  72.9 1.1 constant_dynamic-update-slice_fusion
  74.6 0.6 collective-permute-start.7
  75.2 3.4 %copy-done.4 = bf16[1,1,4096,1024]{3,2,1,0:T(8,128)(2,1)S(1)} copy-done((bf16[1,1,4096,1024]{3,2,1,0:T(8,128)(2,1)S(1)}, bf16[1,1,4096,1024]{3,2,1,0:T(8,128)(2,1)}, u32[]{:S(2)}) %copy-start.4) | copy-done | bytes 8388632
  78.6 4.4 %shard_map.176 = bf16[4,256,512]{2,1,0:T(8,128)(2,1)} custom-call(s32[4]{0:T(128)S(1)} %broadcast_xor_fusion.2.table_ref, s32[1]{0:T(128)} %bitcast.1.limit_ref, bf16[256,1024]{1,0:T(8,128)(2,1)} %collective-permute-done.rows_ref, bf16[8,512,1024]{2,1,0:T(8,128)(2,1)S(1)} %bitcast.106), custom_call_target="tpu_custom_call" | custom-call | flops 1073741824 | bytes 5767168 | tf_op jit(solution)/shard_map/pallas_call | solution.py:40
  83.0 1.5 collective-permute-start.1
  84.5 4.6 %shard_map.178 = bf16[4,256,512]{2,1,0:T(8,128)(2,1)} custom-call(s32[4]{0:T(128)S(1)} %broadcast_xor_fusion.table_ref, s32[1]{0:T(128)} %bitcast.21.limit_ref, bf16[256,1024]{1,0:T(8,128)(2,1)} %collective-permute-done.6.rows_ref, bf16[8,512,1024]{2,1,0:T(8,128)(2,1)S(1)} %bitcast.107), custom_call_target="tpu_custom_call" | custom-call | flops 1073741824 | bytes 5767168 | tf_op jit(solution)/shard_map/pallas_call | solution.py:40
  89.6 1.6 collective-permute-start.8
  91.2 1.2 fusion
  92.4 21.7 %collective-permute-done.8 = f32[32,512]{1,0:T(8,128)S(1)} collective-permute-done((f32[32,512]{1,0:T(8,128)S(1)}, f32[32,512]{1,0:T(8,128)S(1)}, u32[]{:S(2)}, u32[]{:S(2)}) %collective-permute-start.8) | collective-permute-done | bytes 65568 | tf_op jit(solution)/shard_map/ppermute | solution.py:15
  114.2 0.7 collective-permute-start.9
  114.9 3.5 %shard_map.175 = f32[4,256,512]{2,1,0:T(8,128)S(1)} custom-call(s32[4]{0:T(128)S(1)} %broadcast_xor_fusion.3.table_ref, s32[1]{0:T(128)} %bitcast.1.limit_ref, bf16[256,1024]{1,0:T(8,128)(2,1)} %collective-permute-done.rows_ref, bf16[8,512,1024]{2,1,0:T(8,128)(2,1)S(1)} %bitcast.108), custom_call_target="tpu_custom_call" | custom-call | flops 1073741824 | bytes 5767168 | tf_op jit(solution)/shard_map/pallas_call | solution.py:40
  118.4 1.4 copy-done.9
  119.8 3.3 %collective-permute-start.10 = (bf16[2,32,512]{2,1,0:T(8,128)(2,1)S(1)}, bf16[2,32,512]{2,1,0:T(8,128)(2,1)S(1)}, u32[]{:S(2)}, u32[]{:S(2)}) collective-permute-start(bf16[2,32,512]{2,1,0:T(8,128)(2,1)S(1)} %pad_maximum_fusion.6), channel_id=1, source_target_pairs={{0,8},{1,9},{2,10},{3,11},{4,12},{5,13},{6,14},{7,15},{8,0},{9,1},... | collective-permute-start | bytes 196616 | tf_op jit(solution)/shard_map/ppermute | solution.py:15
  123.1 3.5 %shard_map.177 = f32[4,256,512]{2,1,0:T(8,128)S(1)} custom-call(s32[4]{0:T(128)S(1)} %broadcast_xor_fusion.1.table_ref, s32[1]{0:T(128)} %bitcast.21.limit_ref, bf16[256,1024]{1,0:T(8,128)(2,1)} %collective-permute-done.6.rows_ref, bf16[8,512,1024]{2,1,0:T(8,128)(2,1)S(1)} %bitcast.111), custom_call_target="tpu_custom_call" | custom-call | flops 1073741824 | bytes 5767168 | tf_op jit(solution)/shard_map/pallas_call | solution.py:40
  126.7 1.3 copy-done.7
  128.1 1.4 broadcast_select_fusion.1
  129.5 2.0 %select_n.336 = bf16[512,2,1,256]{3,1,0,2:T(2,128)(2,1)} reshape(bf16[8,64,512]{2,1,0:T(8,128)(2,1)} %get-tuple-element.15) | data formatting | bytes 1048576 | tf_op jit(solution)/shard_map/jit(_where)/select_n | solution.py:65
  131.5 2.0 %select_n.338 = bf16[512,2,1,256]{3,1,0,2:T(2,128)(2,1)} reshape(bf16[8,64,512]{2,1,0:T(8,128)(2,1)} %get-tuple-element.16) | data formatting | bytes 1048576 | tf_op jit(solution)/shard_map/jit(_where)/select_n | solution.py:65
  133.4 2.7 %fusion.22 = f32[512,512]{1,0:T(8,128)} fusion(bf16[512,512]{1,0:T(8,128)(2,1)} %bitcast.113, bf16[512,512]{1,0:T(8,128)(2,1)} %bitcast.115), kind=kOutput, calls=%fused_computation.115 | convolution fusion | flops 268435456 | bytes 2097152 | tf_op jit(solution)/shard_map/dot_general | solution.py:173
  136.1 2.5 %pad_maximum_fusion.1 = bf16[512,2,2,256]{3,1,0,2:T(2,128)(2,1)} fusion(bf16[512,2,1,256]{3,1,0,2:T(2,128)(2,1)S(1)} %copy-done.14, bf16[512,2,1,256]{3,1,0,2:T(2,128)(2,1)S(1)} %copy-done.13), kind=kLoop, calls=%fused_computation.17 | loop fusion | flops 524288 | bytes 2097152 | tf_op jit(solution)/shard_map/stack | solution.py:185
  138.7 3.7 %copy.24 = bf16[512,2,2,256]{0,3,2,1:T(8,128)(2,1)} copy(bf16[512,2,2,256]{3,1,0,2:T(2,128)(2,1)} %pad_maximum_fusion.1) | data formatting | bytes 2097152 | tf_op jit(solution)/shard_map/stack | solution.py:185
  142.3 2.8 %convolution_convert_fusion = bf16[512,512]{1,0:T(8,128)(2,1)} fusion(bf16[512,1024]{0,1:T(8,128)(2,1)} %bitcast.117, bf16[1024,512]{1,0:T(8,128)(2,1)S(1)} %bitcast.101), kind=kOutput, calls=%fused_computation.6 | convolution fusion | flops 537133056 | bytes 2621440 | tf_op jit(solution)/shard_map/dot_general | solution.py:191
  145.1 1.6 convert_add_fusion.1
  146.8 1.6 collective-permute-start.18
  148.9 1.6 convert_add_fusion
  151.2 8.0 %collective-permute-done.18 = bf16[2,256,512]{2,1,0:T(8,128)(2,1)S(1)} collective-permute-done((bf16[2,256,512]{2,1,0:T(8,128)(2,1)S(1)}, bf16[2,256,512]{2,1,0:T(8,128)(2,1)S(1)}, u32[]{:S(2)}, u32[]{:S(2)}) %collective-permute-start.18) | collective-permute-done | bytes 524320 | tf_op jit(solution)/shard_map/ppermute | solution.py:15
  159.5 1.6 convert_add_fusion.3
  161.2 1.8 collective-permute-start.2
  163.7 1.6 convert_add_fusion.2
  166.0 1.2 collective-permute-start.24
  167.1 0.8 collective-permute-start.23
  168.0 7.5 %collective-permute-done.2 = bf16[2,256,512]{2,1,0:T(8,128)(2,1)S(1)} collective-permute-done((bf16[2,256,512]{2,1,0:T(8,128)(2,1)S(1)}, bf16[2,256,512]{2,1,0:T(8,128)(2,1)S(1)}, u32[]{:S(2)}, u32[]{:S(2)}) %collective-permute-start.2) | collective-permute-done | bytes 524320 | tf_op jit(solution)/shard_map/ppermute | solution.py:15
  175.7 0.7 collective-permute-start.12
  176.4 3.3 %collective-permute-done.14 = bf16[2,256,512]{2,1,0:T(8,128)(2,1)S(1)} collective-permute-done((bf16[2,256,512]{2,1,0:T(8,128)(2,1)S(1)}, bf16[2,256,512]{2,1,0:T(8,128)(2,1)S(1)}, u32[]{:S(2)}, u32[]{:S(2)}) %collective-permute-start.14) | collective-permute-done | bytes 524320 | tf_op jit(solution)/shard_map/ppermute | solution.py:15
  180.2 1.5 collective-permute-start.16
  181.8 2.4 %collective-permute-done.12 = bf16[256,512]{1,0:T(8,128)(2,1)S(1)} collective-permute-done((bf16[256,512]{1,0:T(8,128)(2,1)S(1)}, bf16[256,512]{1,0:T(8,128)(2,1)S(1)}, u32[]{:S(2)}, u32[]{:S(2)}) %collective-permute-start.12) | collective-permute-done | bytes 262176 | tf_op jit(solution)/shard_map/ppermute | solution.py:25
  184.3 5.4 %collective-permute-done.16 = bf16[256,512]{1,0:T(8,128)(2,1)S(1)} collective-permute-done((bf16[256,512]{1,0:T(8,128)(2,1)S(1)}, bf16[256,512]{1,0:T(8,128)(2,1)S(1)}, u32[]{:S(2)}, u32[]{:S(2)}) %collective-permute-start.16) | collective-permute-done | bytes 262176 | tf_op jit(solution)/shard_map/ppermute | solution.py:25
  189.9 1.0 maximum_bitcast_fusion
  (135 shorter events, 6.7 us)
Async XLA Ops:
  0.6 141.7 %copy-start = (bf16[1,2,512,512]{3,2,1,0:T(8,128)(2,1)S(1)}, bf16[1,2,512,512]{3,2,1,0:T(8,128)(2,1)}, u32[]{:S(2)}) copy-start(bf16[1,2,512,512]{3,2,1,0:T(8,128)(2,1)} %param.17) | copy-start | bytes 3145732
  0.6 8.3 %copy-start.19 = (s32[1,2,4]{2,1,0:T(2,128)S(1)}, s32[1,2,4]{2,1,0:T(2,128)}, u32[]{:S(2)}) copy-start(s32[1,2,4]{2,1,0:T(2,128)} %param.22) | copy-start | bytes 100
  0.7 8.5 %copy-start.21 = (s32[1,2]{1,0:T(1,128)S(1)}, s32[1,2]{1,0:T(1,128)}, u32[]{:S(2)}) copy-start(s32[1,2]{1,0:T(1,128)} %param.23) | copy-start | bytes 28
  0.7 8.6 %copy-start.17 = (bf16[1,1,8,32,1024]{4,3,2,1,0:T(8,128)(2,1)S(1)}, bf16[1,1,8,32,1024]{4,3,2,1,0:T(8,128)(2,1)}, u32[]{:S(2)}) copy-start(bf16[1,1,8,32,1024]{4,3,2,1,0:T(8,128)(2,1)} %param.21) | copy-start | bytes 1572868
  0.7 25.9 %collective-permute-start.25 = (bf16[2,32,64]{2,1,0:T(8,128)(2,1)}, bf16[2,32,64]{2,1,0:T(8,128)(2,1)S(1)}, u32[]{:S(2)}, u32[]{:S(2)}) collective-permute-start(bf16[2,32,64]{2,1,0:T(8,128)(2,1)} %bitcast.130), channel_id=1, source_target_pairs={{0,1},{1,0},{2,3},{3,2},{4,5},{5,4},{6,7},{7,6},{8,9},{9,8},{10,11... | collective-permute-start | bytes 24584 | tf_op jit(solution)/shard_map/ppermute | solution.py:15
  5.9 6.7 %copy-start.25 = (s32[4]{0:T(128)S(1)}, s32[4]{0:T(128)}, u32[]{:S(2)}) copy-start(s32[4]{0:T(128)} %constant.80.clone) | copy-start | bytes 52
  5.9 65.9 %collective-permute-start = (bf16[256,1024]{1,0:T(8,128)(2,1)}, bf16[256,1024]{1,0:T(8,128)(2,1)}, u32[]{:S(2)}, u32[]{:S(2)}) collective-permute-start(bf16[256,1024]{1,0:T(8,128)(2,1)} %get-tuple-element.13.rows_ref), channel_id=1, source_target_pairs={{0,8},{1,9},{2,10},{3,11},{4,12},{5,13},{6,14},{7,15},{8,0},{9,1},... | collective-permute-start | bytes 1572872 | tf_op jit(solution)/shard_map/ppermute | solution.py:15
  8.5 64.4 %collective-permute-start.6 = (bf16[256,1024]{1,0:T(8,128)(2,1)}, bf16[256,1024]{1,0:T(8,128)(2,1)}, u32[]{:S(2)}, u32[]{:S(2)}) collective-permute-start(bf16[256,1024]{1,0:T(8,128)(2,1)} %get-tuple-element.14.rows_ref), channel_id=1, source_target_pairs={{0,8},{1,9},{2,10},{3,11},{4,12},{5,13},{6,14},{7,15},{8,0},{9,1},... | collective-permute-start | bytes 1572872 | tf_op jit(solution)/shard_map/ppermute | solution.py:15
  11.0 47.1 %collective-permute-start.3 = (f32[32,512]{1,0:T(8,128)S(1)}, f32[32,512]{1,0:T(8,128)}, u32[]{:S(2)}, u32[]{:S(2)}) collective-permute-start(f32[32,512]{1,0:T(8,128)S(1)} %select_reduce_fusion.1), channel_id=1, source_target_pairs={{0,1},{1,0},{2,3},{3,2},{4,5},{5,4},{6,7},{7,6},{8,9},{9,8},{10,11... | collective-permute-start | bytes 196616 | tf_op jit(solution)/shard_map/ppermute | solution.py:15
  12.7 3.4 %copy-start.1 = (bf16[1,1,4096,1024]{3,2,1,0:T(8,128)(2,1)S(1)}, bf16[1,1,4096,1024]{3,2,1,0:T(8,128)(2,1)}, u32[]{:S(2)}) copy-start(bf16[1,1,4096,1024]{3,2,1,0:T(8,128)(2,1)} %param.19) | copy-start | bytes 25165828
  16.1 6.3 %copy-start.24 = (s32[4]{0:T(128)S(1)}, s32[4]{0:T(128)}, u32[]{:S(2)}) copy-start(s32[4]{0:T(128)} %constant.81.clone) | copy-start | bytes 52
  16.1 6.3 %copy-start.23 = (s32[4]{0:T(128)S(1)}, s32[4]{0:T(128)}, u32[]{:S(2)}) copy-start(s32[4]{0:T(128)} %constant.82.clone) | copy-start | bytes 52
  16.1 6.3 %copy-start.22 = (s32[4]{0:T(128)S(1)}, s32[4]{0:T(128)}, u32[]{:S(2)}) copy-start(s32[4]{0:T(128)} %constant.83.clone) | copy-start | bytes 52
  20.5 124.6 %collective-permute-start.17 = (bf16[4,256,512]{2,1,0:T(8,128)(2,1)}, bf16[4,256,512]{2,1,0:T(8,128)(2,1)}, u32[]{:S(2)}, u32[]{:S(2)}) collective-permute-start(bf16[4,256,512]{2,1,0:T(8,128)(2,1)} %shard_map.180), channel_id=1, source_target_pairs={{0,1},{1,0},{2,3},{3,2},{4,5},{5,4},{6,7},{7,6},{8,9},{9,8},{10,11... | collective-permute-start | bytes 3145736 | tf_op jit(solution)/shard_map/ppermute | solution.py:15
  22.4 4.3 %copy-start.20 = (bf16[1,2,32,64]{3,2,1,0:T(8,128)(2,1)S(1)}, bf16[1,2,32,64]{3,2,1,0:T(8,128)(2,1)}, u32[]{:S(2)}) copy-start(bf16[1,2,32,64]{3,2,1,0:T(8,128)(2,1)} %param.18) | copy-start | bytes 24580
  26.6 9.4 %collective-permute-start.26 = (bf16[2,64,64]{2,1,0:T(8,128)(2,1)S(1)}, bf16[2,64,64]{2,1,0:T(8,128)(2,1)S(1)}, u32[]{:S(2)}, u32[]{:S(2)}) collective-permute-start(bf16[2,64,64]{2,1,0:T(8,128)(2,1)S(1)} %maximum_select_fusion.2), channel_id=1, source_target_pairs={{0,2},{1,3},{2,0},{3,1},{4,6},{5,7},{6,4},{7,5},{8,10},{9,11},{10,... | collective-permute-start | bytes 49160 | tf_op jit(solution)/shard_map/ppermute | solution.py:15
  28.2 3.4 %copy-start.2 = (bf16[1,1,4096,1024]{3,2,1,0:T(8,128)(2,1)S(1)}, bf16[1,1,4096,1024]{3,2,1,0:T(8,128)(2,1)}, u32[]{:S(2)}) copy-start(bf16[1,1,4096,1024]{3,2,1,0:T(8,128)(2,1)} %param.19) | copy-start | bytes 25165828
  36.1 19.4 %collective-permute-start.27 = (bf16[2,128,64]{2,1,0:T(8,128)(2,1)S(1)}, bf16[2,128,64]{2,1,0:T(8,128)(2,1)S(1)}, u32[]{:S(2)}, u32[]{:S(2)}) collective-permute-start(bf16[2,128,64]{2,1,0:T(8,128)(2,1)S(1)} %maximum_select_fusion.1), channel_id=1, source_target_pairs={{0,4},{1,5},{2,6},{3,7},{4,0},{5,1},{6,2},{7,3},{8,12},{9,13},{10,... | collective-permute-start | bytes 98312 | tf_op jit(solution)/shard_map/ppermute | solution.py:15
  37.7 3.4 %copy-start.3 = (bf16[1,1,4096,1024]{3,2,1,0:T(8,128)(2,1)S(1)}, bf16[1,1,4096,1024]{3,2,1,0:T(8,128)(2,1)}, u32[]{:S(2)}) copy-start(bf16[1,1,4096,1024]{3,2,1,0:T(8,128)(2,1)} %param.19) | copy-start | bytes 25165828
  44.7 1.3 copy-start.5
  56.4 9.4 %collective-permute-start.28 = (bf16[2,256,32]{2,1,0:T(8,128)(2,1)}, bf16[2,256,32]{2,1,0:T(8,128)(2,1)S(1)}, u32[]{:S(2)}, u32[]{:S(2)}) collective-permute-start(bf16[2,256,32]{2,1,0:T(8,128)(2,1)} %get-tuple-element.17), channel_id=1, source_target_pairs={{0,8},{1,9},{2,10},{3,11},{4,12},{5,13},{6,14},{7,15},{8,0},{9,1},... | collective-permute-start | bytes 98312 | tf_op jit(solution)/shard_map/ppermute | solution.py:15
  59.0 8.5 %collective-permute-start.4 = (f32[32,512]{1,0:T(8,128)S(1)}, f32[32,512]{1,0:T(8,128)S(1)}, u32[]{:S(2)}, u32[]{:S(2)}) collective-permute-start(f32[32,512]{1,0:T(8,128)S(1)} %add.165), channel_id=1, source_target_pairs={{0,2},{1,3},{2,0},{3,1},{4,6},{5,7},{6,4},{7,5},{8,10},{9,11},{10,... | collective-permute-start | bytes 196616 | tf_op jit(solution)/shard_map/ppermute | solution.py:15
  65.8 83.0 %collective-permute-start.21 = (bf16[4,256,512]{2,1,0:T(8,128)(2,1)}, bf16[4,256,512]{2,1,0:T(8,128)(2,1)}, u32[]{:S(2)}, u32[]{:S(2)}) collective-permute-start(bf16[4,256,512]{2,1,0:T(8,128)(2,1)} %shard_map.182), channel_id=1, source_target_pairs={{0,2},{1,3},{2,0},{3,1},{4,6},{5,7},{6,4},{7,5},{8,10},{9,11},{10,... | collective-permute-start | bytes 3145736 | tf_op jit(solution)/shard_map/ppermute | solution.py:15
  67.5 6.6 %copy-start.18 = (bf16[1,1,8,32,1024]{4,3,2,1,0:T(8,128)(2,1)S(1)}, bf16[1,1,8,32,1024]{4,3,2,1,0:T(8,128)(2,1)}, u32[]{:S(2)}) copy-start(bf16[1,1,8,32,1024]{4,3,2,1,0:T(8,128)(2,1)} %param.21) | copy-start | bytes 1572868
  67.5 4.3 %collective-permute-start.5 = (f32[32,512]{1,0:T(8,128)S(1)}, f32[32,512]{1,0:T(8,128)S(1)}, u32[]{:S(2)}, u32[]{:S(2)}) collective-permute-start(f32[32,512]{1,0:T(8,128)S(1)} %add.166), channel_id=1, source_target_pairs={{0,4},{1,5},{2,6},{3,7},{4,0},{5,1},{6,2},{7,3},{8,12},{9,13},{10,... | collective-permute-start | bytes 196616 | tf_op jit(solution)/shard_map/ppermute | solution.py:15
  74.6 15.0 %collective-permute-start.7 = (f32[32,512]{1,0:T(8,128)S(1)}, f32[32,512]{1,0:T(8,128)S(1)}, u32[]{:S(2)}, u32[]{:S(2)}) collective-permute-start(f32[32,512]{1,0:T(8,128)S(1)} %select_reduce_fusion), channel_id=1, source_target_pairs={{0,1},{1,0},{2,3},{3,2},{4,5},{5,4},{6,7},{7,6},{8,9},{9,8},{10,11... | collective-permute-start | bytes 196616 | tf_op jit(solution)/shard_map/ppermute | solution.py:15
  75.2 3.4 %copy-start.4 = (bf16[1,1,4096,1024]{3,2,1,0:T(8,128)(2,1)S(1)}, bf16[1,1,4096,1024]{3,2,1,0:T(8,128)(2,1)}, u32[]{:S(2)}) copy-start(bf16[1,1,4096,1024]{3,2,1,0:T(8,128)(2,1)} %param.19) | copy-start | bytes 25165828
  83.0 76.5 %collective-permute-start.1 = (bf16[4,256,512]{2,1,0:T(8,128)(2,1)}, bf16[4,256,512]{2,1,0:T(8,128)(2,1)}, u32[]{:S(2)}, u32[]{:S(2)}) collective-permute-start(bf16[4,256,512]{2,1,0:T(8,128)(2,1)} %shard_map.176), channel_id=1, source_target_pairs={{0,1},{1,0},{2,3},{3,2},{4,5},{5,4},{6,7},{7,6},{8,9},{9,8},{10,11... | collective-permute-start | bytes 3145736 | tf_op jit(solution)/shard_map/ppermute | solution.py:15
  84.5 6.7 %copy-start.16 = (f32[256,1024]{1,0:T(8,128)S(1)}, f32[256,1024]{1,0:T(8,128)}, u32[]{:S(2)}) copy-start(f32[256,1024]{1,0:T(8,128)} %fusion.1) | copy-start | bytes 3145732
  84.5 38.7 %slice-start = ((s8[8388608]{0:T(1024)(128)(4,1)}), s8[4194304]{0:T(1024)(128)(4,1)S(1)}, s32[]{:S(2)}) async-start(s8[8388608]{0:T(1024)(128)(4,1)} %bitcast.109), calls=%async_computation | async-start | bytes 8388608
  89.1 74.6 %collective-permute-start.13 = (bf16[4,256,512]{2,1,0:T(8,128)(2,1)}, bf16[4,256,512]{2,1,0:T(8,128)(2,1)}, u32[]{:S(2)}, u32[]{:S(2)}) collective-permute-start(bf16[4,256,512]{2,1,0:T(8,128)(2,1)} %shard_map.178), channel_id=1, source_target_pairs={{0,2},{1,3},{2,0},{3,1},{4,6},{5,7},{6,4},{7,5},{8,10},{9,11},{10,... | collective-permute-start | bytes 3145736 | tf_op jit(solution)/shard_map/ppermute | solution.py:15
  89.6 24.6 %collective-permute-start.8 = (f32[32,512]{1,0:T(8,128)S(1)}, f32[32,512]{1,0:T(8,128)S(1)}, u32[]{:S(2)}, u32[]{:S(2)}) collective-permute-start(f32[32,512]{1,0:T(8,128)S(1)} %add.168), channel_id=1, source_target_pairs={{0,2},{1,3},{2,0},{3,1},{4,6},{5,7},{6,4},{7,5},{8,10},{9,11},{10,... | collective-permute-start | bytes 196616 | tf_op jit(solution)/shard_map/ppermute | solution.py:15
  91.2 31.9 %slice-start.1 = ((s8[8388608]{0:T(1024)(128)(4,1)}), s8[4194304]{0:T(1024)(128)(4,1)S(1)}, s32[]{:S(2)}) async-start(s8[8388608]{0:T(1024)(128)(4,1)} %bitcast.109), calls=%async_computation.1 | async-start | bytes 8388608
  114.2 5.6 %collective-permute-start.9 = (f32[32,512]{1,0:T(8,128)S(1)}, f32[32,512]{1,0:T(8,128)S(1)}, u32[]{:S(2)}, u32[]{:S(2)}) collective-permute-start(f32[32,512]{1,0:T(8,128)S(1)} %add.169), channel_id=1, source_target_pairs={{0,4},{1,5},{2,6},{3,7},{4,0},{5,1},{6,2},{7,3},{8,12},{9,13},{10,... | collective-permute-start | bytes 196616 | tf_op jit(solution)/shard_map/ppermute | solution.py:15
  118.4 1.4 copy-start.9
  119.8 8.3 %collective-permute-start.10 = (bf16[2,32,512]{2,1,0:T(8,128)(2,1)S(1)}, bf16[2,32,512]{2,1,0:T(8,128)(2,1)S(1)}, u32[]{:S(2)}, u32[]{:S(2)}) collective-permute-start(bf16[2,32,512]{2,1,0:T(8,128)(2,1)S(1)} %pad_maximum_fusion.6), channel_id=1, source_target_pairs={{0,8},{1,9},{2,10},{3,11},{4,12},{5,13},{6,14},{7,15},{8,0},{9,1},... | collective-permute-start | bytes 196616 | tf_op jit(solution)/shard_map/ppermute | solution.py:15
  126.7 1.4 copy-start.7
  133.4 2.7 %copy-start.13 = (bf16[512,2,1,256]{3,1,0,2:T(2,128)(2,1)S(1)}, bf16[512,2,1,256]{3,1,0,2:T(2,128)(2,1)}, u32[]{:S(2)}) copy-start(bf16[512,2,1,256]{3,1,0,2:T(2,128)(2,1)} %select_n.336) | copy-start | bytes 1572868
  133.4 2.7 %copy-start.14 = (bf16[512,2,1,256]{3,1,0,2:T(2,128)(2,1)S(1)}, bf16[512,2,1,256]{3,1,0,2:T(2,128)(2,1)}, u32[]{:S(2)}) copy-start(bf16[512,2,1,256]{3,1,0,2:T(2,128)(2,1)} %select_n.338) | copy-start | bytes 1572868
  145.1 3.3 %copy-start.12 = (bf16[8,64,512]{2,1,0:T(8,128)(2,1)S(1)}, bf16[8,64,512]{2,1,0:T(8,128)(2,1)}, u32[]{:S(2)}) copy-start(bf16[8,64,512]{2,1,0:T(8,128)(2,1)} %get-tuple-element.24) | copy-start | bytes 1572868
  145.1 3.3 %copy-start.15 = (bf16[1,8,64,512]{3,2,1,0:T(8,128)(2,1)S(1)}, bf16[1,8,64,512]{3,2,1,0:T(8,128)(2,1)}, u32[]{:S(2)}) copy-start(bf16[1,8,64,512]{3,2,1,0:T(8,128)(2,1)} %param.20) | copy-start | bytes 1572868
  146.7 2.2 %copy-start.6 = (f32[4,256,512]{2,1,0:T(8,128)S(1)}, f32[4,256,512]{2,1,0:T(8,128)}, u32[]{:S(2)}) copy-start(f32[4,256,512]{2,1,0:T(8,128)} %copy-done.5) | copy-start | bytes 6291460
  146.8 12.4 %collective-permute-start.18 = (bf16[2,256,512]{2,1,0:T(8,128)(2,1)S(1)}, bf16[2,256,512]{2,1,0:T(8,128)(2,1)S(1)}, u32[]{:S(2)}, u32[]{:S(2)}) collective-permute-start(bf16[2,256,512]{2,1,0:T(8,128)(2,1)S(1)} %slice.227), channel_id=1, source_target_pairs={{0,2},{1,3},{2,0},{3,1},{4,6},{5,7},{6,4},{7,5},{8,10},{9,11},{10,... | collective-permute-start | bytes 1572872 | tf_op jit(solution)/shard_map/ppermute | solution.py:15
  150.5 9.0 %copy-start.10 = (f32[4,256,512]{2,1,0:T(8,128)S(1)}, f32[4,256,512]{2,1,0:T(8,128)}, u32[]{:S(2)}) copy-start(f32[4,256,512]{2,1,0:T(8,128)} %copy-done.9) | copy-start | bytes 6291460
  150.6 12.5 %collective-permute-start.22 = (bf16[2,256,512]{2,1,0:T(8,128)(2,1)S(1)}, bf16[2,256,512]{2,1,0:T(8,128)(2,1)S(1)}, u32[]{:S(2)}, u32[]{:S(2)}) collective-permute-start(bf16[2,256,512]{2,1,0:T(8,128)(2,1)S(1)} %slice.226), channel_id=1, source_target_pairs={{0,1},{1,0},{2,3},{3,2},{4,5},{5,4},{6,7},{7,6},{8,9},{9,8},{10,11... | collective-permute-start | bytes 1572872 | tf_op jit(solution)/shard_map/ppermute | solution.py:15
  159.4 7.7 %collective-permute-start.20 = (bf16[256,512]{1,0:T(8,128)(2,1)S(1)}, bf16[256,512]{1,0:T(8,128)(2,1)S(1)}, u32[]{:S(2)}, u32[]{:S(2)}) collective-permute-start(bf16[256,512]{1,0:T(8,128)(2,1)S(1)} %fusion.13), channel_id=1, source_target_pairs={{0,20},{1,21},{2,22},{3,23},{4,16},{5,17},{6,18},{7,19},{8,28},{9,... | collective-permute-start | bytes 786440 | tf_op jit(solution)/shard_map/ppermute | solution.py:25
  161.1 2.1 %copy-start.11 = (f32[512,512]{1,0:T(8,128)S(1)}, f32[512,512]{1,0:T(8,128)}, u32[]{:S(2)}) copy-start(f32[512,512]{1,0:T(8,128)} %fusion.22) | copy-start | bytes 3145732
  161.2 2.4 %copy-start.8 = (f32[4,256,512]{2,1,0:T(8,128)S(1)}, f32[4,256,512]{2,1,0:T(8,128)}, u32[]{:S(2)}) copy-start(f32[4,256,512]{2,1,0:T(8,128)} %copy-done.7) | copy-start | bytes 6291460
  161.2 14.3 %collective-permute-start.2 = (bf16[2,256,512]{2,1,0:T(8,128)(2,1)S(1)}, bf16[2,256,512]{2,1,0:T(8,128)(2,1)S(1)}, u32[]{:S(2)}, u32[]{:S(2)}) collective-permute-start(bf16[2,256,512]{2,1,0:T(8,128)(2,1)S(1)} %slice.229), channel_id=1, source_target_pairs={{0,2},{1,3},{2,0},{3,1},{4,6},{5,7},{6,4},{7,5},{8,10},{9,11},{10,... | collective-permute-start | bytes 1572872 | tf_op jit(solution)/shard_map/ppermute | solution.py:15
  163.5 4.4 %collective-permute-start.19 = (bf16[256,512]{1,0:T(8,128)(2,1)S(1)}, bf16[256,512]{1,0:T(8,128)(2,1)S(1)}, u32[]{:S(2)}, u32[]{:S(2)}) collective-permute-start(bf16[256,512]{1,0:T(8,128)(2,1)S(1)} %get-tuple-element.11), channel_id=1, source_target_pairs={{0,16},{1,17},{2,18},{3,19},{4,20},{5,21},{6,22},{7,23},{8,24},{9,... | collective-permute-start | bytes 786440 | tf_op jit(solution)/shard_map/ppermute | solution.py:25
  165.3 14.3 %collective-permute-start.14 = (bf16[2,256,512]{2,1,0:T(8,128)(2,1)S(1)}, bf16[2,256,512]{2,1,0:T(8,128)(2,1)S(1)}, u32[]{:S(2)}, u32[]{:S(2)}) collective-permute-start(bf16[2,256,512]{2,1,0:T(8,128)(2,1)S(1)} %slice.228), channel_id=1, source_target_pairs={{0,1},{1,0},{2,3},{3,2},{4,5},{5,4},{6,7},{7,6},{8,9},{9,8},{10,11... | collective-permute-start | bytes 1572872 | tf_op jit(solution)/shard_map/ppermute | solution.py:15
  166.0 15.7 %collective-permute-start.24 = (bf16[256,512]{1,0:T(8,128)(2,1)S(1)}, bf16[256,512]{1,0:T(8,128)(2,1)S(1)}, u32[]{:S(2)}, u32[]{:S(2)}) collective-permute-start(bf16[256,512]{1,0:T(8,128)(2,1)S(1)} %fusion.14), channel_id=1, source_target_pairs={{0,20},{1,21},{2,22},{3,23},{4,16},{5,17},{6,18},{7,19},{8,28},{9,... | collective-permute-start | bytes 786440 | tf_op jit(solution)/shard_map/ppermute | solution.py:25
  167.1 14.6 %collective-permute-start.23 = (bf16[256,512]{1,0:T(8,128)(2,1)S(1)}, bf16[256,512]{1,0:T(8,128)(2,1)S(1)}, u32[]{:S(2)}, u32[]{:S(2)}) collective-permute-start(bf16[256,512]{1,0:T(8,128)(2,1)S(1)} %get-tuple-element.12), channel_id=1, source_target_pairs={{0,16},{1,17},{2,18},{3,19},{4,20},{5,21},{6,22},{7,23},{8,24},{9,... | collective-permute-start | bytes 786440 | tf_op jit(solution)/shard_map/ppermute | solution.py:25
  175.7 8.5 %collective-permute-start.12 = (bf16[256,512]{1,0:T(8,128)(2,1)S(1)}, bf16[256,512]{1,0:T(8,128)(2,1)S(1)}, u32[]{:S(2)}, u32[]{:S(2)}) collective-permute-start(bf16[256,512]{1,0:T(8,128)(2,1)S(1)} %fusion.11), channel_id=1, source_target_pairs={{0,20},{1,21},{2,22},{3,23},{4,16},{5,17},{6,18},{7,19},{8,28},{9,... | collective-permute-start | bytes 786440 | tf_op jit(solution)/shard_map/ppermute | solution.py:25
  180.1 4.1 %collective-permute-start.11 = (bf16[256,512]{1,0:T(8,128)(2,1)S(1)}, bf16[256,512]{1,0:T(8,128)(2,1)S(1)}, u32[]{:S(2)}, u32[]{:S(2)}) collective-permute-start(bf16[256,512]{1,0:T(8,128)(2,1)S(1)} %get-tuple-element.9), channel_id=1, source_target_pairs={{0,16},{1,17},{2,18},{3,19},{4,20},{5,21},{6,22},{7,23},{8,24},{9,... | collective-permute-start | bytes 786440 | tf_op jit(solution)/shard_map/ppermute | solution.py:25
  180.2 9.5 %collective-permute-start.16 = (bf16[256,512]{1,0:T(8,128)(2,1)S(1)}, bf16[256,512]{1,0:T(8,128)(2,1)S(1)}, u32[]{:S(2)}, u32[]{:S(2)}) collective-permute-start(bf16[256,512]{1,0:T(8,128)(2,1)S(1)} %fusion.12), channel_id=1, source_target_pairs={{0,20},{1,21},{2,22},{3,23},{4,16},{5,17},{6,18},{7,19},{8,28},{9,... | collective-permute-start | bytes 786440 | tf_op jit(solution)/shard_map/ppermute | solution.py:25
  181.7 8.0 %collective-permute-start.15 = (bf16[256,512]{1,0:T(8,128)(2,1)S(1)}, bf16[256,512]{1,0:T(8,128)(2,1)S(1)}, u32[]{:S(2)}, u32[]{:S(2)}) collective-permute-start(bf16[256,512]{1,0:T(8,128)(2,1)S(1)} %get-tuple-element.10), channel_id=1, source_target_pairs={{0,16},{1,17},{2,18},{3,19},{4,20},{5,21},{6,22},{7,23},{8,24},{9,... | collective-permute-start | bytes 786440 | tf_op jit(solution)/shard_map/ppermute | solution.py:25

commit v2 on v1

v2 whole, which is shorter than its diff:
```python
import jax
import jax.numpy as jnp
from jax import lax
from jax.experimental import pallas as pl
from jax.experimental.pallas import tpu as pltpu
from jax.sharding import PartitionSpec as P

SEG = 128
BF16 = jnp.bfloat16
F32 = jnp.float32


def partner(value, mask):
    pairs = [(source, source ^ mask) for source in range(lax.axis_size("tensor"))]
    return lax.ppermute(value, "tensor", pairs)


def relay(value, mask):
    sections, tiles = lax.axis_size("pipe"), lax.axis_size("tensor")
    pairs = [
        (p * tiles + t, (p - 1) % sections * tiles + (t ^ mask))
        for p in range(sections)
        for t in range(tiles)
    ]
    return lax.ppermute(value, ("pipe", "tensor"), pairs)


def product_body(table_ref, limit_ref, rows_ref, weight_ref, out_ref, turned_ref):
    @pl.when(pl.program_id(0) == 0)
    def _():
        turned_ref[...] = rows_ref[...].reshape(turned_ref.shape[::-1]).T

    value = jnp.dot(weight_ref[0], turned_ref[...], preferred_element_type=F32)
    row = lax.broadcasted_iota(jnp.int32, value.shape, 1)
    out_ref[0] = jnp.where(row < limit_ref[0], value, 0.0).astype(out_ref.dtype)


def product(rows, micro, weight_blocks, table, limit, dtype):
    _, count, depth = rows.shape
    _, width, _ = weight_blocks.shape
    blocks = table.shape[0]
    return pl.pallas_call(
        product_body,
        grid_spec=pltpu.PrefetchScalarGridSpec(
            num_scalar_prefetch=2,
            grid=(blocks,),
            in_specs=[
                pl.BlockSpec((1, count, depth), lambda k, table, limit: (micro, 0, 0)),
                pl.BlockSpec((1, width, depth), lambda k, table, limit: (table[k], 0, 0)),
            ],
            out_specs=pl.BlockSpec((1, width, count), lambda k, table, limit: (k, 0, 0)),
            scratch_shapes=[pltpu.VMEM((depth, count), rows.dtype)],
        ),
        out_shape=jax.ShapeDtypeStruct((blocks, width, count), dtype),
        cost_estimate=pl.CostEstimate(
            flops=2 * blocks * count * width * depth,
            bytes_accessed=2 * (blocks * width * depth + count * depth + blocks * count * width),
            transcendentals=0,
        ),
    )(table, limit, rows, weight_blocks)


def finish_body(micro_count, high_size, high_ref, kept_ref, *refs):
    *got_refs, out_ref = refs
    _, _, count = kept_ref.shape
    for k in range(high_size):
        start = pl.multiple_of((high_ref[0] ^ k) * count, count)
        for m in range(micro_count):
            at = k * micro_count + m
            total = kept_ref[at].astype(F32) + got_refs[at][...].astype(F32)
            out_ref[m, pl.ds(start, count), :] = total.T.astype(out_ref.dtype)


def finish(kept, got, high, micro_count):
    _, width, count = kept.shape
    high_size = len(got) // micro_count
    return pl.pallas_call(
        lambda *refs: finish_body(micro_count, high_size, *refs),
        in_specs=[pl.BlockSpec(memory_space=pltpu.SMEM)]
        + [pl.BlockSpec(memory_space=pltpu.VMEM)] * (1 + len(got)),
        out_specs=pl.BlockSpec(memory_space=pltpu.VMEM),
        out_shape=jax.ShapeDtypeStruct((micro_count, high_size * count, width), BF16),
    )(high[None], kept, *got)


def unrelate(parts, own):
    bits = len(parts).bit_length() - 1
    for bit in range(bits):
        swap = (own >> bit) & 1 == 1
        parts = [jnp.where(swap, parts[k ^ (1 << bit)], parts[k]) for k in range(len(parts))]
    return parts


def shards(
    output_gradient,
    forward_input,
    saved_rank_outputs,
    projection_weight,
    adapter_down_maps,
    adapter_up_maps,
    segment_adapter_class,
    live_segment_table,
):
    grad_tile = output_gradient[0, 0]
    micro_count, tile_rows, tile_cols = grad_tile.shape
    up_tile = adapter_up_maps[0, 0]
    class_count, rank_part, _ = up_tile.shape
    down = adapter_down_maps[0]
    rank = down.shape[1]
    portion = down.shape[2]
    tiles = lax.axis_size("tensor")
    low_size = min(tiles, 8)
    low_bits = low_size.bit_length() - 1
    high_size = tiles // low_size
    position = lax.axis_index("tensor")
    low = position % low_size
    high = position // low_size
    batch_rows = tile_rows * high_size
    weight_blocks = projection_weight[0, 0].reshape(low_size, portion, tile_cols)
    classes = segment_adapter_class[0]
    live_count = live_segment_table[0]

    groups = [(k, m) for k in range(high_size) for m in range(micro_count)]

    grads = {(0, m): (grad_tile, m) for m in range(micro_count)}
    for k in range(1, high_size):
        for m in range(micro_count):
            grads[k, m] = (partner(grad_tile[m], k * low_size)[None], 0)

    def order_of(m):
        bits = list(range(low_bits))
        if m % 2 == 1 and low_bits > 1:
            bits[0], bits[1] = bits[1], bits[0]
        return bits

    def relative_blocks(bits, first):
        blocks = [first]
        for bit in reversed(bits):
            blocks = blocks + [b | 1 << bit for b in blocks]
        return jnp.array(blocks, jnp.int32) ^ low

    def limit_of(k, m):
        return jnp.clip(live_count[m] * SEG - (high ^ k) * tile_rows, 0, tile_rows)[None]

    def sent_product(k, m):
        bits = order_of(m)
        table = relative_blocks(bits[1:], 1 << bits[0])
        return product(*grads[k, m], weight_blocks, table, limit_of(k, m), BF16)

    def kept_product(k, m):
        table = relative_blocks(order_of(m)[1:], 0)
        return product(*grads[k, m], weight_blocks, table, limit_of(k, m), F32)

    first = {(0, m): sent_product(0, m) for m in range(micro_count)}
    held = lax.optimization_barrier(
        (*first.values(), up_tile, saved_rank_outputs[0], forward_input[0], down)
    )
    first = dict(zip(first, held))
    up_tile, hidden, inputs, down = held[-4:]

    def row_classes(k, m):
        segs = ((high ^ k) * tile_rows + jnp.arange(tile_rows, dtype=jnp.int32)) // SEG
        chosen = jnp.zeros((tile_rows,), jnp.int32)
        for s in range(classes.shape[1]):
            chosen = jnp.where(segs == s, classes[m, s], chosen)
        chosen = jnp.where(segs < live_count[m], chosen, -1)
        return (chosen[None] == jnp.arange(class_count, dtype=jnp.int32)[:, None])[:, None]

    indicator = {g: row_classes(*g) for g in groups}

    def base_sum(k, m):
        bits = order_of(m)
        sent = first[k, m] if (k, m) in first else sent_product(k, m)
        got = partner(sent, 1 << bits[0])
        total = kept_product(k, m)
        for bit in bits[1:]:
            total = total + got
            half = total.shape[0] // 2
            got = total[half:].astype(BF16)
            total = total[:half]
            if bit == bits[-1]:
                return total[0], relay(got[0], 1 << bit)
            got = partner(got, 1 << bit)

    sums = {g: base_sum(*g) for g in groups}

    up_flat = up_tile.reshape(class_count * rank_part, tile_cols)
    parts = []
    for g in groups:
        rows, at = grads[g]
        every = lax.dot_general(
            up_flat, rows[at], (((1,), (1,)), ((), ())), preferred_element_type=F32
        ).reshape(class_count, rank_part, tile_rows)
        parts.append(jnp.sum(jnp.where(indicator[g], every, 0.0), 0))
    own_rank = jnp.concatenate(parts, 1)
    for bit in range(low_bits):
        own_rank = own_rank + partner(own_rank, 1 << bit)
    own_rank = own_rank.astype(BF16)

    def by_group(whole):
        return dict(zip(groups, jnp.split(whole, len(groups), 1)))

    ranks = [by_group(own_rank)]
    for j in range(1, high_size):
        got = by_group(partner(own_rank, j * low_size))
        ranks.append({(k, m): got[k ^ j, m] for k, m in groups})
    spread = {}
    for g in groups:
        whole = jnp.concatenate(unrelate([r[g] for r in ranks], high), 0)
        spread[g] = jnp.where(indicator[g], whole[None], jnp.zeros((), BF16)).reshape(
            class_count * rank, tile_rows
        )

    down_flat = down.reshape(class_count * rank, portion)
    kept = []
    for g in groups:
        adapter = lax.dot_general(
            down_flat, spread[g], (((0,), (0,)), ((), ())), preferred_element_type=F32
        )
        kept.append((sums[g][0] + adapter).astype(BF16))
    kept = relay(jnp.stack(kept), 0)
    grad_prev = finish(kept, [sums[g][1] for g in groups], high, micro_count)

    inputs = inputs.reshape(micro_count, high_size, tile_rows, portion)
    down_total = 0.0
    for k, m in groups:
        rows = lax.dynamic_index_in_dim(inputs[m], high ^ k, 0, False)
        down_total = down_total + jnp.dot(spread[k, m], rows, preferred_element_type=F32)
    down_map_gradient = down_total.astype(BF16)

    for bit in range(low_bits):
        got = partner(hidden, 1 << bit)
        upper = (position >> bit) & 1 == 1
        hidden = jnp.where(
            upper, jnp.concatenate([got, hidden], 1), jnp.concatenate([hidden, got], 1)
        )
    up_total = 0.0
    for k in range(high_size):
        wanted = lax.dynamic_slice_in_dim(hidden, (high ^ k) * rank_part, rank_part, 2)
        if k > 0:
            wanted = partner(wanted, k * low_size)
        for m in range(micro_count):
            rows, at = grads[k, m]
            wide = jnp.where(indicator[k, m], wanted[m].T[None], jnp.zeros((), BF16))
            up_total = up_total + jnp.dot(
                wide.reshape(class_count * rank_part, tile_rows),
                rows[at],
                preferred_element_type=F32,
            )
    up_map_gradient = up_total.astype(BF16)
    return (
        grad_prev[None],
        down_map_gradient.reshape(1, class_count, rank, portion),
        up_map_gradient.reshape(1, 1, class_count, rank_part, tile_cols),
    )


def solution(mesh):
    in_specs = (
        P("pipe", "tensor", None, None, None),
        P("pipe", None, None, "tensor"),
        P("pipe", None, "tensor", None),
        P("pipe", "tensor", None, None),
        P("pipe", None, None, "tensor"),
        P("pipe", "tensor", None, None, None),
        P("pipe", None, None),
        P("pipe", None),
    )
    out_specs = (
        P("pipe", None, None, "tensor"),
        P("pipe", None, None, "tensor"),
        P("pipe", "tensor", None, None, None),
    )
    return jax.shard_map(shards, mesh=mesh, in_specs=in_specs, out_specs=out_specs, check_vma=False)
```

time: 192 us -> 203 us (1.057)
  local copies, waits for them, and re-layouts: 31.9 us -> 8.36 us
  Pallas kernels: 32.1 us -> 50.7 us
  waiting for transfers between devices: 64.9 us -> 77.8 us
  other arithmetic: 14.3 us -> 21.8 us
  starting transfers between devices: 33.2 us -> 28.1 us
    unnamed x59 -> x44, local copies, waits for them, and re-layouts: 18.7 us -> 2.33 us
    pallas_call x8, Pallas kernels: 32.1 us -> 47.9 us  [product(): pl.pallas_call(product_body, grid_spec=pltpu.PrefetchScalarGridSpec(num_s...]
    select_n x4 -> x12, other arithmetic: 0.08 us -> 12.6 us  [the longest x4 12.4 us: row_classes(): chosen = jnp.where(segs < live_count[m], chosen, -1)]
    ppermute x8 -> x5, waiting for transfers between devices: 7.87 us -> 20 us  [relay(): return lax.ppermute(value, ('pipe', 'tensor'), pairs)]
    ppermute x21 -> x18, starting transfers between devices: 28.8 us -> 24.3 us  [partner(): return lax.ppermute(value, 'tensor', pairs)]
    select_n x2 -> x0, local copies, waits for them, and re-layouts: 3.92 us -> none  [unrelate(): jnp.where(swap, parts[k ^ 1 << bit], parts[k])]
    another operation x1 -> x0, local copies, waits for them, and re-layouts: 3.67 us -> none  [shards(): jnp.stack(unrelate([s.reshape(class_count * rank, micro_count, tile_rows)...]
    xor x4, other arithmetic: 0.01 us -> 3.56 us  [relative_blocks(): return jnp.array(blocks, jnp.int32) ^ low]
  transfers between devices with their start and end apart: 29 -> 23, of which waited for: 9 -> 10; matrix products, arithmetic and copies ran while one was open for 21% -> 18% of each run, Pallas kernels for 17% -> 18%
where the time goes in v2:
time: 203 us; the launch traced here: 202 us
  waiting for transfers between devices  77.8 us (38%)
  Pallas kernels  50.7 us (25%)
  starting transfers between devices  28.1 us (14%)
  other arithmetic  21.8 us (11%)
  matrix products  12.3 us (6%)
  local copies, waits for them, and re-layouts  8.36 us (4%)
  between operations  2.59 us (1%)
    ppermute x18, waiting for transfers between devices, partner(): return lax.ppermute(value, 'tensor', pairs)  57.8 us
    pallas_call x8, Pallas kernels, product(): pl.pallas_call(product_body, grid_spec=pltpu.PrefetchScalarGridSpec(num_s...  47.9 us
    ppermute x18, starting transfers between devices, partner(): return lax.ppermute(value, 'tensor', pairs)  24.3 us
    ppermute x5, waiting for transfers between devices, relay(): return lax.ppermute(value, ('pipe', 'tensor'), pairs)  20 us
    select_n x4, other arithmetic, row_classes(): chosen = jnp.where(segs < live_count[m], chosen, -1)  12.4 us
    dot_general x4, matrix products, shards(): lax.dot_general(up_flat, rows[at], (((1,), (1,)), ((), ())), preferred_el...  5.91 us
    add x8, other arithmetic, base_sum(): total = total + got  5.31 us
  transfers between devices with their start and end apart: 23, of which 10 were waited for; matrix products, arithmetic and copies ran while one was open for 18% of the time, Pallas kernels for 18%

profile of v2, /device:TPU:0, one launch (start us, length us, event | category | flops | bytes accessed | tf_op | source)
XLA Modules:
  0.0 201.8 jit_solution(7615793480825793177)
XLA Ops:
  0.7 1.3 broadcast_xor_fusion.2.table_ref
  2.0 1.2 broadcast_xor_fusion.1.table_ref
  3.2 1.4 fusion.50
  5.9 5.8 %shard_map.176 = bf16[4,512,256]{2,1,0:T(8,128)(2,1)} custom-call(s32[4]{0:T(128)} %broadcast_xor_fusion.2.table_ref, s32[1]{0:T(128)} %bitcast.2.limit_ref, bf16[2,256,1024]{2,1,0:T(8,128)(2,1)} %bitcast.179, bf16[8,512,1024]{2,1,0:T(8,128)(2,1)} %bitcast.171), custom_call_target="tpu_custom_call" | custom-call | flops 1073741824 | bytes 5767168 | tf_op jit(solution)/shard_map/pallas_call | solution.py:42
  11.8 6.0 %shard_map.177 = bf16[4,512,256]{2,1,0:T(8,128)(2,1)} custom-call(s32[4]{0:T(128)} %broadcast_xor_fusion.1.table_ref, s32[1]{0:T(128)} %bitcast.6.limit_ref, bf16[2,256,1024]{2,1,0:T(8,128)(2,1)} %bitcast.180, bf16[8,512,1024]{2,1,0:T(8,128)(2,1)} %bitcast.172), custom_call_target="tpu_custom_call" | custom-call | flops 1073741824 | bytes 5767168 | tf_op jit(solution)/shard_map/pallas_call | solution.py:42
  17.7 3.0 %collective-permute-start.19 = (bf16[2,32,64]{2,1,0:T(8,128)(2,1)S(1)}, bf16[2,32,64]{2,1,0:T(8,128)(2,1)S(1)}, u32[]{:S(2)}, u32[]{:S(2)}) collective-permute-start(bf16[2,32,64]{2,1,0:T(8,128)(2,1)S(1)} %bitcast.204), channel_id=1, source_target_pairs={{0,1},{1,0},{2,3},{3,2},{4,5},{5,4},{6,7},{7,6},{8,9},{9,8},{10,11... | collective-permute-start | bytes 24584 | tf_op jit(solution)/shard_map/ppermute | solution.py:15
  20.7 1.0 slice_bitcast_fusion.5
  21.8 2.6 %collective-permute-start.2 = (bf16[256,1024]{1,0:T(8,128)(2,1)}, bf16[256,1024]{1,0:T(8,128)(2,1)S(1)}, u32[]{:S(2)}, u32[]{:S(2)}) collective-permute-start(bf16[256,1024]{1,0:T(8,128)(2,1)} %get-tuple-element.17), channel_id=1, source_target_pairs={{0,8},{1,9},{2,10},{3,11},{4,12},{5,13},{6,14},{7,15},{8,0},{9,1},... | collective-permute-start | bytes 1572872 | tf_op jit(solution)/shard_map/ppermute | solution.py:15
  24.9 1.8 collective-permute-start.8
  26.8 0.7 fusion.49
  27.4 3.0 %compare_select_fusion.3 = s32[256]{0:T(256)S(1)} fusion(s32[]{:T(128)} %bitcast.16, s32[]{:T(128)} %bitcast.15, s32[]{:T(128)} %bitcast.14, s32[]{:T(128)} %bitcast.13, s32[]{:T(128)} %bitcast.1, s32[]{:T(128)S(6)} %mul.13), kind=kLoop, calls=%fused_computation.111 | loop fusion | flops 6656 | bytes 1048 | tf_op jit(solution)/shard_map/jit(_where)/select_n | solution.py:166
  30.5 3.0 %compare_select_fusion.1 = s32[256]{0:T(256)S(1)} fusion(s32[]{:T(128)} %bitcast.16, s32[]{:T(128)} %bitcast.15, s32[]{:T(128)} %bitcast.14, s32[]{:T(128)} %bitcast.13, s32[]{:T(128)} %bitcast.1, s32[]{:T(128)S(6)} %mul.15), kind=kLoop, calls=%fused_computation.108 | loop fusion | flops 6656 | bytes 1048 | tf_op jit(solution)/shard_map/jit(_where)/select_n | solution.py:166
  33.5 3.2 %compare_select_fusion.2 = s32[256]{0:T(256)S(1)} fusion(s32[]{:T(128)} %bitcast.22, s32[]{:T(128)} %bitcast.21, s32[]{:T(128)} %bitcast.20, s32[]{:T(128)} %bitcast.19, s32[]{:T(128)} %bitcast.5, s32[]{:T(128)S(6)} %mul.13), kind=kLoop, calls=%fused_computation.110 | loop fusion | flops 6656 | bytes 1048 | tf_op jit(solution)/shard_map/jit(_where)/select_n | solution.py:166
  36.7 3.2 %compare_select_fusion = s32[256]{0:T(256)S(1)} fusion(s32[]{:T(128)} %bitcast.22, s32[]{:T(128)} %bitcast.21, s32[]{:T(128)} %bitcast.20, s32[]{:T(128)} %bitcast.19, s32[]{:T(128)} %bitcast.5, s32[]{:T(128)S(6)} %mul.15), kind=kLoop, calls=%fused_computation.107 | loop fusion | flops 6656 | bytes 1048 | tf_op jit(solution)/shard_map/jit(_where)/select_n | solution.py:166
  39.9 0.5 broadcast_xor_fusion.3.table_ref
  40.5 0.5 broadcast_xor_fusion.table_ref
  41.0 2.1 %fusion.48 = (bf16[1,512,512]{2,1,0:T(8,128)(2,1)S(1)}, bf16[1,512,512]{2,1,0:T(8,128)(2,1)}) fusion(bf16[2,512,512]{2,1,0:T(8,128)(2,1)} %bitcast.192), kind=kLoop, calls=%fused_computation.142 | loop fusion | bytes 2097152 | tf_op jit(solution)/shard_map/slice | solution.py:227
  43.1 1.4 fusion.4
  44.5 1.4 fusion.3
  46.2 6.0 %shard_map.178 = f32[4,512,256]{2,1,0:T(8,128)} custom-call(s32[4]{0:T(128)} %broadcast_xor_fusion.table_ref, s32[1]{0:T(128)} %bitcast.6.limit_ref, bf16[2,256,1024]{2,1,0:T(8,128)(2,1)} %bitcast.181, bf16[8,512,1024]{2,1,0:T(8,128)(2,1)} %bitcast.173), custom_call_target="tpu_custom_call" | custom-call | flops 1073741824 | bytes 5767168 | tf_op jit(solution)/shard_map/pallas_call | solution.py:42
  52.2 1.9 collective-permute-start.21
  54.2 6.0 %shard_map.175 = f32[4,512,256]{2,1,0:T(8,128)} custom-call(s32[4]{0:T(128)} %broadcast_xor_fusion.3.table_ref, s32[1]{0:T(128)} %bitcast.2.limit_ref, bf16[2,256,1024]{2,1,0:T(8,128)(2,1)} %bitcast.182, bf16[8,512,1024]{2,1,0:T(8,128)(2,1)} %bitcast.174), custom_call_target="tpu_custom_call" | custom-call | flops 1073741824 | bytes 5767168 | tf_op jit(solution)/shard_map/pallas_call | solution.py:42
  60.2 11.2 %collective-permute-done.21 = bf16[2,128,64]{2,1,0:T(8,128)(2,1)S(1)} collective-permute-done((bf16[2,128,64]{2,1,0:T(8,128)(2,1)S(1)}, bf16[2,128,64]{2,1,0:T(8,128)(2,1)S(1)}, u32[]{:S(2)}, u32[]{:S(2)}) %collective-permute-start.21) | collective-permute-done | bytes 32800 | tf_op jit(solution)/shard_map/ppermute | solution.py:15
  71.9 1.6 collective-permute-start.22
  73.8 1.3 convolution_add_fusion.1
  75.1 5.9 %collective-permute-done.22 = bf16[2,256,32]{2,1,0:T(8,128)(2,1)S(1)} collective-permute-done((bf16[2,256,32]{2,1,0:T(8,128)(2,1)S(1)}, bf16[2,256,32]{2,1,0:T(8,128)(2,1)S(1)}, u32[]{:S(2)}, u32[]{:S(2)}) %collective-permute-start.22) | collective-permute-done | bytes 32800 | tf_op jit(solution)/shard_map/ppermute | solution.py:15
  81.3 1.6 fusion.5
  82.9 1.6 fusion.6
  84.5 0.5 collective-permute-start.4
  85.1 5.9 %shard_map.180 = bf16[4,512,256]{2,1,0:T(8,128)(2,1)} custom-call(s32[4]{0:T(128)} %broadcast_xor_fusion.2.table_ref, s32[1]{0:T(128)} %bitcast.32.limit_ref, bf16[1,256,1024]{2,1,0:T(8,128)(2,1)} %bitcast.183, bf16[8,512,1024]{2,1,0:T(8,128)(2,1)} %bitcast.175), custom_call_target="tpu_custom_call" | custom-call | flops 1073741824 | bytes 5767168 | tf_op jit(solution)/shard_map/pallas_call | solution.py:42
  90.9 1.5 collective-permute-start.10
  92.5 6.1 %shard_map.182 = bf16[4,512,256]{2,1,0:T(8,128)(2,1)} custom-call(s32[4]{0:T(128)} %broadcast_xor_fusion.1.table_ref, s32[1]{0:T(128)} %bitcast.37.limit_ref, bf16[1,256,1024]{2,1,0:T(8,128)(2,1)} %bitcast.185, bf16[8,512,1024]{2,1,0:T(8,128)(2,1)} %bitcast.176), custom_call_target="tpu_custom_call" | custom-call | flops 1073741824 | bytes 5767168 | tf_op jit(solution)/shard_map/pallas_call | solution.py:42
  98.6 1.4 collective-permute-start.12
  100.1 0.7 collective-permute-start.5
  101.1 24.3 %collective-permute-done.5 = f32[32,1024]{1,0:T(8,128)S(1)} collective-permute-done((f32[32,1024]{1,0:T(8,128)S(1)}, f32[32,1024]{1,0:T(8,128)S(1)}, u32[]{:S(2)}, u32[]{:S(2)}) %collective-permute-start.5) | collective-permute-done | bytes 131104 | tf_op jit(solution)/shard_map/ppermute | solution.py:15
  125.4 0.6 collective-permute-start.6
  125.9 1.1 fusion.1
  127.0 6.0 %shard_map.179 = f32[4,512,256]{2,1,0:T(8,128)} custom-call(s32[4]{0:T(128)} %broadcast_xor_fusion.3.table_ref, s32[1]{0:T(128)} %bitcast.32.limit_ref, bf16[1,256,1024]{2,1,0:T(8,128)(2,1)} %bitcast.184, bf16[8,512,1024]{2,1,0:T(8,128)(2,1)} %bitcast.177), custom_call_target="tpu_custom_call" | custom-call | flops 1073741824 | bytes 5767168 | tf_op jit(solution)/shard_map/pallas_call | solution.py:42
  133.1 3.4 %collective-permute-start.7 = (bf16[32,1024]{1,0:T(8,128)(2,1)S(1)}, bf16[32,1024]{1,0:T(8,128)(2,1)S(1)}, u32[]{:S(2)}, u32[]{:S(2)}) collective-permute-start(bf16[32,1024]{1,0:T(8,128)(2,1)S(1)} %add_convert_fusion), channel_id=1, source_target_pairs={{0,8},{1,9},{2,10},{3,11},{4,12},{5,13},{6,14},{7,15},{8,0},{9,1},... | collective-permute-start | bytes 196616 | tf_op jit(solution)/shard_map/ppermute | solution.py:15
  136.5 6.0 %shard_map.181 = f32[4,512,256]{2,1,0:T(8,128)} custom-call(s32[4]{0:T(128)} %broadcast_xor_fusion.table_ref, s32[1]{0:T(128)} %bitcast.37.limit_ref, bf16[1,256,1024]{2,1,0:T(8,128)(2,1)} %bitcast.186, bf16[8,512,1024]{2,1,0:T(8,128)(2,1)} %bitcast.178), custom_call_target="tpu_custom_call" | custom-call | flops 1073741824 | bytes 5767168 | tf_op jit(solution)/shard_map/pallas_call | solution.py:42
  143.7 1.2 copy-done.3
  144.9 1.5 convert_add_fusion.2
  146.5 0.6 collective-permute-start.9
  147.1 1.5 convert_add_fusion.3
  148.8 1.5 collective-permute-start.1
  150.3 1.5 convert_add_fusion.1
  151.8 0.7 collective-permute-start.11
  152.9 1.5 collective-permute-start.13
  154.4 7.1 %collective-permute-done.9 = bf16[2,512,256]{2,1,0:T(8,128)(2,1)S(1)} collective-permute-done((bf16[2,512,256]{2,1,0:T(8,128)(2,1)S(1)}, bf16[2,512,256]{2,1,0:T(8,128)(2,1)S(1)}, u32[]{:S(2)}, u32[]{:S(2)}) %collective-permute-start.9) | collective-permute-done | bytes 524320 | tf_op jit(solution)/shard_map/ppermute | solution.py:15
  161.9 1.8 collective-permute-done.1
  164.1 7.5 %collective-permute-done.11 = bf16[2,512,256]{2,1,0:T(8,128)(2,1)S(1)} collective-permute-done((bf16[2,512,256]{2,1,0:T(8,128)(2,1)S(1)}, bf16[2,512,256]{2,1,0:T(8,128)(2,1)S(1)}, u32[]{:S(2)}, u32[]{:S(2)}) %collective-permute-start.11) | collective-permute-done | bytes 524320 | tf_op jit(solution)/shard_map/ppermute | solution.py:15
  172.3 0.3 fusion.24
  172.9 0.5 collective-permute-start.16
  173.4 1.4 collective-permute-start.15
  174.9 0.5 collective-permute-start.17
  175.4 1.4 collective-permute-start.18
  176.8 1.1 fusion.2
  177.9 3.1 %collective-permute-done.16.refs_3_ = bf16[512,256]{1,0:T(8,128)(2,1)S(1)} collective-permute-done((bf16[512,256]{1,0:T(8,128)(2,1)S(1)}, bf16[512,256]{1,0:T(8,128)(2,1)S(1)}, u32[]{:S(2)}, u32[]{:S(2)}) %collective-permute-start.16) | collective-permute-done | bytes 262176 | tf_op jit(solution)/shard_map/ppermute | solution.py:25
  181.0 5.6 %collective-permute-done.15.refs_2_ = bf16[512,256]{1,0:T(8,128)(2,1)S(1)} collective-permute-done((bf16[512,256]{1,0:T(8,128)(2,1)S(1)}, bf16[512,256]{1,0:T(8,128)(2,1)S(1)}, u32[]{:S(2)}, u32[]{:S(2)}) %collective-permute-start.15) | collective-permute-done | bytes 262176 | tf_op jit(solution)/shard_map/ppermute | solution.py:25
  186.6 5.6 %collective-permute-done.17.refs_4_ = bf16[512,256]{1,0:T(8,128)(2,1)S(1)} collective-permute-done((bf16[512,256]{1,0:T(8,128)(2,1)S(1)}, bf16[512,256]{1,0:T(8,128)(2,1)S(1)}, u32[]{:S(2)}, u32[]{:S(2)}) %collective-permute-start.17) | collective-permute-done | bytes 262176 | tf_op jit(solution)/shard_map/ppermute | solution.py:25
  192.2 5.6 %collective-permute-done.18.refs_5_ = bf16[512,256]{1,0:T(8,128)(2,1)S(1)} collective-permute-done((bf16[512,256]{1,0:T(8,128)(2,1)S(1)}, bf16[512,256]{1,0:T(8,128)(2,1)S(1)}, u32[]{:S(2)}, u32[]{:S(2)}) %collective-permute-start.18) | collective-permute-done | bytes 262176 | tf_op jit(solution)/shard_map/ppermute | solution.py:25
  197.9 0.7 copy-done.17
  198.5 0.4 copy-done.13
  198.9 2.9 %shard_map.183 = bf16[2,512,512]{2,1,0:T(8,128)(2,1)} custom-call(s32[1]{0:T(128)} %bitcast.refs_0_, bf16[4,512,256]{2,1,0:T(8,128)(2,1)} %copy-done.13, bf16[512,256]{1,0:T(8,128)(2,1)} %copy-done.15, bf16[512,256]{1,0:T(8,128)(2,1)} %copy-done.14, bf16[512,256]{1,0:T(8,128)(2,1)} %copy-done.16, bf16[512,256]{1,0:T(8,128)(2,1)} %copy-done.17), custom_call_target="tpu_custom_call" | custom-call | tf_op jit(solution)/shard_map/pallas_call | solution.py:77
  (109 shorter events, 5.7 us)
Async XLA Ops:
  0.6 17.1 %copy-start = (bf16[1,8,64,512]{3,2,1,0:T(8,128)(2,1)S(1)}, bf16[1,8,64,512]{3,2,1,0:T(8,128)(2,1)}, u32[]{:S(2)}) copy-start(bf16[1,8,64,512]{3,2,1,0:T(8,128)(2,1)} %param.20) | copy-start | bytes 1572868
  11.8 6.0 %copy-start.19 = (bf16[1,2,32,64]{3,2,1,0:T(8,128)(2,1)S(1)}, bf16[1,2,32,64]{3,2,1,0:T(8,128)(2,1)}, u32[]{:S(2)}) copy-start(bf16[1,2,32,64]{3,2,1,0:T(8,128)(2,1)} %param.18) | copy-start | bytes 24580
  11.8 9.0 %copy-start.1 = (bf16[1,1,2,256,1024]{4,3,2,1,0:T(8,128)(2,1)S(1)}, bf16[1,1,2,256,1024]{4,3,2,1,0:T(8,128)(2,1)}, u32[]{:S(2)}) copy-start(bf16[1,1,2,256,1024]{4,3,2,1,0:T(8,128)(2,1)} %param.16) | copy-start | bytes 3145732
  17.7 9.1 %copy-start.18 = (s32[1,2,4]{2,1,0:T(2,128)S(1)}, s32[1,2,4]{2,1,0:T(2,128)}, u32[]{:S(2)}) copy-start(s32[1,2,4]{2,1,0:T(2,128)} %param.22) | copy-start | bytes 100
  17.7 22.2 %copy-start.21 = (s32[4]{0:T(128)S(1)}, s32[4]{0:T(128)}, u32[]{:S(2)}) copy-start(s32[4]{0:T(128)} %constant.93.clone) | copy-start | bytes 52
  17.7 22.7 %copy-start.20 = (s32[4]{0:T(128)S(1)}, s32[4]{0:T(128)}, u32[]{:S(2)}) copy-start(s32[4]{0:T(128)} %constant.94.clone) | copy-start | bytes 52
  17.7 28.1 %collective-permute-start.19 = (bf16[2,32,64]{2,1,0:T(8,128)(2,1)S(1)}, bf16[2,32,64]{2,1,0:T(8,128)(2,1)S(1)}, u32[]{:S(2)}, u32[]{:S(2)}) collective-permute-start(bf16[2,32,64]{2,1,0:T(8,128)(2,1)S(1)} %bitcast.204), channel_id=1, source_target_pairs={{0,1},{1,0},{2,3},{3,2},{4,5},{5,4},{6,7},{7,6},{8,9},{9,8},{10,11... | collective-permute-start | bytes 24584 | tf_op jit(solution)/shard_map/ppermute | solution.py:15
  21.8 59.5 %collective-permute-start.2 = (bf16[256,1024]{1,0:T(8,128)(2,1)}, bf16[256,1024]{1,0:T(8,128)(2,1)S(1)}, u32[]{:S(2)}, u32[]{:S(2)}) collective-permute-start(bf16[256,1024]{1,0:T(8,128)(2,1)} %get-tuple-element.17), channel_id=1, source_target_pairs={{0,8},{1,9},{2,10},{3,11},{4,12},{5,13},{6,14},{7,15},{8,0},{9,1},... | collective-permute-start | bytes 1572872 | tf_op jit(solution)/shard_map/ppermute | solution.py:15
  24.4 58.5 %collective-permute-start.3 = (bf16[256,1024]{1,0:T(8,128)(2,1)}, bf16[256,1024]{1,0:T(8,128)(2,1)S(1)}, u32[]{:S(2)}, u32[]{:S(2)}) collective-permute-start(bf16[256,1024]{1,0:T(8,128)(2,1)} %get-tuple-element.18), channel_id=1, source_target_pairs={{0,8},{1,9},{2,10},{3,11},{4,12},{5,13},{6,14},{7,15},{8,0},{9,1},... | collective-permute-start | bytes 1572872 | tf_op jit(solution)/shard_map/ppermute | solution.py:15
  24.7 122.4 %collective-permute-start = (bf16[4,512,256]{2,1,0:T(8,128)(2,1)}, bf16[4,512,256]{2,1,0:T(8,128)(2,1)}, u32[]{:S(2)}, u32[]{:S(2)}) collective-permute-start(bf16[4,512,256]{2,1,0:T(8,128)(2,1)} %shard_map.176), channel_id=1, source_target_pairs={{0,1},{1,0},{2,3},{3,2},{4,5},{5,4},{6,7},{7,6},{8,9},{9,8},{10,11... | collective-permute-start | bytes 3145736 | tf_op jit(solution)/shard_map/ppermute | solution.py:15
  24.9 118.8 %collective-permute-start.8 = (bf16[4,512,256]{2,1,0:T(8,128)(2,1)}, bf16[4,512,256]{2,1,0:T(8,128)(2,1)}, u32[]{:S(2)}, u32[]{:S(2)}) collective-permute-start(bf16[4,512,256]{2,1,0:T(8,128)(2,1)} %shard_map.177), channel_id=1, source_target_pairs={{0,2},{1,3},{2,0},{3,1},{4,6},{5,7},{6,4},{7,5},{8,10},{9,11},{10,... | collective-permute-start | bytes 3145736 | tf_op jit(solution)/shard_map/ppermute | solution.py:15
  45.9 6.3 %collective-permute-start.20 = (bf16[2,64,64]{2,1,0:T(8,128)(2,1)S(1)}, bf16[2,64,64]{2,1,0:T(8,128)(2,1)S(1)}, u32[]{:S(2)}, u32[]{:S(2)}) collective-permute-start(bf16[2,64,64]{2,1,0:T(8,128)(2,1)S(1)} %maximum_select_fusion.2), channel_id=1, source_target_pairs={{0,2},{1,3},{2,0},{3,1},{4,6},{5,7},{6,4},{7,5},{8,10},{9,11},{10,... | collective-permute-start | bytes 49160 | tf_op jit(solution)/shard_map/ppermute | solution.py:15
  52.2 21.3 %copy-start.2 = (bf16[1,1,2,256,1024]{4,3,2,1,0:T(8,128)(2,1)S(1)}, bf16[1,1,2,256,1024]{4,3,2,1,0:T(8,128)(2,1)}, u32[]{:S(2)}) copy-start(bf16[1,1,2,256,1024]{4,3,2,1,0:T(8,128)(2,1)} %param.16) | copy-start | bytes 3145732
  52.2 19.2 %collective-permute-start.21 = (bf16[2,128,64]{2,1,0:T(8,128)(2,1)S(1)}, bf16[2,128,64]{2,1,0:T(8,128)(2,1)S(1)}, u32[]{:S(2)}, u32[]{:S(2)}) collective-permute-start(bf16[2,128,64]{2,1,0:T(8,128)(2,1)S(1)} %maximum_select_fusion.1), channel_id=1, source_target_pairs={{0,4},{1,5},{2,6},{3,7},{4,0},{5,1},{6,2},{7,3},{8,12},{9,13},{10,... | collective-permute-start | bytes 98312 | tf_op jit(solution)/shard_map/ppermute | solution.py:15
  71.9 9.2 %collective-permute-start.22 = (bf16[2,256,32]{2,1,0:T(8,128)(2,1)S(1)}, bf16[2,256,32]{2,1,0:T(8,128)(2,1)S(1)}, u32[]{:S(2)}, u32[]{:S(2)}) collective-permute-start(bf16[2,256,32]{2,1,0:T(8,128)(2,1)S(1)} %constant_dynamic-slice_fusion), channel_id=1, source_target_pairs={{0,8},{1,9},{2,10},{3,11},{4,12},{5,13},{6,14},{7,15},{8,0},{9,1},... | collective-permute-start | bytes 98312 | tf_op jit(solution)/shard_map/ppermute | solution.py:15
  81.3 3.8 %copy-start.7 = (bf16[256,1024]{1,0:T(8,128)(2,1)}, bf16[256,1024]{1,0:T(8,128)(2,1)S(1)}, u32[]{:S(2)}) copy-start(bf16[256,1024]{1,0:T(8,128)(2,1)S(1)} %collective-permute-done.2) | copy-start | bytes 1572868
  82.9 8.0 %copy-start.9 = (bf16[256,1024]{1,0:T(8,128)(2,1)}, bf16[256,1024]{1,0:T(8,128)(2,1)S(1)}, u32[]{:S(2)}) copy-start(bf16[256,1024]{1,0:T(8,128)(2,1)S(1)} %collective-permute-done.3) | copy-start | bytes 1572868
  84.5 15.5 %collective-permute-start.4 = (f32[32,1024]{1,0:T(8,128)S(1)}, f32[32,1024]{1,0:T(8,128)S(1)}, u32[]{:S(2)}, u32[]{:S(2)}) collective-permute-start(f32[32,1024]{1,0:T(8,128)S(1)} %pad_maximum_fusion.1), channel_id=1, source_target_pairs={{0,1},{1,0},{2,3},{3,2},{4,5},{5,4},{6,7},{7,6},{8,9},{9,8},{10,11... | collective-permute-start | bytes 393224 | tf_op jit(solution)/shard_map/ppermute | solution.py:15
  90.9 59.3 %collective-permute-start.10 = (bf16[4,512,256]{2,1,0:T(8,128)(2,1)}, bf16[4,512,256]{2,1,0:T(8,128)(2,1)}, u32[]{:S(2)}, u32[]{:S(2)}) collective-permute-start(bf16[4,512,256]{2,1,0:T(8,128)(2,1)} %shard_map.180), channel_id=1, source_target_pairs={{0,1},{1,0},{2,3},{3,2},{4,5},{5,4},{6,7},{7,6},{8,9},{9,8},{10,11... | collective-permute-start | bytes 3145736 | tf_op jit(solution)/shard_map/ppermute | solution.py:15
  92.5 8.3 %copy-start.10 = (bf16[256,1024]{1,0:T(8,128)(2,1)S(1)}, bf16[256,1024]{1,0:T(8,128)(2,1)}, u32[]{:S(2)}) copy-start(bf16[256,1024]{1,0:T(8,128)(2,1)} %copy-done.9) | copy-start | bytes 1572868
  98.6 27.3 %copy-start.8 = (bf16[256,1024]{1,0:T(8,128)(2,1)S(1)}, bf16[256,1024]{1,0:T(8,128)(2,1)}, u32[]{:S(2)}) copy-start(bf16[256,1024]{1,0:T(8,128)(2,1)} %copy-done.7) | copy-start | bytes 1572868
  98.6 27.3 %copy-start.11 = (f32[256,1024]{1,0:T(8,128)S(1)}, f32[256,1024]{1,0:T(8,128)}, u32[]{:S(2)}) copy-start(f32[256,1024]{1,0:T(8,128)} %convolution_add_fusion.1) | copy-start | bytes 3145732
  98.6 53.9 %collective-permute-start.12 = (bf16[4,512,256]{2,1,0:T(8,128)(2,1)}, bf16[4,512,256]{2,1,0:T(8,128)(2,1)S(1)}, u32[]{:S(2)}, u32[]{:S(2)}) collective-permute-start(bf16[4,512,256]{2,1,0:T(8,128)(2,1)} %shard_map.182), channel_id=1, source_target_pairs={{0,2},{1,3},{2,0},{3,1},{4,6},{5,7},{6,4},{7,5},{8,10},{9,11},{10,... | collective-permute-start | bytes 3145736 | tf_op jit(solution)/shard_map/ppermute | solution.py:15
  100.1 25.3 %collective-permute-start.5 = (f32[32,1024]{1,0:T(8,128)S(1)}, f32[32,1024]{1,0:T(8,128)S(1)}, u32[]{:S(2)}, u32[]{:S(2)}) collective-permute-start(f32[32,1024]{1,0:T(8,128)S(1)} %fusion.46), channel_id=1, source_target_pairs={{0,2},{1,3},{2,0},{3,1},{4,6},{5,7},{6,4},{7,5},{8,10},{9,11},{10,... | collective-permute-start | bytes 393224 | tf_op jit(solution)/shard_map/ppermute | solution.py:15
  125.4 7.7 %collective-permute-start.6 = (f32[32,1024]{1,0:T(8,128)S(1)}, f32[32,1024]{1,0:T(8,128)S(1)}, u32[]{:S(2)}, u32[]{:S(2)}) collective-permute-start(f32[32,1024]{1,0:T(8,128)S(1)} %add.137), channel_id=1, source_target_pairs={{0,4},{1,5},{2,6},{3,7},{4,0},{5,1},{6,2},{7,3},{8,12},{9,13},{10,... | collective-permute-start | bytes 393224 | tf_op jit(solution)/shard_map/ppermute | solution.py:15
  133.1 9.6 %copy-start.12 = (bf16[1,512,512]{2,1,0:T(8,128)(2,1)S(1)}, bf16[1,512,512]{2,1,0:T(8,128)(2,1)}, u32[]{:S(2)}) copy-start(bf16[1,512,512]{2,1,0:T(8,128)(2,1)} %get-tuple-element.16) | copy-start | bytes 1572868
  133.1 9.5 %collective-permute-start.7 = (bf16[32,1024]{1,0:T(8,128)(2,1)S(1)}, bf16[32,1024]{1,0:T(8,128)(2,1)S(1)}, u32[]{:S(2)}, u32[]{:S(2)}) collective-permute-start(bf16[32,1024]{1,0:T(8,128)(2,1)S(1)} %add_convert_fusion), channel_id=1, source_target_pairs={{0,8},{1,9},{2,10},{3,11},{4,12},{5,13},{6,14},{7,15},{8,0},{9,1},... | collective-permute-start | bytes 196616 | tf_op jit(solution)/shard_map/ppermute | solution.py:15
  143.3 1.6 copy-start.3
  143.7 3.4 %copy-start.4 = (f32[4,512,256]{2,1,0:T(8,128)S(1)}, f32[4,512,256]{2,1,0:T(8,128)}, u32[]{:S(2)}) copy-start(f32[4,512,256]{2,1,0:T(8,128)} %shard_map.175) | copy-start | bytes 6291460
  146.5 3.8 %copy-start.5 = (f32[4,512,256]{2,1,0:T(8,128)S(1)}, f32[4,512,256]{2,1,0:T(8,128)}, u32[]{:S(2)}) copy-start(f32[4,512,256]{2,1,0:T(8,128)} %shard_map.179) | copy-start | bytes 6291460
  146.5 14.9 %collective-permute-start.9 = (bf16[2,512,256]{2,1,0:T(8,128)(2,1)S(1)}, bf16[2,512,256]{2,1,0:T(8,128)(2,1)S(1)}, u32[]{:S(2)}, u32[]{:S(2)}) collective-permute-start(bf16[2,512,256]{2,1,0:T(8,128)(2,1)S(1)} %slice.256), channel_id=1, source_target_pairs={{0,1},{1,0},{2,3},{3,2},{4,5},{5,4},{6,7},{7,6},{8,9},{9,8},{10,11... | collective-permute-start | bytes 1572872 | tf_op jit(solution)/shard_map/ppermute | solution.py:15
  148.7 3.8 %copy-start.6 = (f32[4,512,256]{2,1,0:T(8,128)S(1)}, f32[4,512,256]{2,1,0:T(8,128)}, u32[]{:S(2)}) copy-start(f32[4,512,256]{2,1,0:T(8,128)} %shard_map.181) | copy-start | bytes 6291460
  148.8 14.9 %collective-permute-start.1 = (bf16[2,512,256]{2,1,0:T(8,128)(2,1)S(1)}, bf16[2,512,256]{2,1,0:T(8,128)(2,1)S(1)}, u32[]{:S(2)}, u32[]{:S(2)}) collective-permute-start(bf16[2,512,256]{2,1,0:T(8,128)(2,1)S(1)} %slice.257), channel_id=1, source_target_pairs={{0,2},{1,3},{2,0},{3,1},{4,6},{5,7},{6,4},{7,5},{8,10},{9,11},{10,... | collective-permute-start | bytes 1572872 | tf_op jit(solution)/shard_map/ppermute | solution.py:15
  151.8 19.8 %collective-permute-start.11 = (bf16[2,512,256]{2,1,0:T(8,128)(2,1)S(1)}, bf16[2,512,256]{2,1,0:T(8,128)(2,1)S(1)}, u32[]{:S(2)}, u32[]{:S(2)}) collective-permute-start(bf16[2,512,256]{2,1,0:T(8,128)(2,1)S(1)} %slice.255), channel_id=1, source_target_pairs={{0,2},{1,3},{2,0},{3,1},{4,6},{5,7},{6,4},{7,5},{8,10},{9,11},{10,... | collective-permute-start | bytes 1572872 | tf_op jit(solution)/shard_map/ppermute | solution.py:15
  152.9 19.3 %collective-permute-start.13 = (bf16[2,512,256]{2,1,0:T(8,128)(2,1)S(1)}, bf16[2,512,256]{2,1,0:T(8,128)(2,1)S(1)}, u32[]{:S(2)}, u32[]{:S(2)}) collective-permute-start(bf16[2,512,256]{2,1,0:T(8,128)(2,1)S(1)} %slice.254), channel_id=1, source_target_pairs={{0,1},{1,0},{2,3},{3,2},{4,5},{5,4},{6,7},{7,6},{8,9},{9,8},{10,11... | collective-permute-start | bytes 1572872 | tf_op jit(solution)/shard_map/ppermute | solution.py:15
  172.8 25.0 %collective-permute-start.14 = (bf16[4,512,256]{2,1,0:T(8,128)(2,1)S(1)}, bf16[4,512,256]{2,1,0:T(8,128)(2,1)S(1)}, u32[]{:S(2)}, u32[]{:S(2)}) collective-permute-start(bf16[4,512,256]{2,1,0:T(8,128)(2,1)S(1)} %pad_maximum_fusion), channel_id=1, source_target_pairs={{0,16},{1,17},{2,18},{3,19},{4,20},{5,21},{6,22},{7,23},{8,24},{9,... | collective-permute-start | bytes 3145736 | tf_op jit(solution)/shard_map/ppermute | solution.py:25
  172.9 8.0 %collective-permute-start.16 = (bf16[512,256]{1,0:T(8,128)(2,1)S(1)}, bf16[512,256]{1,0:T(8,128)(2,1)S(1)}, u32[]{:S(2)}, u32[]{:S(2)}) collective-permute-start(bf16[512,256]{1,0:T(8,128)(2,1)S(1)} %fusion.26), channel_id=1, source_target_pairs={{0,20},{1,21},{2,22},{3,23},{4,16},{5,17},{6,18},{7,19},{8,28},{9,... | collective-permute-start | bytes 786440 | tf_op jit(solution)/shard_map/ppermute | solution.py:25
  173.4 13.2 %collective-permute-start.15 = (bf16[512,256]{1,0:T(8,128)(2,1)S(1)}, bf16[512,256]{1,0:T(8,128)(2,1)S(1)}, u32[]{:S(2)}, u32[]{:S(2)}) collective-permute-start(bf16[512,256]{1,0:T(8,128)(2,1)S(1)} %fusion.25), channel_id=1, source_target_pairs={{0,20},{1,21},{2,22},{3,23},{4,16},{5,17},{6,18},{7,19},{8,28},{9,... | collective-permute-start | bytes 786440 | tf_op jit(solution)/shard_map/ppermute | solution.py:25
  174.9 17.3 %collective-permute-start.17 = (bf16[512,256]{1,0:T(8,128)(2,1)S(1)}, bf16[512,256]{1,0:T(8,128)(2,1)S(1)}, u32[]{:S(2)}, u32[]{:S(2)}) collective-permute-start(bf16[512,256]{1,0:T(8,128)(2,1)S(1)} %fusion.27), channel_id=1, source_target_pairs={{0,20},{1,21},{2,22},{3,23},{4,16},{5,17},{6,18},{7,19},{8,28},{9,... | collective-permute-start | bytes 786440 | tf_op jit(solution)/shard_map/ppermute | solution.py:25
  175.4 22.4 %collective-permute-start.18 = (bf16[512,256]{1,0:T(8,128)(2,1)S(1)}, bf16[512,256]{1,0:T(8,128)(2,1)S(1)}, u32[]{:S(2)}, u32[]{:S(2)}) collective-permute-start(bf16[512,256]{1,0:T(8,128)(2,1)S(1)} %fusion.28), channel_id=1, source_target_pairs={{0,20},{1,21},{2,22},{3,23},{4,16},{5,17},{6,18},{7,19},{8,28},{9,... | collective-permute-start | bytes 786440 | tf_op jit(solution)/shard_map/ppermute | solution.py:25
  181.0 16.9 %copy-start.14 = (bf16[512,256]{1,0:T(8,128)(2,1)}, bf16[512,256]{1,0:T(8,128)(2,1)S(1)}, u32[]{:S(2)}) copy-start(bf16[512,256]{1,0:T(8,128)(2,1)S(1)} %collective-permute-done.16.refs_3_) | copy-start | bytes 786436
  186.6 11.3 %copy-start.15 = (bf16[512,256]{1,0:T(8,128)(2,1)}, bf16[512,256]{1,0:T(8,128)(2,1)S(1)}, u32[]{:S(2)}) copy-start(bf16[512,256]{1,0:T(8,128)(2,1)S(1)} %collective-permute-done.15.refs_2_) | copy-start | bytes 786436
  192.2 5.6 %copy-start.16 = (bf16[512,256]{1,0:T(8,128)(2,1)}, bf16[512,256]{1,0:T(8,128)(2,1)S(1)}, u32[]{:S(2)}) copy-start(bf16[512,256]{1,0:T(8,128)(2,1)S(1)} %collective-permute-done.17.refs_4_) | copy-start | bytes 786436
  197.8 0.7 copy-start.17
  197.8 1.1 copy-start.13

commit v3 on v0

v3 whole, which is shorter than its diff:
```python
import functools

import jax
import jax.numpy as jnp
from jax import lax
from jax.experimental import pallas as pl
from jax.experimental.pallas import tpu as pltpu
from jax.sharding import PartitionSpec as P

SEG = 128
BF16 = jnp.bfloat16
F32 = jnp.float32
SMEM = pl.BlockSpec(memory_space=pltpu.SMEM)
VMEM = pl.BlockSpec(memory_space=pltpu.VMEM)
NT = (((1,), (1,)), ((), ()))
TN = (((0,), (0,)), ((), ()))


def partner(value, mask):
    pairs = [(source, source ^ mask) for source in range(lax.axis_size("tensor"))]
    return lax.ppermute(value, "tensor", pairs)


def relay(value, mask):
    sections, tiles = lax.axis_size("pipe"), lax.axis_size("tensor")
    pairs = [
        (p * tiles + t, (p - 1) % sections * tiles + (t ^ mask))
        for p in range(sections)
        for t in range(tiles)
    ]
    return lax.ppermute(value, ("pipe", "tensor"), pairs)


def segment_of(high, piece, tile_rows):
    k, _, offset = piece
    return ((high ^ k) * tile_rows + offset) // SEG


def product_body(low_size, tile_rows, pieces, tiles, subs, *refs):
    pos_ref, classes_ref, live_ref = refs[:3]
    grad_refs = refs[3 : 3 + tiles]
    weight_refs = refs[3 + tiles : 3 + tiles + subs]
    up_ref = refs[3 + tiles + subs]
    sent_x, kept_x, sent_y, kept_y, rank_ref, rows_ref = refs[4 + tiles + subs :]
    step = pl.program_id(0)
    high = pos_ref[0] // low_size
    size = pieces[0][3]
    half = rows_ref.shape[0] // 2

    @pl.when(step == 0)
    def _():
        for at, (tile, index, piece, _) in enumerate(pieces):
            seg = segment_of(high, piece, tile_rows)
            alive = seg < live_ref[piece[1]]
            place = slice(at * size, (at + 1) * size)

            @pl.when(alive)
            def _():
                rows = grad_refs[tile][index, piece[2] : piece[2] + size, :]
                rows_ref[place, :] = rows
                up = up_ref[classes_ref[piece[1], seg]]
                rank_ref[:, place] = lax.dot_general(up, rows, NT, preferred_element_type=F32)

            @pl.when(jnp.logical_not(alive))
            def _():
                rows_ref[place, :] = jnp.zeros((size, rows_ref.shape[1]), rows_ref.dtype)
                rank_ref[:, place] = jnp.zeros((rank_ref.shape[0], size), F32)

    for sub, weight_ref in enumerate(weight_refs):
        width = weight_ref.shape[1]
        columns = slice(sub * width, (sub + 1) * width)
        value = lax.dot_general(rows_ref[...], weight_ref[0], NT, preferred_element_type=F32)

        @pl.when(step < 4)
        def _():
            sent_x[0, :, columns] = value[:half].astype(BF16)

        @pl.when(step >= 4)
        def _():
            kept_x[0, :, columns] = value[:half]

        @pl.when(step & 2 == 0)
        def _():
            sent_y[0, :, columns] = value[half:].astype(BF16)

        @pl.when(step & 2 != 0)
        def _():
            kept_y[0, :, columns] = value[half:]


def product(scalars, grads, pieces, weight_blocks, up_tile, low_size):
    blocks, width, depth = weight_blocks.shape
    tile_rows = grads[0].shape[1]
    rows = len(pieces) * pieces[0][3]
    half = rows // 2
    subs = 2 if width % 512 == 0 else 1

    def block_of(k):
        return 1 - k // 4 + (2 - (k & 2)) + 4 * (k & 1)

    def whole(array):
        return pl.BlockSpec(array.shape, lambda k, *_: (0,) * array.ndim)

    def weight_spec(sub):
        return pl.BlockSpec(
            (1, width // subs, depth), lambda k, pos, *_: (block_of(k) ^ (pos[0] % low_size), sub, 0)
        )

    def slot(place):
        return pl.BlockSpec((1, half, width), lambda k, *_: (place(k), 0, 0))

    def by_y(k):
        return 2 - (k & 2) + (k & 1)

    outs = [
        (BF16, lambda k: jnp.where(k < 4, by_y(k), 1)),
        (F32, lambda k: jnp.where(k < 4, 2, by_y(k))),
        (BF16, lambda k: 2 * (1 - k // 4) + jnp.where(k & 2 == 0, k & 1, 1)),
        (F32, lambda k: 2 * (1 - k // 4) + jnp.where(k & 2 == 0, 0, k & 1)),
    ]
    rank_part = up_tile.shape[1]
    return pl.pallas_call(
        functools.partial(product_body, low_size, tile_rows, pieces, len(grads), subs),
        grid_spec=pltpu.PrefetchScalarGridSpec(
            num_scalar_prefetch=3,
            grid=(blocks,),
            in_specs=[whole(g) for g in grads]
            + [weight_spec(sub) for sub in range(subs)]
            + [whole(up_tile)],
            out_specs=[slot(place) for _, place in outs]
            + [pl.BlockSpec((rank_part, rows), lambda k, *_: (0, 0))],
            scratch_shapes=[pltpu.VMEM((rows, depth), BF16)],
        ),
        out_shape=[jax.ShapeDtypeStruct((blocks // 2, half, width), dtype) for dtype, _ in outs]
        + [jax.ShapeDtypeStruct((rank_part, rows), F32)],
        cost_estimate=pl.CostEstimate(
            flops=2 * blocks * rows * width * depth,
            bytes_accessed=2 * blocks * width * depth + 8 * blocks * rows * width,
            transcendentals=0,
        ),
    )(*scalars, *grads, *([weight_blocks] * subs), up_tile)


def up_body(low_size, tile_rows, pieces, tiles, *refs):
    pos_ref, classes_ref, live_ref = refs[:3]
    grad_refs = refs[3 : 3 + tiles]
    hidden_refs = refs[3 + tiles : -2]
    out_ref, total_ref = refs[-2:]
    high = pos_ref[0] // low_size
    total_ref[...] = jnp.zeros_like(total_ref)
    for tile, index, piece, size in pieces:
        k, m, offset = piece
        seg = segment_of(high, piece, tile_rows)

        @pl.when(seg < live_ref[m])
        def _():
            total_ref[classes_ref[m, seg]] += lax.dot_general(
                hidden_refs[k][m, offset : offset + size, :],
                grad_refs[tile][index, offset : offset + size, :],
                TN,
                preferred_element_type=F32,
            )

    out_ref[...] = total_ref[...].astype(BF16)


def shards(
    output_gradient,
    forward_input,
    saved_rank_outputs,
    projection_weight,
    adapter_down_maps,
    adapter_up_maps,
    segment_adapter_class,
    live_segment_table,
):
    grad_tile = output_gradient[0, 0]
    micro_count, tile_rows, tile_cols = grad_tile.shape
    up_tile = adapter_up_maps[0, 0]
    class_count, rank_part, _ = up_tile.shape
    rank, portion = adapter_down_maps.shape[2:]
    tiles = lax.axis_size("tensor")
    low_size = min(tiles, 8)
    low_bits = low_size.bit_length() - 1
    high_size = tiles // low_size
    position = lax.axis_index("tensor")
    high = position // low_size
    weight_blocks = projection_weight[0, 0].reshape(low_size, portion, tile_cols)
    scalars = (position.astype(jnp.int32)[None], segment_adapter_class[0], live_segment_table[0])
    size = min(SEG, tile_rows)
    offsets = range(0, tile_rows, size)

    own_pieces = [(0, m, (0, m, o), size) for m in range(micro_count) for o in offsets]
    chunks = [([grad_tile], own_pieces)]
    for m in range(micro_count):
        got = [partner(grad_tile[m], k * low_size)[None] for k in range(1, high_size)]
        pieces = [(k - 1, 0, (k, m, o), size) for k in range(1, high_size) for o in offsets]
        chunks.append((got, pieces))
    order = [piece for _, pieces in chunks for _, _, piece, _ in pieces]

    hidden = saved_rank_outputs[0]
    sums, got_last, parts = [], [], []
    for grads, pieces in chunks:
        sent_x, kept_x, sent_y, kept_y, part = product(
            scalars, grads, pieces, weight_blocks, up_tile, low_size
        )
        parts.append(part)
        if not sums:
            sent_x, sent_y, hidden = lax.optimization_barrier((sent_x, sent_y, hidden))
        for bits, sent, kept in (((0, 1, 2), sent_x, kept_x), ((1, 0, 2), sent_y, kept_y)):
            got = partner(sent, 1 << bits[0])
            second = partner((kept[2:] + got[2:]).astype(BF16), 1 << bits[1])
            third = (kept[1] + got[1] + second[1]).astype(BF16)
            got_last.append(relay(third, 1 << bits[2]))
            sums.append((kept, got, second))

    for bit in range(low_bits):
        got = partner(hidden, 1 << bit)
        upper = (position >> bit) & 1 == 1
        hidden = jnp.where(
            upper, jnp.concatenate([got, hidden], 1), jnp.concatenate([hidden, got], 1)
        )
    hiddens = []
    for k in range(high_size):
        wanted = lax.dynamic_slice_in_dim(hidden, (high ^ k) * rank_part, rank_part, 2)
        hiddens.append(partner(wanted, k * low_size) if k > 0 else wanted)

    all_grads, all_pieces = [], []
    for grads, pieces in chunks:
        all_pieces += [(tile + len(all_grads), index, piece, size) for tile, index, piece, size in pieces]
        all_grads += grads
    up_map_gradient = pl.pallas_call(
        functools.partial(up_body, low_size, tile_rows, all_pieces, len(all_grads)),
        in_specs=[SMEM] * 3 + [VMEM] * (len(all_grads) + high_size),
        out_specs=VMEM,
        out_shape=jax.ShapeDtypeStruct(up_tile.shape, BF16),
        scratch_shapes=[pltpu.VMEM(up_tile.shape, F32)],
        cost_estimate=pl.CostEstimate(
            flops=2 * len(order) * size * rank_part * tile_cols,
            bytes_accessed=2 * len(order) * size * tile_cols,
            transcendentals=0,
        ),
    )(*scalars, *all_grads, *hiddens)

    own_rank = jnp.concatenate(parts, 1)
    for bit in range(low_bits):
        own_rank = own_rank + partner(own_rank, 1 << bit)
    own_rank = own_rank.astype(BF16)
    ranks = [own_rank] + [partner(own_rank, j * low_size) for j in range(1, high_size)]

    def columns_of(j, piece):
        k, m, offset = piece
        at = order.index((k ^ j, m, offset))
        return slice(at * size, (at + 1) * size)

    down_parts = adapter_down_maps[0].reshape(class_count, high_size, rank_part, portion)

    def adapter_kernel(pos_ref, classes_ref, live_ref, down_ref, *refs):
        rank_refs, sum_refs = refs[:high_size], refs[high_size:-2]
        out_ref, total_ref = refs[-2:]
        own = pos_ref[0] // low_size
        start = 0
        for g in range(len(sums)):
            kept_ref, got_ref, second_ref = sum_refs[3 * g : 3 * g + 3]
            count = kept_ref.shape[1]
            total_ref[start : start + count, :] = (
                kept_ref[0] + got_ref[0].astype(F32) + second_ref[0].astype(F32)
            )
            start += count
        for at, piece in enumerate(order):
            seg = segment_of(own, piece, tile_rows)
            rows = slice(at * size, (at + 1) * size)
            adapter = 0.0
            for j in range(high_size):
                adapter = adapter + lax.dot_general(
                    rank_refs[j][:, columns_of(j, piece)],
                    down_ref[classes_ref[piece[1], seg], own ^ j],
                    TN,
                    preferred_element_type=F32,
                )
            out_ref[rows, :] = (total_ref[rows, :] + adapter).astype(BF16)

    rows_total = len(order) * size
    kept = pl.pallas_call(
        adapter_kernel,
        grid=(1,),
        in_specs=[SMEM] * 3
        + [pl.BlockSpec(a.shape, lambda _, n=a.ndim: (0,) * n) for a in [down_parts, *ranks]]
        + [pl.BlockSpec((1,) + a.shape[1:], lambda _: (0, 0, 0)) for three in sums for a in three],
        out_specs=pl.BlockSpec((rows_total, portion), lambda _: (0, 0)),
        out_shape=jax.ShapeDtypeStruct((rows_total, portion), BF16),
        scratch_shapes=[pltpu.VMEM((rows_total, portion), F32)],
        compiler_params=pltpu.CompilerParams(vmem_limit_bytes=40 * 2**20),
        cost_estimate=pl.CostEstimate(
            flops=2 * rows_total * rank * portion,
            bytes_accessed=10 * rows_total * portion,
            transcendentals=0,
        ),
    )(*scalars, down_parts, *ranks, *[a for three in sums for a in three])
    kept = relay(kept, 0)

    def finish_kernel(pos_ref, kept_ref, *refs):
        got_refs, out_ref = refs[:-1], refs[-1]
        own = pos_ref[0] // low_size
        start, found = 0, []
        for got_ref in got_refs:
            for row in range(0, got_ref.shape[0], 16):
                found.append((got_ref, row))
        for at, (k, m, offset) in enumerate(order):
            base = pl.multiple_of((own ^ k) * tile_rows + offset, size)
            row = 0
            while row < size:
                got_ref, first = found[(at * size + row) // 16]
                count = min(size - row, got_ref.shape[0] - first)
                spot = at * size + row
                out_ref[m, pl.ds(base + row, count), :] = (
                    kept_ref[spot : spot + count, :].astype(F32)
                    + got_ref[first : first + count, :].astype(F32)
                ).astype(BF16)
                row += count

    grad_prev = pl.pallas_call(
        finish_kernel,
        in_specs=[SMEM] + [VMEM] * (1 + len(got_last)),
        out_specs=VMEM,
        out_shape=jax.ShapeDtypeStruct((micro_count, high_size * tile_rows, portion), BF16),
    )(scalars[0], kept, *got_last)

    def down_kernel(pos_ref, classes_ref, live_ref, inputs_ref, *refs):
        rank_refs, out_ref, total_ref = refs[:-2], refs[-2], refs[-1]
        own = pos_ref[0] // low_size
        total_ref[...] = jnp.zeros_like(total_ref)
        for piece in order:
            k, m, offset = piece
            seg = segment_of(own, piece, tile_rows)

            @pl.when(seg < live_ref[m])
            def _():
                base = pl.multiple_of((own ^ k) * tile_rows + offset, size)
                rows = inputs_ref[m, pl.ds(base, size), :]
                for j in range(high_size):
                    total_ref[classes_ref[m, seg], own ^ j] += jnp.dot(
                        rank_refs[j][:, columns_of(j, piece)], rows, preferred_element_type=F32
                    )

        out_ref[...] = total_ref[...].astype(BF16)

    down_map_gradient = pl.pallas_call(
        down_kernel,
        in_specs=[SMEM] * 3 + [VMEM] * (1 + high_size),
        out_specs=VMEM,
        out_shape=jax.ShapeDtypeStruct(down_parts.shape, BF16),
        scratch_shapes=[pltpu.VMEM(down_parts.shape, F32)],
        cost_estimate=pl.CostEstimate(
            flops=2 * rows_total * rank * portion,
            bytes_accessed=2 * rows_total * portion,
            transcendentals=0,
        ),
    )(*scalars, forward_input[0], *ranks)

    return (
        grad_prev[None],
        down_map_gradient.reshape(1, class_count, rank, portion),
        up_map_gradient[None, None],
    )


def solution(mesh):
    in_specs = (
        P("pipe", "tensor", None, None, None),
        P("pipe", None, None, "tensor"),
        P("pipe", None, "tensor", None),
        P("pipe", "tensor", None, None),
        P("pipe", None, None, "tensor"),
        P("pipe", "tensor", None, None, None),
        P("pipe", None, None),
        P("pipe", None),
    )
    out_specs = (
        P("pipe", None, None, "tensor"),
        P("pipe", None, None, "tensor"),
        P("pipe", "tensor", None, None, None),
    )
    return jax.shard_map(shards, mesh=mesh, in_specs=in_specs, out_specs=out_specs, check_vma=False)
```

time: 545 us -> 165 us (0.30)
  waiting for transfers between devices: 309 us -> 57.1 us
  blocking collectives: 149 us -> 0 us
  Pallas kernels: 0 us -> 54.6 us
  other arithmetic: 48.9 us -> 6.52 us
  starting transfers between devices: 7.44 us -> 37.2 us
  matrix products: 22.8 us -> 0 us
    ppermute x5 -> x29, waiting for transfers between devices: 309 us -> 57.1 us  [the longest x22 49.3 us: partner(): return lax.ppermute(value, 'tensor', pairs)]
    psum x1 -> x0, blocking collectives: 112 us -> none  [shards(): lowrank = lax.psum(padded_rank, 'tensor').astype(jnp.bfloat16)]
    pallas_call x0 -> x7, Pallas kernels: none -> 54.6 us  [the longest x3 42.2 us: product(): pl.pallas_call(functools.partial(product_body, low_size, tile_rows, piece...]
    all_gather x1 -> x0, blocking collectives: 36.9 us -> none  [shards(): hidden = lax.all_gather(saved_rank_outputs[0], 'tensor', axis=1, tiled=True)]
    ppermute x5 -> x29, starting transfers between devices: 7.44 us -> 37.2 us  [the longest x22 31.2 us: partner(): return lax.ppermute(value, 'tensor', pairs)]
    select_n x7 -> x3, other arithmetic: 28.4 us -> 1.53 us  [shards(): jnp.where(upper, jnp.concatenate([got, hidden], 1), jnp.concatenate([hidd...]
    dot_general x10 -> x0, matrix products: 22.8 us -> none  [the longest x2 14.6 us: project(): jnp.einsum('mrd,id->mri', rows_block, weight, preferred_element_type=jnp....]
    add x2, other arithmetic: 15.9 us -> 0.03 us  [shards(): own_rank = own_rank + partner(own_rank, 1 << bit)]
  transfers between devices with their start and end apart: 5 -> 29, of which waited for: 3 -> 11; matrix products, arithmetic and copies ran while one was open for 4% -> 6% of each run, Pallas kernels for 0% -> 32%
where the time goes in v3:
time: 165 us; the launch traced here: 164 us
  waiting for transfers between devices  57.1 us (35%)
  Pallas kernels  54.6 us (33%)
  starting transfers between devices  37.2 us (23%)
  local copies, waits for them, and re-layouts  7.35 us (4%)
  other arithmetic  6.52 us (4%)
    ppermute x22, waiting for transfers between devices, partner(): return lax.ppermute(value, 'tensor', pairs)  49.3 us
    pallas_call x3, Pallas kernels, product(): pl.pallas_call(functools.partial(product_body, low_size, tile_rows, piece...  42.2 us
    ppermute x22, starting transfers between devices, partner(): return lax.ppermute(value, 'tensor', pairs)  31.2 us
    ppermute x7, waiting for transfers between devices, relay(): return lax.ppermute(value, ('pipe', 'tensor'), pairs)  7.83 us
    ppermute x7, starting transfers between devices, relay(): return lax.ppermute(value, ('pipe', 'tensor'), pairs)  5.98 us
    unnamed x40, local copies, waits for them, and re-layouts  4.53 us
    pallas_call x1, Pallas kernels, shards(): pl.pallas_call(functools.partial(up_body, low_size, tile_rows, all_pieces...  3.66 us
  transfers between devices with their start and end apart: 29, of which 11 were waited for; matrix products, arithmetic and copies ran while one was open for 6% of the time, Pallas kernels for 32%

profile of v3, /device:TPU:0, one launch (start us, length us, event | category | flops | bytes accessed | tf_op | source)
XLA Modules:
  0.0 163.6 jit_solution(17458792662436845769)
XLA Ops:
  0.6 1.3 slice_bitcast_fusion
  1.9 4.1 %collective-permute-start = (bf16[256,1024]{1,0:T(8,128)(2,1)S(1)}, bf16[256,1024]{1,0:T(8,128)(2,1)S(1)}, u32[]{:S(2)}, u32[]{:S(2)}) collective-permute-start(bf16[256,1024]{1,0:T(8,128)(2,1)S(1)} %get-tuple-element.40), channel_id=1, source_target_pairs={{0,8},{1,9},{2,10},{3,11},{4,12},{5,13},{6,14},{7,15},{8,0},{9,1},... | collective-permute-start | bytes 1572872 | tf_op jit(solution)/shard_map/ppermute | solution.py:21
  6.0 0.1 collective-permute-start.1
  6.1 17.6 %shard_map.103 = (bf16[4,256,512]{2,1,0:T(8,128)(2,1)}, f32[4,256,512]{2,1,0:T(8,128)}, bf16[4,256,512]{2,1,0:T(8,128)(2,1)}, f32[4,256,512]{2,1,0:T(8,128)}, f32[32,512]{1,0:T(8,128)}) custom-call(s32[1]{0:T(128)} %bitcast.refs_0_.pos_ref, s32[2,4]{1,0:T(2,128)} %bitcast.31, s32[2]{0:T(128)} %bitcast.37, bf16[2,256,1024]{2,1,0:T(8,128)(2,1)} %bitcast.49, ...), custom_call_target="tpu_custom_call" | custom-call | flops 4294967296 | bytes 25165824 | tf_op jit(solution)/shard_map/pallas_call | solution.py:122
  23.7 1.8 %collective-permute-start.25 = (bf16[2,32,64]{2,1,0:T(8,128)(2,1)S(1)}, bf16[2,32,64]{2,1,0:T(8,128)(2,1)S(1)}, u32[]{:S(2)}, u32[]{:S(2)}) collective-permute-start(bf16[2,32,64]{2,1,0:T(8,128)(2,1)S(1)} %bitcast.62), channel_id=1, source_target_pairs={{0,1},{1,0},{2,3},{3,2},{4,5},{5,4},{6,7},{7,6},{8,9},{9,8},{10,11... | collective-permute-start | bytes 24584 | tf_op jit(solution)/shard_map/ppermute | solution.py:21
  25.5 1.5 collective-permute-start.8
  27.0 0.5 collective-permute-start.6
  27.5 0.8 constant_dynamic-update-slice_fusion.2
  28.4 12.9 %collective-permute-done = bf16[256,1024]{1,0:T(8,128)(2,1)S(1)} collective-permute-done((bf16[256,1024]{1,0:T(8,128)(2,1)S(1)}, bf16[256,1024]{1,0:T(8,128)(2,1)S(1)}, u32[]{:S(2)}, u32[]{:S(2)}) %collective-permute-start) | collective-permute-done | bytes 524320 | tf_op jit(solution)/shard_map/ppermute | solution.py:21
  41.2 0.8 copy-done.10
  42.0 12.3 %shard_map.104 = (bf16[4,128,512]{2,1,0:T(8,128)(2,1)}, f32[4,128,512]{2,1,0:T(8,128)}, bf16[4,128,512]{2,1,0:T(8,128)(2,1)}, f32[4,128,512]{2,1,0:T(8,128)}, f32[32,256]{1,0:T(8,128)}) custom-call(s32[1]{0:T(128)} %bitcast.refs_0_.pos_ref, s32[2,4]{1,0:T(2,128)} %bitcast.32, s32[2]{0:T(128)} %bitcast.38, bf16[1,256,1024]{2,1,0:T(8,128)(2,1)} %bitcast.54, ...), custom_call_target="tpu_custom_call" | custom-call | flops 2147483648 | bytes 16777216 | tf_op jit(solution)/shard_map/pallas_call | solution.py:122
  54.3 0.8 constant_dynamic-update-slice_fusion.1
  55.1 0.8 copy-done.11
  55.9 12.3 %shard_map.105 = (bf16[4,128,512]{2,1,0:T(8,128)(2,1)}, f32[4,128,512]{2,1,0:T(8,128)}, bf16[4,128,512]{2,1,0:T(8,128)(2,1)}, f32[4,128,512]{2,1,0:T(8,128)}, f32[32,256]{1,0:T(8,128)}) custom-call(s32[1]{0:T(128)} %bitcast.refs_0_.pos_ref, s32[2,4]{1,0:T(2,128)} %bitcast.33, s32[2]{0:T(128)} %bitcast.39, bf16[1,256,1024]{2,1,0:T(8,128)(2,1)} %bitcast.56, ...), custom_call_target="tpu_custom_call" | custom-call | flops 2147483648 | bytes 16777216 | tf_op jit(solution)/shard_map/pallas_call | solution.py:122
  68.2 0.8 constant_dynamic-update-slice_fusion
  69.0 1.8 %collective-permute-start.2 = (f32[32,1024]{1,0:T(8,128)S(1)}, f32[32,1024]{1,0:T(8,128)S(1)}, u32[]{:S(2)}, u32[]{:S(2)}) collective-permute-start(f32[32,1024]{1,0:T(8,128)S(1)} %constant_dynamic-update-slice_fusion), channel_id=1, source_target_pairs={{0,1},{1,0},{2,3},{3,2},{4,5},{5,4},{6,7},{7,6},{8,9},{9,8},{10,11... | collective-permute-start | bytes 393224 | tf_op jit(solution)/shard_map/ppermute | solution.py:21
  70.8 0.6 maximum_select_fusion.2
  71.4 1.5 collective-permute-start.26
  73.0 1.0 collective-permute-done.2
  74.0 1.9 %collective-permute-start.3 = (f32[32,1024]{1,0:T(8,128)S(1)}, f32[32,1024]{1,0:T(8,128)S(1)}, u32[]{:S(2)}, u32[]{:S(2)}) collective-permute-start(f32[32,1024]{1,0:T(8,128)S(1)} %add.82), channel_id=1, source_target_pairs={{0,2},{1,3},{2,0},{3,1},{4,6},{5,7},{6,4},{7,5},{8,10},{9,11},{10,... | collective-permute-start | bytes 393224 | tf_op jit(solution)/shard_map/ppermute | solution.py:21
  75.9 0.9 maximum_select_fusion.1
  76.9 2.1 %collective-permute-done.3 = f32[32,1024]{1,0:T(8,128)S(1)} collective-permute-done((f32[32,1024]{1,0:T(8,128)S(1)}, f32[32,1024]{1,0:T(8,128)S(1)}, u32[]{:S(2)}, u32[]{:S(2)}) %collective-permute-start.3) | collective-permute-done | bytes 131104 | tf_op jit(solution)/shard_map/ppermute | solution.py:21
  79.0 0.4 collective-permute-start.4
  79.4 1.7 %collective-permute-done.27 = bf16[2,128,64]{2,1,0:T(8,128)(2,1)S(1)} collective-permute-done((bf16[2,128,64]{2,1,0:T(8,128)(2,1)S(1)}, bf16[2,128,64]{2,1,0:T(8,128)(2,1)S(1)}, u32[]{:S(2)}, u32[]{:S(2)}) %collective-permute-start.27) | collective-permute-done | bytes 32800 | tf_op jit(solution)/shard_map/ppermute | solution.py:21
  81.1 0.8 constant_dynamic-slice_fusion
  81.9 1.5 collective-permute-start.10
  83.4 0.7 collective-permute-start.12
  84.2 1.7 %collective-permute-start.14 = (bf16[4,128,512]{2,1,0:T(8,128)(2,1)}, bf16[4,128,512]{2,1,0:T(8,128)(2,1)S(1)}, u32[]{:S(2)}, u32[]{:S(2)}) collective-permute-start(bf16[4,128,512]{2,1,0:T(8,128)(2,1)} %get-tuple-element.35), channel_id=1, source_target_pairs={{0,1},{1,0},{2,3},{3,2},{4,5},{5,4},{6,7},{7,6},{8,9},{9,8},{10,11... | collective-permute-start | bytes 1572872 | tf_op jit(solution)/shard_map/ppermute | solution.py:21
  85.9 1.6 collective-permute-start.16
  87.5 1.6 add_convert_fusion
  89.1 0.6 collective-permute-start.9
  89.8 0.2 add_convert_fusion.1
  89.9 7.1 %collective-permute-done.10.refs_9_ = bf16[4,128,512]{2,1,0:T(8,128)(2,1)S(1)} collective-permute-done((bf16[4,128,512]{2,1,0:T(8,128)(2,1)}, bf16[4,128,512]{2,1,0:T(8,128)(2,1)S(1)}, u32[]{:S(2)}, u32[]{:S(2)}) %collective-permute-start.10) | collective-permute-done | bytes 524320 | tf_op jit(solution)/shard_map/ppermute | solution.py:21
  97.0 1.3 collective-permute-start.7
  98.3 0.1 add_convert_fusion.7
  98.4 0.1 collective-permute-done.12.refs_12_
  98.5 0.7 collective-permute-start.11
  99.3 0.1 add_convert_fusion.6
  99.3 8.9 %collective-permute-done.14.refs_15_ = bf16[4,128,512]{2,1,0:T(8,128)(2,1)S(1)} collective-permute-done((bf16[4,128,512]{2,1,0:T(8,128)(2,1)}, bf16[4,128,512]{2,1,0:T(8,128)(2,1)S(1)}, u32[]{:S(2)}, u32[]{:S(2)}) %collective-permute-start.14) | collective-permute-done | bytes 524320 | tf_op jit(solution)/shard_map/ppermute | solution.py:21
  108.2 1.5 collective-permute-start.13
  109.7 0.1 add_convert_fusion.5
  109.8 0.8 collective-permute-start.15
  110.7 13.3 %collective-permute-done.11.refs_10_ = bf16[2,128,512]{2,1,0:T(8,128)(2,1)S(1)} collective-permute-done((bf16[2,128,512]{2,1,0:T(8,128)(2,1)S(1)}, bf16[2,128,512]{2,1,0:T(8,128)(2,1)S(1)}, u32[]{:S(2)}, u32[]{:S(2)}) %collective-permute-start.11) | collective-permute-done | bytes 262176 | tf_op jit(solution)/shard_map/ppermute | solution.py:21
  124.1 0.5 collective-permute-start.17
  124.7 3.4 %collective-permute-start.5 = (bf16[32,1024]{1,0:T(8,128)(2,1)S(1)}, bf16[32,1024]{1,0:T(8,128)(2,1)S(1)}, u32[]{:S(2)}, u32[]{:S(2)}) collective-permute-start(bf16[32,1024]{1,0:T(8,128)(2,1)S(1)} %add_convert_fusion.12.refs_0_), channel_id=1, source_target_pairs={{0,8},{1,9},{2,10},{3,11},{4,12},{5,13},{6,14},{7,15},{8,0},{9,1},... | collective-permute-start | bytes 196616 | tf_op jit(solution)/shard_map/ppermute | solution.py:21
  128.1 2.2 %collective-permute-done.5.refs_1_ = bf16[32,1024]{1,0:T(8,128)(2,1)S(1)} collective-permute-done((bf16[32,1024]{1,0:T(8,128)(2,1)S(1)}, bf16[32,1024]{1,0:T(8,128)(2,1)S(1)}, u32[]{:S(2)}, u32[]{:S(2)}) %collective-permute-start.5) | collective-permute-done | bytes 65568 | tf_op jit(solution)/shard_map/ppermute | solution.py:21
  130.3 2.9 %collective-permute-start.28 = (bf16[2,256,32]{2,1,0:T(8,128)(2,1)S(1)}, bf16[2,256,32]{2,1,0:T(8,128)(2,1)S(1)}, u32[]{:S(2)}, u32[]{:S(2)}) collective-permute-start(bf16[2,256,32]{2,1,0:T(8,128)(2,1)S(1)} %get-tuple-element.41), channel_id=1, source_target_pairs={{0,8},{1,9},{2,10},{3,11},{4,12},{5,13},{6,14},{7,15},{8,0},{9,1},... | collective-permute-start | bytes 98312 | tf_op jit(solution)/shard_map/ppermute | solution.py:21
  133.2 1.7 %collective-permute-start.22 = (bf16[128,512]{1,0:T(8,128)(2,1)S(1)}, bf16[128,512]{1,0:T(8,128)(2,1)S(1)}, u32[]{:S(2)}, u32[]{:S(2)}) collective-permute-start(bf16[128,512]{1,0:T(8,128)(2,1)S(1)} %fusion.3), channel_id=1, source_target_pairs={{0,20},{1,21},{2,22},{3,23},{4,16},{5,17},{6,18},{7,19},{8,28},{9,... | collective-permute-start | bytes 393224 | tf_op jit(solution)/shard_map/ppermute | solution.py:31
  135.0 2.9 %shard_map.106 = bf16[1024,512]{1,0:T(8,128)(2,1)} custom-call(s32[1]{0:T(128)} %bitcast.refs_0_.pos_ref, s32[2,4]{1,0:T(2,128)S(1)} %bitcast.36, s32[2]{0:T(128)S(1)} %bitcast.42, bf16[8,2,32,512]{3,2,1,0:T(8,128)(2,1)S(1)} %bitcast.30, bf16[32,1024]{1,0:T(8,128)(2,1)S(1)} %add_convert_fusion.12.refs_0_, ...), custom_call_target="tpu_custom_call" | custom-call | flops 67108864 | bytes 5242880 | tf_op jit(solution)/shard_map/pallas_call | solution.py:284
  137.9 0.6 collective-permute-start.18
  138.5 0.7 fusion.4
  139.2 1.2 fusion.1
  140.4 1.7 %collective-permute-start.20 = (bf16[256,512]{1,0:T(8,128)(2,1)S(1)}, bf16[256,512]{1,0:T(8,128)(2,1)}, u32[]{:S(2)}, u32[]{:S(2)}) collective-permute-start(bf16[256,512]{1,0:T(8,128)(2,1)S(1)} %fusion.1), channel_id=1, source_target_pairs={{0,20},{1,21},{2,22},{3,23},{4,16},{5,17},{6,18},{7,19},{8,28},{9,... | collective-permute-start | bytes 786440 | tf_op jit(solution)/shard_map/ppermute | solution.py:31
  142.2 0.8 fusion
  143.0 0.1 collective-permute-start.19
  143.1 1.8 %collective-permute-start.23 = (bf16[128,512]{1,0:T(8,128)(2,1)}, bf16[128,512]{1,0:T(8,128)(2,1)S(1)}, u32[]{:S(2)}, u32[]{:S(2)}) collective-permute-start(bf16[128,512]{1,0:T(8,128)(2,1)} %fusion.4), channel_id=1, source_target_pairs={{0,20},{1,21},{2,22},{3,23},{4,16},{5,17},{6,18},{7,19},{8,28},{9,... | collective-permute-start | bytes 393224 | tf_op jit(solution)/shard_map/ppermute | solution.py:31
  145.0 0.6 copy-done.15
  145.5 3.7 %shard_map.109 = bf16[8,32,1024]{2,1,0:T(8,128)(2,1)} custom-call(s32[1]{0:T(128)} %bitcast.refs_0_.pos_ref, s32[2,4]{1,0:T(2,128)} %bitcast.34, s32[2]{0:T(128)} %bitcast.40, bf16[2,256,1024]{2,1,0:T(8,128)(2,1)} %bitcast.50, bf16[1,256,1024]{2,1,0:T(8,128)(2,1)} %bitcast.55, bf16[1,256,1024]{2,1,0:T(8,128)(2,1)} %bitcast.57, ...), custom_call_target="tpu_custom_call" | custom-call | flops 67108864 | bytes 2097152 | tf_op jit(solution)/shard_map/pallas_call | solution.py:232
  149.2 3.1 %shard_map.108 = bf16[8,2,32,512]{3,2,1,0:T(8,128)(2,1)} custom-call(s32[1]{0:T(128)} %bitcast.refs_0_.pos_ref, s32[2,4]{1,0:T(2,128)} %bitcast.35, s32[2]{0:T(128)} %bitcast.41, bf16[2,512,512]{2,1,0:T(8,128)(2,1)} %bitcast.58, bf16[32,1024]{1,0:T(8,128)(2,1)} %copy-done.5, bf16[32,1024]{1,0:T(8,128)(2,1)} %copy-done.7), custom_call_target="tpu_custom_call" | custom-call | flops 67108864 | bytes 1048576 | tf_op jit(solution)/shard_map/pallas_call | solution.py:348
  152.3 5.0 %collective-permute-done.23.refs_4_ = bf16[128,512]{1,0:T(8,128)(2,1)S(1)} collective-permute-done((bf16[128,512]{1,0:T(8,128)(2,1)}, bf16[128,512]{1,0:T(8,128)(2,1)S(1)}, u32[]{:S(2)}, u32[]{:S(2)}) %collective-permute-start.23) | collective-permute-done | bytes 131104 | tf_op jit(solution)/shard_map/ppermute | solution.py:31
  157.3 2.8 %collective-permute-done.24.refs_5_ = bf16[128,512]{1,0:T(8,128)(2,1)S(1)} collective-permute-done((bf16[128,512]{1,0:T(8,128)(2,1)S(1)}, bf16[128,512]{1,0:T(8,128)(2,1)S(1)}, u32[]{:S(2)}, u32[]{:S(2)}) %collective-permute-start.24) | collective-permute-done | bytes 131104 | tf_op jit(solution)/shard_map/ppermute | solution.py:31
  160.2 0.6 copy-done.17
  160.8 0.1 copy-done.12
  160.9 2.8 %shard_map.107 = bf16[2,512,512]{2,1,0:T(8,128)(2,1)} custom-call(s32[1]{0:T(128)} %bitcast.refs_0_.pos_ref, bf16[1024,512]{1,0:T(8,128)(2,1)} %collective-permute-done.18.kept_ref, bf16[256,512]{1,0:T(8,128)(2,1)} %copy-done.12, bf16[256,512]{1,0:T(8,128)(2,1)} %collective-permute-done.20.refs_1_, bf16[128,512]{1,0:T(8,128)(2,1)} %copy-done.14, ...), custom_call_target="tpu_custom_call" | custom-call | tf_op jit(solution)/shard_map/pallas_call | solution.py:322
  (62 shorter events, 0.6 us)
Async XLA Ops:
  1.9 39.3 %collective-permute-start = (bf16[256,1024]{1,0:T(8,128)(2,1)S(1)}, bf16[256,1024]{1,0:T(8,128)(2,1)S(1)}, u32[]{:S(2)}, u32[]{:S(2)}) collective-permute-start(bf16[256,1024]{1,0:T(8,128)(2,1)S(1)} %get-tuple-element.40), channel_id=1, source_target_pairs={{0,8},{1,9},{2,10},{3,11},{4,12},{5,13},{6,14},{7,15},{8,0},{9,1},... | collective-permute-start | bytes 1572872 | tf_op jit(solution)/shard_map/ppermute | solution.py:21
  6.0 49.1 %collective-permute-start.1 = (bf16[256,1024]{1,0:T(8,128)(2,1)S(1)}, bf16[256,1024]{1,0:T(8,128)(2,1)S(1)}, u32[]{:S(2)}, u32[]{:S(2)}) collective-permute-start(bf16[256,1024]{1,0:T(8,128)(2,1)S(1)} %get-tuple-element.39), channel_id=1, source_target_pairs={{0,8},{1,9},{2,10},{3,11},{4,12},{5,13},{6,14},{7,15},{8,0},{9,1},... | collective-permute-start | bytes 1572872 | tf_op jit(solution)/shard_map/ppermute | solution.py:21
  6.1 17.6 %copy-start.18 = (bf16[1,2,32,64]{3,2,1,0:T(8,128)(2,1)S(1)}, bf16[1,2,32,64]{3,2,1,0:T(8,128)(2,1)}, u32[]{:S(2)}) copy-start(bf16[1,2,32,64]{3,2,1,0:T(8,128)(2,1)} %param.10) | copy-start | bytes 24580
  23.7 47.2 %collective-permute-start.25 = (bf16[2,32,64]{2,1,0:T(8,128)(2,1)S(1)}, bf16[2,32,64]{2,1,0:T(8,128)(2,1)S(1)}, u32[]{:S(2)}, u32[]{:S(2)}) collective-permute-start(bf16[2,32,64]{2,1,0:T(8,128)(2,1)S(1)} %bitcast.62), channel_id=1, source_target_pairs={{0,1},{1,0},{2,3},{3,2},{4,5},{5,4},{6,7},{7,6},{8,9},{9,8},{10,11... | collective-permute-start | bytes 24584 | tf_op jit(solution)/shard_map/ppermute | solution.py:21
  25.5 60.5 %collective-permute-start.8 = (bf16[4,256,512]{2,1,0:T(8,128)(2,1)}, bf16[4,256,512]{2,1,0:T(8,128)(2,1)}, u32[]{:S(2)}, u32[]{:S(2)}) collective-permute-start(bf16[4,256,512]{2,1,0:T(8,128)(2,1)} %get-tuple-element.29), channel_id=1, source_target_pairs={{0,2},{1,3},{2,0},{3,1},{4,6},{5,7},{6,4},{7,5},{8,10},{9,11},{10,... | collective-permute-start | bytes 3145736 | tf_op jit(solution)/shard_map/ppermute | solution.py:21
  27.0 62.2 %collective-permute-start.6 = (bf16[4,256,512]{2,1,0:T(8,128)(2,1)}, bf16[4,256,512]{2,1,0:T(8,128)(2,1)S(1)}, u32[]{:S(2)}, u32[]{:S(2)}) collective-permute-start(bf16[4,256,512]{2,1,0:T(8,128)(2,1)} %get-tuple-element.27), channel_id=1, source_target_pairs={{0,1},{1,0},{2,3},{3,2},{4,5},{5,4},{6,7},{7,6},{8,9},{9,8},{10,11... | collective-permute-start | bytes 3145736 | tf_op jit(solution)/shard_map/ppermute | solution.py:21
  41.2 0.8 copy-start.10
  55.1 0.8 copy-start.11
  69.0 5.0 %collective-permute-start.2 = (f32[32,1024]{1,0:T(8,128)S(1)}, f32[32,1024]{1,0:T(8,128)S(1)}, u32[]{:S(2)}, u32[]{:S(2)}) collective-permute-start(f32[32,1024]{1,0:T(8,128)S(1)} %constant_dynamic-update-slice_fusion), channel_id=1, source_target_pairs={{0,1},{1,0},{2,3},{3,2},{4,5},{5,4},{6,7},{7,6},{8,9},{9,8},{10,11... | collective-permute-start | bytes 393224 | tf_op jit(solution)/shard_map/ppermute | solution.py:21
  71.4 4.5 %collective-permute-start.26 = (bf16[2,64,64]{2,1,0:T(8,128)(2,1)}, bf16[2,64,64]{2,1,0:T(8,128)(2,1)}, u32[]{:S(2)}, u32[]{:S(2)}) collective-permute-start(bf16[2,64,64]{2,1,0:T(8,128)(2,1)} %maximum_select_fusion.2), channel_id=1, source_target_pairs={{0,2},{1,3},{2,0},{3,1},{4,6},{5,7},{6,4},{7,5},{8,10},{9,11},{10,... | collective-permute-start | bytes 49160 | tf_op jit(solution)/shard_map/ppermute | solution.py:21
  73.0 16.8 %copy-start = (f32[4,256,512]{2,1,0:T(8,128)S(1)}, f32[4,256,512]{2,1,0:T(8,128)}, u32[]{:S(2)}) copy-start(f32[4,256,512]{2,1,0:T(8,128)} %get-tuple-element.24.refs_2_) | copy-start | bytes 6291460
  74.0 5.0 %collective-permute-start.3 = (f32[32,1024]{1,0:T(8,128)S(1)}, f32[32,1024]{1,0:T(8,128)S(1)}, u32[]{:S(2)}, u32[]{:S(2)}) collective-permute-start(f32[32,1024]{1,0:T(8,128)S(1)} %add.82), channel_id=1, source_target_pairs={{0,2},{1,3},{2,0},{3,1},{4,6},{5,7},{6,4},{7,5},{8,10},{9,11},{10,... | collective-permute-start | bytes 393224 | tf_op jit(solution)/shard_map/ppermute | solution.py:21
  76.8 4.3 %collective-permute-start.27 = (bf16[2,128,64]{2,1,0:T(8,128)(2,1)S(1)}, bf16[2,128,64]{2,1,0:T(8,128)(2,1)S(1)}, u32[]{:S(2)}, u32[]{:S(2)}) collective-permute-start(bf16[2,128,64]{2,1,0:T(8,128)(2,1)S(1)} %maximum_select_fusion.1), channel_id=1, source_target_pairs={{0,4},{1,5},{2,6},{3,7},{4,0},{5,1},{6,2},{7,3},{8,12},{9,13},{10,... | collective-permute-start | bytes 98312 | tf_op jit(solution)/shard_map/ppermute | solution.py:21
  79.0 5.2 %collective-permute-start.4 = (f32[32,1024]{1,0:T(8,128)S(1)}, f32[32,1024]{1,0:T(8,128)S(1)}, u32[]{:S(2)}, u32[]{:S(2)}) collective-permute-start(f32[32,1024]{1,0:T(8,128)S(1)} %add.83), channel_id=1, source_target_pairs={{0,4},{1,5},{2,6},{3,7},{4,0},{5,1},{6,2},{7,3},{8,12},{9,13},{10,... | collective-permute-start | bytes 393224 | tf_op jit(solution)/shard_map/ppermute | solution.py:21
  81.9 15.1 %collective-permute-start.10 = (bf16[4,128,512]{2,1,0:T(8,128)(2,1)}, bf16[4,128,512]{2,1,0:T(8,128)(2,1)S(1)}, u32[]{:S(2)}, u32[]{:S(2)}) collective-permute-start(bf16[4,128,512]{2,1,0:T(8,128)(2,1)} %get-tuple-element.31), channel_id=1, source_target_pairs={{0,1},{1,0},{2,3},{3,2},{4,5},{5,4},{6,7},{7,6},{8,9},{9,8},{10,11... | collective-permute-start | bytes 1572872 | tf_op jit(solution)/shard_map/ppermute | solution.py:21
  83.4 15.1 %collective-permute-start.12 = (bf16[4,128,512]{2,1,0:T(8,128)(2,1)}, bf16[4,128,512]{2,1,0:T(8,128)(2,1)S(1)}, u32[]{:S(2)}, u32[]{:S(2)}) collective-permute-start(bf16[4,128,512]{2,1,0:T(8,128)(2,1)} %get-tuple-element.33), channel_id=1, source_target_pairs={{0,2},{1,3},{2,0},{3,1},{4,6},{5,7},{6,4},{7,5},{8,10},{9,11},{10,... | collective-permute-start | bytes 1572872 | tf_op jit(solution)/shard_map/ppermute | solution.py:21
  84.2 24.1 %collective-permute-start.14 = (bf16[4,128,512]{2,1,0:T(8,128)(2,1)}, bf16[4,128,512]{2,1,0:T(8,128)(2,1)S(1)}, u32[]{:S(2)}, u32[]{:S(2)}) collective-permute-start(bf16[4,128,512]{2,1,0:T(8,128)(2,1)} %get-tuple-element.35), channel_id=1, source_target_pairs={{0,1},{1,0},{2,3},{3,2},{4,5},{5,4},{6,7},{7,6},{8,9},{9,8},{10,11... | collective-permute-start | bytes 1572872 | tf_op jit(solution)/shard_map/ppermute | solution.py:21
  85.9 49.1 %copy-start.5 = (bf16[32,1024]{1,0:T(8,128)(2,1)}, bf16[32,1024]{1,0:T(8,128)(2,1)S(1)}, u32[]{:S(2)}) copy-start(bf16[32,1024]{1,0:T(8,128)(2,1)S(1)} %add_convert_fusion.12.refs_0_) | copy-start | bytes 196612
  85.9 23.9 %collective-permute-start.16 = (bf16[4,128,512]{2,1,0:T(8,128)(2,1)}, bf16[4,128,512]{2,1,0:T(8,128)(2,1)S(1)}, u32[]{:S(2)}, u32[]{:S(2)}) collective-permute-start(bf16[4,128,512]{2,1,0:T(8,128)(2,1)} %get-tuple-element.37), channel_id=1, source_target_pairs={{0,2},{1,3},{2,0},{3,1},{4,6},{5,7},{6,4},{7,5},{8,10},{9,11},{10,... | collective-permute-start | bytes 1572872 | tf_op jit(solution)/shard_map/ppermute | solution.py:21
  87.5 10.8 %copy-start.2 = (f32[4,128,512]{2,1,0:T(8,128)S(1)}, f32[4,128,512]{2,1,0:T(8,128)}, u32[]{:S(2)}) copy-start(f32[4,128,512]{2,1,0:T(8,128)} %get-tuple-element.30.refs_8_) | copy-start | bytes 3145732
  89.1 10.1 %copy-start.3 = (f32[4,128,512]{2,1,0:T(8,128)S(1)}, f32[4,128,512]{2,1,0:T(8,128)}, u32[]{:S(2)}) copy-start(f32[4,128,512]{2,1,0:T(8,128)} %get-tuple-element.32.refs_11_) | copy-start | bytes 3145732
  89.1 45.8 %collective-permute-start.9 = (bf16[2,256,512]{2,1,0:T(8,128)(2,1)S(1)}, bf16[2,256,512]{2,1,0:T(8,128)(2,1)S(1)}, u32[]{:S(2)}, u32[]{:S(2)}) collective-permute-start(bf16[2,256,512]{2,1,0:T(8,128)(2,1)S(1)} %add_convert_fusion), channel_id=1, source_target_pairs={{0,1},{1,0},{2,3},{3,2},{4,5},{5,4},{6,7},{7,6},{8,9},{9,8},{10,11... | collective-permute-start | bytes 1572872 | tf_op jit(solution)/shard_map/ppermute | solution.py:21
  89.8 20.0 %copy-start.4 = (f32[4,128,512]{2,1,0:T(8,128)S(1)}, f32[4,128,512]{2,1,0:T(8,128)}, u32[]{:S(2)}) copy-start(f32[4,128,512]{2,1,0:T(8,128)} %get-tuple-element.34.refs_14_) | copy-start | bytes 3145732
  89.9 20.7 %copy-start.1 = (f32[4,128,512]{2,1,0:T(8,128)S(1)}, f32[4,128,512]{2,1,0:T(8,128)}, u32[]{:S(2)}) copy-start(f32[4,128,512]{2,1,0:T(8,128)} %get-tuple-element.36.refs_17_) | copy-start | bytes 3145732
  97.0 38.0 %collective-permute-start.7 = (bf16[2,256,512]{2,1,0:T(8,128)(2,1)S(1)}, bf16[2,256,512]{2,1,0:T(8,128)(2,1)S(1)}, u32[]{:S(2)}, u32[]{:S(2)}) collective-permute-start(bf16[2,256,512]{2,1,0:T(8,128)(2,1)S(1)} %add_convert_fusion.1), channel_id=1, source_target_pairs={{0,2},{1,3},{2,0},{3,1},{4,6},{5,7},{6,4},{7,5},{8,10},{9,11},{10,... | collective-permute-start | bytes 1572872 | tf_op jit(solution)/shard_map/ppermute | solution.py:21
  98.5 25.6 %collective-permute-start.11 = (bf16[2,128,512]{2,1,0:T(8,128)(2,1)S(1)}, bf16[2,128,512]{2,1,0:T(8,128)(2,1)S(1)}, u32[]{:S(2)}, u32[]{:S(2)}) collective-permute-start(bf16[2,128,512]{2,1,0:T(8,128)(2,1)S(1)} %add_convert_fusion.7), channel_id=1, source_target_pairs={{0,2},{1,3},{2,0},{3,1},{4,6},{5,7},{6,4},{7,5},{8,10},{9,11},{10,... | collective-permute-start | bytes 786440 | tf_op jit(solution)/shard_map/ppermute | solution.py:21
  99.2 35.8 %copy-start.6 = (bf16[1,8,64,512]{3,2,1,0:T(8,128)(2,1)S(1)}, bf16[1,8,64,512]{3,2,1,0:T(8,128)(2,1)}, u32[]{:S(2)}) copy-start(bf16[1,8,64,512]{3,2,1,0:T(8,128)(2,1)} %param.12) | copy-start | bytes 1572868
  99.2 35.8 %copy-start.8 = (s32[1,2,4]{2,1,0:T(2,128)S(1)}, s32[1,2,4]{2,1,0:T(2,128)}, u32[]{:S(2)}) copy-start(s32[1,2,4]{2,1,0:T(2,128)} %param.14) | copy-start | bytes 100
  99.3 35.8 %copy-start.9 = (s32[1,2]{1,0:T(1,128)S(1)}, s32[1,2]{1,0:T(1,128)}, u32[]{:S(2)}) copy-start(s32[1,2]{1,0:T(1,128)} %param.15) | copy-start | bytes 28
  108.2 16.4 %collective-permute-start.13 = (bf16[2,128,512]{2,1,0:T(8,128)(2,1)S(1)}, bf16[2,128,512]{2,1,0:T(8,128)(2,1)S(1)}, u32[]{:S(2)}, u32[]{:S(2)}) collective-permute-start(bf16[2,128,512]{2,1,0:T(8,128)(2,1)S(1)} %add_convert_fusion.6), channel_id=1, source_target_pairs={{0,1},{1,0},{2,3},{3,2},{4,5},{5,4},{6,7},{7,6},{8,9},{9,8},{10,11... | collective-permute-start | bytes 786440 | tf_op jit(solution)/shard_map/ppermute | solution.py:21
  109.8 23.4 %collective-permute-start.15 = (bf16[2,128,512]{2,1,0:T(8,128)(2,1)S(1)}, bf16[2,128,512]{2,1,0:T(8,128)(2,1)S(1)}, u32[]{:S(2)}, u32[]{:S(2)}) collective-permute-start(bf16[2,128,512]{2,1,0:T(8,128)(2,1)S(1)} %add_convert_fusion.5), channel_id=1, source_target_pairs={{0,2},{1,3},{2,0},{3,1},{4,6},{5,7},{6,4},{7,5},{8,10},{9,11},{10,... | collective-permute-start | bytes 786440 | tf_op jit(solution)/shard_map/ppermute | solution.py:21
  124.1 9.2 %collective-permute-start.17 = (bf16[2,128,512]{2,1,0:T(8,128)(2,1)S(1)}, bf16[2,128,512]{2,1,0:T(8,128)(2,1)S(1)}, u32[]{:S(2)}, u32[]{:S(2)}) collective-permute-start(bf16[2,128,512]{2,1,0:T(8,128)(2,1)S(1)} %add_convert_fusion.4), channel_id=1, source_target_pairs={{0,1},{1,0},{2,3},{3,2},{4,5},{5,4},{6,7},{7,6},{8,9},{9,8},{10,11... | collective-permute-start | bytes 786440 | tf_op jit(solution)/shard_map/ppermute | solution.py:21
  124.7 5.6 %collective-permute-start.5 = (bf16[32,1024]{1,0:T(8,128)(2,1)S(1)}, bf16[32,1024]{1,0:T(8,128)(2,1)S(1)}, u32[]{:S(2)}, u32[]{:S(2)}) collective-permute-start(bf16[32,1024]{1,0:T(8,128)(2,1)S(1)} %add_convert_fusion.12.refs_0_), channel_id=1, source_target_pairs={{0,8},{1,9},{2,10},{3,11},{4,12},{5,13},{6,14},{7,15},{8,0},{9,1},... | collective-permute-start | bytes 196616 | tf_op jit(solution)/shard_map/ppermute | solution.py:21
  130.3 7.6 %copy-start.7 = (bf16[32,1024]{1,0:T(8,128)(2,1)}, bf16[32,1024]{1,0:T(8,128)(2,1)S(1)}, u32[]{:S(2)}) copy-start(bf16[32,1024]{1,0:T(8,128)(2,1)S(1)} %collective-permute-done.5.refs_1_) | copy-start | bytes 196612
  130.3 12.7 %collective-permute-start.28 = (bf16[2,256,32]{2,1,0:T(8,128)(2,1)S(1)}, bf16[2,256,32]{2,1,0:T(8,128)(2,1)S(1)}, u32[]{:S(2)}, u32[]{:S(2)}) collective-permute-start(bf16[2,256,32]{2,1,0:T(8,128)(2,1)S(1)} %get-tuple-element.41), channel_id=1, source_target_pairs={{0,8},{1,9},{2,10},{3,11},{4,12},{5,13},{6,14},{7,15},{8,0},{9,1},... | collective-permute-start | bytes 98312 | tf_op jit(solution)/shard_map/ppermute | solution.py:21
  133.2 9.9 %collective-permute-start.21 = (bf16[128,512]{1,0:T(8,128)(2,1)S(1)}, bf16[128,512]{1,0:T(8,128)(2,1)S(1)}, u32[]{:S(2)}, u32[]{:S(2)}) collective-permute-start(bf16[128,512]{1,0:T(8,128)(2,1)S(1)} %fusion.2), channel_id=1, source_target_pairs={{0,20},{1,21},{2,22},{3,23},{4,16},{5,17},{6,18},{7,19},{8,28},{9,... | collective-permute-start | bytes 393224 | tf_op jit(solution)/shard_map/ppermute | solution.py:31
  133.2 11.6 %collective-permute-start.22 = (bf16[128,512]{1,0:T(8,128)(2,1)S(1)}, bf16[128,512]{1,0:T(8,128)(2,1)S(1)}, u32[]{:S(2)}, u32[]{:S(2)}) collective-permute-start(bf16[128,512]{1,0:T(8,128)(2,1)S(1)} %fusion.3), channel_id=1, source_target_pairs={{0,20},{1,21},{2,22},{3,23},{4,16},{5,17},{6,18},{7,19},{8,28},{9,... | collective-permute-start | bytes 393224 | tf_op jit(solution)/shard_map/ppermute | solution.py:31
  137.9 22.3 %collective-permute-start.18 = (bf16[1024,512]{1,0:T(8,128)(2,1)}, bf16[1024,512]{1,0:T(8,128)(2,1)}, u32[]{:S(2)}, u32[]{:S(2)}) collective-permute-start(bf16[1024,512]{1,0:T(8,128)(2,1)} %shard_map.106), channel_id=1, source_target_pairs={{0,16},{1,17},{2,18},{3,19},{4,20},{5,21},{6,22},{7,23},{8,24},{9,... | collective-permute-start | bytes 3145736 | tf_op jit(solution)/shard_map/ppermute | solution.py:31
  140.4 19.7 %collective-permute-start.20 = (bf16[256,512]{1,0:T(8,128)(2,1)S(1)}, bf16[256,512]{1,0:T(8,128)(2,1)}, u32[]{:S(2)}, u32[]{:S(2)}) collective-permute-start(bf16[256,512]{1,0:T(8,128)(2,1)S(1)} %fusion.1), channel_id=1, source_target_pairs={{0,20},{1,21},{2,22},{3,23},{4,16},{5,17},{6,18},{7,19},{8,28},{9,... | collective-permute-start | bytes 786440 | tf_op jit(solution)/shard_map/ppermute | solution.py:31
  143.0 2.6 %copy-start.13 = (bf16[2,256,32]{2,1,0:T(8,128)(2,1)}, bf16[2,256,32]{2,1,0:T(8,128)(2,1)S(1)}, u32[]{:S(2)}) copy-start(bf16[2,256,32]{2,1,0:T(8,128)(2,1)S(1)} %collective-permute-done.28.refs_7_) | copy-start | bytes 98308
  143.0 17.2 %collective-permute-start.19 = (bf16[256,512]{1,0:T(8,128)(2,1)}, bf16[256,512]{1,0:T(8,128)(2,1)S(1)}, u32[]{:S(2)}, u32[]{:S(2)}) collective-permute-start(bf16[256,512]{1,0:T(8,128)(2,1)} %fusion), channel_id=1, source_target_pairs={{0,20},{1,21},{2,22},{3,23},{4,16},{5,17},{6,18},{7,19},{8,28},{9,... | collective-permute-start | bytes 786440 | tf_op jit(solution)/shard_map/ppermute | solution.py:31
  143.1 1.9 %copy-start.14 = (bf16[128,512]{1,0:T(8,128)(2,1)}, bf16[128,512]{1,0:T(8,128)(2,1)S(1)}, u32[]{:S(2)}) copy-start(bf16[128,512]{1,0:T(8,128)(2,1)S(1)} %collective-permute-done.21.refs_2_) | copy-start | bytes 393220
  143.1 14.2 %collective-permute-start.23 = (bf16[128,512]{1,0:T(8,128)(2,1)}, bf16[128,512]{1,0:T(8,128)(2,1)S(1)}, u32[]{:S(2)}, u32[]{:S(2)}) collective-permute-start(bf16[128,512]{1,0:T(8,128)(2,1)} %fusion.4), channel_id=1, source_target_pairs={{0,20},{1,21},{2,22},{3,23},{4,16},{5,17},{6,18},{7,19},{8,28},{9,... | collective-permute-start | bytes 393224 | tf_op jit(solution)/shard_map/ppermute | solution.py:31
  144.9 0.6 copy-start.15
  144.9 15.3 %collective-permute-start.24 = (bf16[128,512]{1,0:T(8,128)(2,1)S(1)}, bf16[128,512]{1,0:T(8,128)(2,1)S(1)}, u32[]{:S(2)}, u32[]{:S(2)}) collective-permute-start(bf16[128,512]{1,0:T(8,128)(2,1)S(1)} %fusion.5), channel_id=1, source_target_pairs={{0,20},{1,21},{2,22},{3,23},{4,16},{5,17},{6,18},{7,19},{8,28},{9,... | collective-permute-start | bytes 393224 | tf_op jit(solution)/shard_map/ppermute | solution.py:31
  157.3 2.8 %copy-start.16 = (bf16[128,512]{1,0:T(8,128)(2,1)}, bf16[128,512]{1,0:T(8,128)(2,1)S(1)}, u32[]{:S(2)}) copy-start(bf16[128,512]{1,0:T(8,128)(2,1)S(1)} %collective-permute-done.23.refs_4_) | copy-start | bytes 393220
  160.1 0.6 copy-start.17
  160.1 0.7 copy-start.12

commit v4 on v3

--- a/solution.py
+++ b/solution.py
@@ -12,7 +12,6 @@
 F32 = jnp.float32
 SMEM = pl.BlockSpec(memory_space=pltpu.SMEM)
 VMEM = pl.BlockSpec(memory_space=pltpu.VMEM)
-NT = (((1,), (1,)), ((), ()))
 TN = (((0,), (0,)), ((), ()))
 
 
@@ -36,19 +35,24 @@
     return ((high ^ k) * tile_rows + offset) // SEG
 
 
-def product_body(low_size, tile_rows, pieces, tiles, subs, *refs):
+def product_body(low_size, tile_rows, pieces, tiles, half, *refs):
     pos_ref, classes_ref, live_ref = refs[:3]
     grad_refs = refs[3 : 3 + tiles]
-    weight_refs = refs[3 + tiles : 3 + tiles + subs]
-    up_ref = refs[3 + tiles + subs]
-    sent_x, kept_x, sent_y, kept_y, rank_ref, rows_ref = refs[4 + tiles + subs :]
+    weight_hbm, up_ref, sent_x, kept_x, sent_y, kept_y, rank_ref, rows_ref, weight_ref, sems = refs[
+        3 + tiles :
+    ]
     step = pl.program_id(0)
-    high = pos_ref[0] // low_size
+    low, high = pos_ref[0] % low_size, pos_ref[0] // low_size
     size = pieces[0][3]
-    half = rows_ref.shape[0] // 2
+
+    def weight_copy(k):
+        block = (1 - k // 4 + (2 - (k & 2)) + 4 * (k & 1)) ^ low
+        return pltpu.make_async_copy(weight_hbm.at[block], weight_ref.at[k], sems.at[k])
 
     @pl.when(step == 0)
     def _():
+        for k in range(low_size):
+            weight_copy(k).start()
         for at, (tile, index, piece, _) in enumerate(pieces):
             seg = segment_of(high, piece, tile_rows)
             alive = seg < live_ref[piece[1]]
@@ -56,36 +60,34 @@
 
             @pl.when(alive)
             def _():
-                rows = grad_refs[tile][index, piece[2] : piece[2] + size, :]
-                rows_ref[place, :] = rows
+                rows = grad_refs[tile][index, piece[2] : piece[2] + size, :].T
+                rows_ref[:, place] = rows
                 up = up_ref[classes_ref[piece[1], seg]]
-                rank_ref[:, place] = lax.dot_general(up, rows, NT, preferred_element_type=F32)
+                rank_ref[:, place] = jnp.dot(up, rows, preferred_element_type=F32)
 
             @pl.when(jnp.logical_not(alive))
             def _():
-                rows_ref[place, :] = jnp.zeros((size, rows_ref.shape[1]), rows_ref.dtype)
+                rows_ref[:, place] = jnp.zeros((rows_ref.shape[0], size), rows_ref.dtype)
                 rank_ref[:, place] = jnp.zeros((rank_ref.shape[0], size), F32)
 
-    for sub, weight_ref in enumerate(weight_refs):
-        width = weight_ref.shape[1]
-        columns = slice(sub * width, (sub + 1) * width)
-        value = lax.dot_general(rows_ref[...], weight_ref[0], NT, preferred_element_type=F32)
-
-        @pl.when(step < 4)
-        def _():
-            sent_x[0, :, columns] = value[:half].astype(BF16)
-
-        @pl.when(step >= 4)
-        def _():
-            kept_x[0, :, columns] = value[:half]
-
-        @pl.when(step & 2 == 0)
-        def _():
-            sent_y[0, :, columns] = value[half:].astype(BF16)
-
-        @pl.when(step & 2 != 0)
-        def _():
-            kept_y[0, :, columns] = value[half:]
+    weight_copy(step).wait()
+    value = jnp.dot(weight_ref[step], rows_ref[...], preferred_element_type=F32)
+
+    @pl.when(step < 4)
+    def _():
+        sent_x[0] = value[:, :half].astype(BF16)
+
+    @pl.when(step >= 4)
+    def _():
+        kept_x[0] = value[:, :half]
+
+    @pl.when(step & 2 == 0)
+    def _():
+        sent_y[0] = value[:, half:].astype(BF16)
+
+    @pl.when(step & 2 != 0)
+    def _():
+        kept_y[0] = value[:, half:]
 
 
 def product(scalars, grads, pieces, weight_blocks, up_tile, low_size):
@@ -93,52 +95,51 @@
     tile_rows = grads[0].shape[1]
     rows = len(pieces) * pieces[0][3]
     half = rows // 2
-    subs = 2 if width % 512 == 0 else 1
-
-    def block_of(k):
-        return 1 - k // 4 + (2 - (k & 2)) + 4 * (k & 1)
+    if rows > 128 and half % 128:
+        half = half // 128 * 128 + 128
 
     def whole(array):
         return pl.BlockSpec(array.shape, lambda k, *_: (0,) * array.ndim)
 
-    def weight_spec(sub):
-        return pl.BlockSpec(
-            (1, width // subs, depth), lambda k, pos, *_: (block_of(k) ^ (pos[0] % low_size), sub, 0)
-        )
-
-    def slot(place):
-        return pl.BlockSpec((1, half, width), lambda k, *_: (place(k), 0, 0))
-
     def by_y(k):
         return 2 - (k & 2) + (k & 1)
 
     outs = [
-        (BF16, lambda k: jnp.where(k < 4, by_y(k), 1)),
-        (F32, lambda k: jnp.where(k < 4, 2, by_y(k))),
-        (BF16, lambda k: 2 * (1 - k // 4) + jnp.where(k & 2 == 0, k & 1, 1)),
-        (F32, lambda k: 2 * (1 - k // 4) + jnp.where(k & 2 == 0, 0, k & 1)),
+        (half, BF16, lambda k: jnp.where(k < 4, by_y(k), 1)),
+        (half, F32, lambda k: jnp.where(k < 4, 2, by_y(k))),
+        (rows - half, BF16, lambda k: 2 * (1 - k // 4) + jnp.where(k & 2 == 0, k & 1, 1)),
+        (rows - half, F32, lambda k: 2 * (1 - k // 4) + jnp.where(k & 2 == 0, 0, k & 1)),
     ]
     rank_part = up_tile.shape[1]
     return pl.pallas_call(
-        functools.partial(product_body, low_size, tile_rows, pieces, len(grads), subs),
+        functools.partial(product_body, low_size, tile_rows, pieces, len(grads), half),
         grid_spec=pltpu.PrefetchScalarGridSpec(
             num_scalar_prefetch=3,
             grid=(blocks,),
             in_specs=[whole(g) for g in grads]
-            + [weight_spec(sub) for sub in range(subs)]
-            + [whole(up_tile)],
-            out_specs=[slot(place) for _, place in outs]
+            + [pl.BlockSpec(memory_space=pl.ANY), whole(up_tile)],
+            out_specs=[
+                pl.BlockSpec((1, width, count), lambda k, *_, place=place: (place(k), 0, 0))
+                for count, _, place in outs
+            ]
             + [pl.BlockSpec((rank_part, rows), lambda k, *_: (0, 0))],
-            scratch_shapes=[pltpu.VMEM((rows, depth), BF16)],
-        ),
-        out_shape=[jax.ShapeDtypeStruct((blocks // 2, half, width), dtype) for dtype, _ in outs]
+            scratch_shapes=[
+                pltpu.VMEM((depth, rows), BF16),
+                pltpu.VMEM(weight_blocks.shape, BF16),
+                pltpu.SemaphoreType.DMA((blocks,)),
+            ],
+        ),
+        out_shape=[
+            jax.ShapeDtypeStruct((blocks // 2, width, count), dtype) for count, dtype, _ in outs
+        ]
         + [jax.ShapeDtypeStruct((rank_part, rows), F32)],
+        compiler_params=pltpu.CompilerParams(vmem_limit_bytes=48 * 2**20),
         cost_estimate=pl.CostEstimate(
             flops=2 * blocks * rows * width * depth,
-            bytes_accessed=2 * blocks * width * depth + 8 * blocks * rows * width,
+            bytes_accessed=2 * blocks * width * depth + 3 * blocks * rows * width,
             transcendentals=0,
         ),
-    )(*scalars, *grads, *([weight_blocks] * subs), up_tile)
+    )(*scalars, *grads, weight_blocks, up_tile)
 
 
 def up_body(low_size, tile_rows, pieces, tiles, *refs):
@@ -192,14 +193,17 @@
 
     own_pieces = [(0, m, (0, m, o), size) for m in range(micro_count) for o in offsets]
     chunks = [([grad_tile], own_pieces)]
+    source = grad_tile
     for m in range(micro_count):
-        got = [partner(grad_tile[m], k * low_size)[None] for k in range(1, high_size)]
+        got = [partner(source[m], k * low_size)[None] for k in range(1, high_size)]
+        *got, source = lax.optimization_barrier((*got, source))
         pieces = [(k - 1, 0, (k, m, o), size) for k in range(1, high_size) for o in offsets]
         chunks.append((got, pieces))
     order = [piece for _, pieces in chunks for _, _, piece, _ in pieces]
 
     hidden = saved_rank_outputs[0]
     sums, got_last, parts = [], [], []
+    arrived = [None, None]
     for grads, pieces in chunks:
         sent_x, kept_x, sent_y, kept_y, part = product(
             scalars, grads, pieces, weight_blocks, up_tile, low_size
@@ -207,8 +211,11 @@
         parts.append(part)
         if not sums:
             sent_x, sent_y, hidden = lax.optimization_barrier((sent_x, sent_y, hidden))
-        for bits, sent, kept in (((0, 1, 2), sent_x, kept_x), ((1, 0, 2), sent_y, kept_y)):
-            got = partner(sent, 1 << bits[0])
+        ways = (((0, 1, 2), sent_x, kept_x), ((1, 0, 2), sent_y, kept_y))
+        for way, (bits, sent, kept) in enumerate(ways):
+            if arrived[way] is not None:
+                sent, _ = lax.optimization_barrier((sent, arrived[way]))
+            got = arrived[way] = partner(sent, 1 << bits[0])
             second = partner((kept[2:] + got[2:]).astype(BF16), 1 << bits[1])
             third = (kept[1] + got[1] + second[1]).astype(BF16)
             got_last.append(relay(third, 1 << bits[2]))
@@ -262,23 +269,23 @@
         start = 0
         for g in range(len(sums)):
             kept_ref, got_ref, second_ref = sum_refs[3 * g : 3 * g + 3]
-            count = kept_ref.shape[1]
-            total_ref[start : start + count, :] = (
+            count = kept_ref.shape[2]
+            total_ref[:, start : start + count] = (
                 kept_ref[0] + got_ref[0].astype(F32) + second_ref[0].astype(F32)
             )
             start += count
         for at, piece in enumerate(order):
             seg = segment_of(own, piece, tile_rows)
             rows = slice(at * size, (at + 1) * size)
-            adapter = 0.0
+            adapter = total_ref[:, rows]
             for j in range(high_size):
                 adapter = adapter + lax.dot_general(
+                    down_ref[classes_ref[piece[1], seg], own ^ j],
                     rank_refs[j][:, columns_of(j, piece)],
-                    down_ref[classes_ref[piece[1], seg], own ^ j],
                     TN,
                     preferred_element_type=F32,
                 )
-            out_ref[rows, :] = (total_ref[rows, :] + adapter).astype(BF16)
+            out_ref[:, rows] = adapter.astype(BF16)
 
     rows_total = len(order) * size
     kept = pl.pallas_call(
@@ -287,9 +294,9 @@
         in_specs=[SMEM] * 3
         + [pl.BlockSpec(a.shape, lambda _, n=a.ndim: (0,) * n) for a in [down_parts, *ranks]]
         + [pl.BlockSpec((1,) + a.shape[1:], lambda _: (0, 0, 0)) for three in sums for a in three],
-        out_specs=pl.BlockSpec((rows_total, portion), lambda _: (0, 0)),
-        out_shape=jax.ShapeDtypeStruct((rows_total, portion), BF16),
-        scratch_shapes=[pltpu.VMEM((rows_total, portion), F32)],
+        out_specs=pl.BlockSpec((portion, rows_total), lambda _: (0, 0)),
+        out_shape=jax.ShapeDtypeStruct((portion, rows_total), BF16),
+        scratch_shapes=[pltpu.VMEM((portion, rows_total), F32)],
         compiler_params=pltpu.CompilerParams(vmem_limit_bytes=40 * 2**20),
         cost_estimate=pl.CostEstimate(
             flops=2 * rows_total * rank * portion,
@@ -300,30 +307,25 @@
     kept = relay(kept, 0)
 
     def finish_kernel(pos_ref, kept_ref, *refs):
-        got_refs, out_ref = refs[:-1], refs[-1]
+        *got_refs, out_ref, total_ref = refs
         own = pos_ref[0] // low_size
-        start, found = 0, []
+        start = 0
         for got_ref in got_refs:
-            for row in range(0, got_ref.shape[0], 16):
-                found.append((got_ref, row))
+            count = got_ref.shape[1]
+            total_ref[:, start : start + count] = (
+                kept_ref[:, start : start + count].astype(F32) + got_ref[...].astype(F32)
+            ).astype(BF16)
+            start += count
         for at, (k, m, offset) in enumerate(order):
             base = pl.multiple_of((own ^ k) * tile_rows + offset, size)
-            row = 0
-            while row < size:
-                got_ref, first = found[(at * size + row) // 16]
-                count = min(size - row, got_ref.shape[0] - first)
-                spot = at * size + row
-                out_ref[m, pl.ds(base + row, count), :] = (
-                    kept_ref[spot : spot + count, :].astype(F32)
-                    + got_ref[first : first + count, :].astype(F32)
-                ).astype(BF16)
-                row += count
+            out_ref[m, pl.ds(base, size), :] = total_ref[:, at * size : (at + 1) * size].T
 
     grad_prev = pl.pallas_call(
         finish_kernel,
         in_specs=[SMEM] + [VMEM] * (1 + len(got_last)),
         out_specs=VMEM,
         out_shape=jax.ShapeDtypeStruct((micro_count, high_size * tile_rows, portion), BF16),
+        scratch_shapes=[pltpu.VMEM((portion, rows_total), BF16)],
     )(scalars[0], kept, *got_last)
 
     def down_kernel(pos_ref, classes_ref, live_ref, inputs_ref, *refs):

time: 165 us -> 151 us (0.915)
  Pallas kernels: 54.6 us -> 33.3 us
  waiting for transfers between devices: 57.1 us -> 68.3 us
  starting transfers between devices: 37.2 us -> 32.6 us
  local copies, waits for them, and re-layouts: 7.35 us -> 10.5 us
    pallas_call x3, Pallas kernels: 42.2 us -> 22.4 us  [product(): pl.pallas_call(functools.partial(product_body, low_size, tile_rows, piece...]
    ppermute x22, waiting for transfers between devices: 49.3 us -> 55.8 us  [partner(): return lax.ppermute(value, 'tensor', pairs)]
    ppermute x7, waiting for transfers between devices: 7.83 us -> 12.5 us  [relay(): return lax.ppermute(value, ('pipe', 'tensor'), pairs)]
    ppermute x22, starting transfers between devices: 31.2 us -> 27.3 us  [partner(): return lax.ppermute(value, 'tensor', pairs)]
    unnamed x40 -> x46, local copies, waits for them, and re-layouts: 4.53 us -> 7.02 us
  transfers between devices with their start and end apart: 29 -> 29, of which waited for: 11 -> 12; matrix products, arithmetic and copies ran while one was open for 6% -> 4% of each run, Pallas kernels for 32% -> 20%
where the time goes in v4:
time: 151 us
  waiting for transfers between devices  68.3 us (45%)
  Pallas kernels  33.3 us (22%)
  starting transfers between devices  32.6 us (22%)
  local copies, waits for them, and re-layouts  10.5 us (7%)
  other arithmetic  4.98 us (3%)
    ppermute x22, waiting for transfers between devices, partner(): return lax.ppermute(value, 'tensor', pairs)  55.8 us
    ppermute x22, starting transfers between devices, partner(): return lax.ppermute(value, 'tensor', pairs)  27.3 us
    pallas_call x3, Pallas kernels, product(): pl.pallas_call(functools.partial(product_body, low_size, tile_rows, piece...  22.4 us
    ppermute x7, waiting for transfers between devices, relay(): return lax.ppermute(value, ('pipe', 'tensor'), pairs)  12.5 us
    unnamed x46, local copies, waits for them, and re-layouts  7.02 us
    ppermute x7, starting transfers between devices, relay(): return lax.ppermute(value, ('pipe', 'tensor'), pairs)  5.37 us
    pallas_call x1, Pallas kernels, shards(): pl.pallas_call(functools.partial(up_body, low_size, tile_rows, all_pieces...  3.08 us
    pallas_call x1, Pallas kernels, shards(): pl.pallas_call(finish_kernel, in_specs=[SMEM] + [VMEM] * (1 + len(got_las...  3.07 us
  transfers between devices with their start and end apart: 29, of which 12 were waited for; matrix products, arithmetic and copies ran while one was open for 4% of the time, Pallas kernels for 20%

profile of v4, /device:TPU:0, one launch (start us, length us, event | category | flops | bytes accessed | tf_op | source)
XLA Modules:
  0.0 150.7 jit_solution(8970621021166734448)
XLA Ops:
  0.6 1.9 %slice_bitcast_fusion.1 = bf16[256,1024]{1,0:T(8,128)(2,1)} fusion(bf16[1,1,2,256,1024]{4,3,2,1,0:T(8,128)(2,1)} %param.8), kind=kLoop, calls=%fused_computation.9 | loop fusion | bytes 1048576 | tf_op jit(solution)/shard_map/squeeze | solution.py:198
  2.5 4.0 %collective-permute-start = (bf16[256,1024]{1,0:T(8,128)(2,1)}, bf16[256,1024]{1,0:T(8,128)(2,1)}, u32[]{:S(2)}, u32[]{:S(2)}) collective-permute-start(bf16[256,1024]{1,0:T(8,128)(2,1)} %slice_bitcast_fusion.1), channel_id=1, source_target_pairs={{0,8},{1,9},{2,10},{3,11},{4,12},{5,13},{6,14},{7,15},{8,0},{9,1},... | collective-permute-start | bytes 1572872 | tf_op jit(solution)/shard_map/ppermute | solution.py:20
  6.5 1.2 copy-done
  7.8 1.0 copy-done.2
  8.8 0.7 copy-done.8
  9.5 0.7 copy-done.10
  10.2 9.7 %shard_map.103 = (bf16[4,512,256]{2,1,0:T(8,128)(2,1)}, f32[4,512,256]{2,1,0:T(8,128)S(1)}, bf16[4,512,256]{2,1,0:T(8,128)(2,1)}, f32[4,512,256]{2,1,0:T(8,128)}, f32[32,512]{1,0:T(8,128)S(1)}) custom-call(s32[1]{0:T(128)} %bitcast.refs_0_.pos_ref, s32[2,4]{1,0:T(2,128)S(1)} %bitcast.41, s32[2]{0:T(128)S(1)} %bitcast.47, bf16[2,256,1024]{2,1,0:T(8,128)(2,1)S(1)} %bitcast.31, ...), custom_call_target="tpu_custom_call" | custom-call | flops 4294967296 | bytes 14680064 | tf_op jit(solution)/shard_map/pallas_call | solution.py:114
  19.8 1.6 %collective-permute-start.25 = (bf16[2,32,64]{2,1,0:T(8,128)(2,1)S(1)}, bf16[2,32,64]{2,1,0:T(8,128)(2,1)S(1)}, u32[]{:S(2)}, u32[]{:S(2)}) collective-permute-start(bf16[2,32,64]{2,1,0:T(8,128)(2,1)S(1)} %bitcast.58), channel_id=1, source_target_pairs={{0,1},{1,0},{2,3},{3,2},{4,5},{5,4},{6,7},{7,6},{8,9},{9,8},{10,11... | collective-permute-start | bytes 24584 | tf_op jit(solution)/shard_map/ppermute | solution.py:20
  21.4 0.5 collective-permute-start.6
  21.9 1.5 %collective-permute-start.8 = (bf16[4,512,256]{2,1,0:T(8,128)(2,1)}, bf16[4,512,256]{2,1,0:T(8,128)(2,1)}, u32[]{:S(2)}, u32[]{:S(2)}) collective-permute-start(bf16[4,512,256]{2,1,0:T(8,128)(2,1)} %get-tuple-element.39), channel_id=1, source_target_pairs={{0,2},{1,3},{2,0},{3,1},{4,6},{5,7},{6,4},{7,5},{8,10},{9,11},{10,... | collective-permute-start | bytes 3145736 | tf_op jit(solution)/shard_map/ppermute | solution.py:20
  23.4 0.4 collective-permute-done.25
  23.8 1.6 %collective-permute-start.26 = (bf16[2,64,64]{2,1,0:T(8,128)(2,1)S(1)}, bf16[2,64,64]{2,1,0:T(8,128)(2,1)S(1)}, u32[]{:S(2)}, u32[]{:S(2)}) collective-permute-start(bf16[2,64,64]{2,1,0:T(8,128)(2,1)S(1)} %maximum_select_fusion.2), channel_id=1, source_target_pairs={{0,2},{1,3},{2,0},{3,1},{4,6},{5,7},{6,4},{7,5},{8,10},{9,11},{10,... | collective-permute-start | bytes 49160 | tf_op jit(solution)/shard_map/ppermute | solution.py:20
  25.4 4.6 %collective-permute-done = bf16[256,1024]{1,0:T(8,128)(2,1)} collective-permute-done((bf16[256,1024]{1,0:T(8,128)(2,1)}, bf16[256,1024]{1,0:T(8,128)(2,1)}, u32[]{:S(2)}, u32[]{:S(2)}) %collective-permute-start) | collective-permute-done | bytes 524320 | tf_op jit(solution)/shard_map/ppermute | solution.py:20
  30.0 0.8 slice_bitcast_fusion
  30.9 16.0 %collective-permute-done.26 = bf16[2,64,64]{2,1,0:T(8,128)(2,1)S(1)} collective-permute-done((bf16[2,64,64]{2,1,0:T(8,128)(2,1)S(1)}, bf16[2,64,64]{2,1,0:T(8,128)(2,1)S(1)}, u32[]{:S(2)}, u32[]{:S(2)}) %collective-permute-start.26) | collective-permute-done | bytes 16416 | tf_op jit(solution)/shard_map/ppermute | solution.py:20
  46.9 1.6 %collective-permute-start.27 = (bf16[2,128,64]{2,1,0:T(8,128)(2,1)S(1)}, bf16[2,128,64]{2,1,0:T(8,128)(2,1)S(1)}, u32[]{:S(2)}, u32[]{:S(2)}) collective-permute-start(bf16[2,128,64]{2,1,0:T(8,128)(2,1)S(1)} %maximum_select_fusion.1), channel_id=1, source_target_pairs={{0,4},{1,5},{2,6},{3,7},{4,0},{5,1},{6,2},{7,3},{8,12},{9,13},{10,... | collective-permute-start | bytes 98312 | tf_op jit(solution)/shard_map/ppermute | solution.py:20
  48.6 1.0 copy-done.3
  49.6 6.9 %shard_map.104 = (bf16[4,512,128]{2,1,0:T(8,128)(2,1)S(1)}, f32[4,512,128]{2,1,0:T(8,128)S(1)}, bf16[4,512,128]{2,1,0:T(8,128)(2,1)S(1)}, f32[4,512,128]{2,1,0:T(8,128)S(1)}, f32[32,256]{1,0:T(8,128)S(1)}) custom-call(s32[1]{0:T(128)} %bitcast.refs_0_.pos_ref, s32[2,4]{1,0:T(2,128)S(1)} %bitcast.42, s32[2]{0:T(128)S(1)} %bitcast.48, ...), custom_call_target="tpu_custom_call" | custom-call | flops 2147483648 | bytes 11534336 | tf_op jit(solution)/shard_map/pallas_call | solution.py:114
  56.5 5.9 %shard_map.105 = (bf16[4,512,128]{2,1,0:T(8,128)(2,1)S(1)}, f32[4,512,128]{2,1,0:T(8,128)S(1)}, bf16[4,512,128]{2,1,0:T(8,128)(2,1)S(1)}, f32[4,512,128]{2,1,0:T(8,128)S(1)}, f32[32,256]{1,0:T(8,128)S(1)}) custom-call(s32[1]{0:T(128)} %bitcast.refs_0_.pos_ref, s32[2,4]{1,0:T(2,128)S(1)} %bitcast.43, s32[2]{0:T(128)S(1)} %bitcast.49, ...), custom_call_target="tpu_custom_call" | custom-call | flops 2147483648 | bytes 11534336 | tf_op jit(solution)/shard_map/pallas_call | solution.py:114
  62.5 1.6 %collective-permute-start.2 = (f32[32,1024]{1,0:T(8,128)S(1)}, f32[32,1024]{1,0:T(8,128)S(1)}, u32[]{:S(2)}, u32[]{:S(2)}) collective-permute-start(f32[32,1024]{1,0:T(8,128)S(1)} %constant_dynamic-update-slice_fusion), channel_id=1, source_target_pairs={{0,1},{1,0},{2,3},{3,2},{4,5},{5,4},{6,7},{7,6},{8,9},{9,8},{10,11... | collective-permute-start | bytes 393224 | tf_op jit(solution)/shard_map/ppermute | solution.py:20
  64.1 0.8 constant_dynamic-slice_fusion
  64.9 0.5 collective-permute-start.10
  65.4 1.5 %collective-permute-start.12 = (bf16[4,512,128]{2,1,0:T(8,128)(2,1)S(1)}, bf16[4,512,128]{2,1,0:T(8,128)(2,1)S(1)}, u32[]{:S(2)}, u32[]{:S(2)}) collective-permute-start(bf16[4,512,128]{2,1,0:T(8,128)(2,1)S(1)} %get-tuple-element.45), channel_id=1, source_target_pairs={{0,2},{1,3},{2,0},{3,1},{4,6},{5,7},{6,4},{7,5},{8,10},{9,11},{10,... | collective-permute-start | bytes 1572872 | tf_op jit(solution)/shard_map/ppermute | solution.py:20
  66.9 2.0 %collective-permute-done.2 = f32[32,1024]{1,0:T(8,128)S(1)} collective-permute-done((f32[32,1024]{1,0:T(8,128)S(1)}, f32[32,1024]{1,0:T(8,128)S(1)}, u32[]{:S(2)}, u32[]{:S(2)}) %collective-permute-start.2) | collective-permute-done | bytes 131104 | tf_op jit(solution)/shard_map/ppermute | solution.py:20
  68.9 1.6 %collective-permute-start.3 = (f32[32,1024]{1,0:T(8,128)S(1)}, f32[32,1024]{1,0:T(8,128)S(1)}, u32[]{:S(2)}, u32[]{:S(2)}) collective-permute-start(f32[32,1024]{1,0:T(8,128)S(1)} %add.82), channel_id=1, source_target_pairs={{0,2},{1,3},{2,0},{3,1},{4,6},{5,7},{6,4},{7,5},{8,10},{9,11},{10,... | collective-permute-start | bytes 393224 | tf_op jit(solution)/shard_map/ppermute | solution.py:20
  70.5 1.2 add_convert_fusion.1
  71.7 0.6 collective-permute-start.7
  72.2 10.8 %collective-permute-done.3 = f32[32,1024]{1,0:T(8,128)S(1)} collective-permute-done((f32[32,1024]{1,0:T(8,128)S(1)}, f32[32,1024]{1,0:T(8,128)S(1)}, u32[]{:S(2)}, u32[]{:S(2)}) %collective-permute-start.3) | collective-permute-done | bytes 131104 | tf_op jit(solution)/shard_map/ppermute | solution.py:20
  83.1 0.5 collective-permute-start.4
  83.6 1.2 add_convert_fusion
  84.8 1.6 %collective-permute-start.9 = (bf16[2,512,256]{2,1,0:T(8,128)(2,1)S(1)}, bf16[2,512,256]{2,1,0:T(8,128)(2,1)S(1)}, u32[]{:S(2)}, u32[]{:S(2)}) collective-permute-start(bf16[2,512,256]{2,1,0:T(8,128)(2,1)S(1)} %add_convert_fusion), channel_id=1, source_target_pairs={{0,1},{1,0},{2,3},{3,2},{4,5},{5,4},{6,7},{7,6},{8,9},{9,8},{10,11... | collective-permute-start | bytes 1572872 | tf_op jit(solution)/shard_map/ppermute | solution.py:20
  86.4 0.5 collective-permute-start.14
  86.9 1.2 collective-permute-done.4
  88.2 1.6 %collective-permute-start.16 = (bf16[4,512,128]{2,1,0:T(8,128)(2,1)S(1)}, bf16[4,512,128]{2,1,0:T(8,128)(2,1)S(1)}, u32[]{:S(2)}, u32[]{:S(2)}) collective-permute-start(bf16[4,512,128]{2,1,0:T(8,128)(2,1)S(1)} %get-tuple-element.51), channel_id=1, source_target_pairs={{0,2},{1,3},{2,0},{3,1},{4,6},{5,7},{6,4},{7,5},{8,10},{9,11},{10,... | collective-permute-start | bytes 1572872 | tf_op jit(solution)/shard_map/ppermute | solution.py:20
  89.8 0.1 add_convert_fusion.7
  89.8 0.6 collective-permute-start.11
  90.4 17.8 %collective-permute-done.14.refs_15_ = bf16[4,512,128]{2,1,0:T(8,128)(2,1)S(1)} collective-permute-done((bf16[4,512,128]{2,1,0:T(8,128)(2,1)S(1)}, bf16[4,512,128]{2,1,0:T(8,128)(2,1)S(1)}, u32[]{:S(2)}, u32[]{:S(2)}) %collective-permute-start.14) | collective-permute-done | bytes 524320 | tf_op jit(solution)/shard_map/ppermute | solution.py:20
  108.2 1.3 collective-permute-start.13
  109.5 0.1 add_convert_fusion.5
  109.6 1.6 %collective-permute-start.15 = (bf16[2,512,128]{2,1,0:T(8,128)(2,1)S(1)}, bf16[2,512,128]{2,1,0:T(8,128)(2,1)S(1)}, u32[]{:S(2)}, u32[]{:S(2)}) collective-permute-start(bf16[2,512,128]{2,1,0:T(8,128)(2,1)S(1)} %add_convert_fusion.5), channel_id=1, source_target_pairs={{0,2},{1,3},{2,0},{3,1},{4,6},{5,7},{6,4},{7,5},{8,10},{9,11},{10,... | collective-permute-start | bytes 786440 | tf_op jit(solution)/shard_map/ppermute | solution.py:20
  111.1 0.1 add_convert_fusion.4
  111.2 0.6 collective-permute-start.17
  111.8 1.0 fusion
  112.8 1.2 collective-permute-start.5
  114.0 1.0 fusion.1
  115.1 3.0 %collective-permute-done.5.refs_1_ = bf16[32,1024]{1,0:T(8,128)(2,1)S(1)} collective-permute-done((bf16[32,1024]{1,0:T(8,128)(2,1)S(1)}, bf16[32,1024]{1,0:T(8,128)(2,1)S(1)}, u32[]{:S(2)}, u32[]{:S(2)}) %collective-permute-start.5) | collective-permute-done | bytes 65568 | tf_op jit(solution)/shard_map/ppermute | solution.py:20
  118.1 1.2 collective-permute-start.28
  119.3 1.7 %collective-permute-start.20 = (bf16[512,256]{1,0:T(8,128)(2,1)S(1)}, bf16[512,256]{1,0:T(8,128)(2,1)S(1)}, u32[]{:S(2)}, u32[]{:S(2)}) collective-permute-start(bf16[512,256]{1,0:T(8,128)(2,1)S(1)} %fusion.1), channel_id=1, source_target_pairs={{0,20},{1,21},{2,22},{3,23},{4,16},{5,17},{6,18},{7,19},{8,28},{9,... | collective-permute-start | bytes 786440 | tf_op jit(solution)/shard_map/ppermute | solution.py:30
  121.1 2.0 %shard_map.106 = bf16[512,1024]{1,0:T(8,128)(2,1)S(1)} custom-call(s32[1]{0:T(128)} %bitcast.refs_0_.pos_ref, s32[2,4]{1,0:T(2,128)S(1)} %bitcast.44, s32[2]{0:T(128)S(1)} %bitcast.50, bf16[8,2,32,512]{3,2,1,0:T(8,128)(2,1)S(1)} %bitcast.38, bf16[32,1024]{1,0:T(8,128)(2,1)S(1)} %add_convert_fusion.12.refs_0_, ...), custom_call_target="tpu_custom_call" | custom-call | flops 67108864 | bytes 5242880 | tf_op jit(solution)/shard_map/pallas_call | solution.py:291
  123.1 0.1 collective-permute-start.18
  123.3 1.7 %collective-permute-start.21 = (bf16[512,128]{1,0:T(8,128)(2,1)S(1)}, bf16[512,128]{1,0:T(8,128)(2,1)S(1)}, u32[]{:S(2)}, u32[]{:S(2)}) collective-permute-start(bf16[512,128]{1,0:T(8,128)(2,1)S(1)} %fusion.2), channel_id=1, source_target_pairs={{0,20},{1,21},{2,22},{3,23},{4,16},{5,17},{6,18},{7,19},{8,28},{9,... | collective-permute-start | bytes 393224 | tf_op jit(solution)/shard_map/ppermute | solution.py:30
  125.2 0.1 collective-permute-start.22
  125.4 3.8 %collective-permute-done.19.refs_0_ = bf16[512,256]{1,0:T(8,128)(2,1)S(1)} collective-permute-done((bf16[512,256]{1,0:T(8,128)(2,1)S(1)}, bf16[512,256]{1,0:T(8,128)(2,1)S(1)}, u32[]{:S(2)}, u32[]{:S(2)}) %collective-permute-start.19) | collective-permute-done | bytes 262176 | tf_op jit(solution)/shard_map/ppermute | solution.py:30
  129.2 0.8 collective-permute-start.23
  130.0 4.8 %collective-permute-done.20.refs_1_ = bf16[512,256]{1,0:T(8,128)(2,1)S(1)} collective-permute-done((bf16[512,256]{1,0:T(8,128)(2,1)S(1)}, bf16[512,256]{1,0:T(8,128)(2,1)S(1)}, u32[]{:S(2)}, u32[]{:S(2)}) %collective-permute-start.20) | collective-permute-done | bytes 262176 | tf_op jit(solution)/shard_map/ppermute | solution.py:30
  134.8 0.7 copy-done.15
  135.5 0.8 collective-permute-start.24
  136.3 3.1 %shard_map.109 = bf16[8,32,1024]{2,1,0:T(8,128)(2,1)} custom-call(s32[1]{0:T(128)} %bitcast.refs_0_.pos_ref, s32[2,4]{1,0:T(2,128)} %bitcast.39, s32[2]{0:T(128)} %bitcast.45, bf16[2,256,1024]{2,1,0:T(8,128)(2,1)} %bitcast.30, bf16[1,256,1024]{2,1,0:T(8,128)(2,1)} %bitcast.8.refs_3_.refs_4_, bf16[1,256,1024]{2,1,0:T(8,128)(2,1)} %bitcast.37, ...), custom_call_target="tpu_custom_call" | custom-call | flops 67108864 | bytes 2097152 | tf_op jit(solution)/shard_map/pallas_call | solution.py:239
  139.4 2.7 %shard_map.108 = bf16[8,2,32,512]{3,2,1,0:T(8,128)(2,1)} custom-call(s32[1]{0:T(128)} %bitcast.refs_0_.pos_ref, s32[2,4]{1,0:T(2,128)} %bitcast.40, s32[2]{0:T(128)} %bitcast.46, bf16[2,512,512]{2,1,0:T(8,128)(2,1)} %bitcast.54, bf16[32,1024]{1,0:T(8,128)(2,1)} %copy-done.5, bf16[32,1024]{1,0:T(8,128)(2,1)} %copy-done.7), custom_call_target="tpu_custom_call" | custom-call | flops 67108864 | bytes 1048576 | tf_op jit(solution)/shard_map/pallas_call | solution.py:350
  142.1 1.1 collective-permute-done.23.refs_4_
  143.2 2.8 %collective-permute-done.24.refs_5_ = bf16[512,128]{1,0:T(8,128)(2,1)S(1)} collective-permute-done((bf16[512,128]{1,0:T(8,128)(2,1)S(1)}, bf16[512,128]{1,0:T(8,128)(2,1)S(1)}, u32[]{:S(2)}, u32[]{:S(2)}) %collective-permute-start.24) | collective-permute-done | bytes 131104 | tf_op jit(solution)/shard_map/ppermute | solution.py:30
  146.0 0.6 copy-done.20
  146.7 1.0 copy-done.13
  147.6 3.1 %shard_map.107 = bf16[2,512,512]{2,1,0:T(8,128)(2,1)} custom-call(s32[1]{0:T(128)} %bitcast.refs_0_.pos_ref, bf16[512,1024]{1,0:T(8,128)(2,1)} %copy-done.13, bf16[512,256]{1,0:T(8,128)(2,1)} %copy-done.14, bf16[512,256]{1,0:T(8,128)(2,1)} %copy-done.15, bf16[512,128]{1,0:T(8,128)(2,1)} %copy-done.17, bf16[512,128]{1,0:T(8,128)(2,1)} %copy-done.18, ...), custom_call_target="tpu_custom_call" | custom-call | tf_op jit(solution)/shard_map/pallas_call | solution.py:323
  (69 shorter events, 0.5 us)
Async XLA Ops:
  2.5 27.5 %collective-permute-start = (bf16[256,1024]{1,0:T(8,128)(2,1)}, bf16[256,1024]{1,0:T(8,128)(2,1)}, u32[]{:S(2)}, u32[]{:S(2)}) collective-permute-start(bf16[256,1024]{1,0:T(8,128)(2,1)} %slice_bitcast_fusion.1), channel_id=1, source_target_pairs={{0,8},{1,9},{2,10},{3,11},{4,12},{5,13},{6,14},{7,15},{8,0},{9,1},... | collective-permute-start | bytes 1572872 | tf_op jit(solution)/shard_map/ppermute | solution.py:20
  6.5 1.2 copy-start
  7.8 1.0 copy-start.2
  8.8 0.7 copy-start.8
  9.5 0.7 copy-start.10
  10.1 9.7 %copy-start.21 = (bf16[1,2,32,64]{3,2,1,0:T(8,128)(2,1)S(1)}, bf16[1,2,32,64]{3,2,1,0:T(8,128)(2,1)}, u32[]{:S(2)}) copy-start(bf16[1,2,32,64]{3,2,1,0:T(8,128)(2,1)} %param.10) | copy-start | bytes 24580
  10.1 19.9 %copy-start.1 = (bf16[1,1,2,256,1024]{4,3,2,1,0:T(8,128)(2,1)S(1)}, bf16[1,1,2,256,1024]{4,3,2,1,0:T(8,128)(2,1)}, u32[]{:S(2)}) copy-start(bf16[1,1,2,256,1024]{4,3,2,1,0:T(8,128)(2,1)} %param.8) | copy-start | bytes 3145732
  10.1 38.4 %copy-start.9 = (s32[1,2,4]{2,1,0:T(2,128)S(1)}, s32[1,2,4]{2,1,0:T(2,128)}, u32[]{:S(2)}) copy-start(s32[1,2,4]{2,1,0:T(2,128)} %param.14) | copy-start | bytes 100
  10.1 38.4 %copy-start.11 = (s32[1,2]{1,0:T(1,128)S(1)}, s32[1,2]{1,0:T(1,128)}, u32[]{:S(2)}) copy-start(s32[1,2]{1,0:T(1,128)} %param.15) | copy-start | bytes 28
  19.8 4.0 %collective-permute-start.25 = (bf16[2,32,64]{2,1,0:T(8,128)(2,1)S(1)}, bf16[2,32,64]{2,1,0:T(8,128)(2,1)S(1)}, u32[]{:S(2)}, u32[]{:S(2)}) collective-permute-start(bf16[2,32,64]{2,1,0:T(8,128)(2,1)S(1)} %bitcast.58), channel_id=1, source_target_pairs={{0,1},{1,0},{2,3},{3,2},{4,5},{5,4},{6,7},{7,6},{8,9},{9,8},{10,11... | collective-permute-start | bytes 24584 | tf_op jit(solution)/shard_map/ppermute | solution.py:20
  21.4 43.5 %collective-permute-start.6 = (bf16[4,512,256]{2,1,0:T(8,128)(2,1)}, bf16[4,512,256]{2,1,0:T(8,128)(2,1)}, u32[]{:S(2)}, u32[]{:S(2)}) collective-permute-start(bf16[4,512,256]{2,1,0:T(8,128)(2,1)} %get-tuple-element.37), channel_id=1, source_target_pairs={{0,1},{1,0},{2,3},{3,2},{4,5},{5,4},{6,7},{7,6},{8,9},{9,8},{10,11... | collective-permute-start | bytes 3145736 | tf_op jit(solution)/shard_map/ppermute | solution.py:20
  21.9 43.5 %collective-permute-start.8 = (bf16[4,512,256]{2,1,0:T(8,128)(2,1)}, bf16[4,512,256]{2,1,0:T(8,128)(2,1)}, u32[]{:S(2)}, u32[]{:S(2)}) collective-permute-start(bf16[4,512,256]{2,1,0:T(8,128)(2,1)} %get-tuple-element.39), channel_id=1, source_target_pairs={{0,2},{1,3},{2,0},{3,1},{4,6},{5,7},{6,4},{7,5},{8,10},{9,11},{10,... | collective-permute-start | bytes 3145736 | tf_op jit(solution)/shard_map/ppermute | solution.py:20
  23.8 23.1 %collective-permute-start.26 = (bf16[2,64,64]{2,1,0:T(8,128)(2,1)S(1)}, bf16[2,64,64]{2,1,0:T(8,128)(2,1)S(1)}, u32[]{:S(2)}, u32[]{:S(2)}) collective-permute-start(bf16[2,64,64]{2,1,0:T(8,128)(2,1)S(1)} %maximum_select_fusion.2), channel_id=1, source_target_pairs={{0,2},{1,3},{2,0},{3,1},{4,6},{5,7},{6,4},{7,5},{8,10},{9,11},{10,... | collective-permute-start | bytes 49160 | tf_op jit(solution)/shard_map/ppermute | solution.py:20
  30.8 25.7 %collective-permute-start.1 = (bf16[256,1024]{1,0:T(8,128)(2,1)}, bf16[256,1024]{1,0:T(8,128)(2,1)S(1)}, u32[]{:S(2)}, u32[]{:S(2)}) collective-permute-start(bf16[256,1024]{1,0:T(8,128)(2,1)} %slice_bitcast_fusion), channel_id=1, source_target_pairs={{0,8},{1,9},{2,10},{3,11},{4,12},{5,13},{6,14},{7,15},{8,0},{9,1},... | collective-permute-start | bytes 1572872 | tf_op jit(solution)/shard_map/ppermute | solution.py:20
  46.9 17.1 %collective-permute-start.27 = (bf16[2,128,64]{2,1,0:T(8,128)(2,1)S(1)}, bf16[2,128,64]{2,1,0:T(8,128)(2,1)S(1)}, u32[]{:S(2)}, u32[]{:S(2)}) collective-permute-start(bf16[2,128,64]{2,1,0:T(8,128)(2,1)S(1)} %maximum_select_fusion.1), channel_id=1, source_target_pairs={{0,4},{1,5},{2,6},{3,7},{4,0},{5,1},{6,2},{7,3},{8,12},{9,13},{10,... | collective-permute-start | bytes 98312 | tf_op jit(solution)/shard_map/ppermute | solution.py:20
  48.6 1.0 copy-start.3
  56.5 5.9 %copy-start.4 = (bf16[256,1024]{1,0:T(8,128)(2,1)}, bf16[256,1024]{1,0:T(8,128)(2,1)S(1)}, u32[]{:S(2)}) copy-start(bf16[256,1024]{1,0:T(8,128)(2,1)S(1)} %collective-permute-done.1) | copy-start | bytes 1572868
  62.4 21.2 %copy-start.12 = (f32[4,512,256]{2,1,0:T(8,128)S(1)}, f32[4,512,256]{2,1,0:T(8,128)}, u32[]{:S(2)}) copy-start(f32[4,512,256]{2,1,0:T(8,128)} %get-tuple-element.38.refs_5_) | copy-start | bytes 6291460
  62.5 6.4 %collective-permute-start.2 = (f32[32,1024]{1,0:T(8,128)S(1)}, f32[32,1024]{1,0:T(8,128)S(1)}, u32[]{:S(2)}, u32[]{:S(2)}) collective-permute-start(f32[32,1024]{1,0:T(8,128)S(1)} %constant_dynamic-update-slice_fusion), channel_id=1, source_target_pairs={{0,1},{1,0},{2,3},{3,2},{4,5},{5,4},{6,7},{7,6},{8,9},{9,8},{10,11... | collective-permute-start | bytes 393224 | tf_op jit(solution)/shard_map/ppermute | solution.py:20
  64.9 21.5 %collective-permute-start.10 = (bf16[4,512,128]{2,1,0:T(8,128)(2,1)S(1)}, bf16[4,512,128]{2,1,0:T(8,128)(2,1)S(1)}, u32[]{:S(2)}, u32[]{:S(2)}) collective-permute-start(bf16[4,512,128]{2,1,0:T(8,128)(2,1)S(1)} %get-tuple-element.42), channel_id=1, source_target_pairs={{0,1},{1,0},{2,3},{3,2},{4,5},{5,4},{6,7},{7,6},{8,9},{9,8},{10,11... | collective-permute-start | bytes 1572872 | tf_op jit(solution)/shard_map/ppermute | solution.py:20
  65.4 22.8 %collective-permute-start.12 = (bf16[4,512,128]{2,1,0:T(8,128)(2,1)S(1)}, bf16[4,512,128]{2,1,0:T(8,128)(2,1)S(1)}, u32[]{:S(2)}, u32[]{:S(2)}) collective-permute-start(bf16[4,512,128]{2,1,0:T(8,128)(2,1)S(1)} %get-tuple-element.45), channel_id=1, source_target_pairs={{0,2},{1,3},{2,0},{3,1},{4,6},{5,7},{6,4},{7,5},{8,10},{9,11},{10,... | collective-permute-start | bytes 1572872 | tf_op jit(solution)/shard_map/ppermute | solution.py:20
  68.9 14.2 %collective-permute-start.3 = (f32[32,1024]{1,0:T(8,128)S(1)}, f32[32,1024]{1,0:T(8,128)S(1)}, u32[]{:S(2)}, u32[]{:S(2)}) collective-permute-start(f32[32,1024]{1,0:T(8,128)S(1)} %add.82), channel_id=1, source_target_pairs={{0,2},{1,3},{2,0},{3,1},{4,6},{5,7},{6,4},{7,5},{8,10},{9,11},{10,... | collective-permute-start | bytes 393224 | tf_op jit(solution)/shard_map/ppermute | solution.py:20
  71.7 39.5 %collective-permute-start.7 = (bf16[2,512,256]{2,1,0:T(8,128)(2,1)S(1)}, bf16[2,512,256]{2,1,0:T(8,128)(2,1)S(1)}, u32[]{:S(2)}, u32[]{:S(2)}) collective-permute-start(bf16[2,512,256]{2,1,0:T(8,128)(2,1)S(1)} %add_convert_fusion.1), channel_id=1, source_target_pairs={{0,2},{1,3},{2,0},{3,1},{4,6},{5,7},{6,4},{7,5},{8,10},{9,11},{10,... | collective-permute-start | bytes 1572872 | tf_op jit(solution)/shard_map/ppermute | solution.py:20
  83.1 5.0 %collective-permute-start.4 = (f32[32,1024]{1,0:T(8,128)S(1)}, f32[32,1024]{1,0:T(8,128)S(1)}, u32[]{:S(2)}, u32[]{:S(2)}) collective-permute-start(f32[32,1024]{1,0:T(8,128)S(1)} %add.83), channel_id=1, source_target_pairs={{0,4},{1,5},{2,6},{3,7},{4,0},{5,1},{6,2},{7,3},{8,12},{9,13},{10,... | collective-permute-start | bytes 393224 | tf_op jit(solution)/shard_map/ppermute | solution.py:20
  84.8 28.0 %collective-permute-start.9 = (bf16[2,512,256]{2,1,0:T(8,128)(2,1)S(1)}, bf16[2,512,256]{2,1,0:T(8,128)(2,1)S(1)}, u32[]{:S(2)}, u32[]{:S(2)}) collective-permute-start(bf16[2,512,256]{2,1,0:T(8,128)(2,1)S(1)} %add_convert_fusion), channel_id=1, source_target_pairs={{0,1},{1,0},{2,3},{3,2},{4,5},{5,4},{6,7},{7,6},{8,9},{9,8},{10,11... | collective-permute-start | bytes 1572872 | tf_op jit(solution)/shard_map/ppermute | solution.py:20
  86.4 21.8 %collective-permute-start.14 = (bf16[4,512,128]{2,1,0:T(8,128)(2,1)S(1)}, bf16[4,512,128]{2,1,0:T(8,128)(2,1)S(1)}, u32[]{:S(2)}, u32[]{:S(2)}) collective-permute-start(bf16[4,512,128]{2,1,0:T(8,128)(2,1)S(1)} %get-tuple-element.48), channel_id=1, source_target_pairs={{0,1},{1,0},{2,3},{3,2},{4,5},{5,4},{6,7},{7,6},{8,9},{9,8},{10,11... | collective-permute-start | bytes 1572872 | tf_op jit(solution)/shard_map/ppermute | solution.py:20
  88.1 32.9 %copy-start.5 = (bf16[32,1024]{1,0:T(8,128)(2,1)}, bf16[32,1024]{1,0:T(8,128)(2,1)S(1)}, u32[]{:S(2)}) copy-start(bf16[32,1024]{1,0:T(8,128)(2,1)S(1)} %add_convert_fusion.12.refs_0_) | copy-start | bytes 196612
  88.2 21.4 %collective-permute-start.16 = (bf16[4,512,128]{2,1,0:T(8,128)(2,1)S(1)}, bf16[4,512,128]{2,1,0:T(8,128)(2,1)S(1)}, u32[]{:S(2)}, u32[]{:S(2)}) collective-permute-start(bf16[4,512,128]{2,1,0:T(8,128)(2,1)S(1)} %get-tuple-element.51), channel_id=1, source_target_pairs={{0,2},{1,3},{2,0},{3,1},{4,6},{5,7},{6,4},{7,5},{8,10},{9,11},{10,... | collective-permute-start | bytes 1572872 | tf_op jit(solution)/shard_map/ppermute | solution.py:20
  89.8 29.5 %collective-permute-start.11 = (bf16[2,512,128]{2,1,0:T(8,128)(2,1)S(1)}, bf16[2,512,128]{2,1,0:T(8,128)(2,1)S(1)}, u32[]{:S(2)}, u32[]{:S(2)}) collective-permute-start(bf16[2,512,128]{2,1,0:T(8,128)(2,1)S(1)} %add_convert_fusion.7), channel_id=1, source_target_pairs={{0,2},{1,3},{2,0},{3,1},{4,6},{5,7},{6,4},{7,5},{8,10},{9,11},{10,... | collective-permute-start | bytes 786440 | tf_op jit(solution)/shard_map/ppermute | solution.py:20
  108.2 11.1 %collective-permute-start.13 = (bf16[2,512,128]{2,1,0:T(8,128)(2,1)S(1)}, bf16[2,512,128]{2,1,0:T(8,128)(2,1)S(1)}, u32[]{:S(2)}, u32[]{:S(2)}) collective-permute-start(bf16[2,512,128]{2,1,0:T(8,128)(2,1)S(1)} %add_convert_fusion.6), channel_id=1, source_target_pairs={{0,1},{1,0},{2,3},{3,2},{4,5},{5,4},{6,7},{7,6},{8,9},{9,8},{10,11... | collective-permute-start | bytes 786440 | tf_op jit(solution)/shard_map/ppermute | solution.py:20
  109.5 11.5 %copy-start.6 = (bf16[1,8,64,512]{3,2,1,0:T(8,128)(2,1)S(1)}, bf16[1,8,64,512]{3,2,1,0:T(8,128)(2,1)}, u32[]{:S(2)}) copy-start(bf16[1,8,64,512]{3,2,1,0:T(8,128)(2,1)} %param.12) | copy-start | bytes 1572868
  109.6 11.5 %collective-permute-start.15 = (bf16[2,512,128]{2,1,0:T(8,128)(2,1)S(1)}, bf16[2,512,128]{2,1,0:T(8,128)(2,1)S(1)}, u32[]{:S(2)}, u32[]{:S(2)}) collective-permute-start(bf16[2,512,128]{2,1,0:T(8,128)(2,1)S(1)} %add_convert_fusion.5), channel_id=1, source_target_pairs={{0,2},{1,3},{2,0},{3,1},{4,6},{5,7},{6,4},{7,5},{8,10},{9,11},{10,... | collective-permute-start | bytes 786440 | tf_op jit(solution)/shard_map/ppermute | solution.py:20
  111.2 9.9 %collective-permute-start.17 = (bf16[2,512,128]{2,1,0:T(8,128)(2,1)S(1)}, bf16[2,512,128]{2,1,0:T(8,128)(2,1)S(1)}, u32[]{:S(2)}, u32[]{:S(2)}) collective-permute-start(bf16[2,512,128]{2,1,0:T(8,128)(2,1)S(1)} %add_convert_fusion.4), channel_id=1, source_target_pairs={{0,1},{1,0},{2,3},{3,2},{4,5},{5,4},{6,7},{7,6},{8,9},{9,8},{10,11... | collective-permute-start | bytes 786440 | tf_op jit(solution)/shard_map/ppermute | solution.py:20
  112.8 5.2 %collective-permute-start.5 = (bf16[32,1024]{1,0:T(8,128)(2,1)S(1)}, bf16[32,1024]{1,0:T(8,128)(2,1)S(1)}, u32[]{:S(2)}, u32[]{:S(2)}) collective-permute-start(bf16[32,1024]{1,0:T(8,128)(2,1)S(1)} %add_convert_fusion.12.refs_0_), channel_id=1, source_target_pairs={{0,8},{1,9},{2,10},{3,11},{4,12},{5,13},{6,14},{7,15},{8,0},{9,1},... | collective-permute-start | bytes 196616 | tf_op jit(solution)/shard_map/ppermute | solution.py:20
  118.1 5.0 %copy-start.7 = (bf16[32,1024]{1,0:T(8,128)(2,1)}, bf16[32,1024]{1,0:T(8,128)(2,1)S(1)}, u32[]{:S(2)}) copy-start(bf16[32,1024]{1,0:T(8,128)(2,1)S(1)} %collective-permute-done.5.refs_1_) | copy-start | bytes 196612
  118.1 7.1 %collective-permute-start.28 = (bf16[2,256,32]{2,1,0:T(8,128)(2,1)S(1)}, bf16[2,256,32]{2,1,0:T(8,128)(2,1)S(1)}, u32[]{:S(2)}, u32[]{:S(2)}) collective-permute-start(bf16[2,256,32]{2,1,0:T(8,128)(2,1)S(1)} %get-tuple-element.53), channel_id=1, source_target_pairs={{0,8},{1,9},{2,10},{3,11},{4,12},{5,13},{6,14},{7,15},{8,0},{9,1},... | collective-permute-start | bytes 98312 | tf_op jit(solution)/shard_map/ppermute | solution.py:20
  119.3 9.8 %collective-permute-start.19 = (bf16[512,256]{1,0:T(8,128)(2,1)S(1)}, bf16[512,256]{1,0:T(8,128)(2,1)S(1)}, u32[]{:S(2)}, u32[]{:S(2)}) collective-permute-start(bf16[512,256]{1,0:T(8,128)(2,1)S(1)} %fusion), channel_id=1, source_target_pairs={{0,20},{1,21},{2,22},{3,23},{4,16},{5,17},{6,18},{7,19},{8,28},{9,... | collective-permute-start | bytes 786440 | tf_op jit(solution)/shard_map/ppermute | solution.py:30
  119.3 15.4 %collective-permute-start.20 = (bf16[512,256]{1,0:T(8,128)(2,1)S(1)}, bf16[512,256]{1,0:T(8,128)(2,1)S(1)}, u32[]{:S(2)}, u32[]{:S(2)}) collective-permute-start(bf16[512,256]{1,0:T(8,128)(2,1)S(1)} %fusion.1), channel_id=1, source_target_pairs={{0,20},{1,21},{2,22},{3,23},{4,16},{5,17},{6,18},{7,19},{8,28},{9,... | collective-permute-start | bytes 786440 | tf_op jit(solution)/shard_map/ppermute | solution.py:30
  123.1 22.9 %collective-permute-start.18 = (bf16[512,1024]{1,0:T(8,128)(2,1)S(1)}, bf16[512,1024]{1,0:T(8,128)(2,1)S(1)}, u32[]{:S(2)}, u32[]{:S(2)}) collective-permute-start(bf16[512,1024]{1,0:T(8,128)(2,1)S(1)} %shard_map.106), channel_id=1, source_target_pairs={{0,16},{1,17},{2,18},{3,19},{4,20},{5,21},{6,22},{7,23},{8,24},{9,... | collective-permute-start | bytes 3145736 | tf_op jit(solution)/shard_map/ppermute | solution.py:30
  123.3 18.7 %collective-permute-start.21 = (bf16[512,128]{1,0:T(8,128)(2,1)S(1)}, bf16[512,128]{1,0:T(8,128)(2,1)S(1)}, u32[]{:S(2)}, u32[]{:S(2)}) collective-permute-start(bf16[512,128]{1,0:T(8,128)(2,1)S(1)} %fusion.2), channel_id=1, source_target_pairs={{0,20},{1,21},{2,22},{3,23},{4,16},{5,17},{6,18},{7,19},{8,28},{9,... | collective-permute-start | bytes 393224 | tf_op jit(solution)/shard_map/ppermute | solution.py:30
  125.2 11.1 %copy-start.16 = (bf16[2,256,32]{2,1,0:T(8,128)(2,1)}, bf16[2,256,32]{2,1,0:T(8,128)(2,1)S(1)}, u32[]{:S(2)}) copy-start(bf16[2,256,32]{2,1,0:T(8,128)(2,1)S(1)} %collective-permute-done.28.refs_7_) | copy-start | bytes 98308
  125.2 16.8 %collective-permute-start.22 = (bf16[512,128]{1,0:T(8,128)(2,1)S(1)}, bf16[512,128]{1,0:T(8,128)(2,1)S(1)}, u32[]{:S(2)}, u32[]{:S(2)}) collective-permute-start(bf16[512,128]{1,0:T(8,128)(2,1)S(1)} %fusion.3), channel_id=1, source_target_pairs={{0,20},{1,21},{2,22},{3,23},{4,16},{5,17},{6,18},{7,19},{8,28},{9,... | collective-permute-start | bytes 393224 | tf_op jit(solution)/shard_map/ppermute | solution.py:30
  129.1 12.9 %copy-start.14 = (bf16[512,256]{1,0:T(8,128)(2,1)}, bf16[512,256]{1,0:T(8,128)(2,1)S(1)}, u32[]{:S(2)}) copy-start(bf16[512,256]{1,0:T(8,128)(2,1)S(1)} %collective-permute-done.19.refs_0_) | copy-start | bytes 786436
  129.2 14.0 %collective-permute-start.23 = (bf16[512,128]{1,0:T(8,128)(2,1)S(1)}, bf16[512,128]{1,0:T(8,128)(2,1)S(1)}, u32[]{:S(2)}, u32[]{:S(2)}) collective-permute-start(bf16[512,128]{1,0:T(8,128)(2,1)S(1)} %fusion.4), channel_id=1, source_target_pairs={{0,20},{1,21},{2,22},{3,23},{4,16},{5,17},{6,18},{7,19},{8,28},{9,... | collective-permute-start | bytes 393224 | tf_op jit(solution)/shard_map/ppermute | solution.py:30
  134.8 0.7 copy-start.15
  135.5 10.5 %collective-permute-start.24 = (bf16[512,128]{1,0:T(8,128)(2,1)S(1)}, bf16[512,128]{1,0:T(8,128)(2,1)S(1)}, u32[]{:S(2)}, u32[]{:S(2)}) collective-permute-start(bf16[512,128]{1,0:T(8,128)(2,1)S(1)} %fusion.5), channel_id=1, source_target_pairs={{0,20},{1,21},{2,22},{3,23},{4,16},{5,17},{6,18},{7,19},{8,28},{9,... | collective-permute-start | bytes 393224 | tf_op jit(solution)/shard_map/ppermute | solution.py:30
  142.0 4.0 %copy-start.17 = (bf16[512,128]{1,0:T(8,128)(2,1)}, bf16[512,128]{1,0:T(8,128)(2,1)S(1)}, u32[]{:S(2)}) copy-start(bf16[512,128]{1,0:T(8,128)(2,1)S(1)} %collective-permute-done.21.refs_2_) | copy-start | bytes 393220
  142.0 4.0 %copy-start.18 = (bf16[512,128]{1,0:T(8,128)(2,1)}, bf16[512,128]{1,0:T(8,128)(2,1)S(1)}, u32[]{:S(2)}) copy-start(bf16[512,128]{1,0:T(8,128)(2,1)S(1)} %collective-permute-done.22.refs_3_) | copy-start | bytes 393220
  143.2 2.8 %copy-start.19 = (bf16[512,128]{1,0:T(8,128)(2,1)}, bf16[512,128]{1,0:T(8,128)(2,1)S(1)}, u32[]{:S(2)}) copy-start(bf16[512,128]{1,0:T(8,128)(2,1)S(1)} %collective-permute-done.23.refs_4_) | copy-start | bytes 393220
  146.0 0.6 copy-start.20
  146.6 1.0 copy-start.13

commit v5 on v4

--- a/solution.py
+++ b/solution.py
@@ -35,111 +35,111 @@
     return ((high ^ k) * tile_rows + offset) // SEG
 
 
-def product_body(low_size, tile_rows, pieces, tiles, half, *refs):
+def product_body(low_size, tile_rows, pieces, tiles, half, sends, keeps, *refs):
     pos_ref, classes_ref, live_ref = refs[:3]
     grad_refs = refs[3 : 3 + tiles]
-    weight_hbm, up_ref, sent_x, kept_x, sent_y, kept_y, rank_ref, rows_ref, weight_ref, sems = refs[
-        3 + tiles :
-    ]
-    step = pl.program_id(0)
+    weight_hbm = refs[3 + tiles]
+    rows_ref, weight_ref, sems = refs[-3:]
+    rest = list(refs[4 + tiles : -3])
+    up_ref = rest.pop(0) if keeps else None
+    sent_x, sent_y = (rest.pop(0), rest.pop(0)) if sends else (None, None)
+    kept_x, kept_y, rank_ref = rest if keeps else (None, None, None)
     low, high = pos_ref[0] % low_size, pos_ref[0] // low_size
     size = pieces[0][3]
-
-    def weight_copy(k):
-        block = (1 - k // 4 + (2 - (k & 2)) + 4 * (k & 1)) ^ low
-        return pltpu.make_async_copy(weight_hbm.at[block], weight_ref.at[k], sems.at[k])
-
-    @pl.when(step == 0)
-    def _():
-        for k in range(low_size):
-            weight_copy(k).start()
-        for at, (tile, index, piece, _) in enumerate(pieces):
-            seg = segment_of(high, piece, tile_rows)
-            alive = seg < live_ref[piece[1]]
-            place = slice(at * size, (at + 1) * size)
-
-            @pl.when(alive)
-            def _():
-                rows = grad_refs[tile][index, piece[2] : piece[2] + size, :].T
-                rows_ref[:, place] = rows
+    total = rows_ref.shape[1]
+
+    def weight_copy(block):
+        return pltpu.make_async_copy(
+            weight_hbm.at[block ^ low], weight_ref.at[block], sems.at[block]
+        )
+
+    jobs = []
+    for x, y in ((1, 1), (1, 0), (0, 1), (0, 0)):
+        to_x = (sent_x if x else kept_x, 2 * y)
+        to_y = (sent_y if y else kept_y, 2 * x)
+        start = 0 if to_x[0] is not None else half
+        stop = total if to_y[0] is not None else half
+        if start < stop:
+            jobs.append((x + 2 * y, start, stop, to_x, to_y))
+    for block, *_ in jobs:
+        for z in range(2):
+            weight_copy(block + 4 * z).start()
+
+    for at, (tile, index, piece, _) in enumerate(pieces):
+        seg = segment_of(high, piece, tile_rows)
+        alive = seg < live_ref[piece[1]]
+        place = slice(at * size, (at + 1) * size)
+
+        @pl.when(alive)
+        def _():
+            rows = grad_refs[tile][index, piece[2] : piece[2] + size, :].T
+            rows_ref[:, place] = rows
+            if keeps:
                 up = up_ref[classes_ref[piece[1], seg]]
                 rank_ref[:, place] = jnp.dot(up, rows, preferred_element_type=F32)
 
-            @pl.when(jnp.logical_not(alive))
-            def _():
-                rows_ref[:, place] = jnp.zeros((rows_ref.shape[0], size), rows_ref.dtype)
+        @pl.when(jnp.logical_not(alive))
+        def _():
+            rows_ref[:, place] = jnp.zeros((rows_ref.shape[0], size), rows_ref.dtype)
+            if keeps:
                 rank_ref[:, place] = jnp.zeros((rank_ref.shape[0], size), F32)
 
-    weight_copy(step).wait()
-    value = jnp.dot(weight_ref[step], rows_ref[...], preferred_element_type=F32)
-
-    @pl.when(step < 4)
-    def _():
-        sent_x[0] = value[:, :half].astype(BF16)
-
-    @pl.when(step >= 4)
-    def _():
-        kept_x[0] = value[:, :half]
-
-    @pl.when(step & 2 == 0)
-    def _():
-        sent_y[0] = value[:, half:].astype(BF16)
-
-    @pl.when(step & 2 != 0)
-    def _():
-        kept_y[0] = value[:, half:]
-
-
-def product(scalars, grads, pieces, weight_blocks, up_tile, low_size):
+    for block, start, stop, to_x, to_y in jobs:
+
+        @pl.loop(0, 2)
+        def _(z):
+            weight_copy(block + 4 * z).wait()
+            value = jnp.dot(
+                weight_ref[block + 4 * z], rows_ref[:, start:stop], preferred_element_type=F32
+            )
+            if to_x[0] is not None:
+                to_x[0][to_x[1] + z] = value[:, : half - start].astype(to_x[0].dtype)
+            if to_y[0] is not None:
+                to_y[0][to_y[1] + z] = value[:, half - start :].astype(to_y[0].dtype)
+
+
+def product(scalars, grads, pieces, weight_blocks, up_tile, low_size, sends, keeps):
     blocks, width, depth = weight_blocks.shape
     tile_rows = grads[0].shape[1]
     rows = len(pieces) * pieces[0][3]
     half = rows // 2
     if rows > 128 and half % 128:
         half = half // 128 * 128 + 128
-
-    def whole(array):
-        return pl.BlockSpec(array.shape, lambda k, *_: (0,) * array.ndim)
-
-    def by_y(k):
-        return 2 - (k & 2) + (k & 1)
-
-    outs = [
-        (half, BF16, lambda k: jnp.where(k < 4, by_y(k), 1)),
-        (half, F32, lambda k: jnp.where(k < 4, 2, by_y(k))),
-        (rows - half, BF16, lambda k: 2 * (1 - k // 4) + jnp.where(k & 2 == 0, k & 1, 1)),
-        (rows - half, F32, lambda k: 2 * (1 - k // 4) + jnp.where(k & 2 == 0, 0, k & 1)),
-    ]
-    rank_part = up_tile.shape[1]
+    outs = []
+    for wanted, dtype in ((sends, BF16), (keeps, F32)):
+        if wanted:
+            outs += [
+                jax.ShapeDtypeStruct((blocks // 2, width, n), dtype) for n in (half, rows - half)
+            ]
+    if keeps:
+        outs.append(jax.ShapeDtypeStruct((up_tile.shape[1], rows), F32))
+    share = (sends + keeps) / 2
     return pl.pallas_call(
-        functools.partial(product_body, low_size, tile_rows, pieces, len(grads), half),
-        grid_spec=pltpu.PrefetchScalarGridSpec(
-            num_scalar_prefetch=3,
-            grid=(blocks,),
-            in_specs=[whole(g) for g in grads]
-            + [pl.BlockSpec(memory_space=pl.ANY), whole(up_tile)],
-            out_specs=[
-                pl.BlockSpec((1, width, count), lambda k, *_, place=place: (place(k), 0, 0))
-                for count, _, place in outs
-            ]
-            + [pl.BlockSpec((rank_part, rows), lambda k, *_: (0, 0))],
-            scratch_shapes=[
-                pltpu.VMEM((depth, rows), BF16),
-                pltpu.VMEM(weight_blocks.shape, BF16),
-                pltpu.SemaphoreType.DMA((blocks,)),
-            ],
+        functools.partial(
+            product_body, low_size, tile_rows, pieces, len(grads), half, sends, keeps
         ),
-        out_shape=[
-            jax.ShapeDtypeStruct((blocks // 2, width, count), dtype) for count, dtype, _ in outs
-        ]
-        + [jax.ShapeDtypeStruct((rank_part, rows), F32)],
-        compiler_params=pltpu.CompilerParams(vmem_limit_bytes=48 * 2**20),
+        in_specs=[SMEM] * 3
+        + [VMEM] * len(grads)
+        + [pl.BlockSpec(memory_space=pl.ANY)]
+        + [VMEM] * keeps,
+        out_specs=[VMEM] * len(outs),
+        out_shape=outs,
+        scratch_shapes=[
+            pltpu.VMEM((depth, rows), BF16),
+            pltpu.VMEM(weight_blocks.shape, BF16),
+            pltpu.SemaphoreType.DMA((blocks,)),
+        ],
+        compiler_params=pltpu.CompilerParams(vmem_limit_bytes=32 * 2**20),
         cost_estimate=pl.CostEstimate(
-            flops=2 * blocks * rows * width * depth,
-            bytes_accessed=2 * blocks * width * depth + 3 * blocks * rows * width,
+            flops=int(2 * share * blocks * rows * width * depth),
+            bytes_accessed=int(share * (2 * blocks * width * depth + 3 * blocks * rows * width)),
             transcendentals=0,
         ),
-    )(*scalars, *grads, weight_blocks, up_tile)
+    )(*scalars, *grads, weight_blocks, *([up_tile] * keeps))
+
+
+def after(value, *others):
+    return lax.optimization_barrier((value, *others))[0]
 
 
 def up_body(low_size, tile_rows, pieces, tiles, *refs):
@@ -182,55 +182,100 @@
     rank, portion = adapter_down_maps.shape[2:]
     tiles = lax.axis_size("tensor")
     low_size = min(tiles, 8)
-    low_bits = low_size.bit_length() - 1
     high_size = tiles // low_size
     position = lax.axis_index("tensor")
     high = position // low_size
     weight_blocks = projection_weight[0, 0].reshape(low_size, portion, tile_cols)
-    scalars = (position.astype(jnp.int32)[None], segment_adapter_class[0], live_segment_table[0])
+    position, classes, live = lax.optimization_barrier(
+        (position.astype(jnp.int32)[None], segment_adapter_class[0] + 0, live_segment_table[0] + 0)
+    )
+    scalars = position, classes, live
+    position = position[0]
     size = min(SEG, tile_rows)
     offsets = range(0, tile_rows, size)
 
+    def send_rows(source, m):
+        return [partner(source[m], k * low_size)[None] for k in range(1, high_size)]
+
+    def pieces_of(m):
+        return [(k - 1, 0, (k, m, o), size) for k in range(1, high_size) for o in offsets]
+
     own_pieces = [(0, m, (0, m, o), size) for m in range(micro_count) for o in offsets]
-    chunks = [([grad_tile], own_pieces)]
-    source = grad_tile
-    for m in range(micro_count):
-        got = [partner(source[m], k * low_size)[None] for k in range(1, high_size)]
-        *got, source = lax.optimization_barrier((*got, source))
-        pieces = [(k - 1, 0, (k, m, o), size) for k in range(1, high_size) for o in offsets]
-        chunks.append((got, pieces))
-    order = [piece for _, pieces in chunks for _, _, piece, _ in pieces]
+
+    def produce(grads, pieces, sends, keeps):
+        return product(scalars, grads, pieces, weight_blocks, up_tile, low_size, sends, keeps)
 
     hidden = saved_rank_outputs[0]
-    sums, got_last, parts = [], [], []
-    arrived = [None, None]
-    for grads, pieces in chunks:
-        sent_x, kept_x, sent_y, kept_y, part = product(
-            scalars, grads, pieces, weight_blocks, up_tile, low_size
-        )
-        parts.append(part)
-        if not sums:
-            sent_x, sent_y, hidden = lax.optimization_barrier((sent_x, sent_y, hidden))
-        ways = (((0, 1, 2), sent_x, kept_x), ((1, 0, 2), sent_y, kept_y))
-        for way, (bits, sent, kept) in enumerate(ways):
-            if arrived[way] is not None:
-                sent, _ = lax.optimization_barrier((sent, arrived[way]))
-            got = arrived[way] = partner(sent, 1 << bits[0])
-            second = partner((kept[2:] + got[2:]).astype(BF16), 1 << bits[1])
-            third = (kept[1] + got[1] + second[1]).astype(BF16)
-            got_last.append(relay(third, 1 << bits[2]))
-            sums.append((kept, got, second))
-
-    for bit in range(low_bits):
+
+    def spread_hidden(hidden, bit):
         got = partner(hidden, 1 << bit)
         upper = (position >> bit) & 1 == 1
-        hidden = jnp.where(
+        return jnp.where(
             upper, jnp.concatenate([got, hidden], 1), jnp.concatenate([hidden, got], 1)
         )
+
+    def second_part(kept, got):
+        return (kept[2:] + got[2:]).astype(BF16)
+
+    got0 = send_rows(grad_tile, 0)
+    hidden = spread_hidden(hidden, 0)
+    sent_x, sent_y = produce([grad_tile], own_pieces, True, False)
+    first_x, first_y = partner(sent_x, 1), partner(sent_y, 2)
+    own_kept = produce([after(grad_tile, sent_x, sent_y)], own_pieces, False, True)
+    kept_x, kept_y, part = own_kept
+    parts = [part]
+    chunks = [([grad_tile], own_pieces), (got0, pieces_of(0))]
+    rows0 = after(got0[0], part), *got0[1:]
+    c_sent_x, c_sent_y, c_kept_x, c_kept_y, part = produce(list(rows0), pieces_of(0), True, True)
+    parts.append(part)
+    got1 = send_rows(after(grad_tile, *got0), 1)
+
+    c_sent_x, c_sent_y = after(c_sent_x, first_x, first_y), after(c_sent_y, first_x, first_y)
+    c_first_x, c_first_y = partner(c_sent_x, 1), partner(c_sent_y, 2)
+    second_x = partner(second_part(kept_x, first_x), 2)
+    second_y = partner(second_part(kept_y, first_y), 1)
+    hidden = spread_hidden(after(hidden, first_x, first_y), 1)
+    own_sums = (kept_x, first_x, second_x), (kept_y, first_y, second_y)
+
+    chunks.append((got1, pieces_of(1)))
+    order = [piece for _, pieces in chunks for _, _, piece, _ in pieces]
+    rows1 = after(got1[0], part), *got1[1:]
+    d_sent_x, d_sent_y, d_kept_x, d_kept_y, part = produce(list(rows1), pieces_of(1), True, True)
+    parts.append(part)
+    slot = c_first_x, c_first_y, second_x, second_y
+    own_rank = jnp.concatenate(parts, 1)
+    own_rank = after(own_rank, *slot)
+    own_rank = own_rank + partner(own_rank, 1)
+    d_first_x = partner(after(d_sent_x, *slot), 1)
+    d_first_y = partner(after(d_sent_y, *slot), 2)
+    c_second_x = partner(second_part(c_kept_x, c_first_x), 2)
+    c_second_y = partner(second_part(c_kept_y, c_first_y), 1)
+    c_sums = (c_kept_x, c_first_x, c_second_x), (c_kept_y, c_first_y, c_second_y)
+
+    def third_part(sums):
+        return [(kept[1] + got[1] + second[1]).astype(BF16) for kept, got, second in sums]
+
+    own_last = [relay(third, 4) for third in third_part(own_sums)]
+    hidden = spread_hidden(after(hidden, *slot), 2)
+    own_rank = own_rank + partner(own_rank, 4)
     hiddens = []
     for k in range(high_size):
         wanted = lax.dynamic_slice_in_dim(hidden, (high ^ k) * rank_part, rank_part, 2)
         hiddens.append(partner(wanted, k * low_size) if k > 0 else wanted)
+
+    slot = d_first_x, d_first_y, *own_last
+    own_rank = after(own_rank, *slot)
+    own_rank = (own_rank + partner(own_rank, 2)).astype(BF16)
+    d_second_x = partner(second_part(d_kept_x, after(d_first_x, *slot)), 2)
+    d_second_y = partner(second_part(d_kept_y, after(d_first_y, *slot)), 1)
+    d_sums = (d_kept_x, d_first_x, d_second_x), (d_kept_y, d_first_y, d_second_y)
+    c_last = [relay(third, 4) for third in third_part(c_sums)]
+    ranks = [own_rank] + [partner(own_rank, j * low_size) for j in range(1, high_size)]
+
+    slot = d_second_x, d_second_y, *c_last
+    d_last = [relay(third, 4) for third in third_part(d_sums)]
+    sums = own_sums + c_sums + d_sums
+    got_last = own_last + c_last + d_last
 
     all_grads, all_pieces = [], []
     for grads, pieces in chunks:
@@ -248,12 +293,6 @@
             transcendentals=0,
         ),
     )(*scalars, *all_grads, *hiddens)
-
-    own_rank = jnp.concatenate(parts, 1)
-    for bit in range(low_bits):
-        own_rank = own_rank + partner(own_rank, 1 << bit)
-    own_rank = own_rank.astype(BF16)
-    ranks = [own_rank] + [partner(own_rank, j * low_size) for j in range(1, high_size)]
 
     def columns_of(j, piece):
         k, m, offset = piece

time: 151 us -> 143 us (0.947)
  waiting for transfers between devices: 68.3 us -> 50.3 us
  local copies, waits for them, and re-layouts: 10.5 us -> 19.1 us
    unnamed x46 -> x54, local copies, waits for them, and re-layouts: 7.02 us -> 17.5 us
    ppermute x7, waiting for transfers between devices: 12.5 us -> 2.74 us  [relay(): return lax.ppermute(value, ('pipe', 'tensor'), pairs)]
    ppermute x22, waiting for transfers between devices: 55.8 us -> 47.6 us  [partner(): return lax.ppermute(value, 'tensor', pairs)]
    squeeze x2, local copies, waits for them, and re-layouts: 2.7 us -> 0.86 us  [send_rows(): return [partner(source[m], k * low_size)[None] for k in range(1, high_size)]]
    pallas_call x3 -> x4, Pallas kernels: 22.4 us -> 21.6 us  [product(): pl.pallas_call(functools.partial(product_body, low_size, tile_rows, piece...]
  transfers between devices with their start and end apart: 29 -> 29, of which waited for: 12 -> 9; matrix products, arithmetic and copies ran while one was open for 4% -> 5% of each run, Pallas kernels for 20% -> 18%
where the time goes in v5:
time: 143 us
  waiting for transfers between devices  50.3 us (35%)
  Pallas kernels  34.5 us (24%)
  starting transfers between devices  32.5 us (23%)
  local copies, waits for them, and re-layouts  19.1 us (13%)
  other arithmetic  5.06 us (4%)
    ppermute x22, waiting for transfers between devices, partner(): return lax.ppermute(value, 'tensor', pairs)  47.6 us
    ppermute x22, starting transfers between devices, partner(): return lax.ppermute(value, 'tensor', pairs)  27.9 us
    pallas_call x4, Pallas kernels, product(): pl.pallas_call(functools.partial(product_body, low_size, tile_rows, piece...  21.6 us
    unnamed x54, local copies, waits for them, and re-layouts  17.5 us
    ppermute x7, starting transfers between devices, relay(): return lax.ppermute(value, ('pipe', 'tensor'), pairs)  4.59 us
    pallas_call x1, Pallas kernels, shards(): pl.pallas_call(functools.partial(up_body, low_size, tile_rows, all_pieces...  3.66 us
    pallas_call x1, Pallas kernels, shards(): pl.pallas_call(down_kernel, in_specs=[SMEM] * 3 + [VMEM] * (1 + high_size...  3.14 us
    pallas_call x1, Pallas kernels, shards(): pl.pallas_call(finish_kernel, in_specs=[SMEM] + [VMEM] * (1 + len(got_las...  3.07 us
  transfers between devices with their start and end apart: 29, of which 9 were waited for; matrix products, arithmetic and copies ran while one was open for 5% of the time, Pallas kernels for 18%

profile of v5, /device:TPU:0, one launch (start us, length us, event | category | flops | bytes accessed | tf_op | source)
XLA Modules:
  0.0 142.6 jit_solution(5393713406364743426)
XLA Ops:
  0.6 3.4 %copy-done = bf16[1,1,4096,1024]{3,2,1,0:T(8,128)(2,1)S(1)} copy-done((bf16[1,1,4096,1024]{3,2,1,0:T(8,128)(2,1)S(1)}, bf16[1,1,4096,1024]{3,2,1,0:T(8,128)(2,1)}, u32[]{:S(2)}) %copy-start) | copy-done | bytes 8388632
  4.0 1.2 copy-done.3
  5.2 0.7 copy-done.14
  5.9 0.7 copy-done.16
  6.6 5.8 %shard_map.103 = (bf16[4,512,256]{2,1,0:T(8,128)(2,1)}, bf16[4,512,256]{2,1,0:T(8,128)(2,1)}) custom-call(s32[1]{0:T(128)} %bitcast.refs_0_.pos_ref, s32[2,4]{1,0:T(2,128)S(1)} %bitcast.49, s32[2]{0:T(128)S(1)} %bitcast.56, bf16[2,256,1024]{2,1,0:T(8,128)(2,1)S(1)} %bitcast.38, bf16[8,512,1024]{2,1,0:T(8,128)(2,1)S(1)} %bitcast.33), custom_call_target="tpu_custom_call" | custom-call | flops 2147483648 | bytes 7340032 | tf_op jit(solution)/shard_map/pallas_call | solution.py:117
  12.4 3.0 %collective-permute-start.2 = (bf16[4,512,256]{2,1,0:T(8,128)(2,1)}, bf16[4,512,256]{2,1,0:T(8,128)(2,1)}, u32[]{:S(2)}, u32[]{:S(2)}) collective-permute-start(bf16[4,512,256]{2,1,0:T(8,128)(2,1)} %get-tuple-element.38), channel_id=1, source_target_pairs={{0,1},{1,0},{2,3},{3,2},{4,5},{5,4},{6,7},{7,6},{8,9},{9,8},{10,11... | collective-permute-start | bytes 3145736 | tf_op jit(solution)/shard_map/ppermute | solution.py:20
  15.4 1.5 %collective-permute-start.3 = (bf16[4,512,256]{2,1,0:T(8,128)(2,1)}, bf16[4,512,256]{2,1,0:T(8,128)(2,1)}, u32[]{:S(2)}, u32[]{:S(2)}) collective-permute-start(bf16[4,512,256]{2,1,0:T(8,128)(2,1)} %get-tuple-element.39), channel_id=1, source_target_pairs={{0,2},{1,3},{2,0},{3,1},{4,6},{5,7},{6,4},{7,5},{8,10},{9,11},{10,... | collective-permute-start | bytes 3145736 | tf_op jit(solution)/shard_map/ppermute | solution.py:20
  16.9 0.8 slice_bitcast_fusion.1
  17.7 2.4 %collective-permute-start = (bf16[256,1024]{1,0:T(8,128)(2,1)}, bf16[256,1024]{1,0:T(8,128)(2,1)}, u32[]{:S(2)}, u32[]{:S(2)}) collective-permute-start(bf16[256,1024]{1,0:T(8,128)(2,1)} %slice_bitcast_fusion.1), channel_id=1, source_target_pairs={{0,8},{1,9},{2,10},{3,11},{4,12},{5,13},{6,14},{7,15},{8,0},{9,1},... | collective-permute-start | bytes 1572872 | tf_op jit(solution)/shard_map/ppermute | solution.py:20
  20.1 0.5 collective-permute-start.25
  20.7 5.2 %shard_map.104 = (f32[4,512,256]{2,1,0:T(8,128)S(1)}, f32[4,512,256]{2,1,0:T(8,128)S(1)}, f32[32,512]{1,0:T(8,128)S(1)}) custom-call(s32[1]{0:T(128)} %bitcast.refs_0_.pos_ref, s32[2,4]{1,0:T(2,128)S(1)} %bitcast.50, s32[2]{0:T(128)S(1)} %bitcast.57, bf16[2,256,1024]{2,1,0:T(8,128)(2,1)S(1)} %bitcast.39, bf16[8,512,1024]{2,1,0:T(8,128)(2,1)S(1)} %bitcast.34, ...), custom_call_target="tpu_custom_call" | custom-call | flops 2147483648 | bytes 7340032 | tf_op jit(solution)/shard_map/pallas_call | solution.py:117
  25.9 1.3 copy-done.5
  27.3 11.7 %collective-permute-done.25 = bf16[2,32,64]{2,1,0:T(8,128)(2,1)S(1)} collective-permute-done((bf16[2,32,64]{2,1,0:T(8,128)(2,1)S(1)}, bf16[2,32,64]{2,1,0:T(8,128)(2,1)S(1)}, u32[]{:S(2)}, u32[]{:S(2)}) %collective-permute-start.25) | collective-permute-done | bytes 8224 | tf_op jit(solution)/shard_map/ppermute | solution.py:20
  38.9 4.2 %collective-permute-done = bf16[256,1024]{1,0:T(8,128)(2,1)} collective-permute-done((bf16[256,1024]{1,0:T(8,128)(2,1)}, bf16[256,1024]{1,0:T(8,128)(2,1)}, u32[]{:S(2)}, u32[]{:S(2)}) %collective-permute-start) | collective-permute-done | bytes 524320 | tf_op jit(solution)/shard_map/ppermute | solution.py:20
  43.1 0.1 collective-permute-start.1
  43.2 3.4 %copy-done.1 = bf16[1,1,4096,1024]{3,2,1,0:T(8,128)(2,1)S(1)} copy-done((bf16[1,1,4096,1024]{3,2,1,0:T(8,128)(2,1)S(1)}, bf16[1,1,4096,1024]{3,2,1,0:T(8,128)(2,1)}, u32[]{:S(2)}) %copy-start.1) | copy-done | bytes 8388632
  46.6 1.0 copy-done.8
  47.7 5.5 %shard_map.105 = (bf16[4,512,128]{2,1,0:T(8,128)(2,1)S(1)}, bf16[4,512,128]{2,1,0:T(8,128)(2,1)S(1)}, f32[4,512,128]{2,1,0:T(8,128)S(1)}, f32[4,512,128]{2,1,0:T(8,128)S(1)}, f32[32,256]{1,0:T(8,128)S(1)}) custom-call(s32[1]{0:T(128)} %bitcast.refs_0_.pos_ref, s32[2,4]{1,0:T(2,128)S(1)} %bitcast.51, s32[2]{0:T(128)S(1)} %bitcast.58, ...), custom_call_target="tpu_custom_call" | custom-call | flops 2147483648 | bytes 11534336 | tf_op jit(solution)/shard_map/pallas_call | solution.py:117
  53.1 0.6 collective-permute-start.26
  53.7 1.3 add_convert_fusion
  55.0 1.1 collective-permute-start.7
  56.0 1.2 add_convert_fusion.1
  57.2 1.1 collective-permute-start.6
  58.3 9.8 %collective-permute-done.1 = bf16[256,1024]{1,0:T(8,128)(2,1)S(1)} collective-permute-done((bf16[256,1024]{1,0:T(8,128)(2,1)S(1)}, bf16[256,1024]{1,0:T(8,128)(2,1)S(1)}, u32[]{:S(2)}, u32[]{:S(2)}) %collective-permute-start.1) | collective-permute-done | bytes 524320 | tf_op jit(solution)/shard_map/ppermute | solution.py:20
  68.1 0.5 collective-permute-start.5
  68.6 0.2 collective-permute-start.4
  68.8 3.4 %copy-done.2 = bf16[1,1,4096,1024]{3,2,1,0:T(8,128)(2,1)S(1)} copy-done((bf16[1,1,4096,1024]{3,2,1,0:T(8,128)(2,1)S(1)}, bf16[1,1,4096,1024]{3,2,1,0:T(8,128)(2,1)}, u32[]{:S(2)}) %copy-start.2) | copy-done | bytes 8388632
  72.2 5.2 %shard_map.106 = (bf16[4,512,128]{2,1,0:T(8,128)(2,1)S(1)}, bf16[4,512,128]{2,1,0:T(8,128)(2,1)S(1)}, f32[4,512,128]{2,1,0:T(8,128)S(1)}, f32[4,512,128]{2,1,0:T(8,128)S(1)}, f32[32,256]{1,0:T(8,128)S(1)}) custom-call(s32[1]{0:T(128)} %bitcast.refs_0_.pos_ref, s32[2,4]{1,0:T(2,128)S(1)} %bitcast.52, s32[2]{0:T(128)S(1)} %bitcast.59, ...), custom_call_target="tpu_custom_call" | custom-call | flops 2147483648 | bytes 11534336 | tf_op jit(solution)/shard_map/pallas_call | solution.py:117
  77.5 1.0 fusion.1
  78.5 0.1 collective-permute-start.13
  78.6 1.8 %collective-permute-done.5.refs_12_ = bf16[4,512,128]{2,1,0:T(8,128)(2,1)S(1)} collective-permute-done((bf16[4,512,128]{2,1,0:T(8,128)(2,1)S(1)}, bf16[4,512,128]{2,1,0:T(8,128)(2,1)S(1)}, u32[]{:S(2)}, u32[]{:S(2)}) %collective-permute-start.5) | collective-permute-done | bytes 524320 | tf_op jit(solution)/shard_map/ppermute | solution.py:20
  80.4 4.5 %collective-permute-start.27 = (bf16[2,128,64]{2,1,0:T(8,128)(2,1)S(1)}, bf16[2,128,64]{2,1,0:T(8,128)(2,1)S(1)}, u32[]{:S(2)}, u32[]{:S(2)}) collective-permute-start(bf16[2,128,64]{2,1,0:T(8,128)(2,1)S(1)} %maximum_select_fusion.1), channel_id=1, source_target_pairs={{0,4},{1,5},{2,6},{3,7},{4,0},{5,1},{6,2},{7,3},{8,12},{9,13},{10,... | collective-permute-start | bytes 98312 | tf_op jit(solution)/shard_map/ppermute | solution.py:20
  84.9 1.5 %collective-permute-start.8 = (f32[32,1024]{1,0:T(8,128)S(1)}, f32[32,1024]{1,0:T(8,128)S(1)}, u32[]{:S(2)}, u32[]{:S(2)}) collective-permute-start(f32[32,1024]{1,0:T(8,128)S(1)} %pad_maximum_fusion), channel_id=1, source_target_pairs={{0,1},{1,0},{2,3},{3,2},{4,5},{5,4},{6,7},{7,6},{8,9},{9,8},{10,11... | collective-permute-start | bytes 393224 | tf_op jit(solution)/shard_map/ppermute | solution.py:20
  86.4 1.5 %collective-permute-start.11 = (bf16[4,512,128]{2,1,0:T(8,128)(2,1)S(1)}, bf16[4,512,128]{2,1,0:T(8,128)(2,1)S(1)}, u32[]{:S(2)}, u32[]{:S(2)}) collective-permute-start(bf16[4,512,128]{2,1,0:T(8,128)(2,1)S(1)} %get-tuple-element.57), channel_id=1, source_target_pairs={{0,2},{1,3},{2,0},{3,1},{4,6},{5,7},{6,4},{7,5},{8,10},{9,11},{10,... | collective-permute-start | bytes 1572872 | tf_op jit(solution)/shard_map/ppermute | solution.py:20
  87.9 0.5 collective-permute-start.10
  88.5 1.0 fusion
  89.6 1.6 %collective-permute-done.8 = f32[32,1024]{1,0:T(8,128)S(1)} collective-permute-done((f32[32,1024]{1,0:T(8,128)S(1)}, f32[32,1024]{1,0:T(8,128)S(1)}, u32[]{:S(2)}, u32[]{:S(2)}) %collective-permute-start.8) | collective-permute-done | bytes 131104 | tf_op jit(solution)/shard_map/ppermute | solution.py:20
  91.2 0.1 collective-permute-start.9
  91.4 0.1 add_convert_fusion.5
  91.5 8.7 %collective-permute-done.9 = f32[32,1024]{1,0:T(8,128)S(1)} collective-permute-done((f32[32,1024]{1,0:T(8,128)S(1)}, f32[32,1024]{1,0:T(8,128)S(1)}, u32[]{:S(2)}, u32[]{:S(2)}) %collective-permute-start.9) | collective-permute-done | bytes 131104 | tf_op jit(solution)/shard_map/ppermute | solution.py:20
  100.2 1.5 %collective-permute-start.17 = (bf16[2,512,128]{2,1,0:T(8,128)(2,1)S(1)}, bf16[2,512,128]{2,1,0:T(8,128)(2,1)S(1)}, u32[]{:S(2)}, u32[]{:S(2)}) collective-permute-start(bf16[2,512,128]{2,1,0:T(8,128)(2,1)S(1)} %add_convert_fusion.4), channel_id=1, source_target_pairs={{0,1},{1,0},{2,3},{3,2},{4,5},{5,4},{6,7},{7,6},{8,9},{9,8},{10,11... | collective-permute-start | bytes 786440 | tf_op jit(solution)/shard_map/ppermute | solution.py:20
  101.8 1.6 %collective-permute-start.16 = (bf16[2,512,128]{2,1,0:T(8,128)(2,1)S(1)}, bf16[2,512,128]{2,1,0:T(8,128)(2,1)S(1)}, u32[]{:S(2)}, u32[]{:S(2)}) collective-permute-start(bf16[2,512,128]{2,1,0:T(8,128)(2,1)S(1)} %add_convert_fusion.5), channel_id=1, source_target_pairs={{0,2},{1,3},{2,0},{3,1},{4,6},{5,7},{6,4},{7,5},{8,10},{9,11},{10,... | collective-permute-start | bytes 786440 | tf_op jit(solution)/shard_map/ppermute | solution.py:20
  103.4 0.5 collective-permute-start.14
  104.0 0.1 copy-done.20
  104.2 0.6 collective-permute-start.19
  104.8 1.5 %collective-permute-start.18 = (bf16[2,512,128]{2,1,0:T(8,128)(2,1)S(1)}, bf16[2,512,128]{2,1,0:T(8,128)(2,1)S(1)}, u32[]{:S(2)}, u32[]{:S(2)}) collective-permute-start(bf16[2,512,128]{2,1,0:T(8,128)(2,1)S(1)} %add_convert_fusion.3), channel_id=1, source_target_pairs={{0,2},{1,3},{2,0},{3,1},{4,6},{5,7},{6,4},{7,5},{8,10},{9,11},{10,... | collective-permute-start | bytes 786440 | tf_op jit(solution)/shard_map/ppermute | solution.py:20
  106.3 7.5 %collective-permute-done.14 = f32[32,1024]{1,0:T(8,128)S(1)} collective-permute-done((f32[32,1024]{1,0:T(8,128)S(1)}, f32[32,1024]{1,0:T(8,128)S(1)}, u32[]{:S(2)}, u32[]{:S(2)}) %collective-permute-start.14) | collective-permute-done | bytes 131104 | tf_op jit(solution)/shard_map/ppermute | solution.py:20
  113.8 0.6 collective-permute-start.15
  114.3 0.8 constant_dynamic-slice_fusion
  115.1 2.4 %collective-permute-start.28 = (bf16[2,256,32]{2,1,0:T(8,128)(2,1)S(1)}, bf16[2,256,32]{2,1,0:T(8,128)(2,1)S(1)}, u32[]{:S(2)}, u32[]{:S(2)}) collective-permute-start(bf16[2,256,32]{2,1,0:T(8,128)(2,1)S(1)} %get-tuple-element.67), channel_id=1, source_target_pairs={{0,8},{1,9},{2,10},{3,11},{4,12},{5,13},{6,14},{7,15},{8,0},{9,1},... | collective-permute-start | bytes 98312 | tf_op jit(solution)/shard_map/ppermute | solution.py:20
  117.6 2.4 %collective-permute-done.15.refs_1_ = bf16[32,1024]{1,0:T(8,128)(2,1)S(1)} collective-permute-done((bf16[32,1024]{1,0:T(8,128)(2,1)S(1)}, bf16[32,1024]{1,0:T(8,128)(2,1)S(1)}, u32[]{:S(2)}, u32[]{:S(2)}) %collective-permute-start.15) | collective-permute-done | bytes 65568 | tf_op jit(solution)/shard_map/ppermute | solution.py:20
  119.9 3.0 %shard_map.107 = bf16[512,1024]{1,0:T(8,128)(2,1)} custom-call(s32[1]{0:T(128)} %bitcast.refs_0_.pos_ref, s32[2,4]{1,0:T(2,128)S(1)} %bitcast.53, s32[2]{0:T(128)S(1)} %bitcast.60, bf16[8,2,32,512]{3,2,1,0:T(8,128)(2,1)S(1)} %bitcast.46, bf16[32,1024]{1,0:T(8,128)(2,1)S(1)} %add_convert_fusion.12.refs_0_, ...), custom_call_target="tpu_custom_call" | custom-call | flops 67108864 | bytes 5242880 | tf_op jit(solution)/shard_map/pallas_call | solution.py:330
  123.0 0.1 collective-permute-start.20
  123.1 2.5 %collective-permute-start.22 = (bf16[512,128]{1,0:T(8,128)(2,1)S(1)}, bf16[512,128]{1,0:T(8,128)(2,1)S(1)}, u32[]{:S(2)}, u32[]{:S(2)}) collective-permute-start(bf16[512,128]{1,0:T(8,128)(2,1)S(1)} %fusion.3), channel_id=1, source_target_pairs={{0,20},{1,21},{2,22},{3,23},{4,16},{5,17},{6,18},{7,19},{8,28},{9,... | collective-permute-start | bytes 393224 | tf_op jit(solution)/shard_map/ppermute | solution.py:30
  125.6 0.1 collective-permute-start.21
  125.8 1.8 %collective-permute-start.24 = (bf16[512,128]{1,0:T(8,128)(2,1)S(1)}, bf16[512,128]{1,0:T(8,128)(2,1)S(1)}, u32[]{:S(2)}, u32[]{:S(2)}) collective-permute-start(bf16[512,128]{1,0:T(8,128)(2,1)S(1)} %fusion.5), channel_id=1, source_target_pairs={{0,20},{1,21},{2,22},{3,23},{4,16},{5,17},{6,18},{7,19},{8,28},{9,... | collective-permute-start | bytes 393224 | tf_op jit(solution)/shard_map/ppermute | solution.py:30
  127.6 0.1 collective-permute-start.23
  127.7 0.6 copy-done.21
  128.3 3.7 %shard_map.110 = bf16[8,32,1024]{2,1,0:T(8,128)(2,1)} custom-call(s32[1]{0:T(128)} %bitcast.refs_0_.pos_ref, s32[2,4]{1,0:T(2,128)} %bitcast.47, s32[2]{0:T(128)} %bitcast.54, bf16[2,256,1024]{2,1,0:T(8,128)(2,1)} %bitcast.37, bf16[1,256,1024]{2,1,0:T(8,128)(2,1)} %bitcast.8.refs_3_.refs_4_, bf16[1,256,1024]{2,1,0:T(8,128)(2,1)} %bitcast.45, ...), custom_call_target="tpu_custom_call" | custom-call | flops 67108864 | bytes 2097152 | tf_op jit(solution)/shard_map/pallas_call | solution.py:284
  131.9 3.1 %shard_map.109 = bf16[8,2,32,512]{3,2,1,0:T(8,128)(2,1)} custom-call(s32[1]{0:T(128)} %bitcast.refs_0_.pos_ref, s32[2,4]{1,0:T(2,128)} %bitcast.48, s32[2]{0:T(128)} %bitcast.55, bf16[2,512,512]{2,1,0:T(8,128)(2,1)} %bitcast.61, bf16[32,1024]{1,0:T(8,128)(2,1)} %copy-done.11, bf16[32,1024]{1,0:T(8,128)(2,1)} %copy-done.13), custom_call_target="tpu_custom_call" | custom-call | flops 67108864 | bytes 1048576 | tf_op jit(solution)/shard_map/pallas_call | solution.py:389
  135.1 2.7 %collective-permute-done.23.refs_4_ = bf16[512,128]{1,0:T(8,128)(2,1)S(1)} collective-permute-done((bf16[512,128]{1,0:T(8,128)(2,1)S(1)}, bf16[512,128]{1,0:T(8,128)(2,1)S(1)}, u32[]{:S(2)}, u32[]{:S(2)}) %collective-permute-start.23) | collective-permute-done | bytes 131104 | tf_op jit(solution)/shard_map/ppermute | solution.py:30
  137.9 0.6 copy-done.25
  138.5 1.0 copy-done.18
  139.5 3.1 %shard_map.108 = bf16[2,512,512]{2,1,0:T(8,128)(2,1)} custom-call(s32[1]{0:T(128)} %bitcast.refs_0_.pos_ref, bf16[512,1024]{1,0:T(8,128)(2,1)} %copy-done.18, bf16[512,256]{1,0:T(8,128)(2,1)} %copy-done.20, bf16[512,256]{1,0:T(8,128)(2,1)} %copy-done.19, bf16[512,128]{1,0:T(8,128)(2,1)} %copy-done.23, bf16[512,128]{1,0:T(8,128)(2,1)} %copy-done.22, ...), custom_call_target="tpu_custom_call" | custom-call | tf_op jit(solution)/shard_map/pallas_call | solution.py:362
  (78 shorter events, 0.7 us)
Async XLA Ops:
  0.6 3.4 %copy-start = (bf16[1,1,4096,1024]{3,2,1,0:T(8,128)(2,1)S(1)}, bf16[1,1,4096,1024]{3,2,1,0:T(8,128)(2,1)}, u32[]{:S(2)}) copy-start(bf16[1,1,4096,1024]{3,2,1,0:T(8,128)(2,1)} %param.11) | copy-start | bytes 25165828
  4.0 1.2 copy-start.3
  5.2 0.7 copy-start.14
  5.9 0.7 copy-start.16
  6.6 13.6 %copy-start.26 = (bf16[1,2,32,64]{3,2,1,0:T(8,128)(2,1)S(1)}, bf16[1,2,32,64]{3,2,1,0:T(8,128)(2,1)}, u32[]{:S(2)}) copy-start(bf16[1,2,32,64]{3,2,1,0:T(8,128)(2,1)} %param.10) | copy-start | bytes 24580
  6.6 14.1 %copy-start.4 = (bf16[1,1,2,256,1024]{4,3,2,1,0:T(8,128)(2,1)S(1)}, bf16[1,1,2,256,1024]{4,3,2,1,0:T(8,128)(2,1)}, u32[]{:S(2)}) copy-start(bf16[1,1,2,256,1024]{4,3,2,1,0:T(8,128)(2,1)} %param.8) | copy-start | bytes 3145732
  6.6 14.1 %copy-start.7 = (bf16[1,1,8,32,1024]{4,3,2,1,0:T(8,128)(2,1)S(1)}, bf16[1,1,8,32,1024]{4,3,2,1,0:T(8,128)(2,1)}, u32[]{:S(2)}) copy-start(bf16[1,1,8,32,1024]{4,3,2,1,0:T(8,128)(2,1)} %param.13) | copy-start | bytes 1572868
  12.4 40.8 %collective-permute-start.2 = (bf16[4,512,256]{2,1,0:T(8,128)(2,1)}, bf16[4,512,256]{2,1,0:T(8,128)(2,1)}, u32[]{:S(2)}, u32[]{:S(2)}) collective-permute-start(bf16[4,512,256]{2,1,0:T(8,128)(2,1)} %get-tuple-element.38), channel_id=1, source_target_pairs={{0,1},{1,0},{2,3},{3,2},{4,5},{5,4},{6,7},{7,6},{8,9},{9,8},{10,11... | collective-permute-start | bytes 3145736 | tf_op jit(solution)/shard_map/ppermute | solution.py:20
  15.4 37.8 %collective-permute-start.3 = (bf16[4,512,256]{2,1,0:T(8,128)(2,1)}, bf16[4,512,256]{2,1,0:T(8,128)(2,1)}, u32[]{:S(2)}, u32[]{:S(2)}) collective-permute-start(bf16[4,512,256]{2,1,0:T(8,128)(2,1)} %get-tuple-element.39), channel_id=1, source_target_pairs={{0,2},{1,3},{2,0},{3,1},{4,6},{5,7},{6,4},{7,5},{8,10},{9,11},{10,... | collective-permute-start | bytes 3145736 | tf_op jit(solution)/shard_map/ppermute | solution.py:20
  17.7 25.4 %collective-permute-start = (bf16[256,1024]{1,0:T(8,128)(2,1)}, bf16[256,1024]{1,0:T(8,128)(2,1)}, u32[]{:S(2)}, u32[]{:S(2)}) collective-permute-start(bf16[256,1024]{1,0:T(8,128)(2,1)} %slice_bitcast_fusion.1), channel_id=1, source_target_pairs={{0,8},{1,9},{2,10},{3,11},{4,12},{5,13},{6,14},{7,15},{8,0},{9,1},... | collective-permute-start | bytes 1572872 | tf_op jit(solution)/shard_map/ppermute | solution.py:20
  20.1 18.8 %collective-permute-start.25 = (bf16[2,32,64]{2,1,0:T(8,128)(2,1)S(1)}, bf16[2,32,64]{2,1,0:T(8,128)(2,1)S(1)}, u32[]{:S(2)}, u32[]{:S(2)}) collective-permute-start(bf16[2,32,64]{2,1,0:T(8,128)(2,1)S(1)} %bitcast.65), channel_id=1, source_target_pairs={{0,1},{1,0},{2,3},{3,2},{4,5},{5,4},{6,7},{7,6},{8,9},{9,8},{10,11... | collective-permute-start | bytes 24584 | tf_op jit(solution)/shard_map/ppermute | solution.py:20
  20.7 22.5 %copy-start.15 = (s32[1,2,4]{2,1,0:T(2,128)S(1)}, s32[1,2,4]{2,1,0:T(2,128)}, u32[]{:S(2)}) copy-start(s32[1,2,4]{2,1,0:T(2,128)} %param.14) | copy-start | bytes 100
  20.7 22.6 %copy-start.17 = (s32[1,2]{1,0:T(1,128)S(1)}, s32[1,2]{1,0:T(1,128)}, u32[]{:S(2)}) copy-start(s32[1,2]{1,0:T(1,128)} %param.15) | copy-start | bytes 28
  25.9 1.4 copy-start.5
  43.1 25.0 %collective-permute-start.1 = (bf16[256,1024]{1,0:T(8,128)(2,1)S(1)}, bf16[256,1024]{1,0:T(8,128)(2,1)S(1)}, u32[]{:S(2)}, u32[]{:S(2)}) collective-permute-start(bf16[256,1024]{1,0:T(8,128)(2,1)S(1)} %slice_bitcast_fusion), channel_id=1, source_target_pairs={{0,8},{1,9},{2,10},{3,11},{4,12},{5,13},{6,14},{7,15},{8,0},{9,1},... | collective-permute-start | bytes 1572872 | tf_op jit(solution)/shard_map/ppermute | solution.py:20
  43.2 3.4 %copy-start.1 = (bf16[1,1,4096,1024]{3,2,1,0:T(8,128)(2,1)S(1)}, bf16[1,1,4096,1024]{3,2,1,0:T(8,128)(2,1)}, u32[]{:S(2)}) copy-start(bf16[1,1,4096,1024]{3,2,1,0:T(8,128)(2,1)} %param.11) | copy-start | bytes 25165828
  46.6 1.0 copy-start.8
  47.7 6.1 %copy-start.6 = (f32[4,512,256]{2,1,0:T(8,128)S(1)}, f32[4,512,256]{2,1,0:T(8,128)}, u32[]{:S(2)}) copy-start(f32[4,512,256]{2,1,0:T(8,128)} %copy-done.5) | copy-start | bytes 6291460
  53.1 24.3 %collective-permute-start.26 = (bf16[2,64,64]{2,1,0:T(8,128)(2,1)S(1)}, bf16[2,64,64]{2,1,0:T(8,128)(2,1)S(1)}, u32[]{:S(2)}, u32[]{:S(2)}) collective-permute-start(bf16[2,64,64]{2,1,0:T(8,128)(2,1)S(1)} %maximum_select_fusion.2), channel_id=1, source_target_pairs={{0,2},{1,3},{2,0},{3,1},{4,6},{5,7},{6,4},{7,5},{8,10},{9,11},{10,... | collective-permute-start | bytes 49160 | tf_op jit(solution)/shard_map/ppermute | solution.py:20
  53.7 15.1 %copy-start.9 = (bf16[1,1,8,32,1024]{4,3,2,1,0:T(8,128)(2,1)S(1)}, bf16[1,1,8,32,1024]{4,3,2,1,0:T(8,128)(2,1)}, u32[]{:S(2)}) copy-start(bf16[1,1,8,32,1024]{4,3,2,1,0:T(8,128)(2,1)} %param.13) | copy-start | bytes 1572868
  55.0 22.5 %collective-permute-start.7 = (bf16[2,512,256]{2,1,0:T(8,128)(2,1)S(1)}, bf16[2,512,256]{2,1,0:T(8,128)(2,1)S(1)}, u32[]{:S(2)}, u32[]{:S(2)}) collective-permute-start(bf16[2,512,256]{2,1,0:T(8,128)(2,1)S(1)} %add_convert_fusion), channel_id=1, source_target_pairs={{0,1},{1,0},{2,3},{3,2},{4,5},{5,4},{6,7},{7,6},{8,9},{9,8},{10,11... | collective-permute-start | bytes 1572872 | tf_op jit(solution)/shard_map/ppermute | solution.py:20
  57.2 21.4 %collective-permute-start.6 = (bf16[2,512,256]{2,1,0:T(8,128)(2,1)S(1)}, bf16[2,512,256]{2,1,0:T(8,128)(2,1)S(1)}, u32[]{:S(2)}, u32[]{:S(2)}) collective-permute-start(bf16[2,512,256]{2,1,0:T(8,128)(2,1)S(1)} %add_convert_fusion.1), channel_id=1, source_target_pairs={{0,2},{1,3},{2,0},{3,1},{4,6},{5,7},{6,4},{7,5},{8,10},{9,11},{10,... | collective-permute-start | bytes 1572872 | tf_op jit(solution)/shard_map/ppermute | solution.py:20
  68.1 9.3 %copy-start.10 = (bf16[256,1024]{1,0:T(8,128)(2,1)}, bf16[256,1024]{1,0:T(8,128)(2,1)S(1)}, u32[]{:S(2)}) copy-start(bf16[256,1024]{1,0:T(8,128)(2,1)S(1)} %collective-permute-done.1) | copy-start | bytes 1572868
  68.1 12.3 %collective-permute-start.5 = (bf16[4,512,128]{2,1,0:T(8,128)(2,1)S(1)}, bf16[4,512,128]{2,1,0:T(8,128)(2,1)S(1)}, u32[]{:S(2)}, u32[]{:S(2)}) collective-permute-start(bf16[4,512,128]{2,1,0:T(8,128)(2,1)S(1)} %get-tuple-element.50), channel_id=1, source_target_pairs={{0,2},{1,3},{2,0},{3,1},{4,6},{5,7},{6,4},{7,5},{8,10},{9,11},{10,... | collective-permute-start | bytes 1572872 | tf_op jit(solution)/shard_map/ppermute | solution.py:20
  68.6 11.8 %collective-permute-start.4 = (bf16[4,512,128]{2,1,0:T(8,128)(2,1)S(1)}, bf16[4,512,128]{2,1,0:T(8,128)(2,1)S(1)}, u32[]{:S(2)}, u32[]{:S(2)}) collective-permute-start(bf16[4,512,128]{2,1,0:T(8,128)(2,1)S(1)} %get-tuple-element.48), channel_id=1, source_target_pairs={{0,1},{1,0},{2,3},{3,2},{4,5},{5,4},{6,7},{7,6},{8,9},{9,8},{10,11... | collective-permute-start | bytes 1572872 | tf_op jit(solution)/shard_map/ppermute | solution.py:20
  68.8 3.4 %copy-start.2 = (bf16[1,1,4096,1024]{3,2,1,0:T(8,128)(2,1)S(1)}, bf16[1,1,4096,1024]{3,2,1,0:T(8,128)(2,1)}, u32[]{:S(2)}) copy-start(bf16[1,1,4096,1024]{3,2,1,0:T(8,128)(2,1)} %param.11) | copy-start | bytes 25165828
  78.5 23.3 %collective-permute-start.13 = (bf16[512,256]{1,0:T(8,128)(2,1)S(1)}, bf16[512,256]{1,0:T(8,128)(2,1)S(1)}, u32[]{:S(2)}, u32[]{:S(2)}) collective-permute-start(bf16[512,256]{1,0:T(8,128)(2,1)S(1)} %fusion.1), channel_id=1, source_target_pairs={{0,20},{1,21},{2,22},{3,23},{4,16},{5,17},{6,18},{7,19},{8,28},{9,... | collective-permute-start | bytes 786440 | tf_op jit(solution)/shard_map/ppermute | solution.py:30
  80.4 10.9 %collective-permute-start.27 = (bf16[2,128,64]{2,1,0:T(8,128)(2,1)S(1)}, bf16[2,128,64]{2,1,0:T(8,128)(2,1)S(1)}, u32[]{:S(2)}, u32[]{:S(2)}) collective-permute-start(bf16[2,128,64]{2,1,0:T(8,128)(2,1)S(1)} %maximum_select_fusion.1), channel_id=1, source_target_pairs={{0,4},{1,5},{2,6},{3,7},{4,0},{5,1},{6,2},{7,3},{8,12},{9,13},{10,... | collective-permute-start | bytes 98312 | tf_op jit(solution)/shard_map/ppermute | solution.py:20
  84.9 6.3 %collective-permute-start.8 = (f32[32,1024]{1,0:T(8,128)S(1)}, f32[32,1024]{1,0:T(8,128)S(1)}, u32[]{:S(2)}, u32[]{:S(2)}) collective-permute-start(f32[32,1024]{1,0:T(8,128)S(1)} %pad_maximum_fusion), channel_id=1, source_target_pairs={{0,1},{1,0},{2,3},{3,2},{4,5},{5,4},{6,7},{7,6},{8,9},{9,8},{10,11... | collective-permute-start | bytes 393224 | tf_op jit(solution)/shard_map/ppermute | solution.py:20
  86.4 17.0 %collective-permute-start.11 = (bf16[4,512,128]{2,1,0:T(8,128)(2,1)S(1)}, bf16[4,512,128]{2,1,0:T(8,128)(2,1)S(1)}, u32[]{:S(2)}, u32[]{:S(2)}) collective-permute-start(bf16[4,512,128]{2,1,0:T(8,128)(2,1)S(1)} %get-tuple-element.57), channel_id=1, source_target_pairs={{0,2},{1,3},{2,0},{3,1},{4,6},{5,7},{6,4},{7,5},{8,10},{9,11},{10,... | collective-permute-start | bytes 1572872 | tf_op jit(solution)/shard_map/ppermute | solution.py:20
  87.9 15.5 %collective-permute-start.10 = (bf16[4,512,128]{2,1,0:T(8,128)(2,1)S(1)}, bf16[4,512,128]{2,1,0:T(8,128)(2,1)S(1)}, u32[]{:S(2)}, u32[]{:S(2)}) collective-permute-start(bf16[4,512,128]{2,1,0:T(8,128)(2,1)S(1)} %get-tuple-element.55), channel_id=1, source_target_pairs={{0,1},{1,0},{2,3},{3,2},{4,5},{5,4},{6,7},{7,6},{8,9},{9,8},{10,11... | collective-permute-start | bytes 1572872 | tf_op jit(solution)/shard_map/ppermute | solution.py:20
  91.2 12.2 %collective-permute-start.12 = (bf16[512,256]{1,0:T(8,128)(2,1)S(1)}, bf16[512,256]{1,0:T(8,128)(2,1)S(1)}, u32[]{:S(2)}, u32[]{:S(2)}) collective-permute-start(bf16[512,256]{1,0:T(8,128)(2,1)S(1)} %fusion), channel_id=1, source_target_pairs={{0,20},{1,21},{2,22},{3,23},{4,16},{5,17},{6,18},{7,19},{8,28},{9,... | collective-permute-start | bytes 786440 | tf_op jit(solution)/shard_map/ppermute | solution.py:30
  91.2 9.0 %collective-permute-start.9 = (f32[32,1024]{1,0:T(8,128)S(1)}, f32[32,1024]{1,0:T(8,128)S(1)}, u32[]{:S(2)}, u32[]{:S(2)}) collective-permute-start(f32[32,1024]{1,0:T(8,128)S(1)} %add.84), channel_id=1, source_target_pairs={{0,4},{1,5},{2,6},{3,7},{4,0},{5,1},{6,2},{7,3},{8,12},{9,13},{10,... | collective-permute-start | bytes 393224 | tf_op jit(solution)/shard_map/ppermute | solution.py:20
  91.4 28.5 %copy-start.12 = (bf16[1,8,64,512]{3,2,1,0:T(8,128)(2,1)S(1)}, bf16[1,8,64,512]{3,2,1,0:T(8,128)(2,1)}, u32[]{:S(2)}) copy-start(bf16[1,8,64,512]{3,2,1,0:T(8,128)(2,1)} %param.12) | copy-start | bytes 1572868
  100.2 14.9 %collective-permute-start.17 = (bf16[2,512,128]{2,1,0:T(8,128)(2,1)S(1)}, bf16[2,512,128]{2,1,0:T(8,128)(2,1)S(1)}, u32[]{:S(2)}, u32[]{:S(2)}) collective-permute-start(bf16[2,512,128]{2,1,0:T(8,128)(2,1)S(1)} %add_convert_fusion.4), channel_id=1, source_target_pairs={{0,1},{1,0},{2,3},{3,2},{4,5},{5,4},{6,7},{7,6},{8,9},{9,8},{10,11... | collective-permute-start | bytes 786440 | tf_op jit(solution)/shard_map/ppermute | solution.py:20
  101.8 21.2 %copy-start.19 = (bf16[512,256]{1,0:T(8,128)(2,1)}, bf16[512,256]{1,0:T(8,128)(2,1)S(1)}, u32[]{:S(2)}) copy-start(bf16[512,256]{1,0:T(8,128)(2,1)S(1)} %collective-permute-done.13.refs_1_) | copy-start | bytes 786436
  101.8 15.8 %collective-permute-start.16 = (bf16[2,512,128]{2,1,0:T(8,128)(2,1)S(1)}, bf16[2,512,128]{2,1,0:T(8,128)(2,1)S(1)}, u32[]{:S(2)}, u32[]{:S(2)}) collective-permute-start(bf16[2,512,128]{2,1,0:T(8,128)(2,1)S(1)} %add_convert_fusion.5), channel_id=1, source_target_pairs={{0,2},{1,3},{2,0},{3,1},{4,6},{5,7},{6,4},{7,5},{8,10},{9,11},{10,... | collective-permute-start | bytes 786440 | tf_op jit(solution)/shard_map/ppermute | solution.py:20
  103.4 0.7 copy-start.20
  103.4 10.3 %collective-permute-start.14 = (f32[32,1024]{1,0:T(8,128)S(1)}, f32[32,1024]{1,0:T(8,128)S(1)}, u32[]{:S(2)}, u32[]{:S(2)}) collective-permute-start(f32[32,1024]{1,0:T(8,128)S(1)} %add.85), channel_id=1, source_target_pairs={{0,2},{1,3},{2,0},{3,1},{4,6},{5,7},{6,4},{7,5},{8,10},{9,11},{10,... | collective-permute-start | bytes 393224 | tf_op jit(solution)/shard_map/ppermute | solution.py:20
  104.2 15.8 %collective-permute-start.19 = (bf16[2,512,128]{2,1,0:T(8,128)(2,1)S(1)}, bf16[2,512,128]{2,1,0:T(8,128)(2,1)S(1)}, u32[]{:S(2)}, u32[]{:S(2)}) collective-permute-start(bf16[2,512,128]{2,1,0:T(8,128)(2,1)S(1)} %add_convert_fusion.2), channel_id=1, source_target_pairs={{0,1},{1,0},{2,3},{3,2},{4,5},{5,4},{6,7},{7,6},{8,9},{9,8},{10,11... | collective-permute-start | bytes 786440 | tf_op jit(solution)/shard_map/ppermute | solution.py:20
  104.8 15.1 %collective-permute-start.18 = (bf16[2,512,128]{2,1,0:T(8,128)(2,1)S(1)}, bf16[2,512,128]{2,1,0:T(8,128)(2,1)S(1)}, u32[]{:S(2)}, u32[]{:S(2)}) collective-permute-start(bf16[2,512,128]{2,1,0:T(8,128)(2,1)S(1)} %add_convert_fusion.3), channel_id=1, source_target_pairs={{0,2},{1,3},{2,0},{3,1},{4,6},{5,7},{6,4},{7,5},{8,10},{9,11},{10,... | collective-permute-start | bytes 786440 | tf_op jit(solution)/shard_map/ppermute | solution.py:20
  113.8 9.2 %copy-start.11 = (bf16[32,1024]{1,0:T(8,128)(2,1)}, bf16[32,1024]{1,0:T(8,128)(2,1)S(1)}, u32[]{:S(2)}) copy-start(bf16[32,1024]{1,0:T(8,128)(2,1)S(1)} %add_convert_fusion.12.refs_0_) | copy-start | bytes 196612
  113.8 6.1 %collective-permute-start.15 = (bf16[32,1024]{1,0:T(8,128)(2,1)S(1)}, bf16[32,1024]{1,0:T(8,128)(2,1)S(1)}, u32[]{:S(2)}, u32[]{:S(2)}) collective-permute-start(bf16[32,1024]{1,0:T(8,128)(2,1)S(1)} %add_convert_fusion.12.refs_0_), channel_id=1, source_target_pairs={{0,8},{1,9},{2,10},{3,11},{4,12},{5,13},{6,14},{7,15},{8,0},{9,1},... | collective-permute-start | bytes 196616 | tf_op jit(solution)/shard_map/ppermute | solution.py:20
  115.1 12.5 %collective-permute-start.28 = (bf16[2,256,32]{2,1,0:T(8,128)(2,1)S(1)}, bf16[2,256,32]{2,1,0:T(8,128)(2,1)S(1)}, u32[]{:S(2)}, u32[]{:S(2)}) collective-permute-start(bf16[2,256,32]{2,1,0:T(8,128)(2,1)S(1)} %get-tuple-element.67), channel_id=1, source_target_pairs={{0,8},{1,9},{2,10},{3,11},{4,12},{5,13},{6,14},{7,15},{8,0},{9,1},... | collective-permute-start | bytes 98312 | tf_op jit(solution)/shard_map/ppermute | solution.py:20
  119.9 3.0 %copy-start.13 = (bf16[32,1024]{1,0:T(8,128)(2,1)}, bf16[32,1024]{1,0:T(8,128)(2,1)S(1)}, u32[]{:S(2)}) copy-start(bf16[32,1024]{1,0:T(8,128)(2,1)S(1)} %collective-permute-done.15.refs_1_) | copy-start | bytes 196612
  123.0 14.9 %collective-permute-start.20 = (bf16[512,1024]{1,0:T(8,128)(2,1)}, bf16[512,1024]{1,0:T(8,128)(2,1)S(1)}, u32[]{:S(2)}, u32[]{:S(2)}) collective-permute-start(bf16[512,1024]{1,0:T(8,128)(2,1)} %shard_map.107), channel_id=1, source_target_pairs={{0,16},{1,17},{2,18},{3,19},{4,20},{5,21},{6,22},{7,23},{8,24},{9,... | collective-permute-start | bytes 3145736 | tf_op jit(solution)/shard_map/ppermute | solution.py:30
  123.1 12.0 %collective-permute-start.22 = (bf16[512,128]{1,0:T(8,128)(2,1)S(1)}, bf16[512,128]{1,0:T(8,128)(2,1)S(1)}, u32[]{:S(2)}, u32[]{:S(2)}) collective-permute-start(bf16[512,128]{1,0:T(8,128)(2,1)S(1)} %fusion.3), channel_id=1, source_target_pairs={{0,20},{1,21},{2,22},{3,23},{4,16},{5,17},{6,18},{7,19},{8,28},{9,... | collective-permute-start | bytes 393224 | tf_op jit(solution)/shard_map/ppermute | solution.py:30
  125.6 9.5 %collective-permute-start.21 = (bf16[512,128]{1,0:T(8,128)(2,1)S(1)}, bf16[512,128]{1,0:T(8,128)(2,1)S(1)}, u32[]{:S(2)}, u32[]{:S(2)}) collective-permute-start(bf16[512,128]{1,0:T(8,128)(2,1)S(1)} %fusion.2), channel_id=1, source_target_pairs={{0,20},{1,21},{2,22},{3,23},{4,16},{5,17},{6,18},{7,19},{8,28},{9,... | collective-permute-start | bytes 393224 | tf_op jit(solution)/shard_map/ppermute | solution.py:30
  125.8 9.4 %collective-permute-start.24 = (bf16[512,128]{1,0:T(8,128)(2,1)S(1)}, bf16[512,128]{1,0:T(8,128)(2,1)S(1)}, u32[]{:S(2)}, u32[]{:S(2)}) collective-permute-start(bf16[512,128]{1,0:T(8,128)(2,1)S(1)} %fusion.5), channel_id=1, source_target_pairs={{0,20},{1,21},{2,22},{3,23},{4,16},{5,17},{6,18},{7,19},{8,28},{9,... | collective-permute-start | bytes 393224 | tf_op jit(solution)/shard_map/ppermute | solution.py:30
  127.6 0.7 copy-start.21
  127.6 10.2 %collective-permute-start.23 = (bf16[512,128]{1,0:T(8,128)(2,1)S(1)}, bf16[512,128]{1,0:T(8,128)(2,1)S(1)}, u32[]{:S(2)}, u32[]{:S(2)}) collective-permute-start(bf16[512,128]{1,0:T(8,128)(2,1)S(1)} %fusion.4), channel_id=1, source_target_pairs={{0,20},{1,21},{2,22},{3,23},{4,16},{5,17},{6,18},{7,19},{8,28},{9,... | collective-permute-start | bytes 393224 | tf_op jit(solution)/shard_map/ppermute | solution.py:30
  135.1 2.8 %copy-start.22 = (bf16[512,128]{1,0:T(8,128)(2,1)}, bf16[512,128]{1,0:T(8,128)(2,1)S(1)}, u32[]{:S(2)}) copy-start(bf16[512,128]{1,0:T(8,128)(2,1)S(1)} %collective-permute-done.22.refs_3_) | copy-start | bytes 393220
  135.1 2.8 %copy-start.23 = (bf16[512,128]{1,0:T(8,128)(2,1)}, bf16[512,128]{1,0:T(8,128)(2,1)S(1)}, u32[]{:S(2)}) copy-start(bf16[512,128]{1,0:T(8,128)(2,1)S(1)} %collective-permute-done.21.refs_2_) | copy-start | bytes 393220
  135.1 2.8 %copy-start.24 = (bf16[512,128]{1,0:T(8,128)(2,1)}, bf16[512,128]{1,0:T(8,128)(2,1)S(1)}, u32[]{:S(2)}) copy-start(bf16[512,128]{1,0:T(8,128)(2,1)S(1)} %collective-permute-done.24.refs_5_) | copy-start | bytes 393220
  137.9 0.6 copy-start.25
  138.5 1.0 copy-start.18

commit v6 on v5

--- a/solution.py
+++ b/solution.py
@@ -13,6 +13,8 @@
 SMEM = pl.BlockSpec(memory_space=pltpu.SMEM)
 VMEM = pl.BlockSpec(memory_space=pltpu.VMEM)
 TN = (((0,), (0,)), ((), ()))
+QUICK = pl.CostEstimate(flops=1000, bytes_accessed=1000, transcendentals=0)
+LONG = pl.CostEstimate(flops=4 * 10**10, bytes_accessed=1000, transcendentals=0)
 
 
 def partner(value, mask):
@@ -35,7 +37,7 @@
     return ((high ^ k) * tile_rows + offset) // SEG
 
 
-def product_body(low_size, tile_rows, pieces, tiles, half, sends, keeps, *refs):
+def product_body(low_size, tile_rows, pieces, tiles, half, turns, sends, keeps, *refs):
     pos_ref, classes_ref, live_ref = refs[:3]
     grad_refs = refs[3 : 3 + tiles]
     weight_hbm = refs[3 + tiles]
@@ -55,8 +57,8 @@
 
     jobs = []
     for x, y in ((1, 1), (1, 0), (0, 1), (0, 0)):
-        to_x = (sent_x if x else kept_x, 2 * y)
-        to_y = (sent_y if y else kept_y, 2 * x)
+        to_x = (sent_x if x else kept_x, 2 * y, 1)
+        to_y = (sent_y if y else kept_y, *((x, 2) if turns else (2 * x, 1)))
         start = 0 if to_x[0] is not None else half
         stop = total if to_y[0] is not None else half
         if start < stop:
@@ -93,12 +95,12 @@
                 weight_ref[block + 4 * z], rows_ref[:, start:stop], preferred_element_type=F32
             )
             if to_x[0] is not None:
-                to_x[0][to_x[1] + z] = value[:, : half - start].astype(to_x[0].dtype)
+                to_x[0][to_x[1] + to_x[2] * z] = value[:, : half - start].astype(to_x[0].dtype)
             if to_y[0] is not None:
-                to_y[0][to_y[1] + z] = value[:, half - start :].astype(to_y[0].dtype)
-
-
-def product(scalars, grads, pieces, weight_blocks, up_tile, low_size, sends, keeps):
+                to_y[0][to_y[1] + to_y[2] * z] = value[:, half - start :].astype(to_y[0].dtype)
+
+
+def product(scalars, grads, pieces, weight_blocks, up_tile, low_size, turns, sends, keeps):
     blocks, width, depth = weight_blocks.shape
     tile_rows = grads[0].shape[1]
     rows = len(pieces) * pieces[0][3]
@@ -113,10 +115,9 @@
             ]
     if keeps:
         outs.append(jax.ShapeDtypeStruct((up_tile.shape[1], rows), F32))
-    share = (sends + keeps) / 2
     return pl.pallas_call(
         functools.partial(
-            product_body, low_size, tile_rows, pieces, len(grads), half, sends, keeps
+            product_body, low_size, tile_rows, pieces, len(grads), half, turns, sends, keeps
         ),
         in_specs=[SMEM] * 3
         + [VMEM] * len(grads)
@@ -129,12 +130,8 @@
             pltpu.VMEM(weight_blocks.shape, BF16),
             pltpu.SemaphoreType.DMA((blocks,)),
         ],
-        compiler_params=pltpu.CompilerParams(vmem_limit_bytes=32 * 2**20),
-        cost_estimate=pl.CostEstimate(
-            flops=int(2 * share * blocks * rows * width * depth),
-            bytes_accessed=int(share * (2 * blocks * width * depth + 3 * blocks * rows * width)),
-            transcendentals=0,
-        ),
+        compiler_params=pltpu.CompilerParams(vmem_limit_bytes=56 * 2**20),
+        cost_estimate=LONG if keeps else QUICK,
     )(*scalars, *grads, weight_blocks, *([up_tile] * keeps))
 
 
@@ -202,8 +199,10 @@
 
     own_pieces = [(0, m, (0, m, o), size) for m in range(micro_count) for o in offsets]
 
-    def produce(grads, pieces, sends, keeps):
-        return product(scalars, grads, pieces, weight_blocks, up_tile, low_size, sends, keeps)
+    def produce(grads, pieces, turns, sends, keeps):
+        return product(
+            scalars, grads, pieces, weight_blocks, up_tile, low_size, turns, sends, keeps
+        )
 
     hidden = saved_rank_outputs[0]
 
@@ -217,34 +216,38 @@
     def second_part(kept, got):
         return (kept[2:] + got[2:]).astype(BF16)
 
-    got0 = send_rows(grad_tile, 0)
+    first_rows, hidden = lax.optimization_barrier((grad_tile[0], hidden))
+    got0 = [partner(first_rows, k * low_size)[None] for k in range(1, high_size)]
     hidden = spread_hidden(hidden, 0)
-    sent_x, sent_y = produce([grad_tile], own_pieces, True, False)
+    own_grads = after(grad_tile, first_rows)
+    sent_x, sent_y = produce([own_grads], own_pieces, False, True, False)
     first_x, first_y = partner(sent_x, 1), partner(sent_y, 2)
-    own_kept = produce([after(grad_tile, sent_x, sent_y)], own_pieces, False, True)
+    rows0 = after(got0[0], sent_x, sent_y), *got0[1:]
+    c_sent_x, c_sent_y, c_kept_x, c_kept_y, part = produce(
+        list(rows0), pieces_of(0), False, True, True
+    )
+    parts = [part]
+    own_kept = produce([after(grad_tile, part)], own_pieces, False, False, True)
     kept_x, kept_y, part = own_kept
-    parts = [part]
-    chunks = [([grad_tile], own_pieces), (got0, pieces_of(0))]
-    rows0 = after(got0[0], part), *got0[1:]
-    c_sent_x, c_sent_y, c_kept_x, c_kept_y, part = produce(list(rows0), pieces_of(0), True, True)
-    parts.append(part)
+    parts.insert(0, part)
     got1 = send_rows(after(grad_tile, *got0), 1)
 
-    c_sent_x, c_sent_y = after(c_sent_x, first_x, first_y), after(c_sent_y, first_x, first_y)
-    c_first_x, c_first_y = partner(c_sent_x, 1), partner(c_sent_y, 2)
+    slot = first_x, first_y
+    c_first_x, c_first_y = partner(after(c_sent_x, *slot), 1), partner(after(c_sent_y, *slot), 2)
     second_x = partner(second_part(kept_x, first_x), 2)
     second_y = partner(second_part(kept_y, first_y), 1)
-    hidden = spread_hidden(after(hidden, first_x, first_y), 1)
+    hidden = spread_hidden(after(hidden, *slot), 1)
     own_sums = (kept_x, first_x, second_x), (kept_y, first_y, second_y)
 
-    chunks.append((got1, pieces_of(1)))
+    chunks = [([grad_tile], own_pieces), (got0, pieces_of(0)), (got1, pieces_of(1))]
     order = [piece for _, pieces in chunks for _, _, piece, _ in pieces]
     rows1 = after(got1[0], part), *got1[1:]
-    d_sent_x, d_sent_y, d_kept_x, d_kept_y, part = produce(list(rows1), pieces_of(1), True, True)
+    d_sent_x, d_sent_y, d_kept_x, d_kept_y, part = produce(
+        list(rows1), pieces_of(1), True, True, True
+    )
     parts.append(part)
-    slot = c_first_x, c_first_y, second_x, second_y
-    own_rank = jnp.concatenate(parts, 1)
-    own_rank = after(own_rank, *slot)
+    slot = c_first_x, c_first_y, second_x, second_y, hidden
+    own_rank = after(jnp.concatenate(parts, 1), *slot)
     own_rank = own_rank + partner(own_rank, 1)
     d_first_x = partner(after(d_sent_x, *slot), 1)
     d_first_y = partner(after(d_sent_y, *slot), 2)
@@ -252,28 +255,32 @@
     c_second_y = partner(second_part(c_kept_y, c_first_y), 1)
     c_sums = (c_kept_x, c_first_x, c_second_x), (c_kept_y, c_first_y, c_second_y)
 
-    def third_part(sums):
-        return [(kept[1] + got[1] + second[1]).astype(BF16) for kept, got, second in sums]
-
-    own_last = [relay(third, 4) for third in third_part(own_sums)]
-    hidden = spread_hidden(after(hidden, *slot), 2)
+    def third_part(three):
+        kept, got, second = three
+        return (kept[1] + got[1] + second[1]).astype(BF16)
+
     own_rank = own_rank + partner(own_rank, 4)
+    own_last = [relay(after(third_part(three), own_rank), 4) for three in own_sums]
+    hidden = spread_hidden(hidden, 2)
+
+    slot = d_first_x, d_first_y, c_second_x, c_second_y, *own_last, own_rank, hidden
+    own_rank = after(own_rank, *slot)
+    own_rank = (own_rank + partner(own_rank, 2)).astype(BF16)
+    d_second_x = partner(second_part(d_kept_x, after(d_first_x, *slot)), 2)
+    d_second_y = partner(second_part(d_kept_y, after(d_first_y, *slot)), 4)
+    d_sums = (d_kept_x, d_first_x, d_second_x), (d_kept_y, d_first_y, d_second_y)
+    c_last = [relay(after(third_part(three), *slot), 4) for three in c_sums]
     hiddens = []
     for k in range(high_size):
         wanted = lax.dynamic_slice_in_dim(hidden, (high ^ k) * rank_part, rank_part, 2)
         hiddens.append(partner(wanted, k * low_size) if k > 0 else wanted)
-
-    slot = d_first_x, d_first_y, *own_last
-    own_rank = after(own_rank, *slot)
-    own_rank = (own_rank + partner(own_rank, 2)).astype(BF16)
-    d_second_x = partner(second_part(d_kept_x, after(d_first_x, *slot)), 2)
-    d_second_y = partner(second_part(d_kept_y, after(d_first_y, *slot)), 1)
-    d_sums = (d_kept_x, d_first_x, d_second_x), (d_kept_y, d_first_y, d_second_y)
-    c_last = [relay(third, 4) for third in third_part(c_sums)]
     ranks = [own_rank] + [partner(own_rank, j * low_size) for j in range(1, high_size)]
 
-    slot = d_second_x, d_second_y, *c_last
-    d_last = [relay(third, 4) for third in third_part(d_sums)]
+    d_last = [
+        relay(third_part((d_kept_x, d_first_x, after(d_second_x, c_last[1]))), 4),
+        relay(third_part((d_kept_y, d_first_y, after(d_second_y, c_last[1]))), 1),
+    ]
+    ranks[-1] = after(ranks[-1], *c_last, *hiddens)
     sums = own_sums + c_sums + d_sums
     got_last = own_last + c_last + d_last
 
@@ -287,11 +294,7 @@
         out_specs=VMEM,
         out_shape=jax.ShapeDtypeStruct(up_tile.shape, BF16),
         scratch_shapes=[pltpu.VMEM(up_tile.shape, F32)],
-        cost_estimate=pl.CostEstimate(
-            flops=2 * len(order) * size * rank_part * tile_cols,
-            bytes_accessed=2 * len(order) * size * tile_cols,
-            transcendentals=0,
-        ),
+        cost_estimate=LONG,
     )(*scalars, *all_grads, *hiddens)
 
     def columns_of(j, piece):
@@ -337,11 +340,7 @@
         out_shape=jax.ShapeDtypeStruct((portion, rows_total), BF16),
         scratch_shapes=[pltpu.VMEM((portion, rows_total), F32)],
         compiler_params=pltpu.CompilerParams(vmem_limit_bytes=40 * 2**20),
-        cost_estimate=pl.CostEstimate(
-            flops=2 * rows_total * rank * portion,
-            bytes_accessed=10 * rows_total * portion,
-            transcendentals=0,
-        ),
+        cost_estimate=QUICK,
     )(*scalars, down_parts, *ranks, *[a for three in sums for a in three])
     kept = relay(kept, 0)
 
@@ -392,11 +391,7 @@
         out_specs=VMEM,
         out_shape=jax.ShapeDtypeStruct(down_parts.shape, BF16),
         scratch_shapes=[pltpu.VMEM(down_parts.shape, F32)],
-        cost_estimate=pl.CostEstimate(
-            flops=2 * rows_total * rank * portion,
-            bytes_accessed=2 * rows_total * portion,
-            transcendentals=0,
-        ),
+        cost_estimate=LONG,
     )(*scalars, forward_input[0], *ranks)
 
     return (

time: 143 us -> 153 us (1.070)
  other arithmetic: 5.06 us -> 13.4 us
  Pallas kernels: 34.5 us -> 42.6 us
  starting transfers between devices: 32.5 us -> 28.2 us
  waiting for transfers between devices: 50.3 us -> 48.6 us
    ppermute x22, waiting for transfers between devices: 47.6 us -> 36.2 us  [partner(): return lax.ppermute(value, 'tensor', pairs)]
    ppermute x7, waiting for transfers between devices: 2.74 us -> 12.4 us  [relay(): return lax.ppermute(value, ('pipe', 'tensor'), pairs)]
    pallas_call x4, Pallas kernels: 21.6 us -> 29.4 us  [product(): pl.pallas_call(functools.partial(product_body, low_size, tile_rows, piece...]
    ppermute x22, starting transfers between devices: 27.9 us -> 22.8 us  [partner(): return lax.ppermute(value, 'tensor', pairs)]
    convert_element_type x6, other arithmetic: 2.27 us -> 7.29 us  [third_part(): return (kept[1] + got[1] + second[1]).astype(BF16)]
    convert_element_type x6, other arithmetic: 2.65 us -> 5.05 us  [second_part(): return (kept[2:] + got[2:]).astype(BF16)]
    unnamed x54 -> x80, local copies, waits for them, and re-layouts: 17.5 us -> 16 us
  transfers between devices with their start and end apart: 29 -> 29, of which waited for: 9 -> 10; matrix products, arithmetic and copies ran while one was open for 5% -> 9% of each run, Pallas kernels for 18% -> 26%
where the time goes in v6:
time: 153 us; the launch traced here: 152 us
  waiting for transfers between devices  48.6 us (32%)
  Pallas kernels  42.6 us (28%)
  starting transfers between devices  28.2 us (18%)
  local copies, waits for them, and re-layouts  17.9 us (12%)
  other arithmetic  13.4 us (9%)
    ppermute x22, waiting for transfers between devices, partner(): return lax.ppermute(value, 'tensor', pairs)  36.2 us
    pallas_call x4, Pallas kernels, product(): pl.pallas_call(functools.partial(product_body, low_size, tile_rows, piece...  29.4 us
    ppermute x22, starting transfers between devices, partner(): return lax.ppermute(value, 'tensor', pairs)  22.8 us
    unnamed x80, local copies, waits for them, and re-layouts  16 us
    ppermute x7, waiting for transfers between devices, relay(): return lax.ppermute(value, ('pipe', 'tensor'), pairs)  12.4 us
    convert_element_type x6, other arithmetic, third_part(): return (kept[1] + got[1] + second[1]).astype(BF16)  7.29 us
    ppermute x7, starting transfers between devices, relay(): return lax.ppermute(value, ('pipe', 'tensor'), pairs)  5.35 us
    convert_element_type x6, other arithmetic, second_part(): return (kept[2:] + got[2:]).astype(BF16)  5.05 us
  transfers between devices with their start and end apart: 29, of which 10 were waited for; matrix products, arithmetic and copies ran while one was open for 9% of the time, Pallas kernels for 26%

profile of v6, /device:TPU:0, one launch (start us, length us, event | category | flops | bytes accessed | tf_op | source)
XLA Modules:
  0.0 151.7 jit_solution(14752734981919577021)
XLA Ops:
  0.6 1.1 slice_bitcast_fusion.1
  1.7 4.1 %collective-permute-start = (bf16[256,1024]{1,0:T(8,128)(2,1)S(1)}, bf16[256,1024]{1,0:T(8,128)(2,1)S(1)}, u32[]{:S(2)}, u32[]{:S(2)}) collective-permute-start(bf16[256,1024]{1,0:T(8,128)(2,1)S(1)} %slice_bitcast_fusion.1), channel_id=1, source_target_pairs={{0,8},{1,9},{2,10},{3,11},{4,12},{5,13},{6,14},{7,15},{8,0},{9,1},... | collective-permute-start | bytes 1572872 | tf_op jit(solution)/shard_map/ppermute | solution.py:22
  5.8 1.5 collective-permute-start.8
  7.3 6.9 %shard_map.103 = (bf16[4,512,256]{2,1,0:T(8,128)(2,1)}, bf16[4,512,256]{2,1,0:T(8,128)(2,1)}) custom-call(s32[1]{0:T(128)} %bitcast.refs_0_.pos_ref, s32[2,4]{1,0:T(2,128)} %bitcast.34, s32[2]{0:T(128)} %bitcast.41, bf16[2,256,1024]{2,1,0:T(8,128)(2,1)} %bitcast.52, bf16[8,512,1024]{2,1,0:T(8,128)(2,1)} %bitcast.48), custom_call_target="tpu_custom_call" | custom-call | flops 1000 | bytes 1000 | tf_op jit(solution)/shard_map/pallas_call | solution.py:118
  14.2 0.6 collective-permute-start.2
  14.8 1.5 %collective-permute-start.3 = (bf16[4,512,256]{2,1,0:T(8,128)(2,1)}, bf16[4,512,256]{2,1,0:T(8,128)(2,1)}, u32[]{:S(2)}, u32[]{:S(2)}) collective-permute-start(bf16[4,512,256]{2,1,0:T(8,128)(2,1)} %get-tuple-element.50), channel_id=1, source_target_pairs={{0,2},{1,3},{2,0},{3,1},{4,6},{5,7},{6,4},{7,5},{8,10},{9,11},{10,... | collective-permute-start | bytes 3145736 | tf_op jit(solution)/shard_map/ppermute | solution.py:22
  16.3 12.7 %collective-permute-done = bf16[256,1024]{1,0:T(8,128)(2,1)S(1)} collective-permute-done((bf16[256,1024]{1,0:T(8,128)(2,1)S(1)}, bf16[256,1024]{1,0:T(8,128)(2,1)S(1)}, u32[]{:S(2)}, u32[]{:S(2)}) %collective-permute-start) | collective-permute-done | bytes 524320 | tf_op jit(solution)/shard_map/ppermute | solution.py:22
  29.1 0.7 copy-done.35
  29.8 7.4 %shard_map.104 = (bf16[4,512,128]{2,1,0:T(8,128)(2,1)}, bf16[4,512,128]{2,1,0:T(8,128)(2,1)}, f32[4,512,128]{2,1,0:T(8,128)}, f32[4,512,128]{2,1,0:T(8,128)}, f32[32,256]{1,0:T(8,128)}) custom-call(s32[1]{0:T(128)} %bitcast.refs_0_.pos_ref, s32[2,4]{1,0:T(2,128)} %bitcast.35, s32[2]{0:T(128)} %bitcast.42, bf16[1,256,1024]{2,1,0:T(8,128)(2,1)} %bitcast.63, ...), custom_call_target="tpu_custom_call" | custom-call | flops 40000000000 | bytes 1000 | tf_op jit(solution)/shard_map/pallas_call | solution.py:118
  37.2 7.8 %shard_map.105 = (f32[4,512,256]{2,1,0:T(8,128)}, f32[4,512,256]{2,1,0:T(8,128)}, f32[32,512]{1,0:T(8,128)}) custom-call(s32[1]{0:T(128)} %bitcast.refs_0_.pos_ref, s32[2,4]{1,0:T(2,128)} %bitcast.36, s32[2]{0:T(128)} %bitcast.43, bf16[2,256,1024]{2,1,0:T(8,128)(2,1)} %bitcast.53, bf16[8,512,1024]{2,1,0:T(8,128)(2,1)} %bitcast.50, bf16[8,32,1024]{2,1,0:T(8,128)(2,1)} %bitcast.61), custom_call_target="tpu_custom_call" | custom-call | flops 40000000000 | bytes 1000 | tf_op jit(solution)/shard_map/pallas_call | solution.py:118
  45.1 1.6 %collective-permute-start.9 = (bf16[2,64,64]{2,1,0:T(8,128)(2,1)S(1)}, bf16[2,64,64]{2,1,0:T(8,128)(2,1)S(1)}, u32[]{:S(2)}, u32[]{:S(2)}) collective-permute-start(bf16[2,64,64]{2,1,0:T(8,128)(2,1)S(1)} %maximum_select_fusion.2), channel_id=1, source_target_pairs={{0,2},{1,3},{2,0},{3,1},{4,6},{5,7},{6,4},{7,5},{8,10},{9,11},{10,... | collective-permute-start | bytes 49160 | tf_op jit(solution)/shard_map/ppermute | solution.py:22
  47.1 1.5 %collective-permute-start.4 = (bf16[4,512,128]{2,1,0:T(8,128)(2,1)}, bf16[4,512,128]{2,1,0:T(8,128)(2,1)S(1)}, u32[]{:S(2)}, u32[]{:S(2)}) collective-permute-start(bf16[4,512,128]{2,1,0:T(8,128)(2,1)} %get-tuple-element.59), channel_id=1, source_target_pairs={{0,1},{1,0},{2,3},{3,2},{4,5},{5,4},{6,7},{7,6},{8,9},{9,8},{10,11... | collective-permute-start | bytes 1572872 | tf_op jit(solution)/shard_map/ppermute | solution.py:22
  48.7 5.6 %collective-permute-done.1 = bf16[256,1024]{1,0:T(8,128)(2,1)S(1)} collective-permute-done((bf16[256,1024]{1,0:T(8,128)(2,1)S(1)}, bf16[256,1024]{1,0:T(8,128)(2,1)S(1)}, u32[]{:S(2)}, u32[]{:S(2)}) %collective-permute-start.1) | collective-permute-done | bytes 524320 | tf_op jit(solution)/shard_map/ppermute | solution.py:22
  54.3 2.5 %add_convert_fusion = bf16[2,512,256]{2,1,0:T(8,128)(2,1)} fusion(f32[4,512,256]{2,1,0:T(8,128)} %get-tuple-element.63.refs_5_, bf16[4,512,256]{2,1,0:T(8,128)(2,1)} %collective-permute-done.3.refs_6_), kind=kLoop, calls=%fused_computation | loop fusion | flops 786432 | bytes 2097152 | tf_op jit(solution)/shard_map/convert_element_type | solution.py:217
  56.8 1.2 collective-permute-start.7
  58.0 1.0 add_convert_fusion.1
  59.0 1.6 %collective-permute-start.6 = (bf16[2,512,256]{2,1,0:T(8,128)(2,1)}, bf16[2,512,256]{2,1,0:T(8,128)(2,1)S(1)}, u32[]{:S(2)}, u32[]{:S(2)}) collective-permute-start(bf16[2,512,256]{2,1,0:T(8,128)(2,1)} %add_convert_fusion.1), channel_id=1, source_target_pairs={{0,2},{1,3},{2,0},{3,1},{4,6},{5,7},{6,4},{7,5},{8,10},{9,11},{10,... | collective-permute-start | bytes 1572872 | tf_op jit(solution)/shard_map/ppermute | solution.py:22
  60.6 7.3 %shard_map.106 = (bf16[4,512,128]{2,1,0:T(8,128)(2,1)}, bf16[4,512,128]{2,1,0:T(8,128)(2,1)}, f32[4,512,128]{2,1,0:T(8,128)}, f32[4,512,128]{2,1,0:T(8,128)}, f32[32,256]{1,0:T(8,128)}) custom-call(s32[1]{0:T(128)} %bitcast.refs_0_.pos_ref, s32[2,4]{1,0:T(2,128)} %bitcast.37, s32[2]{0:T(128)} %bitcast.44, bf16[1,256,1024]{2,1,0:T(8,128)(2,1)} %bitcast.65, ...), custom_call_target="tpu_custom_call" | custom-call | flops 40000000000 | bytes 1000 | tf_op jit(solution)/shard_map/pallas_call | solution.py:118
  68.1 0.9 pad_maximum_fusion
  69.0 3.3 %collective-permute-done.18 = bf16[2,128,64]{2,1,0:T(8,128)(2,1)S(1)} collective-permute-done((bf16[2,128,64]{2,1,0:T(8,128)(2,1)S(1)}, bf16[2,128,64]{2,1,0:T(8,128)(2,1)S(1)}, u32[]{:S(2)}, u32[]{:S(2)}) %collective-permute-start.18) | collective-permute-done | bytes 32800 | tf_op jit(solution)/shard_map/ppermute | solution.py:22
  72.4 0.8 constant_dynamic-slice_fusion
  73.2 0.6 collective-permute-start.15
  73.9 0.8 collective-permute-start.14
  74.8 0.9 copy-done.19
  75.8 1.2 collective-permute-start.10
  77.1 1.5 %collective-permute-start.13 = (bf16[4,512,128]{2,1,0:T(8,128)(2,1)S(1)}, bf16[4,512,128]{2,1,0:T(8,128)(2,1)S(1)}, u32[]{:S(2)}, u32[]{:S(2)}) collective-permute-start(bf16[4,512,128]{2,1,0:T(8,128)(2,1)S(1)} %copy-done.38), channel_id=1, source_target_pairs={{0,2},{1,3},{2,0},{3,1},{4,6},{5,7},{6,4},{7,5},{8,10},{9,11},{10,... | collective-permute-start | bytes 1572872 | tf_op jit(solution)/shard_map/ppermute | solution.py:22
  78.6 0.5 collective-permute-start.12
  79.1 1.3 fusion.1
  80.4 5.0 %collective-permute-done.10 = f32[32,1024]{1,0:T(8,128)S(1)} collective-permute-done((f32[32,1024]{1,0:T(8,128)S(1)}, f32[32,1024]{1,0:T(8,128)S(1)}, u32[]{:S(2)}, u32[]{:S(2)}) %collective-permute-start.10) | collective-permute-done | bytes 131104 | tf_op jit(solution)/shard_map/ppermute | solution.py:22
  85.5 1.1 fusion
  86.6 3.8 %collective-permute-done.11 = f32[32,1024]{1,0:T(8,128)S(1)} collective-permute-done((f32[32,1024]{1,0:T(8,128)S(1)}, f32[32,1024]{1,0:T(8,128)S(1)}, u32[]{:S(2)}, u32[]{:S(2)}) %collective-permute-start.11) | collective-permute-done | bytes 131104 | tf_op jit(solution)/shard_map/ppermute | solution.py:22
  90.5 1.7 %collective-permute-start.17 = (bf16[512,256]{1,0:T(8,128)(2,1)S(1)}, bf16[512,256]{1,0:T(8,128)(2,1)S(1)}, u32[]{:S(2)}, u32[]{:S(2)}) collective-permute-start(bf16[512,256]{1,0:T(8,128)(2,1)S(1)} %fusion.1), channel_id=1, source_target_pairs={{0,20},{1,21},{2,22},{3,23},{4,16},{5,17},{6,18},{7,19},{8,28},{9,... | collective-permute-start | bytes 786440 | tf_op jit(solution)/shard_map/ppermute | solution.py:32
  92.3 0.7 fusion.3
  93.0 0.7 fusion.2
  93.7 8.3 %collective-permute-done.16.refs_0_ = bf16[512,256]{1,0:T(8,128)(2,1)S(1)} collective-permute-done((bf16[512,256]{1,0:T(8,128)(2,1)S(1)}, bf16[512,256]{1,0:T(8,128)(2,1)S(1)}, u32[]{:S(2)}, u32[]{:S(2)}) %collective-permute-start.16) | collective-permute-done | bytes 262176 | tf_op jit(solution)/shard_map/ppermute | solution.py:32
  102.0 4.1 %collective-permute-done.17.refs_1_ = bf16[512,256]{1,0:T(8,128)(2,1)S(1)} collective-permute-done((bf16[512,256]{1,0:T(8,128)(2,1)S(1)}, bf16[512,256]{1,0:T(8,128)(2,1)S(1)}, u32[]{:S(2)}, u32[]{:S(2)}) %collective-permute-start.17) | collective-permute-done | bytes 262176 | tf_op jit(solution)/shard_map/ppermute | solution.py:32
  106.1 1.5 collective-permute-start.19
  107.7 1.7 %collective-permute-start.22 = (bf16[512,128]{1,0:T(8,128)(2,1)}, bf16[512,128]{1,0:T(8,128)(2,1)}, u32[]{:S(2)}, u32[]{:S(2)}) collective-permute-start(bf16[512,128]{1,0:T(8,128)(2,1)} %fusion.3), channel_id=1, source_target_pairs={{0,20},{1,21},{2,22},{3,23},{4,16},{5,17},{6,18},{7,19},{8,28},{9,... | collective-permute-start | bytes 393224 | tf_op jit(solution)/shard_map/ppermute | solution.py:32
  109.4 0.8 add_convert_fusion.2
  110.2 0.8 add_convert_fusion.3
  111.2 1.6 %collective-permute-start.24 = (bf16[2,512,128]{2,1,0:T(8,128)(2,1)}, bf16[2,512,128]{2,1,0:T(8,128)(2,1)}, u32[]{:S(2)}, u32[]{:S(2)}) collective-permute-start(bf16[2,512,128]{2,1,0:T(8,128)(2,1)} %add_convert_fusion.3), channel_id=1, source_target_pairs={{0,2},{1,3},{2,0},{3,1},{4,6},{5,7},{6,4},{7,5},{8,10},{9,11},{10,... | collective-permute-start | bytes 786440 | tf_op jit(solution)/shard_map/ppermute | solution.py:22
  112.8 0.7 collective-permute-start.20
  113.5 3.9 %shard_map.110 = bf16[8,32,1024]{2,1,0:T(8,128)(2,1)} custom-call(s32[1]{0:T(128)} %bitcast.refs_0_.pos_ref, s32[2,4]{1,0:T(2,128)} %bitcast.38, s32[2]{0:T(128)} %bitcast.45, bf16[2,256,1024]{2,1,0:T(8,128)(2,1)} %bitcast.54, bf16[1,256,1024]{2,1,0:T(8,128)(2,1)} %bitcast.64, bf16[1,256,1024]{2,1,0:T(8,128)(2,1)} %bitcast.66, ...), custom_call_target="tpu_custom_call" | custom-call | flops 40000000000 | bytes 1000 | tf_op jit(solution)/shard_map/pallas_call | solution.py:291
  117.4 2.9 %collective-permute-done.20.refs_1_ = bf16[32,1024]{1,0:T(8,128)(2,1)S(1)} collective-permute-done((bf16[32,1024]{1,0:T(8,128)(2,1)S(1)}, bf16[32,1024]{1,0:T(8,128)(2,1)S(1)}, u32[]{:S(2)}, u32[]{:S(2)}) %collective-permute-start.20) | collective-permute-done | bytes 65568 | tf_op jit(solution)/shard_map/ppermute | solution.py:22
  120.3 2.5 %collective-permute-done.25.refs_19_ = bf16[2,512,128]{2,1,0:T(8,128)(2,1)} collective-permute-done((bf16[2,512,128]{2,1,0:T(8,128)(2,1)}, bf16[2,512,128]{2,1,0:T(8,128)(2,1)}, u32[]{:S(2)}, u32[]{:S(2)}) %collective-permute-start.25) | collective-permute-done | bytes 262176 | tf_op jit(solution)/shard_map/ppermute | solution.py:22
  122.8 1.7 %fusion.5 = bf16[512,128]{1,0:T(8,128)(2,1)} fusion(f32[4,512,128]{2,1,0:T(8,128)} %get-tuple-element.81.refs_17_, bf16[4,512,128]{2,1,0:T(8,128)(2,1)} %copy-done.13, bf16[2,512,128]{2,1,0:T(8,128)(2,1)} %collective-permute-done.25.refs_19_), kind=kLoop, calls=%fused_computation.19 | loop fusion | flops 327680 | bytes 655360 | tf_op jit(solution)/shard_map/convert_element_type | solution.py:260
  124.6 1.4 collective-permute-start.28
  126.0 1.7 %fusion.4 = bf16[512,128]{1,0:T(8,128)(2,1)} fusion(f32[4,512,128]{2,1,0:T(8,128)} %get-tuple-element.79.refs_14_, bf16[4,512,128]{2,1,0:T(8,128)(2,1)} %copy-done.15, bf16[2,512,128]{2,1,0:T(8,128)(2,1)} %collective-permute-done.24.refs_16_), kind=kLoop, calls=%fused_computation.18 | loop fusion | flops 327680 | bytes 655360 | tf_op jit(solution)/shard_map/convert_element_type | solution.py:260
  127.7 1.2 copy-done.2
  129.0 1.2 copy-done.4
  130.2 1.2 copy-done.6
  131.4 1.2 copy-done.8
  132.6 1.0 copy-done.10
  133.7 1.0 copy-done.12
  134.7 1.0 copy-done.14
  135.8 1.0 copy-done.16
  136.8 1.0 copy-done.18
  137.9 1.0 copy-done.20
  138.9 0.9 copy-done.22
  139.8 1.0 copy-done.23
  140.9 2.9 %shard_map.107 = bf16[512,1024]{1,0:T(8,128)(2,1)} custom-call(s32[1]{0:T(128)} %bitcast.refs_0_.pos_ref, s32[2,4]{1,0:T(2,128)S(1)} %bitcast.40, s32[2]{0:T(128)S(1)} %bitcast.47, bf16[8,2,32,512]{3,2,1,0:T(8,128)(2,1)S(1)} %bitcast.33, bf16[32,1024]{1,0:T(8,128)(2,1)S(1)} %add_convert_fusion.12.refs_0_, ...), custom_call_target="tpu_custom_call" | custom-call | flops 1000 | bytes 1000 | tf_op jit(solution)/shard_map/pallas_call | solution.py:333
  144.2 3.3 %shard_map.109 = bf16[8,2,32,512]{3,2,1,0:T(8,128)(2,1)} custom-call(s32[1]{0:T(128)} %bitcast.refs_0_.pos_ref, s32[2,4]{1,0:T(2,128)} %bitcast.39, s32[2]{0:T(128)} %bitcast.46, bf16[2,512,512]{2,1,0:T(8,128)(2,1)} %bitcast.59, bf16[32,1024]{1,0:T(8,128)(2,1)} %copy-done.24, bf16[32,1024]{1,0:T(8,128)(2,1)} %copy-done.25), custom_call_target="tpu_custom_call" | custom-call | flops 40000000000 | bytes 1000 | tf_op jit(solution)/shard_map/pallas_call | solution.py:388
  147.6 1.0 copy-done.29
  148.6 3.1 %shard_map.108 = bf16[2,512,512]{2,1,0:T(8,128)(2,1)} custom-call(s32[1]{0:T(128)} %bitcast.refs_0_.pos_ref, bf16[512,1024]{1,0:T(8,128)(2,1)} %copy-done.29, bf16[512,256]{1,0:T(8,128)(2,1)} %copy-done.30, bf16[512,256]{1,0:T(8,128)(2,1)} %copy-done.31, bf16[512,128]{1,0:T(8,128)(2,1)} %collective-permute-done.21.refs_2_, ...), custom_call_target="tpu_custom_call" | custom-call | tf_op jit(solution)/shard_map/pallas_call | solution.py:361
  (104 shorter events, 2.0 us)
Async XLA Ops:
  1.7 27.3 %collective-permute-start = (bf16[256,1024]{1,0:T(8,128)(2,1)S(1)}, bf16[256,1024]{1,0:T(8,128)(2,1)S(1)}, u32[]{:S(2)}, u32[]{:S(2)}) collective-permute-start(bf16[256,1024]{1,0:T(8,128)(2,1)S(1)} %slice_bitcast_fusion.1), channel_id=1, source_target_pairs={{0,8},{1,9},{2,10},{3,11},{4,12},{5,13},{6,14},{7,15},{8,0},{9,1},... | collective-permute-start | bytes 1572872 | tf_op jit(solution)/shard_map/ppermute | solution.py:22
  5.8 10.5 %collective-permute-start.8 = (bf16[2,32,64]{2,1,0:T(8,128)(2,1)}, bf16[2,32,64]{2,1,0:T(8,128)(2,1)S(1)}, u32[]{:S(2)}, u32[]{:S(2)}) collective-permute-start(bf16[2,32,64]{2,1,0:T(8,128)(2,1)} %bitcast.57), channel_id=1, source_target_pairs={{0,1},{1,0},{2,3},{3,2},{4,5},{5,4},{6,7},{7,6},{8,9},{9,8},{10,11... | collective-permute-start | bytes 24584 | tf_op jit(solution)/shard_map/ppermute | solution.py:22
  7.3 9.0 %copy-start.34 = (bf16[1,2,32,64]{3,2,1,0:T(8,128)(2,1)S(1)}, bf16[1,2,32,64]{3,2,1,0:T(8,128)(2,1)}, u32[]{:S(2)}) copy-start(bf16[1,2,32,64]{3,2,1,0:T(8,128)(2,1)} %param.10) | copy-start | bytes 24580
  7.3 21.7 %copy-start.28 = (bf16[1,1,2,256,1024]{4,3,2,1,0:T(8,128)(2,1)S(1)}, bf16[1,1,2,256,1024]{4,3,2,1,0:T(8,128)(2,1)}, u32[]{:S(2)}) copy-start(bf16[1,1,2,256,1024]{4,3,2,1,0:T(8,128)(2,1)} %param.8) | copy-start | bytes 3145732
  14.2 30.9 %collective-permute-start.2 = (bf16[4,512,256]{2,1,0:T(8,128)(2,1)}, bf16[4,512,256]{2,1,0:T(8,128)(2,1)S(1)}, u32[]{:S(2)}, u32[]{:S(2)}) collective-permute-start(bf16[4,512,256]{2,1,0:T(8,128)(2,1)} %get-tuple-element.49), channel_id=1, source_target_pairs={{0,1},{1,0},{2,3},{3,2},{4,5},{5,4},{6,7},{7,6},{8,9},{9,8},{10,11... | collective-permute-start | bytes 3145736 | tf_op jit(solution)/shard_map/ppermute | solution.py:22
  14.8 30.3 %collective-permute-start.3 = (bf16[4,512,256]{2,1,0:T(8,128)(2,1)}, bf16[4,512,256]{2,1,0:T(8,128)(2,1)}, u32[]{:S(2)}, u32[]{:S(2)}) collective-permute-start(bf16[4,512,256]{2,1,0:T(8,128)(2,1)} %get-tuple-element.50), channel_id=1, source_target_pairs={{0,2},{1,3},{2,0},{3,1},{4,6},{5,7},{6,4},{7,5},{8,10},{9,11},{10,... | collective-permute-start | bytes 3145736 | tf_op jit(solution)/shard_map/ppermute | solution.py:22
  29.0 25.3 %collective-permute-start.1 = (bf16[256,1024]{1,0:T(8,128)(2,1)S(1)}, bf16[256,1024]{1,0:T(8,128)(2,1)S(1)}, u32[]{:S(2)}, u32[]{:S(2)}) collective-permute-start(bf16[256,1024]{1,0:T(8,128)(2,1)S(1)} %slice_bitcast_fusion), channel_id=1, source_target_pairs={{0,8},{1,9},{2,10},{3,11},{4,12},{5,13},{6,14},{7,15},{8,0},{9,1},... | collective-permute-start | bytes 1572872 | tf_op jit(solution)/shard_map/ppermute | solution.py:22
  45.0 13.0 %copy-start = (f32[4,512,256]{2,1,0:T(8,128)S(1)}, f32[4,512,256]{2,1,0:T(8,128)}, u32[]{:S(2)}) copy-start(f32[4,512,256]{2,1,0:T(8,128)} %get-tuple-element.62.refs_2_) | copy-start | bytes 6291460
  45.1 22.9 %collective-permute-start.9 = (bf16[2,64,64]{2,1,0:T(8,128)(2,1)S(1)}, bf16[2,64,64]{2,1,0:T(8,128)(2,1)S(1)}, u32[]{:S(2)}, u32[]{:S(2)}) collective-permute-start(bf16[2,64,64]{2,1,0:T(8,128)(2,1)S(1)} %maximum_select_fusion.2), channel_id=1, source_target_pairs={{0,2},{1,3},{2,0},{3,1},{4,6},{5,7},{6,4},{7,5},{8,10},{9,11},{10,... | collective-permute-start | bytes 49160 | tf_op jit(solution)/shard_map/ppermute | solution.py:22
  46.7 26.5 %collective-permute-start.5 = (bf16[4,512,128]{2,1,0:T(8,128)(2,1)}, bf16[4,512,128]{2,1,0:T(8,128)(2,1)S(1)}, u32[]{:S(2)}, u32[]{:S(2)}) collective-permute-start(bf16[4,512,128]{2,1,0:T(8,128)(2,1)} %get-tuple-element.61), channel_id=1, source_target_pairs={{0,2},{1,3},{2,0},{3,1},{4,6},{5,7},{6,4},{7,5},{8,10},{9,11},{10,... | collective-permute-start | bytes 1572872 | tf_op jit(solution)/shard_map/ppermute | solution.py:22
  47.1 26.7 %collective-permute-start.4 = (bf16[4,512,128]{2,1,0:T(8,128)(2,1)}, bf16[4,512,128]{2,1,0:T(8,128)(2,1)S(1)}, u32[]{:S(2)}, u32[]{:S(2)}) collective-permute-start(bf16[4,512,128]{2,1,0:T(8,128)(2,1)} %get-tuple-element.59), channel_id=1, source_target_pairs={{0,1},{1,0},{2,3},{3,2},{4,5},{5,4},{6,7},{7,6},{8,9},{9,8},{10,11... | collective-permute-start | bytes 1572872 | tf_op jit(solution)/shard_map/ppermute | solution.py:22
  54.3 4.7 %copy-start.36 = (bf16[256,1024]{1,0:T(8,128)(2,1)}, bf16[256,1024]{1,0:T(8,128)(2,1)S(1)}, u32[]{:S(2)}) copy-start(bf16[256,1024]{1,0:T(8,128)(2,1)S(1)} %collective-permute-done.1) | copy-start | bytes 1572868
  56.8 18.0 %collective-permute-start.7 = (bf16[2,512,256]{2,1,0:T(8,128)(2,1)}, bf16[2,512,256]{2,1,0:T(8,128)(2,1)S(1)}, u32[]{:S(2)}, u32[]{:S(2)}) collective-permute-start(bf16[2,512,256]{2,1,0:T(8,128)(2,1)} %add_convert_fusion), channel_id=1, source_target_pairs={{0,1},{1,0},{2,3},{3,2},{4,5},{5,4},{6,7},{7,6},{8,9},{9,8},{10,11... | collective-permute-start | bytes 1572872 | tf_op jit(solution)/shard_map/ppermute | solution.py:22
  59.0 9.1 %copy-start.32 = (f32[32,512]{1,0:T(8,128)S(1)}, f32[32,512]{1,0:T(8,128)}, u32[]{:S(2)}) copy-start(f32[32,512]{1,0:T(8,128)} %get-tuple-element.54) | copy-start | bytes 196612
  59.0 9.1 %copy-start.33 = (f32[32,256]{1,0:T(8,128)S(1)}, f32[32,256]{1,0:T(8,128)}, u32[]{:S(2)}) copy-start(f32[32,256]{1,0:T(8,128)} %get-tuple-element.52) | copy-start | bytes 98308
  59.0 14.2 %copy-start.3 = (f32[4,512,128]{2,1,0:T(8,128)S(1)}, f32[4,512,128]{2,1,0:T(8,128)}, u32[]{:S(2)}) copy-start(f32[4,512,128]{2,1,0:T(8,128)} %get-tuple-element.72.refs_11_) | copy-start | bytes 3145732
  59.0 15.7 %collective-permute-start.6 = (bf16[2,512,256]{2,1,0:T(8,128)(2,1)}, bf16[2,512,256]{2,1,0:T(8,128)(2,1)S(1)}, u32[]{:S(2)}, u32[]{:S(2)}) collective-permute-start(bf16[2,512,256]{2,1,0:T(8,128)(2,1)} %add_convert_fusion.1), channel_id=1, source_target_pairs={{0,2},{1,3},{2,0},{3,1},{4,6},{5,7},{6,4},{7,5},{8,10},{9,11},{10,... | collective-permute-start | bytes 1572872 | tf_op jit(solution)/shard_map/ppermute | solution.py:22
  67.9 5.9 %copy-start.1 = (f32[4,512,128]{2,1,0:T(8,128)S(1)}, f32[4,512,128]{2,1,0:T(8,128)}, u32[]{:S(2)}) copy-start(f32[4,512,128]{2,1,0:T(8,128)} %get-tuple-element.71.refs_8_) | copy-start | bytes 3145732
  68.0 9.1 %copy-start.38 = (bf16[4,512,128]{2,1,0:T(8,128)(2,1)S(1)}, bf16[4,512,128]{2,1,0:T(8,128)(2,1)}, u32[]{:S(2)}) copy-start(bf16[4,512,128]{2,1,0:T(8,128)(2,1)} %get-tuple-element.70) | copy-start | bytes 1572868
  68.0 10.6 %copy-start.37 = (bf16[4,512,128]{2,1,0:T(8,128)(2,1)S(1)}, bf16[4,512,128]{2,1,0:T(8,128)(2,1)}, u32[]{:S(2)}) copy-start(bf16[4,512,128]{2,1,0:T(8,128)(2,1)} %get-tuple-element.68) | copy-start | bytes 1572868
  68.0 4.3 %collective-permute-start.18 = (bf16[2,128,64]{2,1,0:T(8,128)(2,1)S(1)}, bf16[2,128,64]{2,1,0:T(8,128)(2,1)S(1)}, u32[]{:S(2)}, u32[]{:S(2)}) collective-permute-start(bf16[2,128,64]{2,1,0:T(8,128)(2,1)S(1)} %maximum_select_fusion.1), channel_id=1, source_target_pairs={{0,4},{1,5},{2,6},{3,7},{4,0},{5,1},{6,2},{7,3},{8,12},{9,13},{10,... | collective-permute-start | bytes 98312 | tf_op jit(solution)/shard_map/ppermute | solution.py:22
  73.2 19.1 %copy-start.9 = (bf16[4,512,128]{2,1,0:T(8,128)(2,1)}, bf16[4,512,128]{2,1,0:T(8,128)(2,1)S(1)}, u32[]{:S(2)}) copy-start(bf16[4,512,128]{2,1,0:T(8,128)(2,1)S(1)} %collective-permute-done.5.refs_12_) | copy-start | bytes 1572868
  73.2 17.3 %collective-permute-start.15 = (bf16[2,512,128]{2,1,0:T(8,128)(2,1)S(1)}, bf16[2,512,128]{2,1,0:T(8,128)(2,1)S(1)}, u32[]{:S(2)}, u32[]{:S(2)}) collective-permute-start(bf16[2,512,128]{2,1,0:T(8,128)(2,1)S(1)} %add_convert_fusion.6), channel_id=1, source_target_pairs={{0,1},{1,0},{2,3},{3,2},{4,5},{5,4},{6,7},{7,6},{8,9},{9,8},{10,11... | collective-permute-start | bytes 786440 | tf_op jit(solution)/shard_map/ppermute | solution.py:22
  73.9 19.1 %copy-start.11 = (bf16[4,512,128]{2,1,0:T(8,128)(2,1)}, bf16[4,512,128]{2,1,0:T(8,128)(2,1)S(1)}, u32[]{:S(2)}) copy-start(bf16[4,512,128]{2,1,0:T(8,128)(2,1)S(1)} %collective-permute-done.4.refs_9_) | copy-start | bytes 1572868
  73.9 19.1 %collective-permute-start.14 = (bf16[2,512,128]{2,1,0:T(8,128)(2,1)S(1)}, bf16[2,512,128]{2,1,0:T(8,128)(2,1)S(1)}, u32[]{:S(2)}, u32[]{:S(2)}) collective-permute-start(bf16[2,512,128]{2,1,0:T(8,128)(2,1)S(1)} %add_convert_fusion.7), channel_id=1, source_target_pairs={{0,2},{1,3},{2,0},{3,1},{4,6},{5,7},{6,4},{7,5},{8,10},{9,11},{10,... | collective-permute-start | bytes 786440 | tf_op jit(solution)/shard_map/ppermute | solution.py:22
  74.7 1.1 copy-start.17
  75.8 33.6 %copy-start.7 = (f32[4,512,128]{2,1,0:T(8,128)S(1)}, f32[4,512,128]{2,1,0:T(8,128)}, u32[]{:S(2)}) copy-start(f32[4,512,128]{2,1,0:T(8,128)} %get-tuple-element.81.refs_17_) | copy-start | bytes 3145732
  75.8 9.5 %collective-permute-start.10 = (f32[32,1024]{1,0:T(8,128)S(1)}, f32[32,1024]{1,0:T(8,128)S(1)}, u32[]{:S(2)}, u32[]{:S(2)}) collective-permute-start(f32[32,1024]{1,0:T(8,128)S(1)} %pad_maximum_fusion), channel_id=1, source_target_pairs={{0,1},{1,0},{2,3},{3,2},{4,5},{5,4},{6,7},{7,6},{8,9},{9,8},{10,11... | collective-permute-start | bytes 393224 | tf_op jit(solution)/shard_map/ppermute | solution.py:22
  77.1 29.0 %collective-permute-start.13 = (bf16[4,512,128]{2,1,0:T(8,128)(2,1)S(1)}, bf16[4,512,128]{2,1,0:T(8,128)(2,1)S(1)}, u32[]{:S(2)}, u32[]{:S(2)}) collective-permute-start(bf16[4,512,128]{2,1,0:T(8,128)(2,1)S(1)} %copy-done.38), channel_id=1, source_target_pairs={{0,2},{1,3},{2,0},{3,1},{4,6},{5,7},{6,4},{7,5},{8,10},{9,11},{10,... | collective-permute-start | bytes 1572872 | tf_op jit(solution)/shard_map/ppermute | solution.py:22
  78.6 27.5 %collective-permute-start.12 = (bf16[4,512,128]{2,1,0:T(8,128)(2,1)S(1)}, bf16[4,512,128]{2,1,0:T(8,128)(2,1)S(1)}, u32[]{:S(2)}, u32[]{:S(2)}) collective-permute-start(bf16[4,512,128]{2,1,0:T(8,128)(2,1)S(1)} %copy-done.37), channel_id=1, source_target_pairs={{0,1},{1,0},{2,3},{3,2},{4,5},{5,4},{6,7},{7,6},{8,9},{9,8},{10,11... | collective-permute-start | bytes 1572872 | tf_op jit(solution)/shard_map/ppermute | solution.py:22
  85.4 24.8 %copy-start.5 = (f32[4,512,128]{2,1,0:T(8,128)S(1)}, f32[4,512,128]{2,1,0:T(8,128)}, u32[]{:S(2)}) copy-start(f32[4,512,128]{2,1,0:T(8,128)} %get-tuple-element.79.refs_14_) | copy-start | bytes 3145732
  85.4 5.0 %collective-permute-start.11 = (f32[32,1024]{1,0:T(8,128)S(1)}, f32[32,1024]{1,0:T(8,128)S(1)}, u32[]{:S(2)}, u32[]{:S(2)}) collective-permute-start(f32[32,1024]{1,0:T(8,128)S(1)} %add.84), channel_id=1, source_target_pairs={{0,4},{1,5},{2,6},{3,7},{4,0},{5,1},{6,2},{7,3},{8,12},{9,13},{10,... | collective-permute-start | bytes 393224 | tf_op jit(solution)/shard_map/ppermute | solution.py:22
  90.5 11.5 %collective-permute-start.16 = (bf16[512,256]{1,0:T(8,128)(2,1)S(1)}, bf16[512,256]{1,0:T(8,128)(2,1)S(1)}, u32[]{:S(2)}, u32[]{:S(2)}) collective-permute-start(bf16[512,256]{1,0:T(8,128)(2,1)S(1)} %fusion), channel_id=1, source_target_pairs={{0,20},{1,21},{2,22},{3,23},{4,16},{5,17},{6,18},{7,19},{8,28},{9,... | collective-permute-start | bytes 786440 | tf_op jit(solution)/shard_map/ppermute | solution.py:32
  90.5 15.6 %collective-permute-start.17 = (bf16[512,256]{1,0:T(8,128)(2,1)S(1)}, bf16[512,256]{1,0:T(8,128)(2,1)S(1)}, u32[]{:S(2)}, u32[]{:S(2)}) collective-permute-start(bf16[512,256]{1,0:T(8,128)(2,1)S(1)} %fusion.1), channel_id=1, source_target_pairs={{0,20},{1,21},{2,22},{3,23},{4,16},{5,17},{6,18},{7,19},{8,28},{9,... | collective-permute-start | bytes 786440 | tf_op jit(solution)/shard_map/ppermute | solution.py:32
  93.0 19.8 %copy-start.21 = (bf16[2,512,128]{2,1,0:T(8,128)(2,1)}, bf16[2,512,128]{2,1,0:T(8,128)(2,1)S(1)}, u32[]{:S(2)}) copy-start(bf16[2,512,128]{2,1,0:T(8,128)(2,1)S(1)} %collective-permute-done.14.refs_10_) | copy-start | bytes 786436
  93.0 19.8 %collective-permute-start.23 = (bf16[2,256,32]{2,1,0:T(8,128)(2,1)S(1)}, bf16[2,256,32]{2,1,0:T(8,128)(2,1)S(1)}, u32[]{:S(2)}, u32[]{:S(2)}) collective-permute-start(bf16[2,256,32]{2,1,0:T(8,128)(2,1)S(1)} %get-tuple-element.85), channel_id=1, source_target_pairs={{0,8},{1,9},{2,10},{3,11},{4,12},{5,13},{6,14},{7,15},{8,0},{9,1},... | collective-permute-start | bytes 98312 | tf_op jit(solution)/shard_map/ppermute | solution.py:22
  102.0 4.1 %copy-start.30 = (bf16[512,256]{1,0:T(8,128)(2,1)}, bf16[512,256]{1,0:T(8,128)(2,1)S(1)}, u32[]{:S(2)}) copy-start(bf16[512,256]{1,0:T(8,128)(2,1)S(1)} %collective-permute-done.16.refs_0_) | copy-start | bytes 786436
  106.1 7.3 %copy-start.31 = (bf16[512,256]{1,0:T(8,128)(2,1)}, bf16[512,256]{1,0:T(8,128)(2,1)S(1)}, u32[]{:S(2)}) copy-start(bf16[512,256]{1,0:T(8,128)(2,1)S(1)} %collective-permute-done.17.refs_1_) | copy-start | bytes 786436
  106.1 4.8 %copy-start.13 = (bf16[4,512,128]{2,1,0:T(8,128)(2,1)}, bf16[4,512,128]{2,1,0:T(8,128)(2,1)S(1)}, u32[]{:S(2)}) copy-start(bf16[4,512,128]{2,1,0:T(8,128)(2,1)S(1)} %collective-permute-done.13.refs_18_) | copy-start | bytes 1572868
  106.1 5.0 %copy-start.15 = (bf16[4,512,128]{2,1,0:T(8,128)(2,1)}, bf16[4,512,128]{2,1,0:T(8,128)(2,1)S(1)}, u32[]{:S(2)}) copy-start(bf16[4,512,128]{2,1,0:T(8,128)(2,1)S(1)} %collective-permute-done.12.refs_15_) | copy-start | bytes 1572868
  106.1 5.0 %collective-permute-start.19 = (f32[32,1024]{1,0:T(8,128)S(1)}, f32[32,1024]{1,0:T(8,128)S(1)}, u32[]{:S(2)}, u32[]{:S(2)}) collective-permute-start(f32[32,1024]{1,0:T(8,128)S(1)} %add.85), channel_id=1, source_target_pairs={{0,2},{1,3},{2,0},{3,1},{4,6},{5,7},{6,4},{7,5},{8,10},{9,11},{10,... | collective-permute-start | bytes 393224 | tf_op jit(solution)/shard_map/ppermute | solution.py:22
  107.7 9.7 %collective-permute-start.21 = (bf16[512,128]{1,0:T(8,128)(2,1)}, bf16[512,128]{1,0:T(8,128)(2,1)}, u32[]{:S(2)}, u32[]{:S(2)}) collective-permute-start(bf16[512,128]{1,0:T(8,128)(2,1)} %fusion.2), channel_id=1, source_target_pairs={{0,20},{1,21},{2,22},{3,23},{4,16},{5,17},{6,18},{7,19},{8,28},{9,... | collective-permute-start | bytes 393224 | tf_op jit(solution)/shard_map/ppermute | solution.py:32
  107.7 9.7 %collective-permute-start.22 = (bf16[512,128]{1,0:T(8,128)(2,1)}, bf16[512,128]{1,0:T(8,128)(2,1)}, u32[]{:S(2)}, u32[]{:S(2)}) collective-permute-start(bf16[512,128]{1,0:T(8,128)(2,1)} %fusion.3), channel_id=1, source_target_pairs={{0,20},{1,21},{2,22},{3,23},{4,16},{5,17},{6,18},{7,19},{8,28},{9,... | collective-permute-start | bytes 393224 | tf_op jit(solution)/shard_map/ppermute | solution.py:32
  110.2 12.7 %collective-permute-start.25 = (bf16[2,512,128]{2,1,0:T(8,128)(2,1)}, bf16[2,512,128]{2,1,0:T(8,128)(2,1)}, u32[]{:S(2)}, u32[]{:S(2)}) collective-permute-start(bf16[2,512,128]{2,1,0:T(8,128)(2,1)} %add_convert_fusion.2), channel_id=1, source_target_pairs={{0,4},{1,5},{2,6},{3,7},{4,0},{5,1},{6,2},{7,3},{8,12},{9,13},{10,... | collective-permute-start | bytes 786440 | tf_op jit(solution)/shard_map/ppermute | solution.py:22
  111.2 14.8 %collective-permute-start.24 = (bf16[2,512,128]{2,1,0:T(8,128)(2,1)}, bf16[2,512,128]{2,1,0:T(8,128)(2,1)}, u32[]{:S(2)}, u32[]{:S(2)}) collective-permute-start(bf16[2,512,128]{2,1,0:T(8,128)(2,1)} %add_convert_fusion.3), channel_id=1, source_target_pairs={{0,2},{1,3},{2,0},{3,1},{4,6},{5,7},{6,4},{7,5},{8,10},{9,11},{10,... | collective-permute-start | bytes 786440 | tf_op jit(solution)/shard_map/ppermute | solution.py:22
  112.8 15.0 %copy-start.24 = (bf16[32,1024]{1,0:T(8,128)(2,1)}, bf16[32,1024]{1,0:T(8,128)(2,1)S(1)}, u32[]{:S(2)}) copy-start(bf16[32,1024]{1,0:T(8,128)(2,1)S(1)} %add_convert_fusion.12.refs_0_) | copy-start | bytes 196612
  112.8 7.5 %collective-permute-start.20 = (bf16[32,1024]{1,0:T(8,128)(2,1)S(1)}, bf16[32,1024]{1,0:T(8,128)(2,1)S(1)}, u32[]{:S(2)}, u32[]{:S(2)}) collective-permute-start(bf16[32,1024]{1,0:T(8,128)(2,1)S(1)} %add_convert_fusion.12.refs_0_), channel_id=1, source_target_pairs={{0,8},{1,9},{2,10},{3,11},{4,12},{5,13},{6,14},{7,15},{8,0},{9,1},... | collective-permute-start | bytes 196616 | tf_op jit(solution)/shard_map/ppermute | solution.py:22
  113.5 14.3 %copy-start.26 = (s32[1,2,4]{2,1,0:T(2,128)S(1)}, s32[1,2,4]{2,1,0:T(2,128)}, u32[]{:S(2)}) copy-start(s32[1,2,4]{2,1,0:T(2,128)} %param.14) | copy-start | bytes 100
  113.5 14.3 %copy-start.27 = (s32[1,2]{1,0:T(1,128)S(1)}, s32[1,2]{1,0:T(1,128)}, u32[]{:S(2)}) copy-start(s32[1,2]{1,0:T(1,128)} %param.15) | copy-start | bytes 28
  120.3 23.5 %copy-start.25 = (bf16[32,1024]{1,0:T(8,128)(2,1)}, bf16[32,1024]{1,0:T(8,128)(2,1)S(1)}, u32[]{:S(2)}) copy-start(bf16[32,1024]{1,0:T(8,128)(2,1)S(1)} %collective-permute-done.20.refs_1_) | copy-start | bytes 196612
  124.6 23.0 %collective-permute-start.28 = (bf16[512,128]{1,0:T(8,128)(2,1)}, bf16[512,128]{1,0:T(8,128)(2,1)}, u32[]{:S(2)}, u32[]{:S(2)}) collective-permute-start(bf16[512,128]{1,0:T(8,128)(2,1)} %fusion.5), channel_id=1, source_target_pairs={{0,17},{1,16},{2,19},{3,18},{4,21},{5,20},{6,23},{7,22},{8,25},{9,... | collective-permute-start | bytes 393224 | tf_op jit(solution)/shard_map/ppermute | solution.py:32
  127.7 19.8 %collective-permute-start.27 = (bf16[512,128]{1,0:T(8,128)(2,1)}, bf16[512,128]{1,0:T(8,128)(2,1)}, u32[]{:S(2)}, u32[]{:S(2)}) collective-permute-start(bf16[512,128]{1,0:T(8,128)(2,1)} %fusion.4), channel_id=1, source_target_pairs={{0,20},{1,21},{2,22},{3,23},{4,16},{5,17},{6,18},{7,19},{8,28},{9,... | collective-permute-start | bytes 393224 | tf_op jit(solution)/shard_map/ppermute | solution.py:32
  127.7 1.2 copy-start.2
  129.0 1.2 copy-start.4
  130.2 1.2 copy-start.6
  131.4 1.2 copy-start.8
  132.6 1.0 copy-start.10
  133.7 1.0 copy-start.12
  134.7 1.0 copy-start.14
  135.8 1.0 copy-start.16
  136.8 1.0 copy-start.18
  137.8 1.0 copy-start.20
  139.8 1.0 copy-start.23
  143.8 3.7 %collective-permute-start.26 = (bf16[512,1024]{1,0:T(8,128)(2,1)}, bf16[512,1024]{1,0:T(8,128)(2,1)S(1)}, u32[]{:S(2)}, u32[]{:S(2)}) collective-permute-start(bf16[512,1024]{1,0:T(8,128)(2,1)} %shard_map.107), channel_id=1, source_target_pairs={{0,16},{1,17},{2,18},{3,19},{4,20},{5,21},{6,22},{7,23},{8,24},{9,... | collective-permute-start | bytes 3145736 | tf_op jit(solution)/shard_map/ppermute | solution.py:32
  (5 other events, 4.3 us)

commit v7 on v6

--- a/solution.py
+++ b/solution.py
@@ -100,7 +100,7 @@
                 to_y[0][to_y[1] + to_y[2] * z] = value[:, half - start :].astype(to_y[0].dtype)
 
 
-def product(scalars, grads, pieces, weight_blocks, up_tile, low_size, turns, sends, keeps):
+def product(scalars, grads, pieces, weight_blocks, up_tile, low_size, turns, sends, keeps, cost):
     blocks, width, depth = weight_blocks.shape
     tile_rows = grads[0].shape[1]
     rows = len(pieces) * pieces[0][3]
@@ -121,7 +121,7 @@
         ),
         in_specs=[SMEM] * 3
         + [VMEM] * len(grads)
-        + [pl.BlockSpec(memory_space=pl.ANY)]
+        + [pl.BlockSpec(memory_space=pltpu.HBM)]
         + [VMEM] * keeps,
         out_specs=[VMEM] * len(outs),
         out_shape=outs,
@@ -130,13 +130,39 @@
             pltpu.VMEM(weight_blocks.shape, BF16),
             pltpu.SemaphoreType.DMA((blocks,)),
         ],
-        compiler_params=pltpu.CompilerParams(vmem_limit_bytes=56 * 2**20),
-        cost_estimate=LONG if keeps else QUICK,
-    )(*scalars, *grads, weight_blocks, *([up_tile] * keeps))
+        compiler_params=pltpu.CompilerParams(vmem_limit_bytes=24 * 2**20),
+        cost_estimate=cost,
+    )(*in_hbm(*scalars), *grads, *in_hbm(weight_blocks), *in_hbm(*[up_tile] * keeps))
+
+
+def in_hbm(*arrays):
+    return [pltpu.with_memory_space_constraint(array, pltpu.HBM) for array in arrays]
 
 
 def after(value, *others):
     return lax.optimization_barrier((value, *others))[0]
+
+
+def halve_kernel(*refs):
+    ways = len(refs) // 4
+    for way in range(ways):
+        kept_ref, got_ref, sent_ref, rest_ref = refs[way::ways]
+        half = kept_ref.shape[0] // 2
+        sent_ref[...] = (kept_ref[half:] + got_ref[half:].astype(F32)).astype(BF16)
+        rest_ref[...] = kept_ref[:half] + got_ref[:half].astype(F32)
+
+
+def halve(kept, got):
+    shapes = [(k.shape[0] // 2,) + k.shape[1:] for k in kept]
+    outs = pl.pallas_call(
+        halve_kernel,
+        in_specs=[VMEM] * (2 * len(kept)),
+        out_specs=[VMEM] * (2 * len(kept)),
+        out_shape=[jax.ShapeDtypeStruct(s, dtype) for dtype in (BF16, F32) for s in shapes],
+        compiler_params=pltpu.CompilerParams(vmem_limit_bytes=24 * 2**20),
+        cost_estimate=QUICK,
+    )(*kept, *got)
+    return outs[: len(kept)], outs[len(kept) :]
 
 
 def up_body(low_size, tile_rows, pieces, tiles, *refs):
@@ -199,9 +225,9 @@
 
     own_pieces = [(0, m, (0, m, o), size) for m in range(micro_count) for o in offsets]
 
-    def produce(grads, pieces, turns, sends, keeps):
+    def produce(grads, pieces, turns, sends, keeps, cost):
         return product(
-            scalars, grads, pieces, weight_blocks, up_tile, low_size, turns, sends, keeps
+            scalars, grads, pieces, weight_blocks, up_tile, low_size, turns, sends, keeps, cost
         )
 
     hidden = saved_rank_outputs[0]
@@ -213,76 +239,67 @@
             upper, jnp.concatenate([got, hidden], 1), jnp.concatenate([hidden, got], 1)
         )
 
-    def second_part(kept, got):
-        return (kept[2:] + got[2:]).astype(BF16)
-
-    first_rows, hidden = lax.optimization_barrier((grad_tile[0], hidden))
+    first_rows = lax.optimization_barrier(grad_tile[0])
     got0 = [partner(first_rows, k * low_size)[None] for k in range(1, high_size)]
-    hidden = spread_hidden(hidden, 0)
-    own_grads = after(grad_tile, first_rows)
-    sent_x, sent_y = produce([own_grads], own_pieces, False, True, False)
+    (own_grads,) = in_hbm(after(grad_tile, first_rows))
+    sent_x, sent_y = produce([own_grads], own_pieces, False, True, False, QUICK)
     first_x, first_y = partner(sent_x, 1), partner(sent_y, 2)
+    hidden = spread_hidden(after(hidden, sent_x, sent_y), 0)
     rows0 = after(got0[0], sent_x, sent_y), *got0[1:]
     c_sent_x, c_sent_y, c_kept_x, c_kept_y, part = produce(
-        list(rows0), pieces_of(0), False, True, True
+        list(rows0), pieces_of(0), False, True, True, LONG
     )
     parts = [part]
-    own_kept = produce([after(grad_tile, part)], own_pieces, False, False, True)
-    kept_x, kept_y, part = own_kept
+    (own_grads,) = in_hbm(after(grad_tile, part))
+    kept_x, kept_y, part = produce([own_grads], own_pieces, False, False, True, LONG)
     parts.insert(0, part)
     got1 = send_rows(after(grad_tile, *got0), 1)
 
-    slot = first_x, first_y
-    c_first_x, c_first_y = partner(after(c_sent_x, *slot), 1), partner(after(c_sent_y, *slot), 2)
-    second_x = partner(second_part(kept_x, first_x), 2)
-    second_y = partner(second_part(kept_y, first_y), 1)
-    hidden = spread_hidden(after(hidden, *slot), 1)
-    own_sums = (kept_x, first_x, second_x), (kept_y, first_y, second_y)
+    (sent_x, sent_y), (kept_x, kept_y) = halve((kept_x, kept_y), (first_x, first_y))
+    second_x, second_y = partner(sent_x, 2), partner(sent_y, 1)
+    c_first_x = partner(after(c_sent_x, sent_x, sent_y), 1)
+    c_first_y = partner(after(c_sent_y, sent_x, sent_y), 2)
+    hidden = spread_hidden(after(hidden, sent_x, sent_y), 1)
+    own_sums = (kept_x, second_x), (kept_y, second_y)
+
+    def third_part(two):
+        kept, second = two
+        return (kept[1] + second[1]).astype(BF16)
 
     chunks = [([grad_tile], own_pieces), (got0, pieces_of(0)), (got1, pieces_of(1))]
     order = [piece for _, pieces in chunks for _, _, piece, _ in pieces]
     rows1 = after(got1[0], part), *got1[1:]
     d_sent_x, d_sent_y, d_kept_x, d_kept_y, part = produce(
-        list(rows1), pieces_of(1), True, True, True
+        list(rows1), pieces_of(1), True, True, True, LONG
     )
     parts.append(part)
-    slot = c_first_x, c_first_y, second_x, second_y, hidden
+    own_last = [relay(third_part(two), 4) for two in own_sums]
+    slot = c_first_x, c_first_y, second_x, second_y
     own_rank = after(jnp.concatenate(parts, 1), *slot)
     own_rank = own_rank + partner(own_rank, 1)
     d_first_x = partner(after(d_sent_x, *slot), 1)
     d_first_y = partner(after(d_sent_y, *slot), 2)
-    c_second_x = partner(second_part(c_kept_x, c_first_x), 2)
-    c_second_y = partner(second_part(c_kept_y, c_first_y), 1)
-    c_sums = (c_kept_x, c_first_x, c_second_x), (c_kept_y, c_first_y, c_second_y)
-
-    def third_part(three):
-        kept, got, second = three
-        return (kept[1] + got[1] + second[1]).astype(BF16)
-
-    own_rank = own_rank + partner(own_rank, 4)
-    own_last = [relay(after(third_part(three), own_rank), 4) for three in own_sums]
-    hidden = spread_hidden(hidden, 2)
-
-    slot = d_first_x, d_first_y, c_second_x, c_second_y, *own_last, own_rank, hidden
+    (c_sent_x, c_sent_y), c_kept = halve((c_kept_x, c_kept_y), (c_first_x, c_first_y))
+    c_second_x, c_second_y = partner(c_sent_x, 2), partner(c_sent_y, 1)
+    c_sums = (c_kept[0], c_second_x), (c_kept[1], c_second_y)
+    own_rank = own_rank + partner(after(own_rank, *own_last), 4)
+    hidden = spread_hidden(after(hidden, own_rank), 2)
+
+    slot = d_first_x, d_first_y, c_second_x, c_second_y, own_rank
     own_rank = after(own_rank, *slot)
     own_rank = (own_rank + partner(own_rank, 2)).astype(BF16)
-    d_second_x = partner(second_part(d_kept_x, after(d_first_x, *slot)), 2)
-    d_second_y = partner(second_part(d_kept_y, after(d_first_y, *slot)), 4)
-    d_sums = (d_kept_x, d_first_x, d_second_x), (d_kept_y, d_first_y, d_second_y)
-    c_last = [relay(after(third_part(three), *slot), 4) for three in c_sums]
+    (d_sent_x, d_sent_y), d_kept = halve(
+        (d_kept_x, d_kept_y), (after(d_first_x, *slot), after(d_first_y, *slot))
+    )
+    d_second_x, d_second_y = partner(d_sent_x, 2), partner(d_sent_y, 4)
+    d_sums = (d_kept[0], d_second_x), (d_kept[1], d_second_y)
+    c_last = [relay(after(third_part(two), *slot), 4) for two in c_sums]
+    ranks = [own_rank] + [partner(own_rank, j * low_size) for j in range(1, high_size)]
     hiddens = []
     for k in range(high_size):
         wanted = lax.dynamic_slice_in_dim(hidden, (high ^ k) * rank_part, rank_part, 2)
+        wanted = after(wanted, ranks[-1])
         hiddens.append(partner(wanted, k * low_size) if k > 0 else wanted)
-    ranks = [own_rank] + [partner(own_rank, j * low_size) for j in range(1, high_size)]
-
-    d_last = [
-        relay(third_part((d_kept_x, d_first_x, after(d_second_x, c_last[1]))), 4),
-        relay(third_part((d_kept_y, d_first_y, after(d_second_y, c_last[1]))), 1),
-    ]
-    ranks[-1] = after(ranks[-1], *c_last, *hiddens)
-    sums = own_sums + c_sums + d_sums
-    got_last = own_last + c_last + d_last
 
     all_grads, all_pieces = [], []
     for grads, pieces in chunks:
@@ -295,7 +312,7 @@
         out_shape=jax.ShapeDtypeStruct(up_tile.shape, BF16),
         scratch_shapes=[pltpu.VMEM(up_tile.shape, F32)],
         cost_estimate=LONG,
-    )(*scalars, *all_grads, *hiddens)
+    )(*in_hbm(*scalars), *all_grads, *hiddens)
 
     def columns_of(j, piece):
         k, m, offset = piece
@@ -304,19 +321,22 @@
 
     down_parts = adapter_down_maps[0].reshape(class_count, high_size, rank_part, portion)
 
-    def adapter_kernel(pos_ref, classes_ref, live_ref, down_ref, *refs):
-        rank_refs, sum_refs = refs[:high_size], refs[high_size:-2]
-        out_ref, total_ref = refs[-2:]
+    def adapter_kernel(first, with_last, groups, *refs):
+        pos_ref, classes_ref, _, down_ref = refs[:4]
+        rank_refs = refs[4 : 4 + high_size]
+        sum_refs = refs[4 + high_size : 4 + high_size + 2 * groups]
+        *last_refs, out_ref, total_ref = refs[4 + high_size + 2 * groups :]
         own = pos_ref[0] // low_size
         start = 0
-        for g in range(len(sums)):
-            kept_ref, got_ref, second_ref = sum_refs[3 * g : 3 * g + 3]
+        for g in range(groups):
+            kept_ref, second_ref = sum_refs[2 * g : 2 * g + 2]
             count = kept_ref.shape[2]
-            total_ref[:, start : start + count] = (
-                kept_ref[0] + got_ref[0].astype(F32) + second_ref[0].astype(F32)
-            )
+            total_ref[:, start : start + count] = kept_ref[0] + second_ref[0].astype(F32)
+            if with_last:
+                last_refs[g][...] = (kept_ref[1] + second_ref[1].astype(F32)).astype(BF16)
             start += count
-        for at, piece in enumerate(order):
+        for at in range(start // size):
+            piece = order[first + at]
             seg = segment_of(own, piece, tile_rows)
             rows = slice(at * size, (at + 1) * size)
             adapter = total_ref[:, rows]
@@ -329,23 +349,24 @@
                 )
             out_ref[:, rows] = adapter.astype(BF16)
 
-    rows_total = len(order) * size
-    kept = pl.pallas_call(
-        adapter_kernel,
-        grid=(1,),
-        in_specs=[SMEM] * 3
-        + [pl.BlockSpec(a.shape, lambda _, n=a.ndim: (0,) * n) for a in [down_parts, *ranks]]
-        + [pl.BlockSpec((1,) + a.shape[1:], lambda _: (0, 0, 0)) for three in sums for a in three],
-        out_specs=pl.BlockSpec((portion, rows_total), lambda _: (0, 0)),
-        out_shape=jax.ShapeDtypeStruct((portion, rows_total), BF16),
-        scratch_shapes=[pltpu.VMEM((portion, rows_total), F32)],
-        compiler_params=pltpu.CompilerParams(vmem_limit_bytes=40 * 2**20),
-        cost_estimate=QUICK,
-    )(*scalars, down_parts, *ranks, *[a for three in sums for a in three])
-    kept = relay(kept, 0)
-
-    def finish_kernel(pos_ref, kept_ref, *refs):
-        *got_refs, out_ref, total_ref = refs
+    def with_adapter(sums, first, with_last):
+        counts = [kept.shape[2] for kept, _ in sums]
+        shapes = [(portion, n) for n in counts] * with_last + [(portion, sum(counts))]
+        outs = pl.pallas_call(
+            functools.partial(adapter_kernel, first, with_last, len(sums)),
+            in_specs=[SMEM] * 3 + [VMEM] * (1 + high_size + 2 * len(sums)),
+            out_specs=[VMEM] * len(shapes),
+            out_shape=[jax.ShapeDtypeStruct(shape, BF16) for shape in shapes],
+            scratch_shapes=[pltpu.VMEM(shapes[-1], F32)],
+            compiler_params=pltpu.CompilerParams(vmem_limit_bytes=24 * 2**20),
+            cost_estimate=QUICK,
+        )(*in_hbm(*scalars), *in_hbm(down_parts), *ranks, *[a for two in sums for a in two])
+        return outs[:-1], outs[-1]
+
+    def finish_kernel(first, groups, *refs):
+        pos_ref, kept_ref = refs[:2]
+        got_refs = refs[2 : 2 + groups]
+        out_ref, total_ref, turned_ref, sem = refs[-4:]
         own = pos_ref[0] // low_size
         start = 0
         for got_ref in got_refs:
@@ -354,17 +375,47 @@
                 kept_ref[:, start : start + count].astype(F32) + got_ref[...].astype(F32)
             ).astype(BF16)
             start += count
-        for at, (k, m, offset) in enumerate(order):
+        copies = []
+        for at in range(start // size):
+            k, m, offset = order[first + at]
             base = pl.multiple_of((own ^ k) * tile_rows + offset, size)
-            out_ref[m, pl.ds(base, size), :] = total_ref[:, at * size : (at + 1) * size].T
-
-    grad_prev = pl.pallas_call(
-        finish_kernel,
-        in_specs=[SMEM] + [VMEM] * (1 + len(got_last)),
-        out_specs=VMEM,
-        out_shape=jax.ShapeDtypeStruct((micro_count, high_size * tile_rows, portion), BF16),
-        scratch_shapes=[pltpu.VMEM((portion, rows_total), BF16)],
-    )(scalars[0], kept, *got_last)
+            rows = slice(at * size, (at + 1) * size)
+            turned_ref[rows, :] = total_ref[:, rows].T
+            copies.append(
+                pltpu.make_async_copy(
+                    turned_ref.at[rows, :], out_ref.at[m, pl.ds(base, size), :], sem.at[at]
+                )
+            )
+            copies[-1].start()
+        for copy in copies:
+            copy.wait()
+
+    def finish(kept, got, first, result):
+        rows = kept.shape[1]
+        shape = jax.ShapeDtypeStruct((micro_count, high_size * tile_rows, portion), BF16)
+        hbm = pl.BlockSpec(memory_space=pltpu.HBM)
+        before = [] if result is None else [result]
+        return pl.pallas_call(
+            functools.partial(finish_kernel, first, len(got)),
+            in_specs=[SMEM] + [VMEM] * (1 + len(got)) + [hbm] * len(before),
+            out_specs=hbm,
+            out_shape=shape,
+            input_output_aliases={2 + len(got): 0} if before else {},
+            scratch_shapes=[
+                pltpu.VMEM((portion, rows), BF16),
+                pltpu.VMEM((rows, portion), BF16),
+                pltpu.SemaphoreType.DMA((rows // size,)),
+            ],
+            cost_estimate=QUICK,
+        )(*in_hbm(scalars[0]), kept, *got, *before)
+
+    _, kept = with_adapter(own_sums + c_sums, 0, False)
+    early = relay(kept, 0)
+    d_lasts, d_kept = with_adapter(d_sums, kept.shape[1] // size, True)
+    d_last = [relay(d_lasts[0], 4), relay(d_lasts[1], 1)]
+    d_kept = relay(d_kept, 0)
+    grad_prev = finish(early, own_last + c_last, 0, None)
+    grad_prev = finish(d_kept, d_last, kept.shape[1] // size, grad_prev)
 
     def down_kernel(pos_ref, classes_ref, live_ref, inputs_ref, *refs):
         rank_refs, out_ref, total_ref = refs[:-2], refs[-2], refs[-1]
@@ -392,7 +443,7 @@
         out_shape=jax.ShapeDtypeStruct(down_parts.shape, BF16),
         scratch_shapes=[pltpu.VMEM(down_parts.shape, F32)],
         cost_estimate=LONG,
-    )(*scalars, forward_input[0], *ranks)
+    )(*in_hbm(*scalars, forward_input[0]), *ranks)
 
     return (
         grad_prev[None],

time: 153 us -> 133 us (0.87)
  waiting for transfers between devices: 48.6 us -> 34.7 us
  starting transfers between devices: 28.2 us -> 37.6 us
  other arithmetic: 13.4 us -> 4.84 us
  local copies, waits for them, and re-layouts: 17.9 us -> 11.9 us
    ppermute x7 -> x8, waiting for transfers between devices: 12.4 us -> 0.04 us  [relay(): return lax.ppermute(value, ('pipe', 'tensor'), pairs)]
    ppermute x22, starting transfers between devices: 22.8 us -> 33.3 us  [partner(): return lax.ppermute(value, 'tensor', pairs)]
    convert_element_type x12 -> x4, other arithmetic: 12.3 us -> 2.96 us  [third_part(): return (kept[1] + second[1]).astype(BF16)]
    unnamed x80 -> x62, local copies, waits for them, and re-layouts: 16 us -> 10 us
    pallas_call x2 -> x7, Pallas kernels: 6.01 us -> 11.9 us  [the longest x2 4.31 us: finish(): pl.pallas_call(functools.partial(finish_kernel, first, len(got)), in_spec...]
    pallas_call x4, Pallas kernels: 29.4 us -> 24 us  [product(): pl.pallas_call(functools.partial(product_body, low_size, tile_rows, piece...]
    ppermute x22, waiting for transfers between devices: 36.2 us -> 34.6 us  [partner(): return lax.ppermute(value, 'tensor', pairs)]
    ppermute x7 -> x8, starting transfers between devices: 5.35 us -> 4.33 us  [relay(): return lax.ppermute(value, ('pipe', 'tensor'), pairs)]
  transfers between devices with their start and end apart: 29 -> 30, of which waited for: 10 -> 10; matrix products, arithmetic and copies ran while one was open for 9% -> 4% of each run, Pallas kernels for 26% -> 30%
where the time goes in v7:
time: 133 us; the launch traced here: 132 us
  Pallas kernels  41.6 us (31%)
  starting transfers between devices  37.6 us (28%)
  waiting for transfers between devices  34.7 us (26%)
  local copies, waits for them, and re-layouts  11.9 us (9%)
  other arithmetic  4.84 us (4%)
    ppermute x22, waiting for transfers between devices, partner(): return lax.ppermute(value, 'tensor', pairs)  34.6 us
    ppermute x22, starting transfers between devices, partner(): return lax.ppermute(value, 'tensor', pairs)  33.3 us
    pallas_call x4, Pallas kernels, product(): pl.pallas_call(functools.partial(product_body, low_size, tile_rows, piece...  24 us
    unnamed x62, local copies, waits for them, and re-layouts  10 us
    ppermute x8, starting transfers between devices, relay(): return lax.ppermute(value, ('pipe', 'tensor'), pairs)  4.33 us
    pallas_call x2, Pallas kernels, finish(): pl.pallas_call(functools.partial(finish_kernel, first, len(got)), in_spec...  4.31 us
    pallas_call x2, Pallas kernels, with_adapter(): pl.pallas_call(functools.partial(adapter_kernel, first, with_last, len(su...  4.23 us
    pallas_call x3, Pallas kernels, halve(): pl.pallas_call(halve_kernel, in_specs=[VMEM] * (2 * len(kept)), out_specs...  3.32 us
  transfers between devices with their start and end apart: 30, of which 10 were waited for; matrix products, arithmetic and copies ran while one was open for 4% of the time, Pallas kernels for 30%

profile of v7, /device:TPU:0, one launch (start us, length us, event | category | flops | bytes accessed | tf_op | source)
XLA Modules:
  0.0 131.6 jit_solution(7351126143231867529)
XLA Ops:
  0.6 1.1 slice_bitcast_fusion.1
  1.7 4.1 %collective-permute-start = (bf16[256,1024]{1,0:T(8,128)(2,1)S(1)}, bf16[256,1024]{1,0:T(8,128)(2,1)S(1)}, u32[]{:S(2)}, u32[]{:S(2)}) collective-permute-start(bf16[256,1024]{1,0:T(8,128)(2,1)S(1)} %slice_bitcast_fusion.1), channel_id=1, source_target_pairs={{0,8},{1,9},{2,10},{3,11},{4,12},{5,13},{6,14},{7,15},{8,0},{9,1},... | collective-permute-start | bytes 1572872 | tf_op jit(solution)/shard_map/ppermute | solution.py:22
  5.8 5.8 %shard_map.103 = (bf16[4,512,256]{2,1,0:T(8,128)(2,1)S(1)}, bf16[4,512,256]{2,1,0:T(8,128)(2,1)S(1)}) custom-call(s32[1]{0:T(128)} %bitcast.refs_0_.pos_ref, s32[2,4]{1,0:T(2,128)} %bitcast.46, s32[2]{0:T(128)} %bitcast.54, bf16[2,256,1024]{2,1,0:T(8,128)(2,1)} %bitcast.37, bf16[8,512,1024]{2,1,0:T(8,128)(2,1)} %bitcast.33), custom_call_target="tpu_custom_call" | custom-call | flops 1000 | bytes 1000 | tf_op jit(solution)/shard_map/pallas_call | solution.py:118
  11.6 1.6 %collective-permute-start.26 = (bf16[2,32,64]{2,1,0:T(8,128)(2,1)S(1)}, bf16[2,32,64]{2,1,0:T(8,128)(2,1)S(1)}, u32[]{:S(2)}, u32[]{:S(2)}) collective-permute-start(bf16[2,32,64]{2,1,0:T(8,128)(2,1)S(1)} %bitcast.44), channel_id=1, source_target_pairs={{0,1},{1,0},{2,3},{3,2},{4,5},{5,4},{6,7},{7,6},{8,9},{9,8},{10,11... | collective-permute-start | bytes 24584 | tf_op jit(solution)/shard_map/ppermute | solution.py:22
  13.2 0.5 collective-permute-start.2
  13.7 1.5 %collective-permute-start.3 = (bf16[4,512,256]{2,1,0:T(8,128)(2,1)S(1)}, bf16[4,512,256]{2,1,0:T(8,128)(2,1)S(1)}, u32[]{:S(2)}, u32[]{:S(2)}) collective-permute-start(bf16[4,512,256]{2,1,0:T(8,128)(2,1)S(1)} %get-tuple-element.62), channel_id=1, source_target_pairs={{0,2},{1,3},{2,0},{3,1},{4,6},{5,7},{6,4},{7,5},{8,10},{9,11},{10,... | collective-permute-start | bytes 3145736 | tf_op jit(solution)/shard_map/ppermute | solution.py:22
  15.6 13.3 %collective-permute-done = bf16[256,1024]{1,0:T(8,128)(2,1)S(1)} collective-permute-done((bf16[256,1024]{1,0:T(8,128)(2,1)S(1)}, bf16[256,1024]{1,0:T(8,128)(2,1)S(1)}, u32[]{:S(2)}, u32[]{:S(2)}) %collective-permute-start) | collective-permute-done | bytes 524320 | tf_op jit(solution)/shard_map/ppermute | solution.py:22
  29.1 5.9 %shard_map.104 = (bf16[4,512,128]{2,1,0:T(8,128)(2,1)S(1)}, bf16[4,512,128]{2,1,0:T(8,128)(2,1)S(1)}, f32[4,512,128]{2,1,0:T(8,128)S(1)}, f32[4,512,128]{2,1,0:T(8,128)S(1)}, f32[32,256]{1,0:T(8,128)S(1)}) custom-call(s32[1]{0:T(128)} %bitcast.refs_0_.pos_ref, s32[2,4]{1,0:T(2,128)} %bitcast.47, s32[2]{0:T(128)} %bitcast.55, ...), custom_call_target="tpu_custom_call" | custom-call | flops 40000000000 | bytes 1000 | tf_op jit(solution)/shard_map/pallas_call | solution.py:118
  35.0 5.8 %shard_map.105 = (f32[4,512,256]{2,1,0:T(8,128)S(1)}, f32[4,512,256]{2,1,0:T(8,128)S(1)}, f32[32,512]{1,0:T(8,128)S(1)}) custom-call(s32[1]{0:T(128)} %bitcast.refs_0_.pos_ref, s32[2,4]{1,0:T(2,128)} %bitcast.48, s32[2]{0:T(128)} %bitcast.56, bf16[2,256,1024]{2,1,0:T(8,128)(2,1)} %bitcast.38, bf16[8,512,1024]{2,1,0:T(8,128)(2,1)} %bitcast.35, ...), custom_call_target="tpu_custom_call" | custom-call | flops 40000000000 | bytes 1000 | tf_op jit(solution)/shard_map/pallas_call | solution.py:118
  41.3 1.6 %collective-permute-start.6 = (bf16[2,512,256]{2,1,0:T(8,128)(2,1)S(1)}, bf16[2,512,256]{2,1,0:T(8,128)(2,1)S(1)}, u32[]{:S(2)}, u32[]{:S(2)}) collective-permute-start(bf16[2,512,256]{2,1,0:T(8,128)(2,1)S(1)} %get-tuple-element.73), channel_id=1, source_target_pairs={{0,2},{1,3},{2,0},{3,1},{4,6},{5,7},{6,4},{7,5},{8,10},{9,11},{10,... | collective-permute-start | bytes 1572872 | tf_op jit(solution)/shard_map/ppermute | solution.py:22
  42.9 1.5 %collective-permute-start.7 = (bf16[2,512,256]{2,1,0:T(8,128)(2,1)S(1)}, bf16[2,512,256]{2,1,0:T(8,128)(2,1)S(1)}, u32[]{:S(2)}, u32[]{:S(2)}) collective-permute-start(bf16[2,512,256]{2,1,0:T(8,128)(2,1)S(1)} %get-tuple-element.74), channel_id=1, source_target_pairs={{0,1},{1,0},{2,3},{3,2},{4,5},{5,4},{6,7},{7,6},{8,9},{9,8},{10,11... | collective-permute-start | bytes 1572872 | tf_op jit(solution)/shard_map/ppermute | solution.py:22
  44.4 9.9 %collective-permute-done.1 = bf16[256,1024]{1,0:T(8,128)(2,1)S(1)} collective-permute-done((bf16[256,1024]{1,0:T(8,128)(2,1)S(1)}, bf16[256,1024]{1,0:T(8,128)(2,1)S(1)}, u32[]{:S(2)}, u32[]{:S(2)}) %collective-permute-start.1) | collective-permute-done | bytes 524320 | tf_op jit(solution)/shard_map/ppermute | solution.py:22
  54.3 1.3 collective-permute-start.27
  55.6 1.5 %collective-permute-start.4 = (bf16[4,512,128]{2,1,0:T(8,128)(2,1)S(1)}, bf16[4,512,128]{2,1,0:T(8,128)(2,1)S(1)}, u32[]{:S(2)}, u32[]{:S(2)}) collective-permute-start(bf16[4,512,128]{2,1,0:T(8,128)(2,1)S(1)} %get-tuple-element.75), channel_id=1, source_target_pairs={{0,1},{1,0},{2,3},{3,2},{4,5},{5,4},{6,7},{7,6},{8,9},{9,8},{10,11... | collective-permute-start | bytes 1572872 | tf_op jit(solution)/shard_map/ppermute | solution.py:22
  57.1 0.5 collective-permute-start.5
  57.6 6.4 %shard_map.106 = (bf16[4,512,128]{2,1,0:T(8,128)(2,1)}, bf16[4,512,128]{2,1,0:T(8,128)(2,1)}, f32[4,512,128]{2,1,0:T(8,128)S(1)}, f32[4,512,128]{2,1,0:T(8,128)S(1)}, f32[32,256]{1,0:T(8,128)S(1)}) custom-call(s32[1]{0:T(128)} %bitcast.refs_0_.pos_ref, s32[2,4]{1,0:T(2,128)} %bitcast.49, s32[2]{0:T(128)} %bitcast.57, bf16[1,256,1024]{2,1,0:T(8,128)(2,1)S(1)} %bitcast.31, ...), custom_call_target="tpu_custom_call" | custom-call | flops 40000000000 | bytes 1000 | tf_op jit(solution)/shard_map/pallas_call | solution.py:118
  64.1 0.9 fusion
  64.9 2.3 %collective-permute-done.4.refs_2_ = bf16[4,512,128]{2,1,0:T(8,128)(2,1)S(1)} collective-permute-done((bf16[4,512,128]{2,1,0:T(8,128)(2,1)S(1)}, bf16[4,512,128]{2,1,0:T(8,128)(2,1)S(1)}, u32[]{:S(2)}, u32[]{:S(2)}) %collective-permute-start.4) | collective-permute-done | bytes 524320 | tf_op jit(solution)/shard_map/ppermute | solution.py:22
  67.2 1.6 %collective-permute-done.5.refs_3_ = bf16[4,512,128]{2,1,0:T(8,128)(2,1)S(1)} collective-permute-done((bf16[4,512,128]{2,1,0:T(8,128)(2,1)S(1)}, bf16[4,512,128]{2,1,0:T(8,128)(2,1)S(1)}, u32[]{:S(2)}, u32[]{:S(2)}) %collective-permute-start.5) | collective-permute-done | bytes 524320 | tf_op jit(solution)/shard_map/ppermute | solution.py:22
  68.8 0.5 collective-permute-start.8
  69.3 1.0 collective-permute-start.13
  70.4 0.9 collective-permute-start.12
  71.3 0.7 fusion.1
  72.1 0.8 collective-permute-start.10
  72.9 0.9 shard_map.108
  73.7 0.7 copy-done.21
  74.4 0.8 collective-permute-done.8
  75.2 0.7 copy-done.25
  75.9 0.5 collective-permute-start.14
  76.4 1.1 collective-permute-start.15
  77.5 0.9 maximum_select_fusion.1
  78.4 0.9 add.32
  79.3 3.5 %collective-permute-start.11 = (f32[32,1024]{1,0:T(8,128)S(1)}, f32[32,1024]{1,0:T(8,128)S(1)}, u32[]{:S(2)}, u32[]{:S(2)}) collective-permute-start(f32[32,1024]{1,0:T(8,128)S(1)} %add.32), channel_id=1, source_target_pairs={{0,4},{1,5},{2,6},{3,7},{4,0},{5,1},{6,2},{7,3},{8,12},{9,13},{10,... | collective-permute-start | bytes 393224 | tf_op jit(solution)/shard_map/ppermute | solution.py:22
  82.8 2.5 %collective-permute-done.14.refs_11_ = bf16[2,512,128]{2,1,0:T(8,128)(2,1)S(1)} collective-permute-done((bf16[2,512,128]{2,1,0:T(8,128)(2,1)}, bf16[2,512,128]{2,1,0:T(8,128)(2,1)S(1)}, u32[]{:S(2)}, u32[]{:S(2)}) %collective-permute-start.14) | collective-permute-done | bytes 262176 | tf_op jit(solution)/shard_map/ppermute | solution.py:22
  85.3 0.7 fusion.2
  86.0 0.8 collective-permute-done.11
  86.8 4.8 %collective-permute-start.28 = (bf16[2,128,64]{2,1,0:T(8,128)(2,1)S(1)}, bf16[2,128,64]{2,1,0:T(8,128)(2,1)S(1)}, u32[]{:S(2)}, u32[]{:S(2)}) collective-permute-start(bf16[2,128,64]{2,1,0:T(8,128)(2,1)S(1)} %maximum_select_fusion.1), channel_id=1, source_target_pairs={{0,4},{1,5},{2,6},{3,7},{4,0},{5,1},{6,2},{7,3},{8,12},{9,13},{10,... | collective-permute-start | bytes 98312 | tf_op jit(solution)/shard_map/ppermute | solution.py:22
  91.6 1.3 collective-permute-start.16
  92.9 0.7 fusion.3
  93.9 2.8 %collective-permute-done.16 = f32[32,1024]{1,0:T(8,128)S(1)} collective-permute-done((f32[32,1024]{1,0:T(8,128)S(1)}, f32[32,1024]{1,0:T(8,128)S(1)}, u32[]{:S(2)}, u32[]{:S(2)}) %collective-permute-start.16) | collective-permute-done | bytes 131104 | tf_op jit(solution)/shard_map/ppermute | solution.py:22
  96.7 1.4 %collective-permute-start.17 = (bf16[32,1024]{1,0:T(8,128)(2,1)S(1)}, bf16[32,1024]{1,0:T(8,128)(2,1)S(1)}, u32[]{:S(2)}, u32[]{:S(2)}) collective-permute-start(bf16[32,1024]{1,0:T(8,128)(2,1)S(1)} %add_convert_fusion.4.refs_4_.refs_0_), channel_id=1, source_target_pairs={{0,8},{1,9},{2,10},{3,11},{4,12},{5,13},{6,14},{7,15},{8,0},{9,1},... | collective-permute-start | bytes 196616 | tf_op jit(solution)/shard_map/ppermute | solution.py:22
  98.1 0.8 constant_dynamic-slice_fusion
  98.9 1.7 %collective-permute-start.25 = (bf16[512,128]{1,0:T(8,128)(2,1)}, bf16[512,128]{1,0:T(8,128)(2,1)}, u32[]{:S(2)}, u32[]{:S(2)}) collective-permute-start(bf16[512,128]{1,0:T(8,128)(2,1)} %fusion.3), channel_id=1, source_target_pairs={{0,20},{1,21},{2,22},{3,23},{4,16},{5,17},{6,18},{7,19},{8,28},{9,... | collective-permute-start | bytes 393224 | tf_op jit(solution)/shard_map/ppermute | solution.py:32
  100.7 2.1 %shard_map.109 = (bf16[2,512,128]{2,1,0:T(8,128)(2,1)}, bf16[2,512,128]{2,1,0:T(8,128)(2,1)}, f32[2,512,128]{2,1,0:T(8,128)S(1)}, f32[2,512,128]{2,1,0:T(8,128)S(1)}) custom-call(f32[4,512,128]{2,1,0:T(8,128)S(1)} %copy-done.5, f32[4,512,128]{2,1,0:T(8,128)S(1)} %copy-done.7, bf16[4,512,128]{2,1,0:T(8,128)(2,1)} %collective-permute-done.12.refs_2_, ...), custom_call_target="tpu_custom_call" | custom-call | flops 1000 | bytes 1000 | tf_op jit(solution)/shard_map/pallas_call | solution.py:157
  102.8 0.8 copy-done.13
  103.6 0.8 copy-done.15
  104.4 0.9 collective-permute-start.18
  105.3 0.7 collective-permute-start.19
  106.0 2.4 %collective-permute-start.29 = (bf16[2,256,32]{2,1,0:T(8,128)(2,1)}, bf16[2,256,32]{2,1,0:T(8,128)(2,1)}, u32[]{:S(2)}, u32[]{:S(2)}) collective-permute-start(bf16[2,256,32]{2,1,0:T(8,128)(2,1)} %get-tuple-element.110), channel_id=1, source_target_pairs={{0,8},{1,9},{2,10},{3,11},{4,12},{5,13},{6,14},{7,15},{8,0},{9,1},... | collective-permute-start | bytes 98312 | tf_op jit(solution)/shard_map/ppermute | solution.py:22
  108.4 2.7 %shard_map.114 = bf16[8,2,32,512]{3,2,1,0:T(8,128)(2,1)} custom-call(s32[1]{0:T(128)} %bitcast.refs_0_.pos_ref, s32[2,4]{1,0:T(2,128)} %bitcast.50, s32[2]{0:T(128)} %bitcast.58, bf16[2,512,512]{2,1,0:T(8,128)(2,1)} %bitcast.62, bf16[32,1024]{1,0:T(8,128)(2,1)} %copy-done.8, bf16[32,1024]{1,0:T(8,128)(2,1)} %copy-done.17), custom_call_target="tpu_custom_call" | custom-call | flops 40000000000 | bytes 1000 | tf_op jit(solution)/shard_map/pallas_call | solution.py:439
  111.1 1.0 copy-done.1
  112.1 1.0 copy-done.3
  113.2 0.8 copy-done.9
  114.0 0.9 copy-done.12
  115.0 0.8 copy-done.18
  115.8 2.7 %shard_map.111 = bf16[512,768]{1,0:T(8,128)(2,1)} custom-call(s32[1]{0:T(128)} %bitcast.refs_0_.pos_ref, s32[2,4]{1,0:T(2,128)} %bitcast.51, s32[2]{0:T(128)} %bitcast.59, bf16[8,2,32,512]{3,2,1,0:T(8,128)(2,1)} %bitcast.42, bf16[32,1024]{1,0:T(8,128)(2,1)S(1)} %copy-done.9, bf16[32,1024]{1,0:T(8,128)(2,1)S(1)} %copy-done.18, ...), custom_call_target="tpu_custom_call" | custom-call | flops 1000 | bytes 1000 | tf_op jit(solution)/shard_map/pallas_call | solution.py:355
  118.5 1.6 %shard_map.110 = (bf16[512,128]{1,0:T(8,128)(2,1)S(1)}, bf16[512,128]{1,0:T(8,128)(2,1)S(1)}, bf16[512,256]{1,0:T(8,128)(2,1)S(1)}) custom-call(s32[1]{0:T(128)} %bitcast.refs_0_.pos_ref, s32[2,4]{1,0:T(2,128)} %bitcast.52, s32[2]{0:T(128)} %bitcast.60, bf16[8,2,32,512]{3,2,1,0:T(8,128)(2,1)} %bitcast.43, bf16[32,1024]{1,0:T(8,128)(2,1)S(1)} %copy-done.10, ...), custom_call_target="tpu_custom_call" | custom-call | flops 1000 | bytes 1000 | tf_op jit(solution)/shard_map/pallas_call | solution.py:355
  120.1 1.0 collective-permute-start.21
  121.9 3.1 %shard_map.115 = bf16[8,32,1024]{2,1,0:T(8,128)(2,1)} custom-call(s32[1]{0:T(128)} %bitcast.refs_0_.pos_ref, s32[2,4]{1,0:T(2,128)} %bitcast.53, s32[2]{0:T(128)} %bitcast.61, bf16[2,256,1024]{2,1,0:T(8,128)(2,1)} %bitcast.39, bf16[1,256,1024]{2,1,0:T(8,128)(2,1)} %bitcast.30, bf16[1,256,1024]{2,1,0:T(8,128)(2,1)} %bitcast.32, ...), custom_call_target="tpu_custom_call" | custom-call | flops 40000000000 | bytes 1000 | tf_op jit(solution)/shard_map/pallas_call | solution.py:308
  125.0 0.9 copy-done.23
  125.9 2.4 %shard_map.112.refs_4_ = bf16[2,512,512]{2,1,0:T(8,128)(2,1)} custom-call(s32[1]{0:T(128)} %bitcast.refs_0_.pos_ref, bf16[512,768]{1,0:T(8,128)(2,1)} %copy-done.23, bf16[512,256]{1,0:T(8,128)(2,1)} %collective-permute-done.9.refs_2_, bf16[512,256]{1,0:T(8,128)(2,1)} %collective-permute-done.10.refs_3_, bf16[512,128]{1,0:T(8,128)(2,1)} %collective-permute-done.24.refs_4_, ...), custom_call_target="tpu_custom_call" | custom-call | flops 1000 | bytes 1000 | tf_op jit(solution)/shard_map/pallas_call | solution.py:398
  128.4 0.6 copy-done.26
  129.0 0.7 copy-done.24
  129.7 1.9 %shard_map.113 = bf16[2,512,512]{2,1,0:T(8,128)(2,1)} custom-call(s32[1]{0:T(128)} %bitcast.refs_0_.pos_ref, bf16[512,256]{1,0:T(8,128)(2,1)} %copy-done.24, bf16[512,128]{1,0:T(8,128)(2,1)} %copy-done.26, bf16[512,128]{1,0:T(8,128)(2,1)} %copy-done.27, bf16[2,512,512]{2,1,0:T(8,128)(2,1)} %shard_map.112.refs_4_), custom_call_target="tpu_custom_call", output_to_operand_aliasing={{}: (4, {})} | custom-call | flops 1000 | bytes 1000 | tf_op jit(solution)/shard_map/pallas_call | solution.py:398
  (85 shorter events, 2.1 us)
Async XLA Ops:
  1.7 27.3 %collective-permute-start = (bf16[256,1024]{1,0:T(8,128)(2,1)S(1)}, bf16[256,1024]{1,0:T(8,128)(2,1)S(1)}, u32[]{:S(2)}, u32[]{:S(2)}) collective-permute-start(bf16[256,1024]{1,0:T(8,128)(2,1)S(1)} %slice_bitcast_fusion.1), channel_id=1, source_target_pairs={{0,8},{1,9},{2,10},{3,11},{4,12},{5,13},{6,14},{7,15},{8,0},{9,1},... | collective-permute-start | bytes 1572872 | tf_op jit(solution)/shard_map/ppermute | solution.py:22
  5.8 5.8 %copy-start.30 = (bf16[1,2,32,64]{3,2,1,0:T(8,128)(2,1)S(1)}, bf16[1,2,32,64]{3,2,1,0:T(8,128)(2,1)}, u32[]{:S(2)}) copy-start(bf16[1,2,32,64]{3,2,1,0:T(8,128)(2,1)} %param.10) | copy-start | bytes 24580
  5.8 23.2 %copy-start.22 = (bf16[1,1,2,256,1024]{4,3,2,1,0:T(8,128)(2,1)S(1)}, bf16[1,1,2,256,1024]{4,3,2,1,0:T(8,128)(2,1)}, u32[]{:S(2)}) copy-start(bf16[1,1,2,256,1024]{4,3,2,1,0:T(8,128)(2,1)} %param.8) | copy-start | bytes 3145732
  11.6 4.0 %collective-permute-start.26 = (bf16[2,32,64]{2,1,0:T(8,128)(2,1)S(1)}, bf16[2,32,64]{2,1,0:T(8,128)(2,1)S(1)}, u32[]{:S(2)}, u32[]{:S(2)}) collective-permute-start(bf16[2,32,64]{2,1,0:T(8,128)(2,1)S(1)} %bitcast.44), channel_id=1, source_target_pairs={{0,1},{1,0},{2,3},{3,2},{4,5},{5,4},{6,7},{7,6},{8,9},{9,8},{10,11... | collective-permute-start | bytes 24584 | tf_op jit(solution)/shard_map/ppermute | solution.py:22
  13.2 27.7 %collective-permute-start.2 = (bf16[4,512,256]{2,1,0:T(8,128)(2,1)S(1)}, bf16[4,512,256]{2,1,0:T(8,128)(2,1)S(1)}, u32[]{:S(2)}, u32[]{:S(2)}) collective-permute-start(bf16[4,512,256]{2,1,0:T(8,128)(2,1)S(1)} %get-tuple-element.61), channel_id=1, source_target_pairs={{0,1},{1,0},{2,3},{3,2},{4,5},{5,4},{6,7},{7,6},{8,9},{9,8},{10,11... | collective-permute-start | bytes 3145736 | tf_op jit(solution)/shard_map/ppermute | solution.py:22
  13.7 27.2 %collective-permute-start.3 = (bf16[4,512,256]{2,1,0:T(8,128)(2,1)S(1)}, bf16[4,512,256]{2,1,0:T(8,128)(2,1)S(1)}, u32[]{:S(2)}, u32[]{:S(2)}) collective-permute-start(bf16[4,512,256]{2,1,0:T(8,128)(2,1)S(1)} %get-tuple-element.62), channel_id=1, source_target_pairs={{0,2},{1,3},{2,0},{3,1},{4,6},{5,7},{6,4},{7,5},{8,10},{9,11},{10,... | collective-permute-start | bytes 3145736 | tf_op jit(solution)/shard_map/ppermute | solution.py:22
  15.6 38.7 %copy-start.28 = (bf16[2,64,64]{2,1,0:T(8,128)(2,1)}, bf16[2,64,64]{2,1,0:T(8,128)(2,1)S(1)}, u32[]{:S(2)}) copy-start(bf16[2,64,64]{2,1,0:T(8,128)(2,1)S(1)} %maximum_select_fusion.2) | copy-start | bytes 49156
  29.0 6.1 %copy-start.19 = (bf16[256,1024]{1,0:T(8,128)(2,1)}, bf16[256,1024]{1,0:T(8,128)(2,1)S(1)}, u32[]{:S(2)}) copy-start(bf16[256,1024]{1,0:T(8,128)(2,1)S(1)} %collective-permute-done) | copy-start | bytes 1572868
  29.0 25.3 %collective-permute-start.1 = (bf16[256,1024]{1,0:T(8,128)(2,1)S(1)}, bf16[256,1024]{1,0:T(8,128)(2,1)S(1)}, u32[]{:S(2)}, u32[]{:S(2)}) collective-permute-start(bf16[256,1024]{1,0:T(8,128)(2,1)S(1)} %slice_bitcast_fusion), channel_id=1, source_target_pairs={{0,8},{1,9},{2,10},{3,11},{4,12},{5,13},{6,14},{7,15},{8,0},{9,1},... | collective-permute-start | bytes 1572872 | tf_op jit(solution)/shard_map/ppermute | solution.py:22
  41.3 22.8 %collective-permute-start.6 = (bf16[2,512,256]{2,1,0:T(8,128)(2,1)S(1)}, bf16[2,512,256]{2,1,0:T(8,128)(2,1)S(1)}, u32[]{:S(2)}, u32[]{:S(2)}) collective-permute-start(bf16[2,512,256]{2,1,0:T(8,128)(2,1)S(1)} %get-tuple-element.73), channel_id=1, source_target_pairs={{0,2},{1,3},{2,0},{3,1},{4,6},{5,7},{6,4},{7,5},{8,10},{9,11},{10,... | collective-permute-start | bytes 1572872 | tf_op jit(solution)/shard_map/ppermute | solution.py:22
  42.9 25.9 %collective-permute-start.7 = (bf16[2,512,256]{2,1,0:T(8,128)(2,1)S(1)}, bf16[2,512,256]{2,1,0:T(8,128)(2,1)S(1)}, u32[]{:S(2)}, u32[]{:S(2)}) collective-permute-start(bf16[2,512,256]{2,1,0:T(8,128)(2,1)S(1)} %get-tuple-element.74), channel_id=1, source_target_pairs={{0,1},{1,0},{2,3},{3,2},{4,5},{5,4},{6,7},{7,6},{8,9},{9,8},{10,11... | collective-permute-start | bytes 1572872 | tf_op jit(solution)/shard_map/ppermute | solution.py:22
  54.3 9.7 %copy-start.20 = (bf16[256,1024]{1,0:T(8,128)(2,1)}, bf16[256,1024]{1,0:T(8,128)(2,1)S(1)}, u32[]{:S(2)}) copy-start(bf16[256,1024]{1,0:T(8,128)(2,1)S(1)} %collective-permute-done.1) | copy-start | bytes 1572868
  54.3 17.7 %collective-permute-start.27 = (bf16[2,64,64]{2,1,0:T(8,128)(2,1)S(1)}, bf16[2,64,64]{2,1,0:T(8,128)(2,1)S(1)}, u32[]{:S(2)}, u32[]{:S(2)}) collective-permute-start(bf16[2,64,64]{2,1,0:T(8,128)(2,1)S(1)} %maximum_select_fusion.2), channel_id=1, source_target_pairs={{0,2},{1,3},{2,0},{3,1},{4,6},{5,7},{6,4},{7,5},{8,10},{9,11},{10,... | collective-permute-start | bytes 49160 | tf_op jit(solution)/shard_map/ppermute | solution.py:22
  55.6 11.6 %collective-permute-start.4 = (bf16[4,512,128]{2,1,0:T(8,128)(2,1)S(1)}, bf16[4,512,128]{2,1,0:T(8,128)(2,1)S(1)}, u32[]{:S(2)}, u32[]{:S(2)}) collective-permute-start(bf16[4,512,128]{2,1,0:T(8,128)(2,1)S(1)} %get-tuple-element.75), channel_id=1, source_target_pairs={{0,1},{1,0},{2,3},{3,2},{4,5},{5,4},{6,7},{7,6},{8,9},{9,8},{10,11... | collective-permute-start | bytes 1572872 | tf_op jit(solution)/shard_map/ppermute | solution.py:22
  57.1 11.7 %collective-permute-start.5 = (bf16[4,512,128]{2,1,0:T(8,128)(2,1)S(1)}, bf16[4,512,128]{2,1,0:T(8,128)(2,1)S(1)}, u32[]{:S(2)}, u32[]{:S(2)}) collective-permute-start(bf16[4,512,128]{2,1,0:T(8,128)(2,1)S(1)} %get-tuple-element.77), channel_id=1, source_target_pairs={{0,2},{1,3},{2,0},{3,1},{4,6},{5,7},{6,4},{7,5},{8,10},{9,11},{10,... | collective-permute-start | bytes 1572872 | tf_op jit(solution)/shard_map/ppermute | solution.py:22
  64.0 8.8 %copy-start.4 = (f32[4,512,128]{2,1,0:T(8,128)}, f32[4,512,128]{2,1,0:T(8,128)S(1)}, u32[]{:S(2)}) copy-start(f32[4,512,128]{2,1,0:T(8,128)S(1)} %get-tuple-element.91.refs_0_) | copy-start | bytes 3145732
  64.0 8.8 %copy-start.6 = (f32[4,512,128]{2,1,0:T(8,128)}, f32[4,512,128]{2,1,0:T(8,128)S(1)}, u32[]{:S(2)}) copy-start(f32[4,512,128]{2,1,0:T(8,128)S(1)} %get-tuple-element.92.refs_1_) | copy-start | bytes 3145732
  64.1 9.6 %copy-start = (bf16[2,512,256]{2,1,0:T(8,128)(2,1)}, bf16[2,512,256]{2,1,0:T(8,128)(2,1)S(1)}, u32[]{:S(2)}) copy-start(bf16[2,512,256]{2,1,0:T(8,128)(2,1)S(1)} %collective-permute-done.6.refs_7_) | copy-start | bytes 1572868
  64.9 11.5 %collective-permute-start.9 = (bf16[512,256]{1,0:T(8,128)(2,1)}, bf16[512,256]{1,0:T(8,128)(2,1)}, u32[]{:S(2)}, u32[]{:S(2)}) collective-permute-start(bf16[512,256]{1,0:T(8,128)(2,1)} %fusion), channel_id=1, source_target_pairs={{0,20},{1,21},{2,22},{3,23},{4,16},{5,17},{6,18},{7,19},{8,28},{9,... | collective-permute-start | bytes 786440 | tf_op jit(solution)/shard_map/ppermute | solution.py:32
  68.8 4.9 %copy-start.2 = (bf16[2,512,256]{2,1,0:T(8,128)(2,1)}, bf16[2,512,256]{2,1,0:T(8,128)(2,1)S(1)}, u32[]{:S(2)}) copy-start(bf16[2,512,256]{2,1,0:T(8,128)(2,1)S(1)} %collective-permute-done.7.refs_9_) | copy-start | bytes 1572868
  68.8 6.4 %collective-permute-start.8 = (f32[32,1024]{1,0:T(8,128)S(1)}, f32[32,1024]{1,0:T(8,128)S(1)}, u32[]{:S(2)}, u32[]{:S(2)}) collective-permute-start(f32[32,1024]{1,0:T(8,128)S(1)} %pad_maximum_fusion), channel_id=1, source_target_pairs={{0,1},{1,0},{2,3},{3,2},{4,5},{5,4},{6,7},{7,6},{8,9},{9,8},{10,11... | collective-permute-start | bytes 393224 | tf_op jit(solution)/shard_map/ppermute | solution.py:22
  69.3 22.3 %collective-permute-start.13 = (bf16[4,512,128]{2,1,0:T(8,128)(2,1)}, bf16[4,512,128]{2,1,0:T(8,128)(2,1)}, u32[]{:S(2)}, u32[]{:S(2)}) collective-permute-start(bf16[4,512,128]{2,1,0:T(8,128)(2,1)} %get-tuple-element.85), channel_id=1, source_target_pairs={{0,2},{1,3},{2,0},{3,1},{4,6},{5,7},{6,4},{7,5},{8,10},{9,11},{10,... | collective-permute-start | bytes 1572872 | tf_op jit(solution)/shard_map/ppermute | solution.py:22
  70.4 21.3 %collective-permute-start.12 = (bf16[4,512,128]{2,1,0:T(8,128)(2,1)}, bf16[4,512,128]{2,1,0:T(8,128)(2,1)}, u32[]{:S(2)}, u32[]{:S(2)}) collective-permute-start(bf16[4,512,128]{2,1,0:T(8,128)(2,1)} %get-tuple-element.83), channel_id=1, source_target_pairs={{0,1},{1,0},{2,3},{3,2},{4,5},{5,4},{6,7},{7,6},{8,9},{9,8},{10,11... | collective-permute-start | bytes 1572872 | tf_op jit(solution)/shard_map/ppermute | solution.py:22
  72.1 3.2 %copy-start.29 = (bf16[2,64,64]{2,1,0:T(8,128)(2,1)}, bf16[2,64,64]{2,1,0:T(8,128)(2,1)S(1)}, u32[]{:S(2)}) copy-start(bf16[2,64,64]{2,1,0:T(8,128)(2,1)S(1)} %collective-permute-done.27) | copy-start | bytes 49156
  72.1 7.2 %collective-permute-start.10 = (bf16[512,256]{1,0:T(8,128)(2,1)}, bf16[512,256]{1,0:T(8,128)(2,1)}, u32[]{:S(2)}, u32[]{:S(2)}) collective-permute-start(bf16[512,256]{1,0:T(8,128)(2,1)} %fusion.1), channel_id=1, source_target_pairs={{0,20},{1,21},{2,22},{3,23},{4,16},{5,17},{6,18},{7,19},{8,28},{9,... | collective-permute-start | bytes 786440 | tf_op jit(solution)/shard_map/ppermute | solution.py:32
  73.7 0.7 copy-start.21
  75.2 0.7 copy-start.25
  75.9 9.4 %collective-permute-start.14 = (bf16[2,512,128]{2,1,0:T(8,128)(2,1)}, bf16[2,512,128]{2,1,0:T(8,128)(2,1)S(1)}, u32[]{:S(2)}, u32[]{:S(2)}) collective-permute-start(bf16[2,512,128]{2,1,0:T(8,128)(2,1)} %get-tuple-element.88), channel_id=1, source_target_pairs={{0,2},{1,3},{2,0},{3,1},{4,6},{5,7},{6,4},{7,5},{8,10},{9,11},{10,... | collective-permute-start | bytes 786440 | tf_op jit(solution)/shard_map/ppermute | solution.py:22
  76.4 24.2 %copy-start.5 = (f32[4,512,128]{2,1,0:T(8,128)S(1)}, f32[4,512,128]{2,1,0:T(8,128)}, u32[]{:S(2)}) copy-start(f32[4,512,128]{2,1,0:T(8,128)} %copy-done.4) | copy-start | bytes 3145732
  76.4 24.2 %copy-start.7 = (f32[4,512,128]{2,1,0:T(8,128)S(1)}, f32[4,512,128]{2,1,0:T(8,128)}, u32[]{:S(2)}) copy-start(f32[4,512,128]{2,1,0:T(8,128)} %copy-done.6) | copy-start | bytes 3145732
  76.4 15.2 %collective-permute-start.15 = (bf16[2,512,128]{2,1,0:T(8,128)(2,1)}, bf16[2,512,128]{2,1,0:T(8,128)(2,1)S(1)}, u32[]{:S(2)}, u32[]{:S(2)}) collective-permute-start(bf16[2,512,128]{2,1,0:T(8,128)(2,1)} %copy-done.21), channel_id=1, source_target_pairs={{0,1},{1,0},{2,3},{3,2},{4,5},{5,4},{6,7},{7,6},{8,9},{9,8},{10,11... | collective-permute-start | bytes 786440 | tf_op jit(solution)/shard_map/ppermute | solution.py:22
  79.3 7.5 %collective-permute-start.11 = (f32[32,1024]{1,0:T(8,128)S(1)}, f32[32,1024]{1,0:T(8,128)S(1)}, u32[]{:S(2)}, u32[]{:S(2)}) collective-permute-start(f32[32,1024]{1,0:T(8,128)S(1)} %add.32), channel_id=1, source_target_pairs={{0,4},{1,5},{2,6},{3,7},{4,0},{5,1},{6,2},{7,3},{8,12},{9,13},{10,... | collective-permute-start | bytes 393224 | tf_op jit(solution)/shard_map/ppermute | solution.py:22
  86.8 7.0 %collective-permute-start.28 = (bf16[2,128,64]{2,1,0:T(8,128)(2,1)S(1)}, bf16[2,128,64]{2,1,0:T(8,128)(2,1)S(1)}, u32[]{:S(2)}, u32[]{:S(2)}) collective-permute-start(bf16[2,128,64]{2,1,0:T(8,128)(2,1)S(1)} %maximum_select_fusion.1), channel_id=1, source_target_pairs={{0,4},{1,5},{2,6},{3,7},{4,0},{5,1},{6,2},{7,3},{8,12},{9,13},{10,... | collective-permute-start | bytes 98312 | tf_op jit(solution)/shard_map/ppermute | solution.py:22
  91.6 5.1 %copy-start.11 = (bf16[2,512,128]{2,1,0:T(8,128)(2,1)}, bf16[2,512,128]{2,1,0:T(8,128)(2,1)S(1)}, u32[]{:S(2)}) copy-start(bf16[2,512,128]{2,1,0:T(8,128)(2,1)S(1)} %collective-permute-done.15.refs_13_) | copy-start | bytes 786436
  91.6 5.0 %collective-permute-start.16 = (f32[32,1024]{1,0:T(8,128)S(1)}, f32[32,1024]{1,0:T(8,128)S(1)}, u32[]{:S(2)}, u32[]{:S(2)}) collective-permute-start(f32[32,1024]{1,0:T(8,128)S(1)} %add.35), channel_id=1, source_target_pairs={{0,2},{1,3},{2,0},{3,1},{4,6},{5,7},{6,4},{7,5},{8,10},{9,11},{10,... | collective-permute-start | bytes 393224 | tf_op jit(solution)/shard_map/ppermute | solution.py:22
  96.7 11.7 %copy-start.8 = (bf16[32,1024]{1,0:T(8,128)(2,1)}, bf16[32,1024]{1,0:T(8,128)(2,1)S(1)}, u32[]{:S(2)}) copy-start(bf16[32,1024]{1,0:T(8,128)(2,1)S(1)} %add_convert_fusion.4.refs_4_.refs_0_) | copy-start | bytes 196612
  96.7 9.3 %collective-permute-start.17 = (bf16[32,1024]{1,0:T(8,128)(2,1)S(1)}, bf16[32,1024]{1,0:T(8,128)(2,1)S(1)}, u32[]{:S(2)}, u32[]{:S(2)}) collective-permute-start(bf16[32,1024]{1,0:T(8,128)(2,1)S(1)} %add_convert_fusion.4.refs_4_.refs_0_), channel_id=1, source_target_pairs={{0,8},{1,9},{2,10},{3,11},{4,12},{5,13},{6,14},{7,15},{8,0},{9,1},... | collective-permute-start | bytes 196616 | tf_op jit(solution)/shard_map/ppermute | solution.py:22
  98.9 22.2 %collective-permute-start.24 = (bf16[512,128]{1,0:T(8,128)(2,1)}, bf16[512,128]{1,0:T(8,128)(2,1)}, u32[]{:S(2)}, u32[]{:S(2)}) collective-permute-start(bf16[512,128]{1,0:T(8,128)(2,1)} %fusion.2), channel_id=1, source_target_pairs={{0,20},{1,21},{2,22},{3,23},{4,16},{5,17},{6,18},{7,19},{8,28},{9,... | collective-permute-start | bytes 393224 | tf_op jit(solution)/shard_map/ppermute | solution.py:32
  98.9 26.1 %collective-permute-start.25 = (bf16[512,128]{1,0:T(8,128)(2,1)}, bf16[512,128]{1,0:T(8,128)(2,1)}, u32[]{:S(2)}, u32[]{:S(2)}) collective-permute-start(bf16[512,128]{1,0:T(8,128)(2,1)} %fusion.3), channel_id=1, source_target_pairs={{0,20},{1,21},{2,22},{3,23},{4,16},{5,17},{6,18},{7,19},{8,28},{9,... | collective-permute-start | bytes 393224 | tf_op jit(solution)/shard_map/ppermute | solution.py:32
  102.8 0.8 copy-start.13
  103.6 0.8 copy-start.15
  104.4 14.1 %collective-permute-start.18 = (bf16[2,512,128]{2,1,0:T(8,128)(2,1)}, bf16[2,512,128]{2,1,0:T(8,128)(2,1)}, u32[]{:S(2)}, u32[]{:S(2)}) collective-permute-start(bf16[2,512,128]{2,1,0:T(8,128)(2,1)} %get-tuple-element.96), channel_id=1, source_target_pairs={{0,2},{1,3},{2,0},{3,1},{4,6},{5,7},{6,4},{7,5},{8,10},{9,11},{10,... | collective-permute-start | bytes 786440 | tf_op jit(solution)/shard_map/ppermute | solution.py:22
  105.3 13.2 %collective-permute-start.19 = (bf16[2,512,128]{2,1,0:T(8,128)(2,1)}, bf16[2,512,128]{2,1,0:T(8,128)(2,1)}, u32[]{:S(2)}, u32[]{:S(2)}) collective-permute-start(bf16[2,512,128]{2,1,0:T(8,128)(2,1)} %get-tuple-element.98), channel_id=1, source_target_pairs={{0,4},{1,5},{2,6},{3,7},{4,0},{5,1},{6,2},{7,3},{8,12},{9,13},{10,... | collective-permute-start | bytes 786440 | tf_op jit(solution)/shard_map/ppermute | solution.py:22
  106.0 2.4 %copy-start.17 = (bf16[32,1024]{1,0:T(8,128)(2,1)}, bf16[32,1024]{1,0:T(8,128)(2,1)S(1)}, u32[]{:S(2)}) copy-start(bf16[32,1024]{1,0:T(8,128)(2,1)S(1)} %collective-permute-done.17.refs_5_.refs_1_) | copy-start | bytes 196612
  106.0 15.4 %collective-permute-start.29 = (bf16[2,256,32]{2,1,0:T(8,128)(2,1)}, bf16[2,256,32]{2,1,0:T(8,128)(2,1)}, u32[]{:S(2)}, u32[]{:S(2)}) collective-permute-start(bf16[2,256,32]{2,1,0:T(8,128)(2,1)} %get-tuple-element.110), channel_id=1, source_target_pairs={{0,8},{1,9},{2,10},{3,11},{4,12},{5,13},{6,14},{7,15},{8,0},{9,1},... | collective-permute-start | bytes 98312 | tf_op jit(solution)/shard_map/ppermute | solution.py:22
  111.1 1.0 copy-start.1
  112.1 1.0 copy-start.3
  113.2 0.8 copy-start.9
  114.0 0.9 copy-start.12
  115.0 0.8 copy-start.18
  115.8 2.7 %copy-start.10 = (bf16[32,1024]{1,0:T(8,128)(2,1)S(1)}, bf16[32,1024]{1,0:T(8,128)(2,1)}, u32[]{:S(2)}) copy-start(bf16[32,1024]{1,0:T(8,128)(2,1)} %copy-done.8) | copy-start | bytes 196612
  115.8 2.7 %copy-start.14 = (f32[2,512,128]{2,1,0:T(8,128)S(1)}, f32[2,512,128]{2,1,0:T(8,128)}, u32[]{:S(2)}) copy-start(f32[2,512,128]{2,1,0:T(8,128)} %copy-done.13) | copy-start | bytes 1572868
  115.8 2.7 %copy-start.16 = (f32[2,512,128]{2,1,0:T(8,128)S(1)}, f32[2,512,128]{2,1,0:T(8,128)}, u32[]{:S(2)}) copy-start(f32[2,512,128]{2,1,0:T(8,128)} %copy-done.15) | copy-start | bytes 1572868
  118.5 6.5 %collective-permute-start.23 = (bf16[512,768]{1,0:T(8,128)(2,1)}, bf16[512,768]{1,0:T(8,128)(2,1)S(1)}, u32[]{:S(2)}, u32[]{:S(2)}) collective-permute-start(bf16[512,768]{1,0:T(8,128)(2,1)} %shard_map.111), channel_id=1, source_target_pairs={{0,16},{1,17},{2,18},{3,19},{4,20},{5,21},{6,22},{7,23},{8,24},{9,... | collective-permute-start | bytes 2359304 | tf_op jit(solution)/shard_map/ppermute | solution.py:32
  120.1 8.2 %collective-permute-start.21 = (bf16[512,128]{1,0:T(8,128)(2,1)S(1)}, bf16[512,128]{1,0:T(8,128)(2,1)S(1)}, u32[]{:S(2)}, u32[]{:S(2)}) collective-permute-start(bf16[512,128]{1,0:T(8,128)(2,1)S(1)} %get-tuple-element.100), channel_id=1, source_target_pairs={{0,20},{1,21},{2,22},{3,23},{4,16},{5,17},{6,18},{7,19},{8,28},{9,... | collective-permute-start | bytes 393224 | tf_op jit(solution)/shard_map/ppermute | solution.py:32
  121.1 7.2 %collective-permute-start.22 = (bf16[512,128]{1,0:T(8,128)(2,1)S(1)}, bf16[512,128]{1,0:T(8,128)(2,1)S(1)}, u32[]{:S(2)}, u32[]{:S(2)}) collective-permute-start(bf16[512,128]{1,0:T(8,128)(2,1)S(1)} %get-tuple-element.101), channel_id=1, source_target_pairs={{0,17},{1,16},{2,19},{3,18},{4,21},{5,20},{6,23},{7,22},{8,25},{9,... | collective-permute-start | bytes 393224 | tf_op jit(solution)/shard_map/ppermute | solution.py:32
  121.4 7.0 %collective-permute-start.20 = (bf16[512,256]{1,0:T(8,128)(2,1)S(1)}, bf16[512,256]{1,0:T(8,128)(2,1)S(1)}, u32[]{:S(2)}, u32[]{:S(2)}) collective-permute-start(bf16[512,256]{1,0:T(8,128)(2,1)S(1)} %get-tuple-element.99), channel_id=1, source_target_pairs={{0,16},{1,17},{2,18},{3,19},{4,20},{5,21},{6,22},{7,23},{8,24},{9,... | collective-permute-start | bytes 786440 | tf_op jit(solution)/shard_map/ppermute | solution.py:32
  125.0 0.9 copy-start.23
  128.3 0.7 copy-start.26
  128.4 0.7 copy-start.27
  129.0 0.7 copy-start.24

commit v8 on v7

--- a/solution.py
+++ b/solution.py
@@ -13,6 +13,7 @@
 SMEM = pl.BlockSpec(memory_space=pltpu.SMEM)
 VMEM = pl.BlockSpec(memory_space=pltpu.VMEM)
 TN = (((0,), (0,)), ((), ()))
+PARAMS = pltpu.CompilerParams(vmem_limit_bytes=24 * 2**20)
 QUICK = pl.CostEstimate(flops=1000, bytes_accessed=1000, transcendentals=0)
 LONG = pl.CostEstimate(flops=4 * 10**10, bytes_accessed=1000, transcendentals=0)
 
@@ -37,18 +38,20 @@
     return ((high ^ k) * tile_rows + offset) // SEG
 
 
-def product_body(low_size, tile_rows, pieces, tiles, half, turns, sends, keeps, *refs):
+def product_body(low_size, tile_rows, pieces, tiles, half, turns, sends, keeps, with_hidden, *refs):
     pos_ref, classes_ref, live_ref = refs[:3]
     grad_refs = refs[3 : 3 + tiles]
     weight_hbm = refs[3 + tiles]
     rows_ref, weight_ref, sems = refs[-3:]
     rest = list(refs[4 + tiles : -3])
     up_ref = rest.pop(0) if keeps else None
+    hidden_ref = rest.pop(0) if with_hidden else None
     sent_x, sent_y = (rest.pop(0), rest.pop(0)) if sends else (None, None)
+    placed_ref = rest.pop(0) if with_hidden else None
     kept_x, kept_y, rank_ref = rest if keeps else (None, None, None)
     low, high = pos_ref[0] % low_size, pos_ref[0] // low_size
-    size = pieces[0][3]
     total = rows_ref.shape[1]
+    size = total // len(pieces)
 
     def weight_copy(block):
         return pltpu.make_async_copy(
@@ -67,14 +70,27 @@
         for z in range(2):
             weight_copy(block + 4 * z).start()
 
-    for at, (tile, index, piece, _) in enumerate(pieces):
+    if with_hidden:
+        micro_count, count, rank = hidden_ref.shape
+        spot = lax.broadcasted_iota(jnp.int32, (count, half), 1)
+        row = lax.broadcasted_iota(jnp.int32, (count, half), 0)
+        chosen = (spot == low * count + row).astype(F32).astype(BF16)
+        for m in range(micro_count):
+            placed = lax.dot_general(
+                hidden_ref[m], chosen, TN, preferred_element_type=F32
+            ).astype(BF16)
+            placed_ref[m * rank : (m + 1) * rank, :] = placed
+            start = sent_x.shape[0] - (micro_count - m) * rank
+            sent_x[start : start + rank, :] = placed
+
+    for at, (tile, index, piece, first) in enumerate(pieces):
         seg = segment_of(high, piece, tile_rows)
         alive = seg < live_ref[piece[1]]
         place = slice(at * size, (at + 1) * size)
 
         @pl.when(alive)
         def _():
-            rows = grad_refs[tile][index, piece[2] : piece[2] + size, :].T
+            rows = grad_refs[tile][index, first : first + size, :].T
             rows_ref[:, place] = rows
             if keeps:
                 up = up_ref[classes_ref[piece[1], seg]]
@@ -94,35 +110,41 @@
             value = jnp.dot(
                 weight_ref[block + 4 * z], rows_ref[:, start:stop], preferred_element_type=F32
             )
-            if to_x[0] is not None:
-                to_x[0][to_x[1] + to_x[2] * z] = value[:, : half - start].astype(to_x[0].dtype)
-            if to_y[0] is not None:
-                to_y[0][to_y[1] + to_y[2] * z] = value[:, half - start :].astype(to_y[0].dtype)
-
-
-def product(scalars, grads, pieces, weight_blocks, up_tile, low_size, turns, sends, keeps, cost):
+            for (ref, slot, step), part in (
+                (to_x, value[:, : half - start]),
+                (to_y, value[:, half - start :]),
+            ):
+                if ref is not None:
+                    width = part.shape[0]
+                    place = pl.ds(pl.multiple_of((slot + step * z) * width, width), width)
+                    ref[place, :] = part.astype(ref.dtype)
+
+
+def product(scalars, grads, pieces, tile_rows, weight_blocks, up_tile, low_size, turns, sends, keeps, cost, size, hidden=None):
     blocks, width, depth = weight_blocks.shape
-    tile_rows = grads[0].shape[1]
-    rows = len(pieces) * pieces[0][3]
+    rows = len(pieces) * size
     half = rows // 2
     if rows > 128 and half % 128:
         half = half // 128 * 128 + 128
     outs = []
+    extra = 0 if hidden is None else hidden.shape[0] * hidden.shape[2]
     for wanted, dtype in ((sends, BF16), (keeps, F32)):
         if wanted:
-            outs += [
-                jax.ShapeDtypeStruct((blocks // 2, width, n), dtype) for n in (half, rows - half)
-            ]
+            for more, n in ((extra, half), (0, rows - half)):
+                outs.append(jax.ShapeDtypeStruct((blocks // 2 * width + more, n), dtype))
+    if extra:
+        outs.append(jax.ShapeDtypeStruct((extra, half), BF16))
     if keeps:
         outs.append(jax.ShapeDtypeStruct((up_tile.shape[1], rows), F32))
+    more = ([up_tile] if keeps else []) + ([] if hidden is None else [hidden])
     return pl.pallas_call(
         functools.partial(
-            product_body, low_size, tile_rows, pieces, len(grads), half, turns, sends, keeps
+            product_body, low_size, tile_rows, pieces, len(grads), half, turns, sends, keeps, extra > 0
         ),
         in_specs=[SMEM] * 3
         + [VMEM] * len(grads)
         + [pl.BlockSpec(memory_space=pltpu.HBM)]
-        + [VMEM] * keeps,
+        + [VMEM] * len(more),
         out_specs=[VMEM] * len(outs),
         out_shape=outs,
         scratch_shapes=[
@@ -130,9 +152,9 @@
             pltpu.VMEM(weight_blocks.shape, BF16),
             pltpu.SemaphoreType.DMA((blocks,)),
         ],
-        compiler_params=pltpu.CompilerParams(vmem_limit_bytes=24 * 2**20),
+        compiler_params=PARAMS,
         cost_estimate=cost,
-    )(*in_hbm(*scalars), *grads, *in_hbm(weight_blocks), *in_hbm(*[up_tile] * keeps))
+    )(*in_hbm(*scalars), *grads, *in_hbm(weight_blocks, *more))
 
 
 def in_hbm(*arrays):
@@ -143,45 +165,89 @@
     return lax.optimization_barrier((value, *others))[0]
 
 
-def halve_kernel(*refs):
-    ways = len(refs) // 4
+def halve_kernel(ways, *refs):
+    kept_refs, got_refs = refs[:ways], refs[ways : 2 * ways]
+    placed_ref = refs[2 * ways] if len(refs) > 4 * ways else None
+    outs = refs[-2 * ways - (placed_ref is not None) :]
     for way in range(ways):
-        kept_ref, got_ref, sent_ref, rest_ref = refs[way::ways]
+        kept_ref, got_ref, sent_ref, rest_ref = kept_refs[way], got_refs[way], outs[way], outs[ways + way]
         half = kept_ref.shape[0] // 2
-        sent_ref[...] = (kept_ref[half:] + got_ref[half:].astype(F32)).astype(BF16)
-        rest_ref[...] = kept_ref[:half] + got_ref[:half].astype(F32)
-
-
-def halve(kept, got):
-    shapes = [(k.shape[0] // 2,) + k.shape[1:] for k in kept]
+        sent_ref[:half, :] = (kept_ref[half:, :] + got_ref[half : 2 * half, :].astype(F32)).astype(BF16)
+        rest_ref[...] = kept_ref[:half, :] + got_ref[:half, :].astype(F32)
+        if way == 0 and placed_ref is not None:
+            placed = placed_ref[...] + got_ref[2 * half :, :]
+            sent_ref[half:, :] = placed
+            outs[-1][...] = placed
+
+
+def halve(kept, got, placed=None):
+    placed = [] if placed is None else [placed]
+    extra = [placed[0].shape[0] if placed and not way else 0 for way in range(len(kept))]
+    shapes = [(k.shape[0] // 2, k.shape[1]) for k in kept]
     outs = pl.pallas_call(
-        halve_kernel,
-        in_specs=[VMEM] * (2 * len(kept)),
-        out_specs=[VMEM] * (2 * len(kept)),
-        out_shape=[jax.ShapeDtypeStruct(s, dtype) for dtype in (BF16, F32) for s in shapes],
-        compiler_params=pltpu.CompilerParams(vmem_limit_bytes=24 * 2**20),
+        functools.partial(halve_kernel, len(kept)),
+        in_specs=[VMEM] * (2 * len(kept) + len(placed)),
+        out_specs=[VMEM] * (2 * len(kept) + len(placed)),
+        out_shape=[jax.ShapeDtypeStruct((n + e, r), BF16) for (n, r), e in zip(shapes, extra)]
+        + [jax.ShapeDtypeStruct(shape, F32) for shape in shapes]
+        + [jax.ShapeDtypeStruct(p.shape, BF16) for p in placed],
+        compiler_params=PARAMS,
         cost_estimate=QUICK,
-    )(*kept, *got)
-    return outs[: len(kept)], outs[len(kept) :]
-
-
-def up_body(low_size, tile_rows, pieces, tiles, *refs):
+    )(*kept, *got, *placed)
+    ways = len(kept)
+    return outs[:ways], outs[ways : 2 * ways], *outs[2 * ways :]
+
+
+def last_kernel(ways, *refs):
+    kept_refs, got_refs = refs[:ways], refs[ways : 2 * ways]
+    placed_ref = refs[2 * ways] if len(refs) > 3 * ways else None
+    outs = refs[-ways - (placed_ref is not None) :]
+    for way in range(ways):
+        kept_ref, got_ref = kept_refs[way], got_refs[way]
+        half = kept_ref.shape[0] // 2
+        outs[way][...] = (
+            kept_ref[half:, :] + got_ref[half : 2 * half, :].astype(F32)
+        ).astype(BF16)
+        if way == 0 and placed_ref is not None:
+            outs[-1][...] = placed_ref[...] + got_ref[2 * half :, :]
+
+
+def last_parts(kept, got, placed=None):
+    placed = [] if placed is None else [placed]
+    return pl.pallas_call(
+        functools.partial(last_kernel, len(kept)),
+        in_specs=[VMEM] * (2 * len(kept) + len(placed)),
+        out_specs=[VMEM] * (len(kept) + len(placed)),
+        out_shape=[jax.ShapeDtypeStruct((k.shape[0] // 2, k.shape[1]), BF16) for k in kept]
+        + [jax.ShapeDtypeStruct(p.shape, BF16) for p in placed],
+        compiler_params=PARAMS,
+        cost_estimate=QUICK,
+    )(*kept, *got, *placed)
+
+
+def up_body(low_size, tile_rows, pieces, tiles, micro_count, *refs):
     pos_ref, classes_ref, live_ref = refs[:3]
     grad_refs = refs[3 : 3 + tiles]
     hidden_refs = refs[3 + tiles : -2]
     out_ref, total_ref = refs[-2:]
     high = pos_ref[0] // low_size
     total_ref[...] = jnp.zeros_like(total_ref)
-    for tile, index, piece, size in pieces:
+    rank_part = total_ref.shape[1]
+    for tile, index, piece, first in pieces:
         k, m, offset = piece
+        size = min(SEG, tile_rows)
         seg = segment_of(high, piece, tile_rows)
+        near_ref, far_ref = hidden_refs[2 * k : 2 * k + 2]
+        start = m * (near_ref.shape[0] // micro_count)
+        if k == 0:
+            start = pl.multiple_of(start + high * rank_part, rank_part)
 
         @pl.when(seg < live_ref[m])
         def _():
-            total_ref[classes_ref[m, seg]] += lax.dot_general(
-                hidden_refs[k][m, offset : offset + size, :],
-                grad_refs[tile][index, offset : offset + size, :],
-                TN,
+            place = pl.ds(start, rank_part), slice(offset, offset + size)
+            total_ref[classes_ref[m, seg]] += jnp.dot(
+                near_ref[place] + far_ref[place],
+                grad_refs[tile][index, first : first + size, :],
                 preferred_element_type=F32,
             )
 
@@ -217,102 +283,108 @@
     size = min(SEG, tile_rows)
     offsets = range(0, tile_rows, size)
 
-    def send_rows(source, m):
-        return [partner(source[m], k * low_size)[None] for k in range(1, high_size)]
-
-    def pieces_of(m):
-        return [(k - 1, 0, (k, m, o), size) for k in range(1, high_size) for o in offsets]
-
-    own_pieces = [(0, m, (0, m, o), size) for m in range(micro_count) for o in offsets]
-
-    def produce(grads, pieces, turns, sends, keeps, cost):
+    own_pieces = [(0, m, (0, m, o), o) for m in range(micro_count) for o in offsets]
+
+    def pieces_of(m, count=1):
+        span = tile_rows // count
+        return [
+            ((k - 1) * count + o // span, 0, (k, m, o), o % span)
+            for k in range(1, high_size)
+            for o in offsets
+        ]
+
+    def produce(grads, pieces, turns, sends, keeps, cost, hidden=None):
         return product(
-            scalars, grads, pieces, weight_blocks, up_tile, low_size, turns, sends, keeps, cost
+            scalars, grads, pieces, tile_rows, weight_blocks, up_tile, low_size, turns, sends, keeps,
+            cost, size, hidden,
         )
 
     hidden = saved_rank_outputs[0]
-
-    def spread_hidden(hidden, bit):
-        got = partner(hidden, 1 << bit)
-        upper = (position >> bit) & 1 == 1
-        return jnp.where(
-            upper, jnp.concatenate([got, hidden], 1), jnp.concatenate([hidden, got], 1)
-        )
 
     first_rows = lax.optimization_barrier(grad_tile[0])
     got0 = [partner(first_rows, k * low_size)[None] for k in range(1, high_size)]
     (own_grads,) = in_hbm(after(grad_tile, first_rows))
-    sent_x, sent_y = produce([own_grads], own_pieces, False, True, False, QUICK)
+    sent_x, sent_y, placed = produce([own_grads], own_pieces, False, True, False, QUICK, hidden)
     first_x, first_y = partner(sent_x, 1), partner(sent_y, 2)
-    hidden = spread_hidden(after(hidden, sent_x, sent_y), 0)
-    rows0 = after(got0[0], sent_x, sent_y), *got0[1:]
+    (own_grads,) = in_hbm(after(grad_tile, sent_x, sent_y))
+    kept_x, kept_y, part = produce([own_grads], own_pieces, False, False, True, QUICK)
+    parts = [part]
+    rows0 = after(got0[0], part), *got0[1:]
     c_sent_x, c_sent_y, c_kept_x, c_kept_y, part = produce(
         list(rows0), pieces_of(0), False, True, True, LONG
     )
-    parts = [part]
-    (own_grads,) = in_hbm(after(grad_tile, part))
-    kept_x, kept_y, part = produce([own_grads], own_pieces, False, False, True, LONG)
-    parts.insert(0, part)
-    got1 = send_rows(after(grad_tile, *got0), 1)
-
-    (sent_x, sent_y), (kept_x, kept_y) = halve((kept_x, kept_y), (first_x, first_y))
+    parts.append(part)
+    count = 2 if size == SEG and tile_rows >= 2 * SEG else 1
+    source, got1 = after(grad_tile[1], *got0), [[] for _ in range(1, high_size)]
+    for at in range(count):
+        span = tile_rows // count
+        rows = source[at * span : (at + 1) * span]
+        for k in range(1, high_size):
+            got1[k - 1].append(partner(rows, k * low_size)[None])
+        source = after(source, *[got[-1] for got in got1])
+    early, got1 = got1[0][0], [part for got in got1 for part in got]
+
+    (sent_x, sent_y), (kept_x, kept_y), placed = halve(
+        (after(kept_x, part, early), kept_y), (first_x, first_y), placed
+    )
     second_x, second_y = partner(sent_x, 2), partner(sent_y, 1)
     c_first_x = partner(after(c_sent_x, sent_x, sent_y), 1)
     c_first_y = partner(after(c_sent_y, sent_x, sent_y), 2)
-    hidden = spread_hidden(after(hidden, sent_x, sent_y), 1)
+
+    chunks = [([grad_tile], own_pieces), (got0, pieces_of(0)), (got1, pieces_of(1, count))]
+    order = [piece for _, pieces in chunks for _, _, piece, _ in pieces]
+    *own_third, placed = last_parts((kept_x, kept_y), (second_x, second_y), placed)
+    own_last = [relay(third, 4) for third in own_third]
     own_sums = (kept_x, second_x), (kept_y, second_y)
-
-    def third_part(two):
-        kept, second = two
-        return (kept[1] + second[1]).astype(BF16)
-
-    chunks = [([grad_tile], own_pieces), (got0, pieces_of(0)), (got1, pieces_of(1))]
-    order = [piece for _, pieces in chunks for _, _, piece, _ in pieces]
-    rows1 = after(got1[0], part), *got1[1:]
+    rows1 = after(got1[0], part, *own_third), *got1[1:]
     d_sent_x, d_sent_y, d_kept_x, d_kept_y, part = produce(
-        list(rows1), pieces_of(1), True, True, True, LONG
+        list(rows1), pieces_of(1, count), True, True, True, LONG
     )
     parts.append(part)
-    own_last = [relay(third_part(two), 4) for two in own_sums]
-    slot = c_first_x, c_first_y, second_x, second_y
-    own_rank = after(jnp.concatenate(parts, 1), *slot)
-    own_rank = own_rank + partner(own_rank, 1)
-    d_first_x = partner(after(d_sent_x, *slot), 1)
-    d_first_y = partner(after(d_sent_y, *slot), 2)
+    hiddens = [placed, partner(placed, 4)]
+    for k in range(1, high_size):
+        wanted = placed.reshape(micro_count, rank, tile_rows)
+        wanted = lax.dynamic_slice_in_dim(wanted, (high ^ k) * rank_part, rank_part, 1)
+        wanted = wanted.reshape(micro_count * rank_part, tile_rows)
+        hiddens += [partner(wanted, k * low_size), partner(wanted, k * low_size + 4)]
+    own_rank = jnp.concatenate(parts, 1)
+    shared = after(own_rank.astype(BF16), *own_last, *hiddens)
+    for mask in (1, 2, 3):
+        own_rank = own_rank + partner(shared, mask)
     (c_sent_x, c_sent_y), c_kept = halve((c_kept_x, c_kept_y), (c_first_x, c_first_y))
+    slot = own_rank, c_sent_x, c_sent_y
+    d_first_x, d_first_y = partner(after(d_sent_x, *slot), 1), partner(after(d_sent_y, *slot), 2)
     c_second_x, c_second_y = partner(c_sent_x, 2), partner(c_sent_y, 1)
-    c_sums = (c_kept[0], c_second_x), (c_kept[1], c_second_y)
-    own_rank = own_rank + partner(after(own_rank, *own_last), 4)
-    hidden = spread_hidden(after(hidden, own_rank), 2)
-
-    slot = d_first_x, d_first_y, c_second_x, c_second_y, own_rank
-    own_rank = after(own_rank, *slot)
-    own_rank = (own_rank + partner(own_rank, 2)).astype(BF16)
-    (d_sent_x, d_sent_y), d_kept = halve(
-        (d_kept_x, d_kept_y), (after(d_first_x, *slot), after(d_first_y, *slot))
-    )
-    d_second_x, d_second_y = partner(d_sent_x, 2), partner(d_sent_y, 4)
-    d_sums = (d_kept[0], d_second_x), (d_kept[1], d_second_y)
-    c_last = [relay(after(third_part(two), *slot), 4) for two in c_sums]
-    ranks = [own_rank] + [partner(own_rank, j * low_size) for j in range(1, high_size)]
-    hiddens = []
-    for k in range(high_size):
-        wanted = lax.dynamic_slice_in_dim(hidden, (high ^ k) * rank_part, rank_part, 2)
-        wanted = after(wanted, ranks[-1])
-        hiddens.append(partner(wanted, k * low_size) if k > 0 else wanted)
+    shared = own_rank.astype(BF16)
+    ranks = [(own_rank + partner(shared, 4)).astype(BF16)]
+    for j in range(1, high_size):
+        one, other = partner(shared, j * low_size), partner(shared, j * low_size + 4)
+        ranks.append((one.astype(F32) + other.astype(F32)).astype(BF16))
 
     all_grads, all_pieces = [], []
     for grads, pieces in chunks:
-        all_pieces += [(tile + len(all_grads), index, piece, size) for tile, index, piece, size in pieces]
+        all_pieces += [(tile + len(all_grads), *rest) for tile, *rest in pieces]
         all_grads += grads
     up_map_gradient = pl.pallas_call(
-        functools.partial(up_body, low_size, tile_rows, all_pieces, len(all_grads)),
-        in_specs=[SMEM] * 3 + [VMEM] * (len(all_grads) + high_size),
+        functools.partial(
+            up_body, low_size, tile_rows, all_pieces, len(all_grads), micro_count
+        ),
+        in_specs=[SMEM] * 3 + [VMEM] * (len(all_grads) + 2 * high_size),
         out_specs=VMEM,
         out_shape=jax.ShapeDtypeStruct(up_tile.shape, BF16),
         scratch_shapes=[pltpu.VMEM(up_tile.shape, F32)],
-        cost_estimate=LONG,
+        compiler_params=PARAMS,
+        cost_estimate=QUICK,
     )(*in_hbm(*scalars), *all_grads, *hiddens)
+
+    (d_sent_x, d_sent_y), d_kept = halve(
+        (after(d_kept_x, up_map_gradient), d_kept_y), (d_first_x, d_first_y)
+    )
+    d_second_x, d_second_y = partner(d_sent_x, 2), partner(d_sent_y, 4)
+    c_third = last_parts(c_kept, (c_second_x, c_second_y))
+    c_last = [relay(third, 4) for third in c_third]
+    c_sums = (c_kept[0], c_second_x), (c_kept[1], c_second_y)
+    d_sums = (d_kept[0], d_second_x), (d_kept[1], d_second_y)
 
     def columns_of(j, piece):
         k, m, offset = piece
@@ -330,10 +402,14 @@
         start = 0
         for g in range(groups):
             kept_ref, second_ref = sum_refs[2 * g : 2 * g + 2]
-            count = kept_ref.shape[2]
-            total_ref[:, start : start + count] = kept_ref[0] + second_ref[0].astype(F32)
+            half, count = kept_ref.shape[0] // 2, kept_ref.shape[1]
+            total_ref[:, start : start + count] = (
+                kept_ref[:half, :] + second_ref[:half, :].astype(F32)
+            )
             if with_last:
-                last_refs[g][...] = (kept_ref[1] + second_ref[1].astype(F32)).astype(BF16)
+                last_refs[g][...] = (
+                    kept_ref[half:, :] + second_ref[half : 2 * half, :].astype(F32)
+                ).astype(BF16)
             start += count
         for at in range(start // size):
             piece = order[first + at]
@@ -350,7 +426,7 @@
             out_ref[:, rows] = adapter.astype(BF16)
 
     def with_adapter(sums, first, with_last):
-        counts = [kept.shape[2] for kept, _ in sums]
+        counts = [kept.shape[1] for kept, _ in sums]
         shapes = [(portion, n) for n in counts] * with_last + [(portion, sum(counts))]
         outs = pl.pallas_call(
             functools.partial(adapter_kernel, first, with_last, len(sums)),
@@ -358,7 +434,7 @@
             out_specs=[VMEM] * len(shapes),
             out_shape=[jax.ShapeDtypeStruct(shape, BF16) for shape in shapes],
             scratch_shapes=[pltpu.VMEM(shapes[-1], F32)],
-            compiler_params=pltpu.CompilerParams(vmem_limit_bytes=24 * 2**20),
+            compiler_params=PARAMS,
             cost_estimate=QUICK,
         )(*in_hbm(*scalars), *in_hbm(down_parts), *ranks, *[a for two in sums for a in two])
         return outs[:-1], outs[-1]
@@ -406,6 +482,7 @@
                 pltpu.VMEM((rows, portion), BF16),
                 pltpu.SemaphoreType.DMA((rows // size,)),
             ],
+            compiler_params=PARAMS,
             cost_estimate=QUICK,
         )(*in_hbm(scalars[0]), kept, *got, *before)
 
@@ -442,6 +519,7 @@
         out_specs=VMEM,
         out_shape=jax.ShapeDtypeStruct(down_parts.shape, BF16),
         scratch_shapes=[pltpu.VMEM(down_parts.shape, F32)],
+        compiler_params=PARAMS,
         cost_estimate=LONG,
     )(*in_hbm(*scalars, forward_input[0]), *ranks)
 

time: 133 us -> 129 us (0.970)
  waiting for transfers between devices: 34.7 us -> 54.1 us
  local copies, waits for them, and re-layouts: 11.9 us -> 2.74 us
  Pallas kernels: 41.6 us -> 36.4 us
  other arithmetic: 4.84 us -> 0.08 us
  starting transfers between devices: 37.6 us -> 34.2 us
    ppermute x22 -> x24, waiting for transfers between devices: 34.6 us -> 54.1 us  [partner(): return lax.ppermute(value, 'tensor', pairs)]
    unnamed x62 -> x34, local copies, waits for them, and re-layouts: 10 us -> 0.71 us
    convert_element_type x5 -> x4, other arithmetic: 2.97 us -> 0.08 us  [the longest x1 0.03 us: shards(): shared = own_rank.astype(BF16)]
    pallas_call x2, Pallas kernels: 4.31 us -> 1.92 us  [finish(): pl.pallas_call(functools.partial(finish_kernel, first, len(got)), in_spec...]
    ppermute x22 -> x24, starting transfers between devices: 33.3 us -> 31.1 us  [partner(): return lax.ppermute(value, 'tensor', pairs)]
    pallas_call x3 -> x5, Pallas kernels: 3.32 us -> 1.76 us  [the longest x3 1.62 us: halve(): pl.pallas_call(functools.partial(halve_kernel, len(kept)), in_specs=[VMEM...]
  transfers between devices with their start and end apart: 30 -> 32, of which waited for: 10 -> 13; matrix products, arithmetic and copies ran while one was open for 4% -> 1% of each run, Pallas kernels for 30% -> 27%
where the time goes in v8:
time: 129 us; the launch traced here: 128 us
  waiting for transfers between devices  54.1 us (42%)
  Pallas kernels  36.4 us (28%)
  starting transfers between devices  34.2 us (27%)
  local copies, waits for them, and re-layouts  2.74 us (2%)
    ppermute x24, waiting for transfers between devices, partner(): return lax.ppermute(value, 'tensor', pairs)  54.1 us
    ppermute x24, starting transfers between devices, partner(): return lax.ppermute(value, 'tensor', pairs)  31.1 us
    pallas_call x4, Pallas kernels, product(): pl.pallas_call(functools.partial(product_body, low_size, tile_rows, piece...  23.6 us
    pallas_call x2, Pallas kernels, with_adapter(): pl.pallas_call(functools.partial(adapter_kernel, first, with_last, len(su...  3.12 us
    ppermute x8, starting transfers between devices, relay(): return lax.ppermute(value, ('pipe', 'tensor'), pairs)  3.1 us
    pallas_call x1, Pallas kernels, shards(): pl.pallas_call(down_kernel, in_specs=[SMEM] * 3 + [VMEM] * (1 + high_size...  3.1 us
    pallas_call x1, Pallas kernels, shards(): pl.pallas_call(functools.partial(up_body, low_size, tile_rows, all_pieces...  2.86 us
  transfers between devices with their start and end apart: 32, of which 13 were waited for; matrix products, arithmetic and copies ran while one was open for 1% of the time, Pallas kernels for 27%

profile of v8, /device:TPU:0, one launch (start us, length us, event | category | flops | bytes accessed | tf_op | source)
XLA Modules:
  0.0 128.5 jit_solution(437510149916262875)
XLA Ops:
  0.6 1.3 slice_bitcast_fusion
  1.9 0.0 copy-start.13
  1.9 4.1 %collective-permute-start = (bf16[256,1024]{1,0:T(8,128)(2,1)S(1)}, bf16[256,1024]{1,0:T(8,128)(2,1)S(1)}, u32[]{:S(2)}, u32[]{:S(2)}) collective-permute-start(bf16[256,1024]{1,0:T(8,128)(2,1)S(1)} %get-tuple-element.112), channel_id=1, source_target_pairs={{0,8},{1,9},{2,10},{3,11},{4,12},{5,13},{6,14},{7,15},{8,0},{9,1},... | collective-permute-start | bytes 1572872 | tf_op jit(solution)/shard_map/ppermute | solution.py:23
  6.0 5.7 %shard_map.103 = (bf16[2176,256]{1,0:T(8,128)(2,1)S(1)}, bf16[2048,256]{1,0:T(8,128)(2,1)S(1)}, bf16[128,256]{1,0:T(8,128)(2,1)S(1)}) custom-call(s32[1]{0:T(128)} %bitcast.refs_0_.pos_ref, s32[2,4]{1,0:T(2,128)} %bitcast.42, s32[2]{0:T(128)} %bitcast.51, bf16[2,256,1024]{2,1,0:T(8,128)(2,1)} %bitcast.21, bf16[8,512,1024]{2,1,0:T(8,128)(2,1)} %bitcast.29, ...), custom_call_target="tpu_custom_call" | custom-call | flops 1000 | bytes 1000 | tf_op jit(solution)/shard_map/pallas_call | solution.py:140
  11.7 1.6 %collective-permute-start.3 = (bf16[2048,256]{1,0:T(8,128)(2,1)S(1)}, bf16[2048,256]{1,0:T(8,128)(2,1)S(1)}, u32[]{:S(2)}, u32[]{:S(2)}) collective-permute-start(bf16[2048,256]{1,0:T(8,128)(2,1)S(1)} %get-tuple-element.61), channel_id=1, source_target_pairs={{0,2},{1,3},{2,0},{3,1},{4,6},{5,7},{6,4},{7,5},{8,10},{9,11},{10,... | collective-permute-start | bytes 3145736 | tf_op jit(solution)/shard_map/ppermute | solution.py:23
  13.3 1.5 %collective-permute-start.2 = (bf16[2176,256]{1,0:T(8,128)(2,1)S(1)}, bf16[2176,256]{1,0:T(8,128)(2,1)S(1)}, u32[]{:S(2)}, u32[]{:S(2)}) collective-permute-start(bf16[2176,256]{1,0:T(8,128)(2,1)S(1)} %get-tuple-element.60), channel_id=1, source_target_pairs={{0,1},{1,0},{2,3},{3,2},{4,5},{5,4},{6,7},{7,6},{8,9},{9,8},{10,11... | collective-permute-start | bytes 3342344 | tf_op jit(solution)/shard_map/ppermute | solution.py:23
  14.8 5.8 %shard_map.104 = (f32[2048,256]{1,0:T(8,128)S(1)}, f32[2048,256]{1,0:T(8,128)S(1)}, f32[32,512]{1,0:T(8,128)S(1)}) custom-call(s32[1]{0:T(128)} %bitcast.refs_0_.pos_ref, s32[2,4]{1,0:T(2,128)} %bitcast.43, s32[2]{0:T(128)} %bitcast.52, bf16[2,256,1024]{2,1,0:T(8,128)(2,1)} %bitcast.22, bf16[8,512,1024]{2,1,0:T(8,128)(2,1)} %bitcast.30, ...), custom_call_target="tpu_custom_call" | custom-call | flops 1000 | bytes 1000 | tf_op jit(solution)/shard_map/pallas_call | solution.py:140
  20.7 8.5 %collective-permute-done = bf16[256,1024]{1,0:T(8,128)(2,1)S(1)} collective-permute-done((bf16[256,1024]{1,0:T(8,128)(2,1)S(1)}, bf16[256,1024]{1,0:T(8,128)(2,1)S(1)}, u32[]{:S(2)}, u32[]{:S(2)}) %collective-permute-start) | collective-permute-done | bytes 524320 | tf_op jit(solution)/shard_map/ppermute | solution.py:23
  29.2 0.1 collective-permute-start.1
  29.3 6.0 %shard_map.105 = (bf16[2048,128]{1,0:T(8,128)(2,1)S(1)}, bf16[2048,128]{1,0:T(8,128)(2,1)S(1)}, f32[2048,128]{1,0:T(8,128)S(1)}, f32[2048,128]{1,0:T(8,128)S(1)}, f32[32,256]{1,0:T(8,128)S(1)}) custom-call(s32[1]{0:T(128)} %bitcast.refs_0_.pos_ref, s32[2,4]{1,0:T(2,128)} %bitcast.44, s32[2]{0:T(128)} %bitcast.53, bf16[1,256,1024]{2,1,0:T(8,128)(2,1)S(1)} %bitcast.24, ...), custom_call_target="tpu_custom_call" | custom-call | flops 40000000000 | bytes 1000 | tf_op jit(solution)/shard_map/pallas_call | solution.py:140
  35.3 0.0 copy-start.1
  35.3 8.0 %collective-permute-done.1 = bf16[128,1024]{1,0:T(8,128)(2,1)S(1)} collective-permute-done((bf16[128,1024]{1,0:T(8,128)(2,1)S(1)}, bf16[128,1024]{1,0:T(8,128)(2,1)S(1)}, u32[]{:S(2)}, u32[]{:S(2)}) %collective-permute-start.1) | collective-permute-done | bytes 262176 | tf_op jit(solution)/shard_map/ppermute | solution.py:23
  43.3 0.0 collective-permute-done.3.refs_3_
  43.3 0.0 collective-permute-done.2.refs_2_
  43.3 1.3 %shard_map.106 = (bf16[1152,256]{1,0:T(8,128)(2,1)}, bf16[1024,256]{1,0:T(8,128)(2,1)}, f32[1024,256]{1,0:T(8,128)S(1)}, f32[1024,256]{1,0:T(8,128)S(1)}, bf16[128,256]{1,0:T(8,128)(2,1)S(1)}) custom-call(f32[2048,256]{1,0:T(8,128)S(1)} %get-tuple-element.68.refs_0_, f32[2048,256]{1,0:T(8,128)S(1)} %get-tuple-element.69.refs_1_, ...), custom_call_target="tpu_custom_call" | custom-call | flops 1000 | bytes 1000 | tf_op jit(solution)/shard_map/pallas_call | solution.py:187
  44.6 1.3 %collective-permute-start.4 = (bf16[1152,256]{1,0:T(8,128)(2,1)}, bf16[1152,256]{1,0:T(8,128)(2,1)S(1)}, u32[]{:S(2)}, u32[]{:S(2)}) collective-permute-start(bf16[1152,256]{1,0:T(8,128)(2,1)} %get-tuple-element.73), channel_id=1, source_target_pairs={{0,2},{1,3},{2,0},{3,1},{4,6},{5,7},{6,4},{7,5},{8,10},{9,11},{10,... | collective-permute-start | bytes 1769480 | tf_op jit(solution)/shard_map/ppermute | solution.py:23
  46.0 1.5 %collective-permute-start.5 = (bf16[1024,256]{1,0:T(8,128)(2,1)}, bf16[1024,256]{1,0:T(8,128)(2,1)S(1)}, u32[]{:S(2)}, u32[]{:S(2)}) collective-permute-start(bf16[1024,256]{1,0:T(8,128)(2,1)} %get-tuple-element.74), channel_id=1, source_target_pairs={{0,1},{1,0},{2,3},{3,2},{4,5},{5,4},{6,7},{7,6},{8,9},{9,8},{10,11... | collective-permute-start | bytes 1572872 | tf_op jit(solution)/shard_map/ppermute | solution.py:23
  47.4 0.7 slice.17
  48.2 0.6 constant_dynamic-update-slice_fusion.2
  48.8 9.0 %collective-permute-done.5.refs_3_.refs_9_ = bf16[1024,256]{1,0:T(8,128)(2,1)S(1)} collective-permute-done((bf16[1024,256]{1,0:T(8,128)(2,1)}, bf16[1024,256]{1,0:T(8,128)(2,1)S(1)}, u32[]{:S(2)}, u32[]{:S(2)}) %collective-permute-start.5) | collective-permute-done | bytes 524320 | tf_op jit(solution)/shard_map/ppermute | solution.py:23
  57.8 0.7 collective-permute-done.4.refs_2_.refs_7_
  58.5 0.1 shard_map.107
  58.6 2.9 %collective-permute-start.11 = (bf16[64,256]{1,0:T(8,128)(2,1)S(1)}, bf16[64,256]{1,0:T(8,128)(2,1)S(1)}, u32[]{:S(2)}, u32[]{:S(2)}) collective-permute-start(bf16[64,256]{1,0:T(8,128)(2,1)S(1)} %bitcast.40), channel_id=1, source_target_pairs={{0,12},{1,13},{2,14},{3,15},{4,8},{5,9},{6,10},{7,11},{8,4},{9,5},... | collective-permute-start | bytes 98312 | tf_op jit(solution)/shard_map/ppermute | solution.py:23
  61.5 1.3 %collective-permute-start.18 = (bf16[2048,128]{1,0:T(8,128)(2,1)S(1)}, bf16[2048,128]{1,0:T(8,128)(2,1)S(1)}, u32[]{:S(2)}, u32[]{:S(2)}) collective-permute-start(bf16[2048,128]{1,0:T(8,128)(2,1)S(1)} %copy-done.12), channel_id=1, source_target_pairs={{0,1},{1,0},{2,3},{3,2},{4,5},{5,4},{6,7},{7,6},{8,9},{9,8},{10,11... | collective-permute-start | bytes 1572872 | tf_op jit(solution)/shard_map/ppermute | solution.py:23
  62.8 1.5 %collective-permute-start.19 = (bf16[2048,128]{1,0:T(8,128)(2,1)S(1)}, bf16[2048,128]{1,0:T(8,128)(2,1)S(1)}, u32[]{:S(2)}, u32[]{:S(2)}) collective-permute-start(bf16[2048,128]{1,0:T(8,128)(2,1)S(1)} %copy-done.10), channel_id=1, source_target_pairs={{0,2},{1,3},{2,0},{3,1},{4,6},{5,7},{6,4},{7,5},{8,10},{9,11},{10,... | collective-permute-start | bytes 1572872 | tf_op jit(solution)/shard_map/ppermute | solution.py:23
  64.4 0.3 collective-permute-done.11.refs_10_
  64.7 1.4 %collective-permute-start.8 = (bf16[512,256]{1,0:T(8,128)(2,1)S(1)}, bf16[512,256]{1,0:T(8,128)(2,1)S(1)}, u32[]{:S(2)}, u32[]{:S(2)}) collective-permute-start(bf16[512,256]{1,0:T(8,128)(2,1)S(1)} %get-tuple-element.77), channel_id=1, source_target_pairs={{0,20},{1,21},{2,22},{3,23},{4,16},{5,17},{6,18},{7,19},{8,28},{9,... | collective-permute-start | bytes 786440 | tf_op jit(solution)/shard_map/ppermute | solution.py:33
  66.1 6.1 %shard_map.108 = (bf16[2048,128]{1,0:T(8,128)(2,1)S(1)}, bf16[2048,128]{1,0:T(8,128)(2,1)S(1)}, f32[2048,128]{1,0:T(8,128)S(1)}, f32[2048,128]{1,0:T(8,128)S(1)}, f32[32,256]{1,0:T(8,128)S(1)}) custom-call(s32[1]{0:T(128)} %bitcast.refs_0_.pos_ref, s32[2,4]{1,0:T(2,128)} %bitcast.45, s32[2]{0:T(128)} %bitcast.54, bf16[1,128,1024]{2,1,0:T(8,128)(2,1)S(1)} %bitcast.26, ...), custom_call_target="tpu_custom_call" | custom-call | flops 40000000000 | bytes 1000 | tf_op jit(solution)/shard_map/pallas_call | solution.py:140
  72.2 0.0 copy-start
  72.3 1.3 %collective-permute-start.9 = (bf16[128,256]{1,0:T(8,128)(2,1)S(1)}, bf16[128,256]{1,0:T(8,128)(2,1)S(1)}, u32[]{:S(2)}, u32[]{:S(2)}) collective-permute-start(bf16[128,256]{1,0:T(8,128)(2,1)S(1)} %get-tuple-element.81.refs_7_), channel_id=1, source_target_pairs={{0,4},{1,5},{2,6},{3,7},{4,0},{5,1},{6,2},{7,3},{8,12},{9,13},{10,... | collective-permute-start | bytes 196616 | tf_op jit(solution)/shard_map/ppermute | solution.py:23
  73.6 6.4 %collective-permute-done.9.refs_8_ = bf16[128,256]{1,0:T(8,128)(2,1)S(1)} collective-permute-done((bf16[128,256]{1,0:T(8,128)(2,1)S(1)}, bf16[128,256]{1,0:T(8,128)(2,1)S(1)}, u32[]{:S(2)}, u32[]{:S(2)}) %collective-permute-start.9) | collective-permute-done | bytes 65568 | tf_op jit(solution)/shard_map/ppermute | solution.py:23
  80.0 1.1 collective-permute-start.14
  81.1 0.9 collective-permute-start.13
  82.0 1.5 %collective-permute-start.12 = (bf16[32,1024]{1,0:T(8,128)(2,1)S(1)}, bf16[32,1024]{1,0:T(8,128)(2,1)S(1)}, u32[]{:S(2)}, u32[]{:S(2)}) collective-permute-start(bf16[32,1024]{1,0:T(8,128)(2,1)S(1)} %convert_element_type.30), channel_id=1, source_target_pairs={{0,1},{1,0},{2,3},{3,2},{4,5},{5,4},{6,7},{7,6},{8,9},{9,8},{10,11... | collective-permute-start | bytes 196616 | tf_op jit(solution)/shard_map/ppermute | solution.py:23
  83.5 0.2 shard_map.110
  83.7 2.0 %collective-permute-done.14 = bf16[32,1024]{1,0:T(8,128)(2,1)S(1)} collective-permute-done((bf16[32,1024]{1,0:T(8,128)(2,1)S(1)}, bf16[32,1024]{1,0:T(8,128)(2,1)S(1)}, u32[]{:S(2)}, u32[]{:S(2)}) %collective-permute-start.14) | collective-permute-done | bytes 65568 | tf_op jit(solution)/shard_map/ppermute | solution.py:23
  85.7 0.5 collective-permute-done.13
  86.2 0.0 collective-permute-done.12
  86.3 1.2 collective-permute-start.21
  87.5 0.9 collective-permute-start.20
  88.3 1.5 %collective-permute-start.27 = (bf16[1024,128]{1,0:T(8,128)(2,1)S(1)}, bf16[1024,128]{1,0:T(8,128)(2,1)S(1)}, u32[]{:S(2)}, u32[]{:S(2)}) collective-permute-start(bf16[1024,128]{1,0:T(8,128)(2,1)S(1)} %get-tuple-element.93), channel_id=1, source_target_pairs={{0,2},{1,3},{2,0},{3,1},{4,6},{5,7},{6,4},{7,5},{8,10},{9,11},{10,... | collective-permute-start | bytes 786440 | tf_op jit(solution)/shard_map/ppermute | solution.py:23
  89.9 0.5 collective-permute-start.28
  90.4 0.7 collective-permute-start.15
  91.1 2.9 %shard_map.109 = bf16[8,32,1024]{2,1,0:T(8,128)(2,1)} custom-call(s32[1]{0:T(128)} %bitcast.refs_0_.pos_ref, s32[2,4]{1,0:T(2,128)} %bitcast.46, s32[2]{0:T(128)} %bitcast.55, bf16[2,256,1024]{2,1,0:T(8,128)(2,1)S(1)} %bitcast.23, bf16[1,256,1024]{2,1,0:T(8,128)(2,1)S(1)} %bitcast.25, bf16[1,128,1024]{2,1,0:T(8,128)(2,1)S(1)} %bitcast.27, ...), custom_call_target="tpu_custom_call" | custom-call | flops 1000 | bytes 1000 | tf_op jit(solution)/shard_map/pallas_call | solution.py:368
  93.9 11.6 %collective-permute-done.27.refs_11_.refs_2_ = bf16[1024,128]{1,0:T(8,128)(2,1)S(1)} collective-permute-done((bf16[1024,128]{1,0:T(8,128)(2,1)S(1)}, bf16[1024,128]{1,0:T(8,128)(2,1)S(1)}, u32[]{:S(2)}, u32[]{:S(2)}) %collective-permute-start.27) | collective-permute-done | bytes 262176 | tf_op jit(solution)/shard_map/ppermute | solution.py:23
  105.5 0.5 collective-permute-done.28.refs_13_.refs_3_
  106.1 0.1 collective-permute-start.30
  106.2 1.0 collective-permute-start.17
  107.2 1.2 collective-permute-start.16
  108.4 0.2 shard_map.111
  108.6 0.7 collective-permute-start.22
  109.3 2.8 %collective-permute-start.23 = (bf16[1024,128]{1,0:T(8,128)(2,1)S(1)}, bf16[1024,128]{1,0:T(8,128)(2,1)S(1)}, u32[]{:S(2)}, u32[]{:S(2)}) collective-permute-start(bf16[1024,128]{1,0:T(8,128)(2,1)S(1)} %get-tuple-element.101), channel_id=1, source_target_pairs={{0,4},{1,5},{2,6},{3,7},{4,0},{5,1},{6,2},{7,3},{8,12},{9,13},{10,... | collective-permute-start | bytes 786440 | tf_op jit(solution)/shard_map/ppermute | solution.py:23
  112.1 1.1 collective-permute-done.17
  113.2 2.6 %collective-permute-done.16 = bf16[32,1024]{1,0:T(8,128)(2,1)S(1)} collective-permute-done((bf16[32,1024]{1,0:T(8,128)(2,1)S(1)}, bf16[32,1024]{1,0:T(8,128)(2,1)S(1)}, u32[]{:S(2)}, u32[]{:S(2)}) %collective-permute-start.16) | collective-permute-done | bytes 65568 | tf_op jit(solution)/shard_map/ppermute | solution.py:23
  115.8 1.7 %shard_map.113 = bf16[512,768]{1,0:T(8,128)(2,1)S(1)} custom-call(s32[1]{0:T(128)} %bitcast.refs_0_.pos_ref, s32[2,4]{1,0:T(2,128)} %bitcast.47, s32[2]{0:T(128)} %bitcast.56, bf16[8,2,32,512]{3,2,1,0:T(8,128)(2,1)} %bitcast.34, bf16[32,1024]{1,0:T(8,128)(2,1)S(1)} %add_convert_fusion.1.refs_4_.refs_0_, ...), custom_call_target="tpu_custom_call" | custom-call | flops 1000 | bytes 1000 | tf_op jit(solution)/shard_map/pallas_call | solution.py:431
  117.5 0.1 collective-permute-start.29
  117.7 0.0 collective-permute-done.22.refs_7_
  117.7 2.8 %collective-permute-done.23.refs_9_ = bf16[1024,128]{1,0:T(8,128)(2,1)S(1)} collective-permute-done((bf16[1024,128]{1,0:T(8,128)(2,1)S(1)}, bf16[1024,128]{1,0:T(8,128)(2,1)S(1)}, u32[]{:S(2)}, u32[]{:S(2)}) %collective-permute-start.23) | collective-permute-done | bytes 262176 | tf_op jit(solution)/shard_map/ppermute | solution.py:23
  120.5 1.4 %shard_map.112 = (bf16[512,128]{1,0:T(8,128)(2,1)S(1)}, bf16[512,128]{1,0:T(8,128)(2,1)S(1)}, bf16[512,256]{1,0:T(8,128)(2,1)S(1)}) custom-call(s32[1]{0:T(128)} %bitcast.refs_0_.pos_ref, s32[2,4]{1,0:T(2,128)} %bitcast.48, s32[2]{0:T(128)} %bitcast.57, bf16[8,2,32,512]{3,2,1,0:T(8,128)(2,1)} %bitcast.35, ...), custom_call_target="tpu_custom_call" | custom-call | flops 1000 | bytes 1000 | tf_op jit(solution)/shard_map/pallas_call | solution.py:431
  121.9 0.1 collective-permute-start.25
  122.0 1.4 %collective-permute-start.26 = (bf16[512,128]{1,0:T(8,128)(2,1)S(1)}, bf16[512,128]{1,0:T(8,128)(2,1)S(1)}, u32[]{:S(2)}, u32[]{:S(2)}) collective-permute-start(bf16[512,128]{1,0:T(8,128)(2,1)S(1)} %get-tuple-element.104), channel_id=1, source_target_pairs={{0,17},{1,16},{2,19},{3,18},{4,21},{5,20},{6,23},{7,22},{8,25},{9,... | collective-permute-start | bytes 393224 | tf_op jit(solution)/shard_map/ppermute | solution.py:33
  123.4 3.1 %shard_map.117 = bf16[8,2,32,512]{3,2,1,0:T(8,128)(2,1)} custom-call(s32[1]{0:T(128)} %bitcast.refs_0_.pos_ref, s32[2,4]{1,0:T(2,128)} %bitcast.49, s32[2]{0:T(128)} %bitcast.58, bf16[2,512,512]{2,1,0:T(8,128)(2,1)} %bitcast.59, bf16[32,1024]{1,0:T(8,128)(2,1)S(1)} %add_convert_fusion.1.refs_4_.refs_0_, bf16[32,1024]{1,0:T(8,128)(2,1)S(1)} %add_convert_fusion.refs_5_.refs_1_), custom_call_target="tpu_custom_call" | custom-call | flops 40000000000 | bytes 1000 | tf_op jit(solution)/shard_map/pallas_call | solution.py:516
  126.5 1.1 shard_map.115.refs_4_
  127.6 0.8 shard_map.116
  (58 shorter events, 0.3 us)
Async XLA Ops:
  1.9 27.3 %copy-start.13 = (bf16[256,1024]{1,0:T(8,128)(2,1)}, bf16[256,1024]{1,0:T(8,128)(2,1)S(1)}, u32[]{:S(2)}) copy-start(bf16[256,1024]{1,0:T(8,128)(2,1)S(1)} %get-tuple-element.79) | copy-start | bytes 1572868
  1.9 27.3 %collective-permute-start = (bf16[256,1024]{1,0:T(8,128)(2,1)S(1)}, bf16[256,1024]{1,0:T(8,128)(2,1)S(1)}, u32[]{:S(2)}, u32[]{:S(2)}) collective-permute-start(bf16[256,1024]{1,0:T(8,128)(2,1)S(1)} %get-tuple-element.112), channel_id=1, source_target_pairs={{0,8},{1,9},{2,10},{3,11},{4,12},{5,13},{6,14},{7,15},{8,0},{9,1},... | collective-permute-start | bytes 1572872 | tf_op jit(solution)/shard_map/ppermute | solution.py:23
  11.7 31.5 %collective-permute-start.3 = (bf16[2048,256]{1,0:T(8,128)(2,1)S(1)}, bf16[2048,256]{1,0:T(8,128)(2,1)S(1)}, u32[]{:S(2)}, u32[]{:S(2)}) collective-permute-start(bf16[2048,256]{1,0:T(8,128)(2,1)S(1)} %get-tuple-element.61), channel_id=1, source_target_pairs={{0,2},{1,3},{2,0},{3,1},{4,6},{5,7},{6,4},{7,5},{8,10},{9,11},{10,... | collective-permute-start | bytes 3145736 | tf_op jit(solution)/shard_map/ppermute | solution.py:23
  13.3 30.0 %collective-permute-start.2 = (bf16[2176,256]{1,0:T(8,128)(2,1)S(1)}, bf16[2176,256]{1,0:T(8,128)(2,1)S(1)}, u32[]{:S(2)}, u32[]{:S(2)}) collective-permute-start(bf16[2176,256]{1,0:T(8,128)(2,1)S(1)} %get-tuple-element.60), channel_id=1, source_target_pairs={{0,1},{1,0},{2,3},{3,2},{4,5},{5,4},{6,7},{7,6},{8,9},{9,8},{10,11... | collective-permute-start | bytes 3342344 | tf_op jit(solution)/shard_map/ppermute | solution.py:23
  29.2 6.1 %copy-start.5 = (bf16[256,1024]{1,0:T(8,128)(2,1)}, bf16[256,1024]{1,0:T(8,128)(2,1)S(1)}, u32[]{:S(2)}) copy-start(bf16[256,1024]{1,0:T(8,128)(2,1)S(1)} %collective-permute-done) | copy-start | bytes 1572868
  29.2 14.1 %collective-permute-start.1 = (bf16[128,1024]{1,0:T(8,128)(2,1)S(1)}, bf16[128,1024]{1,0:T(8,128)(2,1)S(1)}, u32[]{:S(2)}, u32[]{:S(2)}) collective-permute-start(bf16[128,1024]{1,0:T(8,128)(2,1)S(1)} %slice.16), channel_id=1, source_target_pairs={{0,8},{1,9},{2,10},{3,11},{4,12},{5,13},{6,14},{7,15},{8,0},{9,1},... | collective-permute-start | bytes 786440 | tf_op jit(solution)/shard_map/ppermute | solution.py:23
  35.3 9.3 %copy-start.1 = (f32[2048,128]{1,0:T(8,128)}, f32[2048,128]{1,0:T(8,128)S(1)}, u32[]{:S(2)}) copy-start(f32[2048,128]{1,0:T(8,128)S(1)} %get-tuple-element.87.refs_0_) | copy-start | bytes 3145732
  35.3 9.3 %copy-start.3 = (f32[2048,128]{1,0:T(8,128)}, f32[2048,128]{1,0:T(8,128)S(1)}, u32[]{:S(2)}) copy-start(f32[2048,128]{1,0:T(8,128)S(1)} %get-tuple-element.88.refs_1_) | copy-start | bytes 3145732
  35.3 9.3 %copy-start.7 = (f32[32,256]{1,0:T(8,128)}, f32[32,256]{1,0:T(8,128)S(1)}, u32[]{:S(2)}) copy-start(f32[32,256]{1,0:T(8,128)S(1)} %get-tuple-element.65) | copy-start | bytes 98308
  35.3 9.3 %copy-start.9 = (bf16[2048,128]{1,0:T(8,128)(2,1)}, bf16[2048,128]{1,0:T(8,128)(2,1)S(1)}, u32[]{:S(2)}) copy-start(bf16[2048,128]{1,0:T(8,128)(2,1)S(1)} %get-tuple-element.92) | copy-start | bytes 1572868
  35.3 9.3 %copy-start.11 = (bf16[2048,128]{1,0:T(8,128)(2,1)}, bf16[2048,128]{1,0:T(8,128)(2,1)S(1)}, u32[]{:S(2)}) copy-start(bf16[2048,128]{1,0:T(8,128)(2,1)S(1)} %get-tuple-element.90) | copy-start | bytes 1572868
  43.3 4.2 %copy-start.14 = (bf16[256,1024]{1,0:T(8,128)(2,1)S(1)}, bf16[256,1024]{1,0:T(8,128)(2,1)}, u32[]{:S(2)}) copy-start(bf16[256,1024]{1,0:T(8,128)(2,1)} %copy-done.13) | copy-start | bytes 1572868
  44.6 13.9 %collective-permute-start.4 = (bf16[1152,256]{1,0:T(8,128)(2,1)}, bf16[1152,256]{1,0:T(8,128)(2,1)S(1)}, u32[]{:S(2)}, u32[]{:S(2)}) collective-permute-start(bf16[1152,256]{1,0:T(8,128)(2,1)} %get-tuple-element.73), channel_id=1, source_target_pairs={{0,2},{1,3},{2,0},{3,1},{4,6},{5,7},{6,4},{7,5},{8,10},{9,11},{10,... | collective-permute-start | bytes 1769480 | tf_op jit(solution)/shard_map/ppermute | solution.py:23
  46.0 11.8 %collective-permute-start.5 = (bf16[1024,256]{1,0:T(8,128)(2,1)}, bf16[1024,256]{1,0:T(8,128)(2,1)S(1)}, u32[]{:S(2)}, u32[]{:S(2)}) collective-permute-start(bf16[1024,256]{1,0:T(8,128)(2,1)} %get-tuple-element.74), channel_id=1, source_target_pairs={{0,1},{1,0},{2,3},{3,2},{4,5},{5,4},{6,7},{7,6},{8,9},{9,8},{10,11... | collective-permute-start | bytes 1572872 | tf_op jit(solution)/shard_map/ppermute | solution.py:23
  48.2 16.2 %collective-permute-start.6 = (bf16[128,1024]{1,0:T(8,128)(2,1)}, bf16[128,1024]{1,0:T(8,128)(2,1)}, u32[]{:S(2)}, u32[]{:S(2)}) collective-permute-start(bf16[128,1024]{1,0:T(8,128)(2,1)} %slice.17), channel_id=1, source_target_pairs={{0,8},{1,9},{2,10},{3,11},{4,12},{5,13},{6,14},{7,15},{8,0},{9,1},... | collective-permute-start | bytes 786440 | tf_op jit(solution)/shard_map/ppermute | solution.py:23
  48.8 12.7 %copy-start.8 = (f32[32,256]{1,0:T(8,128)S(1)}, f32[32,256]{1,0:T(8,128)}, u32[]{:S(2)}) copy-start(f32[32,256]{1,0:T(8,128)} %copy-done.7) | copy-start | bytes 98308
  48.8 12.7 %copy-start.15 = (f32[32,1024]{1,0:T(8,128)S(1)}, f32[32,1024]{1,0:T(8,128)}, u32[]{:S(2)}) copy-start(f32[32,1024]{1,0:T(8,128)} %constant_dynamic-update-slice_fusion.2) | copy-start | bytes 393220
  48.8 12.7 %copy-start.12 = (bf16[2048,128]{1,0:T(8,128)(2,1)S(1)}, bf16[2048,128]{1,0:T(8,128)(2,1)}, u32[]{:S(2)}) copy-start(bf16[2048,128]{1,0:T(8,128)(2,1)} %copy-done.11) | copy-start | bytes 1572868
  48.8 14.0 %copy-start.10 = (bf16[2048,128]{1,0:T(8,128)(2,1)S(1)}, bf16[2048,128]{1,0:T(8,128)(2,1)}, u32[]{:S(2)}) copy-start(bf16[2048,128]{1,0:T(8,128)(2,1)} %copy-done.9) | copy-start | bytes 1572868
  58.6 6.1 %collective-permute-start.11 = (bf16[64,256]{1,0:T(8,128)(2,1)S(1)}, bf16[64,256]{1,0:T(8,128)(2,1)S(1)}, u32[]{:S(2)}, u32[]{:S(2)}) collective-permute-start(bf16[64,256]{1,0:T(8,128)(2,1)S(1)} %bitcast.40), channel_id=1, source_target_pairs={{0,12},{1,13},{2,14},{3,15},{4,8},{5,9},{6,10},{7,11},{8,4},{9,5},... | collective-permute-start | bytes 98312 | tf_op jit(solution)/shard_map/ppermute | solution.py:23
  61.5 21.9 %collective-permute-start.18 = (bf16[2048,128]{1,0:T(8,128)(2,1)S(1)}, bf16[2048,128]{1,0:T(8,128)(2,1)S(1)}, u32[]{:S(2)}, u32[]{:S(2)}) collective-permute-start(bf16[2048,128]{1,0:T(8,128)(2,1)S(1)} %copy-done.12), channel_id=1, source_target_pairs={{0,1},{1,0},{2,3},{3,2},{4,5},{5,4},{6,7},{7,6},{8,9},{9,8},{10,11... | collective-permute-start | bytes 1572872 | tf_op jit(solution)/shard_map/ppermute | solution.py:23
  62.8 20.6 %collective-permute-start.19 = (bf16[2048,128]{1,0:T(8,128)(2,1)S(1)}, bf16[2048,128]{1,0:T(8,128)(2,1)S(1)}, u32[]{:S(2)}, u32[]{:S(2)}) collective-permute-start(bf16[2048,128]{1,0:T(8,128)(2,1)S(1)} %copy-done.10), channel_id=1, source_target_pairs={{0,2},{1,3},{2,0},{3,1},{4,6},{5,7},{6,4},{7,5},{8,10},{9,11},{10,... | collective-permute-start | bytes 1572872 | tf_op jit(solution)/shard_map/ppermute | solution.py:23
  64.4 7.9 %collective-permute-start.10 = (bf16[64,256]{1,0:T(8,128)(2,1)S(1)}, bf16[64,256]{1,0:T(8,128)(2,1)S(1)}, u32[]{:S(2)}, u32[]{:S(2)}) collective-permute-start(bf16[64,256]{1,0:T(8,128)(2,1)S(1)} %bitcast.41), channel_id=1, source_target_pairs={{0,8},{1,9},{2,10},{3,11},{4,12},{5,13},{6,14},{7,15},{8,0},{9,1},... | collective-permute-start | bytes 98312 | tf_op jit(solution)/shard_map/ppermute | solution.py:23
  64.4 15.6 %collective-permute-start.7 = (bf16[512,256]{1,0:T(8,128)(2,1)S(1)}, bf16[512,256]{1,0:T(8,128)(2,1)S(1)}, u32[]{:S(2)}, u32[]{:S(2)}) collective-permute-start(bf16[512,256]{1,0:T(8,128)(2,1)S(1)} %get-tuple-element.76), channel_id=1, source_target_pairs={{0,20},{1,21},{2,22},{3,23},{4,16},{5,17},{6,18},{7,19},{8,28},{9,... | collective-permute-start | bytes 786440 | tf_op jit(solution)/shard_map/ppermute | solution.py:33
  64.7 15.3 %collective-permute-start.8 = (bf16[512,256]{1,0:T(8,128)(2,1)S(1)}, bf16[512,256]{1,0:T(8,128)(2,1)S(1)}, u32[]{:S(2)}, u32[]{:S(2)}) collective-permute-start(bf16[512,256]{1,0:T(8,128)(2,1)S(1)} %get-tuple-element.77), channel_id=1, source_target_pairs={{0,20},{1,21},{2,22},{3,23},{4,16},{5,17},{6,18},{7,19},{8,28},{9,... | collective-permute-start | bytes 786440 | tf_op jit(solution)/shard_map/ppermute | solution.py:33
  66.1 17.3 %copy-start.2 = (f32[2048,128]{1,0:T(8,128)S(1)}, f32[2048,128]{1,0:T(8,128)}, u32[]{:S(2)}) copy-start(f32[2048,128]{1,0:T(8,128)} %copy-done.1) | copy-start | bytes 3145732
  66.1 17.3 %copy-start.4 = (f32[2048,128]{1,0:T(8,128)S(1)}, f32[2048,128]{1,0:T(8,128)}, u32[]{:S(2)}) copy-start(f32[2048,128]{1,0:T(8,128)} %copy-done.3) | copy-start | bytes 3145732
  72.2 18.8 %copy-start = (bf16[1,1,2,256,1024]{4,3,2,1,0:T(8,128)(2,1)S(1)}, bf16[1,1,2,256,1024]{4,3,2,1,0:T(8,128)(2,1)}, u32[]{:S(2)}) copy-start(bf16[1,1,2,256,1024]{4,3,2,1,0:T(8,128)(2,1)} %param.8) | copy-start | bytes 3145732
  72.2 18.8 %copy-start.6 = (bf16[256,1024]{1,0:T(8,128)(2,1)S(1)}, bf16[256,1024]{1,0:T(8,128)(2,1)}, u32[]{:S(2)}) copy-start(bf16[256,1024]{1,0:T(8,128)(2,1)} %copy-done.5) | copy-start | bytes 1572868
  72.3 7.7 %collective-permute-start.9 = (bf16[128,256]{1,0:T(8,128)(2,1)S(1)}, bf16[128,256]{1,0:T(8,128)(2,1)S(1)}, u32[]{:S(2)}, u32[]{:S(2)}) collective-permute-start(bf16[128,256]{1,0:T(8,128)(2,1)S(1)} %get-tuple-element.81.refs_7_), channel_id=1, source_target_pairs={{0,4},{1,5},{2,6},{3,7},{4,0},{5,1},{6,2},{7,3},{8,12},{9,13},{10,... | collective-permute-start | bytes 196616 | tf_op jit(solution)/shard_map/ppermute | solution.py:23
  80.0 5.7 %collective-permute-start.14 = (bf16[32,1024]{1,0:T(8,128)(2,1)S(1)}, bf16[32,1024]{1,0:T(8,128)(2,1)S(1)}, u32[]{:S(2)}, u32[]{:S(2)}) collective-permute-start(bf16[32,1024]{1,0:T(8,128)(2,1)S(1)} %convert_element_type.30), channel_id=1, source_target_pairs={{0,3},{1,2},{2,1},{3,0},{4,7},{5,6},{6,5},{7,4},{8,11},{9,10},{10,... | collective-permute-start | bytes 196616 | tf_op jit(solution)/shard_map/ppermute | solution.py:23
  81.1 5.1 %collective-permute-start.13 = (bf16[32,1024]{1,0:T(8,128)(2,1)S(1)}, bf16[32,1024]{1,0:T(8,128)(2,1)S(1)}, u32[]{:S(2)}, u32[]{:S(2)}) collective-permute-start(bf16[32,1024]{1,0:T(8,128)(2,1)S(1)} %convert_element_type.30), channel_id=1, source_target_pairs={{0,2},{1,3},{2,0},{3,1},{4,6},{5,7},{6,4},{7,5},{8,10},{9,11},{10,... | collective-permute-start | bytes 196616 | tf_op jit(solution)/shard_map/ppermute | solution.py:23
  82.0 4.3 %collective-permute-start.12 = (bf16[32,1024]{1,0:T(8,128)(2,1)S(1)}, bf16[32,1024]{1,0:T(8,128)(2,1)S(1)}, u32[]{:S(2)}, u32[]{:S(2)}) collective-permute-start(bf16[32,1024]{1,0:T(8,128)(2,1)S(1)} %convert_element_type.30), channel_id=1, source_target_pairs={{0,1},{1,0},{2,3},{3,2},{4,5},{5,4},{6,7},{7,6},{8,9},{9,8},{10,11... | collective-permute-start | bytes 196616 | tf_op jit(solution)/shard_map/ppermute | solution.py:23
  86.3 20.9 %collective-permute-start.21 = (bf16[2048,128]{1,0:T(8,128)(2,1)S(1)}, bf16[2048,128]{1,0:T(8,128)(2,1)S(1)}, u32[]{:S(2)}, u32[]{:S(2)}) collective-permute-start(bf16[2048,128]{1,0:T(8,128)(2,1)S(1)} %get-tuple-element.97), channel_id=1, source_target_pairs={{0,2},{1,3},{2,0},{3,1},{4,6},{5,7},{6,4},{7,5},{8,10},{9,11},{10,... | collective-permute-start | bytes 1572872 | tf_op jit(solution)/shard_map/ppermute | solution.py:23
  87.5 20.9 %collective-permute-start.20 = (bf16[2048,128]{1,0:T(8,128)(2,1)S(1)}, bf16[2048,128]{1,0:T(8,128)(2,1)S(1)}, u32[]{:S(2)}, u32[]{:S(2)}) collective-permute-start(bf16[2048,128]{1,0:T(8,128)(2,1)S(1)} %get-tuple-element.95), channel_id=1, source_target_pairs={{0,1},{1,0},{2,3},{3,2},{4,5},{5,4},{6,7},{7,6},{8,9},{9,8},{10,11... | collective-permute-start | bytes 1572872 | tf_op jit(solution)/shard_map/ppermute | solution.py:23
  88.3 17.2 %collective-permute-start.27 = (bf16[1024,128]{1,0:T(8,128)(2,1)S(1)}, bf16[1024,128]{1,0:T(8,128)(2,1)S(1)}, u32[]{:S(2)}, u32[]{:S(2)}) collective-permute-start(bf16[1024,128]{1,0:T(8,128)(2,1)S(1)} %get-tuple-element.93), channel_id=1, source_target_pairs={{0,2},{1,3},{2,0},{3,1},{4,6},{5,7},{6,4},{7,5},{8,10},{9,11},{10,... | collective-permute-start | bytes 786440 | tf_op jit(solution)/shard_map/ppermute | solution.py:23
  89.9 16.2 %collective-permute-start.28 = (bf16[1024,128]{1,0:T(8,128)(2,1)S(1)}, bf16[1024,128]{1,0:T(8,128)(2,1)S(1)}, u32[]{:S(2)}, u32[]{:S(2)}) collective-permute-start(bf16[1024,128]{1,0:T(8,128)(2,1)S(1)} %get-tuple-element.94), channel_id=1, source_target_pairs={{0,1},{1,0},{2,3},{3,2},{4,5},{5,4},{6,7},{7,6},{8,9},{9,8},{10,11... | collective-permute-start | bytes 786440 | tf_op jit(solution)/shard_map/ppermute | solution.py:23
  90.4 18.9 %collective-permute-start.15 = (bf16[32,1024]{1,0:T(8,128)(2,1)S(1)}, bf16[32,1024]{1,0:T(8,128)(2,1)S(1)}, u32[]{:S(2)}, u32[]{:S(2)}) collective-permute-start(bf16[32,1024]{1,0:T(8,128)(2,1)S(1)} %get-tuple-element.109), channel_id=1, source_target_pairs={{0,4},{1,5},{2,6},{3,7},{4,0},{5,1},{6,2},{7,3},{8,12},{9,13},{10,... | collective-permute-start | bytes 196616 | tf_op jit(solution)/shard_map/ppermute | solution.py:23
  106.1 17.3 %collective-permute-start.30 = (bf16[512,128]{1,0:T(8,128)(2,1)S(1)}, bf16[512,128]{1,0:T(8,128)(2,1)S(1)}, u32[]{:S(2)}, u32[]{:S(2)}) collective-permute-start(bf16[512,128]{1,0:T(8,128)(2,1)S(1)} %get-tuple-element.107), channel_id=1, source_target_pairs={{0,20},{1,21},{2,22},{3,23},{4,16},{5,17},{6,18},{7,19},{8,28},{9,... | collective-permute-start | bytes 393224 | tf_op jit(solution)/shard_map/ppermute | solution.py:33
  106.2 7.0 %collective-permute-start.17 = (bf16[32,1024]{1,0:T(8,128)(2,1)S(1)}, bf16[32,1024]{1,0:T(8,128)(2,1)S(1)}, u32[]{:S(2)}, u32[]{:S(2)}) collective-permute-start(bf16[32,1024]{1,0:T(8,128)(2,1)S(1)} %get-tuple-element.109), channel_id=1, source_target_pairs={{0,12},{1,13},{2,14},{3,15},{4,8},{5,9},{6,10},{7,11},{8,4},{9,5},... | collective-permute-start | bytes 196616 | tf_op jit(solution)/shard_map/ppermute | solution.py:23
  107.2 8.6 %collective-permute-start.16 = (bf16[32,1024]{1,0:T(8,128)(2,1)S(1)}, bf16[32,1024]{1,0:T(8,128)(2,1)S(1)}, u32[]{:S(2)}, u32[]{:S(2)}) collective-permute-start(bf16[32,1024]{1,0:T(8,128)(2,1)S(1)} %get-tuple-element.109), channel_id=1, source_target_pairs={{0,8},{1,9},{2,10},{3,11},{4,12},{5,13},{6,14},{7,15},{8,0},{9,1},... | collective-permute-start | bytes 196616 | tf_op jit(solution)/shard_map/ppermute | solution.py:23
  108.6 9.1 %collective-permute-start.22 = (bf16[1024,128]{1,0:T(8,128)(2,1)S(1)}, bf16[1024,128]{1,0:T(8,128)(2,1)S(1)}, u32[]{:S(2)}, u32[]{:S(2)}) collective-permute-start(bf16[1024,128]{1,0:T(8,128)(2,1)S(1)} %get-tuple-element.99), channel_id=1, source_target_pairs={{0,2},{1,3},{2,0},{3,1},{4,6},{5,7},{6,4},{7,5},{8,10},{9,11},{10,... | collective-permute-start | bytes 786440 | tf_op jit(solution)/shard_map/ppermute | solution.py:23
  109.3 11.2 %collective-permute-start.23 = (bf16[1024,128]{1,0:T(8,128)(2,1)S(1)}, bf16[1024,128]{1,0:T(8,128)(2,1)S(1)}, u32[]{:S(2)}, u32[]{:S(2)}) collective-permute-start(bf16[1024,128]{1,0:T(8,128)(2,1)S(1)} %get-tuple-element.101), channel_id=1, source_target_pairs={{0,4},{1,5},{2,6},{3,7},{4,0},{5,1},{6,2},{7,3},{8,12},{9,13},{10,... | collective-permute-start | bytes 786440 | tf_op jit(solution)/shard_map/ppermute | solution.py:23
  113.2 13.3 %collective-permute-start.31 = (bf16[512,128]{1,0:T(8,128)(2,1)S(1)}, bf16[512,128]{1,0:T(8,128)(2,1)S(1)}, u32[]{:S(2)}, u32[]{:S(2)}) collective-permute-start(bf16[512,128]{1,0:T(8,128)(2,1)S(1)} %get-tuple-element.108), channel_id=1, source_target_pairs={{0,20},{1,21},{2,22},{3,23},{4,16},{5,17},{6,18},{7,19},{8,28},{9,... | collective-permute-start | bytes 393224 | tf_op jit(solution)/shard_map/ppermute | solution.py:33
  117.5 9.0 %collective-permute-start.29 = (bf16[512,768]{1,0:T(8,128)(2,1)S(1)}, bf16[512,768]{1,0:T(8,128)(2,1)S(1)}, u32[]{:S(2)}, u32[]{:S(2)}) collective-permute-start(bf16[512,768]{1,0:T(8,128)(2,1)S(1)} %shard_map.113), channel_id=1, source_target_pairs={{0,16},{1,17},{2,18},{3,19},{4,20},{5,21},{6,22},{7,23},{8,24},{9,... | collective-permute-start | bytes 2359304 | tf_op jit(solution)/shard_map/ppermute | solution.py:33
  121.9 5.7 %collective-permute-start.25 = (bf16[512,128]{1,0:T(8,128)(2,1)S(1)}, bf16[512,128]{1,0:T(8,128)(2,1)S(1)}, u32[]{:S(2)}, u32[]{:S(2)}) collective-permute-start(bf16[512,128]{1,0:T(8,128)(2,1)S(1)} %get-tuple-element.103), channel_id=1, source_target_pairs={{0,20},{1,21},{2,22},{3,23},{4,16},{5,17},{6,18},{7,19},{8,28},{9,... | collective-permute-start | bytes 393224 | tf_op jit(solution)/shard_map/ppermute | solution.py:33
  122.0 5.6 %collective-permute-start.26 = (bf16[512,128]{1,0:T(8,128)(2,1)S(1)}, bf16[512,128]{1,0:T(8,128)(2,1)S(1)}, u32[]{:S(2)}, u32[]{:S(2)}) collective-permute-start(bf16[512,128]{1,0:T(8,128)(2,1)S(1)} %get-tuple-element.104), channel_id=1, source_target_pairs={{0,17},{1,16},{2,19},{3,18},{4,21},{5,20},{6,23},{7,22},{8,25},{9,... | collective-permute-start | bytes 393224 | tf_op jit(solution)/shard_map/ppermute | solution.py:33
  123.4 4.2 %collective-permute-start.24 = (bf16[512,256]{1,0:T(8,128)(2,1)S(1)}, bf16[512,256]{1,0:T(8,128)(2,1)S(1)}, u32[]{:S(2)}, u32[]{:S(2)}) collective-permute-start(bf16[512,256]{1,0:T(8,128)(2,1)S(1)} %get-tuple-element.102), channel_id=1, source_target_pairs={{0,16},{1,17},{2,18},{3,19},{4,20},{5,21},{6,22},{7,23},{8,24},{9,... | collective-permute-start | bytes 786440 | tf_op jit(solution)/shard_map/ppermute | solution.py:33

commit v9 on v8

--- a/solution.py
+++ b/solution.py
@@ -200,25 +200,27 @@
 
 def last_kernel(ways, *refs):
     kept_refs, got_refs = refs[:ways], refs[ways : 2 * ways]
-    placed_ref = refs[2 * ways] if len(refs) > 3 * ways else None
-    outs = refs[-ways - (placed_ref is not None) :]
-    for way in range(ways):
-        kept_ref, got_ref = kept_refs[way], got_refs[way]
-        half = kept_ref.shape[0] // 2
-        outs[way][...] = (
+    placed_ref = refs[2 * ways] if len(refs) > 2 * ways + 1 else None
+    out_ref = refs[2 * ways + (placed_ref is not None)]
+    start = 0
+    for kept_ref, got_ref in zip(kept_refs, got_refs):
+        half, count = kept_ref.shape[0] // 2, kept_ref.shape[1]
+        out_ref[:, start : start + count] = (
             kept_ref[half:, :] + got_ref[half : 2 * half, :].astype(F32)
         ).astype(BF16)
-        if way == 0 and placed_ref is not None:
-            outs[-1][...] = placed_ref[...] + got_ref[2 * half :, :]
+        start += count
+    if placed_ref is not None:
+        refs[-1][...] = placed_ref[...] + got_refs[0][2 * kept_refs[0].shape[0] // 2 :, :]
 
 
 def last_parts(kept, got, placed=None):
     placed = [] if placed is None else [placed]
+    shape = kept[0].shape[0] // 2, sum(k.shape[1] for k in kept)
     return pl.pallas_call(
         functools.partial(last_kernel, len(kept)),
         in_specs=[VMEM] * (2 * len(kept) + len(placed)),
-        out_specs=[VMEM] * (len(kept) + len(placed)),
-        out_shape=[jax.ShapeDtypeStruct((k.shape[0] // 2, k.shape[1]), BF16) for k in kept]
+        out_specs=[VMEM] * (1 + len(placed)),
+        out_shape=[jax.ShapeDtypeStruct(shape, BF16)]
         + [jax.ShapeDtypeStruct(p.shape, BF16) for p in placed],
         compiler_params=PARAMS,
         cost_estimate=QUICK,
@@ -314,52 +316,44 @@
         list(rows0), pieces_of(0), False, True, True, LONG
     )
     parts.append(part)
-    count = 2 if size == SEG and tile_rows >= 2 * SEG else 1
-    source, got1 = after(grad_tile[1], *got0), [[] for _ in range(1, high_size)]
-    for at in range(count):
-        span = tile_rows // count
-        rows = source[at * span : (at + 1) * span]
-        for k in range(1, high_size):
-            got1[k - 1].append(partner(rows, k * low_size)[None])
-        source = after(source, *[got[-1] for got in got1])
-    early, got1 = got1[0][0], [part for got in got1 for part in got]
+    second_rows = after(grad_tile[1], *got0)
+    got1 = [partner(second_rows, k * low_size)[None] for k in range(1, high_size)]
 
     (sent_x, sent_y), (kept_x, kept_y), placed = halve(
-        (after(kept_x, part, early), kept_y), (first_x, first_y), placed
+        (after(kept_x, part), kept_y), (first_x, first_y), placed
     )
     second_x, second_y = partner(sent_x, 2), partner(sent_y, 1)
     c_first_x = partner(after(c_sent_x, sent_x, sent_y), 1)
     c_first_y = partner(after(c_sent_y, sent_x, sent_y), 2)
 
-    chunks = [([grad_tile], own_pieces), (got0, pieces_of(0)), (got1, pieces_of(1, count))]
+    chunks = [([grad_tile], own_pieces), (got0, pieces_of(0)), (got1, pieces_of(1))]
     order = [piece for _, pieces in chunks for _, _, piece, _ in pieces]
-    *own_third, placed = last_parts((kept_x, kept_y), (second_x, second_y), placed)
-    own_last = [relay(third, 4) for third in own_third]
+    own_third, placed = last_parts((kept_x, kept_y), (second_x, second_y), placed)
+    own_last = relay(own_third, 4)
     own_sums = (kept_x, second_x), (kept_y, second_y)
-    rows1 = after(got1[0], part, *own_third), *got1[1:]
     d_sent_x, d_sent_y, d_kept_x, d_kept_y, part = produce(
-        list(rows1), pieces_of(1, count), True, True, True, LONG
+        [after(got1[0], own_third), *got1[1:]], pieces_of(1), True, True, True, LONG
     )
     parts.append(part)
+    own_rank = jnp.concatenate(parts, 1)
+    shared = after(own_rank.astype(BF16), own_last)
+    for mask in (1, 2, 3):
+        own_rank = own_rank + partner(shared, mask)
+    (c_sent_x, c_sent_y), c_kept = halve((c_kept_x, c_kept_y), (c_first_x, c_first_y))
+    c_second_x, c_second_y = partner(c_sent_x, 2), partner(c_sent_y, 1)
+    slot = own_rank, c_second_x, c_second_y
+    d_first_x, d_first_y = partner(after(d_sent_x, *slot), 1), partner(after(d_sent_y, *slot), 2)
+    shared = own_rank.astype(BF16)
+    ranks = [(own_rank + partner(shared, 4)).astype(BF16)]
+    for j in range(1, high_size):
+        one, other = partner(shared, j * low_size), partner(shared, j * low_size + 4)
+        ranks.append((one.astype(F32) + other.astype(F32)).astype(BF16))
     hiddens = [placed, partner(placed, 4)]
     for k in range(1, high_size):
         wanted = placed.reshape(micro_count, rank, tile_rows)
         wanted = lax.dynamic_slice_in_dim(wanted, (high ^ k) * rank_part, rank_part, 1)
         wanted = wanted.reshape(micro_count * rank_part, tile_rows)
         hiddens += [partner(wanted, k * low_size), partner(wanted, k * low_size + 4)]
-    own_rank = jnp.concatenate(parts, 1)
-    shared = after(own_rank.astype(BF16), *own_last, *hiddens)
-    for mask in (1, 2, 3):
-        own_rank = own_rank + partner(shared, mask)
-    (c_sent_x, c_sent_y), c_kept = halve((c_kept_x, c_kept_y), (c_first_x, c_first_y))
-    slot = own_rank, c_sent_x, c_sent_y
-    d_first_x, d_first_y = partner(after(d_sent_x, *slot), 1), partner(after(d_sent_y, *slot), 2)
-    c_second_x, c_second_y = partner(c_sent_x, 2), partner(c_sent_y, 1)
-    shared = own_rank.astype(BF16)
-    ranks = [(own_rank + partner(shared, 4)).astype(BF16)]
-    for j in range(1, high_size):
-        one, other = partner(shared, j * low_size), partner(shared, j * low_size + 4)
-        ranks.append((one.astype(F32) + other.astype(F32)).astype(BF16))
 
     all_grads, all_pieces = [], []
     for grads, pieces in chunks:
@@ -374,17 +368,8 @@
         out_shape=jax.ShapeDtypeStruct(up_tile.shape, BF16),
         scratch_shapes=[pltpu.VMEM(up_tile.shape, F32)],
         compiler_params=PARAMS,
-        cost_estimate=QUICK,
+        cost_estimate=LONG,
     )(*in_hbm(*scalars), *all_grads, *hiddens)
-
-    (d_sent_x, d_sent_y), d_kept = halve(
-        (after(d_kept_x, up_map_gradient), d_kept_y), (d_first_x, d_first_y)
-    )
-    d_second_x, d_second_y = partner(d_sent_x, 2), partner(d_sent_y, 4)
-    c_third = last_parts(c_kept, (c_second_x, c_second_y))
-    c_last = [relay(third, 4) for third in c_third]
-    c_sums = (c_kept[0], c_second_x), (c_kept[1], c_second_y)
-    d_sums = (d_kept[0], d_second_x), (d_kept[1], d_second_y)
 
     def columns_of(j, piece):
         k, m, offset = piece
@@ -486,14 +471,6 @@
             cost_estimate=QUICK,
         )(*in_hbm(scalars[0]), kept, *got, *before)
 
-    _, kept = with_adapter(own_sums + c_sums, 0, False)
-    early = relay(kept, 0)
-    d_lasts, d_kept = with_adapter(d_sums, kept.shape[1] // size, True)
-    d_last = [relay(d_lasts[0], 4), relay(d_lasts[1], 1)]
-    d_kept = relay(d_kept, 0)
-    grad_prev = finish(early, own_last + c_last, 0, None)
-    grad_prev = finish(d_kept, d_last, kept.shape[1] // size, grad_prev)
-
     def down_kernel(pos_ref, classes_ref, live_ref, inputs_ref, *refs):
         rank_refs, out_ref, total_ref = refs[:-2], refs[-2], refs[-1]
         own = pos_ref[0] // low_size
@@ -520,8 +497,26 @@
         out_shape=jax.ShapeDtypeStruct(down_parts.shape, BF16),
         scratch_shapes=[pltpu.VMEM(down_parts.shape, F32)],
         compiler_params=PARAMS,
-        cost_estimate=LONG,
+        cost_estimate=QUICK,
     )(*in_hbm(*scalars, forward_input[0]), *ranks)
+
+    (c_third,) = last_parts(c_kept, (c_second_x, c_second_y))
+    c_last = relay(c_third, 4)
+    c_sums = (c_kept[0], c_second_x), (c_kept[1], c_second_y)
+    _, kept = with_adapter(own_sums + c_sums, 0, False)
+    early = relay(kept, 0)
+    (d_sent_x, d_sent_y), d_kept = halve(
+        (after(d_kept_x, c_last, *ranks), d_kept_y), (d_first_x, d_first_y)
+    )
+    d_second_x, d_second_y = partner(d_sent_x, 2), partner(d_sent_y, 4)
+
+    d_kept_x = after(d_kept[0], down_map_gradient, kept)
+    d_sums = (d_kept_x, d_second_x), (d_kept[1], d_second_y)
+    d_lasts, d_kept = with_adapter(d_sums, kept.shape[1] // size, True)
+    d_last = [relay(d_lasts[0], 4), relay(d_lasts[1], 1)]
+    d_kept = relay(d_kept, 0)
+    grad_prev = finish(early, [own_last, c_last], 0, None)
+    grad_prev = finish(d_kept, d_last, kept.shape[1] // size, grad_prev)
 
     return (
         grad_prev[None],

time: 129 us -> 128 us (level)
  starting transfers between devices: 34.2 us -> 29.3 us
  local copies, waits for them, and re-layouts: 2.74 us -> 6.44 us
    ppermute x8 -> x6, waiting for transfers between devices: 0.02 us -> 5.5 us  [relay(): return lax.ppermute(value, ('pipe', 'tensor'), pairs)]
    ppermute x24 -> x23, starting transfers between devices: 31.1 us -> 26.1 us  [partner(): return lax.ppermute(value, 'tensor', pairs)]
    ppermute x24 -> x23, waiting for transfers between devices: 54.1 us -> 49.4 us  [partner(): return lax.ppermute(value, 'tensor', pairs)]
    unnamed x34 -> x46, local copies, waits for them, and re-layouts: 0.71 us -> 4.37 us
    ppermute x8 -> x6, starting transfers between devices: 3.1 us -> 3.16 us  [relay(): return lax.ppermute(value, ('pipe', 'tensor'), pairs)]
  transfers between devices with their start and end apart: 32 -> 29, of which waited for: 13 -> 14; matrix products, arithmetic and copies ran while one was open for 1% -> 0% of each run, Pallas kernels for 27% -> 27%
where the time goes in v9:
time: 128 us
  waiting for transfers between devices  54.9 us (43%)
  Pallas kernels  36 us (28%)
  starting transfers between devices  29.3 us (23%)
  local copies, waits for them, and re-layouts  6.44 us (5%)
    ppermute x23, waiting for transfers between devices, partner(): return lax.ppermute(value, 'tensor', pairs)  49.4 us
    ppermute x23, starting transfers between devices, partner(): return lax.ppermute(value, 'tensor', pairs)  26.1 us
    pallas_call x4, Pallas kernels, product(): pl.pallas_call(functools.partial(product_body, low_size, tile_rows, piece...  23.7 us
    ppermute x6, waiting for transfers between devices, relay(): return lax.ppermute(value, ('pipe', 'tensor'), pairs)  5.5 us
    unnamed x46, local copies, waits for them, and re-layouts  4.37 us
    pallas_call x2, Pallas kernels, with_adapter(): pl.pallas_call(functools.partial(adapter_kernel, first, with_last, len(su...  3.47 us
    ppermute x6, starting transfers between devices, relay(): return lax.ppermute(value, ('pipe', 'tensor'), pairs)  3.16 us
    pallas_call x1, Pallas kernels, shards(): pl.pallas_call(down_kernel, in_specs=[SMEM] * 3 + [VMEM] * (1 + high_size...  2.94 us
  transfers between devices with their start and end apart: 29, of which 14 were waited for; matrix products, arithmetic and copies ran while one was open for 0% of the time, Pallas kernels for 27%

profile of v9, /device:TPU:0, one launch (start us, length us, event | category | flops | bytes accessed | tf_op | source)
XLA Modules:
  0.0 127.7 jit_solution(2335859347213503447)
XLA Ops:
  0.6 2.1 %slice_bitcast_fusion = (bf16[256,1024]{1,0:T(8,128)(2,1)}, bf16[256,1024]{1,0:T(8,128)(2,1)S(1)}) fusion(bf16[1,1,2,256,1024]{4,3,2,1,0:T(8,128)(2,1)} %param.8), kind=kLoop, calls=%fused_computation | loop fusion | bytes 2097152 | tf_op jit(solution)/shard_map/squeeze | solution.py:319
  2.7 4.0 %collective-permute-start = (bf16[256,1024]{1,0:T(8,128)(2,1)S(1)}, bf16[256,1024]{1,0:T(8,128)(2,1)S(1)}, u32[]{:S(2)}, u32[]{:S(2)}) collective-permute-start(bf16[256,1024]{1,0:T(8,128)(2,1)S(1)} %get-tuple-element.106), channel_id=1, source_target_pairs={{0,8},{1,9},{2,10},{3,11},{4,12},{5,13},{6,14},{7,15},{8,0},{9,1},... | collective-permute-start | bytes 1572872 | tf_op jit(solution)/shard_map/ppermute | solution.py:23
  6.7 5.7 %shard_map.103 = (bf16[2176,256]{1,0:T(8,128)(2,1)S(1)}, bf16[2048,256]{1,0:T(8,128)(2,1)S(1)}, bf16[128,256]{1,0:T(8,128)(2,1)S(1)}) custom-call(s32[1]{0:T(128)} %bitcast.refs_0_.pos_ref, s32[2,4]{1,0:T(2,128)} %bitcast.42, s32[2]{0:T(128)} %bitcast.51, bf16[2,256,1024]{2,1,0:T(8,128)(2,1)} %bitcast.20, bf16[8,512,1024]{2,1,0:T(8,128)(2,1)} %bitcast.28, ...), custom_call_target="tpu_custom_call" | custom-call | flops 1000 | bytes 1000 | tf_op jit(solution)/shard_map/pallas_call | solution.py:140
  12.5 1.6 %collective-permute-start.2 = (bf16[2176,256]{1,0:T(8,128)(2,1)S(1)}, bf16[2176,256]{1,0:T(8,128)(2,1)S(1)}, u32[]{:S(2)}, u32[]{:S(2)}) collective-permute-start(bf16[2176,256]{1,0:T(8,128)(2,1)S(1)} %get-tuple-element.57), channel_id=1, source_target_pairs={{0,1},{1,0},{2,3},{3,2},{4,5},{5,4},{6,7},{7,6},{8,9},{9,8},{10,11... | collective-permute-start | bytes 3342344 | tf_op jit(solution)/shard_map/ppermute | solution.py:23
  14.0 1.5 %collective-permute-start.3 = (bf16[2048,256]{1,0:T(8,128)(2,1)S(1)}, bf16[2048,256]{1,0:T(8,128)(2,1)S(1)}, u32[]{:S(2)}, u32[]{:S(2)}) collective-permute-start(bf16[2048,256]{1,0:T(8,128)(2,1)S(1)} %get-tuple-element.58), channel_id=1, source_target_pairs={{0,2},{1,3},{2,0},{3,1},{4,6},{5,7},{6,4},{7,5},{8,10},{9,11},{10,... | collective-permute-start | bytes 3145736 | tf_op jit(solution)/shard_map/ppermute | solution.py:23
  15.5 5.8 %shard_map.104 = (f32[2048,256]{1,0:T(8,128)S(1)}, f32[2048,256]{1,0:T(8,128)S(1)}, f32[32,512]{1,0:T(8,128)S(1)}) custom-call(s32[1]{0:T(128)} %bitcast.refs_0_.pos_ref, s32[2,4]{1,0:T(2,128)} %bitcast.43, s32[2]{0:T(128)} %bitcast.52, bf16[2,256,1024]{2,1,0:T(8,128)(2,1)} %bitcast.21, bf16[8,512,1024]{2,1,0:T(8,128)(2,1)} %bitcast.29, ...), custom_call_target="tpu_custom_call" | custom-call | flops 1000 | bytes 1000 | tf_op jit(solution)/shard_map/pallas_call | solution.py:140
  21.4 8.5 %collective-permute-done = bf16[256,1024]{1,0:T(8,128)(2,1)S(1)} collective-permute-done((bf16[256,1024]{1,0:T(8,128)(2,1)S(1)}, bf16[256,1024]{1,0:T(8,128)(2,1)S(1)}, u32[]{:S(2)}, u32[]{:S(2)}) %collective-permute-start) | collective-permute-done | bytes 524320 | tf_op jit(solution)/shard_map/ppermute | solution.py:23
  29.9 6.1 %shard_map.105 = (bf16[2048,128]{1,0:T(8,128)(2,1)S(1)}, bf16[2048,128]{1,0:T(8,128)(2,1)S(1)}, f32[2048,128]{1,0:T(8,128)S(1)}, f32[2048,128]{1,0:T(8,128)S(1)}, f32[32,256]{1,0:T(8,128)S(1)}) custom-call(s32[1]{0:T(128)} %bitcast.refs_0_.pos_ref, s32[2,4]{1,0:T(2,128)} %bitcast.44, s32[2]{0:T(128)} %bitcast.53, bf16[1,256,1024]{2,1,0:T(8,128)(2,1)S(1)} %bitcast.24, ...), custom_call_target="tpu_custom_call" | custom-call | flops 40000000000 | bytes 1000 | tf_op jit(solution)/shard_map/pallas_call | solution.py:140
  36.0 2.4 %collective-permute-done.3.refs_3_ = bf16[2048,256]{1,0:T(8,128)(2,1)S(1)} collective-permute-done((bf16[2048,256]{1,0:T(8,128)(2,1)S(1)}, bf16[2048,256]{1,0:T(8,128)(2,1)S(1)}, u32[]{:S(2)}, u32[]{:S(2)}) %collective-permute-start.3) | collective-permute-done | bytes 1048608 | tf_op jit(solution)/shard_map/ppermute | solution.py:23
  38.4 0.2 collective-permute-done.2.refs_2_
  38.5 0.3 shard_map.106
  38.9 1.6 %collective-permute-start.4 = (bf16[1152,256]{1,0:T(8,128)(2,1)S(1)}, bf16[1152,256]{1,0:T(8,128)(2,1)S(1)}, u32[]{:S(2)}, u32[]{:S(2)}) collective-permute-start(bf16[1152,256]{1,0:T(8,128)(2,1)S(1)} %get-tuple-element.70), channel_id=1, source_target_pairs={{0,2},{1,3},{2,0},{3,1},{4,6},{5,7},{6,4},{7,5},{8,10},{9,11},{10,... | collective-permute-start | bytes 1769480 | tf_op jit(solution)/shard_map/ppermute | solution.py:23
  40.5 1.5 %collective-permute-start.5 = (bf16[1024,256]{1,0:T(8,128)(2,1)S(1)}, bf16[1024,256]{1,0:T(8,128)(2,1)S(1)}, u32[]{:S(2)}, u32[]{:S(2)}) collective-permute-start(bf16[1024,256]{1,0:T(8,128)(2,1)S(1)} %get-tuple-element.71), channel_id=1, source_target_pairs={{0,1},{1,0},{2,3},{3,2},{4,5},{5,4},{6,7},{7,6},{8,9},{9,8},{10,11... | collective-permute-start | bytes 1572872 | tf_op jit(solution)/shard_map/ppermute | solution.py:23
  42.0 0.3 collective-permute-start.1
  42.3 0.6 collective-permute-start.14
  42.9 0.5 collective-permute-start.13
  43.4 12.0 %collective-permute-done.5.refs_3_.refs_9_ = bf16[1024,256]{1,0:T(8,128)(2,1)S(1)} collective-permute-done((bf16[1024,256]{1,0:T(8,128)(2,1)S(1)}, bf16[1024,256]{1,0:T(8,128)(2,1)S(1)}, u32[]{:S(2)}, u32[]{:S(2)}) %collective-permute-start.5) | collective-permute-done | bytes 524320 | tf_op jit(solution)/shard_map/ppermute | solution.py:23
  55.3 0.0 collective-permute-done.4.refs_2_.refs_7_
  55.3 0.1 shard_map.107
  55.4 0.1 collective-permute-start.6
  55.5 10.6 %collective-permute-done.1 = bf16[256,1024]{1,0:T(8,128)(2,1)S(1)} collective-permute-done((bf16[256,1024]{1,0:T(8,128)(2,1)S(1)}, bf16[256,1024]{1,0:T(8,128)(2,1)S(1)}, u32[]{:S(2)}, u32[]{:S(2)}) %collective-permute-start.1) | collective-permute-done | bytes 524320 | tf_op jit(solution)/shard_map/ppermute | solution.py:23
  66.1 6.1 %shard_map.108 = (bf16[2048,128]{1,0:T(8,128)(2,1)S(1)}, bf16[2048,128]{1,0:T(8,128)(2,1)S(1)}, f32[2048,128]{1,0:T(8,128)S(1)}, f32[2048,128]{1,0:T(8,128)S(1)}, f32[32,256]{1,0:T(8,128)S(1)}) custom-call(s32[1]{0:T(128)} %bitcast.refs_0_.pos_ref, s32[2,4]{1,0:T(2,128)} %bitcast.45, s32[2]{0:T(128)} %bitcast.54, bf16[1,256,1024]{2,1,0:T(8,128)(2,1)S(1)} %bitcast.26, ...), custom_call_target="tpu_custom_call" | custom-call | flops 40000000000 | bytes 1000 | tf_op jit(solution)/shard_map/pallas_call | solution.py:140
  72.2 5.0 %collective-permute-done.6.refs_2_ = bf16[512,512]{1,0:T(8,128)(2,1)S(1)} collective-permute-done((bf16[512,512]{1,0:T(8,128)(2,1)S(1)}, bf16[512,512]{1,0:T(8,128)(2,1)S(1)}, u32[]{:S(2)}, u32[]{:S(2)}) %collective-permute-start.6) | collective-permute-done | bytes 524320 | tf_op jit(solution)/shard_map/ppermute | solution.py:33
  77.2 0.8 copy-done.13
  78.1 0.5 collective-permute-start.7
  78.6 0.7 collective-permute-start.8
  79.2 2.3 %collective-permute-start.9 = (bf16[32,1024]{1,0:T(8,128)(2,1)S(1)}, bf16[32,1024]{1,0:T(8,128)(2,1)S(1)}, u32[]{:S(2)}, u32[]{:S(2)}) collective-permute-start(bf16[32,1024]{1,0:T(8,128)(2,1)S(1)} %convert_element_type.30), channel_id=1, source_target_pairs={{0,3},{1,2},{2,1},{3,0},{4,7},{5,6},{6,5},{7,4},{8,11},{9,10},{10,... | collective-permute-start | bytes 196616 | tf_op jit(solution)/shard_map/ppermute | solution.py:23
  81.6 0.2 shard_map.109
  81.7 0.6 collective-permute-start.15
  82.3 0.7 collective-permute-start.16
  83.0 0.5 collective-permute-done.8
  83.6 1.0 collective-permute-done.9
  84.6 0.1 collective-permute-start.11
  84.6 1.9 %collective-permute-start.12 = (bf16[32,1024]{1,0:T(8,128)(2,1)S(1)}, bf16[32,1024]{1,0:T(8,128)(2,1)S(1)}, u32[]{:S(2)}, u32[]{:S(2)}) collective-permute-start(bf16[32,1024]{1,0:T(8,128)(2,1)S(1)} %get-tuple-element.103), channel_id=1, source_target_pairs={{0,12},{1,13},{2,14},{3,15},{4,8},{5,9},{6,10},{7,11},{8,4},{9,5},... | collective-permute-start | bytes 196616 | tf_op jit(solution)/shard_map/ppermute | solution.py:23
  86.5 3.5 %collective-permute-done.15.refs_2_.refs_11_ = bf16[1024,128]{1,0:T(8,128)(2,1)S(1)} collective-permute-done((bf16[1024,128]{1,0:T(8,128)(2,1)S(1)}, bf16[1024,128]{1,0:T(8,128)(2,1)S(1)}, u32[]{:S(2)}, u32[]{:S(2)}) %collective-permute-start.15) | collective-permute-done | bytes 262176 | tf_op jit(solution)/shard_map/ppermute | solution.py:23
  90.0 1.0 collective-permute-start.19
  91.0 0.9 collective-permute-start.18
  92.0 0.1 shard_map.110
  92.0 0.1 collective-permute-start.17
  92.1 0.3 collective-permute-start.10
  92.5 7.4 %collective-permute-done.10 = bf16[32,1024]{1,0:T(8,128)(2,1)S(1)} collective-permute-done((bf16[32,1024]{1,0:T(8,128)(2,1)S(1)}, bf16[32,1024]{1,0:T(8,128)(2,1)S(1)}, u32[]{:S(2)}, u32[]{:S(2)}) %collective-permute-start.10) | collective-permute-done | bytes 65568 | tf_op jit(solution)/shard_map/ppermute | solution.py:23
  99.9 0.4 collective-permute-done.17.refs_3_
  100.3 2.6 %collective-permute-done.19.refs_3_ = bf16[2048,128]{1,0:T(8,128)(2,1)S(1)} collective-permute-done((bf16[2048,128]{1,0:T(8,128)(2,1)S(1)}, bf16[2048,128]{1,0:T(8,128)(2,1)S(1)}, u32[]{:S(2)}, u32[]{:S(2)}) %collective-permute-start.19) | collective-permute-done | bytes 524320 | tf_op jit(solution)/shard_map/ppermute | solution.py:23
  103.0 0.7 collective-permute-done.18.refs_2_
  103.6 0.9 shard_map.111
  104.6 0.8 copy-done.9
  105.4 0.8 copy-done.11
  106.2 1.1 collective-permute-start.20
  107.3 2.0 %collective-permute-start.26 = (bf16[128,256]{1,0:T(8,128)(2,1)S(1)}, bf16[128,256]{1,0:T(8,128)(2,1)S(1)}, u32[]{:S(2)}, u32[]{:S(2)}) collective-permute-start(bf16[128,256]{1,0:T(8,128)(2,1)S(1)} %get-tuple-element.102.refs_6_), channel_id=1, source_target_pairs={{0,4},{1,5},{2,6},{3,7},{4,0},{5,1},{6,2},{7,3},{8,12},{9,13},{10,... | collective-permute-start | bytes 196616 | tf_op jit(solution)/shard_map/ppermute | solution.py:23
  109.3 2.4 %collective-permute-start.28 = (bf16[64,256]{1,0:T(8,128)(2,1)S(1)}, bf16[64,256]{1,0:T(8,128)(2,1)S(1)}, u32[]{:S(2)}, u32[]{:S(2)}) collective-permute-start(bf16[64,256]{1,0:T(8,128)(2,1)S(1)} %bitcast.41), channel_id=1, source_target_pairs={{0,12},{1,13},{2,14},{3,15},{4,8},{5,9},{6,10},{7,11},{8,4},{9,5},... | collective-permute-start | bytes 98312 | tf_op jit(solution)/shard_map/ppermute | solution.py:23
  111.7 2.9 %shard_map.112 = bf16[8,2,32,512]{3,2,1,0:T(8,128)(2,1)} custom-call(s32[1]{0:T(128)} %bitcast.refs_0_.pos_ref, s32[2,4]{1,0:T(2,128)} %bitcast.46, s32[2]{0:T(128)} %bitcast.55, bf16[2,512,512]{2,1,0:T(8,128)(2,1)} %bitcast.35, bf16[32,1024]{1,0:T(8,128)(2,1)S(1)} %add_convert_fusion.1.refs_0_.refs_4_, bf16[32,1024]{1,0:T(8,128)(2,1)S(1)} %add_convert_fusion.refs_1_.refs_5_), custom_call_target="tpu_custom_call" | custom-call | flops 1000 | bytes 1000 | tf_op jit(solution)/shard_map/pallas_call | solution.py:493
  114.7 0.9 copy-done.6
  115.6 0.9 copy-done.8
  116.6 1.8 %shard_map.113 = bf16[512,768]{1,0:T(8,128)(2,1)S(1)} custom-call(s32[1]{0:T(128)} %bitcast.refs_0_.pos_ref, s32[2,4]{1,0:T(2,128)} %bitcast.47, s32[2]{0:T(128)} %bitcast.56, bf16[8,2,32,512]{3,2,1,0:T(8,128)(2,1)} %bitcast.33, bf16[32,1024]{1,0:T(8,128)(2,1)S(1)} %add_convert_fusion.1.refs_0_.refs_4_, ...), custom_call_target="tpu_custom_call" | custom-call | flops 1000 | bytes 1000 | tf_op jit(solution)/shard_map/pallas_call | solution.py:416
  118.4 0.0 copy-start
  118.4 0.1 collective-permute-start.25
  118.5 1.7 %shard_map.114 = (bf16[512,128]{1,0:T(8,128)(2,1)S(1)}, bf16[512,128]{1,0:T(8,128)(2,1)S(1)}, bf16[512,256]{1,0:T(8,128)(2,1)S(1)}) custom-call(s32[1]{0:T(128)} %bitcast.refs_0_.pos_ref, s32[2,4]{1,0:T(2,128)} %bitcast.48, s32[2]{0:T(128)} %bitcast.57, bf16[8,2,32,512]{3,2,1,0:T(8,128)(2,1)} %bitcast.34, ...), custom_call_target="tpu_custom_call" | custom-call | flops 1000 | bytes 1000 | tf_op jit(solution)/shard_map/pallas_call | solution.py:416
  120.2 0.4 collective-permute-start.22
  120.6 0.8 collective-permute-start.23
  121.5 1.7 %collective-permute-start.24 = (bf16[512,128]{1,0:T(8,128)(2,1)S(1)}, bf16[512,128]{1,0:T(8,128)(2,1)S(1)}, u32[]{:S(2)}, u32[]{:S(2)}) collective-permute-start(bf16[512,128]{1,0:T(8,128)(2,1)S(1)} %get-tuple-element.101), channel_id=1, source_target_pairs={{0,17},{1,16},{2,19},{3,18},{4,21},{5,20},{6,23},{7,22},{8,25},{9,... | collective-permute-start | bytes 393224 | tf_op jit(solution)/shard_map/ppermute | solution.py:33
  123.2 2.4 %shard_map.117 = bf16[8,32,1024]{2,1,0:T(8,128)(2,1)} custom-call(s32[1]{0:T(128)} %bitcast.refs_0_.pos_ref, s32[2,4]{1,0:T(2,128)} %bitcast.49, s32[2]{0:T(128)} %bitcast.58, bf16[2,256,1024]{2,1,0:T(8,128)(2,1)S(1)} %bitcast.22, bf16[1,256,1024]{2,1,0:T(8,128)(2,1)S(1)} %bitcast.25, bf16[1,256,1024]{2,1,0:T(8,128)(2,1)S(1)} %bitcast.27, ...), custom_call_target="tpu_custom_call" | custom-call | flops 40000000000 | bytes 1000 | tf_op jit(solution)/shard_map/pallas_call | solution.py:362
  125.6 1.1 shard_map.115.refs_4_
  126.7 0.1 collective-permute-done.24.refs_3_
  126.8 0.8 shard_map.116
  (62 shorter events, 0.2 us)
Async XLA Ops:
  2.7 27.2 %collective-permute-start = (bf16[256,1024]{1,0:T(8,128)(2,1)S(1)}, bf16[256,1024]{1,0:T(8,128)(2,1)S(1)}, u32[]{:S(2)}, u32[]{:S(2)}) collective-permute-start(bf16[256,1024]{1,0:T(8,128)(2,1)S(1)} %get-tuple-element.106), channel_id=1, source_target_pairs={{0,8},{1,9},{2,10},{3,11},{4,12},{5,13},{6,14},{7,15},{8,0},{9,1},... | collective-permute-start | bytes 1572872 | tf_op jit(solution)/shard_map/ppermute | solution.py:23
  12.5 26.1 %collective-permute-start.2 = (bf16[2176,256]{1,0:T(8,128)(2,1)S(1)}, bf16[2176,256]{1,0:T(8,128)(2,1)S(1)}, u32[]{:S(2)}, u32[]{:S(2)}) collective-permute-start(bf16[2176,256]{1,0:T(8,128)(2,1)S(1)} %get-tuple-element.57), channel_id=1, source_target_pairs={{0,1},{1,0},{2,3},{3,2},{4,5},{5,4},{6,7},{7,6},{8,9},{9,8},{10,11... | collective-permute-start | bytes 3342344 | tf_op jit(solution)/shard_map/ppermute | solution.py:23
  14.0 24.3 %collective-permute-start.3 = (bf16[2048,256]{1,0:T(8,128)(2,1)S(1)}, bf16[2048,256]{1,0:T(8,128)(2,1)S(1)}, u32[]{:S(2)}, u32[]{:S(2)}) collective-permute-start(bf16[2048,256]{1,0:T(8,128)(2,1)S(1)} %get-tuple-element.58), channel_id=1, source_target_pairs={{0,2},{1,3},{2,0},{3,1},{4,6},{5,7},{6,4},{7,5},{8,10},{9,11},{10,... | collective-permute-start | bytes 3145736 | tf_op jit(solution)/shard_map/ppermute | solution.py:23
  29.9 6.1 %copy-start.17 = (bf16[256,1024]{1,0:T(8,128)(2,1)}, bf16[256,1024]{1,0:T(8,128)(2,1)S(1)}, u32[]{:S(2)}) copy-start(bf16[256,1024]{1,0:T(8,128)(2,1)S(1)} %collective-permute-done) | copy-start | bytes 1572868
  38.5 3.4 %copy-start.21 = (bf16[256,1024]{1,0:T(8,128)(2,1)S(1)}, bf16[256,1024]{1,0:T(8,128)(2,1)}, u32[]{:S(2)}) copy-start(bf16[256,1024]{1,0:T(8,128)(2,1)} %get-tuple-element.63) | copy-start | bytes 1572868
  38.9 16.4 %collective-permute-start.4 = (bf16[1152,256]{1,0:T(8,128)(2,1)S(1)}, bf16[1152,256]{1,0:T(8,128)(2,1)S(1)}, u32[]{:S(2)}, u32[]{:S(2)}) collective-permute-start(bf16[1152,256]{1,0:T(8,128)(2,1)S(1)} %get-tuple-element.70), channel_id=1, source_target_pairs={{0,2},{1,3},{2,0},{3,1},{4,6},{5,7},{6,4},{7,5},{8,10},{9,11},{10,... | collective-permute-start | bytes 1769480 | tf_op jit(solution)/shard_map/ppermute | solution.py:23
  40.5 14.9 %collective-permute-start.5 = (bf16[1024,256]{1,0:T(8,128)(2,1)S(1)}, bf16[1024,256]{1,0:T(8,128)(2,1)S(1)}, u32[]{:S(2)}, u32[]{:S(2)}) collective-permute-start(bf16[1024,256]{1,0:T(8,128)(2,1)S(1)} %get-tuple-element.71), channel_id=1, source_target_pairs={{0,1},{1,0},{2,3},{3,2},{4,5},{5,4},{6,7},{7,6},{8,9},{9,8},{10,11... | collective-permute-start | bytes 1572872 | tf_op jit(solution)/shard_map/ppermute | solution.py:23
  42.0 24.2 %collective-permute-start.1 = (bf16[256,1024]{1,0:T(8,128)(2,1)S(1)}, bf16[256,1024]{1,0:T(8,128)(2,1)S(1)}, u32[]{:S(2)}, u32[]{:S(2)}) collective-permute-start(bf16[256,1024]{1,0:T(8,128)(2,1)S(1)} %copy-done.21), channel_id=1, source_target_pairs={{0,8},{1,9},{2,10},{3,11},{4,12},{5,13},{6,14},{7,15},{8,0},{9,1},... | collective-permute-start | bytes 1572872 | tf_op jit(solution)/shard_map/ppermute | solution.py:23
  42.3 39.2 %collective-permute-start.14 = (bf16[2048,128]{1,0:T(8,128)(2,1)S(1)}, bf16[2048,128]{1,0:T(8,128)(2,1)S(1)}, u32[]{:S(2)}, u32[]{:S(2)}) collective-permute-start(bf16[2048,128]{1,0:T(8,128)(2,1)S(1)} %get-tuple-element.83), channel_id=1, source_target_pairs={{0,2},{1,3},{2,0},{3,1},{4,6},{5,7},{6,4},{7,5},{8,10},{9,11},{10,... | collective-permute-start | bytes 1572872 | tf_op jit(solution)/shard_map/ppermute | solution.py:23
  42.9 38.7 %collective-permute-start.13 = (bf16[2048,128]{1,0:T(8,128)(2,1)S(1)}, bf16[2048,128]{1,0:T(8,128)(2,1)S(1)}, u32[]{:S(2)}, u32[]{:S(2)}) collective-permute-start(bf16[2048,128]{1,0:T(8,128)(2,1)S(1)} %get-tuple-element.81), channel_id=1, source_target_pairs={{0,1},{1,0},{2,3},{3,2},{4,5},{5,4},{6,7},{7,6},{8,9},{9,8},{10,11... | collective-permute-start | bytes 1572872 | tf_op jit(solution)/shard_map/ppermute | solution.py:23
  55.4 21.8 %collective-permute-start.6 = (bf16[512,512]{1,0:T(8,128)(2,1)S(1)}, bf16[512,512]{1,0:T(8,128)(2,1)S(1)}, u32[]{:S(2)}, u32[]{:S(2)}) collective-permute-start(bf16[512,512]{1,0:T(8,128)(2,1)S(1)} %get-tuple-element.73), channel_id=1, source_target_pairs={{0,20},{1,21},{2,22},{3,23},{4,16},{5,17},{6,18},{7,19},{8,28},{9,... | collective-permute-start | bytes 1572872 | tf_op jit(solution)/shard_map/ppermute | solution.py:33
  66.1 6.1 %copy-start.19 = (bf16[256,1024]{1,0:T(8,128)(2,1)}, bf16[256,1024]{1,0:T(8,128)(2,1)S(1)}, u32[]{:S(2)}) copy-start(bf16[256,1024]{1,0:T(8,128)(2,1)S(1)} %collective-permute-done.1) | copy-start | bytes 1572868
  77.2 0.8 copy-start.13
  78.1 4.9 %collective-permute-start.7 = (bf16[32,1024]{1,0:T(8,128)(2,1)S(1)}, bf16[32,1024]{1,0:T(8,128)(2,1)S(1)}, u32[]{:S(2)}, u32[]{:S(2)}) collective-permute-start(bf16[32,1024]{1,0:T(8,128)(2,1)S(1)} %convert_element_type.30), channel_id=1, source_target_pairs={{0,1},{1,0},{2,3},{3,2},{4,5},{5,4},{6,7},{7,6},{8,9},{9,8},{10,11... | collective-permute-start | bytes 196616 | tf_op jit(solution)/shard_map/ppermute | solution.py:23
  78.6 5.0 %collective-permute-start.8 = (bf16[32,1024]{1,0:T(8,128)(2,1)S(1)}, bf16[32,1024]{1,0:T(8,128)(2,1)S(1)}, u32[]{:S(2)}, u32[]{:S(2)}) collective-permute-start(bf16[32,1024]{1,0:T(8,128)(2,1)S(1)} %convert_element_type.30), channel_id=1, source_target_pairs={{0,2},{1,3},{2,0},{3,1},{4,6},{5,7},{6,4},{7,5},{8,10},{9,11},{10,... | collective-permute-start | bytes 196616 | tf_op jit(solution)/shard_map/ppermute | solution.py:23
  79.2 5.3 %collective-permute-start.9 = (bf16[32,1024]{1,0:T(8,128)(2,1)S(1)}, bf16[32,1024]{1,0:T(8,128)(2,1)S(1)}, u32[]{:S(2)}, u32[]{:S(2)}) collective-permute-start(bf16[32,1024]{1,0:T(8,128)(2,1)S(1)} %convert_element_type.30), channel_id=1, source_target_pairs={{0,3},{1,2},{2,1},{3,0},{4,7},{5,6},{6,5},{7,4},{8,11},{9,10},{10,... | collective-permute-start | bytes 196616 | tf_op jit(solution)/shard_map/ppermute | solution.py:23
  81.7 10.2 %copy-start.1 = (f32[1024,128]{1,0:T(8,128)}, f32[1024,128]{1,0:T(8,128)S(1)}, u32[]{:S(2)}) copy-start(f32[1024,128]{1,0:T(8,128)S(1)} %get-tuple-element.84.refs_0_.refs_10_) | copy-start | bytes 1572868
  81.7 10.3 %copy-start.3 = (f32[1024,128]{1,0:T(8,128)}, f32[1024,128]{1,0:T(8,128)S(1)}, u32[]{:S(2)}) copy-start(f32[1024,128]{1,0:T(8,128)S(1)} %get-tuple-element.85.refs_1_.refs_12_) | copy-start | bytes 1572868
  81.7 8.3 %collective-permute-start.15 = (bf16[1024,128]{1,0:T(8,128)(2,1)S(1)}, bf16[1024,128]{1,0:T(8,128)(2,1)S(1)}, u32[]{:S(2)}, u32[]{:S(2)}) collective-permute-start(bf16[1024,128]{1,0:T(8,128)(2,1)S(1)} %get-tuple-element.86), channel_id=1, source_target_pairs={{0,2},{1,3},{2,0},{3,1},{4,6},{5,7},{6,4},{7,5},{8,10},{9,11},{10,... | collective-permute-start | bytes 786440 | tf_op jit(solution)/shard_map/ppermute | solution.py:23
  82.3 7.7 %collective-permute-start.16 = (bf16[1024,128]{1,0:T(8,128)(2,1)S(1)}, bf16[1024,128]{1,0:T(8,128)(2,1)S(1)}, u32[]{:S(2)}, u32[]{:S(2)}) collective-permute-start(bf16[1024,128]{1,0:T(8,128)(2,1)S(1)} %get-tuple-element.87), channel_id=1, source_target_pairs={{0,1},{1,0},{2,3},{3,2},{4,5},{5,4},{6,7},{7,6},{8,9},{9,8},{10,11... | collective-permute-start | bytes 786440 | tf_op jit(solution)/shard_map/ppermute | solution.py:23
  84.6 7.6 %collective-permute-start.11 = (bf16[32,1024]{1,0:T(8,128)(2,1)S(1)}, bf16[32,1024]{1,0:T(8,128)(2,1)S(1)}, u32[]{:S(2)}, u32[]{:S(2)}) collective-permute-start(bf16[32,1024]{1,0:T(8,128)(2,1)S(1)} %get-tuple-element.103), channel_id=1, source_target_pairs={{0,8},{1,9},{2,10},{3,11},{4,12},{5,13},{6,14},{7,15},{8,0},{9,1},... | collective-permute-start | bytes 196616 | tf_op jit(solution)/shard_map/ppermute | solution.py:23
  84.6 7.8 %collective-permute-start.12 = (bf16[32,1024]{1,0:T(8,128)(2,1)S(1)}, bf16[32,1024]{1,0:T(8,128)(2,1)S(1)}, u32[]{:S(2)}, u32[]{:S(2)}) collective-permute-start(bf16[32,1024]{1,0:T(8,128)(2,1)S(1)} %get-tuple-element.103), channel_id=1, source_target_pairs={{0,12},{1,13},{2,14},{3,15},{4,8},{5,9},{6,10},{7,11},{8,4},{9,5},... | collective-permute-start | bytes 196616 | tf_op jit(solution)/shard_map/ppermute | solution.py:23
  90.0 14.6 %copy-start.5 = (bf16[1024,128]{1,0:T(8,128)(2,1)}, bf16[1024,128]{1,0:T(8,128)(2,1)S(1)}, u32[]{:S(2)}) copy-start(bf16[1024,128]{1,0:T(8,128)(2,1)S(1)} %collective-permute-done.15.refs_2_.refs_11_) | copy-start | bytes 786436
  90.0 14.6 %copy-start.7 = (bf16[1024,128]{1,0:T(8,128)(2,1)}, bf16[1024,128]{1,0:T(8,128)(2,1)S(1)}, u32[]{:S(2)}) copy-start(bf16[1024,128]{1,0:T(8,128)(2,1)S(1)} %collective-permute-done.16.refs_3_.refs_13_) | copy-start | bytes 786436
  90.0 12.9 %collective-permute-start.19 = (bf16[2048,128]{1,0:T(8,128)(2,1)S(1)}, bf16[2048,128]{1,0:T(8,128)(2,1)S(1)}, u32[]{:S(2)}, u32[]{:S(2)}) collective-permute-start(bf16[2048,128]{1,0:T(8,128)(2,1)S(1)} %get-tuple-element.93), channel_id=1, source_target_pairs={{0,2},{1,3},{2,0},{3,1},{4,6},{5,7},{6,4},{7,5},{8,10},{9,11},{10,... | collective-permute-start | bytes 1572872 | tf_op jit(solution)/shard_map/ppermute | solution.py:23
  91.0 12.6 %collective-permute-start.18 = (bf16[2048,128]{1,0:T(8,128)(2,1)S(1)}, bf16[2048,128]{1,0:T(8,128)(2,1)S(1)}, u32[]{:S(2)}, u32[]{:S(2)}) collective-permute-start(bf16[2048,128]{1,0:T(8,128)(2,1)S(1)} %get-tuple-element.91), channel_id=1, source_target_pairs={{0,1},{1,0},{2,3},{3,2},{4,5},{5,4},{6,7},{7,6},{8,9},{9,8},{10,11... | collective-permute-start | bytes 1572872 | tf_op jit(solution)/shard_map/ppermute | solution.py:23
  92.0 8.3 %collective-permute-start.17 = (bf16[512,256]{1,0:T(8,128)(2,1)S(1)}, bf16[512,256]{1,0:T(8,128)(2,1)S(1)}, u32[]{:S(2)}, u32[]{:S(2)}) collective-permute-start(bf16[512,256]{1,0:T(8,128)(2,1)S(1)} %shard_map.110), channel_id=1, source_target_pairs={{0,20},{1,21},{2,22},{3,23},{4,16},{5,17},{6,18},{7,19},{8,28},{9,... | collective-permute-start | bytes 786440 | tf_op jit(solution)/shard_map/ppermute | solution.py:33
  92.1 7.8 %collective-permute-start.10 = (bf16[32,1024]{1,0:T(8,128)(2,1)S(1)}, bf16[32,1024]{1,0:T(8,128)(2,1)S(1)}, u32[]{:S(2)}, u32[]{:S(2)}) collective-permute-start(bf16[32,1024]{1,0:T(8,128)(2,1)S(1)} %get-tuple-element.103), channel_id=1, source_target_pairs={{0,4},{1,5},{2,6},{3,7},{4,0},{5,1},{6,2},{7,3},{8,12},{9,13},{10,... | collective-permute-start | bytes 196616 | tf_op jit(solution)/shard_map/ppermute | solution.py:23
  100.3 5.8 %copy-start.15 = (bf16[512,256]{1,0:T(8,128)(2,1)}, bf16[512,256]{1,0:T(8,128)(2,1)S(1)}, u32[]{:S(2)}) copy-start(bf16[512,256]{1,0:T(8,128)(2,1)S(1)} %collective-permute-done.17.refs_3_) | copy-start | bytes 786436
  104.6 0.8 copy-start.9
  105.4 0.8 copy-start.11
  106.2 12.2 %collective-permute-start.20 = (bf16[1024,128]{1,0:T(8,128)(2,1)}, bf16[1024,128]{1,0:T(8,128)(2,1)}, u32[]{:S(2)}, u32[]{:S(2)}) collective-permute-start(bf16[1024,128]{1,0:T(8,128)(2,1)} %get-tuple-element.96), channel_id=1, source_target_pairs={{0,2},{1,3},{2,0},{3,1},{4,6},{5,7},{6,4},{7,5},{8,10},{9,11},{10,... | collective-permute-start | bytes 786440 | tf_op jit(solution)/shard_map/ppermute | solution.py:23
  107.3 11.2 %collective-permute-start.21 = (bf16[1024,128]{1,0:T(8,128)(2,1)}, bf16[1024,128]{1,0:T(8,128)(2,1)}, u32[]{:S(2)}, u32[]{:S(2)}) collective-permute-start(bf16[1024,128]{1,0:T(8,128)(2,1)} %get-tuple-element.98), channel_id=1, source_target_pairs={{0,4},{1,5},{2,6},{3,7},{4,0},{5,1},{6,2},{7,3},{8,12},{9,13},{10,... | collective-permute-start | bytes 786440 | tf_op jit(solution)/shard_map/ppermute | solution.py:23
  107.3 7.4 %copy-start.2 = (f32[1024,128]{1,0:T(8,128)S(1)}, f32[1024,128]{1,0:T(8,128)}, u32[]{:S(2)}) copy-start(f32[1024,128]{1,0:T(8,128)} %copy-done.1) | copy-start | bytes 1572868
  107.3 7.4 %copy-start.4 = (f32[1024,128]{1,0:T(8,128)S(1)}, f32[1024,128]{1,0:T(8,128)}, u32[]{:S(2)}) copy-start(f32[1024,128]{1,0:T(8,128)} %copy-done.3) | copy-start | bytes 1572868
  107.3 15.9 %collective-permute-start.26 = (bf16[128,256]{1,0:T(8,128)(2,1)S(1)}, bf16[128,256]{1,0:T(8,128)(2,1)S(1)}, u32[]{:S(2)}, u32[]{:S(2)}) collective-permute-start(bf16[128,256]{1,0:T(8,128)(2,1)S(1)} %get-tuple-element.102.refs_6_), channel_id=1, source_target_pairs={{0,4},{1,5},{2,6},{3,7},{4,0},{5,1},{6,2},{7,3},{8,12},{9,13},{10,... | collective-permute-start | bytes 196616 | tf_op jit(solution)/shard_map/ppermute | solution.py:23
  109.3 11.3 %collective-permute-start.27 = (bf16[64,256]{1,0:T(8,128)(2,1)S(1)}, bf16[64,256]{1,0:T(8,128)(2,1)S(1)}, u32[]{:S(2)}, u32[]{:S(2)}) collective-permute-start(bf16[64,256]{1,0:T(8,128)(2,1)S(1)} %bitcast.40), channel_id=1, source_target_pairs={{0,8},{1,9},{2,10},{3,11},{4,12},{5,13},{6,14},{7,15},{8,0},{9,1},... | collective-permute-start | bytes 98312 | tf_op jit(solution)/shard_map/ppermute | solution.py:23
  109.3 12.2 %collective-permute-start.28 = (bf16[64,256]{1,0:T(8,128)(2,1)S(1)}, bf16[64,256]{1,0:T(8,128)(2,1)S(1)}, u32[]{:S(2)}, u32[]{:S(2)}) collective-permute-start(bf16[64,256]{1,0:T(8,128)(2,1)S(1)} %bitcast.41), channel_id=1, source_target_pairs={{0,12},{1,13},{2,14},{3,15},{4,8},{5,9},{6,10},{7,11},{8,4},{9,5},... | collective-permute-start | bytes 98312 | tf_op jit(solution)/shard_map/ppermute | solution.py:23
  114.7 1.0 copy-start.6
  115.6 0.9 copy-start.8
  116.6 1.9 %copy-start.10 = (f32[1024,128]{1,0:T(8,128)S(1)}, f32[1024,128]{1,0:T(8,128)}, u32[]{:S(2)}) copy-start(f32[1024,128]{1,0:T(8,128)} %copy-done.9) | copy-start | bytes 1572868
  116.6 1.9 %copy-start.12 = (f32[1024,128]{1,0:T(8,128)S(1)}, f32[1024,128]{1,0:T(8,128)}, u32[]{:S(2)}) copy-start(f32[1024,128]{1,0:T(8,128)} %copy-done.11) | copy-start | bytes 1572868
  118.4 4.8 %copy-start = (bf16[1,1,2,256,1024]{4,3,2,1,0:T(8,128)(2,1)S(1)}, bf16[1,1,2,256,1024]{4,3,2,1,0:T(8,128)(2,1)}, u32[]{:S(2)}) copy-start(bf16[1,1,2,256,1024]{4,3,2,1,0:T(8,128)(2,1)} %param.8) | copy-start | bytes 3145732
  118.4 4.8 %copy-start.18 = (bf16[256,1024]{1,0:T(8,128)(2,1)S(1)}, bf16[256,1024]{1,0:T(8,128)(2,1)}, u32[]{:S(2)}) copy-start(bf16[256,1024]{1,0:T(8,128)(2,1)} %copy-done.17) | copy-start | bytes 1572868
  118.4 4.8 %copy-start.20 = (bf16[256,1024]{1,0:T(8,128)(2,1)S(1)}, bf16[256,1024]{1,0:T(8,128)(2,1)}, u32[]{:S(2)}) copy-start(bf16[256,1024]{1,0:T(8,128)(2,1)} %copy-done.19) | copy-start | bytes 1572868
  118.4 7.2 %collective-permute-start.25 = (bf16[512,768]{1,0:T(8,128)(2,1)S(1)}, bf16[512,768]{1,0:T(8,128)(2,1)S(1)}, u32[]{:S(2)}, u32[]{:S(2)}) collective-permute-start(bf16[512,768]{1,0:T(8,128)(2,1)S(1)} %shard_map.113), channel_id=1, source_target_pairs={{0,16},{1,17},{2,18},{3,19},{4,20},{5,21},{6,22},{7,23},{8,24},{9,... | collective-permute-start | bytes 2359304 | tf_op jit(solution)/shard_map/ppermute | solution.py:33
  120.2 6.6 %collective-permute-start.22 = (bf16[512,256]{1,0:T(8,128)(2,1)S(1)}, bf16[512,256]{1,0:T(8,128)(2,1)S(1)}, u32[]{:S(2)}, u32[]{:S(2)}) collective-permute-start(bf16[512,256]{1,0:T(8,128)(2,1)S(1)} %get-tuple-element.99), channel_id=1, source_target_pairs={{0,16},{1,17},{2,18},{3,19},{4,20},{5,21},{6,22},{7,23},{8,24},{9,... | collective-permute-start | bytes 786440 | tf_op jit(solution)/shard_map/ppermute | solution.py:33
  120.6 6.1 %collective-permute-start.23 = (bf16[512,128]{1,0:T(8,128)(2,1)S(1)}, bf16[512,128]{1,0:T(8,128)(2,1)S(1)}, u32[]{:S(2)}, u32[]{:S(2)}) collective-permute-start(bf16[512,128]{1,0:T(8,128)(2,1)S(1)} %get-tuple-element.100), channel_id=1, source_target_pairs={{0,20},{1,21},{2,22},{3,23},{4,16},{5,17},{6,18},{7,19},{8,28},{9,... | collective-permute-start | bytes 393224 | tf_op jit(solution)/shard_map/ppermute | solution.py:33
  121.5 4.2 %copy-start.14 = (bf16[512,512]{1,0:T(8,128)(2,1)S(1)}, bf16[512,512]{1,0:T(8,128)(2,1)}, u32[]{:S(2)}) copy-start(bf16[512,512]{1,0:T(8,128)(2,1)} %copy-done.13) | copy-start | bytes 1572868
  121.5 4.2 %copy-start.16 = (bf16[512,256]{1,0:T(8,128)(2,1)S(1)}, bf16[512,256]{1,0:T(8,128)(2,1)}, u32[]{:S(2)}) copy-start(bf16[512,256]{1,0:T(8,128)(2,1)} %copy-done.15) | copy-start | bytes 786436
  121.5 5.4 %collective-permute-start.24 = (bf16[512,128]{1,0:T(8,128)(2,1)S(1)}, bf16[512,128]{1,0:T(8,128)(2,1)S(1)}, u32[]{:S(2)}, u32[]{:S(2)}) collective-permute-start(bf16[512,128]{1,0:T(8,128)(2,1)S(1)} %get-tuple-element.101), channel_id=1, source_target_pairs={{0,17},{1,16},{2,19},{3,18},{4,21},{5,20},{6,23},{7,22},{8,25},{9,... | collective-permute-start | bytes 393224 | tf_op jit(solution)/shard_map/ppermute | solution.py:33

commit v10 on v9

--- a/solution.py
+++ b/solution.py
@@ -328,22 +328,23 @@
 
     chunks = [([grad_tile], own_pieces), (got0, pieces_of(0)), (got1, pieces_of(1))]
     order = [piece for _, pieces in chunks for _, _, piece, _ in pieces]
-    own_third, placed = last_parts((kept_x, kept_y), (second_x, second_y), placed)
+    d_sent_x, d_sent_y, d_kept_x, d_kept_y, part = produce(
+        got1, pieces_of(1), True, True, True, LONG
+    )
+    parts.append(part)
+    own_third, placed = last_parts((after(kept_x, part), kept_y), (second_x, second_y), placed)
     own_last = relay(own_third, 4)
     own_sums = (kept_x, second_x), (kept_y, second_y)
-    d_sent_x, d_sent_y, d_kept_x, d_kept_y, part = produce(
-        [after(got1[0], own_third), *got1[1:]], pieces_of(1), True, True, True, LONG
-    )
-    parts.append(part)
     own_rank = jnp.concatenate(parts, 1)
-    shared = after(own_rank.astype(BF16), own_last)
+    shared = own_rank.astype(BF16)
     for mask in (1, 2, 3):
         own_rank = own_rank + partner(shared, mask)
     (c_sent_x, c_sent_y), c_kept = halve((c_kept_x, c_kept_y), (c_first_x, c_first_y))
     c_second_x, c_second_y = partner(c_sent_x, 2), partner(c_sent_y, 1)
     slot = own_rank, c_second_x, c_second_y
-    d_first_x, d_first_y = partner(after(d_sent_x, *slot), 1), partner(after(d_sent_y, *slot), 2)
-    shared = own_rank.astype(BF16)
+    d_sent_x, d_sent_y = lax.optimization_barrier((d_sent_x, d_sent_y, *slot))[:2]
+    d_first_x, d_first_y = partner(d_sent_x, 1), partner(d_sent_y, 2)
+    shared = after(own_rank.astype(BF16), own_last, d_sent_x)
     ranks = [(own_rank + partner(shared, 4)).astype(BF16)]
     for j in range(1, high_size):
         one, other = partner(shared, j * low_size), partner(shared, j * low_size + 4)

time: 128 us -> 116 us (0.906)
  waiting for transfers between devices: 54.9 us -> 41 us
  starting transfers between devices: 29.3 us -> 32.3 us
    ppermute x23, waiting for transfers between devices: 49.4 us -> 39.2 us  [partner(): return lax.ppermute(value, 'tensor', pairs)]
    ppermute x23, starting transfers between devices: 26.1 us -> 30.7 us  [partner(): return lax.ppermute(value, 'tensor', pairs)]
    ppermute x6, waiting for transfers between devices: 5.5 us -> 1.76 us  [relay(): return lax.ppermute(value, ('pipe', 'tensor'), pairs)]
    ppermute x6, starting transfers between devices: 3.16 us -> 1.61 us  [relay(): return lax.ppermute(value, ('pipe', 'tensor'), pairs)]
    unnamed x46 -> x44, local copies, waits for them, and re-layouts: 4.37 us -> 3.56 us
  transfers between devices with their start and end apart: 29 -> 29, of which waited for: 14 -> 14; matrix products, arithmetic and copies ran while one was open for 0% -> 0% of each run, Pallas kernels for 27% -> 30%
where the time goes in v10:
time: 116 us
  waiting for transfers between devices  41 us (35%)
  Pallas kernels  36 us (31%)
  starting transfers between devices  32.3 us (28%)
  local copies, waits for them, and re-layouts  5.63 us (5%)
    ppermute x23, waiting for transfers between devices, partner(): return lax.ppermute(value, 'tensor', pairs)  39.2 us
    ppermute x23, starting transfers between devices, partner(): return lax.ppermute(value, 'tensor', pairs)  30.7 us
    pallas_call x4, Pallas kernels, product(): pl.pallas_call(functools.partial(product_body, low_size, tile_rows, piece...  23.7 us
    unnamed x44, local copies, waits for them, and re-layouts  3.56 us
    pallas_call x2, Pallas kernels, with_adapter(): pl.pallas_call(functools.partial(adapter_kernel, first, with_last, len(su...  3.47 us
    pallas_call x1, Pallas kernels, shards(): pl.pallas_call(down_kernel, in_specs=[SMEM] * 3 + [VMEM] * (1 + high_size...  2.94 us
    pallas_call x1, Pallas kernels, shards(): pl.pallas_call(functools.partial(up_body, low_size, tile_rows, all_pieces...  2.43 us
  transfers between devices with their start and end apart: 29, of which 14 were waited for; matrix products, arithmetic and copies ran while one was open for 0% of the time, Pallas kernels for 30%

profile of v10, /device:TPU:0, one launch (start us, length us, event | category | flops | bytes accessed | tf_op | source)
XLA Modules:
  0.0 115.9 jit_solution(13590941703021540596)
XLA Ops:
  0.6 2.1 %slice_bitcast_fusion = (bf16[256,1024]{1,0:T(8,128)(2,1)}, bf16[256,1024]{1,0:T(8,128)(2,1)S(1)}) fusion(bf16[1,1,2,256,1024]{4,3,2,1,0:T(8,128)(2,1)} %param.8), kind=kLoop, calls=%fused_computation | loop fusion | bytes 2097152 | tf_op jit(solution)/shard_map/squeeze | solution.py:319
  2.7 4.0 %collective-permute-start = (bf16[256,1024]{1,0:T(8,128)(2,1)S(1)}, bf16[256,1024]{1,0:T(8,128)(2,1)S(1)}, u32[]{:S(2)}, u32[]{:S(2)}) collective-permute-start(bf16[256,1024]{1,0:T(8,128)(2,1)S(1)} %get-tuple-element.106), channel_id=1, source_target_pairs={{0,8},{1,9},{2,10},{3,11},{4,12},{5,13},{6,14},{7,15},{8,0},{9,1},... | collective-permute-start | bytes 1572872 | tf_op jit(solution)/shard_map/ppermute | solution.py:23
  6.7 5.7 %shard_map.103 = (bf16[2176,256]{1,0:T(8,128)(2,1)S(1)}, bf16[2048,256]{1,0:T(8,128)(2,1)S(1)}, bf16[128,256]{1,0:T(8,128)(2,1)S(1)}) custom-call(s32[1]{0:T(128)} %bitcast.refs_0_.pos_ref, s32[2,4]{1,0:T(2,128)} %bitcast.42, s32[2]{0:T(128)} %bitcast.51, bf16[2,256,1024]{2,1,0:T(8,128)(2,1)} %bitcast.20, bf16[8,512,1024]{2,1,0:T(8,128)(2,1)} %bitcast.28, ...), custom_call_target="tpu_custom_call" | custom-call | flops 1000 | bytes 1000 | tf_op jit(solution)/shard_map/pallas_call | solution.py:140
  12.5 1.6 %collective-permute-start.5 = (bf16[2176,256]{1,0:T(8,128)(2,1)S(1)}, bf16[2176,256]{1,0:T(8,128)(2,1)S(1)}, u32[]{:S(2)}, u32[]{:S(2)}) collective-permute-start(bf16[2176,256]{1,0:T(8,128)(2,1)S(1)} %get-tuple-element.57), channel_id=1, source_target_pairs={{0,1},{1,0},{2,3},{3,2},{4,5},{5,4},{6,7},{7,6},{8,9},{9,8},{10,11... | collective-permute-start | bytes 3342344 | tf_op jit(solution)/shard_map/ppermute | solution.py:23
  14.0 1.5 %collective-permute-start.6 = (bf16[2048,256]{1,0:T(8,128)(2,1)S(1)}, bf16[2048,256]{1,0:T(8,128)(2,1)S(1)}, u32[]{:S(2)}, u32[]{:S(2)}) collective-permute-start(bf16[2048,256]{1,0:T(8,128)(2,1)S(1)} %get-tuple-element.58), channel_id=1, source_target_pairs={{0,2},{1,3},{2,0},{3,1},{4,6},{5,7},{6,4},{7,5},{8,10},{9,11},{10,... | collective-permute-start | bytes 3145736 | tf_op jit(solution)/shard_map/ppermute | solution.py:23
  15.5 5.8 %shard_map.104 = (f32[2048,256]{1,0:T(8,128)S(1)}, f32[2048,256]{1,0:T(8,128)S(1)}, f32[32,512]{1,0:T(8,128)S(1)}) custom-call(s32[1]{0:T(128)} %bitcast.refs_0_.pos_ref, s32[2,4]{1,0:T(2,128)} %bitcast.43, s32[2]{0:T(128)} %bitcast.52, bf16[2,256,1024]{2,1,0:T(8,128)(2,1)} %bitcast.21, bf16[8,512,1024]{2,1,0:T(8,128)(2,1)} %bitcast.29, ...), custom_call_target="tpu_custom_call" | custom-call | flops 1000 | bytes 1000 | tf_op jit(solution)/shard_map/pallas_call | solution.py:140
  21.4 8.5 %collective-permute-done = bf16[256,1024]{1,0:T(8,128)(2,1)S(1)} collective-permute-done((bf16[256,1024]{1,0:T(8,128)(2,1)S(1)}, bf16[256,1024]{1,0:T(8,128)(2,1)S(1)}, u32[]{:S(2)}, u32[]{:S(2)}) %collective-permute-start) | collective-permute-done | bytes 524320 | tf_op jit(solution)/shard_map/ppermute | solution.py:23
  29.9 6.1 %shard_map.105 = (bf16[2048,128]{1,0:T(8,128)(2,1)S(1)}, bf16[2048,128]{1,0:T(8,128)(2,1)S(1)}, f32[2048,128]{1,0:T(8,128)S(1)}, f32[2048,128]{1,0:T(8,128)S(1)}, f32[32,256]{1,0:T(8,128)S(1)}) custom-call(s32[1]{0:T(128)} %bitcast.refs_0_.pos_ref, s32[2,4]{1,0:T(2,128)} %bitcast.44, s32[2]{0:T(128)} %bitcast.53, bf16[1,256,1024]{2,1,0:T(8,128)(2,1)S(1)} %bitcast.24, ...), custom_call_target="tpu_custom_call" | custom-call | flops 40000000000 | bytes 1000 | tf_op jit(solution)/shard_map/pallas_call | solution.py:140
  36.0 2.4 %collective-permute-done.6.refs_3_ = bf16[2048,256]{1,0:T(8,128)(2,1)S(1)} collective-permute-done((bf16[2048,256]{1,0:T(8,128)(2,1)S(1)}, bf16[2048,256]{1,0:T(8,128)(2,1)S(1)}, u32[]{:S(2)}, u32[]{:S(2)}) %collective-permute-start.6) | collective-permute-done | bytes 1048608 | tf_op jit(solution)/shard_map/ppermute | solution.py:23
  38.4 0.2 collective-permute-done.5.refs_2_
  38.5 0.3 shard_map.107
  38.9 1.6 %collective-permute-start.7 = (bf16[1152,256]{1,0:T(8,128)(2,1)S(1)}, bf16[1152,256]{1,0:T(8,128)(2,1)S(1)}, u32[]{:S(2)}, u32[]{:S(2)}) collective-permute-start(bf16[1152,256]{1,0:T(8,128)(2,1)S(1)} %get-tuple-element.72), channel_id=1, source_target_pairs={{0,2},{1,3},{2,0},{3,1},{4,6},{5,7},{6,4},{7,5},{8,10},{9,11},{10,... | collective-permute-start | bytes 1769480 | tf_op jit(solution)/shard_map/ppermute | solution.py:23
  40.5 1.5 %collective-permute-start.8 = (bf16[1024,256]{1,0:T(8,128)(2,1)S(1)}, bf16[1024,256]{1,0:T(8,128)(2,1)S(1)}, u32[]{:S(2)}, u32[]{:S(2)}) collective-permute-start(bf16[1024,256]{1,0:T(8,128)(2,1)S(1)} %get-tuple-element.73), channel_id=1, source_target_pairs={{0,1},{1,0},{2,3},{3,2},{4,5},{5,4},{6,7},{7,6},{8,9},{9,8},{10,11... | collective-permute-start | bytes 1572872 | tf_op jit(solution)/shard_map/ppermute | solution.py:23
  42.0 0.5 collective-permute-start.11
  42.5 0.5 collective-permute-start.10
  43.0 12.3 %collective-permute-done.1 = bf16[256,1024]{1,0:T(8,128)(2,1)S(1)} collective-permute-done((bf16[256,1024]{1,0:T(8,128)(2,1)}, bf16[256,1024]{1,0:T(8,128)(2,1)S(1)}, u32[]{:S(2)}, u32[]{:S(2)}) %collective-permute-start.1) | collective-permute-done | bytes 524320 | tf_op jit(solution)/shard_map/ppermute | solution.py:23
  55.3 6.1 %shard_map.106 = (bf16[2048,128]{1,0:T(8,128)(2,1)S(1)}, bf16[2048,128]{1,0:T(8,128)(2,1)S(1)}, f32[2048,128]{1,0:T(8,128)S(1)}, f32[2048,128]{1,0:T(8,128)S(1)}, f32[32,256]{1,0:T(8,128)S(1)}) custom-call(s32[1]{0:T(128)} %bitcast.refs_0_.pos_ref, s32[2,4]{1,0:T(2,128)} %bitcast.45, s32[2]{0:T(128)} %bitcast.54, bf16[1,256,1024]{2,1,0:T(8,128)(2,1)S(1)} %bitcast.26, ...), custom_call_target="tpu_custom_call" | custom-call | flops 40000000000 | bytes 1000 | tf_op jit(solution)/shard_map/pallas_call | solution.py:140
  61.4 0.1 shard_map.108
  61.5 0.1 collective-permute-start.9
  61.7 1.3 %collective-permute-start.2 = (bf16[32,1024]{1,0:T(8,128)(2,1)S(1)}, bf16[32,1024]{1,0:T(8,128)(2,1)S(1)}, u32[]{:S(2)}, u32[]{:S(2)}) collective-permute-start(bf16[32,1024]{1,0:T(8,128)(2,1)S(1)} %convert_element_type.30), channel_id=1, source_target_pairs={{0,1},{1,0},{2,3},{3,2},{4,5},{5,4},{6,7},{7,6},{8,9},{9,8},{10,11... | collective-permute-start | bytes 196616 | tf_op jit(solution)/shard_map/ppermute | solution.py:23
  63.0 1.5 %collective-permute-start.3 = (bf16[32,1024]{1,0:T(8,128)(2,1)S(1)}, bf16[32,1024]{1,0:T(8,128)(2,1)S(1)}, u32[]{:S(2)}, u32[]{:S(2)}) collective-permute-start(bf16[32,1024]{1,0:T(8,128)(2,1)S(1)} %convert_element_type.30), channel_id=1, source_target_pairs={{0,2},{1,3},{2,0},{3,1},{4,6},{5,7},{6,4},{7,5},{8,10},{9,11},{10,... | collective-permute-start | bytes 196616 | tf_op jit(solution)/shard_map/ppermute | solution.py:23
  64.5 2.7 %collective-permute-start.4 = (bf16[32,1024]{1,0:T(8,128)(2,1)S(1)}, bf16[32,1024]{1,0:T(8,128)(2,1)S(1)}, u32[]{:S(2)}, u32[]{:S(2)}) collective-permute-start(bf16[32,1024]{1,0:T(8,128)(2,1)S(1)} %convert_element_type.30), channel_id=1, source_target_pairs={{0,3},{1,2},{2,1},{3,0},{4,7},{5,6},{6,5},{7,4},{8,11},{9,10},{10,... | collective-permute-start | bytes 196616 | tf_op jit(solution)/shard_map/ppermute | solution.py:23
  67.2 0.2 shard_map.109
  67.4 0.6 collective-permute-start.12
  68.0 0.3 collective-permute-start.13
  68.3 2.1 %collective-permute-done.4 = bf16[32,1024]{1,0:T(8,128)(2,1)S(1)} collective-permute-done((bf16[32,1024]{1,0:T(8,128)(2,1)S(1)}, bf16[32,1024]{1,0:T(8,128)(2,1)S(1)}, u32[]{:S(2)}, u32[]{:S(2)}) %collective-permute-start.4) | collective-permute-done | bytes 65568 | tf_op jit(solution)/shard_map/ppermute | solution.py:23
  70.4 3.6 %collective-permute-done.12.refs_2_.refs_11_ = bf16[1024,128]{1,0:T(8,128)(2,1)S(1)} collective-permute-done((bf16[1024,128]{1,0:T(8,128)(2,1)S(1)}, bf16[1024,128]{1,0:T(8,128)(2,1)S(1)}, u32[]{:S(2)}, u32[]{:S(2)}) %collective-permute-start.12) | collective-permute-done | bytes 262176 | tf_op jit(solution)/shard_map/ppermute | solution.py:23
  74.0 0.4 collective-permute-done.13.refs_3_.refs_13_
  74.4 0.0 collective-permute-done.9.refs_2_
  74.4 1.8 %collective-permute-start.15 = (bf16[32,1024]{1,0:T(8,128)(2,1)S(1)}, bf16[32,1024]{1,0:T(8,128)(2,1)S(1)}, u32[]{:S(2)}, u32[]{:S(2)}) collective-permute-start(bf16[32,1024]{1,0:T(8,128)(2,1)S(1)} %get-tuple-element.87), channel_id=1, source_target_pairs={{0,8},{1,9},{2,10},{3,11},{4,12},{5,13},{6,14},{7,15},{8,0},{9,1},... | collective-permute-start | bytes 196616 | tf_op jit(solution)/shard_map/ppermute | solution.py:23
  76.2 3.0 %collective-permute-start.16 = (bf16[32,1024]{1,0:T(8,128)(2,1)S(1)}, bf16[32,1024]{1,0:T(8,128)(2,1)S(1)}, u32[]{:S(2)}, u32[]{:S(2)}) collective-permute-start(bf16[32,1024]{1,0:T(8,128)(2,1)S(1)} %get-tuple-element.87), channel_id=1, source_target_pairs={{0,12},{1,13},{2,14},{3,15},{4,8},{5,9},{6,10},{7,11},{8,4},{9,5},... | collective-permute-start | bytes 196616 | tf_op jit(solution)/shard_map/ppermute | solution.py:23
  79.2 1.4 %collective-permute-start.18 = (bf16[2048,128]{1,0:T(8,128)(2,1)S(1)}, bf16[2048,128]{1,0:T(8,128)(2,1)S(1)}, u32[]{:S(2)}, u32[]{:S(2)}) collective-permute-start(bf16[2048,128]{1,0:T(8,128)(2,1)S(1)} %get-tuple-element.86), channel_id=1, source_target_pairs={{0,1},{1,0},{2,3},{3,2},{4,5},{5,4},{6,7},{7,6},{8,9},{9,8},{10,11... | collective-permute-start | bytes 1572872 | tf_op jit(solution)/shard_map/ppermute | solution.py:23
  80.6 0.8 collective-permute-start.19
  81.4 0.1 shard_map.110
  81.4 0.1 collective-permute-start.17
  81.5 0.6 collective-permute-start.14
  82.1 0.2 collective-permute-done.16
  82.3 5.7 %collective-permute-done.14 = bf16[32,1024]{1,0:T(8,128)(2,1)S(1)} collective-permute-done((bf16[32,1024]{1,0:T(8,128)(2,1)S(1)}, bf16[32,1024]{1,0:T(8,128)(2,1)S(1)}, u32[]{:S(2)}, u32[]{:S(2)}) %collective-permute-start.14) | collective-permute-done | bytes 65568 | tf_op jit(solution)/shard_map/ppermute | solution.py:23
  88.0 0.6 collective-permute-done.17.refs_3_
  88.6 2.3 %collective-permute-done.18.refs_2_ = bf16[2048,128]{1,0:T(8,128)(2,1)S(1)} collective-permute-done((bf16[2048,128]{1,0:T(8,128)(2,1)S(1)}, bf16[2048,128]{1,0:T(8,128)(2,1)S(1)}, u32[]{:S(2)}, u32[]{:S(2)}) %collective-permute-start.18) | collective-permute-done | bytes 524320 | tf_op jit(solution)/shard_map/ppermute | solution.py:23
  90.9 1.5 %collective-permute-done.19.refs_3_ = bf16[2048,128]{1,0:T(8,128)(2,1)S(1)} collective-permute-done((bf16[2048,128]{1,0:T(8,128)(2,1)S(1)}, bf16[2048,128]{1,0:T(8,128)(2,1)S(1)}, u32[]{:S(2)}, u32[]{:S(2)}) %collective-permute-start.19) | collective-permute-done | bytes 524320 | tf_op jit(solution)/shard_map/ppermute | solution.py:23
  92.4 0.9 shard_map.111
  93.3 0.0 copy-start.9
  93.4 0.8 copy-done.9
  94.1 0.8 copy-done.11
  94.9 0.6 collective-permute-start.20
  95.5 0.6 collective-permute-start.21
  96.1 1.5 %collective-permute-start.26 = (bf16[128,256]{1,0:T(8,128)(2,1)S(1)}, bf16[128,256]{1,0:T(8,128)(2,1)S(1)}, u32[]{:S(2)}, u32[]{:S(2)}) collective-permute-start(bf16[128,256]{1,0:T(8,128)(2,1)S(1)} %get-tuple-element.102.refs_6_), channel_id=1, source_target_pairs={{0,4},{1,5},{2,6},{3,7},{4,0},{5,1},{6,2},{7,3},{8,12},{9,13},{10,... | collective-permute-start | bytes 196616 | tf_op jit(solution)/shard_map/ppermute | solution.py:23
  97.5 1.7 %collective-permute-start.27 = (bf16[64,256]{1,0:T(8,128)(2,1)S(1)}, bf16[64,256]{1,0:T(8,128)(2,1)S(1)}, u32[]{:S(2)}, u32[]{:S(2)}) collective-permute-start(bf16[64,256]{1,0:T(8,128)(2,1)S(1)} %bitcast.40), channel_id=1, source_target_pairs={{0,8},{1,9},{2,10},{3,11},{4,12},{5,13},{6,14},{7,15},{8,0},{9,1},... | collective-permute-start | bytes 98312 | tf_op jit(solution)/shard_map/ppermute | solution.py:23
  99.3 1.2 %collective-permute-start.28 = (bf16[64,256]{1,0:T(8,128)(2,1)S(1)}, bf16[64,256]{1,0:T(8,128)(2,1)S(1)}, u32[]{:S(2)}, u32[]{:S(2)}) collective-permute-start(bf16[64,256]{1,0:T(8,128)(2,1)S(1)} %bitcast.41), channel_id=1, source_target_pairs={{0,12},{1,13},{2,14},{3,15},{4,8},{5,9},{6,10},{7,11},{8,4},{9,5},... | collective-permute-start | bytes 98312 | tf_op jit(solution)/shard_map/ppermute | solution.py:23
  100.5 2.9 %shard_map.112 = bf16[8,2,32,512]{3,2,1,0:T(8,128)(2,1)} custom-call(s32[1]{0:T(128)} %bitcast.refs_0_.pos_ref, s32[2,4]{1,0:T(2,128)} %bitcast.46, s32[2]{0:T(128)} %bitcast.55, bf16[2,512,512]{2,1,0:T(8,128)(2,1)} %bitcast.35, bf16[32,1024]{1,0:T(8,128)(2,1)S(1)} %add_convert_fusion.1.refs_0_.refs_4_, bf16[32,1024]{1,0:T(8,128)(2,1)S(1)} %add_convert_fusion.refs_1_.refs_5_), custom_call_target="tpu_custom_call" | custom-call | flops 1000 | bytes 1000 | tf_op jit(solution)/shard_map/pallas_call | solution.py:494
  103.4 0.9 copy-done.6
  104.4 0.9 copy-done.8
  105.3 1.8 %shard_map.113 = bf16[512,768]{1,0:T(8,128)(2,1)S(1)} custom-call(s32[1]{0:T(128)} %bitcast.refs_0_.pos_ref, s32[2,4]{1,0:T(2,128)} %bitcast.47, s32[2]{0:T(128)} %bitcast.56, bf16[8,2,32,512]{3,2,1,0:T(8,128)(2,1)} %bitcast.33, bf16[32,1024]{1,0:T(8,128)(2,1)S(1)} %add_convert_fusion.1.refs_0_.refs_4_, ...), custom_call_target="tpu_custom_call" | custom-call | flops 1000 | bytes 1000 | tf_op jit(solution)/shard_map/pallas_call | solution.py:417
  107.2 0.1 collective-permute-start.25
  107.3 1.7 %shard_map.114 = (bf16[512,128]{1,0:T(8,128)(2,1)S(1)}, bf16[512,128]{1,0:T(8,128)(2,1)S(1)}, bf16[512,256]{1,0:T(8,128)(2,1)S(1)}) custom-call(s32[1]{0:T(128)} %bitcast.refs_0_.pos_ref, s32[2,4]{1,0:T(2,128)} %bitcast.48, s32[2]{0:T(128)} %bitcast.57, bf16[8,2,32,512]{3,2,1,0:T(8,128)(2,1)} %bitcast.34, ...), custom_call_target="tpu_custom_call" | custom-call | flops 1000 | bytes 1000 | tf_op jit(solution)/shard_map/pallas_call | solution.py:417
  109.0 0.4 collective-permute-start.22
  109.4 0.3 collective-permute-start.23
  109.7 0.7 collective-permute-start.24
  110.4 2.4 %shard_map.117 = bf16[8,32,1024]{2,1,0:T(8,128)(2,1)} custom-call(s32[1]{0:T(128)} %bitcast.refs_0_.pos_ref, s32[2,4]{1,0:T(2,128)} %bitcast.49, s32[2]{0:T(128)} %bitcast.58, bf16[2,256,1024]{2,1,0:T(8,128)(2,1)S(1)} %bitcast.22, bf16[1,256,1024]{2,1,0:T(8,128)(2,1)S(1)} %bitcast.25, bf16[1,256,1024]{2,1,0:T(8,128)(2,1)S(1)} %bitcast.27, ...), custom_call_target="tpu_custom_call" | custom-call | flops 40000000000 | bytes 1000 | tf_op jit(solution)/shard_map/pallas_call | solution.py:363
  112.8 1.1 shard_map.115.refs_4_
  113.9 0.9 collective-permute-done.23.refs_2_
  114.8 0.2 collective-permute-done.24.refs_3_
  115.1 0.8 shard_map.116
  (60 shorter events, 0.2 us)
Async XLA Ops:
  2.7 27.2 %collective-permute-start = (bf16[256,1024]{1,0:T(8,128)(2,1)S(1)}, bf16[256,1024]{1,0:T(8,128)(2,1)S(1)}, u32[]{:S(2)}, u32[]{:S(2)}) collective-permute-start(bf16[256,1024]{1,0:T(8,128)(2,1)S(1)} %get-tuple-element.106), channel_id=1, source_target_pairs={{0,8},{1,9},{2,10},{3,11},{4,12},{5,13},{6,14},{7,15},{8,0},{9,1},... | collective-permute-start | bytes 1572872 | tf_op jit(solution)/shard_map/ppermute | solution.py:23
  12.5 26.1 %collective-permute-start.5 = (bf16[2176,256]{1,0:T(8,128)(2,1)S(1)}, bf16[2176,256]{1,0:T(8,128)(2,1)S(1)}, u32[]{:S(2)}, u32[]{:S(2)}) collective-permute-start(bf16[2176,256]{1,0:T(8,128)(2,1)S(1)} %get-tuple-element.57), channel_id=1, source_target_pairs={{0,1},{1,0},{2,3},{3,2},{4,5},{5,4},{6,7},{7,6},{8,9},{9,8},{10,11... | collective-permute-start | bytes 3342344 | tf_op jit(solution)/shard_map/ppermute | solution.py:23
  14.0 24.3 %collective-permute-start.6 = (bf16[2048,256]{1,0:T(8,128)(2,1)S(1)}, bf16[2048,256]{1,0:T(8,128)(2,1)S(1)}, u32[]{:S(2)}, u32[]{:S(2)}) collective-permute-start(bf16[2048,256]{1,0:T(8,128)(2,1)S(1)} %get-tuple-element.58), channel_id=1, source_target_pairs={{0,2},{1,3},{2,0},{3,1},{4,6},{5,7},{6,4},{7,5},{8,10},{9,11},{10,... | collective-permute-start | bytes 3145736 | tf_op jit(solution)/shard_map/ppermute | solution.py:23
  29.9 6.1 %copy-start.17 = (bf16[256,1024]{1,0:T(8,128)(2,1)}, bf16[256,1024]{1,0:T(8,128)(2,1)S(1)}, u32[]{:S(2)}) copy-start(bf16[256,1024]{1,0:T(8,128)(2,1)S(1)} %collective-permute-done) | copy-start | bytes 1572868
  29.9 25.5 %collective-permute-start.1 = (bf16[256,1024]{1,0:T(8,128)(2,1)}, bf16[256,1024]{1,0:T(8,128)(2,1)S(1)}, u32[]{:S(2)}, u32[]{:S(2)}) collective-permute-start(bf16[256,1024]{1,0:T(8,128)(2,1)} %get-tuple-element.63), channel_id=1, source_target_pairs={{0,8},{1,9},{2,10},{3,11},{4,12},{5,13},{6,14},{7,15},{8,0},{9,1},... | collective-permute-start | bytes 1572872 | tf_op jit(solution)/shard_map/ppermute | solution.py:23
  38.9 22.5 %collective-permute-start.7 = (bf16[1152,256]{1,0:T(8,128)(2,1)S(1)}, bf16[1152,256]{1,0:T(8,128)(2,1)S(1)}, u32[]{:S(2)}, u32[]{:S(2)}) collective-permute-start(bf16[1152,256]{1,0:T(8,128)(2,1)S(1)} %get-tuple-element.72), channel_id=1, source_target_pairs={{0,2},{1,3},{2,0},{3,1},{4,6},{5,7},{6,4},{7,5},{8,10},{9,11},{10,... | collective-permute-start | bytes 1769480 | tf_op jit(solution)/shard_map/ppermute | solution.py:23
  40.5 20.9 %collective-permute-start.8 = (bf16[1024,256]{1,0:T(8,128)(2,1)S(1)}, bf16[1024,256]{1,0:T(8,128)(2,1)S(1)}, u32[]{:S(2)}, u32[]{:S(2)}) collective-permute-start(bf16[1024,256]{1,0:T(8,128)(2,1)S(1)} %get-tuple-element.73), channel_id=1, source_target_pairs={{0,1},{1,0},{2,3},{3,2},{4,5},{5,4},{6,7},{7,6},{8,9},{9,8},{10,11... | collective-permute-start | bytes 1572872 | tf_op jit(solution)/shard_map/ppermute | solution.py:23
  42.0 22.5 %collective-permute-start.11 = (bf16[2048,128]{1,0:T(8,128)(2,1)S(1)}, bf16[2048,128]{1,0:T(8,128)(2,1)S(1)}, u32[]{:S(2)}, u32[]{:S(2)}) collective-permute-start(bf16[2048,128]{1,0:T(8,128)(2,1)S(1)} %get-tuple-element.83), channel_id=1, source_target_pairs={{0,2},{1,3},{2,0},{3,1},{4,6},{5,7},{6,4},{7,5},{8,10},{9,11},{10,... | collective-permute-start | bytes 1572872 | tf_op jit(solution)/shard_map/ppermute | solution.py:23
  42.5 24.7 %collective-permute-start.10 = (bf16[2048,128]{1,0:T(8,128)(2,1)S(1)}, bf16[2048,128]{1,0:T(8,128)(2,1)S(1)}, u32[]{:S(2)}, u32[]{:S(2)}) collective-permute-start(bf16[2048,128]{1,0:T(8,128)(2,1)S(1)} %get-tuple-element.81), channel_id=1, source_target_pairs={{0,1},{1,0},{2,3},{3,2},{4,5},{5,4},{6,7},{7,6},{8,9},{9,8},{10,11... | collective-permute-start | bytes 1572872 | tf_op jit(solution)/shard_map/ppermute | solution.py:23
  55.3 6.1 %copy-start.19 = (bf16[256,1024]{1,0:T(8,128)(2,1)}, bf16[256,1024]{1,0:T(8,128)(2,1)S(1)}, u32[]{:S(2)}) copy-start(bf16[256,1024]{1,0:T(8,128)(2,1)S(1)} %collective-permute-done.1) | copy-start | bytes 1572868
  61.5 12.8 %collective-permute-start.9 = (bf16[512,512]{1,0:T(8,128)(2,1)S(1)}, bf16[512,512]{1,0:T(8,128)(2,1)S(1)}, u32[]{:S(2)}, u32[]{:S(2)}) collective-permute-start(bf16[512,512]{1,0:T(8,128)(2,1)S(1)} %get-tuple-element.75), channel_id=1, source_target_pairs={{0,20},{1,21},{2,22},{3,23},{4,16},{5,17},{6,18},{7,19},{8,28},{9,... | collective-permute-start | bytes 1572872 | tf_op jit(solution)/shard_map/ppermute | solution.py:33
  61.7 6.3 %collective-permute-start.2 = (bf16[32,1024]{1,0:T(8,128)(2,1)S(1)}, bf16[32,1024]{1,0:T(8,128)(2,1)S(1)}, u32[]{:S(2)}, u32[]{:S(2)}) collective-permute-start(bf16[32,1024]{1,0:T(8,128)(2,1)S(1)} %convert_element_type.30), channel_id=1, source_target_pairs={{0,1},{1,0},{2,3},{3,2},{4,5},{5,4},{6,7},{7,6},{8,9},{9,8},{10,11... | collective-permute-start | bytes 196616 | tf_op jit(solution)/shard_map/ppermute | solution.py:23
  63.0 5.3 %collective-permute-start.3 = (bf16[32,1024]{1,0:T(8,128)(2,1)S(1)}, bf16[32,1024]{1,0:T(8,128)(2,1)S(1)}, u32[]{:S(2)}, u32[]{:S(2)}) collective-permute-start(bf16[32,1024]{1,0:T(8,128)(2,1)S(1)} %convert_element_type.30), channel_id=1, source_target_pairs={{0,2},{1,3},{2,0},{3,1},{4,6},{5,7},{6,4},{7,5},{8,10},{9,11},{10,... | collective-permute-start | bytes 196616 | tf_op jit(solution)/shard_map/ppermute | solution.py:23
  64.5 5.9 %collective-permute-start.4 = (bf16[32,1024]{1,0:T(8,128)(2,1)S(1)}, bf16[32,1024]{1,0:T(8,128)(2,1)S(1)}, u32[]{:S(2)}, u32[]{:S(2)}) collective-permute-start(bf16[32,1024]{1,0:T(8,128)(2,1)S(1)} %convert_element_type.30), channel_id=1, source_target_pairs={{0,3},{1,2},{2,1},{3,0},{4,7},{5,6},{6,5},{7,4},{8,11},{9,10},{10,... | collective-permute-start | bytes 196616 | tf_op jit(solution)/shard_map/ppermute | solution.py:23
  67.4 14.0 %copy-start.1 = (f32[1024,128]{1,0:T(8,128)}, f32[1024,128]{1,0:T(8,128)S(1)}, u32[]{:S(2)}) copy-start(f32[1024,128]{1,0:T(8,128)S(1)} %get-tuple-element.89.refs_0_.refs_10_) | copy-start | bytes 1572868
  67.4 14.0 %copy-start.3 = (f32[1024,128]{1,0:T(8,128)}, f32[1024,128]{1,0:T(8,128)S(1)}, u32[]{:S(2)}) copy-start(f32[1024,128]{1,0:T(8,128)S(1)} %get-tuple-element.90.refs_1_.refs_12_) | copy-start | bytes 1572868
  67.4 6.6 %collective-permute-start.12 = (bf16[1024,128]{1,0:T(8,128)(2,1)S(1)}, bf16[1024,128]{1,0:T(8,128)(2,1)S(1)}, u32[]{:S(2)}, u32[]{:S(2)}) collective-permute-start(bf16[1024,128]{1,0:T(8,128)(2,1)S(1)} %get-tuple-element.84), channel_id=1, source_target_pairs={{0,2},{1,3},{2,0},{3,1},{4,6},{5,7},{6,4},{7,5},{8,10},{9,11},{10,... | collective-permute-start | bytes 786440 | tf_op jit(solution)/shard_map/ppermute | solution.py:23
  68.0 6.4 %collective-permute-start.13 = (bf16[1024,128]{1,0:T(8,128)(2,1)S(1)}, bf16[1024,128]{1,0:T(8,128)(2,1)S(1)}, u32[]{:S(2)}, u32[]{:S(2)}) collective-permute-start(bf16[1024,128]{1,0:T(8,128)(2,1)S(1)} %get-tuple-element.85), channel_id=1, source_target_pairs={{0,1},{1,0},{2,3},{3,2},{4,5},{5,4},{6,7},{7,6},{8,9},{9,8},{10,11... | collective-permute-start | bytes 786440 | tf_op jit(solution)/shard_map/ppermute | solution.py:23
  74.0 19.3 %copy-start.5 = (bf16[1024,128]{1,0:T(8,128)(2,1)}, bf16[1024,128]{1,0:T(8,128)(2,1)S(1)}, u32[]{:S(2)}) copy-start(bf16[1024,128]{1,0:T(8,128)(2,1)S(1)} %collective-permute-done.12.refs_2_.refs_11_) | copy-start | bytes 786436
  74.4 19.0 %copy-start.7 = (bf16[1024,128]{1,0:T(8,128)(2,1)}, bf16[1024,128]{1,0:T(8,128)(2,1)S(1)}, u32[]{:S(2)}) copy-start(bf16[1024,128]{1,0:T(8,128)(2,1)S(1)} %collective-permute-done.13.refs_3_.refs_13_) | copy-start | bytes 786436
  74.4 19.0 %copy-start.13 = (bf16[512,512]{1,0:T(8,128)(2,1)}, bf16[512,512]{1,0:T(8,128)(2,1)S(1)}, u32[]{:S(2)}) copy-start(bf16[512,512]{1,0:T(8,128)(2,1)S(1)} %collective-permute-done.9.refs_2_) | copy-start | bytes 1572868
  74.4 7.1 %collective-permute-start.15 = (bf16[32,1024]{1,0:T(8,128)(2,1)S(1)}, bf16[32,1024]{1,0:T(8,128)(2,1)S(1)}, u32[]{:S(2)}, u32[]{:S(2)}) collective-permute-start(bf16[32,1024]{1,0:T(8,128)(2,1)S(1)} %get-tuple-element.87), channel_id=1, source_target_pairs={{0,8},{1,9},{2,10},{3,11},{4,12},{5,13},{6,14},{7,15},{8,0},{9,1},... | collective-permute-start | bytes 196616 | tf_op jit(solution)/shard_map/ppermute | solution.py:23
  76.2 6.1 %collective-permute-start.16 = (bf16[32,1024]{1,0:T(8,128)(2,1)S(1)}, bf16[32,1024]{1,0:T(8,128)(2,1)S(1)}, u32[]{:S(2)}, u32[]{:S(2)}) collective-permute-start(bf16[32,1024]{1,0:T(8,128)(2,1)S(1)} %get-tuple-element.87), channel_id=1, source_target_pairs={{0,12},{1,13},{2,14},{3,15},{4,8},{5,9},{6,10},{7,11},{8,4},{9,5},... | collective-permute-start | bytes 196616 | tf_op jit(solution)/shard_map/ppermute | solution.py:23
  79.2 11.7 %collective-permute-start.18 = (bf16[2048,128]{1,0:T(8,128)(2,1)S(1)}, bf16[2048,128]{1,0:T(8,128)(2,1)S(1)}, u32[]{:S(2)}, u32[]{:S(2)}) collective-permute-start(bf16[2048,128]{1,0:T(8,128)(2,1)S(1)} %get-tuple-element.86), channel_id=1, source_target_pairs={{0,1},{1,0},{2,3},{3,2},{4,5},{5,4},{6,7},{7,6},{8,9},{9,8},{10,11... | collective-permute-start | bytes 1572872 | tf_op jit(solution)/shard_map/ppermute | solution.py:23
  80.6 11.8 %collective-permute-start.19 = (bf16[2048,128]{1,0:T(8,128)(2,1)S(1)}, bf16[2048,128]{1,0:T(8,128)(2,1)S(1)}, u32[]{:S(2)}, u32[]{:S(2)}) collective-permute-start(bf16[2048,128]{1,0:T(8,128)(2,1)S(1)} %get-tuple-element.93), channel_id=1, source_target_pairs={{0,2},{1,3},{2,0},{3,1},{4,6},{5,7},{6,4},{7,5},{8,10},{9,11},{10,... | collective-permute-start | bytes 1572872 | tf_op jit(solution)/shard_map/ppermute | solution.py:23
  81.4 7.2 %collective-permute-start.17 = (bf16[512,256]{1,0:T(8,128)(2,1)S(1)}, bf16[512,256]{1,0:T(8,128)(2,1)S(1)}, u32[]{:S(2)}, u32[]{:S(2)}) collective-permute-start(bf16[512,256]{1,0:T(8,128)(2,1)S(1)} %shard_map.110), channel_id=1, source_target_pairs={{0,20},{1,21},{2,22},{3,23},{4,16},{5,17},{6,18},{7,19},{8,28},{9,... | collective-permute-start | bytes 786440 | tf_op jit(solution)/shard_map/ppermute | solution.py:33
  81.5 6.5 %collective-permute-start.14 = (bf16[32,1024]{1,0:T(8,128)(2,1)S(1)}, bf16[32,1024]{1,0:T(8,128)(2,1)S(1)}, u32[]{:S(2)}, u32[]{:S(2)}) collective-permute-start(bf16[32,1024]{1,0:T(8,128)(2,1)S(1)} %get-tuple-element.87), channel_id=1, source_target_pairs={{0,4},{1,5},{2,6},{3,7},{4,0},{5,1},{6,2},{7,3},{8,12},{9,13},{10,... | collective-permute-start | bytes 196616 | tf_op jit(solution)/shard_map/ppermute | solution.py:23
  88.6 6.3 %copy-start.15 = (bf16[512,256]{1,0:T(8,128)(2,1)}, bf16[512,256]{1,0:T(8,128)(2,1)S(1)}, u32[]{:S(2)}) copy-start(bf16[512,256]{1,0:T(8,128)(2,1)S(1)} %collective-permute-done.17.refs_3_) | copy-start | bytes 786436
  93.3 0.8 copy-start.9
  94.1 0.8 copy-start.11
  94.9 12.2 %collective-permute-start.20 = (bf16[1024,128]{1,0:T(8,128)(2,1)}, bf16[1024,128]{1,0:T(8,128)(2,1)}, u32[]{:S(2)}, u32[]{:S(2)}) collective-permute-start(bf16[1024,128]{1,0:T(8,128)(2,1)} %get-tuple-element.96), channel_id=1, source_target_pairs={{0,2},{1,3},{2,0},{3,1},{4,6},{5,7},{6,4},{7,5},{8,10},{9,11},{10,... | collective-permute-start | bytes 786440 | tf_op jit(solution)/shard_map/ppermute | solution.py:23
  95.5 11.7 %collective-permute-start.21 = (bf16[1024,128]{1,0:T(8,128)(2,1)}, bf16[1024,128]{1,0:T(8,128)(2,1)}, u32[]{:S(2)}, u32[]{:S(2)}) collective-permute-start(bf16[1024,128]{1,0:T(8,128)(2,1)} %get-tuple-element.98), channel_id=1, source_target_pairs={{0,4},{1,5},{2,6},{3,7},{4,0},{5,1},{6,2},{7,3},{8,12},{9,13},{10,... | collective-permute-start | bytes 786440 | tf_op jit(solution)/shard_map/ppermute | solution.py:23
  96.1 7.3 %copy-start.2 = (f32[1024,128]{1,0:T(8,128)S(1)}, f32[1024,128]{1,0:T(8,128)}, u32[]{:S(2)}) copy-start(f32[1024,128]{1,0:T(8,128)} %copy-done.1) | copy-start | bytes 1572868
  96.1 7.3 %copy-start.4 = (f32[1024,128]{1,0:T(8,128)S(1)}, f32[1024,128]{1,0:T(8,128)}, u32[]{:S(2)}) copy-start(f32[1024,128]{1,0:T(8,128)} %copy-done.3) | copy-start | bytes 1572868
  96.1 14.3 %collective-permute-start.26 = (bf16[128,256]{1,0:T(8,128)(2,1)S(1)}, bf16[128,256]{1,0:T(8,128)(2,1)S(1)}, u32[]{:S(2)}, u32[]{:S(2)}) collective-permute-start(bf16[128,256]{1,0:T(8,128)(2,1)S(1)} %get-tuple-element.102.refs_6_), channel_id=1, source_target_pairs={{0,4},{1,5},{2,6},{3,7},{4,0},{5,1},{6,2},{7,3},{8,12},{9,13},{10,... | collective-permute-start | bytes 196616 | tf_op jit(solution)/shard_map/ppermute | solution.py:23
  97.5 11.8 %collective-permute-start.27 = (bf16[64,256]{1,0:T(8,128)(2,1)S(1)}, bf16[64,256]{1,0:T(8,128)(2,1)S(1)}, u32[]{:S(2)}, u32[]{:S(2)}) collective-permute-start(bf16[64,256]{1,0:T(8,128)(2,1)S(1)} %bitcast.40), channel_id=1, source_target_pairs={{0,8},{1,9},{2,10},{3,11},{4,12},{5,13},{6,14},{7,15},{8,0},{9,1},... | collective-permute-start | bytes 98312 | tf_op jit(solution)/shard_map/ppermute | solution.py:23
  99.3 10.4 %collective-permute-start.28 = (bf16[64,256]{1,0:T(8,128)(2,1)S(1)}, bf16[64,256]{1,0:T(8,128)(2,1)S(1)}, u32[]{:S(2)}, u32[]{:S(2)}) collective-permute-start(bf16[64,256]{1,0:T(8,128)(2,1)S(1)} %bitcast.41), channel_id=1, source_target_pairs={{0,12},{1,13},{2,14},{3,15},{4,8},{5,9},{6,10},{7,11},{8,4},{9,5},... | collective-permute-start | bytes 98312 | tf_op jit(solution)/shard_map/ppermute | solution.py:23
  103.4 1.0 copy-start.6
  104.4 0.9 copy-start.8
  105.3 1.9 %copy-start.10 = (f32[1024,128]{1,0:T(8,128)S(1)}, f32[1024,128]{1,0:T(8,128)}, u32[]{:S(2)}) copy-start(f32[1024,128]{1,0:T(8,128)} %copy-done.9) | copy-start | bytes 1572868
  105.3 1.9 %copy-start.12 = (f32[1024,128]{1,0:T(8,128)S(1)}, f32[1024,128]{1,0:T(8,128)}, u32[]{:S(2)}) copy-start(f32[1024,128]{1,0:T(8,128)} %copy-done.11) | copy-start | bytes 1572868
  107.1 3.3 %copy-start = (bf16[1,1,2,256,1024]{4,3,2,1,0:T(8,128)(2,1)S(1)}, bf16[1,1,2,256,1024]{4,3,2,1,0:T(8,128)(2,1)}, u32[]{:S(2)}) copy-start(bf16[1,1,2,256,1024]{4,3,2,1,0:T(8,128)(2,1)} %param.8) | copy-start | bytes 3145732
  107.1 3.2 %copy-start.18 = (bf16[256,1024]{1,0:T(8,128)(2,1)S(1)}, bf16[256,1024]{1,0:T(8,128)(2,1)}, u32[]{:S(2)}) copy-start(bf16[256,1024]{1,0:T(8,128)(2,1)} %copy-done.17) | copy-start | bytes 1572868
  107.1 3.2 %copy-start.20 = (bf16[256,1024]{1,0:T(8,128)(2,1)S(1)}, bf16[256,1024]{1,0:T(8,128)(2,1)}, u32[]{:S(2)}) copy-start(bf16[256,1024]{1,0:T(8,128)(2,1)} %copy-done.19) | copy-start | bytes 1572868
  107.2 5.7 %collective-permute-start.25 = (bf16[512,768]{1,0:T(8,128)(2,1)S(1)}, bf16[512,768]{1,0:T(8,128)(2,1)S(1)}, u32[]{:S(2)}, u32[]{:S(2)}) collective-permute-start(bf16[512,768]{1,0:T(8,128)(2,1)S(1)} %shard_map.113), channel_id=1, source_target_pairs={{0,16},{1,17},{2,18},{3,19},{4,20},{5,21},{6,22},{7,23},{8,24},{9,... | collective-permute-start | bytes 2359304 | tf_op jit(solution)/shard_map/ppermute | solution.py:33
  109.0 6.1 %collective-permute-start.22 = (bf16[512,256]{1,0:T(8,128)(2,1)S(1)}, bf16[512,256]{1,0:T(8,128)(2,1)S(1)}, u32[]{:S(2)}, u32[]{:S(2)}) collective-permute-start(bf16[512,256]{1,0:T(8,128)(2,1)S(1)} %get-tuple-element.99), channel_id=1, source_target_pairs={{0,16},{1,17},{2,18},{3,19},{4,20},{5,21},{6,22},{7,23},{8,24},{9,... | collective-permute-start | bytes 786440 | tf_op jit(solution)/shard_map/ppermute | solution.py:33
  109.4 5.5 %collective-permute-start.23 = (bf16[512,128]{1,0:T(8,128)(2,1)S(1)}, bf16[512,128]{1,0:T(8,128)(2,1)S(1)}, u32[]{:S(2)}, u32[]{:S(2)}) collective-permute-start(bf16[512,128]{1,0:T(8,128)(2,1)S(1)} %get-tuple-element.100), channel_id=1, source_target_pairs={{0,20},{1,21},{2,22},{3,23},{4,16},{5,17},{6,18},{7,19},{8,28},{9,... | collective-permute-start | bytes 393224 | tf_op jit(solution)/shard_map/ppermute | solution.py:33
  109.7 3.1 %copy-start.14 = (bf16[512,512]{1,0:T(8,128)(2,1)S(1)}, bf16[512,512]{1,0:T(8,128)(2,1)}, u32[]{:S(2)}) copy-start(bf16[512,512]{1,0:T(8,128)(2,1)} %copy-done.13) | copy-start | bytes 1572868
  109.7 3.1 %copy-start.16 = (bf16[512,256]{1,0:T(8,128)(2,1)S(1)}, bf16[512,256]{1,0:T(8,128)(2,1)}, u32[]{:S(2)}) copy-start(bf16[512,256]{1,0:T(8,128)(2,1)} %copy-done.15) | copy-start | bytes 786436
  109.7 5.4 %collective-permute-start.24 = (bf16[512,128]{1,0:T(8,128)(2,1)S(1)}, bf16[512,128]{1,0:T(8,128)(2,1)S(1)}, u32[]{:S(2)}, u32[]{:S(2)}) collective-permute-start(bf16[512,128]{1,0:T(8,128)(2,1)S(1)} %get-tuple-element.101), channel_id=1, source_target_pairs={{0,17},{1,16},{2,19},{3,18},{4,21},{5,20},{6,23},{7,22},{8,25},{9,... | collective-permute-start | bytes 393224 | tf_op jit(solution)/shard_map/ppermute | solution.py:33

commit v11 on v10

--- a/solution.py
+++ b/solution.py
@@ -13,7 +13,8 @@
 SMEM = pl.BlockSpec(memory_space=pltpu.SMEM)
 VMEM = pl.BlockSpec(memory_space=pltpu.VMEM)
 TN = (((0,), (0,)), ((), ()))
-PARAMS = pltpu.CompilerParams(vmem_limit_bytes=24 * 2**20)
+PARAMS = pltpu.CompilerParams(vmem_limit_bytes=12 * 2**20)
+PRODUCT_PARAMS = pltpu.CompilerParams(vmem_limit_bytes=20 * 2**20)
 QUICK = pl.CostEstimate(flops=1000, bytes_accessed=1000, transcendentals=0)
 LONG = pl.CostEstimate(flops=4 * 10**10, bytes_accessed=1000, transcendentals=0)
 
@@ -152,7 +153,7 @@
             pltpu.VMEM(weight_blocks.shape, BF16),
             pltpu.SemaphoreType.DMA((blocks,)),
         ],
-        compiler_params=PARAMS,
+        compiler_params=PRODUCT_PARAMS,
         cost_estimate=cost,
     )(*in_hbm(*scalars), *grads, *in_hbm(weight_blocks, *more))
 
@@ -180,7 +181,7 @@
             outs[-1][...] = placed
 
 
-def halve(kept, got, placed=None):
+def halve(kept, got, placed=None, cost=QUICK):
     placed = [] if placed is None else [placed]
     extra = [placed[0].shape[0] if placed and not way else 0 for way in range(len(kept))]
     shapes = [(k.shape[0] // 2, k.shape[1]) for k in kept]
@@ -192,7 +193,7 @@
         + [jax.ShapeDtypeStruct(shape, F32) for shape in shapes]
         + [jax.ShapeDtypeStruct(p.shape, BF16) for p in placed],
         compiler_params=PARAMS,
-        cost_estimate=QUICK,
+        cost_estimate=cost,
     )(*kept, *got, *placed)
     ways = len(kept)
     return outs[:ways], outs[ways : 2 * ways], *outs[2 * ways :]
@@ -213,7 +214,7 @@
         refs[-1][...] = placed_ref[...] + got_refs[0][2 * kept_refs[0].shape[0] // 2 :, :]
 
 
-def last_parts(kept, got, placed=None):
+def last_parts(kept, got, placed=None, cost=QUICK):
     placed = [] if placed is None else [placed]
     shape = kept[0].shape[0] // 2, sum(k.shape[1] for k in kept)
     return pl.pallas_call(
@@ -223,32 +224,42 @@
         out_shape=[jax.ShapeDtypeStruct(shape, BF16)]
         + [jax.ShapeDtypeStruct(p.shape, BF16) for p in placed],
         compiler_params=PARAMS,
-        cost_estimate=QUICK,
+        cost_estimate=cost,
     )(*kept, *got, *placed)
 
 
 def up_body(low_size, tile_rows, pieces, tiles, micro_count, *refs):
     pos_ref, classes_ref, live_ref = refs[:3]
     grad_refs = refs[3 : 3 + tiles]
-    hidden_refs = refs[3 + tiles : -2]
+    placed_ref, near_ref, *far_refs = refs[3 + tiles : -2]
     out_ref, total_ref = refs[-2:]
     high = pos_ref[0] // low_size
     total_ref[...] = jnp.zeros_like(total_ref)
     rank_part = total_ref.shape[1]
+    skip = near_ref.shape[0] - placed_ref.shape[0]
     for tile, index, piece, first in pieces:
         k, m, offset = piece
         size = min(SEG, tile_rows)
         seg = segment_of(high, piece, tile_rows)
-        near_ref, far_ref = hidden_refs[2 * k : 2 * k + 2]
-        start = m * (near_ref.shape[0] // micro_count)
-        if k == 0:
-            start = pl.multiple_of(start + high * rank_part, rank_part)
+        lanes = slice(offset, offset + size)
 
         @pl.when(seg < live_ref[m])
         def _():
-            place = pl.ds(start, rank_part), slice(offset, offset + size)
+            if k == 0:
+                start = pl.multiple_of(
+                    m * (placed_ref.shape[0] // micro_count) + high * rank_part, rank_part
+                )
+                other = pl.multiple_of(skip + start, rank_part)
+                hidden = (
+                    placed_ref[pl.ds(start, rank_part), lanes]
+                    + near_ref[pl.ds(other, rank_part), lanes]
+                )
+            else:
+                rows = slice(skip + m * rank_part, skip + (m + 1) * rank_part)
+                one_ref, other_ref = far_refs[2 * k - 2 : 2 * k]
+                hidden = one_ref[rows, lanes] + other_ref[rows, lanes]
             total_ref[classes_ref[m, seg]] += jnp.dot(
-                near_ref[place] + far_ref[place],
+                hidden,
                 grad_refs[tile][index, first : first + size, :],
                 preferred_element_type=F32,
             )
@@ -332,29 +343,126 @@
         got1, pieces_of(1), True, True, True, LONG
     )
     parts.append(part)
-    own_third, placed = last_parts((after(kept_x, part), kept_y), (second_x, second_y), placed)
+    d_first_x, d_first_y = partner(d_sent_x, 1), partner(d_sent_y, 2)
+    own_third, placed = last_parts(
+        (after(kept_x, part, c_first_x, c_first_y), kept_y), (second_x, second_y), placed, LONG
+    )
     own_last = relay(own_third, 4)
     own_sums = (kept_x, second_x), (kept_y, second_y)
-    own_rank = jnp.concatenate(parts, 1)
-    shared = own_rank.astype(BF16)
-    for mask in (1, 2, 3):
-        own_rank = own_rank + partner(shared, mask)
-    (c_sent_x, c_sent_y), c_kept = halve((c_kept_x, c_kept_y), (c_first_x, c_first_y))
+
+    rows_total = len(order) * size
+    blocks = rows_total // tile_rows
+
+    def small(kernel, shapes, *operands, cost=QUICK):
+        return pl.pallas_call(
+            kernel,
+            in_specs=[VMEM] * len(operands),
+            out_specs=[VMEM] * len(shapes),
+            out_shape=[jax.ShapeDtypeStruct(*shape) for shape in shapes],
+            compiler_params=PARAMS,
+            cost_estimate=cost,
+        )(*operands)
+
+    def collect_kernel(*refs):
+        start = 0
+        for ref in refs[:-1]:
+            refs[-1][:, start : start + ref.shape[1]] = ref[...].astype(BF16)
+            start += ref.shape[1]
+
+    parts[-1] = after(parts[-1], own_third)
+    (shared,) = small(collect_kernel, [((rank_part, rows_total), BF16)], *parts)
+    flat = [partner(shared, mask) for mask in (1, 2, 3)]
+
+    (c_sent_x, c_sent_y), c_kept = halve(
+        (after(c_kept_x, shared), c_kept_y), (c_first_x, c_first_y), None, LONG
+    )
     c_second_x, c_second_y = partner(c_sent_x, 2), partner(c_sent_y, 1)
-    slot = own_rank, c_second_x, c_second_y
-    d_sent_x, d_sent_y = lax.optimization_barrier((d_sent_x, d_sent_y, *slot))[:2]
-    d_first_x, d_first_y = partner(d_sent_x, 1), partner(d_sent_y, 2)
-    shared = after(own_rank.astype(BF16), own_last, d_sent_x)
-    ranks = [(own_rank + partner(shared, 4)).astype(BF16)]
-    for j in range(1, high_size):
-        one, other = partner(shared, j * low_size), partner(shared, j * low_size + 4)
-        ranks.append((one.astype(F32) + other.astype(F32)).astype(BF16))
-    hiddens = [placed, partner(placed, 4)]
+    (d_sent_x, d_sent_y), d_kept = halve(
+        (after(d_kept_x, c_sent_x), d_kept_y), (d_first_x, d_first_y)
+    )
+    d_second_x, d_second_y = partner(d_sent_x, 2), partner(d_sent_y, 4)
+
+    wanted = placed.reshape(micro_count, rank, tile_rows)
+    wanted = [
+        lax.dynamic_slice_in_dim(wanted, (high ^ k) * rank_part, rank_part, 1).reshape(
+            micro_count * rank_part, tile_rows
+        )
+        for k in range(1, high_size)
+    ]
+
+    def spread_kernel(*refs):
+        count = len(parts)
+        part_refs, flat_refs, hidden_refs = refs[:count], refs[count : count + 3], refs[count + 3 : -1 - high_size]
+        *message_refs, total_ref = refs[-1 - high_size :]
+        start = 0
+        for part_ref in part_refs:
+            columns = slice(start, start + part_ref.shape[1])
+            total = part_ref[...]
+            for flat_ref in flat_refs:
+                total = total + flat_ref[:, columns].astype(F32)
+            total_ref[:, columns] = total
+            start += part_ref.shape[1]
+        for message_ref, hidden_ref in zip(message_refs, hidden_refs):
+            for block in range(blocks):
+                message_ref[block * rank_part : (block + 1) * rank_part, :] = total_ref[
+                    :, block * tile_rows : (block + 1) * tile_rows
+                ].astype(BF16)
+            message_ref[blocks * rank_part :, :] = hidden_ref[...]
+
+    *messages, total = small(
+        spread_kernel,
+        [
+            ((blocks * rank_part + hidden.shape[0], tile_rows), BF16)
+            for hidden in [placed, *wanted]
+        ]
+        + [((rank_part, rows_total), F32)],
+        *parts,
+        *flat,
+        after(placed, d_sent_x, own_last),
+        *wanted,
+        cost=LONG,
+    )
+    near = partner(messages[0], 4)
+    far = []
     for k in range(1, high_size):
-        wanted = placed.reshape(micro_count, rank, tile_rows)
-        wanted = lax.dynamic_slice_in_dim(wanted, (high ^ k) * rank_part, rank_part, 1)
-        wanted = wanted.reshape(micro_count * rank_part, tile_rows)
-        hiddens += [partner(wanted, k * low_size), partner(wanted, k * low_size + 4)]
+        far += [partner(messages[k], k * low_size), partner(messages[k], k * low_size + 4)]
+
+    def columns_of(j, piece):
+        k, m, offset = piece
+        at = order.index((k ^ j, m, offset))
+        return slice(at * size, (at + 1) * size)
+
+    def block_of(message_ref, columns):
+        block, start = columns.start // tile_rows, columns.start % tile_rows
+        rows = slice(block * rank_part, (block + 1) * rank_part)
+        return message_ref[rows, start : start + size].astype(F32)
+
+    def lowrank_kernel(high_ref, total_ref, near_ref, *refs):
+        *far_refs, out_ref, whole_ref = refs
+        for at, piece in enumerate(order):
+            columns = slice(at * size, (at + 1) * size)
+            for j in range(high_size):
+                if j == 0:
+                    value = total_ref[:, columns] + block_of(near_ref, columns)
+                else:
+                    other = columns_of(j, piece)
+                    value = block_of(far_refs[2 * j - 2], other) + block_of(far_refs[2 * j - 1], other)
+                start = pl.multiple_of(((high_ref[0] // low_size) ^ j) * rank_part, rank_part)
+                whole_ref[pl.ds(start, rank_part), columns] = value
+        out_ref[...] = whole_ref[...].astype(BF16)
+
+    lowrank = pl.pallas_call(
+        lowrank_kernel,
+        in_specs=[SMEM] + [VMEM] * (2 + len(far)),
+        out_specs=VMEM,
+        out_shape=jax.ShapeDtypeStruct((rank, rows_total), BF16),
+        scratch_shapes=[pltpu.VMEM((rank, rows_total), F32)],
+        compiler_params=PARAMS,
+        cost_estimate=QUICK,
+    )(*in_hbm(scalars[0]), total, near, *far)
+
+    (c_third,) = last_parts((after(c_kept[0], lowrank), c_kept[1]), (c_second_x, c_second_y))
+    c_last = relay(c_third, 4)
 
     all_grads, all_pieces = [], []
     for grads, pieces in chunks:
@@ -370,20 +478,14 @@
         scratch_shapes=[pltpu.VMEM(up_tile.shape, F32)],
         compiler_params=PARAMS,
         cost_estimate=LONG,
-    )(*in_hbm(*scalars), *all_grads, *hiddens)
-
-    def columns_of(j, piece):
-        k, m, offset = piece
-        at = order.index((k ^ j, m, offset))
-        return slice(at * size, (at + 1) * size)
-
-    down_parts = adapter_down_maps[0].reshape(class_count, high_size, rank_part, portion)
+    )(*in_hbm(*scalars), *all_grads, placed, near, *far)
+
+    down = adapter_down_maps[0]
 
     def adapter_kernel(first, with_last, groups, *refs):
-        pos_ref, classes_ref, _, down_ref = refs[:4]
-        rank_refs = refs[4 : 4 + high_size]
-        sum_refs = refs[4 + high_size : 4 + high_size + 2 * groups]
-        *last_refs, out_ref, total_ref = refs[4 + high_size + 2 * groups :]
+        pos_ref, classes_ref, _, down_ref, lowrank_ref = refs[:5]
+        sum_refs = refs[5 : 5 + 2 * groups]
+        *last_refs, out_ref, total_ref = refs[5 + 2 * groups :]
         own = pos_ref[0] // low_size
         start = 0
         for g in range(groups):
@@ -401,28 +503,27 @@
             piece = order[first + at]
             seg = segment_of(own, piece, tile_rows)
             rows = slice(at * size, (at + 1) * size)
-            adapter = total_ref[:, rows]
-            for j in range(high_size):
-                adapter = adapter + lax.dot_general(
-                    down_ref[classes_ref[piece[1], seg], own ^ j],
-                    rank_refs[j][:, columns_of(j, piece)],
-                    TN,
-                    preferred_element_type=F32,
-                )
-            out_ref[:, rows] = adapter.astype(BF16)
+            columns = slice((first + at) * size, (first + at + 1) * size)
+            adapter = lax.dot_general(
+                down_ref[classes_ref[piece[1], seg]],
+                lowrank_ref[:, columns],
+                TN,
+                preferred_element_type=F32,
+            )
+            out_ref[:, rows] = (total_ref[:, rows] + adapter).astype(BF16)
 
     def with_adapter(sums, first, with_last):
         counts = [kept.shape[1] for kept, _ in sums]
         shapes = [(portion, n) for n in counts] * with_last + [(portion, sum(counts))]
         outs = pl.pallas_call(
             functools.partial(adapter_kernel, first, with_last, len(sums)),
-            in_specs=[SMEM] * 3 + [VMEM] * (1 + high_size + 2 * len(sums)),
+            in_specs=[SMEM] * 3 + [VMEM] * (2 + 2 * len(sums)),
             out_specs=[VMEM] * len(shapes),
             out_shape=[jax.ShapeDtypeStruct(shape, BF16) for shape in shapes],
             scratch_shapes=[pltpu.VMEM(shapes[-1], F32)],
             compiler_params=PARAMS,
             cost_estimate=QUICK,
-        )(*in_hbm(*scalars), *in_hbm(down_parts), *ranks, *[a for two in sums for a in two])
+        )(*in_hbm(*scalars, down), lowrank, *[a for two in sums for a in two])
         return outs[:-1], outs[-1]
 
     def finish_kernel(first, groups, *refs):
@@ -472,47 +573,38 @@
             cost_estimate=QUICK,
         )(*in_hbm(scalars[0]), kept, *got, *before)
 
-    def down_kernel(pos_ref, classes_ref, live_ref, inputs_ref, *refs):
-        rank_refs, out_ref, total_ref = refs[:-2], refs[-2], refs[-1]
+    def down_kernel(pos_ref, classes_ref, live_ref, inputs_ref, lowrank_ref, out_ref, total_ref):
         own = pos_ref[0] // low_size
         total_ref[...] = jnp.zeros_like(total_ref)
-        for piece in order:
+        for at, piece in enumerate(order):
             k, m, offset = piece
             seg = segment_of(own, piece, tile_rows)
 
             @pl.when(seg < live_ref[m])
             def _():
                 base = pl.multiple_of((own ^ k) * tile_rows + offset, size)
-                rows = inputs_ref[m, pl.ds(base, size), :]
-                for j in range(high_size):
-                    total_ref[classes_ref[m, seg], own ^ j] += jnp.dot(
-                        rank_refs[j][:, columns_of(j, piece)], rows, preferred_element_type=F32
-                    )
+                total_ref[classes_ref[m, seg]] += jnp.dot(
+                    lowrank_ref[:, at * size : (at + 1) * size],
+                    inputs_ref[m, pl.ds(base, size), :],
+                    preferred_element_type=F32,
+                )
 
         out_ref[...] = total_ref[...].astype(BF16)
 
     down_map_gradient = pl.pallas_call(
         down_kernel,
-        in_specs=[SMEM] * 3 + [VMEM] * (1 + high_size),
+        in_specs=[SMEM] * 3 + [VMEM] * 2,
         out_specs=VMEM,
-        out_shape=jax.ShapeDtypeStruct(down_parts.shape, BF16),
-        scratch_shapes=[pltpu.VMEM(down_parts.shape, F32)],
+        out_shape=jax.ShapeDtypeStruct(down.shape, BF16),
+        scratch_shapes=[pltpu.VMEM(down.shape, F32)],
         compiler_params=PARAMS,
         cost_estimate=QUICK,
-    )(*in_hbm(*scalars, forward_input[0]), *ranks)
-
-    (c_third,) = last_parts(c_kept, (c_second_x, c_second_y))
-    c_last = relay(c_third, 4)
+    )(*in_hbm(*scalars, forward_input[0]), lowrank)
+
     c_sums = (c_kept[0], c_second_x), (c_kept[1], c_second_y)
     _, kept = with_adapter(own_sums + c_sums, 0, False)
     early = relay(kept, 0)
-    (d_sent_x, d_sent_y), d_kept = halve(
-        (after(d_kept_x, c_last, *ranks), d_kept_y), (d_first_x, d_first_y)
-    )
-    d_second_x, d_second_y = partner(d_sent_x, 2), partner(d_sent_y, 4)
-
-    d_kept_x = after(d_kept[0], down_map_gradient, kept)
-    d_sums = (d_kept_x, d_second_x), (d_kept[1], d_second_y)
+    d_sums = (d_kept[0], d_second_x), (d_kept[1], d_second_y)
     d_lasts, d_kept = with_adapter(d_sums, kept.shape[1] // size, True)
     d_last = [relay(d_lasts[0], 4), relay(d_lasts[1], 1)]
     d_kept = relay(d_kept, 0)
@@ -521,7 +613,7 @@
 
     return (
         grad_prev[None],
-        down_map_gradient.reshape(1, class_count, rank, portion),
+        down_map_gradient[None],
         up_map_gradient[None, None],
     )
 

time: 116 us -> 120 us (1.034)
  waiting for transfers between devices: 41 us -> 50.9 us
  starting transfers between devices: 32.3 us -> 26 us
  local copies, waits for them, and re-layouts: 5.63 us -> 3.61 us
  Pallas kernels: 36 us -> 37.8 us
    ppermute x23 -> x20, waiting for transfers between devices: 39.2 us -> 48.2 us  [partner(): return lax.ppermute(value, 'tensor', pairs)]
    ppermute x23 -> x20, starting transfers between devices: 30.7 us -> 23.2 us  [partner(): return lax.ppermute(value, 'tensor', pairs)]
    unnamed x44 -> x6, local copies, waits for them, and re-layouts: 3.56 us -> 1.37 us
    pallas_call x1 -> x4, Pallas kernels: 2.94 us -> 3.26 us  [the longest x1 3.17 us: shards(): pl.pallas_call(down_kernel, in_specs=[SMEM] * 3 + [VMEM] * 2, out_specs=V...]
  transfers between devices with their start and end apart: 29 -> 26, of which waited for: 14 -> 13; matrix products, arithmetic and copies ran while one was open for 0% -> 0% of each run, Pallas kernels for 30% -> 31%
where the time goes in v11:
time: 120 us; the launch traced here: 119 us
  waiting for transfers between devices  50.9 us (42%)
  Pallas kernels  37.8 us (31%)
  starting transfers between devices  26 us (22%)
  local copies, waits for them, and re-layouts  3.61 us (3%)
    ppermute x20, waiting for transfers between devices, partner(): return lax.ppermute(value, 'tensor', pairs)  48.2 us
    pallas_call x4, Pallas kernels, product(): pl.pallas_call(functools.partial(product_body, low_size, tile_rows, piece...  24.6 us
    ppermute x20, starting transfers between devices, partner(): return lax.ppermute(value, 'tensor', pairs)  23.2 us
    pallas_call x1, Pallas kernels, shards(): pl.pallas_call(down_kernel, in_specs=[SMEM] * 3 + [VMEM] * 2, out_specs=V...  3.17 us
    pallas_call x1, Pallas kernels, shards(): pl.pallas_call(functools.partial(up_body, low_size, tile_rows, all_pieces...  3.12 us
    pallas_call x2, Pallas kernels, with_adapter(): pl.pallas_call(functools.partial(adapter_kernel, first, with_last, len(su...  2.91 us
    ppermute x6, starting transfers between devices, relay(): return lax.ppermute(value, ('pipe', 'tensor'), pairs)  2.77 us
    ppermute x6, waiting for transfers between devices, relay(): return lax.ppermute(value, ('pipe', 'tensor'), pairs)  2.71 us
  transfers between devices with their start and end apart: 26, of which 13 were waited for; matrix products, arithmetic and copies ran while one was open for 0% of the time, Pallas kernels for 31%

profile of v11, /device:TPU:0, one launch (start us, length us, event | category | flops | bytes accessed | tf_op | source)
XLA Modules:
  0.0 119.1 jit_solution(16555539647459200344)
XLA Ops:
  0.6 2.2 %slice_bitcast_fusion = (bf16[256,1024]{1,0:T(8,128)(2,1)}, bf16[256,1024]{1,0:T(8,128)(2,1)}) fusion(bf16[1,1,2,256,1024]{4,3,2,1,0:T(8,128)(2,1)} %param.8), kind=kLoop, calls=%fused_computation | loop fusion | bytes 2097152 | tf_op jit(solution)/shard_map/squeeze | solution.py:330
  2.9 4.0 %collective-permute-start = (bf16[256,1024]{1,0:T(8,128)(2,1)}, bf16[256,1024]{1,0:T(8,128)(2,1)}, u32[]{:S(2)}, u32[]{:S(2)}) collective-permute-start(bf16[256,1024]{1,0:T(8,128)(2,1)} %get-tuple-element.110), channel_id=1, source_target_pairs={{0,8},{1,9},{2,10},{3,11},{4,12},{5,13},{6,14},{7,15},{8,0},{9,1},... | collective-permute-start | bytes 1572872 | tf_op jit(solution)/shard_map/ppermute | solution.py:24
  6.9 6.7 %shard_map.103 = (bf16[2176,256]{1,0:T(8,128)(2,1)}, bf16[2048,256]{1,0:T(8,128)(2,1)}, bf16[128,256]{1,0:T(8,128)(2,1)S(1)}) custom-call(s32[1]{0:T(128)} %bitcast.refs_0_.high_ref.pos_ref, s32[2,4]{1,0:T(2,128)} %bitcast.39, s32[2]{0:T(128)} %bitcast.48, bf16[2,256,1024]{2,1,0:T(8,128)(2,1)} %bitcast.20, bf16[8,512,1024]{2,1,0:T(8,128)(2,1)} %bitcast.27, ...), custom_call_target="tpu_custom_call" | custom-call | flops 1000 | bytes 1000 | tf_op jit(solution)/shard_map/pallas_call | solution.py:141
  13.6 1.6 %collective-permute-start.2 = (bf16[2176,256]{1,0:T(8,128)(2,1)}, bf16[2176,256]{1,0:T(8,128)(2,1)S(1)}, u32[]{:S(2)}, u32[]{:S(2)}) collective-permute-start(bf16[2176,256]{1,0:T(8,128)(2,1)} %get-tuple-element.60), channel_id=1, source_target_pairs={{0,1},{1,0},{2,3},{3,2},{4,5},{5,4},{6,7},{7,6},{8,9},{9,8},{10,11... | collective-permute-start | bytes 3342344 | tf_op jit(solution)/shard_map/ppermute | solution.py:24
  15.2 1.5 %collective-permute-start.3 = (bf16[2048,256]{1,0:T(8,128)(2,1)}, bf16[2048,256]{1,0:T(8,128)(2,1)}, u32[]{:S(2)}, u32[]{:S(2)}) collective-permute-start(bf16[2048,256]{1,0:T(8,128)(2,1)} %get-tuple-element.61), channel_id=1, source_target_pairs={{0,2},{1,3},{2,0},{3,1},{4,6},{5,7},{6,4},{7,5},{8,10},{9,11},{10,... | collective-permute-start | bytes 3145736 | tf_op jit(solution)/shard_map/ppermute | solution.py:24
  16.7 5.8 %shard_map.104 = (f32[2048,256]{1,0:T(8,128)S(1)}, f32[2048,256]{1,0:T(8,128)S(1)}, f32[32,512]{1,0:T(8,128)S(1)}) custom-call(s32[1]{0:T(128)} %bitcast.refs_0_.high_ref.pos_ref, s32[2,4]{1,0:T(2,128)} %bitcast.40, s32[2]{0:T(128)} %bitcast.49, bf16[2,256,1024]{2,1,0:T(8,128)(2,1)} %bitcast.21, bf16[8,512,1024]{2,1,0:T(8,128)(2,1)} %bitcast.28, ...), custom_call_target="tpu_custom_call" | custom-call | flops 1000 | bytes 1000 | tf_op jit(solution)/shard_map/pallas_call | solution.py:141
  22.5 1.4 %copy-done.1 = f32[2048,256]{1,0:T(8,128)} copy-done((f32[2048,256]{1,0:T(8,128)}, f32[2048,256]{1,0:T(8,128)S(1)}, u32[]{:S(2)}) %copy-start.1) | copy-done | bytes 2097176
  23.9 6.5 %collective-permute-done = bf16[256,1024]{1,0:T(8,128)(2,1)} collective-permute-done((bf16[256,1024]{1,0:T(8,128)(2,1)}, bf16[256,1024]{1,0:T(8,128)(2,1)}, u32[]{:S(2)}, u32[]{:S(2)}) %collective-permute-start) | collective-permute-done | bytes 524320 | tf_op jit(solution)/shard_map/ppermute | solution.py:24
  30.4 0.0 collective-permute-start.1
  30.4 6.2 %shard_map.105 = (bf16[2048,128]{1,0:T(8,128)(2,1)S(1)}, bf16[2048,128]{1,0:T(8,128)(2,1)S(1)}, f32[2048,128]{1,0:T(8,128)S(1)}, f32[2048,128]{1,0:T(8,128)S(1)}, f32[32,256]{1,0:T(8,128)S(1)}) custom-call(s32[1]{0:T(128)} %bitcast.refs_0_.high_ref.pos_ref, s32[2,4]{1,0:T(2,128)} %bitcast.41, s32[2]{0:T(128)} %bitcast.50, ...), custom_call_target="tpu_custom_call" | custom-call | flops 40000000000 | bytes 1000 | tf_op jit(solution)/shard_map/pallas_call | solution.py:141
  36.6 3.3 %collective-permute-done.3.refs_3_ = bf16[2048,256]{1,0:T(8,128)(2,1)} collective-permute-done((bf16[2048,256]{1,0:T(8,128)(2,1)}, bf16[2048,256]{1,0:T(8,128)(2,1)}, u32[]{:S(2)}, u32[]{:S(2)}) %collective-permute-start.3) | collective-permute-done | bytes 1048608 | tf_op jit(solution)/shard_map/ppermute | solution.py:24
  39.8 0.1 collective-permute-done.2.refs_2_
  39.9 1.6 %shard_map.107 = (bf16[1152,256]{1,0:T(8,128)(2,1)S(1)}, bf16[1024,256]{1,0:T(8,128)(2,1)S(1)}, f32[1024,256]{1,0:T(8,128)S(1)}, f32[1024,256]{1,0:T(8,128)S(1)}, bf16[128,256]{1,0:T(8,128)(2,1)S(1)}) custom-call(f32[2048,256]{1,0:T(8,128)S(1)} %get-tuple-element.69.refs_0_, f32[2048,256]{1,0:T(8,128)S(1)} %copy-done.2, ...), custom_call_target="tpu_custom_call" | custom-call | flops 1000 | bytes 1000 | tf_op jit(solution)/shard_map/pallas_call | solution.py:188
  41.5 1.6 %collective-permute-start.6 = (bf16[1152,256]{1,0:T(8,128)(2,1)S(1)}, bf16[1152,256]{1,0:T(8,128)(2,1)S(1)}, u32[]{:S(2)}, u32[]{:S(2)}) collective-permute-start(bf16[1152,256]{1,0:T(8,128)(2,1)S(1)} %get-tuple-element.74), channel_id=1, source_target_pairs={{0,2},{1,3},{2,0},{3,1},{4,6},{5,7},{6,4},{7,5},{8,10},{9,11},{10,... | collective-permute-start | bytes 1769480 | tf_op jit(solution)/shard_map/ppermute | solution.py:24
  43.1 1.5 %collective-permute-start.7 = (bf16[1024,256]{1,0:T(8,128)(2,1)S(1)}, bf16[1024,256]{1,0:T(8,128)(2,1)S(1)}, u32[]{:S(2)}, u32[]{:S(2)}) collective-permute-start(bf16[1024,256]{1,0:T(8,128)(2,1)S(1)} %get-tuple-element.75), channel_id=1, source_target_pairs={{0,1},{1,0},{2,3},{3,2},{4,5},{5,4},{6,7},{7,6},{8,9},{9,8},{10,11... | collective-permute-start | bytes 1572872 | tf_op jit(solution)/shard_map/ppermute | solution.py:24
  44.5 0.5 collective-permute-start.5
  45.1 0.5 collective-permute-start.4
  45.6 10.2 %collective-permute-done.1 = bf16[256,1024]{1,0:T(8,128)(2,1)S(1)} collective-permute-done((bf16[256,1024]{1,0:T(8,128)(2,1)}, bf16[256,1024]{1,0:T(8,128)(2,1)S(1)}, u32[]{:S(2)}, u32[]{:S(2)}) %collective-permute-start.1) | collective-permute-done | bytes 524320 | tf_op jit(solution)/shard_map/ppermute | solution.py:24
  55.8 5.9 %shard_map.106 = (bf16[2048,128]{1,0:T(8,128)(2,1)S(1)}, bf16[2048,128]{1,0:T(8,128)(2,1)S(1)}, f32[2048,128]{1,0:T(8,128)S(1)}, f32[2048,128]{1,0:T(8,128)S(1)}, f32[32,256]{1,0:T(8,128)S(1)}) custom-call(s32[1]{0:T(128)} %bitcast.refs_0_.high_ref.pos_ref, s32[2,4]{1,0:T(2,128)} %bitcast.42, s32[2]{0:T(128)} %bitcast.51, ...), custom_call_target="tpu_custom_call" | custom-call | flops 40000000000 | bytes 1000 | tf_op jit(solution)/shard_map/pallas_call | solution.py:141
  61.7 1.3 %collective-permute-start.11 = (bf16[2048,128]{1,0:T(8,128)(2,1)S(1)}, bf16[2048,128]{1,0:T(8,128)(2,1)S(1)}, u32[]{:S(2)}, u32[]{:S(2)}) collective-permute-start(bf16[2048,128]{1,0:T(8,128)(2,1)S(1)} %get-tuple-element.92), channel_id=1, source_target_pairs={{0,1},{1,0},{2,3},{3,2},{4,5},{5,4},{6,7},{7,6},{8,9},{9,8},{10,11... | collective-permute-start | bytes 1572872 | tf_op jit(solution)/shard_map/ppermute | solution.py:24
  63.0 3.7 %collective-permute-done.5.refs_3_ = bf16[2048,128]{1,0:T(8,128)(2,1)S(1)} collective-permute-done((bf16[2048,128]{1,0:T(8,128)(2,1)S(1)}, bf16[2048,128]{1,0:T(8,128)(2,1)S(1)}, u32[]{:S(2)}, u32[]{:S(2)}) %collective-permute-start.5) | collective-permute-done | bytes 524320 | tf_op jit(solution)/shard_map/ppermute | solution.py:24
  66.8 1.5 %collective-permute-start.12 = (bf16[2048,128]{1,0:T(8,128)(2,1)S(1)}, bf16[2048,128]{1,0:T(8,128)(2,1)S(1)}, u32[]{:S(2)}, u32[]{:S(2)}) collective-permute-start(bf16[2048,128]{1,0:T(8,128)(2,1)S(1)} %get-tuple-element.93), channel_id=1, source_target_pairs={{0,2},{1,3},{2,0},{3,1},{4,6},{5,7},{6,4},{7,5},{8,10},{9,11},{10,... | collective-permute-start | bytes 1572872 | tf_op jit(solution)/shard_map/ppermute | solution.py:24
  68.3 0.9 collective-permute-done.4.refs_2_
  69.2 0.0 collective-permute-done.7.refs_3_.refs_8_
  69.2 0.0 collective-permute-done.6.refs_2_.refs_6_
  69.2 0.1 shard_map.108
  69.3 0.1 collective-permute-start.13
  69.4 1.5 %collective-permute-start.10 = (bf16[32,1024]{1,0:T(8,128)(2,1)S(1)}, bf16[32,1024]{1,0:T(8,128)(2,1)S(1)}, u32[]{:S(2)}, u32[]{:S(2)}) collective-permute-start(bf16[32,1024]{1,0:T(8,128)(2,1)S(1)} %shard_map.109), channel_id=1, source_target_pairs={{0,3},{1,2},{2,1},{3,0},{4,7},{5,6},{6,5},{7,4},{8,11},{9,10},{10,... | collective-permute-start | bytes 196616 | tf_op jit(solution)/shard_map/ppermute | solution.py:24
  70.8 0.5 collective-permute-start.8
  71.4 0.2 shard_map.110
  71.6 7.7 %collective-permute-done.11.refs_2_ = bf16[2048,128]{1,0:T(8,128)(2,1)S(1)} collective-permute-done((bf16[2048,128]{1,0:T(8,128)(2,1)S(1)}, bf16[2048,128]{1,0:T(8,128)(2,1)S(1)}, u32[]{:S(2)}, u32[]{:S(2)}) %collective-permute-start.11) | collective-permute-done | bytes 524320 | tf_op jit(solution)/shard_map/ppermute | solution.py:24
  79.2 0.5 collective-permute-start.9
  79.7 0.8 collective-permute-done.12.refs_3_
  80.5 0.2 shard_map.111
  80.7 2.7 %collective-permute-done.13.refs_2_ = bf16[512,512]{1,0:T(8,128)(2,1)S(1)} collective-permute-done((bf16[512,512]{1,0:T(8,128)(2,1)S(1)}, bf16[512,512]{1,0:T(8,128)(2,1)S(1)}, u32[]{:S(2)}, u32[]{:S(2)}) %collective-permute-start.13) | collective-permute-done | bytes 524320 | tf_op jit(solution)/shard_map/ppermute | solution.py:34
  83.4 0.0 collective-permute-done.10.refs_5_
  83.4 0.0 collective-permute-done.8.refs_3_
  83.4 0.1 collective-permute-done.9.refs_4_
  83.5 0.4 collective-permute-start.15
  83.9 0.8 collective-permute-start.22
  84.7 1.2 %collective-permute-start.23 = (bf16[1024,128]{1,0:T(8,128)(2,1)S(1)}, bf16[1024,128]{1,0:T(8,128)(2,1)S(1)}, u32[]{:S(2)}, u32[]{:S(2)}) collective-permute-start(bf16[1024,128]{1,0:T(8,128)(2,1)S(1)} %get-tuple-element.107), channel_id=1, source_target_pairs={{0,1},{1,0},{2,3},{3,2},{4,5},{5,4},{6,7},{7,6},{8,9},{9,8},{10,11... | collective-permute-start | bytes 786440 | tf_op jit(solution)/shard_map/ppermute | solution.py:24
  85.9 1.5 %collective-permute-start.17 = (bf16[1024,128]{1,0:T(8,128)(2,1)S(1)}, bf16[1024,128]{1,0:T(8,128)(2,1)S(1)}, u32[]{:S(2)}, u32[]{:S(2)}) collective-permute-start(bf16[1024,128]{1,0:T(8,128)(2,1)S(1)} %get-tuple-element.94), channel_id=1, source_target_pairs={{0,2},{1,3},{2,0},{3,1},{4,6},{5,7},{6,4},{7,5},{8,10},{9,11},{10,... | collective-permute-start | bytes 786440 | tf_op jit(solution)/shard_map/ppermute | solution.py:24
  87.5 1.7 %collective-permute-start.18 = (bf16[1024,128]{1,0:T(8,128)(2,1)S(1)}, bf16[1024,128]{1,0:T(8,128)(2,1)S(1)}, u32[]{:S(2)}, u32[]{:S(2)}) collective-permute-start(bf16[1024,128]{1,0:T(8,128)(2,1)S(1)} %get-tuple-element.101), channel_id=1, source_target_pairs={{0,4},{1,5},{2,6},{3,7},{4,0},{5,1},{6,2},{7,3},{8,12},{9,13},{10,... | collective-permute-start | bytes 786440 | tf_op jit(solution)/shard_map/ppermute | solution.py:24
  89.2 1.5 %collective-permute-done.15.refs_0_.refs_8_ = bf16[192,256]{1,0:T(8,128)(2,1)S(1)} collective-permute-done((bf16[192,256]{1,0:T(8,128)(2,1)S(1)}, bf16[192,256]{1,0:T(8,128)(2,1)S(1)}, u32[]{:S(2)}, u32[]{:S(2)}) %collective-permute-start.15) | collective-permute-done | bytes 98336 | tf_op jit(solution)/shard_map/ppermute | solution.py:24
  90.7 1.0 collective-permute-start.16
  91.6 8.5 %collective-permute-done.16.refs_1_.refs_9_ = bf16[192,256]{1,0:T(8,128)(2,1)S(1)} collective-permute-done((bf16[192,256]{1,0:T(8,128)(2,1)S(1)}, bf16[192,256]{1,0:T(8,128)(2,1)S(1)}, u32[]{:S(2)}, u32[]{:S(2)}) %collective-permute-start.16) | collective-permute-done | bytes 98336 | tf_op jit(solution)/shard_map/ppermute | solution.py:24
  100.1 0.0 collective-permute-start.14
  100.1 5.0 %collective-permute-done.14.near_ref.refs_7_ = bf16[256,256]{1,0:T(8,128)(2,1)S(1)} collective-permute-done((bf16[256,256]{1,0:T(8,128)(2,1)S(1)}, bf16[256,256]{1,0:T(8,128)(2,1)S(1)}, u32[]{:S(2)}, u32[]{:S(2)}) %collective-permute-start.14) | collective-permute-done | bytes 131104 | tf_op jit(solution)/shard_map/ppermute | solution.py:24
  105.2 0.0 collective-permute-done.22.refs_10_.refs_2_
  105.2 0.0 collective-permute-done.23.refs_12_.refs_3_
  105.2 0.1 shard_map.116
  105.2 0.1 collective-permute-start.25
  105.3 1.5 %shard_map.115 = bf16[512,768]{1,0:T(8,128)(2,1)S(1)} custom-call(s32[1]{0:T(128)} %bitcast.refs_0_.high_ref.pos_ref, s32[2,4]{1,0:T(2,128)} %bitcast.43, s32[2]{0:T(128)} %bitcast.52, bf16[8,64,512]{2,1,0:T(8,128)(2,1)} %bitcast.32, bf16[64,1024]{1,0:T(8,128)(2,1)S(1)} %shard_map.113.refs_4_.lowrank_ref, f32[1024,256]{1,0:T(8,128)S(1)} %get-tuple-element.79.refs_0_.refs_5_, ...), custom_call_target="tpu_custom_call" | custom-call | flops 1000 | bytes 1000 | tf_op jit(solution)/shard_map/pallas_call | solution.py:518
  106.8 0.0 copy-start
  106.8 0.2 collective-permute-start.24
  107.0 0.0 collective-permute-done.17.refs_6_
  107.0 1.4 %shard_map.114 = (bf16[512,128]{1,0:T(8,128)(2,1)S(1)}, bf16[512,128]{1,0:T(8,128)(2,1)S(1)}, bf16[512,256]{1,0:T(8,128)(2,1)S(1)}) custom-call(s32[1]{0:T(128)} %bitcast.refs_0_.high_ref.pos_ref, s32[2,4]{1,0:T(2,128)} %bitcast.44, s32[2]{0:T(128)} %bitcast.53, bf16[8,64,512]{2,1,0:T(8,128)(2,1)} %bitcast.33, ...), custom_call_target="tpu_custom_call" | custom-call | flops 1000 | bytes 1000 | tf_op jit(solution)/shard_map/pallas_call | solution.py:518
  108.4 0.4 collective-permute-start.19
  108.8 1.7 %collective-permute-start.20 = (bf16[512,128]{1,0:T(8,128)(2,1)S(1)}, bf16[512,128]{1,0:T(8,128)(2,1)S(1)}, u32[]{:S(2)}, u32[]{:S(2)}) collective-permute-start(bf16[512,128]{1,0:T(8,128)(2,1)S(1)} %get-tuple-element.103), channel_id=1, source_target_pairs={{0,20},{1,21},{2,22},{3,23},{4,16},{5,17},{6,18},{7,19},{8,28},{9,... | collective-permute-start | bytes 393224 | tf_op jit(solution)/shard_map/ppermute | solution.py:34
  110.6 0.3 collective-permute-start.21
  110.9 3.1 %shard_map.120 = bf16[8,32,1024]{2,1,0:T(8,128)(2,1)} custom-call(s32[1]{0:T(128)} %bitcast.refs_0_.high_ref.pos_ref, s32[2,4]{1,0:T(2,128)} %bitcast.45, s32[2]{0:T(128)} %bitcast.54, bf16[2,256,1024]{2,1,0:T(8,128)(2,1)S(1)} %bitcast.22, bf16[1,256,1024]{2,1,0:T(8,128)(2,1)} %bitcast.9.refs_3_.refs_4_, bf16[1,256,1024]{2,1,0:T(8,128)(2,1)S(1)} %bitcast.26, ...), custom_call_target="tpu_custom_call" | custom-call | flops 40000000000 | bytes 1000 | tf_op jit(solution)/shard_map/pallas_call | solution.py:471
  114.0 3.2 %shard_map.119 = bf16[8,64,512]{2,1,0:T(8,128)(2,1)} custom-call(s32[1]{0:T(128)} %bitcast.refs_0_.high_ref.pos_ref, s32[2,4]{1,0:T(2,128)} %bitcast.46, s32[2]{0:T(128)} %bitcast.55, bf16[2,512,512]{2,1,0:T(8,128)(2,1)} %bitcast.34, bf16[64,1024]{1,0:T(8,128)(2,1)S(1)} %shard_map.113.refs_4_.lowrank_ref), custom_call_target="tpu_custom_call" | custom-call | flops 1000 | bytes 1000 | tf_op jit(solution)/shard_map/pallas_call | solution.py:594
  117.2 1.1 shard_map.117.refs_4_
  118.3 0.8 shard_map.118
  (14 shorter events, 0.1 us)
Async XLA Ops:
  2.9 27.5 %collective-permute-start = (bf16[256,1024]{1,0:T(8,128)(2,1)}, bf16[256,1024]{1,0:T(8,128)(2,1)}, u32[]{:S(2)}, u32[]{:S(2)}) collective-permute-start(bf16[256,1024]{1,0:T(8,128)(2,1)} %get-tuple-element.110), channel_id=1, source_target_pairs={{0,8},{1,9},{2,10},{3,11},{4,12},{5,13},{6,14},{7,15},{8,0},{9,1},... | collective-permute-start | bytes 1572872 | tf_op jit(solution)/shard_map/ppermute | solution.py:24
  13.6 26.3 %collective-permute-start.2 = (bf16[2176,256]{1,0:T(8,128)(2,1)}, bf16[2176,256]{1,0:T(8,128)(2,1)S(1)}, u32[]{:S(2)}, u32[]{:S(2)}) collective-permute-start(bf16[2176,256]{1,0:T(8,128)(2,1)} %get-tuple-element.60), channel_id=1, source_target_pairs={{0,1},{1,0},{2,3},{3,2},{4,5},{5,4},{6,7},{7,6},{8,9},{9,8},{10,11... | collective-permute-start | bytes 3342344 | tf_op jit(solution)/shard_map/ppermute | solution.py:24
  15.2 24.7 %collective-permute-start.3 = (bf16[2048,256]{1,0:T(8,128)(2,1)}, bf16[2048,256]{1,0:T(8,128)(2,1)}, u32[]{:S(2)}, u32[]{:S(2)}) collective-permute-start(bf16[2048,256]{1,0:T(8,128)(2,1)} %get-tuple-element.61), channel_id=1, source_target_pairs={{0,2},{1,3},{2,0},{3,1},{4,6},{5,7},{6,4},{7,5},{8,10},{9,11},{10,... | collective-permute-start | bytes 3145736 | tf_op jit(solution)/shard_map/ppermute | solution.py:24
  22.5 1.4 %copy-start.1 = (f32[2048,256]{1,0:T(8,128)}, f32[2048,256]{1,0:T(8,128)S(1)}, u32[]{:S(2)}) copy-start(f32[2048,256]{1,0:T(8,128)S(1)} %get-tuple-element.70.refs_1_) | copy-start | bytes 6291460
  30.4 9.5 %copy-start.2 = (f32[2048,256]{1,0:T(8,128)S(1)}, f32[2048,256]{1,0:T(8,128)}, u32[]{:S(2)}) copy-start(f32[2048,256]{1,0:T(8,128)} %copy-done.1) | copy-start | bytes 6291460
  30.4 25.5 %collective-permute-start.1 = (bf16[256,1024]{1,0:T(8,128)(2,1)}, bf16[256,1024]{1,0:T(8,128)(2,1)S(1)}, u32[]{:S(2)}, u32[]{:S(2)}) collective-permute-start(bf16[256,1024]{1,0:T(8,128)(2,1)} %get-tuple-element.66), channel_id=1, source_target_pairs={{0,8},{1,9},{2,10},{3,11},{4,12},{5,13},{6,14},{7,15},{8,0},{9,1},... | collective-permute-start | bytes 1572872 | tf_op jit(solution)/shard_map/ppermute | solution.py:24
  41.5 27.7 %collective-permute-start.6 = (bf16[1152,256]{1,0:T(8,128)(2,1)S(1)}, bf16[1152,256]{1,0:T(8,128)(2,1)S(1)}, u32[]{:S(2)}, u32[]{:S(2)}) collective-permute-start(bf16[1152,256]{1,0:T(8,128)(2,1)S(1)} %get-tuple-element.74), channel_id=1, source_target_pairs={{0,2},{1,3},{2,0},{3,1},{4,6},{5,7},{6,4},{7,5},{8,10},{9,11},{10,... | collective-permute-start | bytes 1769480 | tf_op jit(solution)/shard_map/ppermute | solution.py:24
  43.1 26.1 %collective-permute-start.7 = (bf16[1024,256]{1,0:T(8,128)(2,1)S(1)}, bf16[1024,256]{1,0:T(8,128)(2,1)S(1)}, u32[]{:S(2)}, u32[]{:S(2)}) collective-permute-start(bf16[1024,256]{1,0:T(8,128)(2,1)S(1)} %get-tuple-element.75), channel_id=1, source_target_pairs={{0,1},{1,0},{2,3},{3,2},{4,5},{5,4},{6,7},{7,6},{8,9},{9,8},{10,11... | collective-permute-start | bytes 1572872 | tf_op jit(solution)/shard_map/ppermute | solution.py:24
  44.5 22.2 %collective-permute-start.5 = (bf16[2048,128]{1,0:T(8,128)(2,1)S(1)}, bf16[2048,128]{1,0:T(8,128)(2,1)S(1)}, u32[]{:S(2)}, u32[]{:S(2)}) collective-permute-start(bf16[2048,128]{1,0:T(8,128)(2,1)S(1)} %get-tuple-element.78), channel_id=1, source_target_pairs={{0,2},{1,3},{2,0},{3,1},{4,6},{5,7},{6,4},{7,5},{8,10},{9,11},{10,... | collective-permute-start | bytes 1572872 | tf_op jit(solution)/shard_map/ppermute | solution.py:24
  45.1 24.1 %collective-permute-start.4 = (bf16[2048,128]{1,0:T(8,128)(2,1)S(1)}, bf16[2048,128]{1,0:T(8,128)(2,1)S(1)}, u32[]{:S(2)}, u32[]{:S(2)}) collective-permute-start(bf16[2048,128]{1,0:T(8,128)(2,1)S(1)} %get-tuple-element.76), channel_id=1, source_target_pairs={{0,1},{1,0},{2,3},{3,2},{4,5},{5,4},{6,7},{7,6},{8,9},{9,8},{10,11... | collective-permute-start | bytes 1572872 | tf_op jit(solution)/shard_map/ppermute | solution.py:24
  61.7 17.5 %collective-permute-start.11 = (bf16[2048,128]{1,0:T(8,128)(2,1)S(1)}, bf16[2048,128]{1,0:T(8,128)(2,1)S(1)}, u32[]{:S(2)}, u32[]{:S(2)}) collective-permute-start(bf16[2048,128]{1,0:T(8,128)(2,1)S(1)} %get-tuple-element.92), channel_id=1, source_target_pairs={{0,1},{1,0},{2,3},{3,2},{4,5},{5,4},{6,7},{7,6},{8,9},{9,8},{10,11... | collective-permute-start | bytes 1572872 | tf_op jit(solution)/shard_map/ppermute | solution.py:24
  66.8 13.8 %collective-permute-start.12 = (bf16[2048,128]{1,0:T(8,128)(2,1)S(1)}, bf16[2048,128]{1,0:T(8,128)(2,1)S(1)}, u32[]{:S(2)}, u32[]{:S(2)}) collective-permute-start(bf16[2048,128]{1,0:T(8,128)(2,1)S(1)} %get-tuple-element.93), channel_id=1, source_target_pairs={{0,2},{1,3},{2,0},{3,1},{4,6},{5,7},{6,4},{7,5},{8,10},{9,11},{10,... | collective-permute-start | bytes 1572872 | tf_op jit(solution)/shard_map/ppermute | solution.py:24
  69.3 14.2 %collective-permute-start.13 = (bf16[512,512]{1,0:T(8,128)(2,1)S(1)}, bf16[512,512]{1,0:T(8,128)(2,1)S(1)}, u32[]{:S(2)}, u32[]{:S(2)}) collective-permute-start(bf16[512,512]{1,0:T(8,128)(2,1)S(1)} %get-tuple-element.82), channel_id=1, source_target_pairs={{0,20},{1,21},{2,22},{3,23},{4,16},{5,17},{6,18},{7,19},{8,28},{9,... | collective-permute-start | bytes 1572872 | tf_op jit(solution)/shard_map/ppermute | solution.py:34
  69.4 14.1 %collective-permute-start.10 = (bf16[32,1024]{1,0:T(8,128)(2,1)S(1)}, bf16[32,1024]{1,0:T(8,128)(2,1)S(1)}, u32[]{:S(2)}, u32[]{:S(2)}) collective-permute-start(bf16[32,1024]{1,0:T(8,128)(2,1)S(1)} %shard_map.109), channel_id=1, source_target_pairs={{0,3},{1,2},{2,1},{3,0},{4,7},{5,6},{6,5},{7,4},{8,11},{9,10},{10,... | collective-permute-start | bytes 196616 | tf_op jit(solution)/shard_map/ppermute | solution.py:24
  70.8 12.6 %collective-permute-start.8 = (bf16[32,1024]{1,0:T(8,128)(2,1)S(1)}, bf16[32,1024]{1,0:T(8,128)(2,1)S(1)}, u32[]{:S(2)}, u32[]{:S(2)}) collective-permute-start(bf16[32,1024]{1,0:T(8,128)(2,1)S(1)} %shard_map.109), channel_id=1, source_target_pairs={{0,1},{1,0},{2,3},{3,2},{4,5},{5,4},{6,7},{7,6},{8,9},{9,8},{10,11... | collective-permute-start | bytes 196616 | tf_op jit(solution)/shard_map/ppermute | solution.py:24
  79.2 4.3 %collective-permute-start.9 = (bf16[32,1024]{1,0:T(8,128)(2,1)S(1)}, bf16[32,1024]{1,0:T(8,128)(2,1)S(1)}, u32[]{:S(2)}, u32[]{:S(2)}) collective-permute-start(bf16[32,1024]{1,0:T(8,128)(2,1)S(1)} %shard_map.109), channel_id=1, source_target_pairs={{0,2},{1,3},{2,0},{3,1},{4,6},{5,7},{6,4},{7,5},{8,10},{9,11},{10,... | collective-permute-start | bytes 196616 | tf_op jit(solution)/shard_map/ppermute | solution.py:24
  83.5 7.1 %collective-permute-start.15 = (bf16[192,256]{1,0:T(8,128)(2,1)S(1)}, bf16[192,256]{1,0:T(8,128)(2,1)S(1)}, u32[]{:S(2)}, u32[]{:S(2)}) collective-permute-start(bf16[192,256]{1,0:T(8,128)(2,1)S(1)} %get-tuple-element.98), channel_id=1, source_target_pairs={{0,8},{1,9},{2,10},{3,11},{4,12},{5,13},{6,14},{7,15},{8,0},{9,1},... | collective-permute-start | bytes 294920 | tf_op jit(solution)/shard_map/ppermute | solution.py:24
  83.9 21.2 %collective-permute-start.22 = (bf16[1024,128]{1,0:T(8,128)(2,1)S(1)}, bf16[1024,128]{1,0:T(8,128)(2,1)S(1)}, u32[]{:S(2)}, u32[]{:S(2)}) collective-permute-start(bf16[1024,128]{1,0:T(8,128)(2,1)S(1)} %get-tuple-element.89), channel_id=1, source_target_pairs={{0,2},{1,3},{2,0},{3,1},{4,6},{5,7},{6,4},{7,5},{8,10},{9,11},{10,... | collective-permute-start | bytes 786440 | tf_op jit(solution)/shard_map/ppermute | solution.py:24
  84.7 20.5 %collective-permute-start.23 = (bf16[1024,128]{1,0:T(8,128)(2,1)S(1)}, bf16[1024,128]{1,0:T(8,128)(2,1)S(1)}, u32[]{:S(2)}, u32[]{:S(2)}) collective-permute-start(bf16[1024,128]{1,0:T(8,128)(2,1)S(1)} %get-tuple-element.107), channel_id=1, source_target_pairs={{0,1},{1,0},{2,3},{3,2},{4,5},{5,4},{6,7},{7,6},{8,9},{9,8},{10,11... | collective-permute-start | bytes 786440 | tf_op jit(solution)/shard_map/ppermute | solution.py:24
  85.9 21.1 %collective-permute-start.17 = (bf16[1024,128]{1,0:T(8,128)(2,1)S(1)}, bf16[1024,128]{1,0:T(8,128)(2,1)S(1)}, u32[]{:S(2)}, u32[]{:S(2)}) collective-permute-start(bf16[1024,128]{1,0:T(8,128)(2,1)S(1)} %get-tuple-element.94), channel_id=1, source_target_pairs={{0,2},{1,3},{2,0},{3,1},{4,6},{5,7},{6,4},{7,5},{8,10},{9,11},{10,... | collective-permute-start | bytes 786440 | tf_op jit(solution)/shard_map/ppermute | solution.py:24
  87.5 19.5 %collective-permute-start.18 = (bf16[1024,128]{1,0:T(8,128)(2,1)S(1)}, bf16[1024,128]{1,0:T(8,128)(2,1)S(1)}, u32[]{:S(2)}, u32[]{:S(2)}) collective-permute-start(bf16[1024,128]{1,0:T(8,128)(2,1)S(1)} %get-tuple-element.101), channel_id=1, source_target_pairs={{0,4},{1,5},{2,6},{3,7},{4,0},{5,1},{6,2},{7,3},{8,12},{9,13},{10,... | collective-permute-start | bytes 786440 | tf_op jit(solution)/shard_map/ppermute | solution.py:24
  90.7 9.5 %collective-permute-start.16 = (bf16[192,256]{1,0:T(8,128)(2,1)S(1)}, bf16[192,256]{1,0:T(8,128)(2,1)S(1)}, u32[]{:S(2)}, u32[]{:S(2)}) collective-permute-start(bf16[192,256]{1,0:T(8,128)(2,1)S(1)} %get-tuple-element.98), channel_id=1, source_target_pairs={{0,12},{1,13},{2,14},{3,15},{4,8},{5,9},{6,10},{7,11},{8,4},{9,5},... | collective-permute-start | bytes 294920 | tf_op jit(solution)/shard_map/ppermute | solution.py:24
  100.1 5.0 %collective-permute-start.14 = (bf16[256,256]{1,0:T(8,128)(2,1)S(1)}, bf16[256,256]{1,0:T(8,128)(2,1)S(1)}, u32[]{:S(2)}, u32[]{:S(2)}) collective-permute-start(bf16[256,256]{1,0:T(8,128)(2,1)S(1)} %get-tuple-element.97), channel_id=1, source_target_pairs={{0,4},{1,5},{2,6},{3,7},{4,0},{5,1},{6,2},{7,3},{8,12},{9,13},{10,... | collective-permute-start | bytes 393224 | tf_op jit(solution)/shard_map/ppermute | solution.py:24
  105.2 11.9 %collective-permute-start.25 = (bf16[512,256]{1,0:T(8,128)(2,1)S(1)}, bf16[512,256]{1,0:T(8,128)(2,1)S(1)}, u32[]{:S(2)}, u32[]{:S(2)}) collective-permute-start(bf16[512,256]{1,0:T(8,128)(2,1)S(1)} %shard_map.116), channel_id=1, source_target_pairs={{0,20},{1,21},{2,22},{3,23},{4,16},{5,17},{6,18},{7,19},{8,28},{9,... | collective-permute-start | bytes 786440 | tf_op jit(solution)/shard_map/ppermute | solution.py:34
  106.8 4.1 %copy-start = (bf16[1,1,2,256,1024]{4,3,2,1,0:T(8,128)(2,1)S(1)}, bf16[1,1,2,256,1024]{4,3,2,1,0:T(8,128)(2,1)}, u32[]{:S(2)}) copy-start(bf16[1,1,2,256,1024]{4,3,2,1,0:T(8,128)(2,1)} %param.8) | copy-start | bytes 3145732
  106.8 10.4 %collective-permute-start.24 = (bf16[512,768]{1,0:T(8,128)(2,1)S(1)}, bf16[512,768]{1,0:T(8,128)(2,1)S(1)}, u32[]{:S(2)}, u32[]{:S(2)}) collective-permute-start(bf16[512,768]{1,0:T(8,128)(2,1)S(1)} %shard_map.115), channel_id=1, source_target_pairs={{0,16},{1,17},{2,18},{3,19},{4,20},{5,21},{6,22},{7,23},{8,24},{9,... | collective-permute-start | bytes 2359304 | tf_op jit(solution)/shard_map/ppermute | solution.py:34
  108.4 9.9 %collective-permute-start.19 = (bf16[512,256]{1,0:T(8,128)(2,1)S(1)}, bf16[512,256]{1,0:T(8,128)(2,1)S(1)}, u32[]{:S(2)}, u32[]{:S(2)}) collective-permute-start(bf16[512,256]{1,0:T(8,128)(2,1)S(1)} %get-tuple-element.102), channel_id=1, source_target_pairs={{0,16},{1,17},{2,18},{3,19},{4,20},{5,21},{6,22},{7,23},{8,24},{9,... | collective-permute-start | bytes 786440 | tf_op jit(solution)/shard_map/ppermute | solution.py:34
  108.8 9.5 %collective-permute-start.20 = (bf16[512,128]{1,0:T(8,128)(2,1)S(1)}, bf16[512,128]{1,0:T(8,128)(2,1)S(1)}, u32[]{:S(2)}, u32[]{:S(2)}) collective-permute-start(bf16[512,128]{1,0:T(8,128)(2,1)S(1)} %get-tuple-element.103), channel_id=1, source_target_pairs={{0,20},{1,21},{2,22},{3,23},{4,16},{5,17},{6,18},{7,19},{8,28},{9,... | collective-permute-start | bytes 393224 | tf_op jit(solution)/shard_map/ppermute | solution.py:34
  110.6 7.7 %collective-permute-start.21 = (bf16[512,128]{1,0:T(8,128)(2,1)S(1)}, bf16[512,128]{1,0:T(8,128)(2,1)S(1)}, u32[]{:S(2)}, u32[]{:S(2)}) collective-permute-start(bf16[512,128]{1,0:T(8,128)(2,1)S(1)} %get-tuple-element.104), channel_id=1, source_target_pairs={{0,17},{1,16},{2,19},{3,18},{4,21},{5,20},{6,23},{7,22},{8,25},{9,... | collective-permute-start | bytes 393224 | tf_op jit(solution)/shard_map/ppermute | solution.py:34

commit v12 on v11

--- a/solution.py
+++ b/solution.py
@@ -13,8 +13,8 @@
 SMEM = pl.BlockSpec(memory_space=pltpu.SMEM)
 VMEM = pl.BlockSpec(memory_space=pltpu.VMEM)
 TN = (((0,), (0,)), ((), ()))
-PARAMS = pltpu.CompilerParams(vmem_limit_bytes=12 * 2**20)
-PRODUCT_PARAMS = pltpu.CompilerParams(vmem_limit_bytes=20 * 2**20)
+PARAMS = pltpu.CompilerParams(vmem_limit_bytes=16 * 2**20)
+PRODUCT_PARAMS = pltpu.CompilerParams(vmem_limit_bytes=24 * 2**20)
 QUICK = pl.CostEstimate(flops=1000, bytes_accessed=1000, transcendentals=0)
 LONG = pl.CostEstimate(flops=4 * 10**10, bytes_accessed=1000, transcendentals=0)
 
@@ -343,10 +343,7 @@
         got1, pieces_of(1), True, True, True, LONG
     )
     parts.append(part)
-    d_first_x, d_first_y = partner(d_sent_x, 1), partner(d_sent_y, 2)
-    own_third, placed = last_parts(
-        (after(kept_x, part, c_first_x, c_first_y), kept_y), (second_x, second_y), placed, LONG
-    )
+    own_third, placed = last_parts((after(kept_x, part), kept_y), (second_x, second_y), placed)
     own_last = relay(own_third, 4)
     own_sums = (kept_x, second_x), (kept_y, second_y)
 
@@ -369,18 +366,13 @@
             refs[-1][:, start : start + ref.shape[1]] = ref[...].astype(BF16)
             start += ref.shape[1]
 
-    parts[-1] = after(parts[-1], own_third)
     (shared,) = small(collect_kernel, [((rank_part, rows_total), BF16)], *parts)
     flat = [partner(shared, mask) for mask in (1, 2, 3)]
 
     (c_sent_x, c_sent_y), c_kept = halve(
-        (after(c_kept_x, shared), c_kept_y), (c_first_x, c_first_y), None, LONG
+        (after(c_kept_x, shared), c_kept_y), (c_first_x, c_first_y)
     )
     c_second_x, c_second_y = partner(c_sent_x, 2), partner(c_sent_y, 1)
-    (d_sent_x, d_sent_y), d_kept = halve(
-        (after(d_kept_x, c_sent_x), d_kept_y), (d_first_x, d_first_y)
-    )
-    d_second_x, d_second_y = partner(d_sent_x, 2), partner(d_sent_y, 4)
 
     wanted = placed.reshape(micro_count, rank, tile_rows)
     wanted = [
@@ -418,10 +410,14 @@
         + [((rank_part, rows_total), F32)],
         *parts,
         *flat,
-        after(placed, d_sent_x, own_last),
+        placed,
         *wanted,
-        cost=LONG,
-    )
+    )
+    d_sent_x, d_sent_y, _ = lax.optimization_barrier(
+        (d_sent_x, d_sent_y, total, c_second_x, c_second_y)
+    )[:3]
+    d_first_x, d_first_y = partner(d_sent_x, 1), partner(d_sent_y, 2)
+    messages = lax.optimization_barrier((*messages, d_sent_x, own_last))[:high_size]
     near = partner(messages[0], 4)
     far = []
     for k in range(1, high_size):
@@ -461,7 +457,7 @@
         cost_estimate=QUICK,
     )(*in_hbm(scalars[0]), total, near, *far)
 
-    (c_third,) = last_parts((after(c_kept[0], lowrank), c_kept[1]), (c_second_x, c_second_y))
+    (c_third,) = last_parts((after(c_kept[0], messages[0]), c_kept[1]), (c_second_x, c_second_y))
     c_last = relay(c_third, 4)
 
     all_grads, all_pieces = [], []
@@ -477,7 +473,7 @@
         out_shape=jax.ShapeDtypeStruct(up_tile.shape, BF16),
         scratch_shapes=[pltpu.VMEM(up_tile.shape, F32)],
         compiler_params=PARAMS,
-        cost_estimate=LONG,
+        cost_estimate=QUICK,
     )(*in_hbm(*scalars), *all_grads, placed, near, *far)
 
     down = adapter_down_maps[0]
@@ -512,7 +508,7 @@
             )
             out_ref[:, rows] = (total_ref[:, rows] + adapter).astype(BF16)
 
-    def with_adapter(sums, first, with_last):
+    def with_adapter(sums, first, with_last, cost):
         counts = [kept.shape[1] for kept, _ in sums]
         shapes = [(portion, n) for n in counts] * with_last + [(portion, sum(counts))]
         outs = pl.pallas_call(
@@ -522,7 +518,7 @@
             out_shape=[jax.ShapeDtypeStruct(shape, BF16) for shape in shapes],
             scratch_shapes=[pltpu.VMEM(shapes[-1], F32)],
             compiler_params=PARAMS,
-            cost_estimate=QUICK,
+            cost_estimate=cost,
         )(*in_hbm(*scalars, down), lowrank, *[a for two in sums for a in two])
         return outs[:-1], outs[-1]
 
@@ -601,11 +597,16 @@
         cost_estimate=QUICK,
     )(*in_hbm(*scalars, forward_input[0]), lowrank)
 
-    c_sums = (c_kept[0], c_second_x), (c_kept[1], c_second_y)
-    _, kept = with_adapter(own_sums + c_sums, 0, False)
+    c_sums = (after(c_kept[0], c_third), c_second_x), (c_kept[1], c_second_y)
+    _, kept = with_adapter(own_sums + c_sums, 0, False, QUICK)
+    (d_sent_x, d_sent_y), d_kept = halve(
+        (after(d_kept_x, up_map_gradient, kept), d_kept_y), (d_first_x, d_first_y)
+    )
+    d_second_x, d_second_y = partner(d_sent_x, 2), partner(d_sent_y, 4)
+
     early = relay(kept, 0)
-    d_sums = (d_kept[0], d_second_x), (d_kept[1], d_second_y)
-    d_lasts, d_kept = with_adapter(d_sums, kept.shape[1] // size, True)
+    d_sums = (after(d_kept[0], down_map_gradient, c_last, early), d_second_x), (d_kept[1], d_second_y)
+    d_lasts, d_kept = with_adapter(d_sums, kept.shape[1] // size, True, QUICK)
     d_last = [relay(d_lasts[0], 4), relay(d_lasts[1], 1)]
     d_kept = relay(d_kept, 0)
     grad_prev = finish(early, [own_last, c_last], 0, None)

time: 120 us -> 122 us (1.017)
  waiting for transfers between devices: 50.9 us -> 40.7 us
  local copies, waits for them, and re-layouts: 3.61 us -> 8.24 us
  starting transfers between devices: 26 us -> 30.4 us
  Pallas kernels: 37.8 us -> 40.8 us
    ppermute x20, waiting for transfers between devices: 48.2 us -> 38.4 us  [partner(): return lax.ppermute(value, 'tensor', pairs)]
    unnamed x6 -> x46, local copies, waits for them, and re-layouts: 1.37 us -> 6.17 us
    ppermute x20, starting transfers between devices: 23.2 us -> 25.8 us  [partner(): return lax.ppermute(value, 'tensor', pairs)]
    pallas_call x2, Pallas kernels: 0.15 us -> 2.18 us  [last_parts(): pl.pallas_call(functools.partial(last_kernel, len(kept)), in_specs=[VMEM]...]
    ppermute x6, starting transfers between devices: 2.77 us -> 4.6 us  [relay(): return lax.ppermute(value, ('pipe', 'tensor'), pairs)]
    pallas_call x2, Pallas kernels: 0.05 us -> 1.54 us  [small(): pl.pallas_call(kernel, in_specs=[VMEM] * len(operands), out_specs=[VMEM]...]
  transfers between devices with their start and end apart: 26 -> 26, of which waited for: 13 -> 11; matrix products, arithmetic and copies ran while one was open for 0% -> 0% of each run, Pallas kernels for 31% -> 32%
where the time goes in v12:
time: 122 us; the launch traced here: 121 us
  Pallas kernels  40.8 us (33%)
  waiting for transfers between devices  40.7 us (33%)
  starting transfers between devices  30.4 us (25%)
  local copies, waits for them, and re-layouts  8.24 us (7%)
    ppermute x20, waiting for transfers between devices, partner(): return lax.ppermute(value, 'tensor', pairs)  38.4 us
    ppermute x20, starting transfers between devices, partner(): return lax.ppermute(value, 'tensor', pairs)  25.8 us
    pallas_call x4, Pallas kernels, product(): pl.pallas_call(functools.partial(product_body, low_size, tile_rows, piece...  23.7 us
    unnamed x46, local copies, waits for them, and re-layouts  6.17 us
    ppermute x6, starting transfers between devices, relay(): return lax.ppermute(value, ('pipe', 'tensor'), pairs)  4.6 us
    pallas_call x1, Pallas kernels, shards(): pl.pallas_call(down_kernel, in_specs=[SMEM] * 3 + [VMEM] * 2, out_specs=V...  3.17 us
    pallas_call x2, Pallas kernels, with_adapter(): pl.pallas_call(functools.partial(adapter_kernel, first, with_last, len(su...  3.03 us
    pallas_call x2, Pallas kernels, finish(): pl.pallas_call(functools.partial(finish_kernel, first, len(got)), in_spec...  2.95 us
  transfers between devices with their start and end apart: 26, of which 11 were waited for; matrix products, arithmetic and copies ran while one was open for 0% of the time, Pallas kernels for 32%

profile of v12, /device:TPU:0, one launch (start us, length us, event | category | flops | bytes accessed | tf_op | source)
XLA Modules:
  0.0 121.1 jit_solution(11682926244470887537)
XLA Ops:
  0.6 2.1 %slice_bitcast_fusion = (bf16[256,1024]{1,0:T(8,128)(2,1)}, bf16[256,1024]{1,0:T(8,128)(2,1)S(1)}) fusion(bf16[1,1,2,256,1024]{4,3,2,1,0:T(8,128)(2,1)} %param.8), kind=kLoop, calls=%fused_computation | loop fusion | bytes 2097152 | tf_op jit(solution)/shard_map/squeeze | solution.py:330
  2.7 4.0 %collective-permute-start = (bf16[256,1024]{1,0:T(8,128)(2,1)S(1)}, bf16[256,1024]{1,0:T(8,128)(2,1)S(1)}, u32[]{:S(2)}, u32[]{:S(2)}) collective-permute-start(bf16[256,1024]{1,0:T(8,128)(2,1)S(1)} %get-tuple-element.118), channel_id=1, source_target_pairs={{0,8},{1,9},{2,10},{3,11},{4,12},{5,13},{6,14},{7,15},{8,0},{9,1},... | collective-permute-start | bytes 1572872 | tf_op jit(solution)/shard_map/ppermute | solution.py:24
  6.7 5.7 %shard_map.103 = (bf16[2176,256]{1,0:T(8,128)(2,1)S(1)}, bf16[2048,256]{1,0:T(8,128)(2,1)S(1)}, bf16[128,256]{1,0:T(8,128)(2,1)S(1)}) custom-call(s32[1]{0:T(128)} %bitcast.refs_0_.high_ref.pos_ref, s32[2,4]{1,0:T(2,128)} %bitcast.42, s32[2]{0:T(128)} %bitcast.50, bf16[2,256,1024]{2,1,0:T(8,128)(2,1)} %bitcast.20, bf16[8,512,1024]{2,1,0:T(8,128)(2,1)} %bitcast.29, ...), custom_call_target="tpu_custom_call" | custom-call | flops 1000 | bytes 1000 | tf_op jit(solution)/shard_map/pallas_call | solution.py:141
  12.5 1.6 %collective-permute-start.5 = (bf16[2176,256]{1,0:T(8,128)(2,1)S(1)}, bf16[2176,256]{1,0:T(8,128)(2,1)S(1)}, u32[]{:S(2)}, u32[]{:S(2)}) collective-permute-start(bf16[2176,256]{1,0:T(8,128)(2,1)S(1)} %get-tuple-element.64), channel_id=1, source_target_pairs={{0,1},{1,0},{2,3},{3,2},{4,5},{5,4},{6,7},{7,6},{8,9},{9,8},{10,11... | collective-permute-start | bytes 3342344 | tf_op jit(solution)/shard_map/ppermute | solution.py:24
  14.0 1.5 %collective-permute-start.6 = (bf16[2048,256]{1,0:T(8,128)(2,1)S(1)}, bf16[2048,256]{1,0:T(8,128)(2,1)S(1)}, u32[]{:S(2)}, u32[]{:S(2)}) collective-permute-start(bf16[2048,256]{1,0:T(8,128)(2,1)S(1)} %get-tuple-element.65), channel_id=1, source_target_pairs={{0,2},{1,3},{2,0},{3,1},{4,6},{5,7},{6,4},{7,5},{8,10},{9,11},{10,... | collective-permute-start | bytes 3145736 | tf_op jit(solution)/shard_map/ppermute | solution.py:24
  15.5 5.8 %shard_map.104 = (f32[2048,256]{1,0:T(8,128)S(1)}, f32[2048,256]{1,0:T(8,128)S(1)}, f32[32,512]{1,0:T(8,128)S(1)}) custom-call(s32[1]{0:T(128)} %bitcast.refs_0_.high_ref.pos_ref, s32[2,4]{1,0:T(2,128)} %bitcast.43, s32[2]{0:T(128)} %bitcast.51, bf16[2,256,1024]{2,1,0:T(8,128)(2,1)} %bitcast.21, bf16[8,512,1024]{2,1,0:T(8,128)(2,1)} %bitcast.30, ...), custom_call_target="tpu_custom_call" | custom-call | flops 1000 | bytes 1000 | tf_op jit(solution)/shard_map/pallas_call | solution.py:141
  21.4 8.5 %collective-permute-done = bf16[256,1024]{1,0:T(8,128)(2,1)S(1)} collective-permute-done((bf16[256,1024]{1,0:T(8,128)(2,1)S(1)}, bf16[256,1024]{1,0:T(8,128)(2,1)S(1)}, u32[]{:S(2)}, u32[]{:S(2)}) %collective-permute-start) | collective-permute-done | bytes 524320 | tf_op jit(solution)/shard_map/ppermute | solution.py:24
  29.9 6.1 %shard_map.105 = (bf16[2048,128]{1,0:T(8,128)(2,1)S(1)}, bf16[2048,128]{1,0:T(8,128)(2,1)S(1)}, f32[2048,128]{1,0:T(8,128)S(1)}, f32[2048,128]{1,0:T(8,128)S(1)}, f32[32,256]{1,0:T(8,128)S(1)}) custom-call(s32[1]{0:T(128)} %bitcast.refs_0_.high_ref.pos_ref, s32[2,4]{1,0:T(2,128)} %bitcast.44, s32[2]{0:T(128)} %bitcast.52, ...), custom_call_target="tpu_custom_call" | custom-call | flops 40000000000 | bytes 1000 | tf_op jit(solution)/shard_map/pallas_call | solution.py:141
  36.0 2.4 %collective-permute-done.6.refs_3_ = bf16[2048,256]{1,0:T(8,128)(2,1)S(1)} collective-permute-done((bf16[2048,256]{1,0:T(8,128)(2,1)S(1)}, bf16[2048,256]{1,0:T(8,128)(2,1)S(1)}, u32[]{:S(2)}, u32[]{:S(2)}) %collective-permute-start.6) | collective-permute-done | bytes 1048608 | tf_op jit(solution)/shard_map/ppermute | solution.py:24
  38.4 0.2 collective-permute-done.5.refs_2_
  38.5 0.3 shard_map.108
  38.9 1.6 %collective-permute-start.7 = (bf16[1152,256]{1,0:T(8,128)(2,1)S(1)}, bf16[1152,256]{1,0:T(8,128)(2,1)S(1)}, u32[]{:S(2)}, u32[]{:S(2)}) collective-permute-start(bf16[1152,256]{1,0:T(8,128)(2,1)S(1)} %get-tuple-element.79), channel_id=1, source_target_pairs={{0,2},{1,3},{2,0},{3,1},{4,6},{5,7},{6,4},{7,5},{8,10},{9,11},{10,... | collective-permute-start | bytes 1769480 | tf_op jit(solution)/shard_map/ppermute | solution.py:24
  40.5 1.5 %collective-permute-start.8 = (bf16[1024,256]{1,0:T(8,128)(2,1)S(1)}, bf16[1024,256]{1,0:T(8,128)(2,1)S(1)}, u32[]{:S(2)}, u32[]{:S(2)}) collective-permute-start(bf16[1024,256]{1,0:T(8,128)(2,1)S(1)} %get-tuple-element.80), channel_id=1, source_target_pairs={{0,1},{1,0},{2,3},{3,2},{4,5},{5,4},{6,7},{7,6},{8,9},{9,8},{10,11... | collective-permute-start | bytes 1572872 | tf_op jit(solution)/shard_map/ppermute | solution.py:24
  42.0 0.5 collective-permute-start.10
  42.5 0.5 collective-permute-start.9
  43.0 12.3 %collective-permute-done.1 = bf16[256,1024]{1,0:T(8,128)(2,1)S(1)} collective-permute-done((bf16[256,1024]{1,0:T(8,128)(2,1)}, bf16[256,1024]{1,0:T(8,128)(2,1)S(1)}, u32[]{:S(2)}, u32[]{:S(2)}) %collective-permute-start.1) | collective-permute-done | bytes 524320 | tf_op jit(solution)/shard_map/ppermute | solution.py:24
  55.3 6.1 %shard_map.106 = (bf16[2048,128]{1,0:T(8,128)(2,1)S(1)}, bf16[2048,128]{1,0:T(8,128)(2,1)S(1)}, f32[2048,128]{1,0:T(8,128)S(1)}, f32[2048,128]{1,0:T(8,128)S(1)}, f32[32,256]{1,0:T(8,128)S(1)}) custom-call(s32[1]{0:T(128)} %bitcast.refs_0_.high_ref.pos_ref, s32[2,4]{1,0:T(2,128)} %bitcast.45, s32[2]{0:T(128)} %bitcast.53, ...), custom_call_target="tpu_custom_call" | custom-call | flops 40000000000 | bytes 1000 | tf_op jit(solution)/shard_map/pallas_call | solution.py:141
  61.4 0.0 copy-start.7
  61.5 0.0 copy-start.22
  61.5 1.1 shard_map.109
  62.6 0.7 shard_map.107
  63.3 0.8 collective-permute-done.10.refs_3_
  64.1 0.9 shard_map.111
  65.1 0.8 copy-done.1
  65.8 0.8 copy-done.4
  66.6 1.5 %collective-permute-start.11 = (bf16[1024,128]{1,0:T(8,128)(2,1)}, bf16[1024,128]{1,0:T(8,128)(2,1)S(1)}, u32[]{:S(2)}, u32[]{:S(2)}) collective-permute-start(bf16[1024,128]{1,0:T(8,128)(2,1)} %get-tuple-element.95), channel_id=1, source_target_pairs={{0,2},{1,3},{2,0},{3,1},{4,6},{5,7},{6,4},{7,5},{8,10},{9,11},{10,... | collective-permute-start | bytes 786440 | tf_op jit(solution)/shard_map/ppermute | solution.py:24
  68.1 1.5 %collective-permute-start.12 = (bf16[1024,128]{1,0:T(8,128)(2,1)}, bf16[1024,128]{1,0:T(8,128)(2,1)}, u32[]{:S(2)}, u32[]{:S(2)}) collective-permute-start(bf16[1024,128]{1,0:T(8,128)(2,1)} %get-tuple-element.96), channel_id=1, source_target_pairs={{0,1},{1,0},{2,3},{3,2},{4,5},{5,4},{6,7},{7,6},{8,9},{9,8},{10,11... | collective-permute-start | bytes 786440 | tf_op jit(solution)/shard_map/ppermute | solution.py:24
  69.7 0.5 collective-permute-start.2
  70.2 0.5 collective-permute-start.3
  70.7 5.3 %collective-permute-done.2.refs_3_ = bf16[32,1024]{1,0:T(8,128)(2,1)} collective-permute-done((bf16[32,1024]{1,0:T(8,128)(2,1)}, bf16[32,1024]{1,0:T(8,128)(2,1)}, u32[]{:S(2)}, u32[]{:S(2)}) %collective-permute-start.2) | collective-permute-done | bytes 65568 | tf_op jit(solution)/shard_map/ppermute | solution.py:24
  76.0 1.0 collective-permute-start.4
  77.0 4.4 %collective-permute-done.4.refs_5_ = bf16[32,1024]{1,0:T(8,128)(2,1)S(1)} collective-permute-done((bf16[32,1024]{1,0:T(8,128)(2,1)}, bf16[32,1024]{1,0:T(8,128)(2,1)S(1)}, u32[]{:S(2)}, u32[]{:S(2)}) %collective-permute-start.4) | collective-permute-done | bytes 65568 | tf_op jit(solution)/shard_map/ppermute | solution.py:24
  81.4 0.8 copy-done.16
  82.2 0.8 copy-done.18
  83.0 0.8 copy-done.20
  83.8 0.9 shard_map.110
  84.7 3.0 %collective-permute-start.14 = (bf16[256,256]{1,0:T(8,128)(2,1)S(1)}, bf16[256,256]{1,0:T(8,128)(2,1)S(1)}, u32[]{:S(2)}, u32[]{:S(2)}) collective-permute-start(bf16[256,256]{1,0:T(8,128)(2,1)S(1)} %get-tuple-element.99), channel_id=1, source_target_pairs={{0,4},{1,5},{2,6},{3,7},{4,0},{5,1},{6,2},{7,3},{8,12},{9,13},{10,... | collective-permute-start | bytes 393224 | tf_op jit(solution)/shard_map/ppermute | solution.py:24
  87.7 0.5 collective-permute-start.15
  88.2 1.9 %collective-permute-start.16 = (bf16[192,256]{1,0:T(8,128)(2,1)S(1)}, bf16[192,256]{1,0:T(8,128)(2,1)S(1)}, u32[]{:S(2)}, u32[]{:S(2)}) collective-permute-start(bf16[192,256]{1,0:T(8,128)(2,1)S(1)} %get-tuple-element.100), channel_id=1, source_target_pairs={{0,12},{1,13},{2,14},{3,15},{4,8},{5,9},{6,10},{7,11},{8,4},{9,5},... | collective-permute-start | bytes 294920 | tf_op jit(solution)/shard_map/ppermute | solution.py:24
  90.1 1.5 %collective-permute-start.17 = (bf16[2048,128]{1,0:T(8,128)(2,1)}, bf16[2048,128]{1,0:T(8,128)(2,1)S(1)}, u32[]{:S(2)}, u32[]{:S(2)}) collective-permute-start(bf16[2048,128]{1,0:T(8,128)(2,1)} %copy-done.22), channel_id=1, source_target_pairs={{0,1},{1,0},{2,3},{3,2},{4,5},{5,4},{6,7},{7,6},{8,9},{9,8},{10,11... | collective-permute-start | bytes 1572872 | tf_op jit(solution)/shard_map/ppermute | solution.py:24
  91.6 0.5 collective-permute-start.18
  92.1 1.0 copy-done.2
  93.2 1.0 copy-done.5
  94.2 1.1 shard_map.114
  95.4 0.1 copy-done.6
  95.5 1.7 %shard_map.115 = bf16[512,768]{1,0:T(8,128)(2,1)S(1)} custom-call(s32[1]{0:T(128)} %bitcast.refs_0_.high_ref.pos_ref, s32[2,4]{1,0:T(2,128)} %bitcast.46, s32[2]{0:T(128)} %bitcast.54, bf16[8,64,512]{2,1,0:T(8,128)(2,1)} %bitcast.34, bf16[64,1024]{1,0:T(8,128)(2,1)S(1)} %shard_map.112.refs_4_.lowrank_ref, f32[1024,256]{1,0:T(8,128)S(1)} %get-tuple-element.77.refs_0_.refs_5_, ...), custom_call_target="tpu_custom_call" | custom-call | flops 1000 | bytes 1000 | tf_op jit(solution)/shard_map/pallas_call | solution.py:514
  97.2 0.0 copy-start.8
  97.2 0.1 collective-permute-start.20
  97.3 1.7 %collective-permute-start.19 = (bf16[512,256]{1,0:T(8,128)(2,1)S(1)}, bf16[512,256]{1,0:T(8,128)(2,1)S(1)}, u32[]{:S(2)}, u32[]{:S(2)}) collective-permute-start(bf16[512,256]{1,0:T(8,128)(2,1)S(1)} %shard_map.114), channel_id=1, source_target_pairs={{0,20},{1,21},{2,22},{3,23},{4,16},{5,17},{6,18},{7,19},{8,28},{9,... | collective-permute-start | bytes 786440 | tf_op jit(solution)/shard_map/ppermute | solution.py:34
  99.0 2.8 %shard_map.113 = bf16[8,32,1024]{2,1,0:T(8,128)(2,1)} custom-call(s32[1]{0:T(128)} %bitcast.refs_0_.high_ref.pos_ref, s32[2,4]{1,0:T(2,128)} %bitcast.47, s32[2]{0:T(128)} %bitcast.55, bf16[2,256,1024]{2,1,0:T(8,128)(2,1)S(1)} %bitcast.22, bf16[1,256,1024]{2,1,0:T(8,128)(2,1)S(1)} %bitcast.24, bf16[1,256,1024]{2,1,0:T(8,128)(2,1)S(1)} %bitcast.26, ...), custom_call_target="tpu_custom_call" | custom-call | flops 1000 | bytes 1000 | tf_op jit(solution)/shard_map/pallas_call | solution.py:467
  101.7 0.2 shard_map.116
  101.9 1.1 collective-permute-start.21
  103.0 1.0 collective-permute-start.22
  104.0 3.2 %shard_map.117 = bf16[8,64,512]{2,1,0:T(8,128)(2,1)} custom-call(s32[1]{0:T(128)} %bitcast.refs_0_.high_ref.pos_ref, s32[2,4]{1,0:T(2,128)} %bitcast.48, s32[2]{0:T(128)} %bitcast.56, bf16[2,512,512]{2,1,0:T(8,128)(2,1)} %bitcast.36, bf16[64,1024]{1,0:T(8,128)(2,1)S(1)} %shard_map.112.refs_4_.lowrank_ref), custom_call_target="tpu_custom_call" | custom-call | flops 1000 | bytes 1000 | tf_op jit(solution)/shard_map/pallas_call | solution.py:590
  107.2 2.9 %collective-permute-done.21.refs_6_ = bf16[1024,128]{1,0:T(8,128)(2,1)S(1)} collective-permute-done((bf16[1024,128]{1,0:T(8,128)(2,1)S(1)}, bf16[1024,128]{1,0:T(8,128)(2,1)S(1)}, u32[]{:S(2)}, u32[]{:S(2)}) %collective-permute-start.21) | collective-permute-done | bytes 262176 | tf_op jit(solution)/shard_map/ppermute | solution.py:24
  110.1 1.5 %collective-permute-done.22.refs_8_ = bf16[1024,128]{1,0:T(8,128)(2,1)S(1)} collective-permute-done((bf16[1024,128]{1,0:T(8,128)(2,1)S(1)}, bf16[1024,128]{1,0:T(8,128)(2,1)S(1)}, u32[]{:S(2)}, u32[]{:S(2)}) %collective-permute-start.22) | collective-permute-done | bytes 262176 | tf_op jit(solution)/shard_map/ppermute | solution.py:24
  111.6 1.3 %shard_map.118 = (bf16[512,128]{1,0:T(8,128)(2,1)S(1)}, bf16[512,128]{1,0:T(8,128)(2,1)S(1)}, bf16[512,256]{1,0:T(8,128)(2,1)S(1)}) custom-call(s32[1]{0:T(128)} %bitcast.refs_0_.high_ref.pos_ref, s32[2,4]{1,0:T(2,128)} %bitcast.49, s32[2]{0:T(128)} %bitcast.57, bf16[8,64,512]{2,1,0:T(8,128)(2,1)} %bitcast.35, ...), custom_call_target="tpu_custom_call" | custom-call | flops 1000 | bytes 1000 | tf_op jit(solution)/shard_map/pallas_call | solution.py:514
  112.9 0.1 collective-permute-start.23
  113.0 1.7 %collective-permute-start.24 = (bf16[512,128]{1,0:T(8,128)(2,1)S(1)}, bf16[512,128]{1,0:T(8,128)(2,1)S(1)}, u32[]{:S(2)}, u32[]{:S(2)}) collective-permute-start(bf16[512,128]{1,0:T(8,128)(2,1)S(1)} %get-tuple-element.115), channel_id=1, source_target_pairs={{0,20},{1,21},{2,22},{3,23},{4,16},{5,17},{6,18},{7,19},{8,28},{9,... | collective-permute-start | bytes 393224 | tf_op jit(solution)/shard_map/ppermute | solution.py:34
  114.7 1.2 collective-permute-start.25
  115.8 2.1 %shard_map.119.refs_4_ = bf16[2,512,512]{2,1,0:T(8,128)(2,1)} custom-call(s32[1]{0:T(128)} %bitcast.refs_0_.high_ref.pos_ref, bf16[512,768]{1,0:T(8,128)(2,1)S(1)} %collective-permute-done.20.refs_1_, bf16[512,512]{1,0:T(8,128)(2,1)} %collective-permute-done.13.refs_2_, bf16[512,256]{1,0:T(8,128)(2,1)S(1)} %collective-permute-done.19.refs_3_), custom_call_target="tpu_custom_call" | custom-call | flops 1000 | bytes 1000 | tf_op jit(solution)/shard_map/pallas_call | solution.py:557
  117.9 0.4 collective-permute-done.24.refs_2_
  118.3 1.9 %collective-permute-done.25.refs_3_ = bf16[512,128]{1,0:T(8,128)(2,1)S(1)} collective-permute-done((bf16[512,128]{1,0:T(8,128)(2,1)S(1)}, bf16[512,128]{1,0:T(8,128)(2,1)S(1)}, u32[]{:S(2)}, u32[]{:S(2)}) %collective-permute-start.25) | collective-permute-done | bytes 131104 | tf_op jit(solution)/shard_map/ppermute | solution.py:34
  120.2 0.8 shard_map.120
  (54 shorter events, 0.2 us)
Async XLA Ops:
  2.7 27.2 %collective-permute-start = (bf16[256,1024]{1,0:T(8,128)(2,1)S(1)}, bf16[256,1024]{1,0:T(8,128)(2,1)S(1)}, u32[]{:S(2)}, u32[]{:S(2)}) collective-permute-start(bf16[256,1024]{1,0:T(8,128)(2,1)S(1)} %get-tuple-element.118), channel_id=1, source_target_pairs={{0,8},{1,9},{2,10},{3,11},{4,12},{5,13},{6,14},{7,15},{8,0},{9,1},... | collective-permute-start | bytes 1572872 | tf_op jit(solution)/shard_map/ppermute | solution.py:24
  12.5 26.1 %collective-permute-start.5 = (bf16[2176,256]{1,0:T(8,128)(2,1)S(1)}, bf16[2176,256]{1,0:T(8,128)(2,1)S(1)}, u32[]{:S(2)}, u32[]{:S(2)}) collective-permute-start(bf16[2176,256]{1,0:T(8,128)(2,1)S(1)} %get-tuple-element.64), channel_id=1, source_target_pairs={{0,1},{1,0},{2,3},{3,2},{4,5},{5,4},{6,7},{7,6},{8,9},{9,8},{10,11... | collective-permute-start | bytes 3342344 | tf_op jit(solution)/shard_map/ppermute | solution.py:24
  14.0 24.3 %collective-permute-start.6 = (bf16[2048,256]{1,0:T(8,128)(2,1)S(1)}, bf16[2048,256]{1,0:T(8,128)(2,1)S(1)}, u32[]{:S(2)}, u32[]{:S(2)}) collective-permute-start(bf16[2048,256]{1,0:T(8,128)(2,1)S(1)} %get-tuple-element.65), channel_id=1, source_target_pairs={{0,2},{1,3},{2,0},{3,1},{4,6},{5,7},{6,4},{7,5},{8,10},{9,11},{10,... | collective-permute-start | bytes 3145736 | tf_op jit(solution)/shard_map/ppermute | solution.py:24
  21.4 41.2 %copy-start.15 = (f32[32,512]{1,0:T(8,128)}, f32[32,512]{1,0:T(8,128)S(1)}, u32[]{:S(2)}) copy-start(f32[32,512]{1,0:T(8,128)S(1)} %get-tuple-element.67.refs_0_) | copy-start | bytes 196612
  29.9 6.1 %copy-start.11 = (bf16[256,1024]{1,0:T(8,128)(2,1)}, bf16[256,1024]{1,0:T(8,128)(2,1)S(1)}, u32[]{:S(2)}) copy-start(bf16[256,1024]{1,0:T(8,128)(2,1)S(1)} %collective-permute-done) | copy-start | bytes 1572868
  29.9 25.5 %collective-permute-start.1 = (bf16[256,1024]{1,0:T(8,128)(2,1)}, bf16[256,1024]{1,0:T(8,128)(2,1)S(1)}, u32[]{:S(2)}, u32[]{:S(2)}) collective-permute-start(bf16[256,1024]{1,0:T(8,128)(2,1)} %get-tuple-element.70), channel_id=1, source_target_pairs={{0,8},{1,9},{2,10},{3,11},{4,12},{5,13},{6,14},{7,15},{8,0},{9,1},... | collective-permute-start | bytes 1572872 | tf_op jit(solution)/shard_map/ppermute | solution.py:24
  36.0 26.6 %copy-start.17 = (f32[32,256]{1,0:T(8,128)}, f32[32,256]{1,0:T(8,128)S(1)}, u32[]{:S(2)}) copy-start(f32[32,256]{1,0:T(8,128)S(1)} %get-tuple-element.69.refs_1_) | copy-start | bytes 98308
  38.9 22.6 %collective-permute-start.7 = (bf16[1152,256]{1,0:T(8,128)(2,1)S(1)}, bf16[1152,256]{1,0:T(8,128)(2,1)S(1)}, u32[]{:S(2)}, u32[]{:S(2)}) collective-permute-start(bf16[1152,256]{1,0:T(8,128)(2,1)S(1)} %get-tuple-element.79), channel_id=1, source_target_pairs={{0,2},{1,3},{2,0},{3,1},{4,6},{5,7},{6,4},{7,5},{8,10},{9,11},{10,... | collective-permute-start | bytes 1769480 | tf_op jit(solution)/shard_map/ppermute | solution.py:24
  40.5 21.0 %collective-permute-start.8 = (bf16[1024,256]{1,0:T(8,128)(2,1)S(1)}, bf16[1024,256]{1,0:T(8,128)(2,1)S(1)}, u32[]{:S(2)}, u32[]{:S(2)}) collective-permute-start(bf16[1024,256]{1,0:T(8,128)(2,1)S(1)} %get-tuple-element.80), channel_id=1, source_target_pairs={{0,1},{1,0},{2,3},{3,2},{4,5},{5,4},{6,7},{7,6},{8,9},{9,8},{10,11... | collective-permute-start | bytes 1572872 | tf_op jit(solution)/shard_map/ppermute | solution.py:24
  42.0 22.1 %collective-permute-start.10 = (bf16[2048,128]{1,0:T(8,128)(2,1)S(1)}, bf16[2048,128]{1,0:T(8,128)(2,1)S(1)}, u32[]{:S(2)}, u32[]{:S(2)}) collective-permute-start(bf16[2048,128]{1,0:T(8,128)(2,1)S(1)} %get-tuple-element.94), channel_id=1, source_target_pairs={{0,2},{1,3},{2,0},{3,1},{4,6},{5,7},{6,4},{7,5},{8,10},{9,11},{10,... | collective-permute-start | bytes 1572872 | tf_op jit(solution)/shard_map/ppermute | solution.py:24
  42.5 21.6 %collective-permute-start.9 = (bf16[2048,128]{1,0:T(8,128)(2,1)S(1)}, bf16[2048,128]{1,0:T(8,128)(2,1)S(1)}, u32[]{:S(2)}, u32[]{:S(2)}) collective-permute-start(bf16[2048,128]{1,0:T(8,128)(2,1)S(1)} %get-tuple-element.92), channel_id=1, source_target_pairs={{0,1},{1,0},{2,3},{3,2},{4,5},{5,4},{6,7},{7,6},{8,9},{9,8},{10,11... | collective-permute-start | bytes 1572872 | tf_op jit(solution)/shard_map/ppermute | solution.py:24
  55.3 6.1 %copy-start.13 = (bf16[256,1024]{1,0:T(8,128)(2,1)}, bf16[256,1024]{1,0:T(8,128)(2,1)S(1)}, u32[]{:S(2)}) copy-start(bf16[256,1024]{1,0:T(8,128)(2,1)S(1)} %collective-permute-done.1) | copy-start | bytes 1572868
  61.4 3.6 %copy-start.7 = (f32[2048,128]{1,0:T(8,128)}, f32[2048,128]{1,0:T(8,128)S(1)}, u32[]{:S(2)}) copy-start(f32[2048,128]{1,0:T(8,128)S(1)} %get-tuple-element.106.refs_0_) | copy-start | bytes 3145732
  61.4 3.6 %copy-start.9 = (f32[2048,128]{1,0:T(8,128)}, f32[2048,128]{1,0:T(8,128)S(1)}, u32[]{:S(2)}) copy-start(f32[2048,128]{1,0:T(8,128)S(1)} %get-tuple-element.107.refs_1_) | copy-start | bytes 3145732
  61.4 3.6 %copy-start.19 = (f32[32,256]{1,0:T(8,128)}, f32[32,256]{1,0:T(8,128)S(1)}, u32[]{:S(2)}) copy-start(f32[32,256]{1,0:T(8,128)S(1)} %get-tuple-element.71.refs_2_) | copy-start | bytes 98308
  61.4 3.6 %copy-start.21 = (bf16[2048,128]{1,0:T(8,128)(2,1)}, bf16[2048,128]{1,0:T(8,128)(2,1)S(1)}, u32[]{:S(2)}) copy-start(bf16[2048,128]{1,0:T(8,128)(2,1)S(1)} %get-tuple-element.108) | copy-start | bytes 1572868
  61.5 3.6 %copy-start.22 = (bf16[2048,128]{1,0:T(8,128)(2,1)}, bf16[2048,128]{1,0:T(8,128)(2,1)S(1)}, u32[]{:S(2)}) copy-start(bf16[2048,128]{1,0:T(8,128)(2,1)S(1)} %get-tuple-element.97) | copy-start | bytes 1572868
  62.6 22.1 %collective-permute-start.13 = (bf16[512,512]{1,0:T(8,128)(2,1)}, bf16[512,512]{1,0:T(8,128)(2,1)}, u32[]{:S(2)}, u32[]{:S(2)}) collective-permute-start(bf16[512,512]{1,0:T(8,128)(2,1)} %get-tuple-element.98), channel_id=1, source_target_pairs={{0,20},{1,21},{2,22},{3,23},{4,16},{5,17},{6,18},{7,19},{8,28},{9,... | collective-permute-start | bytes 1572872 | tf_op jit(solution)/shard_map/ppermute | solution.py:34
  65.0 0.8 copy-start.1
  65.8 0.8 copy-start.4
  66.6 18.0 %collective-permute-start.11 = (bf16[1024,128]{1,0:T(8,128)(2,1)}, bf16[1024,128]{1,0:T(8,128)(2,1)S(1)}, u32[]{:S(2)}, u32[]{:S(2)}) collective-permute-start(bf16[1024,128]{1,0:T(8,128)(2,1)} %get-tuple-element.95), channel_id=1, source_target_pairs={{0,2},{1,3},{2,0},{3,1},{4,6},{5,7},{6,4},{7,5},{8,10},{9,11},{10,... | collective-permute-start | bytes 786440 | tf_op jit(solution)/shard_map/ppermute | solution.py:24
  68.1 16.5 %collective-permute-start.12 = (bf16[1024,128]{1,0:T(8,128)(2,1)}, bf16[1024,128]{1,0:T(8,128)(2,1)}, u32[]{:S(2)}, u32[]{:S(2)}) collective-permute-start(bf16[1024,128]{1,0:T(8,128)(2,1)} %get-tuple-element.96), channel_id=1, source_target_pairs={{0,1},{1,0},{2,3},{3,2},{4,5},{5,4},{6,7},{7,6},{8,9},{9,8},{10,11... | collective-permute-start | bytes 786440 | tf_op jit(solution)/shard_map/ppermute | solution.py:24
  69.7 6.4 %collective-permute-start.2 = (bf16[32,1024]{1,0:T(8,128)(2,1)}, bf16[32,1024]{1,0:T(8,128)(2,1)}, u32[]{:S(2)}, u32[]{:S(2)}) collective-permute-start(bf16[32,1024]{1,0:T(8,128)(2,1)} %shard_map.107), channel_id=1, source_target_pairs={{0,1},{1,0},{2,3},{3,2},{4,5},{5,4},{6,7},{7,6},{8,9},{9,8},{10,11... | collective-permute-start | bytes 196616 | tf_op jit(solution)/shard_map/ppermute | solution.py:24
  70.2 6.8 %collective-permute-start.3 = (bf16[32,1024]{1,0:T(8,128)(2,1)}, bf16[32,1024]{1,0:T(8,128)(2,1)S(1)}, u32[]{:S(2)}, u32[]{:S(2)}) collective-permute-start(bf16[32,1024]{1,0:T(8,128)(2,1)} %shard_map.107), channel_id=1, source_target_pairs={{0,2},{1,3},{2,0},{3,1},{4,6},{5,7},{6,4},{7,5},{8,10},{9,11},{10,... | collective-permute-start | bytes 196616 | tf_op jit(solution)/shard_map/ppermute | solution.py:24
  76.0 5.4 %collective-permute-start.4 = (bf16[32,1024]{1,0:T(8,128)(2,1)}, bf16[32,1024]{1,0:T(8,128)(2,1)S(1)}, u32[]{:S(2)}, u32[]{:S(2)}) collective-permute-start(bf16[32,1024]{1,0:T(8,128)(2,1)} %shard_map.107), channel_id=1, source_target_pairs={{0,3},{1,2},{2,1},{3,0},{4,7},{5,6},{6,5},{7,4},{8,11},{9,10},{10,... | collective-permute-start | bytes 196616 | tf_op jit(solution)/shard_map/ppermute | solution.py:24
  81.4 0.8 copy-start.16
  82.2 0.8 copy-start.18
  83.0 0.8 copy-start.20
  84.7 10.7 %collective-permute-start.14 = (bf16[256,256]{1,0:T(8,128)(2,1)S(1)}, bf16[256,256]{1,0:T(8,128)(2,1)S(1)}, u32[]{:S(2)}, u32[]{:S(2)}) collective-permute-start(bf16[256,256]{1,0:T(8,128)(2,1)S(1)} %get-tuple-element.99), channel_id=1, source_target_pairs={{0,4},{1,5},{2,6},{3,7},{4,0},{5,1},{6,2},{7,3},{8,12},{9,13},{10,... | collective-permute-start | bytes 393224 | tf_op jit(solution)/shard_map/ppermute | solution.py:24
  87.7 7.6 %collective-permute-start.15 = (bf16[192,256]{1,0:T(8,128)(2,1)S(1)}, bf16[192,256]{1,0:T(8,128)(2,1)S(1)}, u32[]{:S(2)}, u32[]{:S(2)}) collective-permute-start(bf16[192,256]{1,0:T(8,128)(2,1)S(1)} %get-tuple-element.100), channel_id=1, source_target_pairs={{0,8},{1,9},{2,10},{3,11},{4,12},{5,13},{6,14},{7,15},{8,0},{9,1},... | collective-permute-start | bytes 294920 | tf_op jit(solution)/shard_map/ppermute | solution.py:24
  88.2 7.1 %collective-permute-start.16 = (bf16[192,256]{1,0:T(8,128)(2,1)S(1)}, bf16[192,256]{1,0:T(8,128)(2,1)S(1)}, u32[]{:S(2)}, u32[]{:S(2)}) collective-permute-start(bf16[192,256]{1,0:T(8,128)(2,1)S(1)} %get-tuple-element.100), channel_id=1, source_target_pairs={{0,12},{1,13},{2,14},{3,15},{4,8},{5,9},{6,10},{7,11},{8,4},{9,5},... | collective-permute-start | bytes 294920 | tf_op jit(solution)/shard_map/ppermute | solution.py:24
  90.1 11.6 %collective-permute-start.17 = (bf16[2048,128]{1,0:T(8,128)(2,1)}, bf16[2048,128]{1,0:T(8,128)(2,1)S(1)}, u32[]{:S(2)}, u32[]{:S(2)}) collective-permute-start(bf16[2048,128]{1,0:T(8,128)(2,1)} %copy-done.22), channel_id=1, source_target_pairs={{0,1},{1,0},{2,3},{3,2},{4,5},{5,4},{6,7},{7,6},{8,9},{9,8},{10,11... | collective-permute-start | bytes 1572872 | tf_op jit(solution)/shard_map/ppermute | solution.py:24
  91.6 10.1 %collective-permute-start.18 = (bf16[2048,128]{1,0:T(8,128)(2,1)}, bf16[2048,128]{1,0:T(8,128)(2,1)S(1)}, u32[]{:S(2)}, u32[]{:S(2)}) collective-permute-start(bf16[2048,128]{1,0:T(8,128)(2,1)} %copy-done.21), channel_id=1, source_target_pairs={{0,2},{1,3},{2,0},{3,1},{4,6},{5,7},{6,4},{7,5},{8,10},{9,11},{10,... | collective-permute-start | bytes 1572872 | tf_op jit(solution)/shard_map/ppermute | solution.py:24
  92.1 1.0 copy-start.2
  93.2 1.0 copy-start.5
  94.2 1.2 copy-start.3
  94.2 1.3 %copy-start.6 = (f32[1024,128]{1,0:T(8,128)S(1)}, f32[1024,128]{1,0:T(8,128)}, u32[]{:S(2)}) copy-start(f32[1024,128]{1,0:T(8,128)} %copy-done.4) | copy-start | bytes 1572868
  95.5 3.5 %copy-start = (bf16[1,1,2,256,1024]{4,3,2,1,0:T(8,128)(2,1)S(1)}, bf16[1,1,2,256,1024]{4,3,2,1,0:T(8,128)(2,1)}, u32[]{:S(2)}) copy-start(bf16[1,1,2,256,1024]{4,3,2,1,0:T(8,128)(2,1)} %param.8) | copy-start | bytes 3145732
  95.5 3.5 %copy-start.12 = (bf16[256,1024]{1,0:T(8,128)(2,1)S(1)}, bf16[256,1024]{1,0:T(8,128)(2,1)}, u32[]{:S(2)}) copy-start(bf16[256,1024]{1,0:T(8,128)(2,1)} %copy-done.11) | copy-start | bytes 1572868
  95.5 3.5 %copy-start.14 = (bf16[256,1024]{1,0:T(8,128)(2,1)S(1)}, bf16[256,1024]{1,0:T(8,128)(2,1)}, u32[]{:S(2)}) copy-start(bf16[256,1024]{1,0:T(8,128)(2,1)} %copy-done.13) | copy-start | bytes 1572868
  97.2 4.5 %copy-start.8 = (f32[2048,128]{1,0:T(8,128)S(1)}, f32[2048,128]{1,0:T(8,128)}, u32[]{:S(2)}) copy-start(f32[2048,128]{1,0:T(8,128)} %copy-done.7) | copy-start | bytes 3145732
  97.2 4.5 %copy-start.10 = (f32[2048,128]{1,0:T(8,128)S(1)}, f32[2048,128]{1,0:T(8,128)}, u32[]{:S(2)}) copy-start(f32[2048,128]{1,0:T(8,128)} %copy-done.9) | copy-start | bytes 3145732
  97.2 9.9 %collective-permute-start.20 = (bf16[512,768]{1,0:T(8,128)(2,1)S(1)}, bf16[512,768]{1,0:T(8,128)(2,1)S(1)}, u32[]{:S(2)}, u32[]{:S(2)}) collective-permute-start(bf16[512,768]{1,0:T(8,128)(2,1)S(1)} %shard_map.115), channel_id=1, source_target_pairs={{0,16},{1,17},{2,18},{3,19},{4,20},{5,21},{6,22},{7,23},{8,24},{9,... | collective-permute-start | bytes 2359304 | tf_op jit(solution)/shard_map/ppermute | solution.py:34
  97.3 9.9 %collective-permute-start.19 = (bf16[512,256]{1,0:T(8,128)(2,1)S(1)}, bf16[512,256]{1,0:T(8,128)(2,1)S(1)}, u32[]{:S(2)}, u32[]{:S(2)}) collective-permute-start(bf16[512,256]{1,0:T(8,128)(2,1)S(1)} %shard_map.114), channel_id=1, source_target_pairs={{0,20},{1,21},{2,22},{3,23},{4,16},{5,17},{6,18},{7,19},{8,28},{9,... | collective-permute-start | bytes 786440 | tf_op jit(solution)/shard_map/ppermute | solution.py:34
  101.9 8.2 %collective-permute-start.21 = (bf16[1024,128]{1,0:T(8,128)(2,1)S(1)}, bf16[1024,128]{1,0:T(8,128)(2,1)S(1)}, u32[]{:S(2)}, u32[]{:S(2)}) collective-permute-start(bf16[1024,128]{1,0:T(8,128)(2,1)S(1)} %get-tuple-element.111), channel_id=1, source_target_pairs={{0,2},{1,3},{2,0},{3,1},{4,6},{5,7},{6,4},{7,5},{8,10},{9,11},{10,... | collective-permute-start | bytes 786440 | tf_op jit(solution)/shard_map/ppermute | solution.py:24
  103.0 8.6 %collective-permute-start.22 = (bf16[1024,128]{1,0:T(8,128)(2,1)S(1)}, bf16[1024,128]{1,0:T(8,128)(2,1)S(1)}, u32[]{:S(2)}, u32[]{:S(2)}) collective-permute-start(bf16[1024,128]{1,0:T(8,128)(2,1)S(1)} %get-tuple-element.113), channel_id=1, source_target_pairs={{0,4},{1,5},{2,6},{3,7},{4,0},{5,1},{6,2},{7,3},{8,12},{9,13},{10,... | collective-permute-start | bytes 786440 | tf_op jit(solution)/shard_map/ppermute | solution.py:24
  112.9 7.3 %collective-permute-start.23 = (bf16[512,256]{1,0:T(8,128)(2,1)S(1)}, bf16[512,256]{1,0:T(8,128)(2,1)S(1)}, u32[]{:S(2)}, u32[]{:S(2)}) collective-permute-start(bf16[512,256]{1,0:T(8,128)(2,1)S(1)} %get-tuple-element.114), channel_id=1, source_target_pairs={{0,16},{1,17},{2,18},{3,19},{4,20},{5,21},{6,22},{7,23},{8,24},{9,... | collective-permute-start | bytes 786440 | tf_op jit(solution)/shard_map/ppermute | solution.py:34
  113.0 5.3 %collective-permute-start.24 = (bf16[512,128]{1,0:T(8,128)(2,1)S(1)}, bf16[512,128]{1,0:T(8,128)(2,1)S(1)}, u32[]{:S(2)}, u32[]{:S(2)}) collective-permute-start(bf16[512,128]{1,0:T(8,128)(2,1)S(1)} %get-tuple-element.115), channel_id=1, source_target_pairs={{0,20},{1,21},{2,22},{3,23},{4,16},{5,17},{6,18},{7,19},{8,28},{9,... | collective-permute-start | bytes 393224 | tf_op jit(solution)/shard_map/ppermute | solution.py:34
  114.7 5.6 %collective-permute-start.25 = (bf16[512,128]{1,0:T(8,128)(2,1)S(1)}, bf16[512,128]{1,0:T(8,128)(2,1)S(1)}, u32[]{:S(2)}, u32[]{:S(2)}) collective-permute-start(bf16[512,128]{1,0:T(8,128)(2,1)S(1)} %get-tuple-element.116), channel_id=1, source_target_pairs={{0,17},{1,16},{2,19},{3,18},{4,21},{5,20},{6,23},{7,22},{8,25},{9,... | collective-permute-start | bytes 393224 | tf_op jit(solution)/shard_map/ppermute | solution.py:34

commit v13 on v12

--- a/solution.py
+++ b/solution.py
@@ -350,74 +350,46 @@
     rows_total = len(order) * size
     blocks = rows_total // tile_rows
 
-    def small(kernel, shapes, *operands, cost=QUICK):
+    def small(kernel, shapes, *operands, scratch=(), cost=QUICK):
         return pl.pallas_call(
             kernel,
-            in_specs=[VMEM] * len(operands),
+            in_specs=[SMEM] + [VMEM] * len(operands),
             out_specs=[VMEM] * len(shapes),
             out_shape=[jax.ShapeDtypeStruct(*shape) for shape in shapes],
+            scratch_shapes=list(scratch),
             compiler_params=PARAMS,
             cost_estimate=cost,
-        )(*operands)
-
-    def collect_kernel(*refs):
-        start = 0
-        for ref in refs[:-1]:
-            refs[-1][:, start : start + ref.shape[1]] = ref[...].astype(BF16)
-            start += ref.shape[1]
-
-    (shared,) = small(collect_kernel, [((rank_part, rows_total), BF16)], *parts)
-    flat = [partner(shared, mask) for mask in (1, 2, 3)]
-
-    (c_sent_x, c_sent_y), c_kept = halve(
-        (after(c_kept_x, shared), c_kept_y), (c_first_x, c_first_y)
-    )
-    c_second_x, c_second_y = partner(c_sent_x, 2), partner(c_sent_y, 1)
-
-    wanted = placed.reshape(micro_count, rank, tile_rows)
-    wanted = [
-        lax.dynamic_slice_in_dim(wanted, (high ^ k) * rank_part, rank_part, 1).reshape(
-            micro_count * rank_part, tile_rows
-        )
-        for k in range(1, high_size)
-    ]
-
-    def spread_kernel(*refs):
-        count = len(parts)
-        part_refs, flat_refs, hidden_refs = refs[:count], refs[count : count + 3], refs[count + 3 : -1 - high_size]
-        *message_refs, total_ref = refs[-1 - high_size :]
-        start = 0
+        )(*in_hbm(scalars[0]), *operands)
+
+    def collect_kernel(pos_ref, *refs):
+        part_refs, placed_ref = refs[: len(parts)], refs[len(parts)]
+        *message_refs, wide_ref = refs[len(parts) + 1 :]
+        own = pos_ref[0] // low_size
+        block = 0
         for part_ref in part_refs:
-            columns = slice(start, start + part_ref.shape[1])
-            total = part_ref[...]
-            for flat_ref in flat_refs:
-                total = total + flat_ref[:, columns].astype(F32)
-            total_ref[:, columns] = total
-            start += part_ref.shape[1]
-        for message_ref, hidden_ref in zip(message_refs, hidden_refs):
-            for block in range(blocks):
-                message_ref[block * rank_part : (block + 1) * rank_part, :] = total_ref[
-                    :, block * tile_rows : (block + 1) * tile_rows
+            for start in range(0, part_ref.shape[1], tile_rows):
+                value = part_ref[:, start : start + tile_rows].astype(BF16)
+                for message_ref in message_refs:
+                    message_ref[block * rank_part : (block + 1) * rank_part, :] = value
+                block += 1
+        wide_ref[...] = placed_ref[...].astype(F32)
+        message_refs[0][block * rank_part :, :] = placed_ref[...]
+        for k in range(1, high_size):
+            for m in range(micro_count):
+                start = pl.multiple_of(m * rank + (own ^ k) * rank_part, rank_part)
+                first = (block + m) * rank_part
+                message_refs[k][first : first + rank_part, :] = wide_ref[
+                    pl.ds(start, rank_part), :
                 ].astype(BF16)
-            message_ref[blocks * rank_part :, :] = hidden_ref[...]
-
-    *messages, total = small(
-        spread_kernel,
-        [
-            ((blocks * rank_part + hidden.shape[0], tile_rows), BF16)
-            for hidden in [placed, *wanted]
-        ]
-        + [((rank_part, rows_total), F32)],
+
+    counts = [placed.shape[0]] + [micro_count * rank_part] * (high_size - 1)
+    messages = small(
+        collect_kernel,
+        [((blocks * rank_part + n, tile_rows), BF16) for n in counts],
         *parts,
-        *flat,
         placed,
-        *wanted,
-    )
-    d_sent_x, d_sent_y, _ = lax.optimization_barrier(
-        (d_sent_x, d_sent_y, total, c_second_x, c_second_y)
-    )[:3]
-    d_first_x, d_first_y = partner(d_sent_x, 1), partner(d_sent_y, 2)
-    messages = lax.optimization_barrier((*messages, d_sent_x, own_last))[:high_size]
+        scratch=[pltpu.VMEM(placed.shape, F32)],
+    )
     near = partner(messages[0], 4)
     far = []
     for k in range(1, high_size):
@@ -433,32 +405,88 @@
         rows = slice(block * rank_part, (block + 1) * rank_part)
         return message_ref[rows, start : start + size].astype(F32)
 
-    def lowrank_kernel(high_ref, total_ref, near_ref, *refs):
-        *far_refs, out_ref, whole_ref = refs
+    def lowrank_kernel(pos_ref, *refs):
+        part_refs = refs[: len(parts)]
+        near_ref, *far_refs = refs[len(parts) : -1]
+        out_ref = refs[-1]
+        whole = [(ref, start) for ref in part_refs for start in range(0, ref.shape[1], size)]
         for at, piece in enumerate(order):
             columns = slice(at * size, (at + 1) * size)
             for j in range(high_size):
                 if j == 0:
-                    value = total_ref[:, columns] + block_of(near_ref, columns)
+                    part_ref, start = whole[at]
+                    value = part_ref[:, start : start + size] + block_of(near_ref, columns)
                 else:
                     other = columns_of(j, piece)
                     value = block_of(far_refs[2 * j - 2], other) + block_of(far_refs[2 * j - 1], other)
-                start = pl.multiple_of(((high_ref[0] // low_size) ^ j) * rank_part, rank_part)
-                whole_ref[pl.ds(start, rank_part), columns] = value
-        out_ref[...] = whole_ref[...].astype(BF16)
-
-    lowrank = pl.pallas_call(
-        lowrank_kernel,
-        in_specs=[SMEM] + [VMEM] * (2 + len(far)),
-        out_specs=VMEM,
-        out_shape=jax.ShapeDtypeStruct((rank, rows_total), BF16),
-        scratch_shapes=[pltpu.VMEM((rank, rows_total), F32)],
-        compiler_params=PARAMS,
-        cost_estimate=QUICK,
-    )(*in_hbm(scalars[0]), total, near, *far)
-
-    (c_third,) = last_parts((after(c_kept[0], messages[0]), c_kept[1]), (c_second_x, c_second_y))
-    c_last = relay(c_third, 4)
+                start = pl.multiple_of(((pos_ref[0] // low_size) ^ j) * rank_part, rank_part)
+                out_ref[pl.ds(start, rank_part), columns] = value
+
+    (lowrank,) = small(lowrank_kernel, [((rank, rows_total), F32)], *parts, near, *far)
+
+    halves = [range(0, len(order) // 2), range(len(order) // 2, len(order))]
+
+    def riders(way, count):
+        fit = count // size
+        for i, at in enumerate(halves[way]):
+            rows = slice(i // fit * rank, (i // fit + 1) * rank)
+            yield rows, slice(i % fit * size, (i % fit + 1) * size), slice(at * size, (at + 1) * size)
+
+    def riding(way, count):
+        return -(-len(halves[way]) // (count // size)) * rank
+
+    def ride(ref, first, way, lowrank_ref):
+        for rows, there, whole in riders(way, ref.shape[1]):
+            ref[first + rows.start : first + rows.stop, there] = lowrank_ref[:, whole].astype(BF16)
+
+    def arrive(ref, first, way, lowrank_ref, out_ref):
+        for rows, there, whole in riders(way, ref.shape[1]):
+            got = ref[first + rows.start : first + rows.stop, there].astype(F32)
+            out_ref[:, whole] = (lowrank_ref[:, whole] + got).astype(out_ref.dtype)
+
+    def second_kernel(_, *refs):
+        lowrank_ref = refs[4]
+        for way in range(2):
+            kept_ref, got_ref, sent_ref, rest_ref = refs[way], refs[2 + way], refs[5 + way], refs[7 + way]
+            half = kept_ref.shape[0] // 2
+            sent_ref[:half, :] = (kept_ref[half:, :] + got_ref[half:, :].astype(F32)).astype(BF16)
+            rest_ref[...] = kept_ref[:half, :] + got_ref[:half, :].astype(F32)
+            ride(sent_ref, half, way, lowrank_ref)
+
+    c_counts = [c_kept_x.shape[1], c_kept_y.shape[1]]
+    half_rows = c_kept_x.shape[0] // 2
+    c_sent_x, c_sent_y, *c_kept = small(
+        second_kernel,
+        [((half_rows + riding(way, n), n), BF16) for way, n in enumerate(c_counts)]
+        + [((half_rows, n), F32) for n in c_counts],
+        c_kept_x,
+        c_kept_y,
+        c_first_x,
+        c_first_y,
+        lowrank,
+    )
+    c_second_x, c_second_y = partner(c_sent_x, 2), partner(c_sent_y, 1)
+
+    def append_kernel(_, *refs):
+        lowrank_ref = refs[4]
+        next_ref = refs[7]
+        for way in range(2):
+            sent_ref, got_ref, out_ref = refs[way], refs[2 + way], refs[5 + way]
+            out_ref[: 2 * half_rows, :] = sent_ref[...]
+            arrive(got_ref, half_rows, way, lowrank_ref, next_ref)
+            ride(out_ref, 2 * half_rows, way, next_ref)
+
+    d_sent_x, d_sent_y, lowrank = small(
+        append_kernel,
+        [((2 * half_rows + riding(way, n), n), BF16) for way, n in enumerate(c_counts)]
+        + [((rank, rows_total), F32)],
+        d_sent_x,
+        d_sent_y,
+        c_second_x,
+        c_second_y,
+        lowrank,
+    )
+    d_first_x, d_first_y = partner(d_sent_x, 1), partner(d_sent_y, 2)
 
     all_grads, all_pieces = [], []
     for grads, pieces in chunks:
@@ -473,8 +501,31 @@
         out_shape=jax.ShapeDtypeStruct(up_tile.shape, BF16),
         scratch_shapes=[pltpu.VMEM(up_tile.shape, F32)],
         compiler_params=PARAMS,
-        cost_estimate=QUICK,
+        cost_estimate=LONG,
     )(*in_hbm(*scalars), *all_grads, placed, near, *far)
+
+    def third_kernel(_, *refs):
+        lowrank_ref, whole_ref = refs[4], refs[9]
+        for way in range(2):
+            kept_ref, got_ref, sent_ref, rest_ref = refs[way], refs[2 + way], refs[5 + way], refs[7 + way]
+            half = kept_ref.shape[0] // 2
+            sent_ref[...] = (kept_ref[half:, :] + got_ref[half : 2 * half, :].astype(F32)).astype(BF16)
+            rest_ref[...] = kept_ref[:half, :] + got_ref[:half, :].astype(F32)
+            arrive(got_ref, 2 * half, way, lowrank_ref, whole_ref)
+
+    d_sent_x, d_sent_y, *d_kept, lowrank = small(
+        third_kernel,
+        [((half_rows, n), dtype) for dtype in (BF16, F32) for n in c_counts]
+        + [((rank, rows_total), BF16)],
+        d_kept_x,
+        after(d_kept_y, up_map_gradient, own_last),
+        d_first_x,
+        d_first_y,
+        lowrank,
+    )
+    d_second_x, d_second_y = partner(d_sent_x, 2), partner(d_sent_y, 4)
+    (c_third,) = last_parts((after(c_kept[0], d_sent_x), c_kept[1]), (c_second_x, c_second_y))
+    c_last = relay(c_third, 4)
 
     down = adapter_down_maps[0]
 
@@ -594,18 +645,13 @@
         out_shape=jax.ShapeDtypeStruct(down.shape, BF16),
         scratch_shapes=[pltpu.VMEM(down.shape, F32)],
         compiler_params=PARAMS,
-        cost_estimate=QUICK,
+        cost_estimate=LONG,
     )(*in_hbm(*scalars, forward_input[0]), lowrank)
 
-    c_sums = (after(c_kept[0], c_third), c_second_x), (c_kept[1], c_second_y)
+    c_sums = (after(c_kept[0], c_third, down_map_gradient), c_second_x), (c_kept[1], c_second_y)
     _, kept = with_adapter(own_sums + c_sums, 0, False, QUICK)
-    (d_sent_x, d_sent_y), d_kept = halve(
-        (after(d_kept_x, up_map_gradient, kept), d_kept_y), (d_first_x, d_first_y)
-    )
-    d_second_x, d_second_y = partner(d_sent_x, 2), partner(d_sent_y, 4)
-
     early = relay(kept, 0)
-    d_sums = (after(d_kept[0], down_map_gradient, c_last, early), d_second_x), (d_kept[1], d_second_y)
+    d_sums = (after(d_kept[0], kept), d_second_x), (d_kept[1], d_second_y)
     d_lasts, d_kept = with_adapter(d_sums, kept.shape[1] // size, True, QUICK)
     d_last = [relay(d_lasts[0], 4), relay(d_lasts[1], 1)]
     d_kept = relay(d_kept, 0)

time: 122 us -> 117 us (0.959)
  waiting for transfers between devices: 40.7 us -> 54.8 us
  local copies, waits for them, and re-layouts: 8.24 us -> 1.28 us
  Pallas kernels: 40.8 us -> 35 us
  starting transfers between devices: 30.4 us -> 25 us
    ppermute x20 -> x17, waiting for transfers between devices: 38.4 us -> 47.9 us  [partner(): return lax.ppermute(value, 'tensor', pairs)]
    unnamed x46 -> x2, local copies, waits for them, and re-layouts: 6.17 us -> 0.01 us
    ppermute x6, waiting for transfers between devices: 2.29 us -> 6.95 us  [relay(): return lax.ppermute(value, ('pipe', 'tensor'), pairs)]
    ppermute x20 -> x17, starting transfers between devices: 25.8 us -> 22.7 us  [partner(): return lax.ppermute(value, 'tensor', pairs)]
    ppermute x6, starting transfers between devices: 4.6 us -> 2.27 us  [relay(): return lax.ppermute(value, ('pipe', 'tensor'), pairs)]
    pallas_call x2, Pallas kernels: 2.18 us -> 0.15 us  [last_parts(): pl.pallas_call(functools.partial(last_kernel, len(kept)), in_specs=[VMEM]...]
  transfers between devices with their start and end apart: 26 -> 23, of which waited for: 11 -> 15; matrix products, arithmetic and copies ran while one was open for 0% -> 0% of each run, Pallas kernels for 32% -> 25%
where the time goes in v13:
time: 117 us
  waiting for transfers between devices  54.8 us (47%)
  Pallas kernels  35 us (30%)
  starting transfers between devices  25 us (21%)
  local copies, waits for them, and re-layouts  1.28 us (1%)
    ppermute x17, waiting for transfers between devices, partner(): return lax.ppermute(value, 'tensor', pairs)  47.9 us
    pallas_call x4, Pallas kernels, product(): pl.pallas_call(functools.partial(product_body, low_size, tile_rows, piece...  23.3 us
    ppermute x17, starting transfers between devices, partner(): return lax.ppermute(value, 'tensor', pairs)  22.7 us
    ppermute x6, waiting for transfers between devices, relay(): return lax.ppermute(value, ('pipe', 'tensor'), pairs)  6.95 us
    pallas_call x1, Pallas kernels, shards(): pl.pallas_call(down_kernel, in_specs=[SMEM] * 3 + [VMEM] * 2, out_specs=V...  3.17 us
    pallas_call x2, Pallas kernels, with_adapter(): pl.pallas_call(functools.partial(adapter_kernel, first, with_last, len(su...  2.82 us
    pallas_call x1, Pallas kernels, shards(): pl.pallas_call(functools.partial(up_body, low_size, tile_rows, all_pieces...  2.75 us
  transfers between devices with their start and end apart: 23, of which 15 were waited for; matrix products, arithmetic and copies ran while one was open for 0% of the time, Pallas kernels for 25%

profile of v13, /device:TPU:0, one launch (start us, length us, event | category | flops | bytes accessed | tf_op | source)
XLA Modules:
  0.0 116.9 jit_solution(7704121025624057521)
XLA Ops:
  0.6 1.3 %slice_bitcast_fusion = (bf16[256,1024]{1,0:T(8,128)(2,1)S(1)}, bf16[256,1024]{1,0:T(8,128)(2,1)S(1)}) fusion(bf16[1,1,2,256,1024]{4,3,2,1,0:T(8,128)(2,1)} %param.8), kind=kLoop, calls=%fused_computation | loop fusion | bytes 2097152 | tf_op jit(solution)/shard_map/squeeze | solution.py:317
  1.9 4.1 %collective-permute-start = (bf16[256,1024]{1,0:T(8,128)(2,1)S(1)}, bf16[256,1024]{1,0:T(8,128)(2,1)S(1)}, u32[]{:S(2)}, u32[]{:S(2)}) collective-permute-start(bf16[256,1024]{1,0:T(8,128)(2,1)S(1)} %get-tuple-element.113), channel_id=1, source_target_pairs={{0,8},{1,9},{2,10},{3,11},{4,12},{5,13},{6,14},{7,15},{8,0},{9,1},... | collective-permute-start | bytes 1572872 | tf_op jit(solution)/shard_map/ppermute | solution.py:24
  6.0 5.7 %shard_map.104 = (bf16[2176,256]{1,0:T(8,128)(2,1)S(1)}, bf16[2048,256]{1,0:T(8,128)(2,1)S(1)}, bf16[128,256]{1,0:T(8,128)(2,1)S(1)}) custom-call(s32[1]{0:T(128)} %bitcast.refs_0_.pos_ref._, s32[2,4]{1,0:T(2,128)} %bitcast.36, s32[2]{0:T(128)} %bitcast.44, bf16[2,256,1024]{2,1,0:T(8,128)(2,1)} %bitcast.18, bf16[8,512,1024]{2,1,0:T(8,128)(2,1)} %bitcast.25, ...), custom_call_target="tpu_custom_call" | custom-call | flops 1000 | bytes 1000 | tf_op jit(solution)/shard_map/pallas_call | solution.py:141
  11.7 1.6 %collective-permute-start.2 = (bf16[2176,256]{1,0:T(8,128)(2,1)S(1)}, bf16[2176,256]{1,0:T(8,128)(2,1)S(1)}, u32[]{:S(2)}, u32[]{:S(2)}) collective-permute-start(bf16[2176,256]{1,0:T(8,128)(2,1)S(1)} %get-tuple-element.65), channel_id=1, source_target_pairs={{0,1},{1,0},{2,3},{3,2},{4,5},{5,4},{6,7},{7,6},{8,9},{9,8},{10,11... | collective-permute-start | bytes 3342344 | tf_op jit(solution)/shard_map/ppermute | solution.py:24
  13.3 1.5 %collective-permute-start.3 = (bf16[2048,256]{1,0:T(8,128)(2,1)S(1)}, bf16[2048,256]{1,0:T(8,128)(2,1)S(1)}, u32[]{:S(2)}, u32[]{:S(2)}) collective-permute-start(bf16[2048,256]{1,0:T(8,128)(2,1)S(1)} %get-tuple-element.66), channel_id=1, source_target_pairs={{0,2},{1,3},{2,0},{3,1},{4,6},{5,7},{6,4},{7,5},{8,10},{9,11},{10,... | collective-permute-start | bytes 3145736 | tf_op jit(solution)/shard_map/ppermute | solution.py:24
  14.8 5.8 %shard_map.105 = (f32[2048,256]{1,0:T(8,128)S(1)}, f32[2048,256]{1,0:T(8,128)S(1)}, f32[32,512]{1,0:T(8,128)S(1)}) custom-call(s32[1]{0:T(128)} %bitcast.refs_0_.pos_ref._, s32[2,4]{1,0:T(2,128)} %bitcast.37, s32[2]{0:T(128)} %bitcast.45, bf16[2,256,1024]{2,1,0:T(8,128)(2,1)} %bitcast.19, bf16[8,512,1024]{2,1,0:T(8,128)(2,1)} %bitcast.26, ...), custom_call_target="tpu_custom_call" | custom-call | flops 1000 | bytes 1000 | tf_op jit(solution)/shard_map/pallas_call | solution.py:141
  20.7 8.5 %collective-permute-done = bf16[256,1024]{1,0:T(8,128)(2,1)S(1)} collective-permute-done((bf16[256,1024]{1,0:T(8,128)(2,1)S(1)}, bf16[256,1024]{1,0:T(8,128)(2,1)S(1)}, u32[]{:S(2)}, u32[]{:S(2)}) %collective-permute-start) | collective-permute-done | bytes 524320 | tf_op jit(solution)/shard_map/ppermute | solution.py:24
  29.2 0.0 collective-permute-start.1
  29.2 5.9 %shard_map.106 = (bf16[2048,128]{1,0:T(8,128)(2,1)S(1)}, bf16[2048,128]{1,0:T(8,128)(2,1)S(1)}, f32[2048,128]{1,0:T(8,128)S(1)}, f32[2048,128]{1,0:T(8,128)S(1)}, f32[32,256]{1,0:T(8,128)S(1)}) custom-call(s32[1]{0:T(128)} %bitcast.refs_0_.pos_ref._, s32[2,4]{1,0:T(2,128)} %bitcast.38, s32[2]{0:T(128)} %bitcast.46, bf16[1,256,1024]{2,1,0:T(8,128)(2,1)S(1)} %bitcast.21, ...), custom_call_target="tpu_custom_call" | custom-call | flops 40000000000 | bytes 1000 | tf_op jit(solution)/shard_map/pallas_call | solution.py:141
  35.0 2.6 %collective-permute-done.3.refs_3_ = bf16[2048,256]{1,0:T(8,128)(2,1)S(1)} collective-permute-done((bf16[2048,256]{1,0:T(8,128)(2,1)S(1)}, bf16[2048,256]{1,0:T(8,128)(2,1)S(1)}, u32[]{:S(2)}, u32[]{:S(2)}) %collective-permute-start.3) | collective-permute-done | bytes 1048608 | tf_op jit(solution)/shard_map/ppermute | solution.py:24
  37.6 0.2 collective-permute-done.2.refs_2_
  37.8 0.3 shard_map.107
  38.2 1.6 %collective-permute-start.4 = (bf16[1152,256]{1,0:T(8,128)(2,1)S(1)}, bf16[1152,256]{1,0:T(8,128)(2,1)S(1)}, u32[]{:S(2)}, u32[]{:S(2)}) collective-permute-start(bf16[1152,256]{1,0:T(8,128)(2,1)S(1)} %get-tuple-element.79), channel_id=1, source_target_pairs={{0,2},{1,3},{2,0},{3,1},{4,6},{5,7},{6,4},{7,5},{8,10},{9,11},{10,... | collective-permute-start | bytes 1769480 | tf_op jit(solution)/shard_map/ppermute | solution.py:24
  39.8 1.5 %collective-permute-start.5 = (bf16[1024,256]{1,0:T(8,128)(2,1)S(1)}, bf16[1024,256]{1,0:T(8,128)(2,1)S(1)}, u32[]{:S(2)}, u32[]{:S(2)}) collective-permute-start(bf16[1024,256]{1,0:T(8,128)(2,1)S(1)} %get-tuple-element.80), channel_id=1, source_target_pairs={{0,1},{1,0},{2,3},{3,2},{4,5},{5,4},{6,7},{7,6},{8,9},{9,8},{10,11... | collective-permute-start | bytes 1572872 | tf_op jit(solution)/shard_map/ppermute | solution.py:24
  41.2 0.5 collective-permute-start.11
  41.7 0.5 collective-permute-start.10
  42.3 12.1 %collective-permute-done.1 = bf16[256,1024]{1,0:T(8,128)(2,1)S(1)} collective-permute-done((bf16[256,1024]{1,0:T(8,128)(2,1)S(1)}, bf16[256,1024]{1,0:T(8,128)(2,1)S(1)}, u32[]{:S(2)}, u32[]{:S(2)}) %collective-permute-start.1) | collective-permute-done | bytes 524320 | tf_op jit(solution)/shard_map/ppermute | solution.py:24
  54.4 5.9 %shard_map.103 = (bf16[2048,128]{1,0:T(8,128)(2,1)S(1)}, bf16[2048,128]{1,0:T(8,128)(2,1)S(1)}, f32[2048,128]{1,0:T(8,128)S(1)}, f32[2048,128]{1,0:T(8,128)S(1)}, f32[32,256]{1,0:T(8,128)S(1)}) custom-call(s32[1]{0:T(128)} %bitcast.refs_0_.pos_ref._, s32[2,4]{1,0:T(2,128)} %bitcast.39, s32[2]{0:T(128)} %bitcast.47, bf16[1,256,1024]{2,1,0:T(8,128)(2,1)S(1)} %bitcast.23, ...), custom_call_target="tpu_custom_call" | custom-call | flops 40000000000 | bytes 1000 | tf_op jit(solution)/shard_map/pallas_call | solution.py:141
  60.3 0.0 collective-permute-done.5.refs_3_.refs_8_
  60.3 0.0 collective-permute-done.4.refs_2_.refs_6_
  60.3 0.1 shard_map.108
  60.4 0.1 collective-permute-start.6
  60.5 1.7 %collective-permute-start.7 = (bf16[192,256]{1,0:T(8,128)(2,1)S(1)}, bf16[192,256]{1,0:T(8,128)(2,1)S(1)}, u32[]{:S(2)}, u32[]{:S(2)}) collective-permute-start(bf16[192,256]{1,0:T(8,128)(2,1)S(1)} %get-tuple-element.84), channel_id=1, source_target_pairs={{0,8},{1,9},{2,10},{3,11},{4,12},{5,13},{6,14},{7,15},{8,0},{9,1},... | collective-permute-start | bytes 294920 | tf_op jit(solution)/shard_map/ppermute | solution.py:24
  62.3 2.6 %collective-permute-start.8 = (bf16[192,256]{1,0:T(8,128)(2,1)S(1)}, bf16[192,256]{1,0:T(8,128)(2,1)S(1)}, u32[]{:S(2)}, u32[]{:S(2)}) collective-permute-start(bf16[192,256]{1,0:T(8,128)(2,1)S(1)} %get-tuple-element.84), channel_id=1, source_target_pairs={{0,12},{1,13},{2,14},{3,15},{4,8},{5,9},{6,10},{7,11},{8,4},{9,5},... | collective-permute-start | bytes 294920 | tf_op jit(solution)/shard_map/ppermute | solution.py:24
  64.9 5.5 %collective-permute-done.7.refs_8_.refs_4_ = bf16[192,256]{1,0:T(8,128)(2,1)S(1)} collective-permute-done((bf16[192,256]{1,0:T(8,128)(2,1)S(1)}, bf16[192,256]{1,0:T(8,128)(2,1)S(1)}, u32[]{:S(2)}, u32[]{:S(2)}) %collective-permute-start.7) | collective-permute-done | bytes 98336 | tf_op jit(solution)/shard_map/ppermute | solution.py:24
  70.4 0.0 collective-permute-done.8.refs_9_.refs_5_
  70.4 0.0 collective-permute-done.6.refs_7_.refs_3_
  70.5 0.0 collective-permute-done.11.refs_3_
  70.5 0.0 collective-permute-done.10.refs_2_
  70.5 0.0 copy-start
  70.5 0.2 shard_map.112
  70.7 1.3 %collective-permute-start.12 = (bf16[1280,128]{1,0:T(8,128)(2,1)S(1)}, bf16[1280,128]{1,0:T(8,128)(2,1)S(1)}, u32[]{:S(2)}, u32[]{:S(2)}) collective-permute-start(bf16[1280,128]{1,0:T(8,128)(2,1)S(1)} %get-tuple-element.95), channel_id=1, source_target_pairs={{0,2},{1,3},{2,0},{3,1},{4,6},{5,7},{6,4},{7,5},{8,10},{9,11},{10,... | collective-permute-start | bytes 983048 | tf_op jit(solution)/shard_map/ppermute | solution.py:24
  72.0 1.5 %collective-permute-start.13 = (bf16[1280,128]{1,0:T(8,128)(2,1)S(1)}, bf16[1280,128]{1,0:T(8,128)(2,1)S(1)}, u32[]{:S(2)}, u32[]{:S(2)}) collective-permute-start(bf16[1280,128]{1,0:T(8,128)(2,1)S(1)} %get-tuple-element.96), channel_id=1, source_target_pairs={{0,1},{1,0},{2,3},{3,2},{4,5},{5,4},{6,7},{7,6},{8,9},{9,8},{10,11... | collective-permute-start | bytes 983048 | tf_op jit(solution)/shard_map/ppermute | solution.py:24
  73.5 0.0 collective-permute-start.9
  73.5 4.8 %collective-permute-done.12.refs_2_.refs_10_ = bf16[1280,128]{1,0:T(8,128)(2,1)S(1)} collective-permute-done((bf16[1280,128]{1,0:T(8,128)(2,1)S(1)}, bf16[1280,128]{1,0:T(8,128)(2,1)S(1)}, u32[]{:S(2)}, u32[]{:S(2)}) %collective-permute-start.12) | collective-permute-done | bytes 327712 | tf_op jit(solution)/shard_map/ppermute | solution.py:24
  78.3 1.4 %collective-permute-done.13.refs_3_.refs_12_ = bf16[1280,128]{1,0:T(8,128)(2,1)S(1)} collective-permute-done((bf16[1280,128]{1,0:T(8,128)(2,1)S(1)}, bf16[1280,128]{1,0:T(8,128)(2,1)S(1)}, u32[]{:S(2)}, u32[]{:S(2)}) %collective-permute-start.13) | collective-permute-done | bytes 327712 | tf_op jit(solution)/shard_map/ppermute | solution.py:24
  79.7 0.1 shard_map.113
  79.8 1.6 %collective-permute-start.14 = (bf16[2304,128]{1,0:T(8,128)(2,1)S(1)}, bf16[2304,128]{1,0:T(8,128)(2,1)S(1)}, u32[]{:S(2)}, u32[]{:S(2)}) collective-permute-start(bf16[2304,128]{1,0:T(8,128)(2,1)S(1)} %get-tuple-element.97), channel_id=1, source_target_pairs={{0,1},{1,0},{2,3},{3,2},{4,5},{5,4},{6,7},{7,6},{8,9},{9,8},{10,11... | collective-permute-start | bytes 1769480 | tf_op jit(solution)/shard_map/ppermute | solution.py:24
  81.4 0.5 collective-permute-start.15
  81.9 2.8 %shard_map.110 = bf16[8,32,1024]{2,1,0:T(8,128)(2,1)} custom-call(s32[1]{0:T(128)} %bitcast.refs_0_.pos_ref._, s32[2,4]{1,0:T(2,128)} %bitcast.40, s32[2]{0:T(128)} %bitcast.48, bf16[2,256,1024]{2,1,0:T(8,128)(2,1)S(1)} %bitcast.20, bf16[1,256,1024]{2,1,0:T(8,128)(2,1)S(1)} %bitcast.22, bf16[1,256,1024]{2,1,0:T(8,128)(2,1)S(1)} %bitcast.24, ...), custom_call_target="tpu_custom_call" | custom-call | flops 40000000000 | bytes 1000 | tf_op jit(solution)/shard_map/pallas_call | solution.py:495
  84.6 3.0 %collective-permute-done.9.refs_2_ = bf16[512,512]{1,0:T(8,128)(2,1)S(1)} collective-permute-done((bf16[512,512]{1,0:T(8,128)(2,1)S(1)}, bf16[512,512]{1,0:T(8,128)(2,1)S(1)}, u32[]{:S(2)}, u32[]{:S(2)}) %collective-permute-start.9) | collective-permute-done | bytes 524320 | tf_op jit(solution)/shard_map/ppermute | solution.py:34
  87.6 4.4 %collective-permute-done.14.refs_2_ = bf16[2304,128]{1,0:T(8,128)(2,1)S(1)} collective-permute-done((bf16[2304,128]{1,0:T(8,128)(2,1)S(1)}, bf16[2304,128]{1,0:T(8,128)(2,1)S(1)}, u32[]{:S(2)}, u32[]{:S(2)}) %collective-permute-start.14) | collective-permute-done | bytes 589856 | tf_op jit(solution)/shard_map/ppermute | solution.py:24
  92.0 0.7 collective-permute-done.15.refs_3_
  92.7 0.2 shard_map.114
  92.9 3.2 %shard_map.116 = bf16[8,64,512]{2,1,0:T(8,128)(2,1)} custom-call(s32[1]{0:T(128)} %bitcast.refs_0_.pos_ref._, s32[2,4]{1,0:T(2,128)} %bitcast.41, s32[2]{0:T(128)} %bitcast.49, bf16[2,512,512]{2,1,0:T(8,128)(2,1)} %bitcast.52, bf16[64,1024]{1,0:T(8,128)(2,1)S(1)} %get-tuple-element.100.lowrank_ref.refs_4_), custom_call_target="tpu_custom_call" | custom-call | flops 40000000000 | bytes 1000 | tf_op jit(solution)/shard_map/pallas_call | solution.py:641
  96.0 0.1 shard_map.115
  96.1 1.5 %shard_map.117 = bf16[512,768]{1,0:T(8,128)(2,1)S(1)} custom-call(s32[1]{0:T(128)} %bitcast.refs_0_.pos_ref._, s32[2,4]{1,0:T(2,128)} %bitcast.42, s32[2]{0:T(128)} %bitcast.50, bf16[8,64,512]{2,1,0:T(8,128)(2,1)} %bitcast.30, bf16[64,1024]{1,0:T(8,128)(2,1)S(1)} %get-tuple-element.100.lowrank_ref.refs_4_, ...), custom_call_target="tpu_custom_call" | custom-call | flops 1000 | bytes 1000 | tf_op jit(solution)/shard_map/pallas_call | solution.py:565
  97.6 0.1 collective-permute-start.21
  97.7 0.6 collective-permute-start.16
  98.3 1.5 %collective-permute-start.17 = (bf16[1024,128]{1,0:T(8,128)(2,1)S(1)}, bf16[1024,128]{1,0:T(8,128)(2,1)S(1)}, u32[]{:S(2)}, u32[]{:S(2)}) collective-permute-start(bf16[1024,128]{1,0:T(8,128)(2,1)S(1)} %get-tuple-element.109), channel_id=1, source_target_pairs={{0,4},{1,5},{2,6},{3,7},{4,0},{5,1},{6,2},{7,3},{8,12},{9,13},{10,... | collective-permute-start | bytes 786440 | tf_op jit(solution)/shard_map/ppermute | solution.py:24
  99.8 0.0 collective-permute-start.22
  99.8 6.6 %collective-permute-done.16.refs_6_ = bf16[1024,128]{1,0:T(8,128)(2,1)S(1)} collective-permute-done((bf16[1024,128]{1,0:T(8,128)(2,1)S(1)}, bf16[1024,128]{1,0:T(8,128)(2,1)S(1)}, u32[]{:S(2)}, u32[]{:S(2)}) %collective-permute-start.16) | collective-permute-done | bytes 262176 | tf_op jit(solution)/shard_map/ppermute | solution.py:24
  106.4 1.1 collective-permute-done.17.refs_8_
  107.4 1.3 %shard_map.118 = (bf16[512,128]{1,0:T(8,128)(2,1)S(1)}, bf16[512,128]{1,0:T(8,128)(2,1)S(1)}, bf16[512,256]{1,0:T(8,128)(2,1)S(1)}) custom-call(s32[1]{0:T(128)} %bitcast.refs_0_.pos_ref._, s32[2,4]{1,0:T(2,128)} %bitcast.43, s32[2]{0:T(128)} %bitcast.51, bf16[8,64,512]{2,1,0:T(8,128)(2,1)} %bitcast.31, ...), custom_call_target="tpu_custom_call" | custom-call | flops 1000 | bytes 1000 | tf_op jit(solution)/shard_map/pallas_call | solution.py:565
  108.8 0.1 collective-permute-start.18
  108.9 1.6 %collective-permute-start.19 = (bf16[512,128]{1,0:T(8,128)(2,1)S(1)}, bf16[512,128]{1,0:T(8,128)(2,1)S(1)}, u32[]{:S(2)}, u32[]{:S(2)}) collective-permute-start(bf16[512,128]{1,0:T(8,128)(2,1)S(1)} %get-tuple-element.111), channel_id=1, source_target_pairs={{0,20},{1,21},{2,22},{3,23},{4,16},{5,17},{6,18},{7,19},{8,28},{9,... | collective-permute-start | bytes 393224 | tf_op jit(solution)/shard_map/ppermute | solution.py:34
  110.5 0.5 collective-permute-start.20
  111.0 0.6 collective-permute-done.22.refs_3_
  111.6 0.0 collective-permute-done.21.refs_1_
  111.6 1.1 shard_map.119.refs_4_
  112.7 2.1 %collective-permute-done.19.refs_2_ = bf16[512,128]{1,0:T(8,128)(2,1)S(1)} collective-permute-done((bf16[512,128]{1,0:T(8,128)(2,1)S(1)}, bf16[512,128]{1,0:T(8,128)(2,1)S(1)}, u32[]{:S(2)}, u32[]{:S(2)}) %collective-permute-start.19) | collective-permute-done | bytes 131104 | tf_op jit(solution)/shard_map/ppermute | solution.py:34
  114.8 1.2 %collective-permute-done.20.refs_3_ = bf16[512,128]{1,0:T(8,128)(2,1)S(1)} collective-permute-done((bf16[512,128]{1,0:T(8,128)(2,1)S(1)}, bf16[512,128]{1,0:T(8,128)(2,1)S(1)}, u32[]{:S(2)}, u32[]{:S(2)}) %collective-permute-start.20) | collective-permute-done | bytes 131104 | tf_op jit(solution)/shard_map/ppermute | solution.py:34
  116.0 0.0 collective-permute-done.18.refs_1_
  116.0 0.8 shard_map.120
  (3 shorter events, 0.1 us)
Async XLA Ops:
  1.9 27.3 %collective-permute-start = (bf16[256,1024]{1,0:T(8,128)(2,1)S(1)}, bf16[256,1024]{1,0:T(8,128)(2,1)S(1)}, u32[]{:S(2)}, u32[]{:S(2)}) collective-permute-start(bf16[256,1024]{1,0:T(8,128)(2,1)S(1)} %get-tuple-element.113), channel_id=1, source_target_pairs={{0,8},{1,9},{2,10},{3,11},{4,12},{5,13},{6,14},{7,15},{8,0},{9,1},... | collective-permute-start | bytes 1572872 | tf_op jit(solution)/shard_map/ppermute | solution.py:24
  11.7 26.1 %collective-permute-start.2 = (bf16[2176,256]{1,0:T(8,128)(2,1)S(1)}, bf16[2176,256]{1,0:T(8,128)(2,1)S(1)}, u32[]{:S(2)}, u32[]{:S(2)}) collective-permute-start(bf16[2176,256]{1,0:T(8,128)(2,1)S(1)} %get-tuple-element.65), channel_id=1, source_target_pairs={{0,1},{1,0},{2,3},{3,2},{4,5},{5,4},{6,7},{7,6},{8,9},{9,8},{10,11... | collective-permute-start | bytes 3342344 | tf_op jit(solution)/shard_map/ppermute | solution.py:24
  13.3 24.3 %collective-permute-start.3 = (bf16[2048,256]{1,0:T(8,128)(2,1)S(1)}, bf16[2048,256]{1,0:T(8,128)(2,1)S(1)}, u32[]{:S(2)}, u32[]{:S(2)}) collective-permute-start(bf16[2048,256]{1,0:T(8,128)(2,1)S(1)} %get-tuple-element.66), channel_id=1, source_target_pairs={{0,2},{1,3},{2,0},{3,1},{4,6},{5,7},{6,4},{7,5},{8,10},{9,11},{10,... | collective-permute-start | bytes 3145736 | tf_op jit(solution)/shard_map/ppermute | solution.py:24
  29.2 25.2 %collective-permute-start.1 = (bf16[256,1024]{1,0:T(8,128)(2,1)S(1)}, bf16[256,1024]{1,0:T(8,128)(2,1)S(1)}, u32[]{:S(2)}, u32[]{:S(2)}) collective-permute-start(bf16[256,1024]{1,0:T(8,128)(2,1)S(1)} %get-tuple-element.61), channel_id=1, source_target_pairs={{0,8},{1,9},{2,10},{3,11},{4,12},{5,13},{6,14},{7,15},{8,0},{9,1},... | collective-permute-start | bytes 1572872 | tf_op jit(solution)/shard_map/ppermute | solution.py:24
  38.2 22.1 %collective-permute-start.4 = (bf16[1152,256]{1,0:T(8,128)(2,1)S(1)}, bf16[1152,256]{1,0:T(8,128)(2,1)S(1)}, u32[]{:S(2)}, u32[]{:S(2)}) collective-permute-start(bf16[1152,256]{1,0:T(8,128)(2,1)S(1)} %get-tuple-element.79), channel_id=1, source_target_pairs={{0,2},{1,3},{2,0},{3,1},{4,6},{5,7},{6,4},{7,5},{8,10},{9,11},{10,... | collective-permute-start | bytes 1769480 | tf_op jit(solution)/shard_map/ppermute | solution.py:24
  39.8 20.5 %collective-permute-start.5 = (bf16[1024,256]{1,0:T(8,128)(2,1)S(1)}, bf16[1024,256]{1,0:T(8,128)(2,1)S(1)}, u32[]{:S(2)}, u32[]{:S(2)}) collective-permute-start(bf16[1024,256]{1,0:T(8,128)(2,1)S(1)} %get-tuple-element.80), channel_id=1, source_target_pairs={{0,1},{1,0},{2,3},{3,2},{4,5},{5,4},{6,7},{7,6},{8,9},{9,8},{10,11... | collective-permute-start | bytes 1572872 | tf_op jit(solution)/shard_map/ppermute | solution.py:24
  41.2 29.2 %collective-permute-start.11 = (bf16[2048,128]{1,0:T(8,128)(2,1)S(1)}, bf16[2048,128]{1,0:T(8,128)(2,1)S(1)}, u32[]{:S(2)}, u32[]{:S(2)}) collective-permute-start(bf16[2048,128]{1,0:T(8,128)(2,1)S(1)} %get-tuple-element.94), channel_id=1, source_target_pairs={{0,2},{1,3},{2,0},{3,1},{4,6},{5,7},{6,4},{7,5},{8,10},{9,11},{10,... | collective-permute-start | bytes 1572872 | tf_op jit(solution)/shard_map/ppermute | solution.py:24
  41.7 28.7 %collective-permute-start.10 = (bf16[2048,128]{1,0:T(8,128)(2,1)S(1)}, bf16[2048,128]{1,0:T(8,128)(2,1)S(1)}, u32[]{:S(2)}, u32[]{:S(2)}) collective-permute-start(bf16[2048,128]{1,0:T(8,128)(2,1)S(1)} %get-tuple-element.92), channel_id=1, source_target_pairs={{0,1},{1,0},{2,3},{3,2},{4,5},{5,4},{6,7},{7,6},{8,9},{9,8},{10,11... | collective-permute-start | bytes 1572872 | tf_op jit(solution)/shard_map/ppermute | solution.py:24
  60.4 10.0 %collective-permute-start.6 = (bf16[256,256]{1,0:T(8,128)(2,1)S(1)}, bf16[256,256]{1,0:T(8,128)(2,1)S(1)}, u32[]{:S(2)}, u32[]{:S(2)}) collective-permute-start(bf16[256,256]{1,0:T(8,128)(2,1)S(1)} %get-tuple-element.83), channel_id=1, source_target_pairs={{0,4},{1,5},{2,6},{3,7},{4,0},{5,1},{6,2},{7,3},{8,12},{9,13},{10,... | collective-permute-start | bytes 393224 | tf_op jit(solution)/shard_map/ppermute | solution.py:24
  60.5 9.9 %collective-permute-start.7 = (bf16[192,256]{1,0:T(8,128)(2,1)S(1)}, bf16[192,256]{1,0:T(8,128)(2,1)S(1)}, u32[]{:S(2)}, u32[]{:S(2)}) collective-permute-start(bf16[192,256]{1,0:T(8,128)(2,1)S(1)} %get-tuple-element.84), channel_id=1, source_target_pairs={{0,8},{1,9},{2,10},{3,11},{4,12},{5,13},{6,14},{7,15},{8,0},{9,1},... | collective-permute-start | bytes 294920 | tf_op jit(solution)/shard_map/ppermute | solution.py:24
  62.3 8.2 %collective-permute-start.8 = (bf16[192,256]{1,0:T(8,128)(2,1)S(1)}, bf16[192,256]{1,0:T(8,128)(2,1)S(1)}, u32[]{:S(2)}, u32[]{:S(2)}) collective-permute-start(bf16[192,256]{1,0:T(8,128)(2,1)S(1)} %get-tuple-element.84), channel_id=1, source_target_pairs={{0,12},{1,13},{2,14},{3,15},{4,8},{5,9},{6,10},{7,11},{8,4},{9,5},... | collective-permute-start | bytes 294920 | tf_op jit(solution)/shard_map/ppermute | solution.py:24
  70.5 11.4 %copy-start = (bf16[1,1,2,256,1024]{4,3,2,1,0:T(8,128)(2,1)S(1)}, bf16[1,1,2,256,1024]{4,3,2,1,0:T(8,128)(2,1)}, u32[]{:S(2)}) copy-start(bf16[1,1,2,256,1024]{4,3,2,1,0:T(8,128)(2,1)} %param.8) | copy-start | bytes 3145732
  70.7 7.6 %collective-permute-start.12 = (bf16[1280,128]{1,0:T(8,128)(2,1)S(1)}, bf16[1280,128]{1,0:T(8,128)(2,1)S(1)}, u32[]{:S(2)}, u32[]{:S(2)}) collective-permute-start(bf16[1280,128]{1,0:T(8,128)(2,1)S(1)} %get-tuple-element.95), channel_id=1, source_target_pairs={{0,2},{1,3},{2,0},{3,1},{4,6},{5,7},{6,4},{7,5},{8,10},{9,11},{10,... | collective-permute-start | bytes 983048 | tf_op jit(solution)/shard_map/ppermute | solution.py:24
  72.0 7.7 %collective-permute-start.13 = (bf16[1280,128]{1,0:T(8,128)(2,1)S(1)}, bf16[1280,128]{1,0:T(8,128)(2,1)S(1)}, u32[]{:S(2)}, u32[]{:S(2)}) collective-permute-start(bf16[1280,128]{1,0:T(8,128)(2,1)S(1)} %get-tuple-element.96), channel_id=1, source_target_pairs={{0,1},{1,0},{2,3},{3,2},{4,5},{5,4},{6,7},{7,6},{8,9},{9,8},{10,11... | collective-permute-start | bytes 983048 | tf_op jit(solution)/shard_map/ppermute | solution.py:24
  73.5 14.1 %collective-permute-start.9 = (bf16[512,512]{1,0:T(8,128)(2,1)S(1)}, bf16[512,512]{1,0:T(8,128)(2,1)S(1)}, u32[]{:S(2)}, u32[]{:S(2)}) collective-permute-start(bf16[512,512]{1,0:T(8,128)(2,1)S(1)} %get-tuple-element.85), channel_id=1, source_target_pairs={{0,20},{1,21},{2,22},{3,23},{4,16},{5,17},{6,18},{7,19},{8,28},{9,... | collective-permute-start | bytes 1572872 | tf_op jit(solution)/shard_map/ppermute | solution.py:34
  79.8 12.1 %collective-permute-start.14 = (bf16[2304,128]{1,0:T(8,128)(2,1)S(1)}, bf16[2304,128]{1,0:T(8,128)(2,1)S(1)}, u32[]{:S(2)}, u32[]{:S(2)}) collective-permute-start(bf16[2304,128]{1,0:T(8,128)(2,1)S(1)} %get-tuple-element.97), channel_id=1, source_target_pairs={{0,1},{1,0},{2,3},{3,2},{4,5},{5,4},{6,7},{7,6},{8,9},{9,8},{10,11... | collective-permute-start | bytes 1769480 | tf_op jit(solution)/shard_map/ppermute | solution.py:24
  81.4 11.3 %collective-permute-start.15 = (bf16[2304,128]{1,0:T(8,128)(2,1)S(1)}, bf16[2304,128]{1,0:T(8,128)(2,1)S(1)}, u32[]{:S(2)}, u32[]{:S(2)}) collective-permute-start(bf16[2304,128]{1,0:T(8,128)(2,1)S(1)} %get-tuple-element.98), channel_id=1, source_target_pairs={{0,2},{1,3},{2,0},{3,1},{4,6},{5,7},{6,4},{7,5},{8,10},{9,11},{10,... | collective-permute-start | bytes 1769480 | tf_op jit(solution)/shard_map/ppermute | solution.py:24
  97.6 14.0 %collective-permute-start.21 = (bf16[512,768]{1,0:T(8,128)(2,1)S(1)}, bf16[512,768]{1,0:T(8,128)(2,1)S(1)}, u32[]{:S(2)}, u32[]{:S(2)}) collective-permute-start(bf16[512,768]{1,0:T(8,128)(2,1)S(1)} %shard_map.117), channel_id=1, source_target_pairs={{0,16},{1,17},{2,18},{3,19},{4,20},{5,21},{6,22},{7,23},{8,24},{9,... | collective-permute-start | bytes 2359304 | tf_op jit(solution)/shard_map/ppermute | solution.py:34
  97.7 8.7 %collective-permute-start.16 = (bf16[1024,128]{1,0:T(8,128)(2,1)S(1)}, bf16[1024,128]{1,0:T(8,128)(2,1)S(1)}, u32[]{:S(2)}, u32[]{:S(2)}) collective-permute-start(bf16[1024,128]{1,0:T(8,128)(2,1)S(1)} %get-tuple-element.103), channel_id=1, source_target_pairs={{0,2},{1,3},{2,0},{3,1},{4,6},{5,7},{6,4},{7,5},{8,10},{9,11},{10,... | collective-permute-start | bytes 786440 | tf_op jit(solution)/shard_map/ppermute | solution.py:24
  98.3 9.2 %collective-permute-start.17 = (bf16[1024,128]{1,0:T(8,128)(2,1)S(1)}, bf16[1024,128]{1,0:T(8,128)(2,1)S(1)}, u32[]{:S(2)}, u32[]{:S(2)}) collective-permute-start(bf16[1024,128]{1,0:T(8,128)(2,1)S(1)} %get-tuple-element.109), channel_id=1, source_target_pairs={{0,4},{1,5},{2,6},{3,7},{4,0},{5,1},{6,2},{7,3},{8,12},{9,13},{10,... | collective-permute-start | bytes 786440 | tf_op jit(solution)/shard_map/ppermute | solution.py:24
  99.8 11.8 %collective-permute-start.22 = (bf16[512,256]{1,0:T(8,128)(2,1)S(1)}, bf16[512,256]{1,0:T(8,128)(2,1)S(1)}, u32[]{:S(2)}, u32[]{:S(2)}) collective-permute-start(bf16[512,256]{1,0:T(8,128)(2,1)S(1)} %shard_map.115), channel_id=1, source_target_pairs={{0,20},{1,21},{2,22},{3,23},{4,16},{5,17},{6,18},{7,19},{8,28},{9,... | collective-permute-start | bytes 786440 | tf_op jit(solution)/shard_map/ppermute | solution.py:34
  108.8 7.3 %collective-permute-start.18 = (bf16[512,256]{1,0:T(8,128)(2,1)S(1)}, bf16[512,256]{1,0:T(8,128)(2,1)S(1)}, u32[]{:S(2)}, u32[]{:S(2)}) collective-permute-start(bf16[512,256]{1,0:T(8,128)(2,1)S(1)} %get-tuple-element.110), channel_id=1, source_target_pairs={{0,16},{1,17},{2,18},{3,19},{4,20},{5,21},{6,22},{7,23},{8,24},{9,... | collective-permute-start | bytes 786440 | tf_op jit(solution)/shard_map/ppermute | solution.py:34
  108.9 5.9 %collective-permute-start.19 = (bf16[512,128]{1,0:T(8,128)(2,1)S(1)}, bf16[512,128]{1,0:T(8,128)(2,1)S(1)}, u32[]{:S(2)}, u32[]{:S(2)}) collective-permute-start(bf16[512,128]{1,0:T(8,128)(2,1)S(1)} %get-tuple-element.111), channel_id=1, source_target_pairs={{0,20},{1,21},{2,22},{3,23},{4,16},{5,17},{6,18},{7,19},{8,28},{9,... | collective-permute-start | bytes 393224 | tf_op jit(solution)/shard_map/ppermute | solution.py:34
  110.5 5.6 %collective-permute-start.20 = (bf16[512,128]{1,0:T(8,128)(2,1)S(1)}, bf16[512,128]{1,0:T(8,128)(2,1)S(1)}, u32[]{:S(2)}, u32[]{:S(2)}) collective-permute-start(bf16[512,128]{1,0:T(8,128)(2,1)S(1)} %get-tuple-element.112), channel_id=1, source_target_pairs={{0,17},{1,16},{2,19},{3,18},{4,21},{5,20},{6,23},{7,22},{8,25},{9,... | collective-permute-start | bytes 393224 | tf_op jit(solution)/shard_map/ppermute | solution.py:34

commit v14 on v13

--- a/solution.py
+++ b/solution.py
@@ -340,7 +340,7 @@
     chunks = [([grad_tile], own_pieces), (got0, pieces_of(0)), (got1, pieces_of(1))]
     order = [piece for _, pieces in chunks for _, _, piece, _ in pieces]
     d_sent_x, d_sent_y, d_kept_x, d_kept_y, part = produce(
-        got1, pieces_of(1), True, True, True, LONG
+        got1, pieces_of(1), False, True, True, LONG
     )
     parts.append(part)
     own_third, placed = last_parts((after(kept_x, part), kept_y), (second_x, second_y), placed)
@@ -390,6 +390,10 @@
         placed,
         scratch=[pltpu.VMEM(placed.shape, F32)],
     )
+    (c_sent_x, c_sent_y), c_kept = halve(
+        (after(c_kept_x, messages[0]), c_kept_y), (c_first_x, c_first_y)
+    )
+    c_second_x, c_second_y = partner(c_sent_x, 2), partner(c_sent_y, 1)
     near = partner(messages[0], 4)
     far = []
     for k in range(1, high_size):
@@ -444,47 +448,20 @@
             got = ref[first + rows.start : first + rows.stop, there].astype(F32)
             out_ref[:, whole] = (lowrank_ref[:, whole] + got).astype(out_ref.dtype)
 
-    def second_kernel(_, *refs):
-        lowrank_ref = refs[4]
+    half_rows = d_sent_x.shape[0] // 2
+    d_counts = [d_sent_x.shape[1], d_sent_y.shape[1]]
+
+    def append_kernel(_, *refs):
         for way in range(2):
-            kept_ref, got_ref, sent_ref, rest_ref = refs[way], refs[2 + way], refs[5 + way], refs[7 + way]
-            half = kept_ref.shape[0] // 2
-            sent_ref[:half, :] = (kept_ref[half:, :] + got_ref[half:, :].astype(F32)).astype(BF16)
-            rest_ref[...] = kept_ref[:half, :] + got_ref[:half, :].astype(F32)
-            ride(sent_ref, half, way, lowrank_ref)
-
-    c_counts = [c_kept_x.shape[1], c_kept_y.shape[1]]
-    half_rows = c_kept_x.shape[0] // 2
-    c_sent_x, c_sent_y, *c_kept = small(
-        second_kernel,
-        [((half_rows + riding(way, n), n), BF16) for way, n in enumerate(c_counts)]
-        + [((half_rows, n), F32) for n in c_counts],
-        c_kept_x,
-        c_kept_y,
-        c_first_x,
-        c_first_y,
-        lowrank,
-    )
-    c_second_x, c_second_y = partner(c_sent_x, 2), partner(c_sent_y, 1)
-
-    def append_kernel(_, *refs):
-        lowrank_ref = refs[4]
-        next_ref = refs[7]
-        for way in range(2):
-            sent_ref, got_ref, out_ref = refs[way], refs[2 + way], refs[5 + way]
-            out_ref[: 2 * half_rows, :] = sent_ref[...]
-            arrive(got_ref, half_rows, way, lowrank_ref, next_ref)
-            ride(out_ref, 2 * half_rows, way, next_ref)
-
-    d_sent_x, d_sent_y, lowrank = small(
+            refs[3 + way][: 2 * half_rows, :] = refs[way][...]
+            ride(refs[3 + way], 2 * half_rows, way, refs[2])
+
+    d_sent_x, d_sent_y = small(
         append_kernel,
-        [((2 * half_rows + riding(way, n), n), BF16) for way, n in enumerate(c_counts)]
-        + [((rank, rows_total), F32)],
+        [((2 * half_rows + riding(way, n), n), BF16) for way, n in enumerate(d_counts)],
         d_sent_x,
         d_sent_y,
-        c_second_x,
-        c_second_y,
-        lowrank,
+        after(lowrank, *c_kept),
     )
     d_first_x, d_first_y = partner(d_sent_x, 1), partner(d_sent_y, 2)
 
@@ -504,35 +481,54 @@
         cost_estimate=LONG,
     )(*in_hbm(*scalars), *all_grads, placed, near, *far)
 
+    (c_third,) = last_parts((after(c_kept[0], d_sent_x), c_kept[1]), (c_second_x, c_second_y))
+    c_last = relay(c_third, 4)
+
     def third_kernel(_, *refs):
-        lowrank_ref, whole_ref = refs[4], refs[9]
+        lowrank_ref, next_ref = refs[4], refs[9]
         for way in range(2):
             kept_ref, got_ref, sent_ref, rest_ref = refs[way], refs[2 + way], refs[5 + way], refs[7 + way]
             half = kept_ref.shape[0] // 2
-            sent_ref[...] = (kept_ref[half:, :] + got_ref[half : 2 * half, :].astype(F32)).astype(BF16)
+            sent_ref[:half, :] = (
+                kept_ref[half:, :] + got_ref[half : 2 * half, :].astype(F32)
+            ).astype(BF16)
             rest_ref[...] = kept_ref[:half, :] + got_ref[:half, :].astype(F32)
-            arrive(got_ref, 2 * half, way, lowrank_ref, whole_ref)
+            arrive(got_ref, 2 * half, way, lowrank_ref, next_ref)
+            ride(sent_ref, half, way, next_ref)
 
     d_sent_x, d_sent_y, *d_kept, lowrank = small(
         third_kernel,
-        [((half_rows, n), dtype) for dtype in (BF16, F32) for n in c_counts]
-        + [((rank, rows_total), BF16)],
+        [((half_rows + riding(way, n), n), BF16) for way, n in enumerate(d_counts)]
+        + [((half_rows, n), F32) for n in d_counts]
+        + [((rank, rows_total), F32)],
         d_kept_x,
-        after(d_kept_y, up_map_gradient, own_last),
+        after(d_kept_y, up_map_gradient, own_last, c_third),
         d_first_x,
         d_first_y,
         lowrank,
     )
-    d_second_x, d_second_y = partner(d_sent_x, 2), partner(d_sent_y, 4)
-    (c_third,) = last_parts((after(c_kept[0], d_sent_x), c_kept[1]), (c_second_x, c_second_y))
-    c_last = relay(c_third, 4)
+    d_second_x, d_second_y = partner(d_sent_x, 2), partner(d_sent_y, 1)
+    (d_third,) = last_parts(d_kept, (d_second_x, d_second_y))
+    d_last = relay(d_third, 4)
+
+    def whole_kernel(_, lowrank_ref, got_x_ref, got_y_ref, out_ref):
+        for way, got_ref in enumerate((got_x_ref, got_y_ref)):
+            arrive(got_ref, half_rows, way, lowrank_ref, out_ref)
+
+    (lowrank,) = small(
+        whole_kernel,
+        [((rank, rows_total), BF16)],
+        after(lowrank, d_third),
+        d_second_x,
+        d_second_y,
+    )
 
     down = adapter_down_maps[0]
 
-    def adapter_kernel(first, with_last, groups, *refs):
+    def adapter_kernel(groups, *refs):
         pos_ref, classes_ref, _, down_ref, lowrank_ref = refs[:5]
         sum_refs = refs[5 : 5 + 2 * groups]
-        *last_refs, out_ref, total_ref = refs[5 + 2 * groups :]
+        out_ref, total_ref = refs[5 + 2 * groups :]
         own = pos_ref[0] // low_size
         start = 0
         for g in range(groups):
@@ -541,42 +537,38 @@
             total_ref[:, start : start + count] = (
                 kept_ref[:half, :] + second_ref[:half, :].astype(F32)
             )
-            if with_last:
-                last_refs[g][...] = (
-                    kept_ref[half:, :] + second_ref[half : 2 * half, :].astype(F32)
-                ).astype(BF16)
             start += count
         for at in range(start // size):
-            piece = order[first + at]
+            piece = order[at]
             seg = segment_of(own, piece, tile_rows)
             rows = slice(at * size, (at + 1) * size)
-            columns = slice((first + at) * size, (first + at + 1) * size)
             adapter = lax.dot_general(
                 down_ref[classes_ref[piece[1], seg]],
-                lowrank_ref[:, columns],
+                lowrank_ref[:, rows],
                 TN,
                 preferred_element_type=F32,
             )
             out_ref[:, rows] = (total_ref[:, rows] + adapter).astype(BF16)
 
-    def with_adapter(sums, first, with_last, cost):
-        counts = [kept.shape[1] for kept, _ in sums]
-        shapes = [(portion, n) for n in counts] * with_last + [(portion, sum(counts))]
-        outs = pl.pallas_call(
-            functools.partial(adapter_kernel, first, with_last, len(sums)),
-            in_specs=[SMEM] * 3 + [VMEM] * (2 + 2 * len(sums)),
-            out_specs=[VMEM] * len(shapes),
-            out_shape=[jax.ShapeDtypeStruct(shape, BF16) for shape in shapes],
-            scratch_shapes=[pltpu.VMEM(shapes[-1], F32)],
-            compiler_params=PARAMS,
-            cost_estimate=cost,
-        )(*in_hbm(*scalars, down), lowrank, *[a for two in sums for a in two])
-        return outs[:-1], outs[-1]
-
-    def finish_kernel(first, groups, *refs):
-        pos_ref, kept_ref = refs[:2]
-        got_refs = refs[2 : 2 + groups]
-        out_ref, total_ref, turned_ref, sem = refs[-4:]
+    sums = own_sums + (
+        (c_kept[0], c_second_x),
+        (c_kept[1], c_second_y),
+        (d_kept[0], d_second_x),
+        (d_kept[1], d_second_y),
+    )
+    kept = pl.pallas_call(
+        functools.partial(adapter_kernel, len(sums)),
+        in_specs=[SMEM] * 3 + [VMEM] * (2 + 2 * len(sums)),
+        out_specs=VMEM,
+        out_shape=jax.ShapeDtypeStruct((portion, rows_total), BF16),
+        scratch_shapes=[pltpu.VMEM((portion, rows_total), F32)],
+        compiler_params=PARAMS,
+        cost_estimate=QUICK,
+    )(*in_hbm(*scalars, down), lowrank, *[a for two in sums for a in two])
+    kept = relay(kept, 0)
+
+    def finish_kernel(pos_ref, kept_ref, *refs):
+        *got_refs, out_ref, total_ref, turned_ref, sem = refs
         own = pos_ref[0] // low_size
         start = 0
         for got_ref in got_refs:
@@ -587,7 +579,7 @@
             start += count
         copies = []
         for at in range(start // size):
-            k, m, offset = order[first + at]
+            k, m, offset = order[at]
             base = pl.multiple_of((own ^ k) * tile_rows + offset, size)
             rows = slice(at * size, (at + 1) * size)
             turned_ref[rows, :] = total_ref[:, rows].T
@@ -600,25 +592,20 @@
         for copy in copies:
             copy.wait()
 
-    def finish(kept, got, first, result):
-        rows = kept.shape[1]
-        shape = jax.ShapeDtypeStruct((micro_count, high_size * tile_rows, portion), BF16)
-        hbm = pl.BlockSpec(memory_space=pltpu.HBM)
-        before = [] if result is None else [result]
-        return pl.pallas_call(
-            functools.partial(finish_kernel, first, len(got)),
-            in_specs=[SMEM] + [VMEM] * (1 + len(got)) + [hbm] * len(before),
-            out_specs=hbm,
-            out_shape=shape,
-            input_output_aliases={2 + len(got): 0} if before else {},
-            scratch_shapes=[
-                pltpu.VMEM((portion, rows), BF16),
-                pltpu.VMEM((rows, portion), BF16),
-                pltpu.SemaphoreType.DMA((rows // size,)),
-            ],
-            compiler_params=PARAMS,
-            cost_estimate=QUICK,
-        )(*in_hbm(scalars[0]), kept, *got, *before)
+    got = [own_last, c_last, d_last]
+    grad_prev = pl.pallas_call(
+        finish_kernel,
+        in_specs=[SMEM] + [VMEM] * (1 + len(got)),
+        out_specs=pl.BlockSpec(memory_space=pltpu.HBM),
+        out_shape=jax.ShapeDtypeStruct((micro_count, high_size * tile_rows, portion), BF16),
+        scratch_shapes=[
+            pltpu.VMEM((portion, rows_total), BF16),
+            pltpu.VMEM((rows_total, portion), BF16),
+            pltpu.SemaphoreType.DMA((rows_total // size,)),
+        ],
+        compiler_params=PARAMS,
+        cost_estimate=QUICK,
+    )(*in_hbm(scalars[0]), kept, *got)
 
     def down_kernel(pos_ref, classes_ref, live_ref, inputs_ref, lowrank_ref, out_ref, total_ref):
         own = pos_ref[0] // low_size
@@ -647,16 +634,6 @@
         compiler_params=PARAMS,
         cost_estimate=LONG,
     )(*in_hbm(*scalars, forward_input[0]), lowrank)
-
-    c_sums = (after(c_kept[0], c_third, down_map_gradient), c_second_x), (c_kept[1], c_second_y)
-    _, kept = with_adapter(own_sums + c_sums, 0, False, QUICK)
-    early = relay(kept, 0)
-    d_sums = (after(d_kept[0], kept), d_second_x), (d_kept[1], d_second_y)
-    d_lasts, d_kept = with_adapter(d_sums, kept.shape[1] // size, True, QUICK)
-    d_last = [relay(d_lasts[0], 4), relay(d_lasts[1], 1)]
-    d_kept = relay(d_kept, 0)
-    grad_prev = finish(early, [own_last, c_last], 0, None)
-    grad_prev = finish(d_kept, d_last, kept.shape[1] // size, grad_prev)
 
     return (
         grad_prev[None],

time: 117 us -> 106 us (0.906)
  waiting for transfers between devices: 54.8 us -> 42.6 us
  starting transfers between devices: 25 us -> 28.5 us
  Pallas kernels: 35 us -> 32.6 us
    ppermute x17, waiting for transfers between devices: 47.9 us -> 35.7 us  [partner(): return lax.ppermute(value, 'tensor', pairs)]
    ppermute x6 -> x4, starting transfers between devices: 2.27 us -> 4.94 us  [relay(): return lax.ppermute(value, ('pipe', 'tensor'), pairs)]
    pallas_call x4 -> x2, Pallas kernels: 4.73 us -> 2.85 us  [the longest x1 1.57 us: shards(): pl.pallas_call(functools.partial(adapter_kernel, len(sums)), in_specs=[SM...]
    ppermute x6 -> x4, waiting for transfers between devices: 6.95 us -> 6.81 us  [relay(): return lax.ppermute(value, ('pipe', 'tensor'), pairs)]
  transfers between devices with their start and end apart: 23 -> 21, of which waited for: 15 -> 10; matrix products, arithmetic and copies ran while one was open for 0% -> 0% of each run, Pallas kernels for 25% -> 29%
where the time goes in v14:
time: 106 us
  waiting for transfers between devices  42.6 us (40%)
  Pallas kernels  32.6 us (31%)
  starting transfers between devices  28.5 us (27%)
  local copies, waits for them, and re-layouts  1.27 us (1%)
    ppermute x17, waiting for transfers between devices, partner(): return lax.ppermute(value, 'tensor', pairs)  35.7 us
    ppermute x17, starting transfers between devices, partner(): return lax.ppermute(value, 'tensor', pairs)  23.5 us
    pallas_call x4, Pallas kernels, product(): pl.pallas_call(functools.partial(product_body, low_size, tile_rows, piece...  23.3 us
    ppermute x4, waiting for transfers between devices, relay(): return lax.ppermute(value, ('pipe', 'tensor'), pairs)  6.81 us
    ppermute x4, starting transfers between devices, relay(): return lax.ppermute(value, ('pipe', 'tensor'), pairs)  4.94 us
    pallas_call x1, Pallas kernels, shards(): pl.pallas_call(down_kernel, in_specs=[SMEM] * 3 + [VMEM] * 2, out_specs=V...  2.87 us
    pallas_call x1, Pallas kernels, shards(): pl.pallas_call(functools.partial(up_body, low_size, tile_rows, all_pieces...  2.42 us
  transfers between devices with their start and end apart: 21, of which 10 were waited for; matrix products, arithmetic and copies ran while one was open for 0% of the time, Pallas kernels for 29%

profile of v14, /device:TPU:0, one launch (start us, length us, event | category | flops | bytes accessed | tf_op | source)
XLA Modules:
  0.0 105.7 jit_solution(7462885835488838375)
XLA Ops:
  0.6 1.3 %slice_bitcast_fusion = (bf16[256,1024]{1,0:T(8,128)(2,1)S(1)}, bf16[256,1024]{1,0:T(8,128)(2,1)S(1)}) fusion(bf16[1,1,2,256,1024]{4,3,2,1,0:T(8,128)(2,1)} %param.8), kind=kLoop, calls=%fused_computation | loop fusion | bytes 2097152 | tf_op jit(solution)/shard_map/squeeze | solution.py:317
  1.9 4.1 %collective-permute-start = (bf16[256,1024]{1,0:T(8,128)(2,1)S(1)}, bf16[256,1024]{1,0:T(8,128)(2,1)S(1)}, u32[]{:S(2)}, u32[]{:S(2)}) collective-permute-start(bf16[256,1024]{1,0:T(8,128)(2,1)S(1)} %get-tuple-element.107), channel_id=1, source_target_pairs={{0,8},{1,9},{2,10},{3,11},{4,12},{5,13},{6,14},{7,15},{8,0},{9,1},... | collective-permute-start | bytes 1572872 | tf_op jit(solution)/shard_map/ppermute | solution.py:24
  6.0 5.7 %shard_map.104 = (bf16[2176,256]{1,0:T(8,128)(2,1)S(1)}, bf16[2048,256]{1,0:T(8,128)(2,1)S(1)}, bf16[128,256]{1,0:T(8,128)(2,1)S(1)}) custom-call(s32[1]{0:T(128)} %bitcast.refs_0_.pos_ref._, s32[2,4]{1,0:T(2,128)} %bitcast.35, s32[2]{0:T(128)} %bitcast.42, bf16[2,256,1024]{2,1,0:T(8,128)(2,1)} %bitcast.18, bf16[8,512,1024]{2,1,0:T(8,128)(2,1)} %bitcast.25, ...), custom_call_target="tpu_custom_call" | custom-call | flops 1000 | bytes 1000 | tf_op jit(solution)/shard_map/pallas_call | solution.py:141
  11.7 1.6 %collective-permute-start.2 = (bf16[2176,256]{1,0:T(8,128)(2,1)S(1)}, bf16[2176,256]{1,0:T(8,128)(2,1)S(1)}, u32[]{:S(2)}, u32[]{:S(2)}) collective-permute-start(bf16[2176,256]{1,0:T(8,128)(2,1)S(1)} %get-tuple-element.62), channel_id=1, source_target_pairs={{0,1},{1,0},{2,3},{3,2},{4,5},{5,4},{6,7},{7,6},{8,9},{9,8},{10,11... | collective-permute-start | bytes 3342344 | tf_op jit(solution)/shard_map/ppermute | solution.py:24
  13.3 1.5 %collective-permute-start.3 = (bf16[2048,256]{1,0:T(8,128)(2,1)S(1)}, bf16[2048,256]{1,0:T(8,128)(2,1)S(1)}, u32[]{:S(2)}, u32[]{:S(2)}) collective-permute-start(bf16[2048,256]{1,0:T(8,128)(2,1)S(1)} %get-tuple-element.63), channel_id=1, source_target_pairs={{0,2},{1,3},{2,0},{3,1},{4,6},{5,7},{6,4},{7,5},{8,10},{9,11},{10,... | collective-permute-start | bytes 3145736 | tf_op jit(solution)/shard_map/ppermute | solution.py:24
  14.8 5.8 %shard_map.105 = (f32[2048,256]{1,0:T(8,128)S(1)}, f32[2048,256]{1,0:T(8,128)S(1)}, f32[32,512]{1,0:T(8,128)S(1)}) custom-call(s32[1]{0:T(128)} %bitcast.refs_0_.pos_ref._, s32[2,4]{1,0:T(2,128)} %bitcast.36, s32[2]{0:T(128)} %bitcast.43, bf16[2,256,1024]{2,1,0:T(8,128)(2,1)} %bitcast.19, bf16[8,512,1024]{2,1,0:T(8,128)(2,1)} %bitcast.26, ...), custom_call_target="tpu_custom_call" | custom-call | flops 1000 | bytes 1000 | tf_op jit(solution)/shard_map/pallas_call | solution.py:141
  20.7 8.5 %collective-permute-done = bf16[256,1024]{1,0:T(8,128)(2,1)S(1)} collective-permute-done((bf16[256,1024]{1,0:T(8,128)(2,1)S(1)}, bf16[256,1024]{1,0:T(8,128)(2,1)S(1)}, u32[]{:S(2)}, u32[]{:S(2)}) %collective-permute-start) | collective-permute-done | bytes 524320 | tf_op jit(solution)/shard_map/ppermute | solution.py:24
  29.2 0.0 collective-permute-start.1
  29.2 5.9 %shard_map.106 = (bf16[2048,128]{1,0:T(8,128)(2,1)S(1)}, bf16[2048,128]{1,0:T(8,128)(2,1)S(1)}, f32[2048,128]{1,0:T(8,128)S(1)}, f32[2048,128]{1,0:T(8,128)S(1)}, f32[32,256]{1,0:T(8,128)S(1)}) custom-call(s32[1]{0:T(128)} %bitcast.refs_0_.pos_ref._, s32[2,4]{1,0:T(2,128)} %bitcast.37, s32[2]{0:T(128)} %bitcast.44, bf16[1,256,1024]{2,1,0:T(8,128)(2,1)S(1)} %bitcast.21, ...), custom_call_target="tpu_custom_call" | custom-call | flops 40000000000 | bytes 1000 | tf_op jit(solution)/shard_map/pallas_call | solution.py:141
  35.0 2.6 %collective-permute-done.3.refs_3_ = bf16[2048,256]{1,0:T(8,128)(2,1)S(1)} collective-permute-done((bf16[2048,256]{1,0:T(8,128)(2,1)S(1)}, bf16[2048,256]{1,0:T(8,128)(2,1)S(1)}, u32[]{:S(2)}, u32[]{:S(2)}) %collective-permute-start.3) | collective-permute-done | bytes 1048608 | tf_op jit(solution)/shard_map/ppermute | solution.py:24
  37.6 0.2 collective-permute-done.2.refs_2_
  37.8 0.3 shard_map.107
  38.2 1.6 %collective-permute-start.4 = (bf16[1152,256]{1,0:T(8,128)(2,1)S(1)}, bf16[1152,256]{1,0:T(8,128)(2,1)S(1)}, u32[]{:S(2)}, u32[]{:S(2)}) collective-permute-start(bf16[1152,256]{1,0:T(8,128)(2,1)S(1)} %get-tuple-element.76), channel_id=1, source_target_pairs={{0,2},{1,3},{2,0},{3,1},{4,6},{5,7},{6,4},{7,5},{8,10},{9,11},{10,... | collective-permute-start | bytes 1769480 | tf_op jit(solution)/shard_map/ppermute | solution.py:24
  39.8 1.5 %collective-permute-start.5 = (bf16[1024,256]{1,0:T(8,128)(2,1)S(1)}, bf16[1024,256]{1,0:T(8,128)(2,1)S(1)}, u32[]{:S(2)}, u32[]{:S(2)}) collective-permute-start(bf16[1024,256]{1,0:T(8,128)(2,1)S(1)} %get-tuple-element.77), channel_id=1, source_target_pairs={{0,1},{1,0},{2,3},{3,2},{4,5},{5,4},{6,7},{7,6},{8,9},{9,8},{10,11... | collective-permute-start | bytes 1572872 | tf_op jit(solution)/shard_map/ppermute | solution.py:24
  41.2 0.5 collective-permute-start.11
  41.7 0.5 collective-permute-start.10
  42.3 12.1 %collective-permute-done.1 = bf16[256,1024]{1,0:T(8,128)(2,1)S(1)} collective-permute-done((bf16[256,1024]{1,0:T(8,128)(2,1)S(1)}, bf16[256,1024]{1,0:T(8,128)(2,1)S(1)}, u32[]{:S(2)}, u32[]{:S(2)}) %collective-permute-start.1) | collective-permute-done | bytes 524320 | tf_op jit(solution)/shard_map/ppermute | solution.py:24
  54.4 5.9 %shard_map.103 = (bf16[2048,128]{1,0:T(8,128)(2,1)S(1)}, bf16[2048,128]{1,0:T(8,128)(2,1)S(1)}, f32[2048,128]{1,0:T(8,128)S(1)}, f32[2048,128]{1,0:T(8,128)S(1)}, f32[32,256]{1,0:T(8,128)S(1)}) custom-call(s32[1]{0:T(128)} %bitcast.refs_0_.pos_ref._, s32[2,4]{1,0:T(2,128)} %bitcast.38, s32[2]{0:T(128)} %bitcast.45, bf16[1,256,1024]{2,1,0:T(8,128)(2,1)S(1)} %bitcast.23, ...), custom_call_target="tpu_custom_call" | custom-call | flops 40000000000 | bytes 1000 | tf_op jit(solution)/shard_map/pallas_call | solution.py:141
  60.3 0.0 collective-permute-done.5.refs_3_.refs_8_
  60.3 0.0 collective-permute-done.4.refs_2_.refs_6_
  60.3 0.1 shard_map.108
  60.4 0.1 collective-permute-start.6
  60.5 1.7 %collective-permute-start.7 = (bf16[192,256]{1,0:T(8,128)(2,1)S(1)}, bf16[192,256]{1,0:T(8,128)(2,1)S(1)}, u32[]{:S(2)}, u32[]{:S(2)}) collective-permute-start(bf16[192,256]{1,0:T(8,128)(2,1)S(1)} %get-tuple-element.81), channel_id=1, source_target_pairs={{0,8},{1,9},{2,10},{3,11},{4,12},{5,13},{6,14},{7,15},{8,0},{9,1},... | collective-permute-start | bytes 294920 | tf_op jit(solution)/shard_map/ppermute | solution.py:24
  62.3 2.6 %collective-permute-start.8 = (bf16[192,256]{1,0:T(8,128)(2,1)S(1)}, bf16[192,256]{1,0:T(8,128)(2,1)S(1)}, u32[]{:S(2)}, u32[]{:S(2)}) collective-permute-start(bf16[192,256]{1,0:T(8,128)(2,1)S(1)} %get-tuple-element.81), channel_id=1, source_target_pairs={{0,12},{1,13},{2,14},{3,15},{4,8},{5,9},{6,10},{7,11},{8,4},{9,5},... | collective-permute-start | bytes 294920 | tf_op jit(solution)/shard_map/ppermute | solution.py:24
  64.9 0.0 collective-permute-done.11.refs_3_
  64.9 0.0 collective-permute-done.10.refs_2_
  64.9 0.0 copy-start
  64.9 0.2 shard_map.111
  65.1 1.3 %collective-permute-start.12 = (bf16[1024,128]{1,0:T(8,128)(2,1)S(1)}, bf16[1024,128]{1,0:T(8,128)(2,1)S(1)}, u32[]{:S(2)}, u32[]{:S(2)}) collective-permute-start(bf16[1024,128]{1,0:T(8,128)(2,1)S(1)} %get-tuple-element.97), channel_id=1, source_target_pairs={{0,2},{1,3},{2,0},{3,1},{4,6},{5,7},{6,4},{7,5},{8,10},{9,11},{10,... | collective-permute-start | bytes 786440 | tf_op jit(solution)/shard_map/ppermute | solution.py:24
  66.4 1.5 %collective-permute-start.13 = (bf16[1024,128]{1,0:T(8,128)(2,1)S(1)}, bf16[1024,128]{1,0:T(8,128)(2,1)S(1)}, u32[]{:S(2)}, u32[]{:S(2)}) collective-permute-start(bf16[1024,128]{1,0:T(8,128)(2,1)S(1)} %get-tuple-element.98), channel_id=1, source_target_pairs={{0,1},{1,0},{2,3},{3,2},{4,5},{5,4},{6,7},{7,6},{8,9},{9,8},{10,11... | collective-permute-start | bytes 786440 | tf_op jit(solution)/shard_map/ppermute | solution.py:24
  67.9 2.5 %collective-permute-done.7.refs_8_.refs_4_ = bf16[192,256]{1,0:T(8,128)(2,1)S(1)} collective-permute-done((bf16[192,256]{1,0:T(8,128)(2,1)S(1)}, bf16[192,256]{1,0:T(8,128)(2,1)S(1)}, u32[]{:S(2)}, u32[]{:S(2)}) %collective-permute-start.7) | collective-permute-done | bytes 98336 | tf_op jit(solution)/shard_map/ppermute | solution.py:24
  70.4 0.0 collective-permute-start.9
  70.4 0.0 collective-permute-done.8.refs_9_.refs_5_
  70.4 0.0 collective-permute-done.6.refs_7_.refs_3_
  70.5 0.1 shard_map.113
  70.6 1.3 %collective-permute-start.14 = (bf16[2304,128]{1,0:T(8,128)(2,1)S(1)}, bf16[2304,128]{1,0:T(8,128)(2,1)S(1)}, u32[]{:S(2)}, u32[]{:S(2)}) collective-permute-start(bf16[2304,128]{1,0:T(8,128)(2,1)S(1)} %get-tuple-element.95), channel_id=1, source_target_pairs={{0,1},{1,0},{2,3},{3,2},{4,5},{5,4},{6,7},{7,6},{8,9},{9,8},{10,11... | collective-permute-start | bytes 1769480 | tf_op jit(solution)/shard_map/ppermute | solution.py:24
  71.9 1.5 %collective-permute-start.15 = (bf16[2304,128]{1,0:T(8,128)(2,1)S(1)}, bf16[2304,128]{1,0:T(8,128)(2,1)S(1)}, u32[]{:S(2)}, u32[]{:S(2)}) collective-permute-start(bf16[2304,128]{1,0:T(8,128)(2,1)S(1)} %get-tuple-element.100), channel_id=1, source_target_pairs={{0,2},{1,3},{2,0},{3,1},{4,6},{5,7},{6,4},{7,5},{8,10},{9,11},{10,... | collective-permute-start | bytes 1769480 | tf_op jit(solution)/shard_map/ppermute | solution.py:24
  73.4 0.0 copy-done
  73.4 2.4 %shard_map.110 = bf16[8,32,1024]{2,1,0:T(8,128)(2,1)} custom-call(s32[1]{0:T(128)} %bitcast.refs_0_.pos_ref._, s32[2,4]{1,0:T(2,128)} %bitcast.39, s32[2]{0:T(128)} %bitcast.46, bf16[2,256,1024]{2,1,0:T(8,128)(2,1)S(1)} %bitcast.20, bf16[1,256,1024]{2,1,0:T(8,128)(2,1)S(1)} %bitcast.22, bf16[1,256,1024]{2,1,0:T(8,128)(2,1)S(1)} %bitcast.24, ...), custom_call_target="tpu_custom_call" | custom-call | flops 40000000000 | bytes 1000 | tf_op jit(solution)/shard_map/pallas_call | solution.py:472
  75.8 0.0 collective-permute-done.12.refs_2_.refs_10_
  75.8 0.0 collective-permute-done.13.refs_3_.refs_12_
  75.8 0.1 shard_map.114
  75.9 6.8 %collective-permute-done.9.refs_0_ = bf16[512,512]{1,0:T(8,128)(2,1)S(1)} collective-permute-done((bf16[512,512]{1,0:T(8,128)(2,1)S(1)}, bf16[512,512]{1,0:T(8,128)(2,1)S(1)}, u32[]{:S(2)}, u32[]{:S(2)}) %collective-permute-start.9) | collective-permute-done | bytes 524320 | tf_op jit(solution)/shard_map/ppermute | solution.py:34
  82.7 2.8 %collective-permute-done.14.refs_2_ = bf16[2304,128]{1,0:T(8,128)(2,1)S(1)} collective-permute-done((bf16[2304,128]{1,0:T(8,128)(2,1)S(1)}, bf16[2304,128]{1,0:T(8,128)(2,1)S(1)}, u32[]{:S(2)}, u32[]{:S(2)}) %collective-permute-start.14) | collective-permute-done | bytes 589856 | tf_op jit(solution)/shard_map/ppermute | solution.py:24
  85.5 1.0 collective-permute-done.15.refs_3_
  86.4 0.3 shard_map.115
  86.7 1.6 %collective-permute-start.16 = (bf16[1280,128]{1,0:T(8,128)(2,1)S(1)}, bf16[1280,128]{1,0:T(8,128)(2,1)S(1)}, u32[]{:S(2)}, u32[]{:S(2)}) collective-permute-start(bf16[1280,128]{1,0:T(8,128)(2,1)S(1)} %get-tuple-element.104), channel_id=1, source_target_pairs={{0,2},{1,3},{2,0},{3,1},{4,6},{5,7},{6,4},{7,5},{8,10},{9,11},{10,... | collective-permute-start | bytes 983048 | tf_op jit(solution)/shard_map/ppermute | solution.py:24
  88.3 0.6 collective-permute-start.17
  88.9 1.1 %collective-permute-start.19 = (bf16[512,256]{1,0:T(8,128)(2,1)S(1)}, bf16[512,256]{1,0:T(8,128)(2,1)S(1)}, u32[]{:S(2)}, u32[]{:S(2)}) collective-permute-start(bf16[512,256]{1,0:T(8,128)(2,1)S(1)} %shard_map.114), channel_id=1, source_target_pairs={{0,20},{1,21},{2,22},{3,23},{4,16},{5,17},{6,18},{7,19},{8,28},{9,... | collective-permute-start | bytes 786440 | tf_op jit(solution)/shard_map/ppermute | solution.py:34
  89.9 4.9 %collective-permute-done.16.refs_2_.got_x_ref.refs_14_ = bf16[1280,128]{1,0:T(8,128)(2,1)S(1)} collective-permute-done((bf16[1280,128]{1,0:T(8,128)(2,1)S(1)}, bf16[1280,128]{1,0:T(8,128)(2,1)S(1)}, u32[]{:S(2)}, u32[]{:S(2)}) %collective-permute-start.16) | collective-permute-done | bytes 327712 | tf_op jit(solution)/shard_map/ppermute | solution.py:24
  94.8 1.2 %collective-permute-done.17.refs_3_.got_y_ref.refs_16_ = bf16[1280,128]{1,0:T(8,128)(2,1)S(1)} collective-permute-done((bf16[1280,128]{1,0:T(8,128)(2,1)S(1)}, bf16[1280,128]{1,0:T(8,128)(2,1)S(1)}, u32[]{:S(2)}, u32[]{:S(2)}) %collective-permute-start.17) | collective-permute-done | bytes 327712 | tf_op jit(solution)/shard_map/ppermute | solution.py:24
  96.0 0.1 shard_map.116
  96.1 1.5 %collective-permute-start.20 = (bf16[512,256]{1,0:T(8,128)(2,1)S(1)}, bf16[512,256]{1,0:T(8,128)(2,1)S(1)}, u32[]{:S(2)}, u32[]{:S(2)}) collective-permute-start(bf16[512,256]{1,0:T(8,128)(2,1)S(1)} %shard_map.116), channel_id=1, source_target_pairs={{0,20},{1,21},{2,22},{3,23},{4,16},{5,17},{6,18},{7,19},{8,28},{9,... | collective-permute-start | bytes 786440 | tf_op jit(solution)/shard_map/ppermute | solution.py:34
  97.6 1.6 %shard_map.118 = bf16[512,1024]{1,0:T(8,128)(2,1)S(1)} custom-call(s32[1]{0:T(128)} %bitcast.refs_0_.pos_ref._, s32[2,4]{1,0:T(2,128)} %bitcast.40, s32[2]{0:T(128)} %bitcast.47, bf16[8,64,512]{2,1,0:T(8,128)(2,1)} %bitcast.30, bf16[64,1024]{1,0:T(8,128)(2,1)S(1)} %shard_map.117.refs_4_.lowrank_ref, f32[1024,256]{1,0:T(8,128)S(1)} %get-tuple-element.74.refs_0_.refs_5_, ...), custom_call_target="tpu_custom_call" | custom-call | flops 1000 | bytes 1000 | tf_op jit(solution)/shard_map/pallas_call | solution.py:559
  99.2 2.3 %collective-permute-start.18 = (bf16[512,1024]{1,0:T(8,128)(2,1)S(1)}, bf16[512,1024]{1,0:T(8,128)(2,1)S(1)}, u32[]{:S(2)}, u32[]{:S(2)}) collective-permute-start(bf16[512,1024]{1,0:T(8,128)(2,1)S(1)} %shard_map.118), channel_id=1, source_target_pairs={{0,16},{1,17},{2,18},{3,19},{4,20},{5,21},{6,22},{7,23},{8,24},{9,... | collective-permute-start | bytes 3145736 | tf_op jit(solution)/shard_map/ppermute | solution.py:34
  101.5 2.9 %shard_map.120 = bf16[8,64,512]{2,1,0:T(8,128)(2,1)} custom-call(s32[1]{0:T(128)} %bitcast.refs_0_.pos_ref._, s32[2,4]{1,0:T(2,128)} %bitcast.41, s32[2]{0:T(128)} %bitcast.48, bf16[2,512,512]{2,1,0:T(8,128)(2,1)} %bitcast.49, bf16[64,1024]{1,0:T(8,128)(2,1)S(1)} %shard_map.117.refs_4_.lowrank_ref), custom_call_target="tpu_custom_call" | custom-call | flops 40000000000 | bytes 1000 | tf_op jit(solution)/shard_map/pallas_call | solution.py:628
  104.4 0.0 collective-permute-done.19.refs_1_
  104.4 0.0 collective-permute-done.20.refs_2_
  104.4 0.0 collective-permute-done.18.kept_ref
  104.4 1.3 %shard_map.119 = bf16[2,512,512]{2,1,0:T(8,128)(2,1)} custom-call(s32[1]{0:T(128)} %bitcast.refs_0_.pos_ref._, bf16[512,1024]{1,0:T(8,128)(2,1)S(1)} %collective-permute-done.18.kept_ref, bf16[512,512]{1,0:T(8,128)(2,1)S(1)} %collective-permute-done.9.refs_0_, bf16[512,256]{1,0:T(8,128)(2,1)S(1)} %collective-permute-done.19.refs_1_, ...), custom_call_target="tpu_custom_call" | custom-call | flops 1000 | bytes 1000 | tf_op jit(solution)/shard_map/pallas_call | solution.py:596
  (3 shorter events, 0.1 us)
Async XLA Ops:
  1.9 27.3 %collective-permute-start = (bf16[256,1024]{1,0:T(8,128)(2,1)S(1)}, bf16[256,1024]{1,0:T(8,128)(2,1)S(1)}, u32[]{:S(2)}, u32[]{:S(2)}) collective-permute-start(bf16[256,1024]{1,0:T(8,128)(2,1)S(1)} %get-tuple-element.107), channel_id=1, source_target_pairs={{0,8},{1,9},{2,10},{3,11},{4,12},{5,13},{6,14},{7,15},{8,0},{9,1},... | collective-permute-start | bytes 1572872 | tf_op jit(solution)/shard_map/ppermute | solution.py:24
  11.7 26.1 %collective-permute-start.2 = (bf16[2176,256]{1,0:T(8,128)(2,1)S(1)}, bf16[2176,256]{1,0:T(8,128)(2,1)S(1)}, u32[]{:S(2)}, u32[]{:S(2)}) collective-permute-start(bf16[2176,256]{1,0:T(8,128)(2,1)S(1)} %get-tuple-element.62), channel_id=1, source_target_pairs={{0,1},{1,0},{2,3},{3,2},{4,5},{5,4},{6,7},{7,6},{8,9},{9,8},{10,11... | collective-permute-start | bytes 3342344 | tf_op jit(solution)/shard_map/ppermute | solution.py:24
  13.3 24.3 %collective-permute-start.3 = (bf16[2048,256]{1,0:T(8,128)(2,1)S(1)}, bf16[2048,256]{1,0:T(8,128)(2,1)S(1)}, u32[]{:S(2)}, u32[]{:S(2)}) collective-permute-start(bf16[2048,256]{1,0:T(8,128)(2,1)S(1)} %get-tuple-element.63), channel_id=1, source_target_pairs={{0,2},{1,3},{2,0},{3,1},{4,6},{5,7},{6,4},{7,5},{8,10},{9,11},{10,... | collective-permute-start | bytes 3145736 | tf_op jit(solution)/shard_map/ppermute | solution.py:24
  29.2 25.2 %collective-permute-start.1 = (bf16[256,1024]{1,0:T(8,128)(2,1)S(1)}, bf16[256,1024]{1,0:T(8,128)(2,1)S(1)}, u32[]{:S(2)}, u32[]{:S(2)}) collective-permute-start(bf16[256,1024]{1,0:T(8,128)(2,1)S(1)} %get-tuple-element.58), channel_id=1, source_target_pairs={{0,8},{1,9},{2,10},{3,11},{4,12},{5,13},{6,14},{7,15},{8,0},{9,1},... | collective-permute-start | bytes 1572872 | tf_op jit(solution)/shard_map/ppermute | solution.py:24
  38.2 22.1 %collective-permute-start.4 = (bf16[1152,256]{1,0:T(8,128)(2,1)S(1)}, bf16[1152,256]{1,0:T(8,128)(2,1)S(1)}, u32[]{:S(2)}, u32[]{:S(2)}) collective-permute-start(bf16[1152,256]{1,0:T(8,128)(2,1)S(1)} %get-tuple-element.76), channel_id=1, source_target_pairs={{0,2},{1,3},{2,0},{3,1},{4,6},{5,7},{6,4},{7,5},{8,10},{9,11},{10,... | collective-permute-start | bytes 1769480 | tf_op jit(solution)/shard_map/ppermute | solution.py:24
  39.8 20.5 %collective-permute-start.5 = (bf16[1024,256]{1,0:T(8,128)(2,1)S(1)}, bf16[1024,256]{1,0:T(8,128)(2,1)S(1)}, u32[]{:S(2)}, u32[]{:S(2)}) collective-permute-start(bf16[1024,256]{1,0:T(8,128)(2,1)S(1)} %get-tuple-element.77), channel_id=1, source_target_pairs={{0,1},{1,0},{2,3},{3,2},{4,5},{5,4},{6,7},{7,6},{8,9},{9,8},{10,11... | collective-permute-start | bytes 1572872 | tf_op jit(solution)/shard_map/ppermute | solution.py:24
  41.2 23.7 %collective-permute-start.11 = (bf16[2048,128]{1,0:T(8,128)(2,1)S(1)}, bf16[2048,128]{1,0:T(8,128)(2,1)S(1)}, u32[]{:S(2)}, u32[]{:S(2)}) collective-permute-start(bf16[2048,128]{1,0:T(8,128)(2,1)S(1)} %get-tuple-element.89), channel_id=1, source_target_pairs={{0,2},{1,3},{2,0},{3,1},{4,6},{5,7},{6,4},{7,5},{8,10},{9,11},{10,... | collective-permute-start | bytes 1572872 | tf_op jit(solution)/shard_map/ppermute | solution.py:24
  41.7 23.2 %collective-permute-start.10 = (bf16[2048,128]{1,0:T(8,128)(2,1)S(1)}, bf16[2048,128]{1,0:T(8,128)(2,1)S(1)}, u32[]{:S(2)}, u32[]{:S(2)}) collective-permute-start(bf16[2048,128]{1,0:T(8,128)(2,1)S(1)} %get-tuple-element.87), channel_id=1, source_target_pairs={{0,1},{1,0},{2,3},{3,2},{4,5},{5,4},{6,7},{7,6},{8,9},{9,8},{10,11... | collective-permute-start | bytes 1572872 | tf_op jit(solution)/shard_map/ppermute | solution.py:24
  60.4 10.0 %collective-permute-start.6 = (bf16[256,256]{1,0:T(8,128)(2,1)S(1)}, bf16[256,256]{1,0:T(8,128)(2,1)S(1)}, u32[]{:S(2)}, u32[]{:S(2)}) collective-permute-start(bf16[256,256]{1,0:T(8,128)(2,1)S(1)} %get-tuple-element.80), channel_id=1, source_target_pairs={{0,4},{1,5},{2,6},{3,7},{4,0},{5,1},{6,2},{7,3},{8,12},{9,13},{10,... | collective-permute-start | bytes 393224 | tf_op jit(solution)/shard_map/ppermute | solution.py:24
  60.5 9.9 %collective-permute-start.7 = (bf16[192,256]{1,0:T(8,128)(2,1)S(1)}, bf16[192,256]{1,0:T(8,128)(2,1)S(1)}, u32[]{:S(2)}, u32[]{:S(2)}) collective-permute-start(bf16[192,256]{1,0:T(8,128)(2,1)S(1)} %get-tuple-element.81), channel_id=1, source_target_pairs={{0,8},{1,9},{2,10},{3,11},{4,12},{5,13},{6,14},{7,15},{8,0},{9,1},... | collective-permute-start | bytes 294920 | tf_op jit(solution)/shard_map/ppermute | solution.py:24
  62.3 8.2 %collective-permute-start.8 = (bf16[192,256]{1,0:T(8,128)(2,1)S(1)}, bf16[192,256]{1,0:T(8,128)(2,1)S(1)}, u32[]{:S(2)}, u32[]{:S(2)}) collective-permute-start(bf16[192,256]{1,0:T(8,128)(2,1)S(1)} %get-tuple-element.81), channel_id=1, source_target_pairs={{0,12},{1,13},{2,14},{3,15},{4,8},{5,9},{6,10},{7,11},{8,4},{9,5},... | collective-permute-start | bytes 294920 | tf_op jit(solution)/shard_map/ppermute | solution.py:24
  64.9 8.5 %copy-start = (bf16[1,1,2,256,1024]{4,3,2,1,0:T(8,128)(2,1)S(1)}, bf16[1,1,2,256,1024]{4,3,2,1,0:T(8,128)(2,1)}, u32[]{:S(2)}) copy-start(bf16[1,1,2,256,1024]{4,3,2,1,0:T(8,128)(2,1)} %param.8) | copy-start | bytes 3145732
  65.1 10.7 %collective-permute-start.12 = (bf16[1024,128]{1,0:T(8,128)(2,1)S(1)}, bf16[1024,128]{1,0:T(8,128)(2,1)S(1)}, u32[]{:S(2)}, u32[]{:S(2)}) collective-permute-start(bf16[1024,128]{1,0:T(8,128)(2,1)S(1)} %get-tuple-element.97), channel_id=1, source_target_pairs={{0,2},{1,3},{2,0},{3,1},{4,6},{5,7},{6,4},{7,5},{8,10},{9,11},{10,... | collective-permute-start | bytes 786440 | tf_op jit(solution)/shard_map/ppermute | solution.py:24
  66.4 9.4 %collective-permute-start.13 = (bf16[1024,128]{1,0:T(8,128)(2,1)S(1)}, bf16[1024,128]{1,0:T(8,128)(2,1)S(1)}, u32[]{:S(2)}, u32[]{:S(2)}) collective-permute-start(bf16[1024,128]{1,0:T(8,128)(2,1)S(1)} %get-tuple-element.98), channel_id=1, source_target_pairs={{0,1},{1,0},{2,3},{3,2},{4,5},{5,4},{6,7},{7,6},{8,9},{9,8},{10,11... | collective-permute-start | bytes 786440 | tf_op jit(solution)/shard_map/ppermute | solution.py:24
  70.4 12.3 %collective-permute-start.9 = (bf16[512,512]{1,0:T(8,128)(2,1)S(1)}, bf16[512,512]{1,0:T(8,128)(2,1)S(1)}, u32[]{:S(2)}, u32[]{:S(2)}) collective-permute-start(bf16[512,512]{1,0:T(8,128)(2,1)S(1)} %get-tuple-element.82), channel_id=1, source_target_pairs={{0,20},{1,21},{2,22},{3,23},{4,16},{5,17},{6,18},{7,19},{8,28},{9,... | collective-permute-start | bytes 1572872 | tf_op jit(solution)/shard_map/ppermute | solution.py:34
  70.6 14.9 %collective-permute-start.14 = (bf16[2304,128]{1,0:T(8,128)(2,1)S(1)}, bf16[2304,128]{1,0:T(8,128)(2,1)S(1)}, u32[]{:S(2)}, u32[]{:S(2)}) collective-permute-start(bf16[2304,128]{1,0:T(8,128)(2,1)S(1)} %get-tuple-element.95), channel_id=1, source_target_pairs={{0,1},{1,0},{2,3},{3,2},{4,5},{5,4},{6,7},{7,6},{8,9},{9,8},{10,11... | collective-permute-start | bytes 1769480 | tf_op jit(solution)/shard_map/ppermute | solution.py:24
  71.9 14.6 %collective-permute-start.15 = (bf16[2304,128]{1,0:T(8,128)(2,1)S(1)}, bf16[2304,128]{1,0:T(8,128)(2,1)S(1)}, u32[]{:S(2)}, u32[]{:S(2)}) collective-permute-start(bf16[2304,128]{1,0:T(8,128)(2,1)S(1)} %get-tuple-element.100), channel_id=1, source_target_pairs={{0,2},{1,3},{2,0},{3,1},{4,6},{5,7},{6,4},{7,5},{8,10},{9,11},{10,... | collective-permute-start | bytes 1769480 | tf_op jit(solution)/shard_map/ppermute | solution.py:24
  86.7 8.1 %collective-permute-start.16 = (bf16[1280,128]{1,0:T(8,128)(2,1)S(1)}, bf16[1280,128]{1,0:T(8,128)(2,1)S(1)}, u32[]{:S(2)}, u32[]{:S(2)}) collective-permute-start(bf16[1280,128]{1,0:T(8,128)(2,1)S(1)} %get-tuple-element.104), channel_id=1, source_target_pairs={{0,2},{1,3},{2,0},{3,1},{4,6},{5,7},{6,4},{7,5},{8,10},{9,11},{10,... | collective-permute-start | bytes 983048 | tf_op jit(solution)/shard_map/ppermute | solution.py:24
  88.3 7.7 %collective-permute-start.17 = (bf16[1280,128]{1,0:T(8,128)(2,1)S(1)}, bf16[1280,128]{1,0:T(8,128)(2,1)S(1)}, u32[]{:S(2)}, u32[]{:S(2)}) collective-permute-start(bf16[1280,128]{1,0:T(8,128)(2,1)S(1)} %get-tuple-element.105), channel_id=1, source_target_pairs={{0,1},{1,0},{2,3},{3,2},{4,5},{5,4},{6,7},{7,6},{8,9},{9,8},{10,11... | collective-permute-start | bytes 983048 | tf_op jit(solution)/shard_map/ppermute | solution.py:24
  88.9 15.6 %collective-permute-start.19 = (bf16[512,256]{1,0:T(8,128)(2,1)S(1)}, bf16[512,256]{1,0:T(8,128)(2,1)S(1)}, u32[]{:S(2)}, u32[]{:S(2)}) collective-permute-start(bf16[512,256]{1,0:T(8,128)(2,1)S(1)} %shard_map.114), channel_id=1, source_target_pairs={{0,20},{1,21},{2,22},{3,23},{4,16},{5,17},{6,18},{7,19},{8,28},{9,... | collective-permute-start | bytes 786440 | tf_op jit(solution)/shard_map/ppermute | solution.py:34
  96.1 8.3 %collective-permute-start.20 = (bf16[512,256]{1,0:T(8,128)(2,1)S(1)}, bf16[512,256]{1,0:T(8,128)(2,1)S(1)}, u32[]{:S(2)}, u32[]{:S(2)}) collective-permute-start(bf16[512,256]{1,0:T(8,128)(2,1)S(1)} %shard_map.116), channel_id=1, source_target_pairs={{0,20},{1,21},{2,22},{3,23},{4,16},{5,17},{6,18},{7,19},{8,28},{9,... | collective-permute-start | bytes 786440 | tf_op jit(solution)/shard_map/ppermute | solution.py:34
  99.2 5.2 %collective-permute-start.18 = (bf16[512,1024]{1,0:T(8,128)(2,1)S(1)}, bf16[512,1024]{1,0:T(8,128)(2,1)S(1)}, u32[]{:S(2)}, u32[]{:S(2)}) collective-permute-start(bf16[512,1024]{1,0:T(8,128)(2,1)S(1)} %shard_map.118), channel_id=1, source_target_pairs={{0,16},{1,17},{2,18},{3,19},{4,20},{5,21},{6,22},{7,23},{8,24},{9,... | collective-permute-start | bytes 3145736 | tf_op jit(solution)/shard_map/ppermute | solution.py:34

commit v15 on v14

--- a/solution.py
+++ b/solution.py
@@ -39,12 +39,13 @@
     return ((high ^ k) * tile_rows + offset) // SEG
 
 
-def product_body(low_size, tile_rows, pieces, tiles, half, turns, sends, keeps, with_hidden, *refs):
+def product_body(low_size, tile_rows, pieces, tiles, half, turns, sends, keeps, with_hidden, fetches, *refs):
     pos_ref, classes_ref, live_ref = refs[:3]
     grad_refs = refs[3 : 3 + tiles]
     weight_hbm = refs[3 + tiles]
-    rows_ref, weight_ref, sems = refs[-3:]
-    rest = list(refs[4 + tiles : -3])
+    rows_ref, *scratch = refs[-3:] if fetches else refs[-1:]
+    rest = list(refs[4 + tiles : -1 - len(scratch)])
+    weight_ref, sems = scratch if fetches else (weight_hbm, None)
     up_ref = rest.pop(0) if keeps else None
     hidden_ref = rest.pop(0) if with_hidden else None
     sent_x, sent_y = (rest.pop(0), rest.pop(0)) if sends else (None, None)
@@ -61,15 +62,16 @@
 
     jobs = []
     for x, y in ((1, 1), (1, 0), (0, 1), (0, 0)):
-        to_x = (sent_x if x else kept_x, 2 * y, 1)
+        to_x = (sent_x if x else kept_x, *((y, 2) if turns else (2 * y, 1)))
         to_y = (sent_y if y else kept_y, *((x, 2) if turns else (2 * x, 1)))
         start = 0 if to_x[0] is not None else half
         stop = total if to_y[0] is not None else half
         if start < stop:
             jobs.append((x + 2 * y, start, stop, to_x, to_y))
-    for block, *_ in jobs:
-        for z in range(2):
-            weight_copy(block + 4 * z).start()
+    if fetches:
+        for block, *_ in jobs:
+            for z in range(2):
+                weight_copy(block + 4 * z).start()
 
     if with_hidden:
         micro_count, count, rank = hidden_ref.shape
@@ -107,7 +109,8 @@
 
         @pl.loop(0, 2)
         def _(z):
-            weight_copy(block + 4 * z).wait()
+            if fetches:
+                weight_copy(block + 4 * z).wait()
             value = jnp.dot(
                 weight_ref[block + 4 * z], rows_ref[:, start:stop], preferred_element_type=F32
             )
@@ -121,7 +124,7 @@
                     ref[place, :] = part.astype(ref.dtype)
 
 
-def product(scalars, grads, pieces, tile_rows, weight_blocks, up_tile, low_size, turns, sends, keeps, cost, size, hidden=None):
+def product(scalars, grads, pieces, tile_rows, weight_blocks, up_tile, low_size, turns, sends, keeps, cost, size, hidden=None, fetched=None):
     blocks, width, depth = weight_blocks.shape
     rows = len(pieces) * size
     half = rows // 2
@@ -140,22 +143,51 @@
     more = ([up_tile] if keeps else []) + ([] if hidden is None else [hidden])
     return pl.pallas_call(
         functools.partial(
-            product_body, low_size, tile_rows, pieces, len(grads), half, turns, sends, keeps, extra > 0
+            product_body, low_size, tile_rows, pieces, len(grads), half, turns, sends, keeps, extra > 0,
+            fetched is None,
         ),
         in_specs=[SMEM] * 3
         + [VMEM] * len(grads)
-        + [pl.BlockSpec(memory_space=pltpu.HBM)]
+        + [pl.BlockSpec(memory_space=pltpu.HBM) if fetched is None else VMEM]
         + [VMEM] * len(more),
         out_specs=[VMEM] * len(outs),
         out_shape=outs,
-        scratch_shapes=[
-            pltpu.VMEM((depth, rows), BF16),
-            pltpu.VMEM(weight_blocks.shape, BF16),
-            pltpu.SemaphoreType.DMA((blocks,)),
-        ],
+        scratch_shapes=[pltpu.VMEM((depth, rows), BF16)]
+        + [pltpu.VMEM(weight_blocks.shape, BF16), pltpu.SemaphoreType.DMA((blocks,))]
+        * (fetched is None),
         compiler_params=PRODUCT_PARAMS,
         cost_estimate=cost,
-    )(*in_hbm(*scalars), *grads, *in_hbm(weight_blocks, *more))
+    )(
+        *in_hbm(*scalars),
+        *grads,
+        *(in_hbm(weight_blocks) if fetched is None else [fetched]),
+        *in_hbm(*more),
+    )
+
+
+def fetch_kernel(low_size, pos_ref, weight_ref, out_ref, sems):
+    copies = [
+        pltpu.make_async_copy(
+            weight_ref.at[block ^ (pos_ref[0] % low_size)], out_ref.at[block], sems.at[block]
+        )
+        for block in range(low_size)
+    ]
+    for copy in copies:
+        copy.start()
+    for copy in copies:
+        copy.wait()
+
+
+def fetch(position, weight_blocks, low_size):
+    return pl.pallas_call(
+        functools.partial(fetch_kernel, low_size),
+        in_specs=[SMEM, pl.BlockSpec(memory_space=pltpu.HBM)],
+        out_specs=VMEM,
+        out_shape=pltpu.VMEM(weight_blocks.shape, BF16),
+        scratch_shapes=[pltpu.SemaphoreType.DMA((low_size,))],
+        compiler_params=PARAMS,
+        cost_estimate=QUICK,
+    )(*in_hbm(position, weight_blocks))
 
 
 def in_hbm(*arrays):
@@ -306,10 +338,10 @@
             for o in offsets
         ]
 
-    def produce(grads, pieces, turns, sends, keeps, cost, hidden=None):
+    def produce(grads, pieces, turns, sends, keeps, cost, hidden=None, fetched=None):
         return product(
             scalars, grads, pieces, tile_rows, weight_blocks, up_tile, low_size, turns, sends, keeps,
-            cost, size, hidden,
+            cost, size, hidden, fetched,
         )
 
     hidden = saved_rank_outputs[0]
@@ -337,10 +369,12 @@
     c_first_x = partner(after(c_sent_x, sent_x, sent_y), 1)
     c_first_y = partner(after(c_sent_y, sent_x, sent_y), 2)
 
+    fetched = fetch(after(scalars[0], sent_x, sent_y), weight_blocks, low_size)
+
     chunks = [([grad_tile], own_pieces), (got0, pieces_of(0)), (got1, pieces_of(1))]
     order = [piece for _, pieces in chunks for _, _, piece, _ in pieces]
     d_sent_x, d_sent_y, d_kept_x, d_kept_y, part = produce(
-        got1, pieces_of(1), False, True, True, LONG
+        got1, pieces_of(1), False, True, True, LONG, None, fetched
     )
     parts.append(part)
     own_third, placed = last_parts((after(kept_x, part), kept_y), (second_x, second_y), placed)

time: 106 us -> 105 us (level)
  starting transfers between devices: 28.5 us -> 21.7 us
  waiting for transfers between devices: 42.6 us -> 46.3 us
  Pallas kernels: 32.6 us -> 35.1 us
    ppermute x4, starting transfers between devices: 4.94 us -> 0.85 us  [relay(): return lax.ppermute(value, ('pipe', 'tensor'), pairs)]
    ppermute x17, waiting for transfers between devices: 35.7 us -> 39.2 us  [partner(): return lax.ppermute(value, 'tensor', pairs)]
    pallas_call x0 -> x1, Pallas kernels: none -> 3.47 us  [fetch(): pl.pallas_call(functools.partial(fetch_kernel, low_size), in_specs=[SMEM,...]
    ppermute x17, starting transfers between devices: 23.5 us -> 20.8 us  [partner(): return lax.ppermute(value, 'tensor', pairs)]
  transfers between devices with their start and end apart: 21 -> 21, of which waited for: 10 -> 13; matrix products, arithmetic and copies ran while one was open for 0% -> 0% of each run, Pallas kernels for 29% -> 32%
where the time goes in v15:
time: 105 us
  waiting for transfers between devices  46.3 us (44%)
  Pallas kernels  35.1 us (33%)
  starting transfers between devices  21.7 us (21%)
  local copies, waits for them, and re-layouts  1.27 us (1%)
    ppermute x17, waiting for transfers between devices, partner(): return lax.ppermute(value, 'tensor', pairs)  39.2 us
    pallas_call x4, Pallas kernels, product(): pl.pallas_call(functools.partial(product_body, low_size, tile_rows, piece...  22.3 us
    ppermute x17, starting transfers between devices, partner(): return lax.ppermute(value, 'tensor', pairs)  20.8 us
    ppermute x4, waiting for transfers between devices, relay(): return lax.ppermute(value, ('pipe', 'tensor'), pairs)  7.09 us
    pallas_call x1, Pallas kernels, fetch(): pl.pallas_call(functools.partial(fetch_kernel, low_size), in_specs=[SMEM,...  3.47 us
    pallas_call x1, Pallas kernels, shards(): pl.pallas_call(down_kernel, in_specs=[SMEM] * 3 + [VMEM] * 2, out_specs=V...  2.88 us
    pallas_call x1, Pallas kernels, shards(): pl.pallas_call(functools.partial(up_body, low_size, tile_rows, all_pieces...  2.42 us
  transfers between devices with their start and end apart: 21, of which 13 were waited for; matrix products, arithmetic and copies ran while one was open for 0% of the time, Pallas kernels for 32%

profile of v15, /device:TPU:0, one launch (start us, length us, event | category | flops | bytes accessed | tf_op | source)
XLA Modules:
  0.0 105.1 jit_solution(8791856907105527541)
XLA Ops:
  0.6 1.3 %slice_bitcast_fusion = (bf16[256,1024]{1,0:T(8,128)(2,1)S(1)}, bf16[256,1024]{1,0:T(8,128)(2,1)S(1)}) fusion(bf16[1,1,2,256,1024]{4,3,2,1,0:T(8,128)(2,1)} %param.8), kind=kLoop, calls=%fused_computation | loop fusion | bytes 2097152 | tf_op jit(solution)/shard_map/squeeze | solution.py:349
  1.9 4.1 %collective-permute-start = (bf16[256,1024]{1,0:T(8,128)(2,1)S(1)}, bf16[256,1024]{1,0:T(8,128)(2,1)S(1)}, u32[]{:S(2)}, u32[]{:S(2)}) collective-permute-start(bf16[256,1024]{1,0:T(8,128)(2,1)S(1)} %get-tuple-element.109), channel_id=1, source_target_pairs={{0,8},{1,9},{2,10},{3,11},{4,12},{5,13},{6,14},{7,15},{8,0},{9,1},... | collective-permute-start | bytes 1572872 | tf_op jit(solution)/shard_map/ppermute | solution.py:24
  6.0 5.7 %shard_map.103 = (bf16[2176,256]{1,0:T(8,128)(2,1)S(1)}, bf16[2048,256]{1,0:T(8,128)(2,1)S(1)}, bf16[128,256]{1,0:T(8,128)(2,1)S(1)}) custom-call(s32[1]{0:T(128)} %bitcast.refs_0_.pos_ref._, s32[2,4]{1,0:T(2,128)} %bitcast.35, s32[2]{0:T(128)} %bitcast.42, bf16[2,256,1024]{2,1,0:T(8,128)(2,1)} %bitcast.18, bf16[8,512,1024]{2,1,0:T(8,128)(2,1)} %bitcast.25, ...), custom_call_target="tpu_custom_call" | custom-call | flops 1000 | bytes 1000 | tf_op jit(solution)/shard_map/pallas_call | solution.py:144
  11.7 1.6 %collective-permute-start.3 = (bf16[2048,256]{1,0:T(8,128)(2,1)S(1)}, bf16[2048,256]{1,0:T(8,128)(2,1)S(1)}, u32[]{:S(2)}, u32[]{:S(2)}) collective-permute-start(bf16[2048,256]{1,0:T(8,128)(2,1)S(1)} %get-tuple-element.62), channel_id=1, source_target_pairs={{0,2},{1,3},{2,0},{3,1},{4,6},{5,7},{6,4},{7,5},{8,10},{9,11},{10,... | collective-permute-start | bytes 3145736 | tf_op jit(solution)/shard_map/ppermute | solution.py:24
  13.3 1.5 %collective-permute-start.2 = (bf16[2176,256]{1,0:T(8,128)(2,1)S(1)}, bf16[2176,256]{1,0:T(8,128)(2,1)S(1)}, u32[]{:S(2)}, u32[]{:S(2)}) collective-permute-start(bf16[2176,256]{1,0:T(8,128)(2,1)S(1)} %get-tuple-element.61), channel_id=1, source_target_pairs={{0,1},{1,0},{2,3},{3,2},{4,5},{5,4},{6,7},{7,6},{8,9},{9,8},{10,11... | collective-permute-start | bytes 3342344 | tf_op jit(solution)/shard_map/ppermute | solution.py:24
  14.8 5.8 %shard_map.104 = (f32[2048,256]{1,0:T(8,128)S(1)}, f32[2048,256]{1,0:T(8,128)S(1)}, f32[32,512]{1,0:T(8,128)S(1)}) custom-call(s32[1]{0:T(128)} %bitcast.refs_0_.pos_ref._, s32[2,4]{1,0:T(2,128)} %bitcast.36, s32[2]{0:T(128)} %bitcast.43, bf16[2,256,1024]{2,1,0:T(8,128)(2,1)} %bitcast.19, bf16[8,512,1024]{2,1,0:T(8,128)(2,1)} %bitcast.26, ...), custom_call_target="tpu_custom_call" | custom-call | flops 1000 | bytes 1000 | tf_op jit(solution)/shard_map/pallas_call | solution.py:144
  20.7 8.5 %collective-permute-done = bf16[256,1024]{1,0:T(8,128)(2,1)S(1)} collective-permute-done((bf16[256,1024]{1,0:T(8,128)(2,1)S(1)}, bf16[256,1024]{1,0:T(8,128)(2,1)S(1)}, u32[]{:S(2)}, u32[]{:S(2)}) %collective-permute-start) | collective-permute-done | bytes 524320 | tf_op jit(solution)/shard_map/ppermute | solution.py:24
  29.2 0.0 collective-permute-start.1
  29.2 5.9 %shard_map.105 = (bf16[2048,128]{1,0:T(8,128)(2,1)S(1)}, bf16[2048,128]{1,0:T(8,128)(2,1)S(1)}, f32[2048,128]{1,0:T(8,128)S(1)}, f32[2048,128]{1,0:T(8,128)S(1)}, f32[32,256]{1,0:T(8,128)S(1)}) custom-call(s32[1]{0:T(128)} %bitcast.refs_0_.pos_ref._, s32[2,4]{1,0:T(2,128)} %bitcast.37, s32[2]{0:T(128)} %bitcast.44, bf16[1,256,1024]{2,1,0:T(8,128)(2,1)S(1)} %bitcast.21, ...), custom_call_target="tpu_custom_call" | custom-call | flops 40000000000 | bytes 1000 | tf_op jit(solution)/shard_map/pallas_call | solution.py:144
  35.0 1.4 %collective-permute-done.3.refs_3_ = bf16[2048,256]{1,0:T(8,128)(2,1)S(1)} collective-permute-done((bf16[2048,256]{1,0:T(8,128)(2,1)S(1)}, bf16[2048,256]{1,0:T(8,128)(2,1)S(1)}, u32[]{:S(2)}, u32[]{:S(2)}) %collective-permute-start.3) | collective-permute-done | bytes 1048608 | tf_op jit(solution)/shard_map/ppermute | solution.py:24
  36.4 2.6 %collective-permute-done.2.refs_2_ = bf16[2176,256]{1,0:T(8,128)(2,1)S(1)} collective-permute-done((bf16[2176,256]{1,0:T(8,128)(2,1)S(1)}, bf16[2176,256]{1,0:T(8,128)(2,1)S(1)}, u32[]{:S(2)}, u32[]{:S(2)}) %collective-permute-start.2) | collective-permute-done | bytes 1114144 | tf_op jit(solution)/shard_map/ppermute | solution.py:24
  39.1 0.3 shard_map.106
  39.4 1.6 %collective-permute-start.5 = (bf16[1024,256]{1,0:T(8,128)(2,1)S(1)}, bf16[1024,256]{1,0:T(8,128)(2,1)S(1)}, u32[]{:S(2)}, u32[]{:S(2)}) collective-permute-start(bf16[1024,256]{1,0:T(8,128)(2,1)S(1)} %get-tuple-element.72), channel_id=1, source_target_pairs={{0,1},{1,0},{2,3},{3,2},{4,5},{5,4},{6,7},{7,6},{8,9},{9,8},{10,11... | collective-permute-start | bytes 1572872 | tf_op jit(solution)/shard_map/ppermute | solution.py:24
  41.0 0.5 collective-permute-start.4
  41.5 0.5 collective-permute-start.10
  42.0 1.5 %collective-permute-start.11 = (bf16[2048,128]{1,0:T(8,128)(2,1)S(1)}, bf16[2048,128]{1,0:T(8,128)(2,1)S(1)}, u32[]{:S(2)}, u32[]{:S(2)}) collective-permute-start(bf16[2048,128]{1,0:T(8,128)(2,1)S(1)} %get-tuple-element.91), channel_id=1, source_target_pairs={{0,2},{1,3},{2,0},{3,1},{4,6},{5,7},{6,4},{7,5},{8,10},{9,11},{10,... | collective-permute-start | bytes 1572872 | tf_op jit(solution)/shard_map/ppermute | solution.py:24
  43.5 3.5 %shard_map.107.refs_4_ = bf16[8,512,1024]{2,1,0:T(8,128)(2,1)S(1)} custom-call(s32[1]{0:T(128)} %bitcast.refs_0_.pos_ref._, bf16[8,512,1024]{2,1,0:T(8,128)(2,1)} %bitcast.28), custom_call_target="tpu_custom_call" | custom-call | flops 1000 | bytes 1000 | tf_op jit(solution)/shard_map/pallas_call | solution.py:182
  47.0 7.4 %collective-permute-done.1 = bf16[256,1024]{1,0:T(8,128)(2,1)S(1)} collective-permute-done((bf16[256,1024]{1,0:T(8,128)(2,1)S(1)}, bf16[256,1024]{1,0:T(8,128)(2,1)S(1)}, u32[]{:S(2)}, u32[]{:S(2)}) %collective-permute-start.1) | collective-permute-done | bytes 524320 | tf_op jit(solution)/shard_map/ppermute | solution.py:24
  54.4 4.8 %shard_map.108 = (bf16[2048,128]{1,0:T(8,128)(2,1)S(1)}, bf16[2048,128]{1,0:T(8,128)(2,1)S(1)}, f32[2048,128]{1,0:T(8,128)S(1)}, f32[2048,128]{1,0:T(8,128)S(1)}, f32[32,256]{1,0:T(8,128)S(1)}) custom-call(s32[1]{0:T(128)} %bitcast.refs_0_.pos_ref._, s32[2,4]{1,0:T(2,128)} %bitcast.38, s32[2]{0:T(128)} %bitcast.45, bf16[1,256,1024]{2,1,0:T(8,128)(2,1)S(1)} %bitcast.23, ...), custom_call_target="tpu_custom_call" | custom-call | flops 40000000000 | bytes 1000 | tf_op jit(solution)/shard_map/pallas_call | solution.py:144
  59.3 0.0 collective-permute-done.5.refs_3_.refs_8_
  59.3 0.0 collective-permute-done.4.refs_2_.refs_6_
  59.3 0.1 shard_map.109
  59.4 0.1 collective-permute-start.6
  59.5 1.5 %collective-permute-start.8 = (bf16[192,256]{1,0:T(8,128)(2,1)S(1)}, bf16[192,256]{1,0:T(8,128)(2,1)S(1)}, u32[]{:S(2)}, u32[]{:S(2)}) collective-permute-start(bf16[192,256]{1,0:T(8,128)(2,1)S(1)} %get-tuple-element.83), channel_id=1, source_target_pairs={{0,12},{1,13},{2,14},{3,15},{4,8},{5,9},{6,10},{7,11},{8,4},{9,5},... | collective-permute-start | bytes 294920 | tf_op jit(solution)/shard_map/ppermute | solution.py:24
  61.0 2.0 %collective-permute-start.7 = (bf16[192,256]{1,0:T(8,128)(2,1)S(1)}, bf16[192,256]{1,0:T(8,128)(2,1)S(1)}, u32[]{:S(2)}, u32[]{:S(2)}) collective-permute-start(bf16[192,256]{1,0:T(8,128)(2,1)S(1)} %get-tuple-element.83), channel_id=1, source_target_pairs={{0,8},{1,9},{2,10},{3,11},{4,12},{5,13},{6,14},{7,15},{8,0},{9,1},... | collective-permute-start | bytes 294920 | tf_op jit(solution)/shard_map/ppermute | solution.py:24
  63.0 0.0 collective-permute-done.10.refs_2_
  63.0 2.5 %collective-permute-done.11.refs_3_ = bf16[2048,128]{1,0:T(8,128)(2,1)S(1)} collective-permute-done((bf16[2048,128]{1,0:T(8,128)(2,1)S(1)}, bf16[2048,128]{1,0:T(8,128)(2,1)S(1)}, u32[]{:S(2)}, u32[]{:S(2)}) %collective-permute-start.11) | collective-permute-done | bytes 524320 | tf_op jit(solution)/shard_map/ppermute | solution.py:24
  65.5 0.0 copy-start
  65.5 0.2 shard_map.112
  65.7 0.6 collective-permute-start.12
  66.2 0.5 collective-permute-start.13
  66.8 0.6 collective-permute-done.8.refs_9_.refs_5_
  67.4 0.0 collective-permute-start.9
  67.4 3.8 %collective-permute-done.7.refs_8_.refs_4_ = bf16[192,256]{1,0:T(8,128)(2,1)S(1)} collective-permute-done((bf16[192,256]{1,0:T(8,128)(2,1)S(1)}, bf16[192,256]{1,0:T(8,128)(2,1)S(1)}, u32[]{:S(2)}, u32[]{:S(2)}) %collective-permute-start.7) | collective-permute-done | bytes 98336 | tf_op jit(solution)/shard_map/ppermute | solution.py:24
  71.2 0.0 collective-permute-done.6.refs_7_.refs_3_
  71.2 0.1 shard_map.114
  71.3 1.3 %collective-permute-start.15 = (bf16[2304,128]{1,0:T(8,128)(2,1)S(1)}, bf16[2304,128]{1,0:T(8,128)(2,1)S(1)}, u32[]{:S(2)}, u32[]{:S(2)}) collective-permute-start(bf16[2304,128]{1,0:T(8,128)(2,1)S(1)} %get-tuple-element.102), channel_id=1, source_target_pairs={{0,2},{1,3},{2,0},{3,1},{4,6},{5,7},{6,4},{7,5},{8,10},{9,11},{10,... | collective-permute-start | bytes 1769480 | tf_op jit(solution)/shard_map/ppermute | solution.py:24
  72.7 1.5 %collective-permute-start.14 = (bf16[2304,128]{1,0:T(8,128)(2,1)S(1)}, bf16[2304,128]{1,0:T(8,128)(2,1)S(1)}, u32[]{:S(2)}, u32[]{:S(2)}) collective-permute-start(bf16[2304,128]{1,0:T(8,128)(2,1)S(1)} %get-tuple-element.97), channel_id=1, source_target_pairs={{0,1},{1,0},{2,3},{3,2},{4,5},{5,4},{6,7},{7,6},{8,9},{9,8},{10,11... | collective-permute-start | bytes 1769480 | tf_op jit(solution)/shard_map/ppermute | solution.py:24
  74.2 0.0 copy-done
  74.2 2.4 %shard_map.111 = bf16[8,32,1024]{2,1,0:T(8,128)(2,1)} custom-call(s32[1]{0:T(128)} %bitcast.refs_0_.pos_ref._, s32[2,4]{1,0:T(2,128)} %bitcast.39, s32[2]{0:T(128)} %bitcast.46, bf16[2,256,1024]{2,1,0:T(8,128)(2,1)S(1)} %bitcast.20, bf16[1,256,1024]{2,1,0:T(8,128)(2,1)S(1)} %bitcast.22, bf16[1,256,1024]{2,1,0:T(8,128)(2,1)S(1)} %bitcast.24, ...), custom_call_target="tpu_custom_call" | custom-call | flops 40000000000 | bytes 1000 | tf_op jit(solution)/shard_map/pallas_call | solution.py:506
  76.6 0.0 collective-permute-done.12.refs_2_.refs_10_
  76.6 0.0 collective-permute-done.13.refs_3_.refs_12_
  76.6 0.1 shard_map.115
  76.6 4.6 %collective-permute-done.9.refs_0_ = bf16[512,512]{1,0:T(8,128)(2,1)S(1)} collective-permute-done((bf16[512,512]{1,0:T(8,128)(2,1)S(1)}, bf16[512,512]{1,0:T(8,128)(2,1)S(1)}, u32[]{:S(2)}, u32[]{:S(2)}) %collective-permute-start.9) | collective-permute-done | bytes 524320 | tf_op jit(solution)/shard_map/ppermute | solution.py:34
  81.2 4.9 %collective-permute-done.15.refs_3_ = bf16[2304,128]{1,0:T(8,128)(2,1)S(1)} collective-permute-done((bf16[2304,128]{1,0:T(8,128)(2,1)S(1)}, bf16[2304,128]{1,0:T(8,128)(2,1)S(1)}, u32[]{:S(2)}, u32[]{:S(2)}) %collective-permute-start.15) | collective-permute-done | bytes 589856 | tf_op jit(solution)/shard_map/ppermute | solution.py:24
  86.2 1.0 collective-permute-done.14.refs_2_
  87.2 0.3 shard_map.116
  87.5 0.8 collective-permute-start.16
  88.3 1.2 %collective-permute-start.17 = (bf16[1280,128]{1,0:T(8,128)(2,1)S(1)}, bf16[1280,128]{1,0:T(8,128)(2,1)S(1)}, u32[]{:S(2)}, u32[]{:S(2)}) collective-permute-start(bf16[1280,128]{1,0:T(8,128)(2,1)S(1)} %get-tuple-element.107), channel_id=1, source_target_pairs={{0,1},{1,0},{2,3},{3,2},{4,5},{5,4},{6,7},{7,6},{8,9},{9,8},{10,11... | collective-permute-start | bytes 983048 | tf_op jit(solution)/shard_map/ppermute | solution.py:24
  89.5 0.0 collective-permute-start.19
  89.5 6.0 %collective-permute-done.16.refs_2_.got_x_ref.refs_14_ = bf16[1280,128]{1,0:T(8,128)(2,1)S(1)} collective-permute-done((bf16[1280,128]{1,0:T(8,128)(2,1)S(1)}, bf16[1280,128]{1,0:T(8,128)(2,1)S(1)}, u32[]{:S(2)}, u32[]{:S(2)}) %collective-permute-start.16) | collective-permute-done | bytes 327712 | tf_op jit(solution)/shard_map/ppermute | solution.py:24
  95.5 0.5 collective-permute-done.17.refs_3_.got_y_ref.refs_16_
  96.0 0.1 shard_map.117
  96.0 0.1 collective-permute-start.20
  96.1 1.6 %shard_map.119 = bf16[512,1024]{1,0:T(8,128)(2,1)S(1)} custom-call(s32[1]{0:T(128)} %bitcast.refs_0_.pos_ref._, s32[2,4]{1,0:T(2,128)} %bitcast.40, s32[2]{0:T(128)} %bitcast.47, bf16[8,64,512]{2,1,0:T(8,128)(2,1)} %bitcast.30, bf16[64,1024]{1,0:T(8,128)(2,1)S(1)} %shard_map.118.refs_4_.lowrank_ref, f32[1024,256]{1,0:T(8,128)S(1)} %get-tuple-element.78.refs_0_.refs_5_, ...), custom_call_target="tpu_custom_call" | custom-call | flops 1000 | bytes 1000 | tf_op jit(solution)/shard_map/pallas_call | solution.py:593
  97.7 0.8 collective-permute-start.18
  98.5 2.9 %shard_map.121 = bf16[8,64,512]{2,1,0:T(8,128)(2,1)} custom-call(s32[1]{0:T(128)} %bitcast.refs_0_.pos_ref._, s32[2,4]{1,0:T(2,128)} %bitcast.41, s32[2]{0:T(128)} %bitcast.48, bf16[2,512,512]{2,1,0:T(8,128)(2,1)} %bitcast.49, bf16[64,1024]{1,0:T(8,128)(2,1)S(1)} %shard_map.118.refs_4_.lowrank_ref), custom_call_target="tpu_custom_call" | custom-call | flops 40000000000 | bytes 1000 | tf_op jit(solution)/shard_map/pallas_call | solution.py:662
  101.4 0.0 collective-permute-done.19.refs_1_
  101.4 2.5 %collective-permute-done.20.refs_2_ = bf16[512,256]{1,0:T(8,128)(2,1)S(1)} collective-permute-done((bf16[512,256]{1,0:T(8,128)(2,1)S(1)}, bf16[512,256]{1,0:T(8,128)(2,1)S(1)}, u32[]{:S(2)}, u32[]{:S(2)}) %collective-permute-start.20) | collective-permute-done | bytes 262176 | tf_op jit(solution)/shard_map/ppermute | solution.py:34
  103.9 0.0 collective-permute-done.18.kept_ref
  103.9 1.3 %shard_map.120 = bf16[2,512,512]{2,1,0:T(8,128)(2,1)} custom-call(s32[1]{0:T(128)} %bitcast.refs_0_.pos_ref._, bf16[512,1024]{1,0:T(8,128)(2,1)S(1)} %collective-permute-done.18.kept_ref, bf16[512,512]{1,0:T(8,128)(2,1)S(1)} %collective-permute-done.9.refs_0_, bf16[512,256]{1,0:T(8,128)(2,1)S(1)} %collective-permute-done.19.refs_1_, ...), custom_call_target="tpu_custom_call" | custom-call | flops 1000 | bytes 1000 | tf_op jit(solution)/shard_map/pallas_call | solution.py:630
  (3 shorter events, 0.1 us)
Async XLA Ops:
  1.9 27.3 %collective-permute-start = (bf16[256,1024]{1,0:T(8,128)(2,1)S(1)}, bf16[256,1024]{1,0:T(8,128)(2,1)S(1)}, u32[]{:S(2)}, u32[]{:S(2)}) collective-permute-start(bf16[256,1024]{1,0:T(8,128)(2,1)S(1)} %get-tuple-element.109), channel_id=1, source_target_pairs={{0,8},{1,9},{2,10},{3,11},{4,12},{5,13},{6,14},{7,15},{8,0},{9,1},... | collective-permute-start | bytes 1572872 | tf_op jit(solution)/shard_map/ppermute | solution.py:24
  11.7 24.7 %collective-permute-start.3 = (bf16[2048,256]{1,0:T(8,128)(2,1)S(1)}, bf16[2048,256]{1,0:T(8,128)(2,1)S(1)}, u32[]{:S(2)}, u32[]{:S(2)}) collective-permute-start(bf16[2048,256]{1,0:T(8,128)(2,1)S(1)} %get-tuple-element.62), channel_id=1, source_target_pairs={{0,2},{1,3},{2,0},{3,1},{4,6},{5,7},{6,4},{7,5},{8,10},{9,11},{10,... | collective-permute-start | bytes 3145736 | tf_op jit(solution)/shard_map/ppermute | solution.py:24
  13.3 25.7 %collective-permute-start.2 = (bf16[2176,256]{1,0:T(8,128)(2,1)S(1)}, bf16[2176,256]{1,0:T(8,128)(2,1)S(1)}, u32[]{:S(2)}, u32[]{:S(2)}) collective-permute-start(bf16[2176,256]{1,0:T(8,128)(2,1)S(1)} %get-tuple-element.61), channel_id=1, source_target_pairs={{0,1},{1,0},{2,3},{3,2},{4,5},{5,4},{6,7},{7,6},{8,9},{9,8},{10,11... | collective-permute-start | bytes 3342344 | tf_op jit(solution)/shard_map/ppermute | solution.py:24
  29.2 25.2 %collective-permute-start.1 = (bf16[256,1024]{1,0:T(8,128)(2,1)S(1)}, bf16[256,1024]{1,0:T(8,128)(2,1)S(1)}, u32[]{:S(2)}, u32[]{:S(2)}) collective-permute-start(bf16[256,1024]{1,0:T(8,128)(2,1)S(1)} %get-tuple-element.59), channel_id=1, source_target_pairs={{0,8},{1,9},{2,10},{3,11},{4,12},{5,13},{6,14},{7,15},{8,0},{9,1},... | collective-permute-start | bytes 1572872 | tf_op jit(solution)/shard_map/ppermute | solution.py:24
  39.4 19.9 %collective-permute-start.5 = (bf16[1024,256]{1,0:T(8,128)(2,1)S(1)}, bf16[1024,256]{1,0:T(8,128)(2,1)S(1)}, u32[]{:S(2)}, u32[]{:S(2)}) collective-permute-start(bf16[1024,256]{1,0:T(8,128)(2,1)S(1)} %get-tuple-element.72), channel_id=1, source_target_pairs={{0,1},{1,0},{2,3},{3,2},{4,5},{5,4},{6,7},{7,6},{8,9},{9,8},{10,11... | collective-permute-start | bytes 1572872 | tf_op jit(solution)/shard_map/ppermute | solution.py:24
  41.0 18.3 %collective-permute-start.4 = (bf16[1152,256]{1,0:T(8,128)(2,1)S(1)}, bf16[1152,256]{1,0:T(8,128)(2,1)S(1)}, u32[]{:S(2)}, u32[]{:S(2)}) collective-permute-start(bf16[1152,256]{1,0:T(8,128)(2,1)S(1)} %get-tuple-element.71), channel_id=1, source_target_pairs={{0,2},{1,3},{2,0},{3,1},{4,6},{5,7},{6,4},{7,5},{8,10},{9,11},{10,... | collective-permute-start | bytes 1769480 | tf_op jit(solution)/shard_map/ppermute | solution.py:24
  41.5 21.5 %collective-permute-start.10 = (bf16[2048,128]{1,0:T(8,128)(2,1)S(1)}, bf16[2048,128]{1,0:T(8,128)(2,1)S(1)}, u32[]{:S(2)}, u32[]{:S(2)}) collective-permute-start(bf16[2048,128]{1,0:T(8,128)(2,1)S(1)} %get-tuple-element.89), channel_id=1, source_target_pairs={{0,1},{1,0},{2,3},{3,2},{4,5},{5,4},{6,7},{7,6},{8,9},{9,8},{10,11... | collective-permute-start | bytes 1572872 | tf_op jit(solution)/shard_map/ppermute | solution.py:24
  42.0 23.5 %collective-permute-start.11 = (bf16[2048,128]{1,0:T(8,128)(2,1)S(1)}, bf16[2048,128]{1,0:T(8,128)(2,1)S(1)}, u32[]{:S(2)}, u32[]{:S(2)}) collective-permute-start(bf16[2048,128]{1,0:T(8,128)(2,1)S(1)} %get-tuple-element.91), channel_id=1, source_target_pairs={{0,2},{1,3},{2,0},{3,1},{4,6},{5,7},{6,4},{7,5},{8,10},{9,11},{10,... | collective-permute-start | bytes 1572872 | tf_op jit(solution)/shard_map/ppermute | solution.py:24
  59.4 11.8 %collective-permute-start.6 = (bf16[256,256]{1,0:T(8,128)(2,1)S(1)}, bf16[256,256]{1,0:T(8,128)(2,1)S(1)}, u32[]{:S(2)}, u32[]{:S(2)}) collective-permute-start(bf16[256,256]{1,0:T(8,128)(2,1)S(1)} %get-tuple-element.82), channel_id=1, source_target_pairs={{0,4},{1,5},{2,6},{3,7},{4,0},{5,1},{6,2},{7,3},{8,12},{9,13},{10,... | collective-permute-start | bytes 393224 | tf_op jit(solution)/shard_map/ppermute | solution.py:24
  59.5 7.9 %collective-permute-start.8 = (bf16[192,256]{1,0:T(8,128)(2,1)S(1)}, bf16[192,256]{1,0:T(8,128)(2,1)S(1)}, u32[]{:S(2)}, u32[]{:S(2)}) collective-permute-start(bf16[192,256]{1,0:T(8,128)(2,1)S(1)} %get-tuple-element.83), channel_id=1, source_target_pairs={{0,12},{1,13},{2,14},{3,15},{4,8},{5,9},{6,10},{7,11},{8,4},{9,5},... | collective-permute-start | bytes 294920 | tf_op jit(solution)/shard_map/ppermute | solution.py:24
  61.0 10.2 %collective-permute-start.7 = (bf16[192,256]{1,0:T(8,128)(2,1)S(1)}, bf16[192,256]{1,0:T(8,128)(2,1)S(1)}, u32[]{:S(2)}, u32[]{:S(2)}) collective-permute-start(bf16[192,256]{1,0:T(8,128)(2,1)S(1)} %get-tuple-element.83), channel_id=1, source_target_pairs={{0,8},{1,9},{2,10},{3,11},{4,12},{5,13},{6,14},{7,15},{8,0},{9,1},... | collective-permute-start | bytes 294920 | tf_op jit(solution)/shard_map/ppermute | solution.py:24
  65.5 8.7 %copy-start = (bf16[1,1,2,256,1024]{4,3,2,1,0:T(8,128)(2,1)S(1)}, bf16[1,1,2,256,1024]{4,3,2,1,0:T(8,128)(2,1)}, u32[]{:S(2)}) copy-start(bf16[1,1,2,256,1024]{4,3,2,1,0:T(8,128)(2,1)} %param.8) | copy-start | bytes 3145732
  65.7 10.9 %collective-permute-start.12 = (bf16[1024,128]{1,0:T(8,128)(2,1)S(1)}, bf16[1024,128]{1,0:T(8,128)(2,1)S(1)}, u32[]{:S(2)}, u32[]{:S(2)}) collective-permute-start(bf16[1024,128]{1,0:T(8,128)(2,1)S(1)} %get-tuple-element.99), channel_id=1, source_target_pairs={{0,2},{1,3},{2,0},{3,1},{4,6},{5,7},{6,4},{7,5},{8,10},{9,11},{10,... | collective-permute-start | bytes 786440 | tf_op jit(solution)/shard_map/ppermute | solution.py:24
  66.2 10.3 %collective-permute-start.13 = (bf16[1024,128]{1,0:T(8,128)(2,1)S(1)}, bf16[1024,128]{1,0:T(8,128)(2,1)S(1)}, u32[]{:S(2)}, u32[]{:S(2)}) collective-permute-start(bf16[1024,128]{1,0:T(8,128)(2,1)S(1)} %get-tuple-element.100), channel_id=1, source_target_pairs={{0,1},{1,0},{2,3},{3,2},{4,5},{5,4},{6,7},{7,6},{8,9},{9,8},{10,11... | collective-permute-start | bytes 786440 | tf_op jit(solution)/shard_map/ppermute | solution.py:24
  67.4 13.8 %collective-permute-start.9 = (bf16[512,512]{1,0:T(8,128)(2,1)S(1)}, bf16[512,512]{1,0:T(8,128)(2,1)S(1)}, u32[]{:S(2)}, u32[]{:S(2)}) collective-permute-start(bf16[512,512]{1,0:T(8,128)(2,1)S(1)} %get-tuple-element.84), channel_id=1, source_target_pairs={{0,20},{1,21},{2,22},{3,23},{4,16},{5,17},{6,18},{7,19},{8,28},{9,... | collective-permute-start | bytes 1572872 | tf_op jit(solution)/shard_map/ppermute | solution.py:34
  71.3 14.9 %collective-permute-start.15 = (bf16[2304,128]{1,0:T(8,128)(2,1)S(1)}, bf16[2304,128]{1,0:T(8,128)(2,1)S(1)}, u32[]{:S(2)}, u32[]{:S(2)}) collective-permute-start(bf16[2304,128]{1,0:T(8,128)(2,1)S(1)} %get-tuple-element.102), channel_id=1, source_target_pairs={{0,2},{1,3},{2,0},{3,1},{4,6},{5,7},{6,4},{7,5},{8,10},{9,11},{10,... | collective-permute-start | bytes 1769480 | tf_op jit(solution)/shard_map/ppermute | solution.py:24
  72.7 14.5 %collective-permute-start.14 = (bf16[2304,128]{1,0:T(8,128)(2,1)S(1)}, bf16[2304,128]{1,0:T(8,128)(2,1)S(1)}, u32[]{:S(2)}, u32[]{:S(2)}) collective-permute-start(bf16[2304,128]{1,0:T(8,128)(2,1)S(1)} %get-tuple-element.97), channel_id=1, source_target_pairs={{0,1},{1,0},{2,3},{3,2},{4,5},{5,4},{6,7},{7,6},{8,9},{9,8},{10,11... | collective-permute-start | bytes 1769480 | tf_op jit(solution)/shard_map/ppermute | solution.py:24
  87.5 8.0 %collective-permute-start.16 = (bf16[1280,128]{1,0:T(8,128)(2,1)S(1)}, bf16[1280,128]{1,0:T(8,128)(2,1)S(1)}, u32[]{:S(2)}, u32[]{:S(2)}) collective-permute-start(bf16[1280,128]{1,0:T(8,128)(2,1)S(1)} %get-tuple-element.106), channel_id=1, source_target_pairs={{0,2},{1,3},{2,0},{3,1},{4,6},{5,7},{6,4},{7,5},{8,10},{9,11},{10,... | collective-permute-start | bytes 983048 | tf_op jit(solution)/shard_map/ppermute | solution.py:24
  88.3 7.7 %collective-permute-start.17 = (bf16[1280,128]{1,0:T(8,128)(2,1)S(1)}, bf16[1280,128]{1,0:T(8,128)(2,1)S(1)}, u32[]{:S(2)}, u32[]{:S(2)}) collective-permute-start(bf16[1280,128]{1,0:T(8,128)(2,1)S(1)} %get-tuple-element.107), channel_id=1, source_target_pairs={{0,1},{1,0},{2,3},{3,2},{4,5},{5,4},{6,7},{7,6},{8,9},{9,8},{10,11... | collective-permute-start | bytes 983048 | tf_op jit(solution)/shard_map/ppermute | solution.py:24
  89.5 11.8 %collective-permute-start.19 = (bf16[512,256]{1,0:T(8,128)(2,1)S(1)}, bf16[512,256]{1,0:T(8,128)(2,1)S(1)}, u32[]{:S(2)}, u32[]{:S(2)}) collective-permute-start(bf16[512,256]{1,0:T(8,128)(2,1)S(1)} %shard_map.115), channel_id=1, source_target_pairs={{0,20},{1,21},{2,22},{3,23},{4,16},{5,17},{6,18},{7,19},{8,28},{9,... | collective-permute-start | bytes 786440 | tf_op jit(solution)/shard_map/ppermute | solution.py:34
  96.0 7.8 %collective-permute-start.20 = (bf16[512,256]{1,0:T(8,128)(2,1)S(1)}, bf16[512,256]{1,0:T(8,128)(2,1)S(1)}, u32[]{:S(2)}, u32[]{:S(2)}) collective-permute-start(bf16[512,256]{1,0:T(8,128)(2,1)S(1)} %shard_map.117), channel_id=1, source_target_pairs={{0,20},{1,21},{2,22},{3,23},{4,16},{5,17},{6,18},{7,19},{8,28},{9,... | collective-permute-start | bytes 786440 | tf_op jit(solution)/shard_map/ppermute | solution.py:34
  97.7 6.1 %collective-permute-start.18 = (bf16[512,1024]{1,0:T(8,128)(2,1)S(1)}, bf16[512,1024]{1,0:T(8,128)(2,1)S(1)}, u32[]{:S(2)}, u32[]{:S(2)}) collective-permute-start(bf16[512,1024]{1,0:T(8,128)(2,1)S(1)} %shard_map.119), channel_id=1, source_target_pairs={{0,16},{1,17},{2,18},{3,19},{4,20},{5,21},{6,22},{7,23},{8,24},{9,... | collective-permute-start | bytes 3145736 | tf_op jit(solution)/shard_map/ppermute | solution.py:34

commit v16 on v15

--- a/solution.py
+++ b/solution.py
@@ -263,12 +263,11 @@
 def up_body(low_size, tile_rows, pieces, tiles, micro_count, *refs):
     pos_ref, classes_ref, live_ref = refs[:3]
     grad_refs = refs[3 : 3 + tiles]
-    placed_ref, near_ref, *far_refs = refs[3 + tiles : -2]
+    hidden_refs = refs[3 + tiles : -2]
     out_ref, total_ref = refs[-2:]
     high = pos_ref[0] // low_size
     total_ref[...] = jnp.zeros_like(total_ref)
     rank_part = total_ref.shape[1]
-    skip = near_ref.shape[0] - placed_ref.shape[0]
     for tile, index, piece, first in pieces:
         k, m, offset = piece
         size = min(SEG, tile_rows)
@@ -278,18 +277,11 @@
         @pl.when(seg < live_ref[m])
         def _():
             if k == 0:
-                start = pl.multiple_of(
-                    m * (placed_ref.shape[0] // micro_count) + high * rank_part, rank_part
-                )
-                other = pl.multiple_of(skip + start, rank_part)
-                hidden = (
-                    placed_ref[pl.ds(start, rank_part), lanes]
-                    + near_ref[pl.ds(other, rank_part), lanes]
-                )
+                start = m * (hidden_refs[0].shape[0] // micro_count) + high * rank_part
+                rows = pl.ds(pl.multiple_of(start, rank_part), rank_part)
             else:
-                rows = slice(skip + m * rank_part, skip + (m + 1) * rank_part)
-                one_ref, other_ref = far_refs[2 * k - 2 : 2 * k]
-                hidden = one_ref[rows, lanes] + other_ref[rows, lanes]
+                rows = slice(m * rank_part, (m + 1) * rank_part)
+            hidden = hidden_refs[k][rows, lanes]
             total_ref[classes_ref[m, seg]] += jnp.dot(
                 hidden,
                 grad_refs[tile][index, first : first + size, :],
@@ -395,72 +387,77 @@
             cost_estimate=cost,
         )(*in_hbm(scalars[0]), *operands)
 
-    def collect_kernel(pos_ref, *refs):
-        part_refs, placed_ref = refs[: len(parts)], refs[len(parts)]
-        *message_refs, wide_ref = refs[len(parts) + 1 :]
-        own = pos_ref[0] // low_size
-        block = 0
-        for part_ref in part_refs:
-            for start in range(0, part_ref.shape[1], tile_rows):
-                value = part_ref[:, start : start + tile_rows].astype(BF16)
-                for message_ref in message_refs:
-                    message_ref[block * rank_part : (block + 1) * rank_part, :] = value
-                block += 1
-        wide_ref[...] = placed_ref[...].astype(F32)
-        message_refs[0][block * rank_part :, :] = placed_ref[...]
-        for k in range(1, high_size):
+    whole_parts = [(at, start) for at, part in enumerate(parts) for start in range(0, part.shape[1], tile_rows)]
+
+    def collect_kernel(_, *refs):
+        *part_refs, placed_ref, out_ref = refs
+        for block, (at, start) in enumerate(whole_parts):
+            out_ref[block * rank_part : (block + 1) * rank_part, :] = part_refs[at][
+                :, start : start + tile_rows
+            ].astype(BF16)
+        out_ref[blocks * rank_part :, :] = placed_ref[...]
+
+    message = blocks * rank_part, tile_rows
+    (shared,) = small(
+        collect_kernel, [((message[0] + placed.shape[0], tile_rows), BF16)], *parts, placed
+    )
+    near = partner(shared, 4)
+
+    (c_sent_x, c_sent_y), c_kept = halve(
+        (after(c_kept_x, shared), c_kept_y), (c_first_x, c_first_y)
+    )
+    c_second_x, c_second_y = partner(c_sent_x, 2), partner(c_sent_y, 1)
+
+    def near_kernel(pos_ref, *refs):
+        count = len(parts)
+        part_refs, placed_ref, near_ref = refs[:count], refs[count], refs[count + 1]
+        shared_ref, total_ref, out_ref, *far_refs, wide_ref = refs[count + 2 :]
+        for block, (at, start) in enumerate(whole_parts):
+            rows = slice(block * rank_part, (block + 1) * rank_part)
+            total = part_refs[at][:, start : start + tile_rows] + near_ref[rows, :].astype(F32)
+            total_ref[rows, :] = total
+            shared_ref[rows, :] = total.astype(BF16)
+        out_ref[...] = placed_ref[...] + near_ref[blocks * rank_part :, :]
+        wide_ref[...] = out_ref[...].astype(F32)
+        for k, far_ref in enumerate(far_refs, 1):
             for m in range(micro_count):
-                start = pl.multiple_of(m * rank + (own ^ k) * rank_part, rank_part)
-                first = (block + m) * rank_part
-                message_refs[k][first : first + rank_part, :] = wide_ref[
-                    pl.ds(start, rank_part), :
+                start = m * rank + ((pos_ref[0] // low_size) ^ k) * rank_part
+                far_ref[m * rank_part : (m + 1) * rank_part, :] = wide_ref[
+                    pl.ds(pl.multiple_of(start, rank_part), rank_part), :
                 ].astype(BF16)
 
-    counts = [placed.shape[0]] + [micro_count * rank_part] * (high_size - 1)
-    messages = small(
-        collect_kernel,
-        [((blocks * rank_part + n, tile_rows), BF16) for n in counts],
+    shared, total, placed, *wanted = small(
+        near_kernel,
+        [(message, BF16), (message, F32), (placed.shape, BF16)]
+        + [((micro_count * rank_part, tile_rows), BF16)] * (high_size - 1),
         *parts,
         placed,
+        near,
         scratch=[pltpu.VMEM(placed.shape, F32)],
     )
-    (c_sent_x, c_sent_y), c_kept = halve(
-        (after(c_kept_x, messages[0]), c_kept_y), (c_first_x, c_first_y)
-    )
-    c_second_x, c_second_y = partner(c_sent_x, 2), partner(c_sent_y, 1)
-    near = partner(messages[0], 4)
-    far = []
-    for k in range(1, high_size):
-        far += [partner(messages[k], k * low_size), partner(messages[k], k * low_size + 4)]
+    far = [partner(shared, k * low_size) for k in range(1, high_size)]
 
     def columns_of(j, piece):
         k, m, offset = piece
         at = order.index((k ^ j, m, offset))
         return slice(at * size, (at + 1) * size)
 
-    def block_of(message_ref, columns):
-        block, start = columns.start // tile_rows, columns.start % tile_rows
-        rows = slice(block * rank_part, (block + 1) * rank_part)
-        return message_ref[rows, start : start + size].astype(F32)
-
     def lowrank_kernel(pos_ref, *refs):
-        part_refs = refs[: len(parts)]
-        near_ref, *far_refs = refs[len(parts) : -1]
         out_ref = refs[-1]
-        whole = [(ref, start) for ref in part_refs for start in range(0, ref.shape[1], size)]
         for at, piece in enumerate(order):
-            columns = slice(at * size, (at + 1) * size)
             for j in range(high_size):
-                if j == 0:
-                    part_ref, start = whole[at]
-                    value = part_ref[:, start : start + size] + block_of(near_ref, columns)
-                else:
-                    other = columns_of(j, piece)
-                    value = block_of(far_refs[2 * j - 2], other) + block_of(far_refs[2 * j - 1], other)
+                block, start = divmod(columns_of(j, piece).start, tile_rows)
+                value = refs[j][
+                    block * rank_part : (block + 1) * rank_part, start : start + size
+                ].astype(F32)
                 start = pl.multiple_of(((pos_ref[0] // low_size) ^ j) * rank_part, rank_part)
-                out_ref[pl.ds(start, rank_part), columns] = value
-
-    (lowrank,) = small(lowrank_kernel, [((rank, rows_total), F32)], *parts, near, *far)
+                out_ref[pl.ds(start, rank_part), at * size : (at + 1) * size] = value
+
+    (lowrank,) = small(lowrank_kernel, [((rank, rows_total), F32)], total, *far)
+
+    hiddens = [placed] + [
+        partner(after(w, shared), k * low_size) for k, w in enumerate(wanted, 1)
+    ]
 
     halves = [range(0, len(order) // 2), range(len(order) // 2, len(order))]
 
@@ -507,13 +504,13 @@
         functools.partial(
             up_body, low_size, tile_rows, all_pieces, len(all_grads), micro_count
         ),
-        in_specs=[SMEM] * 3 + [VMEM] * (len(all_grads) + 2 * high_size),
+        in_specs=[SMEM] * 3 + [VMEM] * (len(all_grads) + high_size),
         out_specs=VMEM,
         out_shape=jax.ShapeDtypeStruct(up_tile.shape, BF16),
         scratch_shapes=[pltpu.VMEM(up_tile.shape, F32)],
         compiler_params=PARAMS,
         cost_estimate=LONG,
-    )(*in_hbm(*scalars), *all_grads, placed, near, *far)
+    )(*in_hbm(*scalars), *all_grads, *hiddens)
 
     (c_third,) = last_parts((after(c_kept[0], d_sent_x), c_kept[1]), (c_second_x, c_second_y))
     c_last = relay(c_third, 4)

time: 105 us -> 108 us (1.029)
  starting transfers between devices: 21.7 us -> 22.9 us
    ppermute x4, waiting for transfers between devices: 7.09 us -> 8.45 us  [relay(): return lax.ppermute(value, ('pipe', 'tensor'), pairs)]
  transfers between devices with their start and end apart: 21 -> 21, of which waited for: 13 -> 12; matrix products, arithmetic and copies ran while one was open for 0% -> 0% of each run, Pallas kernels for 32% -> 32%
where the time goes in v16:
time: 108 us; the launch traced here: 107 us
  waiting for transfers between devices  46.7 us (43%)
  Pallas kernels  35.6 us (33%)
  starting transfers between devices  22.9 us (21%)
  local copies, waits for them, and re-layouts  1.27 us (1%)
    ppermute x17, waiting for transfers between devices, partner(): return lax.ppermute(value, 'tensor', pairs)  38.3 us
    pallas_call x4, Pallas kernels, product(): pl.pallas_call(functools.partial(product_body, low_size, tile_rows, piece...  22.5 us
    ppermute x17, starting transfers between devices, partner(): return lax.ppermute(value, 'tensor', pairs)  21.8 us
    ppermute x4, waiting for transfers between devices, relay(): return lax.ppermute(value, ('pipe', 'tensor'), pairs)  8.45 us
    pallas_call x1, Pallas kernels, fetch(): pl.pallas_call(functools.partial(fetch_kernel, low_size), in_specs=[SMEM,...  3.47 us
    pallas_call x1, Pallas kernels, shards(): pl.pallas_call(down_kernel, in_specs=[SMEM] * 3 + [VMEM] * 2, out_specs=V...  3.03 us
    pallas_call x1, Pallas kernels, shards(): pl.pallas_call(functools.partial(up_body, low_size, tile_rows, all_pieces...  2.59 us
  transfers between devices with their start and end apart: 21, of which 12 were waited for; matrix products, arithmetic and copies ran while one was open for 0% of the time, Pallas kernels for 32%

profile of v16, /device:TPU:0, one launch (start us, length us, event | category | flops | bytes accessed | tf_op | source)
XLA Modules:
  0.0 107.3 jit_solution(17420418867399797479)
XLA Ops:
  0.6 1.3 %slice_bitcast_fusion = (bf16[256,1024]{1,0:T(8,128)(2,1)S(1)}, bf16[256,1024]{1,0:T(8,128)(2,1)S(1)}) fusion(bf16[1,1,2,256,1024]{4,3,2,1,0:T(8,128)(2,1)} %param.8), kind=kLoop, calls=%fused_computation | loop fusion | bytes 2097152 | tf_op jit(solution)/shard_map/squeeze | solution.py:341
  1.9 4.1 %collective-permute-start = (bf16[256,1024]{1,0:T(8,128)(2,1)S(1)}, bf16[256,1024]{1,0:T(8,128)(2,1)S(1)}, u32[]{:S(2)}, u32[]{:S(2)}) collective-permute-start(bf16[256,1024]{1,0:T(8,128)(2,1)S(1)} %get-tuple-element.115), channel_id=1, source_target_pairs={{0,8},{1,9},{2,10},{3,11},{4,12},{5,13},{6,14},{7,15},{8,0},{9,1},... | collective-permute-start | bytes 1572872 | tf_op jit(solution)/shard_map/ppermute | solution.py:24
  6.0 5.7 %shard_map.103 = (bf16[2176,256]{1,0:T(8,128)(2,1)S(1)}, bf16[2048,256]{1,0:T(8,128)(2,1)S(1)}, bf16[128,256]{1,0:T(8,128)(2,1)S(1)}) custom-call(s32[1]{0:T(128)} %bitcast.refs_0_.pos_ref._, s32[2,4]{1,0:T(2,128)} %bitcast.35, s32[2]{0:T(128)} %bitcast.42, bf16[2,256,1024]{2,1,0:T(8,128)(2,1)} %bitcast.18, bf16[8,512,1024]{2,1,0:T(8,128)(2,1)} %bitcast.25, ...), custom_call_target="tpu_custom_call" | custom-call | flops 1000 | bytes 1000 | tf_op jit(solution)/shard_map/pallas_call | solution.py:144
  11.7 1.6 %collective-permute-start.3 = (bf16[2048,256]{1,0:T(8,128)(2,1)S(1)}, bf16[2048,256]{1,0:T(8,128)(2,1)S(1)}, u32[]{:S(2)}, u32[]{:S(2)}) collective-permute-start(bf16[2048,256]{1,0:T(8,128)(2,1)S(1)} %get-tuple-element.65), channel_id=1, source_target_pairs={{0,2},{1,3},{2,0},{3,1},{4,6},{5,7},{6,4},{7,5},{8,10},{9,11},{10,... | collective-permute-start | bytes 3145736 | tf_op jit(solution)/shard_map/ppermute | solution.py:24
  13.3 1.5 %collective-permute-start.2 = (bf16[2176,256]{1,0:T(8,128)(2,1)S(1)}, bf16[2176,256]{1,0:T(8,128)(2,1)S(1)}, u32[]{:S(2)}, u32[]{:S(2)}) collective-permute-start(bf16[2176,256]{1,0:T(8,128)(2,1)S(1)} %get-tuple-element.64), channel_id=1, source_target_pairs={{0,1},{1,0},{2,3},{3,2},{4,5},{5,4},{6,7},{7,6},{8,9},{9,8},{10,11... | collective-permute-start | bytes 3342344 | tf_op jit(solution)/shard_map/ppermute | solution.py:24
  14.8 5.8 %shard_map.104 = (f32[2048,256]{1,0:T(8,128)S(1)}, f32[2048,256]{1,0:T(8,128)S(1)}, f32[32,512]{1,0:T(8,128)S(1)}) custom-call(s32[1]{0:T(128)} %bitcast.refs_0_.pos_ref._, s32[2,4]{1,0:T(2,128)} %bitcast.36, s32[2]{0:T(128)} %bitcast.43, bf16[2,256,1024]{2,1,0:T(8,128)(2,1)} %bitcast.19, bf16[8,512,1024]{2,1,0:T(8,128)(2,1)} %bitcast.26, ...), custom_call_target="tpu_custom_call" | custom-call | flops 1000 | bytes 1000 | tf_op jit(solution)/shard_map/pallas_call | solution.py:144
  20.7 8.5 %collective-permute-done = bf16[256,1024]{1,0:T(8,128)(2,1)S(1)} collective-permute-done((bf16[256,1024]{1,0:T(8,128)(2,1)S(1)}, bf16[256,1024]{1,0:T(8,128)(2,1)S(1)}, u32[]{:S(2)}, u32[]{:S(2)}) %collective-permute-start) | collective-permute-done | bytes 524320 | tf_op jit(solution)/shard_map/ppermute | solution.py:24
  29.2 0.0 collective-permute-start.1
  29.2 5.9 %shard_map.105 = (bf16[2048,128]{1,0:T(8,128)(2,1)S(1)}, bf16[2048,128]{1,0:T(8,128)(2,1)S(1)}, f32[2048,128]{1,0:T(8,128)S(1)}, f32[2048,128]{1,0:T(8,128)S(1)}, f32[32,256]{1,0:T(8,128)S(1)}) custom-call(s32[1]{0:T(128)} %bitcast.refs_0_.pos_ref._, s32[2,4]{1,0:T(2,128)} %bitcast.37, s32[2]{0:T(128)} %bitcast.44, bf16[1,256,1024]{2,1,0:T(8,128)(2,1)S(1)} %bitcast.21, ...), custom_call_target="tpu_custom_call" | custom-call | flops 40000000000 | bytes 1000 | tf_op jit(solution)/shard_map/pallas_call | solution.py:144
  35.0 1.4 %collective-permute-done.3.refs_3_ = bf16[2048,256]{1,0:T(8,128)(2,1)S(1)} collective-permute-done((bf16[2048,256]{1,0:T(8,128)(2,1)S(1)}, bf16[2048,256]{1,0:T(8,128)(2,1)S(1)}, u32[]{:S(2)}, u32[]{:S(2)}) %collective-permute-start.3) | collective-permute-done | bytes 1048608 | tf_op jit(solution)/shard_map/ppermute | solution.py:24
  36.4 2.6 %collective-permute-done.2.refs_2_ = bf16[2176,256]{1,0:T(8,128)(2,1)S(1)} collective-permute-done((bf16[2176,256]{1,0:T(8,128)(2,1)S(1)}, bf16[2176,256]{1,0:T(8,128)(2,1)S(1)}, u32[]{:S(2)}, u32[]{:S(2)}) %collective-permute-start.2) | collective-permute-done | bytes 1114144 | tf_op jit(solution)/shard_map/ppermute | solution.py:24
  39.1 0.3 shard_map.106
  39.4 1.6 %collective-permute-start.5 = (bf16[1024,256]{1,0:T(8,128)(2,1)S(1)}, bf16[1024,256]{1,0:T(8,128)(2,1)S(1)}, u32[]{:S(2)}, u32[]{:S(2)}) collective-permute-start(bf16[1024,256]{1,0:T(8,128)(2,1)S(1)} %get-tuple-element.75), channel_id=1, source_target_pairs={{0,1},{1,0},{2,3},{3,2},{4,5},{5,4},{6,7},{7,6},{8,9},{9,8},{10,11... | collective-permute-start | bytes 1572872 | tf_op jit(solution)/shard_map/ppermute | solution.py:24
  41.0 0.5 collective-permute-start.4
  41.5 0.5 collective-permute-start.9
  42.0 1.5 %collective-permute-start.10 = (bf16[2048,128]{1,0:T(8,128)(2,1)S(1)}, bf16[2048,128]{1,0:T(8,128)(2,1)S(1)}, u32[]{:S(2)}, u32[]{:S(2)}) collective-permute-start(bf16[2048,128]{1,0:T(8,128)(2,1)S(1)} %get-tuple-element.96), channel_id=1, source_target_pairs={{0,2},{1,3},{2,0},{3,1},{4,6},{5,7},{6,4},{7,5},{8,10},{9,11},{10,... | collective-permute-start | bytes 1572872 | tf_op jit(solution)/shard_map/ppermute | solution.py:24
  43.5 3.5 %shard_map.107.refs_4_ = bf16[8,512,1024]{2,1,0:T(8,128)(2,1)S(1)} custom-call(s32[1]{0:T(128)} %bitcast.refs_0_.pos_ref._, bf16[8,512,1024]{2,1,0:T(8,128)(2,1)} %bitcast.28), custom_call_target="tpu_custom_call" | custom-call | flops 1000 | bytes 1000 | tf_op jit(solution)/shard_map/pallas_call | solution.py:182
  47.0 7.4 %collective-permute-done.1 = bf16[256,1024]{1,0:T(8,128)(2,1)S(1)} collective-permute-done((bf16[256,1024]{1,0:T(8,128)(2,1)S(1)}, bf16[256,1024]{1,0:T(8,128)(2,1)S(1)}, u32[]{:S(2)}, u32[]{:S(2)}) %collective-permute-start.1) | collective-permute-done | bytes 524320 | tf_op jit(solution)/shard_map/ppermute | solution.py:24
  54.4 5.1 %shard_map.108 = (bf16[2048,128]{1,0:T(8,128)(2,1)S(1)}, bf16[2048,128]{1,0:T(8,128)(2,1)S(1)}, f32[2048,128]{1,0:T(8,128)S(1)}, f32[2048,128]{1,0:T(8,128)S(1)}, f32[32,256]{1,0:T(8,128)S(1)}) custom-call(s32[1]{0:T(128)} %bitcast.refs_0_.pos_ref._, s32[2,4]{1,0:T(2,128)} %bitcast.38, s32[2]{0:T(128)} %bitcast.45, bf16[1,256,1024]{2,1,0:T(8,128)(2,1)S(1)} %bitcast.23, ...), custom_call_target="tpu_custom_call" | custom-call | flops 40000000000 | bytes 1000 | tf_op jit(solution)/shard_map/pallas_call | solution.py:144
  59.5 0.0 collective-permute-done.5.refs_3_.refs_8_
  59.5 0.0 collective-permute-done.4.refs_2_.refs_6_
  59.5 0.1 shard_map.109
  59.6 0.1 collective-permute-start.6
  59.7 5.0 %collective-permute-done.6.refs_4_ = bf16[256,256]{1,0:T(8,128)(2,1)S(1)} collective-permute-done((bf16[256,256]{1,0:T(8,128)(2,1)S(1)}, bf16[256,256]{1,0:T(8,128)(2,1)S(1)}, u32[]{:S(2)}, u32[]{:S(2)}) %collective-permute-start.6) | collective-permute-done | bytes 131104 | tf_op jit(solution)/shard_map/ppermute | solution.py:24
  64.7 0.5 collective-permute-start.11
  65.2 2.5 %collective-permute-start.7 = (bf16[64,256]{1,0:T(8,128)(2,1)S(1)}, bf16[64,256]{1,0:T(8,128)(2,1)S(1)}, u32[]{:S(2)}, u32[]{:S(2)}) collective-permute-start(bf16[64,256]{1,0:T(8,128)(2,1)S(1)} %get-tuple-element.88), channel_id=1, source_target_pairs={{0,8},{1,9},{2,10},{3,11},{4,12},{5,13},{6,14},{7,15},{8,0},{9,1},... | collective-permute-start | bytes 98312 | tf_op jit(solution)/shard_map/ppermute | solution.py:24
  67.7 0.0 collective-permute-done.9.refs_2_
  67.7 0.0 collective-permute-done.10.refs_3_
  67.7 0.0 copy-start
  67.7 0.2 shard_map.113
  67.9 1.3 %collective-permute-start.12 = (bf16[1024,128]{1,0:T(8,128)(2,1)S(1)}, bf16[1024,128]{1,0:T(8,128)(2,1)S(1)}, u32[]{:S(2)}, u32[]{:S(2)}) collective-permute-start(bf16[1024,128]{1,0:T(8,128)(2,1)S(1)} %get-tuple-element.105), channel_id=1, source_target_pairs={{0,2},{1,3},{2,0},{3,1},{4,6},{5,7},{6,4},{7,5},{8,10},{9,11},{10,... | collective-permute-start | bytes 786440 | tf_op jit(solution)/shard_map/ppermute | solution.py:24
  69.2 1.5 %collective-permute-start.13 = (bf16[1024,128]{1,0:T(8,128)(2,1)S(1)}, bf16[1024,128]{1,0:T(8,128)(2,1)S(1)}, u32[]{:S(2)}, u32[]{:S(2)}) collective-permute-start(bf16[1024,128]{1,0:T(8,128)(2,1)S(1)} %get-tuple-element.106), channel_id=1, source_target_pairs={{0,1},{1,0},{2,3},{3,2},{4,5},{5,4},{6,7},{7,6},{8,9},{9,8},{10,11... | collective-permute-start | bytes 786440 | tf_op jit(solution)/shard_map/ppermute | solution.py:24
  70.7 0.0 collective-permute-start.8
  70.7 0.0 collective-permute-done.11.refs_1_
  70.7 0.1 shard_map.115
  70.8 1.0 collective-permute-start.15
  71.9 0.0 collective-permute-done.7.refs_7_
  71.9 1.5 %collective-permute-start.14 = (bf16[2304,128]{1,0:T(8,128)(2,1)S(1)}, bf16[2304,128]{1,0:T(8,128)(2,1)S(1)}, u32[]{:S(2)}, u32[]{:S(2)}) collective-permute-start(bf16[2304,128]{1,0:T(8,128)(2,1)S(1)} %get-tuple-element.103), channel_id=1, source_target_pairs={{0,1},{1,0},{2,3},{3,2},{4,5},{5,4},{6,7},{7,6},{8,9},{9,8},{10,11... | collective-permute-start | bytes 1769480 | tf_op jit(solution)/shard_map/ppermute | solution.py:24
  73.4 0.0 copy-done
  73.4 2.6 %shard_map.112 = bf16[8,32,1024]{2,1,0:T(8,128)(2,1)} custom-call(s32[1]{0:T(128)} %bitcast.refs_0_.pos_ref._, s32[2,4]{1,0:T(2,128)} %bitcast.39, s32[2]{0:T(128)} %bitcast.46, bf16[2,256,1024]{2,1,0:T(8,128)(2,1)S(1)} %bitcast.20, bf16[1,256,1024]{2,1,0:T(8,128)(2,1)S(1)} %bitcast.22, bf16[1,256,1024]{2,1,0:T(8,128)(2,1)S(1)} %bitcast.24, ...), custom_call_target="tpu_custom_call" | custom-call | flops 40000000000 | bytes 1000 | tf_op jit(solution)/shard_map/pallas_call | solution.py:503
  76.0 0.0 collective-permute-done.12.refs_2_.refs_10_
  76.0 1.3 %collective-permute-done.13.refs_3_.refs_12_ = bf16[1024,128]{1,0:T(8,128)(2,1)S(1)} collective-permute-done((bf16[1024,128]{1,0:T(8,128)(2,1)S(1)}, bf16[1024,128]{1,0:T(8,128)(2,1)S(1)}, u32[]{:S(2)}, u32[]{:S(2)}) %collective-permute-start.13) | collective-permute-done | bytes 262176 | tf_op jit(solution)/shard_map/ppermute | solution.py:24
  77.3 0.1 shard_map.116
  77.4 6.1 %collective-permute-done.8.refs_0_ = bf16[512,512]{1,0:T(8,128)(2,1)S(1)} collective-permute-done((bf16[512,512]{1,0:T(8,128)(2,1)S(1)}, bf16[512,512]{1,0:T(8,128)(2,1)S(1)}, u32[]{:S(2)}, u32[]{:S(2)}) %collective-permute-start.8) | collective-permute-done | bytes 524320 | tf_op jit(solution)/shard_map/ppermute | solution.py:34
  83.5 3.5 %collective-permute-done.15.refs_3_ = bf16[2304,128]{1,0:T(8,128)(2,1)S(1)} collective-permute-done((bf16[2304,128]{1,0:T(8,128)(2,1)S(1)}, bf16[2304,128]{1,0:T(8,128)(2,1)S(1)}, u32[]{:S(2)}, u32[]{:S(2)}) %collective-permute-start.15) | collective-permute-done | bytes 589856 | tf_op jit(solution)/shard_map/ppermute | solution.py:24
  86.9 1.3 %collective-permute-done.14.refs_2_ = bf16[2304,128]{1,0:T(8,128)(2,1)S(1)} collective-permute-done((bf16[2304,128]{1,0:T(8,128)(2,1)S(1)}, bf16[2304,128]{1,0:T(8,128)(2,1)S(1)}, u32[]{:S(2)}, u32[]{:S(2)}) %collective-permute-start.14) | collective-permute-done | bytes 589856 | tf_op jit(solution)/shard_map/ppermute | solution.py:24
  88.2 0.3 shard_map.117
  88.5 0.8 collective-permute-start.16
  89.3 1.2 %collective-permute-start.17 = (bf16[1280,128]{1,0:T(8,128)(2,1)S(1)}, bf16[1280,128]{1,0:T(8,128)(2,1)S(1)}, u32[]{:S(2)}, u32[]{:S(2)}) collective-permute-start(bf16[1280,128]{1,0:T(8,128)(2,1)S(1)} %get-tuple-element.113), channel_id=1, source_target_pairs={{0,1},{1,0},{2,3},{3,2},{4,5},{5,4},{6,7},{7,6},{8,9},{9,8},{10,11... | collective-permute-start | bytes 983048 | tf_op jit(solution)/shard_map/ppermute | solution.py:24
  90.6 0.0 collective-permute-start.19
  90.6 6.0 %collective-permute-done.16.refs_2_.got_x_ref.refs_14_ = bf16[1280,128]{1,0:T(8,128)(2,1)S(1)} collective-permute-done((bf16[1280,128]{1,0:T(8,128)(2,1)S(1)}, bf16[1280,128]{1,0:T(8,128)(2,1)S(1)}, u32[]{:S(2)}, u32[]{:S(2)}) %collective-permute-start.16) | collective-permute-done | bytes 327712 | tf_op jit(solution)/shard_map/ppermute | solution.py:24
  96.6 1.3 %collective-permute-done.17.refs_3_.got_y_ref.refs_16_ = bf16[1280,128]{1,0:T(8,128)(2,1)S(1)} collective-permute-done((bf16[1280,128]{1,0:T(8,128)(2,1)S(1)}, bf16[1280,128]{1,0:T(8,128)(2,1)S(1)}, u32[]{:S(2)}, u32[]{:S(2)}) %collective-permute-start.17) | collective-permute-done | bytes 327712 | tf_op jit(solution)/shard_map/ppermute | solution.py:24
  97.9 0.1 shard_map.118
  97.9 0.1 collective-permute-start.20
  98.1 1.6 %shard_map.120 = bf16[512,1024]{1,0:T(8,128)(2,1)S(1)} custom-call(s32[1]{0:T(128)} %bitcast.refs_0_.pos_ref._, s32[2,4]{1,0:T(2,128)} %bitcast.40, s32[2]{0:T(128)} %bitcast.47, bf16[8,64,512]{2,1,0:T(8,128)(2,1)} %bitcast.30, bf16[64,1024]{1,0:T(8,128)(2,1)S(1)} %shard_map.119.refs_4_.lowrank_ref, f32[1024,256]{1,0:T(8,128)S(1)} %get-tuple-element.81.refs_0_.refs_5_, ...), custom_call_target="tpu_custom_call" | custom-call | flops 1000 | bytes 1000 | tf_op jit(solution)/shard_map/pallas_call | solution.py:590
  99.6 1.1 collective-permute-start.18
  100.7 3.0 %shard_map.122 = bf16[8,64,512]{2,1,0:T(8,128)(2,1)} custom-call(s32[1]{0:T(128)} %bitcast.refs_0_.pos_ref._, s32[2,4]{1,0:T(2,128)} %bitcast.41, s32[2]{0:T(128)} %bitcast.48, bf16[2,512,512]{2,1,0:T(8,128)(2,1)} %bitcast.49, bf16[64,1024]{1,0:T(8,128)(2,1)S(1)} %shard_map.119.refs_4_.lowrank_ref), custom_call_target="tpu_custom_call" | custom-call | flops 40000000000 | bytes 1000 | tf_op jit(solution)/shard_map/pallas_call | solution.py:659
  103.7 0.0 collective-permute-done.19.refs_1_
  103.7 2.3 %collective-permute-done.20.refs_2_ = bf16[512,256]{1,0:T(8,128)(2,1)S(1)} collective-permute-done((bf16[512,256]{1,0:T(8,128)(2,1)S(1)}, bf16[512,256]{1,0:T(8,128)(2,1)S(1)}, u32[]{:S(2)}, u32[]{:S(2)}) %collective-permute-start.20) | collective-permute-done | bytes 262176 | tf_op jit(solution)/shard_map/ppermute | solution.py:34
  106.1 0.0 collective-permute-done.18.kept_ref
  106.1 1.3 %shard_map.121 = bf16[2,512,512]{2,1,0:T(8,128)(2,1)} custom-call(s32[1]{0:T(128)} %bitcast.refs_0_.pos_ref._, bf16[512,1024]{1,0:T(8,128)(2,1)S(1)} %collective-permute-done.18.kept_ref, bf16[512,512]{1,0:T(8,128)(2,1)S(1)} %collective-permute-done.8.refs_0_, bf16[512,256]{1,0:T(8,128)(2,1)S(1)} %collective-permute-done.19.refs_1_, ...), custom_call_target="tpu_custom_call" | custom-call | flops 1000 | bytes 1000 | tf_op jit(solution)/shard_map/pallas_call | solution.py:627
  (4 shorter events, 0.1 us)
Async XLA Ops:
  1.9 27.3 %collective-permute-start = (bf16[256,1024]{1,0:T(8,128)(2,1)S(1)}, bf16[256,1024]{1,0:T(8,128)(2,1)S(1)}, u32[]{:S(2)}, u32[]{:S(2)}) collective-permute-start(bf16[256,1024]{1,0:T(8,128)(2,1)S(1)} %get-tuple-element.115), channel_id=1, source_target_pairs={{0,8},{1,9},{2,10},{3,11},{4,12},{5,13},{6,14},{7,15},{8,0},{9,1},... | collective-permute-start | bytes 1572872 | tf_op jit(solution)/shard_map/ppermute | solution.py:24
  11.7 24.7 %collective-permute-start.3 = (bf16[2048,256]{1,0:T(8,128)(2,1)S(1)}, bf16[2048,256]{1,0:T(8,128)(2,1)S(1)}, u32[]{:S(2)}, u32[]{:S(2)}) collective-permute-start(bf16[2048,256]{1,0:T(8,128)(2,1)S(1)} %get-tuple-element.65), channel_id=1, source_target_pairs={{0,2},{1,3},{2,0},{3,1},{4,6},{5,7},{6,4},{7,5},{8,10},{9,11},{10,... | collective-permute-start | bytes 3145736 | tf_op jit(solution)/shard_map/ppermute | solution.py:24
  13.3 25.7 %collective-permute-start.2 = (bf16[2176,256]{1,0:T(8,128)(2,1)S(1)}, bf16[2176,256]{1,0:T(8,128)(2,1)S(1)}, u32[]{:S(2)}, u32[]{:S(2)}) collective-permute-start(bf16[2176,256]{1,0:T(8,128)(2,1)S(1)} %get-tuple-element.64), channel_id=1, source_target_pairs={{0,1},{1,0},{2,3},{3,2},{4,5},{5,4},{6,7},{7,6},{8,9},{9,8},{10,11... | collective-permute-start | bytes 3342344 | tf_op jit(solution)/shard_map/ppermute | solution.py:24
  29.2 25.2 %collective-permute-start.1 = (bf16[256,1024]{1,0:T(8,128)(2,1)S(1)}, bf16[256,1024]{1,0:T(8,128)(2,1)S(1)}, u32[]{:S(2)}, u32[]{:S(2)}) collective-permute-start(bf16[256,1024]{1,0:T(8,128)(2,1)S(1)} %get-tuple-element.62), channel_id=1, source_target_pairs={{0,8},{1,9},{2,10},{3,11},{4,12},{5,13},{6,14},{7,15},{8,0},{9,1},... | collective-permute-start | bytes 1572872 | tf_op jit(solution)/shard_map/ppermute | solution.py:24
  39.4 20.1 %collective-permute-start.5 = (bf16[1024,256]{1,0:T(8,128)(2,1)S(1)}, bf16[1024,256]{1,0:T(8,128)(2,1)S(1)}, u32[]{:S(2)}, u32[]{:S(2)}) collective-permute-start(bf16[1024,256]{1,0:T(8,128)(2,1)S(1)} %get-tuple-element.75), channel_id=1, source_target_pairs={{0,1},{1,0},{2,3},{3,2},{4,5},{5,4},{6,7},{7,6},{8,9},{9,8},{10,11... | collective-permute-start | bytes 1572872 | tf_op jit(solution)/shard_map/ppermute | solution.py:24
  41.0 18.5 %collective-permute-start.4 = (bf16[1152,256]{1,0:T(8,128)(2,1)S(1)}, bf16[1152,256]{1,0:T(8,128)(2,1)S(1)}, u32[]{:S(2)}, u32[]{:S(2)}) collective-permute-start(bf16[1152,256]{1,0:T(8,128)(2,1)S(1)} %get-tuple-element.74), channel_id=1, source_target_pairs={{0,2},{1,3},{2,0},{3,1},{4,6},{5,7},{6,4},{7,5},{8,10},{9,11},{10,... | collective-permute-start | bytes 1769480 | tf_op jit(solution)/shard_map/ppermute | solution.py:24
  41.5 26.2 %collective-permute-start.9 = (bf16[2048,128]{1,0:T(8,128)(2,1)S(1)}, bf16[2048,128]{1,0:T(8,128)(2,1)S(1)}, u32[]{:S(2)}, u32[]{:S(2)}) collective-permute-start(bf16[2048,128]{1,0:T(8,128)(2,1)S(1)} %get-tuple-element.94), channel_id=1, source_target_pairs={{0,1},{1,0},{2,3},{3,2},{4,5},{5,4},{6,7},{7,6},{8,9},{9,8},{10,11... | collective-permute-start | bytes 1572872 | tf_op jit(solution)/shard_map/ppermute | solution.py:24
  42.0 25.7 %collective-permute-start.10 = (bf16[2048,128]{1,0:T(8,128)(2,1)S(1)}, bf16[2048,128]{1,0:T(8,128)(2,1)S(1)}, u32[]{:S(2)}, u32[]{:S(2)}) collective-permute-start(bf16[2048,128]{1,0:T(8,128)(2,1)S(1)} %get-tuple-element.96), channel_id=1, source_target_pairs={{0,2},{1,3},{2,0},{3,1},{4,6},{5,7},{6,4},{7,5},{8,10},{9,11},{10,... | collective-permute-start | bytes 1572872 | tf_op jit(solution)/shard_map/ppermute | solution.py:24
  59.6 5.0 %collective-permute-start.6 = (bf16[256,256]{1,0:T(8,128)(2,1)S(1)}, bf16[256,256]{1,0:T(8,128)(2,1)S(1)}, u32[]{:S(2)}, u32[]{:S(2)}) collective-permute-start(bf16[256,256]{1,0:T(8,128)(2,1)S(1)} %shard_map.110), channel_id=1, source_target_pairs={{0,4},{1,5},{2,6},{3,7},{4,0},{5,1},{6,2},{7,3},{8,12},{9,13},{10,... | collective-permute-start | bytes 393224 | tf_op jit(solution)/shard_map/ppermute | solution.py:24
  64.7 6.0 %collective-permute-start.11 = (bf16[128,256]{1,0:T(8,128)(2,1)S(1)}, bf16[128,256]{1,0:T(8,128)(2,1)S(1)}, u32[]{:S(2)}, u32[]{:S(2)}) collective-permute-start(bf16[128,256]{1,0:T(8,128)(2,1)S(1)} %get-tuple-element.87), channel_id=1, source_target_pairs={{0,8},{1,9},{2,10},{3,11},{4,12},{5,13},{6,14},{7,15},{8,0},{9,1},... | collective-permute-start | bytes 196616 | tf_op jit(solution)/shard_map/ppermute | solution.py:24
  65.2 6.7 %collective-permute-start.7 = (bf16[64,256]{1,0:T(8,128)(2,1)S(1)}, bf16[64,256]{1,0:T(8,128)(2,1)S(1)}, u32[]{:S(2)}, u32[]{:S(2)}) collective-permute-start(bf16[64,256]{1,0:T(8,128)(2,1)S(1)} %get-tuple-element.88), channel_id=1, source_target_pairs={{0,8},{1,9},{2,10},{3,11},{4,12},{5,13},{6,14},{7,15},{8,0},{9,1},... | collective-permute-start | bytes 98312 | tf_op jit(solution)/shard_map/ppermute | solution.py:24
  67.7 5.7 %copy-start = (bf16[1,1,2,256,1024]{4,3,2,1,0:T(8,128)(2,1)S(1)}, bf16[1,1,2,256,1024]{4,3,2,1,0:T(8,128)(2,1)}, u32[]{:S(2)}) copy-start(bf16[1,1,2,256,1024]{4,3,2,1,0:T(8,128)(2,1)} %param.8) | copy-start | bytes 3145732
  67.9 8.1 %collective-permute-start.12 = (bf16[1024,128]{1,0:T(8,128)(2,1)S(1)}, bf16[1024,128]{1,0:T(8,128)(2,1)S(1)}, u32[]{:S(2)}, u32[]{:S(2)}) collective-permute-start(bf16[1024,128]{1,0:T(8,128)(2,1)S(1)} %get-tuple-element.105), channel_id=1, source_target_pairs={{0,2},{1,3},{2,0},{3,1},{4,6},{5,7},{6,4},{7,5},{8,10},{9,11},{10,... | collective-permute-start | bytes 786440 | tf_op jit(solution)/shard_map/ppermute | solution.py:24
  69.2 8.1 %collective-permute-start.13 = (bf16[1024,128]{1,0:T(8,128)(2,1)S(1)}, bf16[1024,128]{1,0:T(8,128)(2,1)S(1)}, u32[]{:S(2)}, u32[]{:S(2)}) collective-permute-start(bf16[1024,128]{1,0:T(8,128)(2,1)S(1)} %get-tuple-element.106), channel_id=1, source_target_pairs={{0,1},{1,0},{2,3},{3,2},{4,5},{5,4},{6,7},{7,6},{8,9},{9,8},{10,11... | collective-permute-start | bytes 786440 | tf_op jit(solution)/shard_map/ppermute | solution.py:24
  70.7 12.8 %collective-permute-start.8 = (bf16[512,512]{1,0:T(8,128)(2,1)S(1)}, bf16[512,512]{1,0:T(8,128)(2,1)S(1)}, u32[]{:S(2)}, u32[]{:S(2)}) collective-permute-start(bf16[512,512]{1,0:T(8,128)(2,1)S(1)} %get-tuple-element.89), channel_id=1, source_target_pairs={{0,20},{1,21},{2,22},{3,23},{4,16},{5,17},{6,18},{7,19},{8,28},{9,... | collective-permute-start | bytes 1572872 | tf_op jit(solution)/shard_map/ppermute | solution.py:34
  70.8 16.1 %collective-permute-start.15 = (bf16[2304,128]{1,0:T(8,128)(2,1)S(1)}, bf16[2304,128]{1,0:T(8,128)(2,1)S(1)}, u32[]{:S(2)}, u32[]{:S(2)}) collective-permute-start(bf16[2304,128]{1,0:T(8,128)(2,1)S(1)} %get-tuple-element.108), channel_id=1, source_target_pairs={{0,2},{1,3},{2,0},{3,1},{4,6},{5,7},{6,4},{7,5},{8,10},{9,11},{10,... | collective-permute-start | bytes 1769480 | tf_op jit(solution)/shard_map/ppermute | solution.py:24
  71.9 16.3 %collective-permute-start.14 = (bf16[2304,128]{1,0:T(8,128)(2,1)S(1)}, bf16[2304,128]{1,0:T(8,128)(2,1)S(1)}, u32[]{:S(2)}, u32[]{:S(2)}) collective-permute-start(bf16[2304,128]{1,0:T(8,128)(2,1)S(1)} %get-tuple-element.103), channel_id=1, source_target_pairs={{0,1},{1,0},{2,3},{3,2},{4,5},{5,4},{6,7},{7,6},{8,9},{9,8},{10,11... | collective-permute-start | bytes 1769480 | tf_op jit(solution)/shard_map/ppermute | solution.py:24
  88.5 8.1 %collective-permute-start.16 = (bf16[1280,128]{1,0:T(8,128)(2,1)S(1)}, bf16[1280,128]{1,0:T(8,128)(2,1)S(1)}, u32[]{:S(2)}, u32[]{:S(2)}) collective-permute-start(bf16[1280,128]{1,0:T(8,128)(2,1)S(1)} %get-tuple-element.112), channel_id=1, source_target_pairs={{0,2},{1,3},{2,0},{3,1},{4,6},{5,7},{6,4},{7,5},{8,10},{9,11},{10,... | collective-permute-start | bytes 983048 | tf_op jit(solution)/shard_map/ppermute | solution.py:24
  89.3 8.5 %collective-permute-start.17 = (bf16[1280,128]{1,0:T(8,128)(2,1)S(1)}, bf16[1280,128]{1,0:T(8,128)(2,1)S(1)}, u32[]{:S(2)}, u32[]{:S(2)}) collective-permute-start(bf16[1280,128]{1,0:T(8,128)(2,1)S(1)} %get-tuple-element.113), channel_id=1, source_target_pairs={{0,1},{1,0},{2,3},{3,2},{4,5},{5,4},{6,7},{7,6},{8,9},{9,8},{10,11... | collective-permute-start | bytes 983048 | tf_op jit(solution)/shard_map/ppermute | solution.py:24
  90.6 13.1 %collective-permute-start.19 = (bf16[512,256]{1,0:T(8,128)(2,1)S(1)}, bf16[512,256]{1,0:T(8,128)(2,1)S(1)}, u32[]{:S(2)}, u32[]{:S(2)}) collective-permute-start(bf16[512,256]{1,0:T(8,128)(2,1)S(1)} %shard_map.116), channel_id=1, source_target_pairs={{0,20},{1,21},{2,22},{3,23},{4,16},{5,17},{6,18},{7,19},{8,28},{9,... | collective-permute-start | bytes 786440 | tf_op jit(solution)/shard_map/ppermute | solution.py:34
  97.9 8.1 %collective-permute-start.20 = (bf16[512,256]{1,0:T(8,128)(2,1)S(1)}, bf16[512,256]{1,0:T(8,128)(2,1)S(1)}, u32[]{:S(2)}, u32[]{:S(2)}) collective-permute-start(bf16[512,256]{1,0:T(8,128)(2,1)S(1)} %shard_map.118), channel_id=1, source_target_pairs={{0,20},{1,21},{2,22},{3,23},{4,16},{5,17},{6,18},{7,19},{8,28},{9,... | collective-permute-start | bytes 786440 | tf_op jit(solution)/shard_map/ppermute | solution.py:34
  99.6 6.4 %collective-permute-start.18 = (bf16[512,1024]{1,0:T(8,128)(2,1)S(1)}, bf16[512,1024]{1,0:T(8,128)(2,1)S(1)}, u32[]{:S(2)}, u32[]{:S(2)}) collective-permute-start(bf16[512,1024]{1,0:T(8,128)(2,1)S(1)} %shard_map.120), channel_id=1, source_target_pairs={{0,16},{1,17},{2,18},{3,19},{4,20},{5,21},{6,22},{7,23},{8,24},{9,... | collective-permute-start | bytes 3145736 | tf_op jit(solution)/shard_map/ppermute | solution.py:34

commit v17 on v16

--- a/solution.py
+++ b/solution.py
@@ -358,8 +358,7 @@
         (after(kept_x, part), kept_y), (first_x, first_y), placed
     )
     second_x, second_y = partner(sent_x, 2), partner(sent_y, 1)
-    c_first_x = partner(after(c_sent_x, sent_x, sent_y), 1)
-    c_first_y = partner(after(c_sent_y, sent_x, sent_y), 2)
+    c_first_x, c_first_y = partner(c_sent_x, 1), partner(c_sent_y, 2)
 
     fetched = fetch(after(scalars[0], sent_x, sent_y), weight_blocks, low_size)
 
@@ -369,10 +368,6 @@
         got1, pieces_of(1), False, True, True, LONG, None, fetched
     )
     parts.append(part)
-    own_third, placed = last_parts((after(kept_x, part), kept_y), (second_x, second_y), placed)
-    own_last = relay(own_third, 4)
-    own_sums = (kept_x, second_x), (kept_y, second_y)
-
     rows_total = len(order) * size
     blocks = rows_total // tile_rows
 
@@ -390,50 +385,31 @@
     whole_parts = [(at, start) for at, part in enumerate(parts) for start in range(0, part.shape[1], tile_rows)]
 
     def collect_kernel(_, *refs):
-        *part_refs, placed_ref, out_ref = refs
         for block, (at, start) in enumerate(whole_parts):
-            out_ref[block * rank_part : (block + 1) * rank_part, :] = part_refs[at][
+            refs[-1][block * rank_part : (block + 1) * rank_part, :] = refs[at][
                 :, start : start + tile_rows
             ].astype(BF16)
-        out_ref[blocks * rank_part :, :] = placed_ref[...]
 
     message = blocks * rank_part, tile_rows
-    (shared,) = small(
-        collect_kernel, [((message[0] + placed.shape[0], tile_rows), BF16)], *parts, placed
-    )
+    (shared,) = small(collect_kernel, [(message, BF16)], *parts)
+    (c_sent_x, c_sent_y), c_kept = halve(
+        (after(c_kept_x, part), c_kept_y), (c_first_x, c_first_y)
+    )
+    c_second_x, c_second_y = partner(c_sent_x, 2), partner(c_sent_y, 1)
+
     near = partner(shared, 4)
 
-    (c_sent_x, c_sent_y), c_kept = halve(
-        (after(c_kept_x, shared), c_kept_y), (c_first_x, c_first_y)
-    )
-    c_second_x, c_second_y = partner(c_sent_x, 2), partner(c_sent_y, 1)
-
-    def near_kernel(pos_ref, *refs):
-        count = len(parts)
-        part_refs, placed_ref, near_ref = refs[:count], refs[count], refs[count + 1]
-        shared_ref, total_ref, out_ref, *far_refs, wide_ref = refs[count + 2 :]
+
+    def near_kernel(_, *refs):
+        near_ref, shared_ref, total_ref = refs[-3:]
         for block, (at, start) in enumerate(whole_parts):
             rows = slice(block * rank_part, (block + 1) * rank_part)
-            total = part_refs[at][:, start : start + tile_rows] + near_ref[rows, :].astype(F32)
+            total = refs[at][:, start : start + tile_rows] + near_ref[rows, :].astype(F32)
             total_ref[rows, :] = total
             shared_ref[rows, :] = total.astype(BF16)
-        out_ref[...] = placed_ref[...] + near_ref[blocks * rank_part :, :]
-        wide_ref[...] = out_ref[...].astype(F32)
-        for k, far_ref in enumerate(far_refs, 1):
-            for m in range(micro_count):
-                start = m * rank + ((pos_ref[0] // low_size) ^ k) * rank_part
-                far_ref[m * rank_part : (m + 1) * rank_part, :] = wide_ref[
-                    pl.ds(pl.multiple_of(start, rank_part), rank_part), :
-                ].astype(BF16)
-
-    shared, total, placed, *wanted = small(
-        near_kernel,
-        [(message, BF16), (message, F32), (placed.shape, BF16)]
-        + [((micro_count * rank_part, tile_rows), BF16)] * (high_size - 1),
-        *parts,
-        placed,
-        near,
-        scratch=[pltpu.VMEM(placed.shape, F32)],
+
+    shared, total = small(
+        near_kernel, [(message, BF16), (message, F32)], *parts[:-1], after(parts[-1], c_sent_x), near
     )
     far = [partner(shared, k * low_size) for k in range(1, high_size)]
 
@@ -455,10 +431,6 @@
 
     (lowrank,) = small(lowrank_kernel, [((rank, rows_total), F32)], total, *far)
 
-    hiddens = [placed] + [
-        partner(after(w, shared), k * low_size) for k, w in enumerate(wanted, 1)
-    ]
-
     halves = [range(0, len(order) // 2), range(len(order) // 2, len(order))]
 
     def riders(way, count):
@@ -492,9 +464,80 @@
         [((2 * half_rows + riding(way, n), n), BF16) for way, n in enumerate(d_counts)],
         d_sent_x,
         d_sent_y,
-        after(lowrank, *c_kept),
+        after(lowrank, c_second_x, c_second_y),
     )
     d_first_x, d_first_y = partner(d_sent_x, 1), partner(d_sent_y, 2)
+
+    own_third, placed = last_parts(
+        (after(kept_x, d_sent_x), kept_y), (second_x, second_y), placed, LONG
+    )
+    own_last = relay(own_third, 4)
+    own_sums = (kept_x, second_x), (kept_y, second_y)
+
+    def hidden_kernel(pos_ref, placed_ref, near_ref, out_ref, *refs):
+        *far_refs, wide_ref = refs
+        out_ref[...] = placed_ref[...] + near_ref[...]
+        wide_ref[...] = out_ref[...].astype(F32)
+        for k, far_ref in enumerate(far_refs, 1):
+            for m in range(micro_count):
+                start = m * rank + ((pos_ref[0] // low_size) ^ k) * rank_part
+                far_ref[m * rank_part : (m + 1) * rank_part, :] = wide_ref[
+                    pl.ds(pl.multiple_of(start, rank_part), rank_part), :
+                ].astype(BF16)
+
+    placed, *wanted = small(
+        hidden_kernel,
+        [(placed.shape, BF16)]
+        + [((micro_count * rank_part, tile_rows), BF16)] * (high_size - 1),
+        placed,
+        partner(placed, 4),
+        scratch=[pltpu.VMEM(placed.shape, F32)],
+    )
+    hiddens = [placed] + [partner(w, k * low_size) for k, w in enumerate(wanted, 1)]
+
+    (c_third,) = last_parts((after(c_kept[0], d_sent_x), c_kept[1]), (c_second_x, c_second_y))
+    c_last = relay(c_third, 4)
+
+    def third_kernel(_, *refs):
+        lowrank_ref, next_ref = refs[4], refs[9]
+        for way in range(2):
+            kept_ref, got_ref, sent_ref, rest_ref = refs[way], refs[2 + way], refs[5 + way], refs[7 + way]
+            half = kept_ref.shape[0] // 2
+            sent_ref[:half, :] = (
+                kept_ref[half:, :] + got_ref[half : 2 * half, :].astype(F32)
+            ).astype(BF16)
+            rest_ref[...] = kept_ref[:half, :] + got_ref[:half, :].astype(F32)
+            arrive(got_ref, 2 * half, way, lowrank_ref, next_ref)
+            ride(sent_ref, half, way, next_ref)
+
+    d_sent_x, d_sent_y, *d_kept, lowrank = small(
+        third_kernel,
+        [((half_rows + riding(way, n), n), BF16) for way, n in enumerate(d_counts)]
+        + [((half_rows, n), F32) for n in d_counts]
+        + [((rank, rows_total), F32)],
+        d_kept_x,
+        after(d_kept_y, own_last, c_third),
+        d_first_x,
+        d_first_y,
+        lowrank,
+    )
+    d_second_x, d_second_y = partner(d_sent_x, 2), partner(d_sent_y, 1)
+    (d_third,) = last_parts(
+        (after(d_kept[0], *hiddens), d_kept[1]), (d_second_x, d_second_y)
+    )
+    d_last = relay(d_third, 4)
+
+    def whole_kernel(_, lowrank_ref, got_x_ref, got_y_ref, out_ref):
+        for way, got_ref in enumerate((got_x_ref, got_y_ref)):
+            arrive(got_ref, half_rows, way, lowrank_ref, out_ref)
+
+    (lowrank,) = small(
+        whole_kernel,
+        [((rank, rows_total), BF16)],
+        after(lowrank, d_third),
+        d_second_x,
+        d_second_y,
+    )
 
     all_grads, all_pieces = [], []
     for grads, pieces in chunks:
@@ -509,50 +552,8 @@
         out_shape=jax.ShapeDtypeStruct(up_tile.shape, BF16),
         scratch_shapes=[pltpu.VMEM(up_tile.shape, F32)],
         compiler_params=PARAMS,
-        cost_estimate=LONG,
-    )(*in_hbm(*scalars), *all_grads, *hiddens)
-
-    (c_third,) = last_parts((after(c_kept[0], d_sent_x), c_kept[1]), (c_second_x, c_second_y))
-    c_last = relay(c_third, 4)
-
-    def third_kernel(_, *refs):
-        lowrank_ref, next_ref = refs[4], refs[9]
-        for way in range(2):
-            kept_ref, got_ref, sent_ref, rest_ref = refs[way], refs[2 + way], refs[5 + way], refs[7 + way]
-            half = kept_ref.shape[0] // 2
-            sent_ref[:half, :] = (
-                kept_ref[half:, :] + got_ref[half : 2 * half, :].astype(F32)
-            ).astype(BF16)
-            rest_ref[...] = kept_ref[:half, :] + got_ref[:half, :].astype(F32)
-            arrive(got_ref, 2 * half, way, lowrank_ref, next_ref)
-            ride(sent_ref, half, way, next_ref)
-
-    d_sent_x, d_sent_y, *d_kept, lowrank = small(
-        third_kernel,
-        [((half_rows + riding(way, n), n), BF16) for way, n in enumerate(d_counts)]
-        + [((half_rows, n), F32) for n in d_counts]
-        + [((rank, rows_total), F32)],
-        d_kept_x,
-        after(d_kept_y, up_map_gradient, own_last, c_third),
-        d_first_x,
-        d_first_y,
-        lowrank,
-    )
-    d_second_x, d_second_y = partner(d_sent_x, 2), partner(d_sent_y, 1)
-    (d_third,) = last_parts(d_kept, (d_second_x, d_second_y))
-    d_last = relay(d_third, 4)
-
-    def whole_kernel(_, lowrank_ref, got_x_ref, got_y_ref, out_ref):
-        for way, got_ref in enumerate((got_x_ref, got_y_ref)):
-            arrive(got_ref, half_rows, way, lowrank_ref, out_ref)
-
-    (lowrank,) = small(
-        whole_kernel,
-        [((rank, rows_total), BF16)],
-        after(lowrank, d_third),
-        d_second_x,
-        d_second_y,
-    )
+        cost_estimate=QUICK,
+    )(*in_hbm(*scalars), *all_grads, after(hiddens[0], d_third), *hiddens[1:])
 
     down = adapter_down_maps[0]
 
@@ -623,6 +624,34 @@
         for copy in copies:
             copy.wait()
 
+    def down_kernel(pos_ref, classes_ref, live_ref, inputs_ref, lowrank_ref, out_ref, total_ref):
+        own = pos_ref[0] // low_size
+        total_ref[...] = jnp.zeros_like(total_ref)
+        for at, piece in enumerate(order):
+            k, m, offset = piece
+            seg = segment_of(own, piece, tile_rows)
+
+            @pl.when(seg < live_ref[m])
+            def _():
+                base = pl.multiple_of((own ^ k) * tile_rows + offset, size)
+                total_ref[classes_ref[m, seg]] += jnp.dot(
+                    lowrank_ref[:, at * size : (at + 1) * size],
+                    inputs_ref[m, pl.ds(base, size), :],
+                    preferred_element_type=F32,
+                )
+
+        out_ref[...] = total_ref[...].astype(BF16)
+
+    down_map_gradient = pl.pallas_call(
+        down_kernel,
+        in_specs=[SMEM] * 3 + [VMEM] * 2,
+        out_specs=VMEM,
+        out_shape=jax.ShapeDtypeStruct(down.shape, BF16),
+        scratch_shapes=[pltpu.VMEM(down.shape, F32)],
+        compiler_params=PARAMS,
+        cost_estimate=LONG,
+    )(*in_hbm(*scalars, forward_input[0]), lowrank)
+
     got = [own_last, c_last, d_last]
     grad_prev = pl.pallas_call(
         finish_kernel,
@@ -636,35 +665,7 @@
         ],
         compiler_params=PARAMS,
         cost_estimate=QUICK,
-    )(*in_hbm(scalars[0]), kept, *got)
-
-    def down_kernel(pos_ref, classes_ref, live_ref, inputs_ref, lowrank_ref, out_ref, total_ref):
-        own = pos_ref[0] // low_size
-        total_ref[...] = jnp.zeros_like(total_ref)
-        for at, piece in enumerate(order):
-            k, m, offset = piece
-            seg = segment_of(own, piece, tile_rows)
-
-            @pl.when(seg < live_ref[m])
-            def _():
-                base = pl.multiple_of((own ^ k) * tile_rows + offset, size)
-                total_ref[classes_ref[m, seg]] += jnp.dot(
-                    lowrank_ref[:, at * size : (at + 1) * size],
-                    inputs_ref[m, pl.ds(base, size), :],
-                    preferred_element_type=F32,
-                )
-
-        out_ref[...] = total_ref[...].astype(BF16)
-
-    down_map_gradient = pl.pallas_call(
-        down_kernel,
-        in_specs=[SMEM] * 3 + [VMEM] * 2,
-        out_specs=VMEM,
-        out_shape=jax.ShapeDtypeStruct(down.shape, BF16),
-        scratch_shapes=[pltpu.VMEM(down.shape, F32)],
-        compiler_params=PARAMS,
-        cost_estimate=LONG,
-    )(*in_hbm(*scalars, forward_input[0]), lowrank)
+    )(*in_hbm(after(scalars[0], up_map_gradient, down_map_gradient)), kept, *got)
 
     return (
         grad_prev[None],

time: 108 us -> 111 us (1.028)
  waiting for transfers between devices: 46.7 us -> 51.8 us
  starting transfers between devices: 22.9 us -> 21.6 us
    ppermute x4, waiting for transfers between devices: 8.45 us -> 15.5 us  [relay(): return lax.ppermute(value, ('pipe', 'tensor'), pairs)]
    ppermute x17 -> x18, waiting for transfers between devices: 38.3 us -> 36.4 us  [partner(): return lax.ppermute(value, 'tensor', pairs)]
    ppermute x17 -> x18, starting transfers between devices: 21.8 us -> 20.1 us  [partner(): return lax.ppermute(value, 'tensor', pairs)]
  transfers between devices with their start and end apart: 21 -> 22, of which waited for: 12 -> 9; matrix products, arithmetic and copies ran while one was open for 0% -> 0% of each run, Pallas kernels for 32% -> 30%
where the time goes in v17:
time: 111 us; the launch traced here: 110 us
  waiting for transfers between devices  51.8 us (47%)
  Pallas kernels  34.7 us (31%)
  starting transfers between devices  21.6 us (19%)
  local copies, waits for them, and re-layouts  1.28 us (1%)
    ppermute x18, waiting for transfers between devices, partner(): return lax.ppermute(value, 'tensor', pairs)  36.4 us
    pallas_call x4, Pallas kernels, product(): pl.pallas_call(functools.partial(product_body, low_size, tile_rows, piece...  22.1 us
    ppermute x18, starting transfers between devices, partner(): return lax.ppermute(value, 'tensor', pairs)  20.1 us
    ppermute x4, waiting for transfers between devices, relay(): return lax.ppermute(value, ('pipe', 'tensor'), pairs)  15.5 us
    pallas_call x1, Pallas kernels, fetch(): pl.pallas_call(functools.partial(fetch_kernel, low_size), in_specs=[SMEM,...  3.47 us
    pallas_call x1, Pallas kernels, shards(): pl.pallas_call(down_kernel, in_specs=[SMEM] * 3 + [VMEM] * 2, out_specs=V...  2.83 us
    pallas_call x1, Pallas kernels, shards(): pl.pallas_call(functools.partial(up_body, low_size, tile_rows, all_pieces...  2.27 us
  transfers between devices with their start and end apart: 22, of which 9 were waited for; matrix products, arithmetic and copies ran while one was open for 0% of the time, Pallas kernels for 30%

profile of v17, /device:TPU:0, one launch (start us, length us, event | category | flops | bytes accessed | tf_op | source)
XLA Modules:
  0.0 110.2 jit_solution(14289880321109118511)
XLA Ops:
  0.6 1.3 %slice_bitcast_fusion = (bf16[256,1024]{1,0:T(8,128)(2,1)S(1)}, bf16[256,1024]{1,0:T(8,128)(2,1)S(1)}) fusion(bf16[1,1,2,256,1024]{4,3,2,1,0:T(8,128)(2,1)} %param.8), kind=kLoop, calls=%fused_computation | loop fusion | bytes 2097152 | tf_op jit(solution)/shard_map/squeeze | solution.py:354
  1.9 4.1 %collective-permute-start = (bf16[256,1024]{1,0:T(8,128)(2,1)S(1)}, bf16[256,1024]{1,0:T(8,128)(2,1)S(1)}, u32[]{:S(2)}, u32[]{:S(2)}) collective-permute-start(bf16[256,1024]{1,0:T(8,128)(2,1)S(1)} %get-tuple-element.118), channel_id=1, source_target_pairs={{0,8},{1,9},{2,10},{3,11},{4,12},{5,13},{6,14},{7,15},{8,0},{9,1},... | collective-permute-start | bytes 1572872 | tf_op jit(solution)/shard_map/ppermute | solution.py:24
  6.0 5.7 %shard_map.103 = (bf16[2176,256]{1,0:T(8,128)(2,1)S(1)}, bf16[2048,256]{1,0:T(8,128)(2,1)S(1)}, bf16[128,256]{1,0:T(8,128)(2,1)S(1)}) custom-call(s32[1]{0:T(128)} %bitcast.refs_0_.pos_ref._, s32[2,4]{1,0:T(2,128)} %bitcast.36, s32[2]{0:T(128)} %bitcast.43, bf16[2,256,1024]{2,1,0:T(8,128)(2,1)} %bitcast.18, bf16[8,512,1024]{2,1,0:T(8,128)(2,1)} %bitcast.25, ...), custom_call_target="tpu_custom_call" | custom-call | flops 1000 | bytes 1000 | tf_op jit(solution)/shard_map/pallas_call | solution.py:144
  11.7 1.6 %collective-permute-start.3 = (bf16[2048,256]{1,0:T(8,128)(2,1)S(1)}, bf16[2048,256]{1,0:T(8,128)(2,1)S(1)}, u32[]{:S(2)}, u32[]{:S(2)}) collective-permute-start(bf16[2048,256]{1,0:T(8,128)(2,1)S(1)} %get-tuple-element.66), channel_id=1, source_target_pairs={{0,2},{1,3},{2,0},{3,1},{4,6},{5,7},{6,4},{7,5},{8,10},{9,11},{10,... | collective-permute-start | bytes 3145736 | tf_op jit(solution)/shard_map/ppermute | solution.py:24
  13.3 1.5 %collective-permute-start.2 = (bf16[2176,256]{1,0:T(8,128)(2,1)S(1)}, bf16[2176,256]{1,0:T(8,128)(2,1)S(1)}, u32[]{:S(2)}, u32[]{:S(2)}) collective-permute-start(bf16[2176,256]{1,0:T(8,128)(2,1)S(1)} %get-tuple-element.65), channel_id=1, source_target_pairs={{0,1},{1,0},{2,3},{3,2},{4,5},{5,4},{6,7},{7,6},{8,9},{9,8},{10,11... | collective-permute-start | bytes 3342344 | tf_op jit(solution)/shard_map/ppermute | solution.py:24
  14.8 5.8 %shard_map.104 = (f32[2048,256]{1,0:T(8,128)S(1)}, f32[2048,256]{1,0:T(8,128)S(1)}, f32[32,512]{1,0:T(8,128)S(1)}) custom-call(s32[1]{0:T(128)} %bitcast.refs_0_.pos_ref._, s32[2,4]{1,0:T(2,128)} %bitcast.37, s32[2]{0:T(128)} %bitcast.44, bf16[2,256,1024]{2,1,0:T(8,128)(2,1)} %bitcast.19, bf16[8,512,1024]{2,1,0:T(8,128)(2,1)} %bitcast.26, ...), custom_call_target="tpu_custom_call" | custom-call | flops 1000 | bytes 1000 | tf_op jit(solution)/shard_map/pallas_call | solution.py:144
  20.7 8.5 %collective-permute-done = bf16[256,1024]{1,0:T(8,128)(2,1)S(1)} collective-permute-done((bf16[256,1024]{1,0:T(8,128)(2,1)S(1)}, bf16[256,1024]{1,0:T(8,128)(2,1)S(1)}, u32[]{:S(2)}, u32[]{:S(2)}) %collective-permute-start) | collective-permute-done | bytes 524320 | tf_op jit(solution)/shard_map/ppermute | solution.py:24
  29.2 0.0 collective-permute-start.1
  29.2 5.9 %shard_map.105 = (bf16[2048,128]{1,0:T(8,128)(2,1)S(1)}, bf16[2048,128]{1,0:T(8,128)(2,1)S(1)}, f32[2048,128]{1,0:T(8,128)S(1)}, f32[2048,128]{1,0:T(8,128)S(1)}, f32[32,256]{1,0:T(8,128)S(1)}) custom-call(s32[1]{0:T(128)} %bitcast.refs_0_.pos_ref._, s32[2,4]{1,0:T(2,128)} %bitcast.38, s32[2]{0:T(128)} %bitcast.45, bf16[1,256,1024]{2,1,0:T(8,128)(2,1)S(1)} %bitcast.21, ...), custom_call_target="tpu_custom_call" | custom-call | flops 40000000000 | bytes 1000 | tf_op jit(solution)/shard_map/pallas_call | solution.py:144
  35.0 1.6 %collective-permute-start.4 = (bf16[2048,128]{1,0:T(8,128)(2,1)S(1)}, bf16[2048,128]{1,0:T(8,128)(2,1)S(1)}, u32[]{:S(2)}, u32[]{:S(2)}) collective-permute-start(bf16[2048,128]{1,0:T(8,128)(2,1)S(1)} %get-tuple-element.85), channel_id=1, source_target_pairs={{0,1},{1,0},{2,3},{3,2},{4,5},{5,4},{6,7},{7,6},{8,9},{9,8},{10,11... | collective-permute-start | bytes 1572872 | tf_op jit(solution)/shard_map/ppermute | solution.py:24
  36.6 1.5 %collective-permute-start.5 = (bf16[2048,128]{1,0:T(8,128)(2,1)S(1)}, bf16[2048,128]{1,0:T(8,128)(2,1)S(1)}, u32[]{:S(2)}, u32[]{:S(2)}) collective-permute-start(bf16[2048,128]{1,0:T(8,128)(2,1)S(1)} %get-tuple-element.86), channel_id=1, source_target_pairs={{0,2},{1,3},{2,0},{3,1},{4,6},{5,7},{6,4},{7,5},{8,10},{9,11},{10,... | collective-permute-start | bytes 1572872 | tf_op jit(solution)/shard_map/ppermute | solution.py:24
  38.2 0.0 collective-permute-done.3.refs_3_
  38.2 2.6 %collective-permute-done.2.refs_2_ = bf16[2176,256]{1,0:T(8,128)(2,1)S(1)} collective-permute-done((bf16[2176,256]{1,0:T(8,128)(2,1)S(1)}, bf16[2176,256]{1,0:T(8,128)(2,1)S(1)}, u32[]{:S(2)}, u32[]{:S(2)}) %collective-permute-start.2) | collective-permute-done | bytes 1114144 | tf_op jit(solution)/shard_map/ppermute | solution.py:24
  40.8 0.3 shard_map.106
  41.2 1.6 %collective-permute-start.11 = (bf16[1024,256]{1,0:T(8,128)(2,1)S(1)}, bf16[1024,256]{1,0:T(8,128)(2,1)S(1)}, u32[]{:S(2)}, u32[]{:S(2)}) collective-permute-start(bf16[1024,256]{1,0:T(8,128)(2,1)S(1)} %get-tuple-element.77), channel_id=1, source_target_pairs={{0,1},{1,0},{2,3},{3,2},{4,5},{5,4},{6,7},{7,6},{8,9},{9,8},{10,11... | collective-permute-start | bytes 1572872 | tf_op jit(solution)/shard_map/ppermute | solution.py:24
  42.7 0.0 collective-permute-start.10
  42.7 3.5 %shard_map.107.refs_4_ = bf16[8,512,1024]{2,1,0:T(8,128)(2,1)S(1)} custom-call(s32[1]{0:T(128)} %bitcast.refs_0_.pos_ref._, bf16[8,512,1024]{2,1,0:T(8,128)(2,1)} %bitcast.28), custom_call_target="tpu_custom_call" | custom-call | flops 1000 | bytes 1000 | tf_op jit(solution)/shard_map/pallas_call | solution.py:182
  46.2 8.2 %collective-permute-done.1 = bf16[256,1024]{1,0:T(8,128)(2,1)S(1)} collective-permute-done((bf16[256,1024]{1,0:T(8,128)(2,1)S(1)}, bf16[256,1024]{1,0:T(8,128)(2,1)S(1)}, u32[]{:S(2)}, u32[]{:S(2)}) %collective-permute-start.1) | collective-permute-done | bytes 524320 | tf_op jit(solution)/shard_map/ppermute | solution.py:24
  54.4 4.7 %shard_map.108 = (bf16[2048,128]{1,0:T(8,128)(2,1)S(1)}, bf16[2048,128]{1,0:T(8,128)(2,1)S(1)}, f32[2048,128]{1,0:T(8,128)S(1)}, f32[2048,128]{1,0:T(8,128)S(1)}, f32[32,256]{1,0:T(8,128)S(1)}) custom-call(s32[1]{0:T(128)} %bitcast.refs_0_.pos_ref._, s32[2,4]{1,0:T(2,128)} %bitcast.39, s32[2]{0:T(128)} %bitcast.46, bf16[1,256,1024]{2,1,0:T(8,128)(2,1)S(1)} %bitcast.23, ...), custom_call_target="tpu_custom_call" | custom-call | flops 40000000000 | bytes 1000 | tf_op jit(solution)/shard_map/pallas_call | solution.py:144
  59.1 0.0 collective-permute-done.4.refs_2_
  59.1 0.0 collective-permute-done.5.refs_3_
  59.1 0.2 shard_map.109
  59.3 1.3 %collective-permute-start.9 = (bf16[1024,128]{1,0:T(8,128)(2,1)S(1)}, bf16[1024,128]{1,0:T(8,128)(2,1)S(1)}, u32[]{:S(2)}, u32[]{:S(2)}) collective-permute-start(bf16[1024,128]{1,0:T(8,128)(2,1)S(1)} %get-tuple-element.91), channel_id=1, source_target_pairs={{0,1},{1,0},{2,3},{3,2},{4,5},{5,4},{6,7},{7,6},{8,9},{9,8},{10,11... | collective-permute-start | bytes 786440 | tf_op jit(solution)/shard_map/ppermute | solution.py:24
  60.6 1.5 %collective-permute-start.8 = (bf16[1024,128]{1,0:T(8,128)(2,1)S(1)}, bf16[1024,128]{1,0:T(8,128)(2,1)S(1)}, u32[]{:S(2)}, u32[]{:S(2)}) collective-permute-start(bf16[1024,128]{1,0:T(8,128)(2,1)S(1)} %get-tuple-element.87), channel_id=1, source_target_pairs={{0,2},{1,3},{2,0},{3,1},{4,6},{5,7},{6,4},{7,5},{8,10},{9,11},{10,... | collective-permute-start | bytes 786440 | tf_op jit(solution)/shard_map/ppermute | solution.py:24
  62.1 0.1 collective-permute-start.6
  62.2 4.3 %collective-permute-done.6.refs_3_ = bf16[128,256]{1,0:T(8,128)(2,1)S(1)} collective-permute-done((bf16[128,256]{1,0:T(8,128)(2,1)S(1)}, bf16[128,256]{1,0:T(8,128)(2,1)S(1)}, u32[]{:S(2)}, u32[]{:S(2)}) %collective-permute-start.6) | collective-permute-done | bytes 65568 | tf_op jit(solution)/shard_map/ppermute | solution.py:24
  66.5 0.2 collective-permute-start.7
  66.7 5.2 %collective-permute-done.7.refs_1_ = bf16[128,256]{1,0:T(8,128)(2,1)S(1)} collective-permute-done((bf16[128,256]{1,0:T(8,128)(2,1)S(1)}, bf16[128,256]{1,0:T(8,128)(2,1)S(1)}, u32[]{:S(2)}, u32[]{:S(2)}) %collective-permute-start.7) | collective-permute-done | bytes 65568 | tf_op jit(solution)/shard_map/ppermute | solution.py:24
  71.9 0.0 collective-permute-done.9.refs_3_.refs_12_
  71.9 0.0 collective-permute-done.8.refs_2_.refs_10_
  71.9 0.1 shard_map.113
  72.0 0.6 collective-permute-start.14
  72.6 0.8 collective-permute-start.15
  73.3 0.0 collective-permute-done.11.refs_3_.refs_8_
  73.3 0.0 collective-permute-done.10.refs_2_.refs_6_
  73.3 0.1 shard_map.114
  73.4 0.1 collective-permute-start.13
  73.5 0.1 shard_map.116
  73.6 13.8 %collective-permute-done.13.refs_0_ = bf16[512,512]{1,0:T(8,128)(2,1)S(1)} collective-permute-done((bf16[512,512]{1,0:T(8,128)(2,1)S(1)}, bf16[512,512]{1,0:T(8,128)(2,1)S(1)}, u32[]{:S(2)}, u32[]{:S(2)}) %collective-permute-start.13) | collective-permute-done | bytes 524320 | tf_op jit(solution)/shard_map/ppermute | solution.py:34
  87.4 0.0 collective-permute-done.15.refs_3_
  87.4 0.0 collective-permute-done.14.refs_2_
  87.4 0.3 shard_map.117
  87.7 0.6 collective-permute-start.17
  88.3 1.5 %collective-permute-start.18 = (bf16[1280,128]{1,0:T(8,128)(2,1)S(1)}, bf16[1280,128]{1,0:T(8,128)(2,1)S(1)}, u32[]{:S(2)}, u32[]{:S(2)}) collective-permute-start(bf16[1280,128]{1,0:T(8,128)(2,1)S(1)} %get-tuple-element.112), channel_id=1, source_target_pairs={{0,1},{1,0},{2,3},{3,2},{4,5},{5,4},{6,7},{7,6},{8,9},{9,8},{10,11... | collective-permute-start | bytes 983048 | tf_op jit(solution)/shard_map/ppermute | solution.py:24
  89.8 1.2 %collective-permute-start.12 = (bf16[128,256]{1,0:T(8,128)(2,1)S(1)}, bf16[128,256]{1,0:T(8,128)(2,1)S(1)}, u32[]{:S(2)}, u32[]{:S(2)}) collective-permute-start(bf16[128,256]{1,0:T(8,128)(2,1)S(1)} %get-tuple-element.97.placed_ref), channel_id=1, source_target_pairs={{0,4},{1,5},{2,6},{3,7},{4,0},{5,1},{6,2},{7,3},{8,12},{9,13},{10,... | collective-permute-start | bytes 196616 | tf_op jit(solution)/shard_map/ppermute | solution.py:24
  91.0 3.1 %collective-permute-done.12.near_ref = bf16[128,256]{1,0:T(8,128)(2,1)S(1)} collective-permute-done((bf16[128,256]{1,0:T(8,128)(2,1)S(1)}, bf16[128,256]{1,0:T(8,128)(2,1)S(1)}, u32[]{:S(2)}, u32[]{:S(2)}) %collective-permute-start.12) | collective-permute-done | bytes 65568 | tf_op jit(solution)/shard_map/ppermute | solution.py:24
  94.1 0.5 collective-permute-start.16
  94.6 0.0 collective-permute-start.20
  94.6 4.5 %collective-permute-done.16.refs_7_ = bf16[64,256]{1,0:T(8,128)(2,1)S(1)} collective-permute-done((bf16[64,256]{1,0:T(8,128)(2,1)S(1)}, bf16[64,256]{1,0:T(8,128)(2,1)S(1)}, u32[]{:S(2)}, u32[]{:S(2)}) %collective-permute-start.16) | collective-permute-done | bytes 32800 | tf_op jit(solution)/shard_map/ppermute | solution.py:24
  99.0 0.0 collective-permute-done.17.refs_2_.got_x_ref.refs_14_
  99.1 0.0 collective-permute-done.18.refs_3_.got_y_ref.refs_16_
  99.1 0.1 shard_map.118
  99.1 0.1 collective-permute-start.21
  99.2 1.6 %shard_map.122 = bf16[512,1024]{1,0:T(8,128)(2,1)S(1)} custom-call(s32[1]{0:T(128)} %bitcast.refs_0_.pos_ref._, s32[2,4]{1,0:T(2,128)} %bitcast.40, s32[2]{0:T(128)} %bitcast.47, bf16[8,64,512]{2,1,0:T(8,128)(2,1)} %bitcast.30, bf16[64,1024]{1,0:T(8,128)(2,1)S(1)} %shard_map.120.lowrank_ref.refs_4_, f32[1024,256]{1,0:T(8,128)S(1)} %get-tuple-element.94.refs_0_.refs_5_, ...), custom_call_target="tpu_custom_call" | custom-call | flops 1000 | bytes 1000 | tf_op jit(solution)/shard_map/pallas_call | solution.py:591
  100.8 1.4 %collective-permute-start.19 = (bf16[512,1024]{1,0:T(8,128)(2,1)S(1)}, bf16[512,1024]{1,0:T(8,128)(2,1)S(1)}, u32[]{:S(2)}, u32[]{:S(2)}) collective-permute-start(bf16[512,1024]{1,0:T(8,128)(2,1)S(1)} %shard_map.122), channel_id=1, source_target_pairs={{0,16},{1,17},{2,18},{3,19},{4,20},{5,21},{6,22},{7,23},{8,24},{9,... | collective-permute-start | bytes 3145736 | tf_op jit(solution)/shard_map/ppermute | solution.py:34
  102.2 0.0 copy-start
  102.2 2.8 %shard_map.121 = bf16[8,64,512]{2,1,0:T(8,128)(2,1)} custom-call(s32[1]{0:T(128)} %bitcast.refs_0_.pos_ref._, s32[2,4]{1,0:T(2,128)} %bitcast.41, s32[2]{0:T(128)} %bitcast.48, bf16[2,512,512]{2,1,0:T(8,128)(2,1)} %bitcast.50, bf16[64,1024]{1,0:T(8,128)(2,1)S(1)} %shard_map.120.lowrank_ref.refs_4_), custom_call_target="tpu_custom_call" | custom-call | flops 40000000000 | bytes 1000 | tf_op jit(solution)/shard_map/pallas_call | solution.py:645
  105.0 0.0 copy-done
  105.0 2.3 %shard_map.119 = bf16[8,32,1024]{2,1,0:T(8,128)(2,1)} custom-call(s32[1]{0:T(128)} %bitcast.refs_0_.pos_ref._, s32[2,4]{1,0:T(2,128)} %bitcast.42, s32[2]{0:T(128)} %bitcast.49, bf16[2,256,1024]{2,1,0:T(8,128)(2,1)S(1)} %bitcast.20, bf16[1,256,1024]{2,1,0:T(8,128)(2,1)S(1)} %bitcast.22, bf16[1,256,1024]{2,1,0:T(8,128)(2,1)S(1)} %bitcast.24, ...), custom_call_target="tpu_custom_call" | custom-call | flops 1000 | bytes 1000 | tf_op jit(solution)/shard_map/pallas_call | solution.py:546
  107.3 0.0 collective-permute-done.20.refs_1_
  107.3 1.6 %collective-permute-done.21.refs_2_ = bf16[512,256]{1,0:T(8,128)(2,1)S(1)} collective-permute-done((bf16[512,256]{1,0:T(8,128)(2,1)S(1)}, bf16[512,256]{1,0:T(8,128)(2,1)S(1)}, u32[]{:S(2)}, u32[]{:S(2)}) %collective-permute-start.21) | collective-permute-done | bytes 262176 | tf_op jit(solution)/shard_map/ppermute | solution.py:34
  108.9 0.0 collective-permute-done.19.kept_ref
  108.9 1.3 %shard_map.123 = bf16[2,512,512]{2,1,0:T(8,128)(2,1)} custom-call(s32[1]{0:T(128)} %bitcast.refs_0_.pos_ref._, bf16[512,1024]{1,0:T(8,128)(2,1)S(1)} %collective-permute-done.19.kept_ref, bf16[512,512]{1,0:T(8,128)(2,1)S(1)} %collective-permute-done.13.refs_0_, bf16[512,256]{1,0:T(8,128)(2,1)S(1)} %collective-permute-done.20.refs_1_, ...), custom_call_target="tpu_custom_call" | custom-call | flops 1000 | bytes 1000 | tf_op jit(solution)/shard_map/pallas_call | solution.py:656
  (5 shorter events, 0.1 us)
Async XLA Ops:
  1.9 27.3 %collective-permute-start = (bf16[256,1024]{1,0:T(8,128)(2,1)S(1)}, bf16[256,1024]{1,0:T(8,128)(2,1)S(1)}, u32[]{:S(2)}, u32[]{:S(2)}) collective-permute-start(bf16[256,1024]{1,0:T(8,128)(2,1)S(1)} %get-tuple-element.118), channel_id=1, source_target_pairs={{0,8},{1,9},{2,10},{3,11},{4,12},{5,13},{6,14},{7,15},{8,0},{9,1},... | collective-permute-start | bytes 1572872 | tf_op jit(solution)/shard_map/ppermute | solution.py:24
  11.7 26.4 %collective-permute-start.3 = (bf16[2048,256]{1,0:T(8,128)(2,1)S(1)}, bf16[2048,256]{1,0:T(8,128)(2,1)S(1)}, u32[]{:S(2)}, u32[]{:S(2)}) collective-permute-start(bf16[2048,256]{1,0:T(8,128)(2,1)S(1)} %get-tuple-element.66), channel_id=1, source_target_pairs={{0,2},{1,3},{2,0},{3,1},{4,6},{5,7},{6,4},{7,5},{8,10},{9,11},{10,... | collective-permute-start | bytes 3145736 | tf_op jit(solution)/shard_map/ppermute | solution.py:24
  13.3 27.5 %collective-permute-start.2 = (bf16[2176,256]{1,0:T(8,128)(2,1)S(1)}, bf16[2176,256]{1,0:T(8,128)(2,1)S(1)}, u32[]{:S(2)}, u32[]{:S(2)}) collective-permute-start(bf16[2176,256]{1,0:T(8,128)(2,1)S(1)} %get-tuple-element.65), channel_id=1, source_target_pairs={{0,1},{1,0},{2,3},{3,2},{4,5},{5,4},{6,7},{7,6},{8,9},{9,8},{10,11... | collective-permute-start | bytes 3342344 | tf_op jit(solution)/shard_map/ppermute | solution.py:24
  29.2 25.2 %collective-permute-start.1 = (bf16[256,1024]{1,0:T(8,128)(2,1)S(1)}, bf16[256,1024]{1,0:T(8,128)(2,1)S(1)}, u32[]{:S(2)}, u32[]{:S(2)}) collective-permute-start(bf16[256,1024]{1,0:T(8,128)(2,1)S(1)} %get-tuple-element.63), channel_id=1, source_target_pairs={{0,8},{1,9},{2,10},{3,11},{4,12},{5,13},{6,14},{7,15},{8,0},{9,1},... | collective-permute-start | bytes 1572872 | tf_op jit(solution)/shard_map/ppermute | solution.py:24
  35.0 24.0 %collective-permute-start.4 = (bf16[2048,128]{1,0:T(8,128)(2,1)S(1)}, bf16[2048,128]{1,0:T(8,128)(2,1)S(1)}, u32[]{:S(2)}, u32[]{:S(2)}) collective-permute-start(bf16[2048,128]{1,0:T(8,128)(2,1)S(1)} %get-tuple-element.85), channel_id=1, source_target_pairs={{0,1},{1,0},{2,3},{3,2},{4,5},{5,4},{6,7},{7,6},{8,9},{9,8},{10,11... | collective-permute-start | bytes 1572872 | tf_op jit(solution)/shard_map/ppermute | solution.py:24
  36.6 22.4 %collective-permute-start.5 = (bf16[2048,128]{1,0:T(8,128)(2,1)S(1)}, bf16[2048,128]{1,0:T(8,128)(2,1)S(1)}, u32[]{:S(2)}, u32[]{:S(2)}) collective-permute-start(bf16[2048,128]{1,0:T(8,128)(2,1)S(1)} %get-tuple-element.86), channel_id=1, source_target_pairs={{0,2},{1,3},{2,0},{3,1},{4,6},{5,7},{6,4},{7,5},{8,10},{9,11},{10,... | collective-permute-start | bytes 1572872 | tf_op jit(solution)/shard_map/ppermute | solution.py:24
  41.2 32.2 %collective-permute-start.11 = (bf16[1024,256]{1,0:T(8,128)(2,1)S(1)}, bf16[1024,256]{1,0:T(8,128)(2,1)S(1)}, u32[]{:S(2)}, u32[]{:S(2)}) collective-permute-start(bf16[1024,256]{1,0:T(8,128)(2,1)S(1)} %get-tuple-element.77), channel_id=1, source_target_pairs={{0,1},{1,0},{2,3},{3,2},{4,5},{5,4},{6,7},{7,6},{8,9},{9,8},{10,11... | collective-permute-start | bytes 1572872 | tf_op jit(solution)/shard_map/ppermute | solution.py:24
  42.7 30.6 %collective-permute-start.10 = (bf16[1152,256]{1,0:T(8,128)(2,1)S(1)}, bf16[1152,256]{1,0:T(8,128)(2,1)S(1)}, u32[]{:S(2)}, u32[]{:S(2)}) collective-permute-start(bf16[1152,256]{1,0:T(8,128)(2,1)S(1)} %get-tuple-element.76), channel_id=1, source_target_pairs={{0,2},{1,3},{2,0},{3,1},{4,6},{5,7},{6,4},{7,5},{8,10},{9,11},{10,... | collective-permute-start | bytes 1769480 | tf_op jit(solution)/shard_map/ppermute | solution.py:24
  59.3 12.6 %collective-permute-start.9 = (bf16[1024,128]{1,0:T(8,128)(2,1)S(1)}, bf16[1024,128]{1,0:T(8,128)(2,1)S(1)}, u32[]{:S(2)}, u32[]{:S(2)}) collective-permute-start(bf16[1024,128]{1,0:T(8,128)(2,1)S(1)} %get-tuple-element.91), channel_id=1, source_target_pairs={{0,1},{1,0},{2,3},{3,2},{4,5},{5,4},{6,7},{7,6},{8,9},{9,8},{10,11... | collective-permute-start | bytes 786440 | tf_op jit(solution)/shard_map/ppermute | solution.py:24
  60.6 11.3 %collective-permute-start.8 = (bf16[1024,128]{1,0:T(8,128)(2,1)S(1)}, bf16[1024,128]{1,0:T(8,128)(2,1)S(1)}, u32[]{:S(2)}, u32[]{:S(2)}) collective-permute-start(bf16[1024,128]{1,0:T(8,128)(2,1)S(1)} %get-tuple-element.87), channel_id=1, source_target_pairs={{0,2},{1,3},{2,0},{3,1},{4,6},{5,7},{6,4},{7,5},{8,10},{9,11},{10,... | collective-permute-start | bytes 786440 | tf_op jit(solution)/shard_map/ppermute | solution.py:24
  62.1 4.3 %collective-permute-start.6 = (bf16[128,256]{1,0:T(8,128)(2,1)S(1)}, bf16[128,256]{1,0:T(8,128)(2,1)S(1)}, u32[]{:S(2)}, u32[]{:S(2)}) collective-permute-start(bf16[128,256]{1,0:T(8,128)(2,1)S(1)} %shard_map.110), channel_id=1, source_target_pairs={{0,4},{1,5},{2,6},{3,7},{4,0},{5,1},{6,2},{7,3},{8,12},{9,13},{10,... | collective-permute-start | bytes 196616 | tf_op jit(solution)/shard_map/ppermute | solution.py:24
  66.5 5.4 %collective-permute-start.7 = (bf16[128,256]{1,0:T(8,128)(2,1)S(1)}, bf16[128,256]{1,0:T(8,128)(2,1)S(1)}, u32[]{:S(2)}, u32[]{:S(2)}) collective-permute-start(bf16[128,256]{1,0:T(8,128)(2,1)S(1)} %get-tuple-element.90), channel_id=1, source_target_pairs={{0,8},{1,9},{2,10},{3,11},{4,12},{5,13},{6,14},{7,15},{8,0},{9,1},... | collective-permute-start | bytes 196616 | tf_op jit(solution)/shard_map/ppermute | solution.py:24
  72.0 15.4 %collective-permute-start.14 = (bf16[2304,128]{1,0:T(8,128)(2,1)S(1)}, bf16[2304,128]{1,0:T(8,128)(2,1)S(1)}, u32[]{:S(2)}, u32[]{:S(2)}) collective-permute-start(bf16[2304,128]{1,0:T(8,128)(2,1)S(1)} %get-tuple-element.93), channel_id=1, source_target_pairs={{0,1},{1,0},{2,3},{3,2},{4,5},{5,4},{6,7},{7,6},{8,9},{9,8},{10,11... | collective-permute-start | bytes 1769480 | tf_op jit(solution)/shard_map/ppermute | solution.py:24
  72.6 14.8 %collective-permute-start.15 = (bf16[2304,128]{1,0:T(8,128)(2,1)S(1)}, bf16[2304,128]{1,0:T(8,128)(2,1)S(1)}, u32[]{:S(2)}, u32[]{:S(2)}) collective-permute-start(bf16[2304,128]{1,0:T(8,128)(2,1)S(1)} %get-tuple-element.106), channel_id=1, source_target_pairs={{0,2},{1,3},{2,0},{3,1},{4,6},{5,7},{6,4},{7,5},{8,10},{9,11},{10,... | collective-permute-start | bytes 1769480 | tf_op jit(solution)/shard_map/ppermute | solution.py:24
  73.4 14.0 %collective-permute-start.13 = (bf16[512,512]{1,0:T(8,128)(2,1)S(1)}, bf16[512,512]{1,0:T(8,128)(2,1)S(1)}, u32[]{:S(2)}, u32[]{:S(2)}) collective-permute-start(bf16[512,512]{1,0:T(8,128)(2,1)S(1)} %get-tuple-element.101), channel_id=1, source_target_pairs={{0,20},{1,21},{2,22},{3,23},{4,16},{5,17},{6,18},{7,19},{8,28},{9,... | collective-permute-start | bytes 1572872 | tf_op jit(solution)/shard_map/ppermute | solution.py:34
  87.7 11.3 %collective-permute-start.17 = (bf16[1280,128]{1,0:T(8,128)(2,1)S(1)}, bf16[1280,128]{1,0:T(8,128)(2,1)S(1)}, u32[]{:S(2)}, u32[]{:S(2)}) collective-permute-start(bf16[1280,128]{1,0:T(8,128)(2,1)S(1)} %get-tuple-element.111), channel_id=1, source_target_pairs={{0,2},{1,3},{2,0},{3,1},{4,6},{5,7},{6,4},{7,5},{8,10},{9,11},{10,... | collective-permute-start | bytes 983048 | tf_op jit(solution)/shard_map/ppermute | solution.py:24
  88.3 10.8 %collective-permute-start.18 = (bf16[1280,128]{1,0:T(8,128)(2,1)S(1)}, bf16[1280,128]{1,0:T(8,128)(2,1)S(1)}, u32[]{:S(2)}, u32[]{:S(2)}) collective-permute-start(bf16[1280,128]{1,0:T(8,128)(2,1)S(1)} %get-tuple-element.112), channel_id=1, source_target_pairs={{0,1},{1,0},{2,3},{3,2},{4,5},{5,4},{6,7},{7,6},{8,9},{9,8},{10,11... | collective-permute-start | bytes 983048 | tf_op jit(solution)/shard_map/ppermute | solution.py:24
  89.8 4.3 %collective-permute-start.12 = (bf16[128,256]{1,0:T(8,128)(2,1)S(1)}, bf16[128,256]{1,0:T(8,128)(2,1)S(1)}, u32[]{:S(2)}, u32[]{:S(2)}) collective-permute-start(bf16[128,256]{1,0:T(8,128)(2,1)S(1)} %get-tuple-element.97.placed_ref), channel_id=1, source_target_pairs={{0,4},{1,5},{2,6},{3,7},{4,0},{5,1},{6,2},{7,3},{8,12},{9,13},{10,... | collective-permute-start | bytes 196616 | tf_op jit(solution)/shard_map/ppermute | solution.py:24
  94.1 5.0 %collective-permute-start.16 = (bf16[64,256]{1,0:T(8,128)(2,1)S(1)}, bf16[64,256]{1,0:T(8,128)(2,1)S(1)}, u32[]{:S(2)}, u32[]{:S(2)}) collective-permute-start(bf16[64,256]{1,0:T(8,128)(2,1)S(1)} %get-tuple-element.108), channel_id=1, source_target_pairs={{0,8},{1,9},{2,10},{3,11},{4,12},{5,13},{6,14},{7,15},{8,0},{9,1},... | collective-permute-start | bytes 98312 | tf_op jit(solution)/shard_map/ppermute | solution.py:24
  94.6 12.7 %collective-permute-start.20 = (bf16[512,256]{1,0:T(8,128)(2,1)S(1)}, bf16[512,256]{1,0:T(8,128)(2,1)S(1)}, u32[]{:S(2)}, u32[]{:S(2)}) collective-permute-start(bf16[512,256]{1,0:T(8,128)(2,1)S(1)} %shard_map.116), channel_id=1, source_target_pairs={{0,20},{1,21},{2,22},{3,23},{4,16},{5,17},{6,18},{7,19},{8,28},{9,... | collective-permute-start | bytes 786440 | tf_op jit(solution)/shard_map/ppermute | solution.py:34
  99.1 9.8 %collective-permute-start.21 = (bf16[512,256]{1,0:T(8,128)(2,1)S(1)}, bf16[512,256]{1,0:T(8,128)(2,1)S(1)}, u32[]{:S(2)}, u32[]{:S(2)}) collective-permute-start(bf16[512,256]{1,0:T(8,128)(2,1)S(1)} %shard_map.118), channel_id=1, source_target_pairs={{0,20},{1,21},{2,22},{3,23},{4,16},{5,17},{6,18},{7,19},{8,28},{9,... | collective-permute-start | bytes 786440 | tf_op jit(solution)/shard_map/ppermute | solution.py:34
  100.8 8.1 %collective-permute-start.19 = (bf16[512,1024]{1,0:T(8,128)(2,1)S(1)}, bf16[512,1024]{1,0:T(8,128)(2,1)S(1)}, u32[]{:S(2)}, u32[]{:S(2)}) collective-permute-start(bf16[512,1024]{1,0:T(8,128)(2,1)S(1)} %shard_map.122), channel_id=1, source_target_pairs={{0,16},{1,17},{2,18},{3,19},{4,20},{5,21},{6,22},{7,23},{8,24},{9,... | collective-permute-start | bytes 3145736 | tf_op jit(solution)/shard_map/ppermute | solution.py:34
  102.2 2.8 %copy-start = (bf16[1,1,2,256,1024]{4,3,2,1,0:T(8,128)(2,1)S(1)}, bf16[1,1,2,256,1024]{4,3,2,1,0:T(8,128)(2,1)}, u32[]{:S(2)}) copy-start(bf16[1,1,2,256,1024]{4,3,2,1,0:T(8,128)(2,1)} %param.8) | copy-start | bytes 3145732

commit v18 on v15

--- a/solution.py
+++ b/solution.py
@@ -62,7 +62,7 @@
 
     jobs = []
     for x, y in ((1, 1), (1, 0), (0, 1), (0, 0)):
-        to_x = (sent_x if x else kept_x, *((y, 2) if turns else (2 * y, 1)))
+        to_x = (sent_x if x else kept_x, 2 * y, 1)
         to_y = (sent_y if y else kept_y, *((x, 2) if turns else (2 * x, 1)))
         start = 0 if to_x[0] is not None else half
         stop = total if to_y[0] is not None else half
@@ -374,7 +374,7 @@
     chunks = [([grad_tile], own_pieces), (got0, pieces_of(0)), (got1, pieces_of(1))]
     order = [piece for _, pieces in chunks for _, _, piece, _ in pieces]
     d_sent_x, d_sent_y, d_kept_x, d_kept_y, part = produce(
-        got1, pieces_of(1), False, True, True, LONG, None, fetched
+        got1, pieces_of(1), True, True, True, LONG, None, fetched
     )
     parts.append(part)
     own_third, placed = last_parts((after(kept_x, part), kept_y), (second_x, second_y), placed)
@@ -519,7 +519,7 @@
     c_last = relay(c_third, 4)
 
     def third_kernel(_, *refs):
-        lowrank_ref, next_ref = refs[4], refs[9]
+        lowrank_ref, next_ref, rider_ref = refs[4], refs[9], refs[10]
         for way in range(2):
             kept_ref, got_ref, sent_ref, rest_ref = refs[way], refs[2 + way], refs[5 + way], refs[7 + way]
             half = kept_ref.shape[0] // 2
@@ -528,33 +528,37 @@
             ).astype(BF16)
             rest_ref[...] = kept_ref[:half, :] + got_ref[:half, :].astype(F32)
             arrive(got_ref, 2 * half, way, lowrank_ref, next_ref)
-            ride(sent_ref, half, way, next_ref)
-
-    d_sent_x, d_sent_y, *d_kept, lowrank = small(
+        ride(refs[5], refs[0].shape[0] // 2, 0, next_ref)
+        rider_ref[...] = next_ref[:, rows_total // 2 :].astype(BF16)
+
+    d_sent_x, d_sent_y, *d_kept, lowrank, rider = small(
         third_kernel,
-        [((half_rows + riding(way, n), n), BF16) for way, n in enumerate(d_counts)]
+        [((half_rows + riding(0, d_counts[0]), d_counts[0]), BF16), ((half_rows, d_counts[1]), BF16)]
         + [((half_rows, n), F32) for n in d_counts]
-        + [((rank, rows_total), F32)],
+        + [((rank, rows_total), F32), ((rank, rows_total // 2), BF16)],
         d_kept_x,
-        after(d_kept_y, up_map_gradient, own_last, c_third),
+        after(d_kept_y, up_map_gradient, own_last, c_last),
         d_first_x,
         d_first_y,
         lowrank,
     )
-    d_second_x, d_second_y = partner(d_sent_x, 2), partner(d_sent_y, 1)
-    (d_third,) = last_parts(d_kept, (d_second_x, d_second_y))
-    d_last = relay(d_third, 4)
-
-    def whole_kernel(_, lowrank_ref, got_x_ref, got_y_ref, out_ref):
-        for way, got_ref in enumerate((got_x_ref, got_y_ref)):
-            arrive(got_ref, half_rows, way, lowrank_ref, out_ref)
+    rider = partner(rider, 1)
+    d_second_x, d_second_y = partner(d_sent_x, 2), partner(d_sent_y, 4)
+    (d_third_x,) = last_parts((d_kept[0],), (d_second_x,))
+    (d_third_y,) = last_parts((d_kept[1],), (d_second_y,))
+    d_last = [relay(d_third_x, 4), relay(d_third_y, 1)]
+
+    def whole_kernel(_, lowrank_ref, got_ref, rider_ref, out_ref):
+        arrive(got_ref, half_rows, 0, lowrank_ref, out_ref)
+        half = rows_total // 2
+        out_ref[:, half:] = (lowrank_ref[:, half:] + rider_ref[...].astype(F32)).astype(BF16)
 
     (lowrank,) = small(
         whole_kernel,
         [((rank, rows_total), BF16)],
-        after(lowrank, d_third),
+        after(lowrank, d_third_x, d_third_y),
         d_second_x,
-        d_second_y,
+        rider,
     )
 
     down = adapter_down_maps[0]
@@ -626,7 +630,7 @@
         for copy in copies:
             copy.wait()
 
-    got = [own_last, c_last, d_last]
+    got = [own_last, c_last, *d_last]
     grad_prev = pl.pallas_call(
         finish_kernel,
         in_specs=[SMEM] + [VMEM] * (1 + len(got)),

time: 105 us -> 113 us (1.076); the launches traced: 105 us -> 112 us
  waiting for transfers between devices: 46.3 us -> 51.4 us
  starting transfers between devices: 21.7 us -> 24 us
    ppermute x4 -> x5, waiting for transfers between devices: 7.09 us -> 12.3 us  [relay(): return lax.ppermute(value, ('pipe', 'tensor'), pairs)]
    ppermute x17 -> x18, starting transfers between devices: 20.8 us -> 22.1 us  [partner(): return lax.ppermute(value, 'tensor', pairs)]
    ppermute x17 -> x18, waiting for transfers between devices: 39.2 us -> 39.1 us  [partner(): return lax.ppermute(value, 'tensor', pairs)]
  transfers between devices with their start and end apart: 21 -> 23, of which waited for: 13 -> 10; matrix products, arithmetic and copies ran while one was open for 0% -> 0% of each run, Pallas kernels for 32% -> 29%
where the time goes in v18:
time: 113 us; the launch traced here: 112 us
  waiting for transfers between devices  51.4 us (45%)
  Pallas kernels  34.3 us (30%)
  starting transfers between devices  24 us (21%)
  local copies, waits for them, and re-layouts  1.28 us (1%)
    ppermute x18, waiting for transfers between devices, partner(): return lax.ppermute(value, 'tensor', pairs)  39.1 us
    ppermute x18, starting transfers between devices, partner(): return lax.ppermute(value, 'tensor', pairs)  22.1 us
    pallas_call x4, Pallas kernels, product(): pl.pallas_call(functools.partial(product_body, low_size, tile_rows, piece...  22.1 us
    ppermute x5, waiting for transfers between devices, relay(): return lax.ppermute(value, ('pipe', 'tensor'), pairs)  12.3 us
    pallas_call x1, Pallas kernels, fetch(): pl.pallas_call(functools.partial(fetch_kernel, low_size), in_specs=[SMEM,...  3.47 us
    pallas_call x1, Pallas kernels, shards(): pl.pallas_call(down_kernel, in_specs=[SMEM] * 3 + [VMEM] * 2, out_specs=V...  2.59 us
  transfers between devices with their start and end apart: 23, of which 10 were waited for; matrix products, arithmetic and copies ran while one was open for 0% of the time, Pallas kernels for 29%

profile of v18, /device:TPU:0, one launch (start us, length us, event | category | flops | bytes accessed | tf_op | source)
XLA Modules:
  0.0 111.8 jit_solution(5658736630216446984)
XLA Ops:
  0.6 1.3 %slice_bitcast_fusion = (bf16[256,1024]{1,0:T(8,128)(2,1)S(1)}, bf16[256,1024]{1,0:T(8,128)(2,1)S(1)}) fusion(bf16[1,1,2,256,1024]{4,3,2,1,0:T(8,128)(2,1)} %param.8), kind=kLoop, calls=%fused_computation | loop fusion | bytes 2097152 | tf_op jit(solution)/shard_map/squeeze | solution.py:349
  1.9 4.1 %collective-permute-start = (bf16[256,1024]{1,0:T(8,128)(2,1)S(1)}, bf16[256,1024]{1,0:T(8,128)(2,1)S(1)}, u32[]{:S(2)}, u32[]{:S(2)}) collective-permute-start(bf16[256,1024]{1,0:T(8,128)(2,1)S(1)} %get-tuple-element.111), channel_id=1, source_target_pairs={{0,8},{1,9},{2,10},{3,11},{4,12},{5,13},{6,14},{7,15},{8,0},{9,1},... | collective-permute-start | bytes 1572872 | tf_op jit(solution)/shard_map/ppermute | solution.py:24
  6.0 5.7 %shard_map.103 = (bf16[2176,256]{1,0:T(8,128)(2,1)S(1)}, bf16[2048,256]{1,0:T(8,128)(2,1)S(1)}, bf16[128,256]{1,0:T(8,128)(2,1)S(1)}) custom-call(s32[1]{0:T(128)} %bitcast.refs_0_.pos_ref._, s32[2,4]{1,0:T(2,128)} %bitcast.35, s32[2]{0:T(128)} %bitcast.42, bf16[2,256,1024]{2,1,0:T(8,128)(2,1)} %bitcast.18, bf16[8,512,1024]{2,1,0:T(8,128)(2,1)} %bitcast.25, ...), custom_call_target="tpu_custom_call" | custom-call | flops 1000 | bytes 1000 | tf_op jit(solution)/shard_map/pallas_call | solution.py:144
  11.7 1.6 %collective-permute-start.3 = (bf16[2048,256]{1,0:T(8,128)(2,1)S(1)}, bf16[2048,256]{1,0:T(8,128)(2,1)S(1)}, u32[]{:S(2)}, u32[]{:S(2)}) collective-permute-start(bf16[2048,256]{1,0:T(8,128)(2,1)S(1)} %get-tuple-element.63), channel_id=1, source_target_pairs={{0,2},{1,3},{2,0},{3,1},{4,6},{5,7},{6,4},{7,5},{8,10},{9,11},{10,... | collective-permute-start | bytes 3145736 | tf_op jit(solution)/shard_map/ppermute | solution.py:24
  13.3 1.5 %collective-permute-start.2 = (bf16[2176,256]{1,0:T(8,128)(2,1)S(1)}, bf16[2176,256]{1,0:T(8,128)(2,1)S(1)}, u32[]{:S(2)}, u32[]{:S(2)}) collective-permute-start(bf16[2176,256]{1,0:T(8,128)(2,1)S(1)} %get-tuple-element.62), channel_id=1, source_target_pairs={{0,1},{1,0},{2,3},{3,2},{4,5},{5,4},{6,7},{7,6},{8,9},{9,8},{10,11... | collective-permute-start | bytes 3342344 | tf_op jit(solution)/shard_map/ppermute | solution.py:24
  14.8 5.8 %shard_map.104 = (f32[2048,256]{1,0:T(8,128)S(1)}, f32[2048,256]{1,0:T(8,128)S(1)}, f32[32,512]{1,0:T(8,128)S(1)}) custom-call(s32[1]{0:T(128)} %bitcast.refs_0_.pos_ref._, s32[2,4]{1,0:T(2,128)} %bitcast.36, s32[2]{0:T(128)} %bitcast.43, bf16[2,256,1024]{2,1,0:T(8,128)(2,1)} %bitcast.19, bf16[8,512,1024]{2,1,0:T(8,128)(2,1)} %bitcast.26, ...), custom_call_target="tpu_custom_call" | custom-call | flops 1000 | bytes 1000 | tf_op jit(solution)/shard_map/pallas_call | solution.py:144
  20.7 8.5 %collective-permute-done = bf16[256,1024]{1,0:T(8,128)(2,1)S(1)} collective-permute-done((bf16[256,1024]{1,0:T(8,128)(2,1)S(1)}, bf16[256,1024]{1,0:T(8,128)(2,1)S(1)}, u32[]{:S(2)}, u32[]{:S(2)}) %collective-permute-start) | collective-permute-done | bytes 524320 | tf_op jit(solution)/shard_map/ppermute | solution.py:24
  29.2 0.0 collective-permute-start.1
  29.2 5.9 %shard_map.105 = (bf16[2048,128]{1,0:T(8,128)(2,1)S(1)}, bf16[2048,128]{1,0:T(8,128)(2,1)S(1)}, f32[2048,128]{1,0:T(8,128)S(1)}, f32[2048,128]{1,0:T(8,128)S(1)}, f32[32,256]{1,0:T(8,128)S(1)}) custom-call(s32[1]{0:T(128)} %bitcast.refs_0_.pos_ref._, s32[2,4]{1,0:T(2,128)} %bitcast.37, s32[2]{0:T(128)} %bitcast.44, bf16[1,256,1024]{2,1,0:T(8,128)(2,1)S(1)} %bitcast.21, ...), custom_call_target="tpu_custom_call" | custom-call | flops 40000000000 | bytes 1000 | tf_op jit(solution)/shard_map/pallas_call | solution.py:144
  35.0 1.4 %collective-permute-done.3.refs_3_ = bf16[2048,256]{1,0:T(8,128)(2,1)S(1)} collective-permute-done((bf16[2048,256]{1,0:T(8,128)(2,1)S(1)}, bf16[2048,256]{1,0:T(8,128)(2,1)S(1)}, u32[]{:S(2)}, u32[]{:S(2)}) %collective-permute-start.3) | collective-permute-done | bytes 1048608 | tf_op jit(solution)/shard_map/ppermute | solution.py:24
  36.4 2.6 %collective-permute-done.2.refs_2_ = bf16[2176,256]{1,0:T(8,128)(2,1)S(1)} collective-permute-done((bf16[2176,256]{1,0:T(8,128)(2,1)S(1)}, bf16[2176,256]{1,0:T(8,128)(2,1)S(1)}, u32[]{:S(2)}, u32[]{:S(2)}) %collective-permute-start.2) | collective-permute-done | bytes 1114144 | tf_op jit(solution)/shard_map/ppermute | solution.py:24
  39.1 0.3 shard_map.106
  39.4 1.6 %collective-permute-start.5 = (bf16[1024,256]{1,0:T(8,128)(2,1)S(1)}, bf16[1024,256]{1,0:T(8,128)(2,1)S(1)}, u32[]{:S(2)}, u32[]{:S(2)}) collective-permute-start(bf16[1024,256]{1,0:T(8,128)(2,1)S(1)} %get-tuple-element.73), channel_id=1, source_target_pairs={{0,1},{1,0},{2,3},{3,2},{4,5},{5,4},{6,7},{7,6},{8,9},{9,8},{10,11... | collective-permute-start | bytes 1572872 | tf_op jit(solution)/shard_map/ppermute | solution.py:24
  41.0 0.5 collective-permute-start.4
  41.5 0.5 collective-permute-start.10
  42.0 1.5 %collective-permute-start.11 = (bf16[2048,128]{1,0:T(8,128)(2,1)S(1)}, bf16[2048,128]{1,0:T(8,128)(2,1)S(1)}, u32[]{:S(2)}, u32[]{:S(2)}) collective-permute-start(bf16[2048,128]{1,0:T(8,128)(2,1)S(1)} %get-tuple-element.92), channel_id=1, source_target_pairs={{0,2},{1,3},{2,0},{3,1},{4,6},{5,7},{6,4},{7,5},{8,10},{9,11},{10,... | collective-permute-start | bytes 1572872 | tf_op jit(solution)/shard_map/ppermute | solution.py:24
  43.5 3.5 %shard_map.107.refs_4_ = bf16[8,512,1024]{2,1,0:T(8,128)(2,1)S(1)} custom-call(s32[1]{0:T(128)} %bitcast.refs_0_.pos_ref._, bf16[8,512,1024]{2,1,0:T(8,128)(2,1)} %bitcast.28), custom_call_target="tpu_custom_call" | custom-call | flops 1000 | bytes 1000 | tf_op jit(solution)/shard_map/pallas_call | solution.py:182
  47.0 7.4 %collective-permute-done.1 = bf16[256,1024]{1,0:T(8,128)(2,1)S(1)} collective-permute-done((bf16[256,1024]{1,0:T(8,128)(2,1)S(1)}, bf16[256,1024]{1,0:T(8,128)(2,1)S(1)}, u32[]{:S(2)}, u32[]{:S(2)}) %collective-permute-start.1) | collective-permute-done | bytes 524320 | tf_op jit(solution)/shard_map/ppermute | solution.py:24
  54.4 4.7 %shard_map.108 = (bf16[2048,128]{1,0:T(8,128)(2,1)S(1)}, bf16[2048,128]{1,0:T(8,128)(2,1)S(1)}, f32[2048,128]{1,0:T(8,128)S(1)}, f32[2048,128]{1,0:T(8,128)S(1)}, f32[32,256]{1,0:T(8,128)S(1)}) custom-call(s32[1]{0:T(128)} %bitcast.refs_0_.pos_ref._, s32[2,4]{1,0:T(2,128)} %bitcast.38, s32[2]{0:T(128)} %bitcast.45, bf16[1,256,1024]{2,1,0:T(8,128)(2,1)S(1)} %bitcast.23, ...), custom_call_target="tpu_custom_call" | custom-call | flops 40000000000 | bytes 1000 | tf_op jit(solution)/shard_map/pallas_call | solution.py:144
  59.1 0.0 collective-permute-done.5.refs_3_.refs_8_
  59.1 0.0 collective-permute-done.4.refs_2_.refs_6_
  59.1 0.1 shard_map.109
  59.2 3.7 %collective-permute-done.10.refs_2_ = bf16[2048,128]{1,0:T(8,128)(2,1)S(1)} collective-permute-done((bf16[2048,128]{1,0:T(8,128)(2,1)S(1)}, bf16[2048,128]{1,0:T(8,128)(2,1)S(1)}, u32[]{:S(2)}, u32[]{:S(2)}) %collective-permute-start.10) | collective-permute-done | bytes 524320 | tf_op jit(solution)/shard_map/ppermute | solution.py:24
  62.9 2.6 %collective-permute-done.11.refs_3_ = bf16[2048,128]{1,0:T(8,128)(2,1)S(1)} collective-permute-done((bf16[2048,128]{1,0:T(8,128)(2,1)S(1)}, bf16[2048,128]{1,0:T(8,128)(2,1)S(1)}, u32[]{:S(2)}, u32[]{:S(2)}) %collective-permute-start.11) | collective-permute-done | bytes 524320 | tf_op jit(solution)/shard_map/ppermute | solution.py:24
  65.5 0.2 shard_map.112
  65.7 0.0 copy-start
  65.7 0.6 collective-permute-start.12
  66.3 0.5 collective-permute-start.13
  66.8 2.5 %collective-permute-start.6 = (bf16[256,256]{1,0:T(8,128)(2,1)S(1)}, bf16[256,256]{1,0:T(8,128)(2,1)S(1)}, u32[]{:S(2)}, u32[]{:S(2)}) collective-permute-start(bf16[256,256]{1,0:T(8,128)(2,1)S(1)} %get-tuple-element.83), channel_id=1, source_target_pairs={{0,4},{1,5},{2,6},{3,7},{4,0},{5,1},{6,2},{7,3},{8,12},{9,13},{10,... | collective-permute-start | bytes 393224 | tf_op jit(solution)/shard_map/ppermute | solution.py:24
  69.3 0.0 collective-permute-start.8
  69.3 1.5 %collective-permute-start.7 = (bf16[192,256]{1,0:T(8,128)(2,1)S(1)}, bf16[192,256]{1,0:T(8,128)(2,1)S(1)}, u32[]{:S(2)}, u32[]{:S(2)}) collective-permute-start(bf16[192,256]{1,0:T(8,128)(2,1)S(1)} %get-tuple-element.84), channel_id=1, source_target_pairs={{0,8},{1,9},{2,10},{3,11},{4,12},{5,13},{6,14},{7,15},{8,0},{9,1},... | collective-permute-start | bytes 294920 | tf_op jit(solution)/shard_map/ppermute | solution.py:24
  70.8 5.0 %collective-permute-done.8.refs_9_.refs_5_ = bf16[192,256]{1,0:T(8,128)(2,1)S(1)} collective-permute-done((bf16[192,256]{1,0:T(8,128)(2,1)S(1)}, bf16[192,256]{1,0:T(8,128)(2,1)S(1)}, u32[]{:S(2)}, u32[]{:S(2)}) %collective-permute-start.8) | collective-permute-done | bytes 98336 | tf_op jit(solution)/shard_map/ppermute | solution.py:24
  75.8 0.0 collective-permute-start.9
  75.8 2.1 %collective-permute-done.7.refs_8_.refs_4_ = bf16[192,256]{1,0:T(8,128)(2,1)S(1)} collective-permute-done((bf16[192,256]{1,0:T(8,128)(2,1)S(1)}, bf16[192,256]{1,0:T(8,128)(2,1)S(1)}, u32[]{:S(2)}, u32[]{:S(2)}) %collective-permute-start.7) | collective-permute-done | bytes 98336 | tf_op jit(solution)/shard_map/ppermute | solution.py:24
  77.9 0.0 collective-permute-done.6.refs_7_.refs_3_
  77.9 0.1 shard_map.114
  78.0 1.6 %collective-permute-start.15 = (bf16[2304,128]{1,0:T(8,128)(2,1)S(1)}, bf16[2304,128]{1,0:T(8,128)(2,1)S(1)}, u32[]{:S(2)}, u32[]{:S(2)}) collective-permute-start(bf16[2304,128]{1,0:T(8,128)(2,1)S(1)} %get-tuple-element.98), channel_id=1, source_target_pairs={{0,1},{1,0},{2,3},{3,2},{4,5},{5,4},{6,7},{7,6},{8,9},{9,8},{10,11... | collective-permute-start | bytes 1769480 | tf_op jit(solution)/shard_map/ppermute | solution.py:24
  79.6 0.6 collective-permute-start.16
  80.2 0.0 collective-permute-done.12.refs_2_.refs_10_
  80.2 0.0 collective-permute-done.13.refs_3_.refs_12_
  80.2 0.1 shard_map.115
  80.2 0.1 collective-permute-start.14
  80.3 0.0 copy-done
  80.3 2.1 %shard_map.111 = bf16[8,32,1024]{2,1,0:T(8,128)(2,1)} custom-call(s32[1]{0:T(128)} %bitcast.refs_0_.pos_ref._, s32[2,4]{1,0:T(2,128)} %bitcast.39, s32[2]{0:T(128)} %bitcast.46, bf16[2,256,1024]{2,1,0:T(8,128)(2,1)S(1)} %bitcast.20, bf16[1,256,1024]{2,1,0:T(8,128)(2,1)S(1)} %bitcast.22, bf16[1,256,1024]{2,1,0:T(8,128)(2,1)S(1)} %bitcast.24, ...), custom_call_target="tpu_custom_call" | custom-call | flops 40000000000 | bytes 1000 | tf_op jit(solution)/shard_map/pallas_call | solution.py:506
  82.4 12.3 %collective-permute-done.14.refs_1_ = bf16[512,256]{1,0:T(8,128)(2,1)S(1)} collective-permute-done((bf16[512,256]{1,0:T(8,128)(2,1)S(1)}, bf16[512,256]{1,0:T(8,128)(2,1)S(1)}, u32[]{:S(2)}, u32[]{:S(2)}) %collective-permute-start.14) | collective-permute-done | bytes 262176 | tf_op jit(solution)/shard_map/ppermute | solution.py:34
  94.7 0.0 collective-permute-done.9.refs_0_
  94.7 0.0 collective-permute-done.16.refs_3_
  94.7 0.0 collective-permute-done.15.refs_2_
  94.8 0.3 shard_map.116
  95.1 1.3 %collective-permute-start.17 = (bf16[1280,128]{1,0:T(8,128)(2,1)S(1)}, bf16[1280,128]{1,0:T(8,128)(2,1)S(1)}, u32[]{:S(2)}, u32[]{:S(2)}) collective-permute-start(bf16[1280,128]{1,0:T(8,128)(2,1)S(1)} %get-tuple-element.106), channel_id=1, source_target_pairs={{0,2},{1,3},{2,0},{3,1},{4,6},{5,7},{6,4},{7,5},{8,10},{9,11},{10,... | collective-permute-start | bytes 983048 | tf_op jit(solution)/shard_map/ppermute | solution.py:24
  96.4 0.8 collective-permute-start.18
  97.2 1.5 %collective-permute-start.19 = (bf16[64,512]{1,0:T(8,128)(2,1)S(1)}, bf16[64,512]{1,0:T(8,128)(2,1)S(1)}, u32[]{:S(2)}, u32[]{:S(2)}) collective-permute-start(bf16[64,512]{1,0:T(8,128)(2,1)S(1)} %get-tuple-element.110), channel_id=1, source_target_pairs={{0,1},{1,0},{2,3},{3,2},{4,5},{5,4},{6,7},{7,6},{8,9},{9,8},{10,11... | collective-permute-start | bytes 196616 | tf_op jit(solution)/shard_map/ppermute | solution.py:24
  98.7 5.8 %collective-permute-done.18.refs_1_.refs_16_ = bf16[1024,128]{1,0:T(8,128)(2,1)S(1)} collective-permute-done((bf16[1024,128]{1,0:T(8,128)(2,1)S(1)}, bf16[1024,128]{1,0:T(8,128)(2,1)S(1)}, u32[]{:S(2)}, u32[]{:S(2)}) %collective-permute-start.18) | collective-permute-done | bytes 262176 | tf_op jit(solution)/shard_map/ppermute | solution.py:24
  104.4 0.2 collective-permute-start.22
  104.6 0.0 collective-permute-done.17.refs_1_.got_ref.refs_14_
  104.6 1.5 %collective-permute-start.21 = (bf16[512,128]{1,0:T(8,128)(2,1)S(1)}, bf16[512,128]{1,0:T(8,128)(2,1)S(1)}, u32[]{:S(2)}, u32[]{:S(2)}) collective-permute-start(bf16[512,128]{1,0:T(8,128)(2,1)S(1)} %shard_map.117), channel_id=1, source_target_pairs={{0,20},{1,21},{2,22},{3,23},{4,16},{5,17},{6,18},{7,19},{8,28},{9,... | collective-permute-start | bytes 393224 | tf_op jit(solution)/shard_map/ppermute | solution.py:34
  106.1 0.0 collective-permute-done.19.rider_ref
  106.2 1.6 %shard_map.120 = bf16[512,1024]{1,0:T(8,128)(2,1)S(1)} custom-call(s32[1]{0:T(128)} %bitcast.refs_0_.pos_ref._, s32[2,4]{1,0:T(2,128)} %bitcast.40, s32[2]{0:T(128)} %bitcast.47, bf16[8,64,512]{2,1,0:T(8,128)(2,1)} %bitcast.30, bf16[64,1024]{1,0:T(8,128)(2,1)S(1)} %shard_map.119.refs_4_.lowrank_ref, f32[1024,256]{1,0:T(8,128)S(1)} %get-tuple-element.79.refs_0_.refs_5_, ...), custom_call_target="tpu_custom_call" | custom-call | flops 1000 | bytes 1000 | tf_op jit(solution)/shard_map/pallas_call | solution.py:597
  107.7 0.2 collective-permute-start.20
  107.9 2.6 %shard_map.122 = bf16[8,64,512]{2,1,0:T(8,128)(2,1)} custom-call(s32[1]{0:T(128)} %bitcast.refs_0_.pos_ref._, s32[2,4]{1,0:T(2,128)} %bitcast.41, s32[2]{0:T(128)} %bitcast.48, bf16[2,512,512]{2,1,0:T(8,128)(2,1)} %bitcast.49, bf16[64,1024]{1,0:T(8,128)(2,1)S(1)} %shard_map.119.refs_4_.lowrank_ref), custom_call_target="tpu_custom_call" | custom-call | flops 40000000000 | bytes 1000 | tf_op jit(solution)/shard_map/pallas_call | solution.py:666
  110.5 0.0 collective-permute-done.22.refs_3_
  110.5 0.0 collective-permute-done.21.refs_2_
  110.5 0.0 collective-permute-done.20.kept_ref
  110.6 1.3 %shard_map.121 = bf16[2,512,512]{2,1,0:T(8,128)(2,1)} custom-call(s32[1]{0:T(128)} %bitcast.refs_0_.pos_ref._, bf16[512,1024]{1,0:T(8,128)(2,1)S(1)} %collective-permute-done.20.kept_ref, bf16[512,512]{1,0:T(8,128)(2,1)S(1)} %collective-permute-done.9.refs_0_, bf16[512,256]{1,0:T(8,128)(2,1)S(1)} %collective-permute-done.14.refs_1_, ...), custom_call_target="tpu_custom_call" | custom-call | flops 1000 | bytes 1000 | tf_op jit(solution)/shard_map/pallas_call | solution.py:634
  (5 shorter events, 0.1 us)
Async XLA Ops:
  1.9 27.3 %collective-permute-start = (bf16[256,1024]{1,0:T(8,128)(2,1)S(1)}, bf16[256,1024]{1,0:T(8,128)(2,1)S(1)}, u32[]{:S(2)}, u32[]{:S(2)}) collective-permute-start(bf16[256,1024]{1,0:T(8,128)(2,1)S(1)} %get-tuple-element.111), channel_id=1, source_target_pairs={{0,8},{1,9},{2,10},{3,11},{4,12},{5,13},{6,14},{7,15},{8,0},{9,1},... | collective-permute-start | bytes 1572872 | tf_op jit(solution)/shard_map/ppermute | solution.py:24
  11.7 24.7 %collective-permute-start.3 = (bf16[2048,256]{1,0:T(8,128)(2,1)S(1)}, bf16[2048,256]{1,0:T(8,128)(2,1)S(1)}, u32[]{:S(2)}, u32[]{:S(2)}) collective-permute-start(bf16[2048,256]{1,0:T(8,128)(2,1)S(1)} %get-tuple-element.63), channel_id=1, source_target_pairs={{0,2},{1,3},{2,0},{3,1},{4,6},{5,7},{6,4},{7,5},{8,10},{9,11},{10,... | collective-permute-start | bytes 3145736 | tf_op jit(solution)/shard_map/ppermute | solution.py:24
  13.3 25.7 %collective-permute-start.2 = (bf16[2176,256]{1,0:T(8,128)(2,1)S(1)}, bf16[2176,256]{1,0:T(8,128)(2,1)S(1)}, u32[]{:S(2)}, u32[]{:S(2)}) collective-permute-start(bf16[2176,256]{1,0:T(8,128)(2,1)S(1)} %get-tuple-element.62), channel_id=1, source_target_pairs={{0,1},{1,0},{2,3},{3,2},{4,5},{5,4},{6,7},{7,6},{8,9},{9,8},{10,11... | collective-permute-start | bytes 3342344 | tf_op jit(solution)/shard_map/ppermute | solution.py:24
  29.2 25.2 %collective-permute-start.1 = (bf16[256,1024]{1,0:T(8,128)(2,1)S(1)}, bf16[256,1024]{1,0:T(8,128)(2,1)S(1)}, u32[]{:S(2)}, u32[]{:S(2)}) collective-permute-start(bf16[256,1024]{1,0:T(8,128)(2,1)S(1)} %get-tuple-element.60), channel_id=1, source_target_pairs={{0,8},{1,9},{2,10},{3,11},{4,12},{5,13},{6,14},{7,15},{8,0},{9,1},... | collective-permute-start | bytes 1572872 | tf_op jit(solution)/shard_map/ppermute | solution.py:24
  39.4 19.7 %collective-permute-start.5 = (bf16[1024,256]{1,0:T(8,128)(2,1)S(1)}, bf16[1024,256]{1,0:T(8,128)(2,1)S(1)}, u32[]{:S(2)}, u32[]{:S(2)}) collective-permute-start(bf16[1024,256]{1,0:T(8,128)(2,1)S(1)} %get-tuple-element.73), channel_id=1, source_target_pairs={{0,1},{1,0},{2,3},{3,2},{4,5},{5,4},{6,7},{7,6},{8,9},{9,8},{10,11... | collective-permute-start | bytes 1572872 | tf_op jit(solution)/shard_map/ppermute | solution.py:24
  41.0 18.1 %collective-permute-start.4 = (bf16[1152,256]{1,0:T(8,128)(2,1)S(1)}, bf16[1152,256]{1,0:T(8,128)(2,1)S(1)}, u32[]{:S(2)}, u32[]{:S(2)}) collective-permute-start(bf16[1152,256]{1,0:T(8,128)(2,1)S(1)} %get-tuple-element.72), channel_id=1, source_target_pairs={{0,2},{1,3},{2,0},{3,1},{4,6},{5,7},{6,4},{7,5},{8,10},{9,11},{10,... | collective-permute-start | bytes 1769480 | tf_op jit(solution)/shard_map/ppermute | solution.py:24
  41.5 21.4 %collective-permute-start.10 = (bf16[2048,128]{1,0:T(8,128)(2,1)S(1)}, bf16[2048,128]{1,0:T(8,128)(2,1)S(1)}, u32[]{:S(2)}, u32[]{:S(2)}) collective-permute-start(bf16[2048,128]{1,0:T(8,128)(2,1)S(1)} %get-tuple-element.90), channel_id=1, source_target_pairs={{0,1},{1,0},{2,3},{3,2},{4,5},{5,4},{6,7},{7,6},{8,9},{9,8},{10,11... | collective-permute-start | bytes 1572872 | tf_op jit(solution)/shard_map/ppermute | solution.py:24
  42.0 23.5 %collective-permute-start.11 = (bf16[2048,128]{1,0:T(8,128)(2,1)S(1)}, bf16[2048,128]{1,0:T(8,128)(2,1)S(1)}, u32[]{:S(2)}, u32[]{:S(2)}) collective-permute-start(bf16[2048,128]{1,0:T(8,128)(2,1)S(1)} %get-tuple-element.92), channel_id=1, source_target_pairs={{0,2},{1,3},{2,0},{3,1},{4,6},{5,7},{6,4},{7,5},{8,10},{9,11},{10,... | collective-permute-start | bytes 1572872 | tf_op jit(solution)/shard_map/ppermute | solution.py:24
  65.7 14.6 %copy-start = (bf16[1,1,2,256,1024]{4,3,2,1,0:T(8,128)(2,1)S(1)}, bf16[1,1,2,256,1024]{4,3,2,1,0:T(8,128)(2,1)}, u32[]{:S(2)}) copy-start(bf16[1,1,2,256,1024]{4,3,2,1,0:T(8,128)(2,1)} %param.8) | copy-start | bytes 3145732
  65.7 14.5 %collective-permute-start.12 = (bf16[1024,128]{1,0:T(8,128)(2,1)S(1)}, bf16[1024,128]{1,0:T(8,128)(2,1)S(1)}, u32[]{:S(2)}, u32[]{:S(2)}) collective-permute-start(bf16[1024,128]{1,0:T(8,128)(2,1)S(1)} %get-tuple-element.100), channel_id=1, source_target_pairs={{0,2},{1,3},{2,0},{3,1},{4,6},{5,7},{6,4},{7,5},{8,10},{9,11},{10,... | collective-permute-start | bytes 786440 | tf_op jit(solution)/shard_map/ppermute | solution.py:24
  66.3 13.9 %collective-permute-start.13 = (bf16[1024,128]{1,0:T(8,128)(2,1)S(1)}, bf16[1024,128]{1,0:T(8,128)(2,1)S(1)}, u32[]{:S(2)}, u32[]{:S(2)}) collective-permute-start(bf16[1024,128]{1,0:T(8,128)(2,1)S(1)} %get-tuple-element.101), channel_id=1, source_target_pairs={{0,1},{1,0},{2,3},{3,2},{4,5},{5,4},{6,7},{7,6},{8,9},{9,8},{10,11... | collective-permute-start | bytes 786440 | tf_op jit(solution)/shard_map/ppermute | solution.py:24
  66.8 11.1 %collective-permute-start.6 = (bf16[256,256]{1,0:T(8,128)(2,1)S(1)}, bf16[256,256]{1,0:T(8,128)(2,1)S(1)}, u32[]{:S(2)}, u32[]{:S(2)}) collective-permute-start(bf16[256,256]{1,0:T(8,128)(2,1)S(1)} %get-tuple-element.83), channel_id=1, source_target_pairs={{0,4},{1,5},{2,6},{3,7},{4,0},{5,1},{6,2},{7,3},{8,12},{9,13},{10,... | collective-permute-start | bytes 393224 | tf_op jit(solution)/shard_map/ppermute | solution.py:24
  69.3 6.5 %collective-permute-start.8 = (bf16[192,256]{1,0:T(8,128)(2,1)S(1)}, bf16[192,256]{1,0:T(8,128)(2,1)S(1)}, u32[]{:S(2)}, u32[]{:S(2)}) collective-permute-start(bf16[192,256]{1,0:T(8,128)(2,1)S(1)} %get-tuple-element.84), channel_id=1, source_target_pairs={{0,12},{1,13},{2,14},{3,15},{4,8},{5,9},{6,10},{7,11},{8,4},{9,5},... | collective-permute-start | bytes 294920 | tf_op jit(solution)/shard_map/ppermute | solution.py:24
  69.3 8.6 %collective-permute-start.7 = (bf16[192,256]{1,0:T(8,128)(2,1)S(1)}, bf16[192,256]{1,0:T(8,128)(2,1)S(1)}, u32[]{:S(2)}, u32[]{:S(2)}) collective-permute-start(bf16[192,256]{1,0:T(8,128)(2,1)S(1)} %get-tuple-element.84), channel_id=1, source_target_pairs={{0,8},{1,9},{2,10},{3,11},{4,12},{5,13},{6,14},{7,15},{8,0},{9,1},... | collective-permute-start | bytes 294920 | tf_op jit(solution)/shard_map/ppermute | solution.py:24
  75.8 18.9 %collective-permute-start.9 = (bf16[512,512]{1,0:T(8,128)(2,1)S(1)}, bf16[512,512]{1,0:T(8,128)(2,1)S(1)}, u32[]{:S(2)}, u32[]{:S(2)}) collective-permute-start(bf16[512,512]{1,0:T(8,128)(2,1)S(1)} %get-tuple-element.85), channel_id=1, source_target_pairs={{0,20},{1,21},{2,22},{3,23},{4,16},{5,17},{6,18},{7,19},{8,28},{9,... | collective-permute-start | bytes 1572872 | tf_op jit(solution)/shard_map/ppermute | solution.py:34
  78.0 16.7 %collective-permute-start.15 = (bf16[2304,128]{1,0:T(8,128)(2,1)S(1)}, bf16[2304,128]{1,0:T(8,128)(2,1)S(1)}, u32[]{:S(2)}, u32[]{:S(2)}) collective-permute-start(bf16[2304,128]{1,0:T(8,128)(2,1)S(1)} %get-tuple-element.98), channel_id=1, source_target_pairs={{0,1},{1,0},{2,3},{3,2},{4,5},{5,4},{6,7},{7,6},{8,9},{9,8},{10,11... | collective-permute-start | bytes 1769480 | tf_op jit(solution)/shard_map/ppermute | solution.py:24
  79.6 15.2 %collective-permute-start.16 = (bf16[2304,128]{1,0:T(8,128)(2,1)S(1)}, bf16[2304,128]{1,0:T(8,128)(2,1)S(1)}, u32[]{:S(2)}, u32[]{:S(2)}) collective-permute-start(bf16[2304,128]{1,0:T(8,128)(2,1)S(1)} %get-tuple-element.103), channel_id=1, source_target_pairs={{0,2},{1,3},{2,0},{3,1},{4,6},{5,7},{6,4},{7,5},{8,10},{9,11},{10,... | collective-permute-start | bytes 1769480 | tf_op jit(solution)/shard_map/ppermute | solution.py:24
  80.2 14.5 %collective-permute-start.14 = (bf16[512,256]{1,0:T(8,128)(2,1)S(1)}, bf16[512,256]{1,0:T(8,128)(2,1)S(1)}, u32[]{:S(2)}, u32[]{:S(2)}) collective-permute-start(bf16[512,256]{1,0:T(8,128)(2,1)S(1)} %shard_map.115), channel_id=1, source_target_pairs={{0,20},{1,21},{2,22},{3,23},{4,16},{5,17},{6,18},{7,19},{8,28},{9,... | collective-permute-start | bytes 786440 | tf_op jit(solution)/shard_map/ppermute | solution.py:34
  95.1 9.5 %collective-permute-start.17 = (bf16[1280,128]{1,0:T(8,128)(2,1)S(1)}, bf16[1280,128]{1,0:T(8,128)(2,1)S(1)}, u32[]{:S(2)}, u32[]{:S(2)}) collective-permute-start(bf16[1280,128]{1,0:T(8,128)(2,1)S(1)} %get-tuple-element.106), channel_id=1, source_target_pairs={{0,2},{1,3},{2,0},{3,1},{4,6},{5,7},{6,4},{7,5},{8,10},{9,11},{10,... | collective-permute-start | bytes 983048 | tf_op jit(solution)/shard_map/ppermute | solution.py:24
  96.4 8.0 %collective-permute-start.18 = (bf16[1024,128]{1,0:T(8,128)(2,1)S(1)}, bf16[1024,128]{1,0:T(8,128)(2,1)S(1)}, u32[]{:S(2)}, u32[]{:S(2)}) collective-permute-start(bf16[1024,128]{1,0:T(8,128)(2,1)S(1)} %get-tuple-element.108), channel_id=1, source_target_pairs={{0,4},{1,5},{2,6},{3,7},{4,0},{5,1},{6,2},{7,3},{8,12},{9,13},{10,... | collective-permute-start | bytes 786440 | tf_op jit(solution)/shard_map/ppermute | solution.py:24
  97.2 9.0 %collective-permute-start.19 = (bf16[64,512]{1,0:T(8,128)(2,1)S(1)}, bf16[64,512]{1,0:T(8,128)(2,1)S(1)}, u32[]{:S(2)}, u32[]{:S(2)}) collective-permute-start(bf16[64,512]{1,0:T(8,128)(2,1)S(1)} %get-tuple-element.110), channel_id=1, source_target_pairs={{0,1},{1,0},{2,3},{3,2},{4,5},{5,4},{6,7},{7,6},{8,9},{9,8},{10,11... | collective-permute-start | bytes 196616 | tf_op jit(solution)/shard_map/ppermute | solution.py:24
  104.4 6.1 %collective-permute-start.22 = (bf16[512,128]{1,0:T(8,128)(2,1)S(1)}, bf16[512,128]{1,0:T(8,128)(2,1)S(1)}, u32[]{:S(2)}, u32[]{:S(2)}) collective-permute-start(bf16[512,128]{1,0:T(8,128)(2,1)S(1)} %shard_map.118), channel_id=1, source_target_pairs={{0,17},{1,16},{2,19},{3,18},{4,21},{5,20},{6,23},{7,22},{8,25},{9,... | collective-permute-start | bytes 393224 | tf_op jit(solution)/shard_map/ppermute | solution.py:34
  104.6 5.9 %collective-permute-start.21 = (bf16[512,128]{1,0:T(8,128)(2,1)S(1)}, bf16[512,128]{1,0:T(8,128)(2,1)S(1)}, u32[]{:S(2)}, u32[]{:S(2)}) collective-permute-start(bf16[512,128]{1,0:T(8,128)(2,1)S(1)} %shard_map.117), channel_id=1, source_target_pairs={{0,20},{1,21},{2,22},{3,23},{4,16},{5,17},{6,18},{7,19},{8,28},{9,... | collective-permute-start | bytes 393224 | tf_op jit(solution)/shard_map/ppermute | solution.py:34
  107.7 2.8 %collective-permute-start.20 = (bf16[512,1024]{1,0:T(8,128)(2,1)S(1)}, bf16[512,1024]{1,0:T(8,128)(2,1)S(1)}, u32[]{:S(2)}, u32[]{:S(2)}) collective-permute-start(bf16[512,1024]{1,0:T(8,128)(2,1)S(1)} %shard_map.120), channel_id=1, source_target_pairs={{0,16},{1,17},{2,18},{3,19},{4,20},{5,21},{6,22},{7,23},{8,24},{9,... | collective-permute-start | bytes 3145736 | tf_op jit(solution)/shard_map/ppermute | solution.py:34

commit v19 on v15

--- a/solution.py
+++ b/solution.py
@@ -362,9 +362,8 @@
     second_rows = after(grad_tile[1], *got0)
     got1 = [partner(second_rows, k * low_size)[None] for k in range(1, high_size)]
 
-    (sent_x, sent_y), (kept_x, kept_y), placed = halve(
-        (after(kept_x, part), kept_y), (first_x, first_y), placed
-    )
+    (sent_y,), (kept_y,) = halve((after(kept_y, part),), (first_y,))
+    (sent_x,), (kept_x,), placed = halve((after(kept_x, part),), (first_x,), placed)
     second_x, second_y = partner(sent_x, 2), partner(sent_y, 1)
     c_first_x = partner(after(c_sent_x, sent_x, sent_y), 1)
     c_first_y = partner(after(c_sent_y, sent_x, sent_y), 2)

time: 105 us -> 105 us (level)
  waiting for transfers between devices: 46.3 us -> 44.8 us
  starting transfers between devices: 21.7 us -> 23.1 us
    ppermute x17, starting transfers between devices: 20.8 us -> 22.6 us  [partner(): return lax.ppermute(value, 'tensor', pairs)]
    ppermute x17, waiting for transfers between devices: 39.2 us -> 37.8 us  [partner(): return lax.ppermute(value, 'tensor', pairs)]
where the time goes in v19:
time: 105 us
  waiting for transfers between devices  44.8 us (43%)
  Pallas kernels  35.1 us (33%)
  starting transfers between devices  23.1 us (22%)
  local copies, waits for them, and re-layouts  1.27 us (1%)
    ppermute x17, waiting for transfers between devices, partner(): return lax.ppermute(value, 'tensor', pairs)  37.8 us
    ppermute x17, starting transfers between devices, partner(): return lax.ppermute(value, 'tensor', pairs)  22.6 us
    pallas_call x4, Pallas kernels, product(): pl.pallas_call(functools.partial(product_body, low_size, tile_rows, piece...  22.3 us
    ppermute x4, waiting for transfers between devices, relay(): return lax.ppermute(value, ('pipe', 'tensor'), pairs)  7.02 us
    pallas_call x1, Pallas kernels, fetch(): pl.pallas_call(functools.partial(fetch_kernel, low_size), in_specs=[SMEM,...  3.47 us
    pallas_call x1, Pallas kernels, shards(): pl.pallas_call(down_kernel, in_specs=[SMEM] * 3 + [VMEM] * 2, out_specs=V...  2.88 us
    pallas_call x1, Pallas kernels, shards(): pl.pallas_call(functools.partial(up_body, low_size, tile_rows, all_pieces...  2.42 us
  transfers between devices with their start and end apart: 21, of which 13 were waited for; matrix products, arithmetic and copies ran while one was open for 0% of the time, Pallas kernels for 32%

profile of v19, /device:TPU:0, one launch (start us, length us, event | category | flops | bytes accessed | tf_op | source)
XLA Modules:
  0.0 105.1 jit_solution(15619199604605616698)
XLA Ops:
  0.6 1.3 %slice_bitcast_fusion = (bf16[256,1024]{1,0:T(8,128)(2,1)S(1)}, bf16[256,1024]{1,0:T(8,128)(2,1)S(1)}) fusion(bf16[1,1,2,256,1024]{4,3,2,1,0:T(8,128)(2,1)} %param.8), kind=kLoop, calls=%fused_computation | loop fusion | bytes 2097152 | tf_op jit(solution)/shard_map/squeeze | solution.py:349
  1.9 4.1 %collective-permute-start = (bf16[256,1024]{1,0:T(8,128)(2,1)S(1)}, bf16[256,1024]{1,0:T(8,128)(2,1)S(1)}, u32[]{:S(2)}, u32[]{:S(2)}) collective-permute-start(bf16[256,1024]{1,0:T(8,128)(2,1)S(1)} %get-tuple-element.111), channel_id=1, source_target_pairs={{0,8},{1,9},{2,10},{3,11},{4,12},{5,13},{6,14},{7,15},{8,0},{9,1},... | collective-permute-start | bytes 1572872 | tf_op jit(solution)/shard_map/ppermute | solution.py:24
  6.0 5.7 %shard_map.103 = (bf16[2176,256]{1,0:T(8,128)(2,1)S(1)}, bf16[2048,256]{1,0:T(8,128)(2,1)S(1)}, bf16[128,256]{1,0:T(8,128)(2,1)S(1)}) custom-call(s32[1]{0:T(128)} %bitcast.refs_0_.pos_ref._, s32[2,4]{1,0:T(2,128)} %bitcast.35, s32[2]{0:T(128)} %bitcast.42, bf16[2,256,1024]{2,1,0:T(8,128)(2,1)} %bitcast.18, bf16[8,512,1024]{2,1,0:T(8,128)(2,1)} %bitcast.25, ...), custom_call_target="tpu_custom_call" | custom-call | flops 1000 | bytes 1000 | tf_op jit(solution)/shard_map/pallas_call | solution.py:144
  11.7 1.6 %collective-permute-start.3 = (bf16[2048,256]{1,0:T(8,128)(2,1)S(1)}, bf16[2048,256]{1,0:T(8,128)(2,1)S(1)}, u32[]{:S(2)}, u32[]{:S(2)}) collective-permute-start(bf16[2048,256]{1,0:T(8,128)(2,1)S(1)} %get-tuple-element.63), channel_id=1, source_target_pairs={{0,2},{1,3},{2,0},{3,1},{4,6},{5,7},{6,4},{7,5},{8,10},{9,11},{10,... | collective-permute-start | bytes 3145736 | tf_op jit(solution)/shard_map/ppermute | solution.py:24
  13.3 1.5 %collective-permute-start.2 = (bf16[2176,256]{1,0:T(8,128)(2,1)S(1)}, bf16[2176,256]{1,0:T(8,128)(2,1)S(1)}, u32[]{:S(2)}, u32[]{:S(2)}) collective-permute-start(bf16[2176,256]{1,0:T(8,128)(2,1)S(1)} %get-tuple-element.62), channel_id=1, source_target_pairs={{0,1},{1,0},{2,3},{3,2},{4,5},{5,4},{6,7},{7,6},{8,9},{9,8},{10,11... | collective-permute-start | bytes 3342344 | tf_op jit(solution)/shard_map/ppermute | solution.py:24
  14.8 5.8 %shard_map.104 = (f32[2048,256]{1,0:T(8,128)S(1)}, f32[2048,256]{1,0:T(8,128)S(1)}, f32[32,512]{1,0:T(8,128)S(1)}) custom-call(s32[1]{0:T(128)} %bitcast.refs_0_.pos_ref._, s32[2,4]{1,0:T(2,128)} %bitcast.36, s32[2]{0:T(128)} %bitcast.43, bf16[2,256,1024]{2,1,0:T(8,128)(2,1)} %bitcast.19, bf16[8,512,1024]{2,1,0:T(8,128)(2,1)} %bitcast.26, ...), custom_call_target="tpu_custom_call" | custom-call | flops 1000 | bytes 1000 | tf_op jit(solution)/shard_map/pallas_call | solution.py:144
  20.7 8.5 %collective-permute-done = bf16[256,1024]{1,0:T(8,128)(2,1)S(1)} collective-permute-done((bf16[256,1024]{1,0:T(8,128)(2,1)S(1)}, bf16[256,1024]{1,0:T(8,128)(2,1)S(1)}, u32[]{:S(2)}, u32[]{:S(2)}) %collective-permute-start) | collective-permute-done | bytes 524320 | tf_op jit(solution)/shard_map/ppermute | solution.py:24
  29.2 0.0 collective-permute-start.1
  29.2 5.9 %shard_map.105 = (bf16[2048,128]{1,0:T(8,128)(2,1)S(1)}, bf16[2048,128]{1,0:T(8,128)(2,1)S(1)}, f32[2048,128]{1,0:T(8,128)S(1)}, f32[2048,128]{1,0:T(8,128)S(1)}, f32[32,256]{1,0:T(8,128)S(1)}) custom-call(s32[1]{0:T(128)} %bitcast.refs_0_.pos_ref._, s32[2,4]{1,0:T(2,128)} %bitcast.37, s32[2]{0:T(128)} %bitcast.44, bf16[1,256,1024]{2,1,0:T(8,128)(2,1)S(1)} %bitcast.21, ...), custom_call_target="tpu_custom_call" | custom-call | flops 40000000000 | bytes 1000 | tf_op jit(solution)/shard_map/pallas_call | solution.py:144
  35.0 1.4 %collective-permute-done.3.refs_1_ = bf16[2048,256]{1,0:T(8,128)(2,1)S(1)} collective-permute-done((bf16[2048,256]{1,0:T(8,128)(2,1)S(1)}, bf16[2048,256]{1,0:T(8,128)(2,1)S(1)}, u32[]{:S(2)}, u32[]{:S(2)}) %collective-permute-start.3) | collective-permute-done | bytes 1048608 | tf_op jit(solution)/shard_map/ppermute | solution.py:24
  36.4 0.2 shard_map.107
  36.6 1.6 %collective-permute-start.5 = (bf16[1024,256]{1,0:T(8,128)(2,1)S(1)}, bf16[1024,256]{1,0:T(8,128)(2,1)S(1)}, u32[]{:S(2)}, u32[]{:S(2)}) collective-permute-start(bf16[1024,256]{1,0:T(8,128)(2,1)S(1)} %get-tuple-element.74), channel_id=1, source_target_pairs={{0,1},{1,0},{2,3},{3,2},{4,5},{5,4},{6,7},{7,6},{8,9},{9,8},{10,11... | collective-permute-start | bytes 1572872 | tf_op jit(solution)/shard_map/ppermute | solution.py:24
  38.1 2.0 %collective-permute-done.2.refs_1_ = bf16[2176,256]{1,0:T(8,128)(2,1)S(1)} collective-permute-done((bf16[2176,256]{1,0:T(8,128)(2,1)S(1)}, bf16[2176,256]{1,0:T(8,128)(2,1)S(1)}, u32[]{:S(2)}, u32[]{:S(2)}) %collective-permute-start.2) | collective-permute-done | bytes 1114144 | tf_op jit(solution)/shard_map/ppermute | solution.py:24
  40.2 0.2 shard_map.106
  40.4 0.1 collective-permute-start.4
  40.4 1.5 %collective-permute-start.10 = (bf16[2048,128]{1,0:T(8,128)(2,1)S(1)}, bf16[2048,128]{1,0:T(8,128)(2,1)S(1)}, u32[]{:S(2)}, u32[]{:S(2)}) collective-permute-start(bf16[2048,128]{1,0:T(8,128)(2,1)S(1)} %get-tuple-element.91), channel_id=1, source_target_pairs={{0,1},{1,0},{2,3},{3,2},{4,5},{5,4},{6,7},{7,6},{8,9},{9,8},{10,11... | collective-permute-start | bytes 1572872 | tf_op jit(solution)/shard_map/ppermute | solution.py:24
  42.0 1.9 %collective-permute-start.11 = (bf16[2048,128]{1,0:T(8,128)(2,1)S(1)}, bf16[2048,128]{1,0:T(8,128)(2,1)S(1)}, u32[]{:S(2)}, u32[]{:S(2)}) collective-permute-start(bf16[2048,128]{1,0:T(8,128)(2,1)S(1)} %get-tuple-element.93), channel_id=1, source_target_pairs={{0,2},{1,3},{2,0},{3,1},{4,6},{5,7},{6,4},{7,5},{8,10},{9,11},{10,... | collective-permute-start | bytes 1572872 | tf_op jit(solution)/shard_map/ppermute | solution.py:24
  43.9 3.5 %shard_map.108.refs_4_ = bf16[8,512,1024]{2,1,0:T(8,128)(2,1)S(1)} custom-call(s32[1]{0:T(128)} %bitcast.refs_0_.pos_ref._, bf16[8,512,1024]{2,1,0:T(8,128)(2,1)} %bitcast.28), custom_call_target="tpu_custom_call" | custom-call | flops 1000 | bytes 1000 | tf_op jit(solution)/shard_map/pallas_call | solution.py:182
  47.4 7.0 %collective-permute-done.1 = bf16[256,1024]{1,0:T(8,128)(2,1)S(1)} collective-permute-done((bf16[256,1024]{1,0:T(8,128)(2,1)S(1)}, bf16[256,1024]{1,0:T(8,128)(2,1)S(1)}, u32[]{:S(2)}, u32[]{:S(2)}) %collective-permute-start.1) | collective-permute-done | bytes 524320 | tf_op jit(solution)/shard_map/ppermute | solution.py:24
  54.4 4.8 %shard_map.109 = (bf16[2048,128]{1,0:T(8,128)(2,1)S(1)}, bf16[2048,128]{1,0:T(8,128)(2,1)S(1)}, f32[2048,128]{1,0:T(8,128)S(1)}, f32[2048,128]{1,0:T(8,128)S(1)}, f32[32,256]{1,0:T(8,128)S(1)}) custom-call(s32[1]{0:T(128)} %bitcast.refs_0_.pos_ref._, s32[2,4]{1,0:T(2,128)} %bitcast.38, s32[2]{0:T(128)} %bitcast.45, bf16[1,256,1024]{2,1,0:T(8,128)(2,1)S(1)} %bitcast.23, ...), custom_call_target="tpu_custom_call" | custom-call | flops 40000000000 | bytes 1000 | tf_op jit(solution)/shard_map/pallas_call | solution.py:144
  59.3 0.0 collective-permute-done.5.refs_3_.refs_8_
  59.3 0.0 collective-permute-done.4.refs_2_.refs_6_
  59.3 0.1 shard_map.110
  59.4 0.1 collective-permute-start.6
  59.5 1.5 %collective-permute-start.8 = (bf16[192,256]{1,0:T(8,128)(2,1)S(1)}, bf16[192,256]{1,0:T(8,128)(2,1)S(1)}, u32[]{:S(2)}, u32[]{:S(2)}) collective-permute-start(bf16[192,256]{1,0:T(8,128)(2,1)S(1)} %get-tuple-element.85), channel_id=1, source_target_pairs={{0,12},{1,13},{2,14},{3,15},{4,8},{5,9},{6,10},{7,11},{8,4},{9,5},... | collective-permute-start | bytes 294920 | tf_op jit(solution)/shard_map/ppermute | solution.py:24
  61.0 2.0 %collective-permute-start.7 = (bf16[192,256]{1,0:T(8,128)(2,1)S(1)}, bf16[192,256]{1,0:T(8,128)(2,1)S(1)}, u32[]{:S(2)}, u32[]{:S(2)}) collective-permute-start(bf16[192,256]{1,0:T(8,128)(2,1)S(1)} %get-tuple-element.85), channel_id=1, source_target_pairs={{0,8},{1,9},{2,10},{3,11},{4,12},{5,13},{6,14},{7,15},{8,0},{9,1},... | collective-permute-start | bytes 294920 | tf_op jit(solution)/shard_map/ppermute | solution.py:24
  63.0 0.0 collective-permute-done.10.refs_2_
  63.0 1.5 %collective-permute-done.11.refs_3_ = bf16[2048,128]{1,0:T(8,128)(2,1)S(1)} collective-permute-done((bf16[2048,128]{1,0:T(8,128)(2,1)S(1)}, bf16[2048,128]{1,0:T(8,128)(2,1)S(1)}, u32[]{:S(2)}, u32[]{:S(2)}) %collective-permute-start.11) | collective-permute-done | bytes 524320 | tf_op jit(solution)/shard_map/ppermute | solution.py:24
  64.4 0.0 copy-start
  64.4 0.2 shard_map.113
  64.6 0.4 collective-permute-start.12
  65.0 1.5 %collective-permute-start.13 = (bf16[1024,128]{1,0:T(8,128)(2,1)S(1)}, bf16[1024,128]{1,0:T(8,128)(2,1)S(1)}, u32[]{:S(2)}, u32[]{:S(2)}) collective-permute-start(bf16[1024,128]{1,0:T(8,128)(2,1)S(1)} %get-tuple-element.102), channel_id=1, source_target_pairs={{0,1},{1,0},{2,3},{3,2},{4,5},{5,4},{6,7},{7,6},{8,9},{9,8},{10,11... | collective-permute-start | bytes 786440 | tf_op jit(solution)/shard_map/ppermute | solution.py:24
  66.5 0.9 collective-permute-done.8.refs_9_.refs_5_
  67.4 0.0 collective-permute-start.9
  67.4 4.2 %collective-permute-done.7.refs_8_.refs_4_ = bf16[192,256]{1,0:T(8,128)(2,1)S(1)} collective-permute-done((bf16[192,256]{1,0:T(8,128)(2,1)S(1)}, bf16[192,256]{1,0:T(8,128)(2,1)S(1)}, u32[]{:S(2)}, u32[]{:S(2)}) %collective-permute-start.7) | collective-permute-done | bytes 98336 | tf_op jit(solution)/shard_map/ppermute | solution.py:24
  71.6 0.0 collective-permute-done.6.refs_7_.refs_3_
  71.6 0.1 shard_map.115
  71.7 1.3 %collective-permute-start.15 = (bf16[2304,128]{1,0:T(8,128)(2,1)S(1)}, bf16[2304,128]{1,0:T(8,128)(2,1)S(1)}, u32[]{:S(2)}, u32[]{:S(2)}) collective-permute-start(bf16[2304,128]{1,0:T(8,128)(2,1)S(1)} %get-tuple-element.104), channel_id=1, source_target_pairs={{0,2},{1,3},{2,0},{3,1},{4,6},{5,7},{6,4},{7,5},{8,10},{9,11},{10,... | collective-permute-start | bytes 1769480 | tf_op jit(solution)/shard_map/ppermute | solution.py:24
  73.0 1.5 %collective-permute-start.14 = (bf16[2304,128]{1,0:T(8,128)(2,1)S(1)}, bf16[2304,128]{1,0:T(8,128)(2,1)S(1)}, u32[]{:S(2)}, u32[]{:S(2)}) collective-permute-start(bf16[2304,128]{1,0:T(8,128)(2,1)S(1)} %get-tuple-element.99), channel_id=1, source_target_pairs={{0,1},{1,0},{2,3},{3,2},{4,5},{5,4},{6,7},{7,6},{8,9},{9,8},{10,11... | collective-permute-start | bytes 1769480 | tf_op jit(solution)/shard_map/ppermute | solution.py:24
  74.5 0.0 copy-done
  74.5 2.4 %shard_map.112 = bf16[8,32,1024]{2,1,0:T(8,128)(2,1)} custom-call(s32[1]{0:T(128)} %bitcast.refs_0_.pos_ref._, s32[2,4]{1,0:T(2,128)} %bitcast.39, s32[2]{0:T(128)} %bitcast.46, bf16[2,256,1024]{2,1,0:T(8,128)(2,1)S(1)} %bitcast.20, bf16[1,256,1024]{2,1,0:T(8,128)(2,1)S(1)} %bitcast.22, bf16[1,256,1024]{2,1,0:T(8,128)(2,1)S(1)} %bitcast.24, ...), custom_call_target="tpu_custom_call" | custom-call | flops 40000000000 | bytes 1000 | tf_op jit(solution)/shard_map/pallas_call | solution.py:505
  76.9 0.0 collective-permute-done.12.refs_2_.refs_10_
  76.9 0.0 collective-permute-done.13.refs_3_.refs_12_
  76.9 0.1 shard_map.116
  77.0 4.5 %collective-permute-done.9.refs_0_ = bf16[512,512]{1,0:T(8,128)(2,1)S(1)} collective-permute-done((bf16[512,512]{1,0:T(8,128)(2,1)S(1)}, bf16[512,512]{1,0:T(8,128)(2,1)S(1)}, u32[]{:S(2)}, u32[]{:S(2)}) %collective-permute-start.9) | collective-permute-done | bytes 524320 | tf_op jit(solution)/shard_map/ppermute | solution.py:34
  81.5 5.0 %collective-permute-done.15.refs_3_ = bf16[2304,128]{1,0:T(8,128)(2,1)S(1)} collective-permute-done((bf16[2304,128]{1,0:T(8,128)(2,1)S(1)}, bf16[2304,128]{1,0:T(8,128)(2,1)S(1)}, u32[]{:S(2)}, u32[]{:S(2)}) %collective-permute-start.15) | collective-permute-done | bytes 589856 | tf_op jit(solution)/shard_map/ppermute | solution.py:24
  86.5 1.0 collective-permute-done.14.refs_2_
  87.5 0.3 shard_map.117
  87.8 0.8 collective-permute-start.16
  88.6 1.2 %collective-permute-start.17 = (bf16[1280,128]{1,0:T(8,128)(2,1)S(1)}, bf16[1280,128]{1,0:T(8,128)(2,1)S(1)}, u32[]{:S(2)}, u32[]{:S(2)}) collective-permute-start(bf16[1280,128]{1,0:T(8,128)(2,1)S(1)} %get-tuple-element.109), channel_id=1, source_target_pairs={{0,1},{1,0},{2,3},{3,2},{4,5},{5,4},{6,7},{7,6},{8,9},{9,8},{10,11... | collective-permute-start | bytes 983048 | tf_op jit(solution)/shard_map/ppermute | solution.py:24
  89.9 0.0 collective-permute-start.19
  89.9 5.9 %collective-permute-done.16.refs_2_.got_x_ref.refs_14_ = bf16[1280,128]{1,0:T(8,128)(2,1)S(1)} collective-permute-done((bf16[1280,128]{1,0:T(8,128)(2,1)S(1)}, bf16[1280,128]{1,0:T(8,128)(2,1)S(1)}, u32[]{:S(2)}, u32[]{:S(2)}) %collective-permute-start.16) | collective-permute-done | bytes 327712 | tf_op jit(solution)/shard_map/ppermute | solution.py:24
  95.8 0.5 collective-permute-done.17.refs_3_.got_y_ref.refs_16_
  96.3 0.1 shard_map.118
  96.3 0.1 collective-permute-start.20
  96.4 1.6 %shard_map.120 = bf16[512,1024]{1,0:T(8,128)(2,1)S(1)} custom-call(s32[1]{0:T(128)} %bitcast.refs_0_.pos_ref._, s32[2,4]{1,0:T(2,128)} %bitcast.40, s32[2]{0:T(128)} %bitcast.47, bf16[8,64,512]{2,1,0:T(8,128)(2,1)} %bitcast.30, bf16[64,1024]{1,0:T(8,128)(2,1)S(1)} %shard_map.119.refs_4_.lowrank_ref, f32[1024,256]{1,0:T(8,128)S(1)} %get-tuple-element.80.refs_0_.refs_5_, ...), custom_call_target="tpu_custom_call" | custom-call | flops 1000 | bytes 1000 | tf_op jit(solution)/shard_map/pallas_call | solution.py:592
  98.0 0.4 collective-permute-start.18
  98.5 2.9 %shard_map.122 = bf16[8,64,512]{2,1,0:T(8,128)(2,1)} custom-call(s32[1]{0:T(128)} %bitcast.refs_0_.pos_ref._, s32[2,4]{1,0:T(2,128)} %bitcast.41, s32[2]{0:T(128)} %bitcast.48, bf16[2,512,512]{2,1,0:T(8,128)(2,1)} %bitcast.49, bf16[64,1024]{1,0:T(8,128)(2,1)S(1)} %shard_map.119.refs_4_.lowrank_ref), custom_call_target="tpu_custom_call" | custom-call | flops 40000000000 | bytes 1000 | tf_op jit(solution)/shard_map/pallas_call | solution.py:661
  101.3 0.0 collective-permute-done.19.refs_1_
  101.3 2.5 %collective-permute-done.20.refs_2_ = bf16[512,256]{1,0:T(8,128)(2,1)S(1)} collective-permute-done((bf16[512,256]{1,0:T(8,128)(2,1)S(1)}, bf16[512,256]{1,0:T(8,128)(2,1)S(1)}, u32[]{:S(2)}, u32[]{:S(2)}) %collective-permute-start.20) | collective-permute-done | bytes 262176 | tf_op jit(solution)/shard_map/ppermute | solution.py:34
  103.8 0.0 collective-permute-done.18.kept_ref
  103.8 1.3 %shard_map.121 = bf16[2,512,512]{2,1,0:T(8,128)(2,1)} custom-call(s32[1]{0:T(128)} %bitcast.refs_0_.pos_ref._, bf16[512,1024]{1,0:T(8,128)(2,1)S(1)} %collective-permute-done.18.kept_ref, bf16[512,512]{1,0:T(8,128)(2,1)S(1)} %collective-permute-done.9.refs_0_, bf16[512,256]{1,0:T(8,128)(2,1)S(1)} %collective-permute-done.19.refs_1_, ...), custom_call_target="tpu_custom_call" | custom-call | flops 1000 | bytes 1000 | tf_op jit(solution)/shard_map/pallas_call | solution.py:629
  (3 shorter events, 0.1 us)
Async XLA Ops:
  1.9 27.3 %collective-permute-start = (bf16[256,1024]{1,0:T(8,128)(2,1)S(1)}, bf16[256,1024]{1,0:T(8,128)(2,1)S(1)}, u32[]{:S(2)}, u32[]{:S(2)}) collective-permute-start(bf16[256,1024]{1,0:T(8,128)(2,1)S(1)} %get-tuple-element.111), channel_id=1, source_target_pairs={{0,8},{1,9},{2,10},{3,11},{4,12},{5,13},{6,14},{7,15},{8,0},{9,1},... | collective-permute-start | bytes 1572872 | tf_op jit(solution)/shard_map/ppermute | solution.py:24
  11.7 24.7 %collective-permute-start.3 = (bf16[2048,256]{1,0:T(8,128)(2,1)S(1)}, bf16[2048,256]{1,0:T(8,128)(2,1)S(1)}, u32[]{:S(2)}, u32[]{:S(2)}) collective-permute-start(bf16[2048,256]{1,0:T(8,128)(2,1)S(1)} %get-tuple-element.63), channel_id=1, source_target_pairs={{0,2},{1,3},{2,0},{3,1},{4,6},{5,7},{6,4},{7,5},{8,10},{9,11},{10,... | collective-permute-start | bytes 3145736 | tf_op jit(solution)/shard_map/ppermute | solution.py:24
  13.3 26.9 %collective-permute-start.2 = (bf16[2176,256]{1,0:T(8,128)(2,1)S(1)}, bf16[2176,256]{1,0:T(8,128)(2,1)S(1)}, u32[]{:S(2)}, u32[]{:S(2)}) collective-permute-start(bf16[2176,256]{1,0:T(8,128)(2,1)S(1)} %get-tuple-element.62), channel_id=1, source_target_pairs={{0,1},{1,0},{2,3},{3,2},{4,5},{5,4},{6,7},{7,6},{8,9},{9,8},{10,11... | collective-permute-start | bytes 3342344 | tf_op jit(solution)/shard_map/ppermute | solution.py:24
  29.2 25.2 %collective-permute-start.1 = (bf16[256,1024]{1,0:T(8,128)(2,1)S(1)}, bf16[256,1024]{1,0:T(8,128)(2,1)S(1)}, u32[]{:S(2)}, u32[]{:S(2)}) collective-permute-start(bf16[256,1024]{1,0:T(8,128)(2,1)S(1)} %get-tuple-element.60), channel_id=1, source_target_pairs={{0,8},{1,9},{2,10},{3,11},{4,12},{5,13},{6,14},{7,15},{8,0},{9,1},... | collective-permute-start | bytes 1572872 | tf_op jit(solution)/shard_map/ppermute | solution.py:24
  36.6 22.7 %collective-permute-start.5 = (bf16[1024,256]{1,0:T(8,128)(2,1)S(1)}, bf16[1024,256]{1,0:T(8,128)(2,1)S(1)}, u32[]{:S(2)}, u32[]{:S(2)}) collective-permute-start(bf16[1024,256]{1,0:T(8,128)(2,1)S(1)} %get-tuple-element.74), channel_id=1, source_target_pairs={{0,1},{1,0},{2,3},{3,2},{4,5},{5,4},{6,7},{7,6},{8,9},{9,8},{10,11... | collective-permute-start | bytes 1572872 | tf_op jit(solution)/shard_map/ppermute | solution.py:24
  40.4 18.9 %collective-permute-start.4 = (bf16[1152,256]{1,0:T(8,128)(2,1)S(1)}, bf16[1152,256]{1,0:T(8,128)(2,1)S(1)}, u32[]{:S(2)}, u32[]{:S(2)}) collective-permute-start(bf16[1152,256]{1,0:T(8,128)(2,1)S(1)} %get-tuple-element.71), channel_id=1, source_target_pairs={{0,2},{1,3},{2,0},{3,1},{4,6},{5,7},{6,4},{7,5},{8,10},{9,11},{10,... | collective-permute-start | bytes 1769480 | tf_op jit(solution)/shard_map/ppermute | solution.py:24
  40.4 22.6 %collective-permute-start.10 = (bf16[2048,128]{1,0:T(8,128)(2,1)S(1)}, bf16[2048,128]{1,0:T(8,128)(2,1)S(1)}, u32[]{:S(2)}, u32[]{:S(2)}) collective-permute-start(bf16[2048,128]{1,0:T(8,128)(2,1)S(1)} %get-tuple-element.91), channel_id=1, source_target_pairs={{0,1},{1,0},{2,3},{3,2},{4,5},{5,4},{6,7},{7,6},{8,9},{9,8},{10,11... | collective-permute-start | bytes 1572872 | tf_op jit(solution)/shard_map/ppermute | solution.py:24
  42.0 22.5 %collective-permute-start.11 = (bf16[2048,128]{1,0:T(8,128)(2,1)S(1)}, bf16[2048,128]{1,0:T(8,128)(2,1)S(1)}, u32[]{:S(2)}, u32[]{:S(2)}) collective-permute-start(bf16[2048,128]{1,0:T(8,128)(2,1)S(1)} %get-tuple-element.93), channel_id=1, source_target_pairs={{0,2},{1,3},{2,0},{3,1},{4,6},{5,7},{6,4},{7,5},{8,10},{9,11},{10,... | collective-permute-start | bytes 1572872 | tf_op jit(solution)/shard_map/ppermute | solution.py:24
  59.4 12.1 %collective-permute-start.6 = (bf16[256,256]{1,0:T(8,128)(2,1)S(1)}, bf16[256,256]{1,0:T(8,128)(2,1)S(1)}, u32[]{:S(2)}, u32[]{:S(2)}) collective-permute-start(bf16[256,256]{1,0:T(8,128)(2,1)S(1)} %get-tuple-element.84), channel_id=1, source_target_pairs={{0,4},{1,5},{2,6},{3,7},{4,0},{5,1},{6,2},{7,3},{8,12},{9,13},{10,... | collective-permute-start | bytes 393224 | tf_op jit(solution)/shard_map/ppermute | solution.py:24
  59.5 7.9 %collective-permute-start.8 = (bf16[192,256]{1,0:T(8,128)(2,1)S(1)}, bf16[192,256]{1,0:T(8,128)(2,1)S(1)}, u32[]{:S(2)}, u32[]{:S(2)}) collective-permute-start(bf16[192,256]{1,0:T(8,128)(2,1)S(1)} %get-tuple-element.85), channel_id=1, source_target_pairs={{0,12},{1,13},{2,14},{3,15},{4,8},{5,9},{6,10},{7,11},{8,4},{9,5},... | collective-permute-start | bytes 294920 | tf_op jit(solution)/shard_map/ppermute | solution.py:24
  61.0 10.6 %collective-permute-start.7 = (bf16[192,256]{1,0:T(8,128)(2,1)S(1)}, bf16[192,256]{1,0:T(8,128)(2,1)S(1)}, u32[]{:S(2)}, u32[]{:S(2)}) collective-permute-start(bf16[192,256]{1,0:T(8,128)(2,1)S(1)} %get-tuple-element.85), channel_id=1, source_target_pairs={{0,8},{1,9},{2,10},{3,11},{4,12},{5,13},{6,14},{7,15},{8,0},{9,1},... | collective-permute-start | bytes 294920 | tf_op jit(solution)/shard_map/ppermute | solution.py:24
  64.4 10.1 %copy-start = (bf16[1,1,2,256,1024]{4,3,2,1,0:T(8,128)(2,1)S(1)}, bf16[1,1,2,256,1024]{4,3,2,1,0:T(8,128)(2,1)}, u32[]{:S(2)}) copy-start(bf16[1,1,2,256,1024]{4,3,2,1,0:T(8,128)(2,1)} %param.8) | copy-start | bytes 3145732
  64.6 12.3 %collective-permute-start.12 = (bf16[1024,128]{1,0:T(8,128)(2,1)S(1)}, bf16[1024,128]{1,0:T(8,128)(2,1)S(1)}, u32[]{:S(2)}, u32[]{:S(2)}) collective-permute-start(bf16[1024,128]{1,0:T(8,128)(2,1)S(1)} %get-tuple-element.101), channel_id=1, source_target_pairs={{0,2},{1,3},{2,0},{3,1},{4,6},{5,7},{6,4},{7,5},{8,10},{9,11},{10,... | collective-permute-start | bytes 786440 | tf_op jit(solution)/shard_map/ppermute | solution.py:24
  65.0 12.0 %collective-permute-start.13 = (bf16[1024,128]{1,0:T(8,128)(2,1)S(1)}, bf16[1024,128]{1,0:T(8,128)(2,1)S(1)}, u32[]{:S(2)}, u32[]{:S(2)}) collective-permute-start(bf16[1024,128]{1,0:T(8,128)(2,1)S(1)} %get-tuple-element.102), channel_id=1, source_target_pairs={{0,1},{1,0},{2,3},{3,2},{4,5},{5,4},{6,7},{7,6},{8,9},{9,8},{10,11... | collective-permute-start | bytes 786440 | tf_op jit(solution)/shard_map/ppermute | solution.py:24
  67.4 14.1 %collective-permute-start.9 = (bf16[512,512]{1,0:T(8,128)(2,1)S(1)}, bf16[512,512]{1,0:T(8,128)(2,1)S(1)}, u32[]{:S(2)}, u32[]{:S(2)}) collective-permute-start(bf16[512,512]{1,0:T(8,128)(2,1)S(1)} %get-tuple-element.86), channel_id=1, source_target_pairs={{0,20},{1,21},{2,22},{3,23},{4,16},{5,17},{6,18},{7,19},{8,28},{9,... | collective-permute-start | bytes 1572872 | tf_op jit(solution)/shard_map/ppermute | solution.py:34
  71.7 14.8 %collective-permute-start.15 = (bf16[2304,128]{1,0:T(8,128)(2,1)S(1)}, bf16[2304,128]{1,0:T(8,128)(2,1)S(1)}, u32[]{:S(2)}, u32[]{:S(2)}) collective-permute-start(bf16[2304,128]{1,0:T(8,128)(2,1)S(1)} %get-tuple-element.104), channel_id=1, source_target_pairs={{0,2},{1,3},{2,0},{3,1},{4,6},{5,7},{6,4},{7,5},{8,10},{9,11},{10,... | collective-permute-start | bytes 1769480 | tf_op jit(solution)/shard_map/ppermute | solution.py:24
  73.0 14.5 %collective-permute-start.14 = (bf16[2304,128]{1,0:T(8,128)(2,1)S(1)}, bf16[2304,128]{1,0:T(8,128)(2,1)S(1)}, u32[]{:S(2)}, u32[]{:S(2)}) collective-permute-start(bf16[2304,128]{1,0:T(8,128)(2,1)S(1)} %get-tuple-element.99), channel_id=1, source_target_pairs={{0,1},{1,0},{2,3},{3,2},{4,5},{5,4},{6,7},{7,6},{8,9},{9,8},{10,11... | collective-permute-start | bytes 1769480 | tf_op jit(solution)/shard_map/ppermute | solution.py:24
  87.8 8.0 %collective-permute-start.16 = (bf16[1280,128]{1,0:T(8,128)(2,1)S(1)}, bf16[1280,128]{1,0:T(8,128)(2,1)S(1)}, u32[]{:S(2)}, u32[]{:S(2)}) collective-permute-start(bf16[1280,128]{1,0:T(8,128)(2,1)S(1)} %get-tuple-element.108), channel_id=1, source_target_pairs={{0,2},{1,3},{2,0},{3,1},{4,6},{5,7},{6,4},{7,5},{8,10},{9,11},{10,... | collective-permute-start | bytes 983048 | tf_op jit(solution)/shard_map/ppermute | solution.py:24
  88.6 7.7 %collective-permute-start.17 = (bf16[1280,128]{1,0:T(8,128)(2,1)S(1)}, bf16[1280,128]{1,0:T(8,128)(2,1)S(1)}, u32[]{:S(2)}, u32[]{:S(2)}) collective-permute-start(bf16[1280,128]{1,0:T(8,128)(2,1)S(1)} %get-tuple-element.109), channel_id=1, source_target_pairs={{0,1},{1,0},{2,3},{3,2},{4,5},{5,4},{6,7},{7,6},{8,9},{9,8},{10,11... | collective-permute-start | bytes 983048 | tf_op jit(solution)/shard_map/ppermute | solution.py:24
  89.9 11.5 %collective-permute-start.19 = (bf16[512,256]{1,0:T(8,128)(2,1)S(1)}, bf16[512,256]{1,0:T(8,128)(2,1)S(1)}, u32[]{:S(2)}, u32[]{:S(2)}) collective-permute-start(bf16[512,256]{1,0:T(8,128)(2,1)S(1)} %shard_map.116), channel_id=1, source_target_pairs={{0,20},{1,21},{2,22},{3,23},{4,16},{5,17},{6,18},{7,19},{8,28},{9,... | collective-permute-start | bytes 786440 | tf_op jit(solution)/shard_map/ppermute | solution.py:34
  96.3 7.5 %collective-permute-start.20 = (bf16[512,256]{1,0:T(8,128)(2,1)S(1)}, bf16[512,256]{1,0:T(8,128)(2,1)S(1)}, u32[]{:S(2)}, u32[]{:S(2)}) collective-permute-start(bf16[512,256]{1,0:T(8,128)(2,1)S(1)} %shard_map.118), channel_id=1, source_target_pairs={{0,20},{1,21},{2,22},{3,23},{4,16},{5,17},{6,18},{7,19},{8,28},{9,... | collective-permute-start | bytes 786440 | tf_op jit(solution)/shard_map/ppermute | solution.py:34
  98.0 5.8 %collective-permute-start.18 = (bf16[512,1024]{1,0:T(8,128)(2,1)S(1)}, bf16[512,1024]{1,0:T(8,128)(2,1)S(1)}, u32[]{:S(2)}, u32[]{:S(2)}) collective-permute-start(bf16[512,1024]{1,0:T(8,128)(2,1)S(1)} %shard_map.120), channel_id=1, source_target_pairs={{0,16},{1,17},{2,18},{3,19},{4,20},{5,21},{6,22},{7,23},{8,24},{9,... | collective-permute-start | bytes 3145736 | tf_op jit(solution)/shard_map/ppermute | solution.py:34
